TPU v7x, 32 devices: a whole 2x2x4 slice. The times are simulated.
32 devices in a mesh: dp: 16 (over z, y, core), ctx: 2 (over x).
Axes of the slice: x: 2, y: 2, z: 4, core: 2. Of those that a mesh axis runs over, the one named last changes fastest.
Arguments:
- normed_input: bfloat16 [4096, 4096], P(('dp', 'ctx')), may hold values from -6 to 6
- queries: bfloat16 [4096, 4096], P(('dp', 'ctx')), may hold values from -120 to 120
- saved_keys: bfloat16 [4096, 512], P(('dp', 'ctx')), may hold values from -6 to 6
- saved_values: bfloat16 [4096, 512], P(('dp', 'ctx')), may hold values from -6 to 6
- attention_output: bfloat16 [4096, 4096], P(('dp', 'ctx')), may hold values from -6 to 6, as said below
- saved_log_totals: float32 [4096, 32], P(('dp', 'ctx')), as said below
- output_gradient: bfloat16 [4096, 4096], P(('dp', 'ctx')), may hold values from -6 to 6
- document_lengths: int32 [16, 4], P('dp'), may hold values from 1 to 128, as said below
Outputs:
- query_gradient: bfloat16 [4096, 4096], P(('dp', 'ctx'))
- key_weight_grad: float32 [4096, 512], P(('dp', 'ctx'))
- value_weight_grad: float32 [4096, 512], P(('dp', 'ctx'))
Inputs may be any that keep to these rules, and one draw needn't show every extreme that they name: `document_lengths`: each sequence holds 4 documents whose lengths sum to 256; the longest is exactly 128. attention_output is the forward's output, the softmax over allowed keys of the scores applied to saved_values, for the given queries, saved_keys, saved_values and document_lengths, rounded to bfloat16. saved_log_totals is the log of the sum of exp of the allowed scores of each query row and head, for the given queries, saved_keys and document_lengths.
All inputs are finite; a program needn't handle non-finite values.
Results may differ from a plain program's by a relative error of at most 0.0051.
Values may be sent and summed in bfloat16 or wider, within the bound.
No kernel may reach another device: no remote copies, remote signals or barrier semaphores. Data moves between devices by JAX's collectives and lax.ppermute only.
A program may use at most 128 MiB of HBM per device.

v0:
```python
import math

import jax
import jax.numpy as jnp
from jax import lax
from jax.sharding import PartitionSpec as P

QUERY_HEADS = 32
KEY_VALUE_HEADS = 4
HEAD_SIZE = 128


def shifted(value, axis, steps):
    count = lax.axis_size(axis)
    pairs = [(source, (source + steps) % count) for source in range(count)]
    return lax.ppermute(value, axis, pairs)


def doc_of(doc_ends, positions):
    return jnp.sum((doc_ends[None, :] <= positions[:, None]).astype(jnp.int32), axis=1)


def local(
    normed_input,
    queries,
    saved_keys,
    saved_values,
    attention_output,
    saved_log_totals,
    output_gradient,
    document_lengths,
):
    token_rows = queries.shape[0]
    key_value_width = saved_keys.shape[1]
    group_count = QUERY_HEADS // KEY_VALUE_HEADS
    ctx_count = lax.axis_size("ctx")
    ctx_rank = lax.axis_index("ctx")
    softmax_scale = 1.0 / math.sqrt(HEAD_SIZE)
    doc_ends = jnp.cumsum(document_lengths[0])
    local_ids = jnp.arange(token_rows, dtype=jnp.int32)
    query_pos = local_ids * ctx_count + ctx_rank
    query_doc = doc_of(doc_ends, query_pos)
    query_tensor_four = queries.reshape(token_rows, KEY_VALUE_HEADS, group_count, HEAD_SIZE)
    output_gradient_four = output_gradient.reshape(
        token_rows, KEY_VALUE_HEADS, group_count, HEAD_SIZE
    )
    key_value = jnp.concatenate([saved_keys, saved_values], axis=1)
    log_softmax_total = jnp.transpose(
        saved_log_totals.reshape(token_rows, KEY_VALUE_HEADS, group_count), (1, 2, 0)
    )
    product_rows = output_gradient_four.astype(jnp.float32) * attention_output.reshape(
        token_rows, KEY_VALUE_HEADS, group_count, HEAD_SIZE
    ).astype(jnp.float32)
    delta_row = jnp.transpose(jnp.sum(product_rows, axis=-1), (1, 2, 0))

    def block_mask(first_row, block_rows):
        key_ids = first_row + jnp.arange(block_rows, dtype=jnp.int32)
        key_pos = key_ids % token_rows * ctx_count + key_ids // token_rows
        key_doc = doc_of(doc_ends, key_pos)
        return (query_doc[:, None] == key_doc[None, :]) & (key_pos[None, :] <= query_pos[:, None])

    def backward_block(key_block_slice, first_row, grad_block, query_grad):
        allowed = block_mask(first_row, key_block_slice.shape[0])
        key_tensor_three = key_block_slice[:, :key_value_width].reshape(
            -1, KEY_VALUE_HEADS, HEAD_SIZE
        )
        value_tensor_three = key_block_slice[:, key_value_width:].reshape(
            -1, KEY_VALUE_HEADS, HEAD_SIZE
        )
        score_matrix = (
            jnp.einsum(
                "szot,mzt->zosm",
                query_tensor_four,
                key_tensor_three,
                preferred_element_type=jnp.float32,
            )
            * softmax_scale
        )
        probs = jnp.where(allowed, jnp.exp(score_matrix - log_softmax_total[..., None]), 0.0)
        grad_probs = jnp.einsum(
            "szot,mzt->zosm",
            output_gradient_four,
            value_tensor_three,
            preferred_element_type=jnp.float32,
        )
        grad_scores = (probs * (grad_probs - delta_row[..., None])).astype(jnp.bfloat16)
        probs_low = probs.astype(jnp.bfloat16)
        query_grad = query_grad + jnp.einsum(
            "sjba,asp->bsjp", grad_scores, key_tensor_three, preferred_element_type=jnp.float32
        )
        key_part = (
            jnp.einsum(
                "hgqk,qhgd->khd", grad_scores, query_tensor_four, preferred_element_type=jnp.float32
            )
            * softmax_scale
        )
        value_part = jnp.einsum(
            "hgqk,qhgd->khd", probs_low, output_gradient_four, preferred_element_type=jnp.float32
        )
        block_rows = key_block_slice.shape[0]
        grad_block = grad_block + jnp.concatenate(
            [
                key_part.reshape(block_rows, key_value_width),
                value_part.reshape(block_rows, key_value_width),
            ],
            axis=1,
        )
        return (grad_block, query_grad)

    def send_grads(grad_block):
        return shifted(grad_block, "ctx", 1)

    grad_block, query_grad = backward_block(
        key_value,
        ctx_rank * token_rows,
        jnp.zeros((token_rows, 2 * key_value_width), jnp.float32),
        jnp.zeros((token_rows, KEY_VALUE_HEADS, group_count, HEAD_SIZE), jnp.float32),
    )

    def backward_step(step_index, state):
        visiting, grad_now, query_now = state
        visiting = shifted(visiting, "ctx", 1)
        grad_now = send_grads(grad_now)
        owner = (ctx_rank - step_index) % ctx_count
        grad_now, query_now = backward_block(visiting, owner * token_rows, grad_now, query_now)
        return (visiting, grad_now, query_now)

    finished = lax.fori_loop(1, ctx_count, backward_step, (key_value, grad_block, query_grad))
    grad_block = send_grads(finished[1])
    query_gradient = (
        (finished[2] * softmax_scale)
        .reshape(token_rows, QUERY_HEADS * HEAD_SIZE)
        .astype(jnp.bfloat16)
    )
    key_grads_low = grad_block.astype(jnp.bfloat16)
    weight_gradient = lax.psum_scatter(
        lax.dot_general(
            normed_input,
            key_grads_low,
            (((0,), (0,)), ((), ())),
            preferred_element_type=jnp.float32,
        ),
        ("dp", "ctx"),
        scatter_dimension=0,
        tiled=True,
    )
    return (
        query_gradient,
        weight_gradient[:, :key_value_width],
        weight_gradient[:, key_value_width:],
    )


def solution(mesh):
    placed = (
        P(("dp", "ctx"), None),
        P(("dp", "ctx"), None),
        P(("dp", "ctx"), None),
        P(("dp", "ctx"), None),
        P(("dp", "ctx"), None),
        P(("dp", "ctx"), None),
        P(("dp", "ctx"), None),
        P("dp", None),
    )
    return jax.shard_map(
        local,
        mesh=mesh,
        in_specs=placed,
        out_specs=(P(("dp", "ctx"), None), P(("dp", "ctx"), None), P(("dp", "ctx"), None)),
        check_vma=False,
    )
```

profile of v0, /device:TPU:0, one launch (start us, length us, event | category | flops | bytes accessed | tf_op | source)
XLA Modules:
  0.0 427.2 jit_solution(10883383647177230438)
XLA Ops:
  7.2 0.0 copy-start
  7.2 0.0 reduce-scatter.2.cloned.1.call-start
  7.2 1.2 copy.88
  8.4 1.0 copy.89
  9.4 0.7 pad_maximum_fusion.1
  10.2 2.9 collective-permute-start
  13.1 0.6 multiply_add_fusion
  13.7 0.9 reshape.212
  14.6 1.6 reshape.215
  16.2 1.4 reduce-window.8
  17.6 0.1 copy.109
  17.8 0.7 copy.132
  18.5 2.4 copy.133
  20.9 1.9 copy.98
  22.8 1.4 convert_bitcast_fusion
  24.3 0.4 copy.134
  24.7 0.8 copy-done.3
  25.5 0.8 multiply_reduce_fusion
  26.3 0.1 copy.85
  26.5 0.8 convert_reduce_fusion
  27.2 0.8 compare_and_fusion
  28.1 1.3 fusion.9
  29.4 0.4 fusion.14
  29.8 0.4 copy-done.7
  30.3 0.4 fusion.7
  30.8 0.4 fusion.11
  31.2 0.1 collective-permute-start.1
  31.3 1.0 fusion.23
  32.3 0.6 fusion.5
  33.0 0.5 fusion.3
  33.5 1.0 copy-done.4
  34.5 0.4 fusion.10
  34.9 0.4 fusion.12
  35.3 9.4 %collective-permute-done.1 = f32[128,1024]{0,1:T(8,128)S(1)} collective-permute-done((f32[128,1024]{0,1:T(8,128)S(1)}, f32[128,1024]{0,1:T(8,128)S(1)}, u32[]{:S(2)}, u32[]{:S(2)}) %collective-permute-start.1) | collective-permute-done | bytes 524320 | tf_op jit(solution)/shard_map/while/body/eval_jaxpr/ppermute | solution.py:16
  44.7 0.1 maximum_add_fusion
  44.8 0.4 collective-permute-start.2
  45.1 6.6 %collective-permute-done.2 = bf16[128,1024]{0,1:T(8,128)(2,1)S(1)} collective-permute-done((bf16[128,1024]{0,1:T(8,128)(2,1)S(1)}, bf16[128,1024]{0,1:T(8,128)(2,1)S(1)}, u32[]{:S(2)}, u32[]{:S(2)}) %collective-permute-start.2) | collective-permute-done | bytes 262176 | tf_op jit(solution)/shard_map/ppermute | solution.py:16
  51.7 8.1 %convolution_bitcast_fusion = f32[4096,1024]{0,1:T(8,128)} fusion(bf16[128,4096]{1,0:T(8,128)(2,1)S(1)} %copy-done, bf16[128,1024]{0,1:T(8,128)(2,1)S(1)} %collective-permute-done.2), kind=kOutput, calls=%fused_computation | convolution fusion | flops 1073741824 | bytes 18087936 | tf_op jit(solution)/shard_map/dot_general | solution.py:137
  59.7 0.0 reduce-scatter.2.cloned.1.call-update
  59.8 1.2 copy-done.2
  61.0 0.4 fusion.24
  61.4 0.8 copy-done.5
  62.2 0.4 fusion.1
  62.6 1.3 copy.103
  63.9 353.6 %reduce-scatter.2.cloned.1.call-done = f32[128,1024]{0,1:T(8,128)} async-done(((f32[4096,1024]{0,1:T(8,128)}), f32[128,1024]{0,1:T(8,128)}) %reduce-scatter.2.cloned.1.call-update) | async-done | bytes 524304 | tf_op jit(solution)/shard_map/reduce_scatter | solution.py:136
  417.6 1.1 fusion.22
  418.6 0.8 copy.105
  419.5 0.8 copy.104
  (15 shorter events, 0.1 us)
Async XLA Ops:
  7.2 44.5 %copy-start = (bf16[128,4096]{1,0:T(8,128)(2,1)S(1)}, bf16[128,4096]{1,0:T(8,128)(2,1)}, u32[]{:S(2)}) copy-start(bf16[128,4096]{1,0:T(8,128)(2,1)} %param.8) | copy-start | bytes 3145732
  7.2 10.6 %copy-start.6 = (bf16[128,4096]{1,0:T(8,128)(2,1)S(1)}, bf16[128,4096]{1,0:T(8,128)(2,1)}, u32[]{:S(2)}) copy-start(bf16[128,4096]{1,0:T(8,128)(2,1)} %param.9) | copy-start | bytes 3145732
  7.2 410.4 %reduce-scatter.2.cloned.1.call-start = ((), (), s32[]{:S(2)}) async-start(), calls=%async_computation.1 | async-start | bytes 17301504 | tf_op jit(solution)/shard_map/reduce_scatter | solution.py:136
  10.2 21.2 %collective-permute-start = (bf16[128,1024]{0,1:T(8,128)(2,1)}, bf16[128,1024]{0,1:T(8,128)(2,1)}, u32[]{:S(2)}, u32[]{:S(2)}) collective-permute-start(bf16[128,1024]{0,1:T(8,128)(2,1)} %pad_maximum_fusion.1), channel_id=1, source_target_pairs={{0,1},{1,0},{2,3},{3,2},{4,5},{5,4},{6,7},{7,6},{8,9},{9,8},{10,11... | collective-permute-start | bytes 786440 | tf_op jit(solution)/shard_map/while/body/eval_jaxpr/ppermute | solution.py:16
  24.3 1.2 copy-start.3
  29.4 0.9 copy-start.7
  30.7 2.2 copy-start.1
  30.8 1.6 copy-start.8
  31.2 13.4 %collective-permute-start.1 = (f32[128,1024]{0,1:T(8,128)S(1)}, f32[128,1024]{0,1:T(8,128)S(1)}, u32[]{:S(2)}, u32[]{:S(2)}) collective-permute-start(f32[128,1024]{0,1:T(8,128)S(1)} %pad_maximum_fusion), channel_id=1, source_target_pairs={{0,1},{1,0},{2,3},{3,2},{4,5},{5,4},{6,7},{7,6},{8,9},{9,8},{10,11... | collective-permute-start | bytes 1572872 | tf_op jit(solution)/shard_map/while/body/eval_jaxpr/ppermute | solution.py:16
  33.5 1.0 copy-start.4
  44.8 6.9 %collective-permute-start.2 = (bf16[128,1024]{0,1:T(8,128)(2,1)S(1)}, bf16[128,1024]{0,1:T(8,128)(2,1)S(1)}, u32[]{:S(2)}, u32[]{:S(2)}) collective-permute-start(bf16[128,1024]{0,1:T(8,128)(2,1)S(1)} %maximum_add_fusion), channel_id=1, source_target_pairs={{0,1},{1,0},{2,3},{3,2},{4,5},{5,4},{6,7},{7,6},{8,9},{9,8},{10,11... | collective-permute-start | bytes 786440 | tf_op jit(solution)/shard_map/ppermute | solution.py:16
  59.7 1.2 copy-start.2
  61.0 1.2 copy-start.5
Sparse Core Ops, SparseCore 0:
  59.9 357.6 reduce-scatter.1
where the time goes:
time: 429 us; the launch traced here: 427 us
  waiting for transfers between devices  370 us (86%)
  local copies, waits for them, and re-layouts  19.7 us (5%)
  between operations  14.3 us (3%)
  matrix products  13.5 us (3%)
  other arithmetic  6.7 us (2%)
    reduce_scatter x1, waiting for transfers between devices, local(): lax.psum_scatter(lax.dot_general(normed_input, key_grads_low, (((0,), (0,...  354 us
    ppermute x3, waiting for transfers between devices, shifted(): return lax.ppermute(value, axis, pairs)  15.9 us
    unnamed x25, local copies, waits for them, and re-layouts  12.3 us
  transfers between devices with their start and end apart: 4, of which 3 were waited for; matrix products, arithmetic and copies ran while one was open for 5% of the time, Pallas kernels for 0%

commit v1 on v0

v1 whole, which is shorter than its diff:
```python
import functools
import math

import jax
import jax.numpy as jnp
from jax import lax
from jax.experimental import pallas as pl
from jax.experimental.pallas import tpu as pltpu
from jax.sharding import PartitionSpec as P

QUERY_HEADS = 32
KEY_VALUE_HEADS = 4
HEAD_SIZE = 128
GROUP = QUERY_HEADS // KEY_VALUE_HEADS
SCALE = 1.0 / math.sqrt(HEAD_SIZE)
CORES = 2
VMEM_LIMIT = 48 * 1024 * 1024

NT = (((1,), (1,)), ((), ()))
TN = (((0,), (0,)), ((), ()))
NN = (((1,), (0,)), ((), ()))


def dot(a, b, dims):
    return lax.dot_general(a, b, dims, preferred_element_type=jnp.float32)


def rows_of_heads(block):
    return jnp.concatenate(
        [block[:, h * HEAD_SIZE : (h + 1) * HEAD_SIZE] for h in range(GROUP)], axis=0
    )


def allowed_mask(lengths_ref, ctx_count, rank, owner, keys, rows):
    key_pos = lax.broadcasted_iota(jnp.int32, (keys, rows), 0) * ctx_count + owner
    query_pos = lax.broadcasted_iota(jnp.int32, (keys, rows), 1) * ctx_count + rank
    allowed = key_pos <= query_pos
    end = jnp.int32(0)
    for j in range(lengths_ref.shape[1]):
        end = end + lengths_ref[0, j]
        allowed = allowed & ((end <= key_pos) == (end <= query_pos))
    return allowed


def block_kernel(
    first, ctx_count, step, lengths_ref, q_ref, do_ref, k_ref, v_ref, lse_ref, delta_in, *refs
):
    if first:
        ds_ref, grad_ref, delta_ref, lse_out = refs
    else:
        ds_ref, grad_ref = refs
    rank = lax.axis_index("ctx")
    owner = lax.rem(rank + ctx_count - step, ctx_count)
    rows = q_ref.shape[0]
    keys = k_ref.shape[0]
    allowed = allowed_mask(lengths_ref, ctx_count, rank, owner, keys, rows)
    q = rows_of_heads(q_ref[...])
    do = rows_of_heads(do_ref[...])
    if first:
        width = GROUP * HEAD_SIZE
        product = do_ref[...].astype(jnp.float32) * delta_in[...].astype(jnp.float32)
        high = product.astype(jnp.bfloat16)
        low = (product - high.astype(jnp.float32)).astype(jnp.bfloat16)
        pick = (
            lax.broadcasted_iota(jnp.int32, (GROUP, width), 1) // HEAD_SIZE
            == lax.broadcasted_iota(jnp.int32, (GROUP, width), 0)
        ).astype(jnp.bfloat16)
        delta = dot(pick, high, NT) + dot(pick, low, NT)
        delta_ref[...] = delta
        g = pl.program_id(0)
        heads = lse_ref.shape[1]
        chosen = (
            lax.broadcasted_iota(jnp.int32, (GROUP, heads), 1)
            == lax.broadcasted_iota(jnp.int32, (GROUP, heads), 0) + g * GROUP
        ).astype(jnp.bfloat16)
        rest = lse_ref[...]
        lse = jnp.zeros((GROUP, rows), jnp.float32)
        for _ in range(3):
            part = rest.astype(jnp.bfloat16)
            rest = rest - part.astype(jnp.float32)
            lse = lse + dot(chosen, part, NT)
        lse_out[...] = lse
    else:
        delta = delta_in[...]
        lse = lse_ref[...]
    scores = dot(k_ref[...], q, NT)
    grad_probs = dot(v_ref[...], do, NT)
    probs_low = []
    grad_scores = []
    for h in range(GROUP):
        at = slice(h * rows, (h + 1) * rows)
        probs = jnp.where(allowed, jnp.exp(scores[:, at] * SCALE - lse[h : h + 1, :]), 0.0)
        grad_scores.append((probs * (grad_probs[:, at] - delta[h : h + 1, :])).astype(jnp.bfloat16))
        probs_low.append(probs.astype(jnp.bfloat16))
    probs_low = jnp.concatenate(probs_low, axis=1)
    grad_scores = jnp.concatenate(grad_scores, axis=1)
    ds_ref[...] = grad_scores
    grad_ref[0] = (dot(grad_scores, q, NN) * SCALE).astype(grad_ref.dtype)
    grad_ref[1] = dot(probs_low, do, NN).astype(grad_ref.dtype)


def block_call(step, ctx_count, lengths, queries, output_gradient, keys, values, lse, delta):
    first = step == 0
    rows = queries.shape[0]
    key_rows = keys.shape[0]
    width = GROUP * HEAD_SIZE
    wide = pl.BlockSpec((rows, width), lambda g: (0, g))
    narrow = pl.BlockSpec((key_rows, HEAD_SIZE), lambda g: (0, g))
    small = pl.BlockSpec((GROUP, rows), lambda g: (g, 0))
    out_specs = [
        pl.BlockSpec((key_rows, GROUP * rows), lambda g: (0, g)),
        pl.BlockSpec((2, key_rows, HEAD_SIZE), lambda g: (0, 0, g)),
    ]
    out_shape = [
        jax.ShapeDtypeStruct((key_rows, QUERY_HEADS * rows), jnp.bfloat16),
        jax.ShapeDtypeStruct(
            (2, key_rows, KEY_VALUE_HEADS * HEAD_SIZE), jnp.float32 if first else jnp.bfloat16
        ),
    ]
    if first:
        out_specs += [small, small]
        out_shape += [jax.ShapeDtypeStruct((QUERY_HEADS, rows), jnp.float32)] * 2
    flops = 8 * rows * key_rows * HEAD_SIZE * QUERY_HEADS
    return pl.pallas_call(
        functools.partial(block_kernel, first, ctx_count, step),
        grid=(KEY_VALUE_HEADS,),
        in_specs=[
            pl.BlockSpec(memory_space=pltpu.SMEM),
            wide,
            wide,
            narrow,
            narrow,
            pl.BlockSpec(lse.shape, lambda g: (0, 0)) if first else small,
            wide if first else small,
        ],
        out_specs=out_specs,
        out_shape=out_shape,
        compiler_params=pltpu.CompilerParams(vmem_limit_bytes=VMEM_LIMIT),
        cost_estimate=pl.CostEstimate(
            flops=flops, bytes_accessed=4 * 2**20, transcendentals=rows * key_rows * QUERY_HEADS
        ),
        name="own_keys" if first else "visiting_keys",
    )(lengths, queries, output_gradient, keys, values, lse, delta)


def query_kernel(count, *refs):
    ds_refs, k_refs, out_ref = refs[:count], refs[count : 2 * count], refs[2 * count]
    rows = out_ref.shape[0]
    keys = jnp.concatenate([k[...] for k in k_refs], axis=0)
    for h in range(GROUP):
        scores = jnp.concatenate([d[:, h * rows : (h + 1) * rows] for d in ds_refs], axis=0)
        out_ref[:, h * HEAD_SIZE : (h + 1) * HEAD_SIZE] = (dot(scores, keys, TN) * SCALE).astype(
            out_ref.dtype
        )


def query_call(grad_scores, keys, rows):
    count = len(keys)
    key_rows = keys[0].shape[0]
    return pl.pallas_call(
        functools.partial(query_kernel, count),
        grid=(KEY_VALUE_HEADS,),
        in_specs=[pl.BlockSpec((key_rows, GROUP * rows), lambda g: (0, g))] * count
        + [pl.BlockSpec((key_rows, HEAD_SIZE), lambda g: (0, g))] * count,
        out_specs=pl.BlockSpec((rows, GROUP * HEAD_SIZE), lambda g: (0, g)),
        out_shape=jax.ShapeDtypeStruct((rows, QUERY_HEADS * HEAD_SIZE), jnp.bfloat16),
        compiler_params=pltpu.CompilerParams(vmem_limit_bytes=VMEM_LIMIT),
        cost_estimate=pl.CostEstimate(
            flops=2 * rows * key_rows * count * HEAD_SIZE * QUERY_HEADS,
            bytes_accessed=3 * 2**20,
            transcendentals=0,
        ),
        name="query_gradient",
    )(*grad_scores, *keys)


def weight_kernel(count, place_ref, *refs):
    n_refs, g_refs, out_ref = refs[:count], refs[count : 2 * count], refs[2 * count]
    half = g_refs[0].shape[2]
    tokens = jnp.concatenate([n[...] for n in n_refs], axis=0)
    for j in range(2):
        grads = jnp.concatenate([g[j] for g in g_refs], axis=0)
        out_ref[0, :, j * half : (j + 1) * half] = dot(tokens, grads, TN).astype(out_ref.dtype)


def weight_call(place, normed, grads, middle, dtype):
    count = len(normed)
    rows, width = normed[0].shape
    block = width // (middle * CORES)
    columns = 2 * grads[0].shape[2]
    return pl.pallas_call(
        functools.partial(weight_kernel, count),
        grid_spec=pltpu.PrefetchScalarGridSpec(
            num_scalar_prefetch=1,
            grid=(middle,),
            in_specs=[pl.BlockSpec((rows, block), lambda y, place: (0, y * CORES + place[0]))]
            * count
            + [pl.BlockSpec(grads[0].shape, lambda y, place: (0, 0, 0))] * count,
            out_specs=pl.BlockSpec((1, block, columns), lambda y, place: (y, 0, 0)),
        ),
        out_shape=jax.ShapeDtypeStruct((middle, block, columns), dtype),
        compiler_params=pltpu.CompilerParams(vmem_limit_bytes=VMEM_LIMIT),
        cost_estimate=pl.CostEstimate(
            flops=2 * rows * count * middle * block * columns,
            bytes_accessed=4 * 2**20,
            transcendentals=0,
        ),
        name="weight_partial",
    )(place, *normed, *grads)


def local(
    normed_input,
    queries,
    saved_keys,
    saved_values,
    attention_output,
    saved_log_totals,
    output_gradient,
    document_lengths,
):
    rows = queries.shape[0]
    half = saved_keys.shape[1]
    ctx_count = lax.axis_size("ctx")
    dp_count = lax.axis_size("dp")
    middle = 2
    line = dp_count // (middle * CORES)
    dp_rank = lax.axis_index("dp")
    ctx_rank = lax.axis_index("ctx")
    z_rank = dp_rank // (middle * CORES)
    y_rank = dp_rank // CORES % middle
    core_rank = dp_rank % CORES
    width = normed_input.shape[1]

    def over_ctx(value, steps):
        pairs = [(s, (s + steps) % ctx_count) for s in range(ctx_count)]
        return lax.ppermute(value, "ctx", pairs)

    def over_line(value, steps):
        stride = middle * CORES
        pairs = [(s, (s + steps * stride) % dp_count) for s in range(dp_count)]
        return lax.ppermute(value, "dp", pairs)

    def over_cores(value):
        return lax.ppermute(value, "dp", [(s, s ^ 1) for s in range(dp_count)])

    def over_plane(value, y_steps, x_steps):
        pairs = []
        for d in range(dp_count):
            for x in range(ctx_count):
                y = d // CORES % middle
                to = d + ((y + y_steps) % middle - y) * CORES
                pairs.append((d * ctx_count + x, to * ctx_count + (x + x_steps) % ctx_count))
        return lax.ppermute(value, ("dp", "ctx"), pairs)

    visiting = [
        (over_ctx(saved_keys, step), over_ctx(saved_values, step)) for step in range(1, ctx_count)
    ]

    piece = width // line

    def piece_for(steps):
        return lax.dynamic_slice_in_dim(
            normed_input, (z_rank + steps) % line * piece, piece, axis=1
        )

    line_tokens = [piece_for(0)] + [over_line(piece_for(s), s) for s in range(1, line)]

    grad_scores, own_grads, delta, lse = block_call(
        0,
        ctx_count,
        document_lengths,
        queries,
        output_gradient,
        saved_keys,
        saved_values,
        saved_log_totals,
        attention_output,
    )
    all_scores = [grad_scores]
    returned = []
    for step in range(1, ctx_count):
        keys, values = visiting[step - 1]
        scores, grads = block_call(
            step, ctx_count, document_lengths, queries, output_gradient, keys, values, lse, delta
        )
        all_scores.append(scores)
        returned.append(over_ctx(grads, -step))
    query_gradient = query_call(
        all_scores, [saved_keys] + [pair[0] for pair in visiting], rows
    )
    total = own_grads
    for grads in returned:
        total = total + grads.astype(jnp.float32)
    total = total.astype(jnp.bfloat16)

    line_grads = [total] + [over_line(total, s) for s in range(1, line)]

    theirs = weight_call((1 - core_rank)[None], line_tokens, line_grads, middle, jnp.bfloat16)
    arriving = over_cores(theirs)
    mine = weight_call(core_rank[None], line_tokens, line_grads, middle, jnp.float32)
    summed = (mine + arriving.astype(jnp.float32)).reshape(middle, ctx_count, -1, 2 * half)

    def block_of(y_steps, x_steps):
        y = (y_rank + y_steps) % middle
        x = (ctx_rank + x_steps) % ctx_count
        start = (y, x, 0, 0)
        return lax.dynamic_slice(summed, start, (1, 1) + summed.shape[2:])[0, 0]

    result = block_of(0, 0)
    for y_steps in range(middle):
        for x_steps in range(ctx_count):
            if y_steps or x_steps:
                sent = block_of(y_steps, x_steps).astype(jnp.bfloat16)
                result = result + over_plane(sent, y_steps, x_steps).astype(jnp.float32)
    return query_gradient, result[:, :half], result[:, half:]


def solution(mesh):
    both = P(("dp", "ctx"), None)
    return jax.shard_map(
        local,
        mesh=mesh,
        in_specs=(both,) * 7 + (P("dp", None),),
        out_specs=(both,) * 3,
        check_vma=False,
    )
```

time: 429 us -> 96.1 us (0.22)
  waiting for transfers between devices: 370 us -> 37.8 us
  starting transfers between devices: 3.4 us -> 28.4 us
  Pallas kernels: 0 us -> 15 us
  between operations: 14.3 us -> 0.73 us
  matrix products: 13.5 us -> 0 us
  local copies, waits for them, and re-layouts: 19.7 us -> 10.8 us
    reduce_scatter x1 -> x0, waiting for transfers between devices: 354 us -> none  [local(): lax.psum_scatter(lax.dot_general(normed_input, key_grads_low, (((0,), (0,...]
    ppermute x3 -> x13, starting transfers between devices: 3.36 us -> 28.4 us  [the longest x6 19.8 us: over_line(): return lax.ppermute(value, 'dp', pairs)]
    ppermute x3 -> x13, waiting for transfers between devices: 15.9 us -> 37.8 us  [the longest x6 26.7 us: over_line(): return lax.ppermute(value, 'dp', pairs)]
    pallas_call x0 -> x5, Pallas kernels: none -> 15 us  [the longest x2 7.23 us: block_call(): pl.pallas_call(functools.partial(block_kernel, first, ctx_count, step), g...]
    dot_general x11 -> x0, matrix products: 13.5 us -> none  [the longest x1 8.05 us: local(): lax.dot_general(normed_input, key_grads_low, (((0,), (0,)), ((), ())), pr...]
    reshape x5 -> x0, local copies, waits for them, and re-layouts: 5.27 us -> none  [the longest x1 1.94 us: local(): output_gradient.reshape(token_rows, KEY_VALUE_HEADS, group_count, HEAD_SIZE)]
    unnamed x25 -> x17, local copies, waits for them, and re-layouts: 12.3 us -> 7.74 us
  transfers between devices with their start and end apart: 4 -> 13, of which waited for: 3 -> 6; matrix products, arithmetic and copies ran while one was open for 5% -> 4% of each run, Pallas kernels for 0% -> 9%
where the time goes in v1:
time: 96.1 us; the launch traced here: 95.6 us
  waiting for transfers between devices  37.8 us (39%)
  starting transfers between devices  28.4 us (30%)
  Pallas kernels  15 us (16%)
  local copies, waits for them, and re-layouts  10.8 us (11%)
  other arithmetic  2.97 us (3%)
    ppermute x6, waiting for transfers between devices, over_line(): return lax.ppermute(value, 'dp', pairs)  26.7 us
    ppermute x6, starting transfers between devices, over_line(): return lax.ppermute(value, 'dp', pairs)  19.8 us
    ppermute x3, waiting for transfers between devices, over_plane(): return lax.ppermute(value, ('dp', 'ctx'), pairs)  10.2 us
    unnamed x17, local copies, waits for them, and re-layouts  7.74 us
    pallas_call x2, Pallas kernels, block_call(): pl.pallas_call(functools.partial(block_kernel, first, ctx_count, step), g...  7.23 us
    ppermute x3, starting transfers between devices, over_ctx(): return lax.ppermute(value, 'ctx', pairs)  5.09 us
    pallas_call x2, Pallas kernels, weight_call(): pl.pallas_call(functools.partial(weight_kernel, count), grid_spec=pltpu.P...  5.09 us
    ppermute x3, starting transfers between devices, over_plane(): return lax.ppermute(value, ('dp', 'ctx'), pairs)  3.55 us
  transfers between devices with their start and end apart: 13, of which 6 were waited for; matrix products, arithmetic and copies ran while one was open for 4% of the time, Pallas kernels for 9%

profile of v1, /device:TPU:0, one launch (start us, length us, event | category | flops | bytes accessed | tf_op | source)
XLA Modules:
  0.0 95.6 jit_solution(12792560499195321925)
XLA Ops:
  0.6 3.0 %collective-permute-start.1 = (bf16[128,512]{1,0:T(8,128)(2,1)}, bf16[128,512]{1,0:T(8,128)(2,1)S(1)}, u32[]{:S(2)}, u32[]{:S(2)}) collective-permute-start(bf16[128,512]{1,0:T(8,128)(2,1)} %v_ref.1), channel_id=1, source_target_pairs={{0,1},{1,0},{2,3},{3,2},{4,5},{5,4},{6,7},{7,6},{8,9},{9,8},{10,11... | collective-permute-start | bytes 393224 | tf_op jit(solution)/shard_map/ppermute | solution.py:237
  3.6 0.1 collective-permute-start
  3.7 0.8 copy.11.lse_ref
  4.5 0.0 copy-start
  4.5 1.2 %copy-done = bf16[128,4096]{1,0:T(8,128)(2,1)S(1)} copy-done((bf16[128,4096]{1,0:T(8,128)(2,1)S(1)}, bf16[128,4096]{1,0:T(8,128)(2,1)}, u32[]{:S(2)}) %copy-start) | copy-done | bytes 1048600
  5.8 1.2 %copy-done.1 = bf16[128,4096]{1,0:T(8,128)(2,1)S(1)} copy-done((bf16[128,4096]{1,0:T(8,128)(2,1)S(1)}, bf16[128,4096]{1,0:T(8,128)(2,1)}, u32[]{:S(2)}) %copy-start.1) | copy-done | bytes 1048600
  7.0 1.2 %copy-done.2 = bf16[128,4096]{1,0:T(8,128)(2,1)S(1)} copy-done((bf16[128,4096]{1,0:T(8,128)(2,1)S(1)}, bf16[128,4096]{1,0:T(8,128)(2,1)}, u32[]{:S(2)}) %copy-start.2) | copy-done | bytes 1048600
  8.2 0.9 copy-done.4
  9.1 0.9 copy-done.6
  10.0 0.7 copy-done.7
  10.7 3.9 %own_keys.1 = (bf16[128,4096]{1,0:T(8,128)(2,1)S(1)}, f32[2,128,512]{2,1,0:T(8,128)S(1)}, f32[32,128]{1,0:T(8,128)S(1)}, f32[32,128]{1,0:T(8,128)S(1)}) custom-call(s32[1,4]{1,0:T(1,128)S(1)} %copy-done.7, bf16[128,4096]{1,0:T(8,128)(2,1)S(1)} %copy-done, bf16[128,4096]{1,0:T(8,128)(2,1)S(1)} %copy-done.1, bf16[128,512]{1,0:T(8,128)(2,1)S(1)} %copy-done.4, ...), custom_call_target="tpu_custom_call" | custom-call | flops 536870912 | bytes 4194304 | tf_op jit(solution)/shard_map/own_keys/pallas_call | solution.py:124
  14.6 0.0 copy-start.3
  14.6 0.8 copy-done.3
  15.4 0.0 collective-permute-done.1.v_ref
  15.4 0.0 collective-permute-done.k_ref.refs_3_
  15.4 3.3 %visiting_keys.1 = (bf16[128,4096]{1,0:T(8,128)(2,1)S(1)}, bf16[2,128,512]{2,1,0:T(8,128)(2,1)S(1)}) custom-call(s32[1,4]{1,0:T(1,128)S(1)} %copy-done.7, bf16[128,4096]{1,0:T(8,128)(2,1)S(1)} %copy-done, bf16[128,4096]{1,0:T(8,128)(2,1)S(1)} %copy-done.1, bf16[128,512]{1,0:T(8,128)(2,1)S(1)} %collective-permute-done.k_ref.refs_3_, ...), custom_call_target="tpu_custom_call" | custom-call | flops 536870912 | bytes 4194304 | tf_op jit(solution)/shard_map/visiting_keys/pallas_call | solution.py:124
  18.7 2.0 %collective-permute-start.5 = (bf16[2,128,512]{2,1,0:T(8,128)(2,1)S(1)}, bf16[2,128,512]{2,1,0:T(8,128)(2,1)}, u32[]{:S(2)}, u32[]{:S(2)}) collective-permute-start(bf16[2,128,512]{2,1,0:T(8,128)(2,1)S(1)} %get-tuple-element.14), channel_id=1, source_target_pairs={{0,1},{1,0},{2,3},{3,2},{4,5},{5,4},{6,7},{7,6},{8,9},{9,8},{10,11... | collective-permute-start | bytes 786440 | tf_op jit(solution)/shard_map/ppermute | solution.py:237
  20.7 2.1 %constant_dynamic-slice_fusion = (bf16[128,1024]{1,0:T(8,128)(2,1)S(1)}, bf16[128,1024]{1,0:T(8,128)(2,1)}, bf16[128,1024]{1,0:T(8,128)(2,1)S(1)}, bf16[128,1024]{1,0:T(8,128)(2,1)}) fusion(bf16[128,4096]{1,0:T(8,128)(2,1)} %param.8, s32[]{:T(128)S(6)} %select_n.95, s32[]{:T(128)S(6)} %select_n.91, s32[]{:T(128)S(6)} %select_n.89, s32[]{:T(128)S(6)} %select_n.93), kind=kLoop, calls=%fused_computation.11 | loop fusion | bytes 2097168 | tf_op jit(solution)/shard_map/dynamic_slice | solution.py:263
  22.8 3.6 %collective-permute-start.4 = (bf16[128,1024]{1,0:T(8,128)(2,1)S(1)}, bf16[128,1024]{1,0:T(8,128)(2,1)S(1)}, u32[]{:S(2)}, u32[]{:S(2)}) collective-permute-start(bf16[128,1024]{1,0:T(8,128)(2,1)S(1)} %get-tuple-element.18), channel_id=1, source_target_pairs={{0,24},{2,26},{4,28},{6,30},{8,0},{10,2},{12,4},{14,6},{16,8},{18,... | collective-permute-start | bytes 786440 | tf_op jit(solution)/shard_map/ppermute | solution.py:242
  26.4 0.0 collective-permute-start.2
  26.4 1.0 %collective-permute-start.3 = (bf16[128,1024]{1,0:T(8,128)(2,1)}, bf16[128,1024]{1,0:T(8,128)(2,1)S(1)}, u32[]{:S(2)}, u32[]{:S(2)}) collective-permute-start(bf16[128,1024]{1,0:T(8,128)(2,1)} %get-tuple-element.21), channel_id=1, source_target_pairs={{0,16},{2,18},{4,20},{6,22},{8,24},{10,26},{12,28},{14,30},{16,0},... | collective-permute-start | bytes 786440 | tf_op jit(solution)/shard_map/ppermute | solution.py:242
  27.4 0.0 collective-permute-done.5
  27.4 1.2 %add_convert_fusion.refs_4_ = bf16[2,128,512]{2,1,0:T(8,128)(2,1)S(1)} fusion(f32[2,128,512]{2,1,0:T(8,128)} %copy-done.3, bf16[2,128,512]{2,1,0:T(8,128)(2,1)} %collective-permute-done.5), kind=kLoop, calls=%fused_computation.7 | loop fusion | flops 393216 | bytes 1048576 | tf_op jit(solution)/shard_map/convert_element_type | solution.py:295
  28.6 3.1 %collective-permute-start.8 = (bf16[2,128,512]{2,1,0:T(8,128)(2,1)S(1)}, bf16[2,128,512]{2,1,0:T(8,128)(2,1)}, u32[]{:S(2)}, u32[]{:S(2)}) collective-permute-start(bf16[2,128,512]{2,1,0:T(8,128)(2,1)S(1)} %add_convert_fusion.refs_4_), channel_id=1, source_target_pairs={{0,24},{2,26},{4,28},{6,30},{8,0},{10,2},{12,4},{14,6},{16,8},{18,... | collective-permute-start | bytes 786440 | tf_op jit(solution)/shard_map/ppermute | solution.py:242
  31.7 1.8 %collective-permute-start.7 = (bf16[2,128,512]{2,1,0:T(8,128)(2,1)S(1)}, bf16[2,128,512]{2,1,0:T(8,128)(2,1)}, u32[]{:S(2)}, u32[]{:S(2)}) collective-permute-start(bf16[2,128,512]{2,1,0:T(8,128)(2,1)S(1)} %add_convert_fusion.refs_4_), channel_id=1, source_target_pairs={{0,16},{2,18},{4,20},{6,22},{8,24},{10,26},{12,28},{14,30},{16,0},... | collective-permute-start | bytes 786440 | tf_op jit(solution)/shard_map/ppermute | solution.py:242
  33.5 0.0 collective-permute-done.4.refs_3_
  33.5 10.3 %collective-permute-start.6 = (bf16[2,128,512]{2,1,0:T(8,128)(2,1)S(1)}, bf16[2,128,512]{2,1,0:T(8,128)(2,1)}, u32[]{:S(2)}, u32[]{:S(2)}) collective-permute-start(bf16[2,128,512]{2,1,0:T(8,128)(2,1)S(1)} %add_convert_fusion.refs_4_), channel_id=1, source_target_pairs={{0,8},{2,10},{4,12},{6,14},{8,16},{10,18},{12,20},{14,22},{16,24},... | collective-permute-start | bytes 786440 | tf_op jit(solution)/shard_map/ppermute | solution.py:242
  43.8 0.0 collective-permute-done.2.refs_1_
  43.8 17.4 %collective-permute-done.3.refs_2_ = bf16[128,1024]{1,0:T(8,128)(2,1)S(1)} collective-permute-done((bf16[128,1024]{1,0:T(8,128)(2,1)}, bf16[128,1024]{1,0:T(8,128)(2,1)S(1)}, u32[]{:S(2)}, u32[]{:S(2)}) %collective-permute-start.3) | collective-permute-done | bytes 262176 | tf_op jit(solution)/shard_map/ppermute | solution.py:242
  61.1 0.0 collective-permute-done.8.refs_7_
  61.1 9.3 %collective-permute-done.7.refs_6_ = bf16[2,128,512]{2,1,0:T(8,128)(2,1)} collective-permute-done((bf16[2,128,512]{2,1,0:T(8,128)(2,1)S(1)}, bf16[2,128,512]{2,1,0:T(8,128)(2,1)}, u32[]{:S(2)}, u32[]{:S(2)}) %collective-permute-start.7) | collective-permute-done | bytes 262176 | tf_op jit(solution)/shard_map/ppermute | solution.py:242
  70.5 0.0 collective-permute-done.6.refs_5_
  70.5 2.9 %weight_partial.3 = bf16[2,256,1024]{2,1,0:T(8,128)(2,1)} custom-call(s32[1]{0:T(128)} %bitcast.1.place_ref, bf16[128,1024]{1,0:T(8,128)(2,1)S(1)} %get-tuple-element.20.refs_0_, bf16[128,1024]{1,0:T(8,128)(2,1)S(1)} %collective-permute-done.2.refs_1_, bf16[128,1024]{1,0:T(8,128)(2,1)S(1)} %collective-permute-done.3.refs_2_, ...), custom_call_target="tpu_custom_call" | custom-call | flops 536870912 | bytes 4194304 | tf_op jit(solution)/shard_map/weight_partial/pallas_call | solution.py:191
  73.4 0.0 collective-permute-start.9
  73.4 2.1 %weight_partial.2 = f32[2,256,1024]{2,1,0:T(8,128)S(1)} custom-call(s32[1]{0:T(128)} %bitcast.place_ref, bf16[128,1024]{1,0:T(8,128)(2,1)S(1)} %get-tuple-element.20.refs_0_, bf16[128,1024]{1,0:T(8,128)(2,1)S(1)} %collective-permute-done.2.refs_1_, bf16[128,1024]{1,0:T(8,128)(2,1)S(1)} %collective-permute-done.3.refs_2_, ...), custom_call_target="tpu_custom_call" | custom-call | flops 536870912 | bytes 4194304 | tf_op jit(solution)/shard_map/weight_partial/pallas_call | solution.py:191
  75.6 0.0 copy-start.5
  75.6 0.8 collective-permute-done.9
  76.4 1.7 %convert_add_fusion = f32[2,256,1024]{2,1,0:T(8,128)S(1)} fusion(f32[2,256,1024]{2,1,0:T(8,128)S(1)} %weight_partial.2, bf16[2,256,1024]{2,1,0:T(8,128)(2,1)} %collective-permute-done.9), kind=kLoop, calls=%fused_computation | loop fusion | flops 1048576 | bytes 5242880 | tf_op jit(solution)/shard_map/add | solution.py:302
  78.1 0.1 fusion.2
  78.2 0.6 collective-permute-start.10
  78.8 2.5 %collective-permute-start.12 = (bf16[128,1024]{1,0:T(8,128)(2,1)S(1)}, bf16[128,1024]{1,0:T(8,128)(2,1)S(1)}, u32[]{:S(2)}, u32[]{:S(2)}) collective-permute-start(bf16[128,1024]{1,0:T(8,128)(2,1)S(1)} %get-tuple-element.16), channel_id=1, source_target_pairs={{0,5},{1,4},{2,7},{3,6},{4,1},{5,0},{6,3},{7,2},{8,13},{9,12},{10,... | collective-permute-start | bytes 786440 | tf_op jit(solution)/shard_map/ppermute | solution.py:254
  81.3 0.5 collective-permute-start.11
  81.8 2.7 %query_gradient.1 = bf16[128,4096]{1,0:T(8,128)(2,1)} custom-call(bf16[128,4096]{1,0:T(8,128)(2,1)S(1)} %get-tuple-element.9.refs_0_, bf16[128,4096]{1,0:T(8,128)(2,1)S(1)} %get-tuple-element.12.refs_1_, bf16[128,512]{1,0:T(8,128)(2,1)S(1)} %copy-done.5, bf16[128,512]{1,0:T(8,128)(2,1)S(1)} %collective-permute-done.k_ref.refs_3_), custom_call_target="tpu_custom_call" | custom-call | flops 268435456 | bytes 3145728 | tf_op jit(solution)/shard_map/query_gradient/pallas_call | solution.py:160
  84.4 3.0 %collective-permute-done.10 = bf16[128,1024]{1,0:T(8,128)(2,1)S(1)} collective-permute-done((bf16[128,1024]{1,0:T(8,128)(2,1)S(1)}, bf16[128,1024]{1,0:T(8,128)(2,1)S(1)}, u32[]{:S(2)}, u32[]{:S(2)}) %collective-permute-start.10) | collective-permute-done | bytes 262176 | tf_op jit(solution)/shard_map/ppermute | solution.py:254
  87.4 5.9 %collective-permute-done.12 = bf16[128,1024]{1,0:T(8,128)(2,1)S(1)} collective-permute-done((bf16[128,1024]{1,0:T(8,128)(2,1)S(1)}, bf16[128,1024]{1,0:T(8,128)(2,1)S(1)}, u32[]{:S(2)}, u32[]{:S(2)}) %collective-permute-start.12) | collective-permute-done | bytes 262176 | tf_op jit(solution)/shard_map/ppermute | solution.py:254
  93.3 1.4 %collective-permute-done.11 = bf16[128,1024]{1,0:T(8,128)(2,1)S(1)} collective-permute-done((bf16[128,1024]{1,0:T(8,128)(2,1)S(1)}, bf16[128,1024]{1,0:T(8,128)(2,1)S(1)}, u32[]{:S(2)}, u32[]{:S(2)}) %collective-permute-start.11) | collective-permute-done | bytes 262176 | tf_op jit(solution)/shard_map/ppermute | solution.py:254
  94.7 0.1 fusion.1
  94.8 0.8 fusion.5
  (6 shorter events, 0.0 us)
Async XLA Ops:
  0.6 14.8 %collective-permute-start.1 = (bf16[128,512]{1,0:T(8,128)(2,1)}, bf16[128,512]{1,0:T(8,128)(2,1)S(1)}, u32[]{:S(2)}, u32[]{:S(2)}) collective-permute-start(bf16[128,512]{1,0:T(8,128)(2,1)} %v_ref.1), channel_id=1, source_target_pairs={{0,1},{1,0},{2,3},{3,2},{4,5},{5,4},{6,7},{7,6},{8,9},{9,8},{10,11... | collective-permute-start | bytes 393224 | tf_op jit(solution)/shard_map/ppermute | solution.py:237
  3.6 11.8 %collective-permute-start = (bf16[128,512]{1,0:T(8,128)(2,1)}, bf16[128,512]{1,0:T(8,128)(2,1)S(1)}, u32[]{:S(2)}, u32[]{:S(2)}) collective-permute-start(bf16[128,512]{1,0:T(8,128)(2,1)} %refs_2_.1), channel_id=1, source_target_pairs={{0,1},{1,0},{2,3},{3,2},{4,5},{5,4},{6,7},{7,6},{8,9},{9,8},{10,11... | collective-permute-start | bytes 393224 | tf_op jit(solution)/shard_map/ppermute | solution.py:237
  4.5 1.2 %copy-start = (bf16[128,4096]{1,0:T(8,128)(2,1)S(1)}, bf16[128,4096]{1,0:T(8,128)(2,1)}, u32[]{:S(2)}) copy-start(bf16[128,4096]{1,0:T(8,128)(2,1)} %q_ref.3) | copy-start | bytes 3145732
  5.8 1.2 %copy-start.1 = (bf16[128,4096]{1,0:T(8,128)(2,1)S(1)}, bf16[128,4096]{1,0:T(8,128)(2,1)}, u32[]{:S(2)}) copy-start(bf16[128,4096]{1,0:T(8,128)(2,1)} %do_ref.3) | copy-start | bytes 3145732
  7.0 1.2 %copy-start.2 = (bf16[128,4096]{1,0:T(8,128)(2,1)S(1)}, bf16[128,4096]{1,0:T(8,128)(2,1)}, u32[]{:S(2)}) copy-start(bf16[128,4096]{1,0:T(8,128)(2,1)} %delta_in.1) | copy-start | bytes 3145732
  8.2 0.9 copy-start.4
  9.1 0.9 copy-start.6
  10.0 0.7 copy-start.7
  14.6 0.8 copy-start.3
  18.7 8.7 %collective-permute-start.5 = (bf16[2,128,512]{2,1,0:T(8,128)(2,1)S(1)}, bf16[2,128,512]{2,1,0:T(8,128)(2,1)}, u32[]{:S(2)}, u32[]{:S(2)}) collective-permute-start(bf16[2,128,512]{2,1,0:T(8,128)(2,1)S(1)} %get-tuple-element.14), channel_id=1, source_target_pairs={{0,1},{1,0},{2,3},{3,2},{4,5},{5,4},{6,7},{7,6},{8,9},{9,8},{10,11... | collective-permute-start | bytes 786440 | tf_op jit(solution)/shard_map/ppermute | solution.py:237
  22.8 10.7 %collective-permute-start.4 = (bf16[128,1024]{1,0:T(8,128)(2,1)S(1)}, bf16[128,1024]{1,0:T(8,128)(2,1)S(1)}, u32[]{:S(2)}, u32[]{:S(2)}) collective-permute-start(bf16[128,1024]{1,0:T(8,128)(2,1)S(1)} %get-tuple-element.18), channel_id=1, source_target_pairs={{0,24},{2,26},{4,28},{6,30},{8,0},{10,2},{12,4},{14,6},{16,8},{18,... | collective-permute-start | bytes 786440 | tf_op jit(solution)/shard_map/ppermute | solution.py:242
  26.4 17.4 %collective-permute-start.2 = (bf16[128,1024]{1,0:T(8,128)(2,1)}, bf16[128,1024]{1,0:T(8,128)(2,1)S(1)}, u32[]{:S(2)}, u32[]{:S(2)}) collective-permute-start(bf16[128,1024]{1,0:T(8,128)(2,1)} %get-tuple-element.19), channel_id=1, source_target_pairs={{0,8},{2,10},{4,12},{6,14},{8,16},{10,18},{12,20},{14,22},{16,24},... | collective-permute-start | bytes 786440 | tf_op jit(solution)/shard_map/ppermute | solution.py:242
  26.4 34.7 %collective-permute-start.3 = (bf16[128,1024]{1,0:T(8,128)(2,1)}, bf16[128,1024]{1,0:T(8,128)(2,1)S(1)}, u32[]{:S(2)}, u32[]{:S(2)}) collective-permute-start(bf16[128,1024]{1,0:T(8,128)(2,1)} %get-tuple-element.21), channel_id=1, source_target_pairs={{0,16},{2,18},{4,20},{6,22},{8,24},{10,26},{12,28},{14,30},{16,0},... | collective-permute-start | bytes 786440 | tf_op jit(solution)/shard_map/ppermute | solution.py:242
  28.6 32.5 %collective-permute-start.8 = (bf16[2,128,512]{2,1,0:T(8,128)(2,1)S(1)}, bf16[2,128,512]{2,1,0:T(8,128)(2,1)}, u32[]{:S(2)}, u32[]{:S(2)}) collective-permute-start(bf16[2,128,512]{2,1,0:T(8,128)(2,1)S(1)} %add_convert_fusion.refs_4_), channel_id=1, source_target_pairs={{0,24},{2,26},{4,28},{6,30},{8,0},{10,2},{12,4},{14,6},{16,8},{18,... | collective-permute-start | bytes 786440 | tf_op jit(solution)/shard_map/ppermute | solution.py:242
  31.7 38.8 %collective-permute-start.7 = (bf16[2,128,512]{2,1,0:T(8,128)(2,1)S(1)}, bf16[2,128,512]{2,1,0:T(8,128)(2,1)}, u32[]{:S(2)}, u32[]{:S(2)}) collective-permute-start(bf16[2,128,512]{2,1,0:T(8,128)(2,1)S(1)} %add_convert_fusion.refs_4_), channel_id=1, source_target_pairs={{0,16},{2,18},{4,20},{6,22},{8,24},{10,26},{12,28},{14,30},{16,0},... | collective-permute-start | bytes 786440 | tf_op jit(solution)/shard_map/ppermute | solution.py:242
  33.5 37.0 %collective-permute-start.6 = (bf16[2,128,512]{2,1,0:T(8,128)(2,1)S(1)}, bf16[2,128,512]{2,1,0:T(8,128)(2,1)}, u32[]{:S(2)}, u32[]{:S(2)}) collective-permute-start(bf16[2,128,512]{2,1,0:T(8,128)(2,1)S(1)} %add_convert_fusion.refs_4_), channel_id=1, source_target_pairs={{0,8},{2,10},{4,12},{6,14},{8,16},{10,18},{12,20},{14,22},{16,24},... | collective-permute-start | bytes 786440 | tf_op jit(solution)/shard_map/ppermute | solution.py:242
  73.4 3.0 %collective-permute-start.9 = (bf16[2,256,1024]{2,1,0:T(8,128)(2,1)}, bf16[2,256,1024]{2,1,0:T(8,128)(2,1)}, u32[]{:S(2)}, u32[]{:S(2)}) collective-permute-start(bf16[2,256,1024]{2,1,0:T(8,128)(2,1)} %weight_partial.3), channel_id=1, source_target_pairs={{0,2},{2,0},{4,6},{6,4},{8,10},{10,8},{12,14},{14,12},{16,18},{18,... | collective-permute-start | bytes 3145736 | tf_op jit(solution)/shard_map/ppermute | solution.py:245
  75.6 6.2 %copy-start.5 = (bf16[128,512]{1,0:T(8,128)(2,1)S(1)}, bf16[128,512]{1,0:T(8,128)(2,1)}, u32[]{:S(2)}) copy-start(bf16[128,512]{1,0:T(8,128)(2,1)} %refs_2_.1) | copy-start | bytes 393220
  78.2 9.2 %collective-permute-start.10 = (bf16[128,1024]{1,0:T(8,128)(2,1)S(1)}, bf16[128,1024]{1,0:T(8,128)(2,1)S(1)}, u32[]{:S(2)}, u32[]{:S(2)}) collective-permute-start(bf16[128,1024]{1,0:T(8,128)(2,1)S(1)} %get-tuple-element.15), channel_id=1, source_target_pairs={{0,1},{1,0},{2,3},{3,2},{4,5},{5,4},{6,7},{7,6},{8,9},{9,8},{10,11... | collective-permute-start | bytes 786440 | tf_op jit(solution)/shard_map/ppermute | solution.py:254
  78.8 14.5 %collective-permute-start.12 = (bf16[128,1024]{1,0:T(8,128)(2,1)S(1)}, bf16[128,1024]{1,0:T(8,128)(2,1)S(1)}, u32[]{:S(2)}, u32[]{:S(2)}) collective-permute-start(bf16[128,1024]{1,0:T(8,128)(2,1)S(1)} %get-tuple-element.16), channel_id=1, source_target_pairs={{0,5},{1,4},{2,7},{3,6},{4,1},{5,0},{6,3},{7,2},{8,13},{9,12},{10,... | collective-permute-start | bytes 786440 | tf_op jit(solution)/shard_map/ppermute | solution.py:254
  81.3 13.4 %collective-permute-start.11 = (bf16[128,1024]{1,0:T(8,128)(2,1)S(1)}, bf16[128,1024]{1,0:T(8,128)(2,1)S(1)}, u32[]{:S(2)}, u32[]{:S(2)}) collective-permute-start(bf16[128,1024]{1,0:T(8,128)(2,1)S(1)} %get-tuple-element.17), channel_id=1, source_target_pairs={{0,4},{1,5},{2,6},{3,7},{4,0},{5,1},{6,2},{7,3},{8,12},{9,13},{10,... | collective-permute-start | bytes 786440 | tf_op jit(solution)/shard_map/ppermute | solution.py:254

commit v2 on v1

v2 whole, which is shorter than its diff:
```python
import functools
import math

import jax
import jax.numpy as jnp
from jax import lax
from jax.experimental import pallas as pl
from jax.experimental.pallas import tpu as pltpu
from jax.sharding import PartitionSpec as P

QUERY_HEADS = 32
KEY_VALUE_HEADS = 4
HEAD_SIZE = 128
GROUP = QUERY_HEADS // KEY_VALUE_HEADS
SCALE = 1.0 / math.sqrt(HEAD_SIZE)
CORES = 2
MIDDLE = 2
PARTS = 1
PART_HEADS = KEY_VALUE_HEADS // PARTS
PART_WIDTH = PART_HEADS * HEAD_SIZE
PARAMS = pltpu.CompilerParams(vmem_limit_bytes=32 * 2**20)
STREAMING = pltpu.CompilerParams(vmem_limit_bytes=60 * 2**20)
COST = pl.CostEstimate(flops=1024, bytes_accessed=1024, transcendentals=0)
WHOLE = pl.BlockSpec(memory_space=pltpu.VMEM)
FAR = pl.BlockSpec(memory_space=pltpu.HBM)
SCALARS = pl.BlockSpec(memory_space=pltpu.SMEM)

NT = (((1,), (1,)), ((), ()))
TN = (((0,), (0,)), ((), ()))
NN = (((1,), (0,)), ((), ()))


def dot(a, b, dims):
    return lax.dot_general(a, b, dims, preferred_element_type=jnp.float32)


def shape(dims, dtype):
    return jax.ShapeDtypeStruct(dims, dtype)


def rows_of_heads(block):
    return jnp.concatenate(
        [block[:, h * HEAD_SIZE : (h + 1) * HEAD_SIZE] for h in range(GROUP)], axis=0
    )


def allowed_mask(lengths_ref, ctx_count, rank, owner, keys, rows):
    key_pos = lax.broadcasted_iota(jnp.int32, (keys, rows), 0) * ctx_count + owner
    query_pos = lax.broadcasted_iota(jnp.int32, (keys, rows), 1) * ctx_count + rank
    allowed = key_pos <= query_pos
    end = jnp.int32(0)
    for j in range(lengths_ref.shape[1]):
        end = end + lengths_ref[0, j]
        allowed = allowed & ((end <= key_pos) == (end <= query_pos))
    return allowed


def block_kernel(
    first, part, ctx_count, step, lengths_ref, q_hbm, do_hbm, k_in, v_in, lse_ref, delta_in, *refs
):
    refs = list(refs)
    if first:
        heads = range(KEY_VALUE_HEADS)
        ds_ref, grad_ref, low_ref, delta_ref = refs[:4]
        q_buf, do_buf, other_buf, sems, k_ref, v_ref, small_sems = refs[4:]
    else:
        heads = range(part * PART_HEADS, (part + 1) * PART_HEADS)
        q_buf, do_buf, sems = refs[-3:]
        ds_ref, grad_ref = refs[-5:-3]
        k_ref, v_ref = k_in, v_in
    width = GROUP * HEAD_SIZE
    sources = [(q_hbm, q_buf), (do_hbm, do_buf)]
    if first:
        sources.append((delta_in, other_buf))
    small = []
    if first:
        small = [
            pltpu.make_async_copy(k_in, k_ref, small_sems.at[0]),
            pltpu.make_async_copy(v_in, v_ref, small_sems.at[1]),
        ]
        for copy in small:
            copy.start()
    copies = []
    for at, g in enumerate(heads):
        copies.append(
            [
                pltpu.make_async_copy(
                    source.at[:, g * width : (g + 1) * width], target.at[at], sems.at[index, at]
                )
                for index, (source, target) in enumerate(sources)
            ]
        )
        for copy in copies[-1]:
            copy.start()
    rank = lax.axis_index("ctx")
    owner = lax.rem(rank + ctx_count - step, ctx_count)
    rows = q_hbm.shape[0]
    keys = k_in.shape[0]
    allowed = allowed_mask(lengths_ref, ctx_count, rank, owner, keys, rows)
    for copy in small:
        copy.wait()
    for at, g in enumerate(heads):
        for copy in copies[at]:
            copy.wait()
        q = rows_of_heads(q_buf[at])
        do = rows_of_heads(do_buf[at])
        group = slice(g * GROUP, (g + 1) * GROUP)
        if first:
            product = do_buf[at].astype(jnp.float32) * other_buf[at].astype(jnp.float32)
            high = product.astype(jnp.bfloat16)
            low = (product - high.astype(jnp.float32)).astype(jnp.bfloat16)
            pick = (
                lax.broadcasted_iota(jnp.int32, (GROUP, width), 1) // HEAD_SIZE
                == lax.broadcasted_iota(jnp.int32, (GROUP, width), 0)
            ).astype(jnp.bfloat16)
            delta = dot(pick, high, NT) + dot(pick, low, NT)
            delta_ref[group, :] = delta
        else:
            delta = delta_in[group, :]
        lse = lse_ref[group, :]
        columns = slice(g * HEAD_SIZE, (g + 1) * HEAD_SIZE)
        scores = dot(k_ref[:, columns], q, NT)
        grad_probs = dot(v_ref[:, columns], do, NT)
        probs_low = []
        grad_scores = []
        for h in range(GROUP):
            cut = slice(h * rows, (h + 1) * rows)
            probs = jnp.where(allowed, jnp.exp(scores[:, cut] * SCALE - lse[h : h + 1, :]), 0.0)
            grad_scores.append(
                (probs * (grad_probs[:, cut] - delta[h : h + 1, :])).astype(jnp.bfloat16)
            )
            probs_low.append(probs.astype(jnp.bfloat16))
        probs_low = jnp.concatenate(probs_low, axis=1)
        grad_scores = jnp.concatenate(grad_scores, axis=1)
        ds_ref[:, at * GROUP * rows : (at + 1) * GROUP * rows] = grad_scores
        key_grad = dot(grad_scores, q, NN) * SCALE
        value_grad = dot(probs_low, do, NN)
        columns = slice(at * HEAD_SIZE, (at + 1) * HEAD_SIZE)
        grad_ref[0, :, columns] = key_grad.astype(grad_ref.dtype)
        grad_ref[1, :, columns] = value_grad.astype(grad_ref.dtype)
        if first:
            low_ref[0, :, columns] = key_grad.astype(low_ref.dtype)
            low_ref[1, :, columns] = value_grad.astype(low_ref.dtype)


def own_call(ctx_count, lengths, queries, output_gradient, keys, values, lse, attention_output):
    rows = queries.shape[0]
    key_rows, half = keys.shape
    buffer = pltpu.VMEM((KEY_VALUE_HEADS, rows, GROUP * HEAD_SIZE), jnp.bfloat16)
    small = pltpu.VMEM((key_rows, half), jnp.bfloat16)
    return pl.pallas_call(
        functools.partial(block_kernel, True, 0, ctx_count, 0),
        in_specs=[SCALARS, FAR, FAR, FAR, FAR, WHOLE, FAR],
        out_specs=[WHOLE] * 4,
        out_shape=[
            shape((key_rows, QUERY_HEADS * rows), jnp.bfloat16),
            shape((2, key_rows, half), jnp.float32),
            shape((2, key_rows, half), jnp.bfloat16),
            shape((QUERY_HEADS, rows), jnp.float32),
        ],
        scratch_shapes=[
            buffer,
            buffer,
            buffer,
            pltpu.SemaphoreType.DMA((3, KEY_VALUE_HEADS)),
            small,
            small,
            pltpu.SemaphoreType.DMA((2,)),
        ],
        compiler_params=pltpu.CompilerParams(vmem_limit_bytes=62 * 2**20),
        cost_estimate=COST,
        name="own_keys",
    )(lengths, queries, output_gradient, keys, values, lse, attention_output)


def visiting_call(
    part, step, ctx_count, lengths, queries, output_gradient, keys, values, lse, delta
):
    rows = queries.shape[0]
    key_rows = keys.shape[0]
    buffer = pltpu.VMEM((PART_HEADS, rows, GROUP * HEAD_SIZE), jnp.bfloat16)
    return pl.pallas_call(
        functools.partial(block_kernel, False, part, ctx_count, step),
        in_specs=[SCALARS, FAR, FAR, WHOLE, WHOLE, WHOLE, WHOLE],
        out_specs=[WHOLE] * 2,
        out_shape=[
            shape((key_rows, PART_HEADS * GROUP * rows), jnp.bfloat16),
            shape((2, key_rows, PART_WIDTH), jnp.bfloat16),
        ],
        scratch_shapes=[buffer, buffer, pltpu.SemaphoreType.DMA((2, PART_HEADS))],
        compiler_params=pltpu.CompilerParams(vmem_limit_bytes=52 * 2**20),
        cost_estimate=COST,
        name="visiting_keys",
    )(lengths, queries, output_gradient, keys, values, lse, delta)


def query_kernel(steps, *refs):
    own_ref, k_refs, out_ref = refs[0], refs[-2 - steps : -1], refs[-1]
    visiting = refs[1 : 1 + steps * PARTS]
    rows = out_ref.shape[0]
    for g in range(KEY_VALUE_HEADS):
        columns = slice(g * HEAD_SIZE, (g + 1) * HEAD_SIZE)
        keys = jnp.concatenate([k[:, columns] for k in k_refs], axis=0)
        part, at = divmod(g, PART_HEADS)
        for h in range(GROUP):
            head = g * GROUP + h
            scores = [own_ref[:, head * rows : (head + 1) * rows]]
            for ref in visiting[part * steps : (part + 1) * steps]:
                inner = at * GROUP + h
                scores.append(ref[:, inner * rows : (inner + 1) * rows])
            out_ref[:, head * HEAD_SIZE : (head + 1) * HEAD_SIZE] = (
                dot(jnp.concatenate(scores, axis=0), keys, TN) * SCALE
            ).astype(out_ref.dtype)


def query_call(own_scores, visiting_scores, keys, rows):
    steps = len(keys) - 1
    operands = [own_scores] + visiting_scores + keys
    return pl.pallas_call(
        functools.partial(query_kernel, steps),
        in_specs=[WHOLE] * len(operands),
        out_specs=WHOLE,
        out_shape=shape((rows, QUERY_HEADS * HEAD_SIZE), jnp.bfloat16),
        compiler_params=PARAMS,
        cost_estimate=COST,
        name="query_gradient",
    )(*operands)


def plane_place(ctx_count):
    return lax.rem(lax.div(lax.axis_index("dp"), CORES), MIDDLE), lax.axis_index("ctx")


def pieces_kernel(line, ctx_count, in_hbm, *refs):
    count = MIDDLE * ctx_count
    out_refs, buf, sems = refs[:count], refs[count], refs[count + 1]
    y_rank, x_rank = plane_place(ctx_count)
    block = out_refs[0].shape[0] // (CORES * line)
    chunk = count * CORES * block
    copies = [
        pltpu.make_async_copy(in_hbm.at[:, z * chunk : (z + 1) * chunk], buf.at[z], sems.at[z])
        for z in range(line)
    ]
    for copy in copies:
        copy.start()
    for z in range(line):
        copies[z].wait()
        for index, out_ref in enumerate(out_refs):
            y = lax.rem(y_rank + index // ctx_count, MIDDLE)
            x = lax.rem(x_rank + index % ctx_count, ctx_count)
            for core in range(CORES):
                column = (y * CORES + core) * ctx_count + x
                start = pl.multiple_of(column * block, block)
                row = (core * line + z) * block
                out_ref[row : row + block, :] = buf[z, :, pl.ds(start, block)].T


def pieces_call(normed, line, ctx_count):
    rows, width = normed.shape
    count = MIDDLE * ctx_count
    block = width // (count * CORES * line)
    if block % 128 == 0:
        return pl.pallas_call(
            functools.partial(pieces_kernel, line, ctx_count),
            in_specs=[FAR],
            out_specs=[WHOLE] * count,
            out_shape=[shape((width // count, rows), normed.dtype)] * count,
            scratch_shapes=[
                pltpu.VMEM((line, rows, width // line), normed.dtype),
                pltpu.SemaphoreType.DMA((line,)),
            ],
            compiler_params=STREAMING,
            cost_estimate=COST,
            name="pieces",
        )(normed)
    y_rank, x_rank = plane_place(ctx_count)
    turned = normed.T.reshape(line, MIDDLE, CORES, ctx_count, block, rows)
    pieces = []
    for index in range(count):
        y = (y_rank + index // ctx_count) % MIDDLE
        x = (x_rank + index % ctx_count) % ctx_count
        piece = lax.dynamic_index_in_dim(turned, y, 1, keepdims=False)
        piece = lax.dynamic_index_in_dim(piece, x, 2, keepdims=False)
        pieces.append(piece.transpose(1, 0, 2, 3).reshape(width // count, rows))
    return pieces


def add_kernel(part, own_ref, back_ref, sent_ref, theirs_ref, out_ref):
    cut = slice(part * PART_WIDTH, (part + 1) * PART_WIDTH)
    out_ref[0] = (own_ref[:, :, cut] + back_ref[...].astype(jnp.float32)).astype(out_ref.dtype)
    out_ref[1] = (
        sent_ref[...].astype(jnp.float32) + theirs_ref[:, :, cut].astype(jnp.float32)
    ).astype(out_ref.dtype)


def add_call(part, own, back, sent, theirs):
    return pl.pallas_call(
        functools.partial(add_kernel, part),
        in_specs=[WHOLE] * 4,
        out_specs=WHOLE,
        out_shape=shape((2,) + back.shape, jnp.bfloat16),
        compiler_params=PARAMS,
        cost_estimate=COST,
        name="grads_total",
    )(own, back, sent, theirs)


def weight_kernel(other, count, *refs):
    n_refs, g_refs, out_ref = refs[:count], refs[count:-1], refs[-1]
    height, columns = out_ref.shape
    width = columns // 2
    core = lax.rem(lax.axis_index("dp"), CORES)
    if other:
        core = 1 - core
    start = pl.multiple_of(core * height, height)
    block = height if height < 256 else 256
    grads = [
        jnp.concatenate([g[i, j] for g in g_refs for i in range(g.shape[0])], axis=0)
        for j in range(2)
    ]
    for row in range(0, height, block):
        tokens = jnp.concatenate([n[pl.ds(start + row, block), :] for n in n_refs], axis=1)
        for j in range(2):
            out_ref[row : row + block, j * width : (j + 1) * width] = dot(
                tokens, grads[j], NN
            ).astype(out_ref.dtype)


def weight_call(other, tokens, grads, dtype):
    operands = list(tokens) + list(grads)
    return pl.pallas_call(
        functools.partial(weight_kernel, other, len(tokens)),
        in_specs=[WHOLE] * len(operands),
        out_specs=WHOLE,
        out_shape=shape((tokens[0].shape[0] // CORES, 2 * grads[0].shape[-1]), dtype),
        compiler_params=PARAMS,
        cost_estimate=COST,
        name="weight_other_core" if other else "weight_this_core",
    )(*operands)


def chip_kernel(line, mine_ref, theirs_ref, own_ref, *out_refs):
    block = own_ref.shape[0]
    z_rank = lax.div(lax.axis_index("dp"), CORES * MIDDLE)
    for index, out_ref in enumerate((own_ref,) + out_refs):
        z = lax.rem(z_rank + index, line)
        at = pl.ds(pl.multiple_of(z * block, block), block)
        out_ref[...] = (mine_ref[at, :] + theirs_ref[at, :].astype(jnp.float32)).astype(
            out_ref.dtype
        )


def chip_call(line, mine, theirs):
    height, columns = mine.shape
    block = height // line
    return pl.pallas_call(
        functools.partial(chip_kernel, line),
        in_specs=[WHOLE] * 2,
        out_specs=[WHOLE] * line,
        out_shape=[shape((block, columns), jnp.float32)]
        + [shape((block, columns), jnp.bfloat16)] * (line - 1),
        compiler_params=PARAMS,
        cost_estimate=COST,
        name="chip_total",
    )(mine, theirs)


def final_kernel(line, *refs):
    key_ref, value_ref = refs[-2:]
    for part in range(PARTS):
        pieces = refs[part * line : (part + 1) * line]
        total = pieces[0][...]
        for piece in pieces[1:]:
            total = total + piece[...].astype(jnp.float32)
        at = slice(part * PART_WIDTH, (part + 1) * PART_WIDTH)
        key_ref[:, at] = total[:, :PART_WIDTH]
        value_ref[:, at] = total[:, PART_WIDTH:]


def final_call(line, pieces):
    block = pieces[0].shape[0]
    return pl.pallas_call(
        functools.partial(final_kernel, line),
        in_specs=[WHOLE] * len(pieces),
        out_specs=[WHOLE] * 2,
        out_shape=[shape((block, KEY_VALUE_HEADS * HEAD_SIZE), jnp.float32)] * 2,
        compiler_params=PARAMS,
        cost_estimate=COST,
        name="weight_total",
    )(*pieces)


def local(
    normed_input,
    queries,
    saved_keys,
    saved_values,
    attention_output,
    saved_log_totals,
    output_gradient,
    document_lengths,
):
    rows = queries.shape[0]
    ctx_count = lax.axis_size("ctx")
    dp_count = lax.axis_size("dp")
    line = dp_count // (MIDDLE * CORES)

    def over_ctx(value, steps):
        pairs = [(s, (s + steps) % ctx_count) for s in range(ctx_count)]
        return lax.ppermute(value, "ctx", pairs)

    def over_line(value, steps):
        stride = MIDDLE * CORES
        pairs = [(s, (s + steps * stride) % dp_count) for s in range(dp_count)]
        return lax.ppermute(value, "dp", pairs)

    def over_cores(value):
        return lax.ppermute(value, "dp", [(s, s ^ 1) for s in range(dp_count)])

    def over_plane(value, y_steps, x_steps):
        pairs = []
        for d in range(dp_count):
            for x in range(ctx_count):
                y = d // CORES % MIDDLE
                to = d + ((y + y_steps) % MIDDLE - y) * CORES
                pairs.append((d * ctx_count + x, to * ctx_count + (x + x_steps) % ctx_count))
        return lax.ppermute(value, ("dp", "ctx"), pairs)

    visiting = [
        (over_ctx(saved_keys, step), over_ctx(saved_values, step)) for step in range(1, ctx_count)
    ]
    pieces = pieces_call(normed_input, line, ctx_count)
    lse = saved_log_totals.T
    scores, own, own_low, delta = own_call(
        ctx_count,
        document_lengths,
        queries,
        output_gradient,
        saved_keys,
        saved_values,
        lse,
        attention_output,
    )
    if ctx_count == 2:
        own_theirs = over_ctx(own_low, 1)
    visiting_scores = []
    summands = []
    tokens = None
    for part in range(PARTS):
        sent = []
        for step in range(1, ctx_count):
            keys, values = visiting[step - 1]
            part_scores, grads = visiting_call(
                part,
                step,
                ctx_count,
                document_lengths,
                queries,
                output_gradient,
                keys,
                values,
                lse,
                delta,
            )
            visiting_scores.append(part_scores)
            sent.append(grads)
        back = [over_ctx(grads, -step) for step, grads in enumerate(sent, 1)]
        if tokens is None:
            back, pieces = lax.optimization_barrier((back, pieces))
            tokens = [
                over_plane(piece, index // ctx_count, index % ctx_count) if index else piece
                for index, piece in enumerate(pieces)
            ]
        if ctx_count == 2:
            grads = add_call(part, own, back[0], sent[0], own_theirs)
        else:
            total = own[:, :, part * PART_WIDTH : (part + 1) * PART_WIDTH]
            for value in back:
                total = total + value.astype(jnp.float32)
            total = total.astype(jnp.bfloat16)
            grads = jnp.stack([total] + [over_ctx(total, s) for s in range(1, ctx_count)])
        plane_grads = [grads] + [over_plane(grads, y, 0) for y in range(1, MIDDLE)]
        theirs = weight_call(True, tokens, plane_grads, jnp.bfloat16)
        arriving = over_cores(theirs)
        mine = weight_call(False, tokens, plane_grads, jnp.float32)
        blocks = chip_call(line, mine, arriving)
        summands.append(blocks[0])
        summands += [over_line(blocks[s], s) for s in range(1, line)]
    query_gradient = query_call(
        scores, visiting_scores, [saved_keys] + [pair[0] for pair in visiting], rows
    )
    key_weight_grad, value_weight_grad = final_call(line, summands)
    return query_gradient, key_weight_grad, value_weight_grad


def solution(mesh):
    both = P(("dp", "ctx"), None)
    return jax.shard_map(
        local,
        mesh=mesh,
        in_specs=(both,) * 7 + (P("dp", None),),
        out_specs=(both,) * 3,
        check_vma=False,
    )
```

time: 96.1 us -> 82.8 us (0.86)
  the two profiles are of different devices: /device:TPU:0 before, /device:TPU:9 now
where the time goes in v2:
time: 82.8 us; the launch traced here: 82.5 us
  waiting for transfers between devices  49 us (59%)
  Pallas kernels  17 us (21%)
  starting transfers between devices  14 us (17%)
  local copies, waits for them, and re-layouts  1.74 us (2%)
    ppermute x3, waiting for transfers between devices, over_line(): return lax.ppermute(value, 'dp', pairs)  20.5 us
    ppermute x4, waiting for transfers between devices, over_plane(): return lax.ppermute(value, ('dp', 'ctx'), pairs)  18.6 us
    ppermute x4, waiting for transfers between devices, over_ctx(): return lax.ppermute(value, 'ctx', pairs)  8.3 us
    pallas_call x1, Pallas kernels, own_call(): pl.pallas_call(functools.partial(block_kernel, True, 0, ctx_count, 0), in...  6.59 us
    ppermute x4, starting transfers between devices, over_plane(): return lax.ppermute(value, ('dp', 'ctx'), pairs)  3.95 us
    ppermute x3, starting transfers between devices, over_line(): return lax.ppermute(value, 'dp', pairs)  3.82 us
    pallas_call x1, Pallas kernels, visiting_call(): pl.pallas_call(functools.partial(block_kernel, False, part, ctx_count, st...  3.78 us
    ppermute x1, starting transfers between devices, over_cores(): return lax.ppermute(value, 'dp', [(s, s ^ 1) for s in range(dp_count)])  3.14 us
  transfers between devices with their start and end apart: 12, of which 8 were waited for; matrix products, arithmetic and copies ran while one was open for 0% of the time, Pallas kernels for 14%

profile of v2, /device:TPU:9, one launch (start us, length us, event | category | flops | bytes accessed | tf_op | source)
XLA Modules:
  0.0 82.5 jit_solution(3022754020898359709)
XLA Ops:
  0.6 0.0 copy-start.6
  0.6 0.0 copy-start.4
  0.7 1.3 %collective-permute-start.1 = (bf16[128,512]{1,0:T(8,128)(2,1)}, bf16[128,512]{1,0:T(8,128)(2,1)S(1)}, u32[]{:S(2)}, u32[]{:S(2)}) collective-permute-start(bf16[128,512]{1,0:T(8,128)(2,1)} %v_in.1), channel_id=1, source_target_pairs={{0,1},{1,0},{2,3},{3,2},{4,5},{5,4},{6,7},{7,6},{8,9},{9,8},{10,11... | collective-permute-start | bytes 393224 | tf_op jit(solution)/shard_map/ppermute | solution.py:410
  1.9 0.3 collective-permute-start
  2.2 6.6 %own_keys.1 = (bf16[128,4096]{1,0:T(8,128)(2,1)}, f32[2,128,512]{2,1,0:T(8,128)}, bf16[2,128,512]{2,1,0:T(8,128)(2,1)}, f32[32,128]{1,0:T(8,128)}) custom-call(s32[1,4]{1,0:T(1,128)} %lengths_ref.3, bf16[128,4096]{1,0:T(8,128)(2,1)} %q_hbm.3, bf16[128,4096]{1,0:T(8,128)(2,1)} %do_hbm.3, bf16[128,512]{1,0:T(8,128)(2,1)} %refs_2_.1, bf16[128,512]{1,0:T(8,128)(2,1)} %v_in.1, ...), custom_call_target="tpu_custom_call" | custom-call | flops 1024 | bytes 1024 | tf_op jit(solution)/shard_map/own_keys/pallas_call | solution.py:151
  8.8 0.0 copy-start.2
  8.8 0.0 collective-permute-done.1.v_in
  8.8 0.0 collective-permute-done.k_in.refs_3_
  8.8 0.0 copy-done.6
  8.8 0.0 copy-done.4
  8.8 0.0 copy-start.5
  8.8 0.8 copy-done.5
  9.6 0.0 copy-start.7
  9.6 3.8 %visiting_keys.1 = (bf16[128,4096]{1,0:T(8,128)(2,1)S(1)}, bf16[2,128,512]{2,1,0:T(8,128)(2,1)S(1)}) custom-call(s32[1,4]{1,0:T(1,128)S(1)} %copy-done.6, bf16[128,4096]{1,0:T(8,128)(2,1)} %q_hbm.3, bf16[128,4096]{1,0:T(8,128)(2,1)} %do_hbm.3, bf16[128,512]{1,0:T(8,128)(2,1)S(1)} %collective-permute-done.k_in.refs_3_, ...), custom_call_target="tpu_custom_call" | custom-call | flops 1024 | bytes 1024 | tf_op jit(solution)/shard_map/visiting_keys/pallas_call | solution.py:182
  13.4 1.3 %collective-permute-start.2 = (bf16[2,128,512]{2,1,0:T(8,128)(2,1)S(1)}, bf16[2,128,512]{2,1,0:T(8,128)(2,1)S(1)}, u32[]{:S(2)}, u32[]{:S(2)}) collective-permute-start(bf16[2,128,512]{2,1,0:T(8,128)(2,1)S(1)} %get-tuple-element.27.sent_ref), channel_id=1, source_target_pairs={{0,1},{1,0},{2,3},{3,2},{4,5},{5,4},{6,7},{7,6},{8,9},{9,8},{10,11... | collective-permute-start | bytes 786440 | tf_op jit(solution)/shard_map/ppermute | solution.py:410
  14.7 0.0 copy-done.7
  14.7 0.3 collective-permute-start.6
  14.9 2.4 %pieces.1 = (bf16[1024,128]{1,0:T(8,128)(2,1)}, bf16[1024,128]{1,0:T(8,128)(2,1)}, bf16[1024,128]{1,0:T(8,128)(2,1)}, bf16[1024,128]{1,0:T(8,128)(2,1)}) custom-call(bf16[128,4096]{1,0:T(8,128)(2,1)} %in_hbm.1), custom_call_target="tpu_custom_call" | custom-call | flops 1024 | bytes 1024 | tf_op jit(solution)/shard_map/pieces/pallas_call | solution.py:263
  17.3 2.7 %collective-permute-done.2.back_ref = bf16[2,128,512]{2,1,0:T(8,128)(2,1)S(1)} collective-permute-done((bf16[2,128,512]{2,1,0:T(8,128)(2,1)S(1)}, bf16[2,128,512]{2,1,0:T(8,128)(2,1)S(1)}, u32[]{:S(2)}, u32[]{:S(2)}) %collective-permute-start.2) | collective-permute-done | bytes 262176 | tf_op jit(solution)/shard_map/ppermute | solution.py:410
  20.0 5.6 %collective-permute-done.6.theirs_ref = bf16[2,128,512]{2,1,0:T(8,128)(2,1)S(1)} collective-permute-done((bf16[2,128,512]{2,1,0:T(8,128)(2,1)S(1)}, bf16[2,128,512]{2,1,0:T(8,128)(2,1)S(1)}, u32[]{:S(2)}, u32[]{:S(2)}) %collective-permute-start.6) | collective-permute-done | bytes 262176 | tf_op jit(solution)/shard_map/ppermute | solution.py:410
  25.6 0.0 copy-done.2
  25.6 0.1 grads_total.1.refs_4_
  25.7 1.3 %collective-permute-start.7 = (bf16[2,2,128,512]{3,2,1,0:T(8,128)(2,1)S(1)}, bf16[2,2,128,512]{3,2,1,0:T(8,128)(2,1)S(1)}, u32[]{:S(2)}, u32[]{:S(2)}) collective-permute-start(bf16[2,2,128,512]{3,2,1,0:T(8,128)(2,1)S(1)} %grads_total.1.refs_4_), channel_id=1, source_target_pairs={{0,4},{1,5},{2,6},{3,7},{4,0},{5,1},{6,2},{7,3},{8,12},{9,13},{10,... | collective-permute-start | bytes 1572872 | tf_op jit(solution)/shard_map/ppermute | solution.py:427
  27.0 1.2 %collective-permute-start.3 = (bf16[1024,128]{1,0:T(8,128)(2,1)}, bf16[1024,128]{1,0:T(8,128)(2,1)S(1)}, u32[]{:S(2)}, u32[]{:S(2)}) collective-permute-start(bf16[1024,128]{1,0:T(8,128)(2,1)} %get-tuple-element.33), channel_id=1, source_target_pairs={{0,1},{1,0},{2,3},{3,2},{4,5},{5,4},{6,7},{7,6},{8,9},{9,8},{10,11... | collective-permute-start | bytes 786440 | tf_op jit(solution)/shard_map/ppermute | solution.py:427
  28.3 0.2 collective-permute-start.4
  28.5 1.2 %collective-permute-start.5 = (bf16[1024,128]{1,0:T(8,128)(2,1)}, bf16[1024,128]{1,0:T(8,128)(2,1)S(1)}, u32[]{:S(2)}, u32[]{:S(2)}) collective-permute-start(bf16[1024,128]{1,0:T(8,128)(2,1)} %get-tuple-element.35), channel_id=1, source_target_pairs={{0,5},{1,4},{2,7},{3,6},{4,1},{5,0},{6,3},{7,2},{8,13},{9,12},{10,... | collective-permute-start | bytes 786440 | tf_op jit(solution)/shard_map/ppermute | solution.py:427
  29.7 3.1 %collective-permute-done.3.refs_1_ = bf16[1024,128]{1,0:T(8,128)(2,1)S(1)} collective-permute-done((bf16[1024,128]{1,0:T(8,128)(2,1)}, bf16[1024,128]{1,0:T(8,128)(2,1)S(1)}, u32[]{:S(2)}, u32[]{:S(2)}) %collective-permute-start.3) | collective-permute-done | bytes 262176 | tf_op jit(solution)/shard_map/ppermute | solution.py:427
  32.8 15.5 %collective-permute-done.4.refs_2_ = bf16[1024,128]{1,0:T(8,128)(2,1)S(1)} collective-permute-done((bf16[1024,128]{1,0:T(8,128)(2,1)}, bf16[1024,128]{1,0:T(8,128)(2,1)S(1)}, u32[]{:S(2)}, u32[]{:S(2)}) %collective-permute-start.4) | collective-permute-done | bytes 262176 | tf_op jit(solution)/shard_map/ppermute | solution.py:427
  48.3 0.0 collective-permute-done.5.refs_3_
  48.3 0.0 collective-permute-done.7.refs_5_
  48.3 0.9 %copy-done = bf16[1024,128]{1,0:T(8,128)(2,1)S(1)} copy-done((bf16[1024,128]{1,0:T(8,128)(2,1)S(1)}, bf16[1024,128]{1,0:T(8,128)(2,1)}, u32[]{:S(2)}) %copy-start) | copy-done | bytes 262168
  49.3 0.7 weight_other_core.1
  50.0 3.1 %collective-permute-start.8 = (bf16[512,1024]{1,0:T(8,128)(2,1)S(1)}, bf16[512,1024]{1,0:T(8,128)(2,1)S(1)}, u32[]{:S(2)}, u32[]{:S(2)}) collective-permute-start(bf16[512,1024]{1,0:T(8,128)(2,1)S(1)} %weight_other_core.1), channel_id=1, source_target_pairs={{0,2},{2,0},{4,6},{6,4},{8,10},{10,8},{12,14},{14,12},{16,18},{18,... | collective-permute-start | bytes 3145736 | tf_op jit(solution)/shard_map/ppermute | solution.py:418
  53.1 0.7 weight_this_core.1.mine_ref
  53.8 0.0 copy-start.1
  53.8 0.0 copy-start.3
  53.9 1.6 %collective-permute-done.8.theirs_ref = bf16[512,1024]{1,0:T(8,128)(2,1)S(1)} collective-permute-done((bf16[512,1024]{1,0:T(8,128)(2,1)S(1)}, bf16[512,1024]{1,0:T(8,128)(2,1)S(1)}, u32[]{:S(2)}, u32[]{:S(2)}) %collective-permute-start.8) | collective-permute-done | bytes 1048608 | tf_op jit(solution)/shard_map/ppermute | solution.py:418
  55.4 0.2 chip_total.1
  55.6 1.3 %collective-permute-start.9 = (bf16[128,1024]{1,0:T(8,128)(2,1)S(1)}, bf16[128,1024]{1,0:T(8,128)(2,1)S(1)}, u32[]{:S(2)}, u32[]{:S(2)}) collective-permute-start(bf16[128,1024]{1,0:T(8,128)(2,1)S(1)} %get-tuple-element.40), channel_id=1, source_target_pairs={{0,8},{2,10},{4,12},{6,14},{8,16},{10,18},{12,20},{14,22},{16,24},... | collective-permute-start | bytes 786440 | tf_op jit(solution)/shard_map/ppermute | solution.py:415
  56.9 1.1 %collective-permute-start.10 = (bf16[128,1024]{1,0:T(8,128)(2,1)S(1)}, bf16[128,1024]{1,0:T(8,128)(2,1)S(1)}, u32[]{:S(2)}, u32[]{:S(2)}) collective-permute-start(bf16[128,1024]{1,0:T(8,128)(2,1)S(1)} %get-tuple-element.41), channel_id=1, source_target_pairs={{0,16},{2,18},{4,20},{6,22},{8,24},{10,26},{12,28},{14,30},{16,0},... | collective-permute-start | bytes 786440 | tf_op jit(solution)/shard_map/ppermute | solution.py:415
  58.0 1.4 %collective-permute-start.11 = (bf16[128,1024]{1,0:T(8,128)(2,1)S(1)}, bf16[128,1024]{1,0:T(8,128)(2,1)S(1)}, u32[]{:S(2)}, u32[]{:S(2)}) collective-permute-start(bf16[128,1024]{1,0:T(8,128)(2,1)S(1)} %get-tuple-element.42), channel_id=1, source_target_pairs={{0,24},{2,26},{4,28},{6,30},{8,0},{10,2},{12,4},{14,6},{16,8},{18,... | collective-permute-start | bytes 786440 | tf_op jit(solution)/shard_map/ppermute | solution.py:415
  59.4 0.0 copy-done.1
  59.4 0.0 copy-done.3
  59.4 1.7 %query_gradient.1 = bf16[128,4096]{1,0:T(8,128)(2,1)} custom-call(bf16[128,4096]{1,0:T(8,128)(2,1)S(1)} %copy-done.1, bf16[128,4096]{1,0:T(8,128)(2,1)S(1)} %get-tuple-element.26.refs_1_, bf16[128,512]{1,0:T(8,128)(2,1)S(1)} %copy-done.3, bf16[128,512]{1,0:T(8,128)(2,1)S(1)} %collective-permute-done.k_in.refs_3_), custom_call_target="tpu_custom_call" | custom-call | flops 1024 | bytes 1024 | tf_op jit(solution)/shard_map/query_gradient/pallas_call | solution.py:219
  61.1 2.0 %collective-permute-done.9.refs_1_ = bf16[128,1024]{1,0:T(8,128)(2,1)S(1)} collective-permute-done((bf16[128,1024]{1,0:T(8,128)(2,1)S(1)}, bf16[128,1024]{1,0:T(8,128)(2,1)S(1)}, u32[]{:S(2)}, u32[]{:S(2)}) %collective-permute-start.9) | collective-permute-done | bytes 262176 | tf_op jit(solution)/shard_map/ppermute | solution.py:415
  63.2 15.9 %collective-permute-done.10.refs_2_ = bf16[128,1024]{1,0:T(8,128)(2,1)S(1)} collective-permute-done((bf16[128,1024]{1,0:T(8,128)(2,1)S(1)}, bf16[128,1024]{1,0:T(8,128)(2,1)S(1)}, u32[]{:S(2)}, u32[]{:S(2)}) %collective-permute-start.10) | collective-permute-done | bytes 262176 | tf_op jit(solution)/shard_map/ppermute | solution.py:415
  79.1 2.6 %collective-permute-done.11.refs_3_ = bf16[128,1024]{1,0:T(8,128)(2,1)S(1)} collective-permute-done((bf16[128,1024]{1,0:T(8,128)(2,1)S(1)}, bf16[128,1024]{1,0:T(8,128)(2,1)S(1)}, u32[]{:S(2)}, u32[]{:S(2)}) %collective-permute-start.11) | collective-permute-done | bytes 262176 | tf_op jit(solution)/shard_map/ppermute | solution.py:415
  81.7 0.8 %weight_total.1 = (f32[128,512]{1,0:T(8,128)}, f32[128,512]{1,0:T(8,128)}) custom-call(f32[128,1024]{1,0:T(8,128)S(1)} %get-tuple-element.39.refs_0_, bf16[128,1024]{1,0:T(8,128)(2,1)S(1)} %collective-permute-done.9.refs_1_, bf16[128,1024]{1,0:T(8,128)(2,1)S(1)} %collective-permute-done.10.refs_2_, bf16[128,1024]{1,0:T(8,128)(2,1)S(1)} %collective-permute-done.11.refs_3_), custom_call_target="tpu_custom_call" | custom-call | flops 1024 | bytes 1024 | tf_op jit(solution)/shard_map/weight_total/pallas_call | solution.py:382
  (1 shorter events, 0.0 us)
Async XLA Ops:
  0.6 8.2 %copy-start.6 = (s32[1,4]{1,0:T(1,128)S(1)}, s32[1,4]{1,0:T(1,128)}, u32[]{:S(2)}) copy-start(s32[1,4]{1,0:T(1,128)} %lengths_ref.3) | copy-start | bytes 52
  0.6 8.2 %copy-start.4 = (f32[128,32]{0,1:T(8,128)S(1)}, f32[128,32]{0,1:T(8,128)}, u32[]{:S(2)}) copy-start(f32[128,32]{0,1:T(8,128)} %param.13) | copy-start | bytes 49156
  0.7 8.1 %collective-permute-start.1 = (bf16[128,512]{1,0:T(8,128)(2,1)}, bf16[128,512]{1,0:T(8,128)(2,1)S(1)}, u32[]{:S(2)}, u32[]{:S(2)}) collective-permute-start(bf16[128,512]{1,0:T(8,128)(2,1)} %v_in.1), channel_id=1, source_target_pairs={{0,1},{1,0},{2,3},{3,2},{4,5},{5,4},{6,7},{7,6},{8,9},{9,8},{10,11... | collective-permute-start | bytes 393224 | tf_op jit(solution)/shard_map/ppermute | solution.py:410
  1.9 6.9 %collective-permute-start = (bf16[128,512]{1,0:T(8,128)(2,1)}, bf16[128,512]{1,0:T(8,128)(2,1)S(1)}, u32[]{:S(2)}, u32[]{:S(2)}) collective-permute-start(bf16[128,512]{1,0:T(8,128)(2,1)} %refs_2_.1), channel_id=1, source_target_pairs={{0,1},{1,0},{2,3},{3,2},{4,5},{5,4},{6,7},{7,6},{8,9},{9,8},{10,11... | collective-permute-start | bytes 393224 | tf_op jit(solution)/shard_map/ppermute | solution.py:410
  8.8 16.9 %copy-start.2 = (f32[2,128,512]{2,1,0:T(8,128)S(1)}, f32[2,128,512]{2,1,0:T(8,128)}, u32[]{:S(2)}) copy-start(f32[2,128,512]{2,1,0:T(8,128)} %get-tuple-element.36.own_ref) | copy-start | bytes 1572868
  8.8 0.8 copy-start.5
  9.6 5.1 %copy-start.7 = (bf16[2,128,512]{2,1,0:T(8,128)(2,1)S(1)}, bf16[2,128,512]{2,1,0:T(8,128)(2,1)}, u32[]{:S(2)}) copy-start(bf16[2,128,512]{2,1,0:T(8,128)(2,1)} %get-tuple-element.38) | copy-start | bytes 786436
  13.4 6.6 %collective-permute-start.2 = (bf16[2,128,512]{2,1,0:T(8,128)(2,1)S(1)}, bf16[2,128,512]{2,1,0:T(8,128)(2,1)S(1)}, u32[]{:S(2)}, u32[]{:S(2)}) collective-permute-start(bf16[2,128,512]{2,1,0:T(8,128)(2,1)S(1)} %get-tuple-element.27.sent_ref), channel_id=1, source_target_pairs={{0,1},{1,0},{2,3},{3,2},{4,5},{5,4},{6,7},{7,6},{8,9},{9,8},{10,11... | collective-permute-start | bytes 786440 | tf_op jit(solution)/shard_map/ppermute | solution.py:410
  14.7 11.0 %collective-permute-start.6 = (bf16[2,128,512]{2,1,0:T(8,128)(2,1)S(1)}, bf16[2,128,512]{2,1,0:T(8,128)(2,1)S(1)}, u32[]{:S(2)}, u32[]{:S(2)}) collective-permute-start(bf16[2,128,512]{2,1,0:T(8,128)(2,1)S(1)} %copy-done.7), channel_id=1, source_target_pairs={{0,1},{1,0},{2,3},{3,2},{4,5},{5,4},{6,7},{7,6},{8,9},{9,8},{10,11... | collective-permute-start | bytes 786440 | tf_op jit(solution)/shard_map/ppermute | solution.py:410
  25.7 22.6 %collective-permute-start.7 = (bf16[2,2,128,512]{3,2,1,0:T(8,128)(2,1)S(1)}, bf16[2,2,128,512]{3,2,1,0:T(8,128)(2,1)S(1)}, u32[]{:S(2)}, u32[]{:S(2)}) collective-permute-start(bf16[2,2,128,512]{3,2,1,0:T(8,128)(2,1)S(1)} %grads_total.1.refs_4_), channel_id=1, source_target_pairs={{0,4},{1,5},{2,6},{3,7},{4,0},{5,1},{6,2},{7,3},{8,12},{9,13},{10,... | collective-permute-start | bytes 1572872 | tf_op jit(solution)/shard_map/ppermute | solution.py:427
  27.0 5.7 %collective-permute-start.3 = (bf16[1024,128]{1,0:T(8,128)(2,1)}, bf16[1024,128]{1,0:T(8,128)(2,1)S(1)}, u32[]{:S(2)}, u32[]{:S(2)}) collective-permute-start(bf16[1024,128]{1,0:T(8,128)(2,1)} %get-tuple-element.33), channel_id=1, source_target_pairs={{0,1},{1,0},{2,3},{3,2},{4,5},{5,4},{6,7},{7,6},{8,9},{9,8},{10,11... | collective-permute-start | bytes 786440 | tf_op jit(solution)/shard_map/ppermute | solution.py:427
  28.3 20.0 %collective-permute-start.4 = (bf16[1024,128]{1,0:T(8,128)(2,1)}, bf16[1024,128]{1,0:T(8,128)(2,1)S(1)}, u32[]{:S(2)}, u32[]{:S(2)}) collective-permute-start(bf16[1024,128]{1,0:T(8,128)(2,1)} %get-tuple-element.34), channel_id=1, source_target_pairs={{0,4},{1,5},{2,6},{3,7},{4,0},{5,1},{6,2},{7,3},{8,12},{9,13},{10,... | collective-permute-start | bytes 786440 | tf_op jit(solution)/shard_map/ppermute | solution.py:427
  28.5 19.8 %collective-permute-start.5 = (bf16[1024,128]{1,0:T(8,128)(2,1)}, bf16[1024,128]{1,0:T(8,128)(2,1)S(1)}, u32[]{:S(2)}, u32[]{:S(2)}) collective-permute-start(bf16[1024,128]{1,0:T(8,128)(2,1)} %get-tuple-element.35), channel_id=1, source_target_pairs={{0,5},{1,4},{2,7},{3,6},{4,1},{5,0},{6,3},{7,2},{8,13},{9,12},{10,... | collective-permute-start | bytes 786440 | tf_op jit(solution)/shard_map/ppermute | solution.py:427
  48.3 1.0 %copy-start = (bf16[1024,128]{1,0:T(8,128)(2,1)S(1)}, bf16[1024,128]{1,0:T(8,128)(2,1)}, u32[]{:S(2)}) copy-start(bf16[1024,128]{1,0:T(8,128)(2,1)} %get-tuple-element.32.refs_0_) | copy-start | bytes 786436
  50.0 5.4 %collective-permute-start.8 = (bf16[512,1024]{1,0:T(8,128)(2,1)S(1)}, bf16[512,1024]{1,0:T(8,128)(2,1)S(1)}, u32[]{:S(2)}, u32[]{:S(2)}) collective-permute-start(bf16[512,1024]{1,0:T(8,128)(2,1)S(1)} %weight_other_core.1), channel_id=1, source_target_pairs={{0,2},{2,0},{4,6},{6,4},{8,10},{10,8},{12,14},{14,12},{16,18},{18,... | collective-permute-start | bytes 3145736 | tf_op jit(solution)/shard_map/ppermute | solution.py:418
  53.8 5.6 %copy-start.1 = (bf16[128,4096]{1,0:T(8,128)(2,1)S(1)}, bf16[128,4096]{1,0:T(8,128)(2,1)}, u32[]{:S(2)}) copy-start(bf16[128,4096]{1,0:T(8,128)(2,1)} %get-tuple-element.24.refs_0_) | copy-start | bytes 3145732
  53.8 5.6 %copy-start.3 = (bf16[128,512]{1,0:T(8,128)(2,1)S(1)}, bf16[128,512]{1,0:T(8,128)(2,1)}, u32[]{:S(2)}) copy-start(bf16[128,512]{1,0:T(8,128)(2,1)} %refs_2_.1) | copy-start | bytes 393220
  55.6 7.6 %collective-permute-start.9 = (bf16[128,1024]{1,0:T(8,128)(2,1)S(1)}, bf16[128,1024]{1,0:T(8,128)(2,1)S(1)}, u32[]{:S(2)}, u32[]{:S(2)}) collective-permute-start(bf16[128,1024]{1,0:T(8,128)(2,1)S(1)} %get-tuple-element.40), channel_id=1, source_target_pairs={{0,8},{2,10},{4,12},{6,14},{8,16},{10,18},{12,20},{14,22},{16,24},... | collective-permute-start | bytes 786440 | tf_op jit(solution)/shard_map/ppermute | solution.py:415
  56.9 22.2 %collective-permute-start.10 = (bf16[128,1024]{1,0:T(8,128)(2,1)S(1)}, bf16[128,1024]{1,0:T(8,128)(2,1)S(1)}, u32[]{:S(2)}, u32[]{:S(2)}) collective-permute-start(bf16[128,1024]{1,0:T(8,128)(2,1)S(1)} %get-tuple-element.41), channel_id=1, source_target_pairs={{0,16},{2,18},{4,20},{6,22},{8,24},{10,26},{12,28},{14,30},{16,0},... | collective-permute-start | bytes 786440 | tf_op jit(solution)/shard_map/ppermute | solution.py:415
  58.0 23.6 %collective-permute-start.11 = (bf16[128,1024]{1,0:T(8,128)(2,1)S(1)}, bf16[128,1024]{1,0:T(8,128)(2,1)S(1)}, u32[]{:S(2)}, u32[]{:S(2)}) collective-permute-start(bf16[128,1024]{1,0:T(8,128)(2,1)S(1)} %get-tuple-element.42), channel_id=1, source_target_pairs={{0,24},{2,26},{4,28},{6,30},{8,0},{10,2},{12,4},{14,6},{16,8},{18,... | collective-permute-start | bytes 786440 | tf_op jit(solution)/shard_map/ppermute | solution.py:415

commit v3 on v2

v3 whole, which is shorter than its diff:
```python
import functools
import math

import jax
import jax.numpy as jnp
from jax import lax
from jax.experimental import pallas as pl
from jax.experimental.pallas import tpu as pltpu
from jax.sharding import PartitionSpec as P

QUERY_HEADS = 32
KEY_VALUE_HEADS = 4
HEAD_SIZE = 128
GROUP = QUERY_HEADS // KEY_VALUE_HEADS
SCALE = 1.0 / math.sqrt(HEAD_SIZE)
CORES = 2
MIDDLE = 2
NEAR = 2
PARTS = 1
PART_HEADS = KEY_VALUE_HEADS // PARTS
PART_WIDTH = PART_HEADS * HEAD_SIZE
OWN_MIB, VISITING_MIB, PREPARE_MIB = 32, 32, 32


def limit(mib):
    return pltpu.CompilerParams(vmem_limit_bytes=mib * 2**20)


PARAMS = limit(32)
COST = pl.CostEstimate(flops=1024, bytes_accessed=1024, transcendentals=0)
WHOLE = pl.BlockSpec(memory_space=pltpu.VMEM)
FAR = pl.BlockSpec(memory_space=pltpu.HBM)
SCALARS = pl.BlockSpec(memory_space=pltpu.SMEM)

NT = (((1,), (1,)), ((), ()))
TN = (((0,), (0,)), ((), ()))
NN = (((1,), (0,)), ((), ()))


def dot(a, b, dims):
    return lax.dot_general(a, b, dims, preferred_element_type=jnp.float32)


def pinned(value):
    return pltpu.with_memory_space_constraint(value, pltpu.HBM)


def shape(dims, dtype):
    return jax.ShapeDtypeStruct(dims, dtype)


def rows_of_heads(block):
    return jnp.concatenate(
        [block[:, h * HEAD_SIZE : (h + 1) * HEAD_SIZE] for h in range(GROUP)], axis=0
    )


def allowed_mask(lengths_ref, ctx_count, rank, owner, keys, rows):
    key_pos = lax.broadcasted_iota(jnp.int32, (keys, rows), 0) * ctx_count + owner
    query_pos = lax.broadcasted_iota(jnp.int32, (keys, rows), 1) * ctx_count + rank
    allowed = key_pos <= query_pos
    end = jnp.int32(0)
    for j in range(lengths_ref.shape[1]):
        end = end + lengths_ref[0, j]
        allowed = allowed & ((end <= key_pos) == (end <= query_pos))
    return allowed


def delta_rows(do, out):
    rows, width = do.shape
    product = do.astype(jnp.float32) * out.astype(jnp.float32)
    high = product.astype(jnp.bfloat16)
    low = (product - high.astype(jnp.float32)).astype(jnp.bfloat16)
    pick = (
        lax.broadcasted_iota(jnp.int32, (GROUP, width), 1) // HEAD_SIZE
        == lax.broadcasted_iota(jnp.int32, (GROUP, width), 0)
    ).astype(jnp.bfloat16)
    return dot(pick, high, NT) + dot(pick, low, NT)


def block_kernel(first, part, ctx_count, step, *refs):
    lengths_ref, q_hbm, do_hbm, k_in, v_in, lse_ref, delta_ref, ds_ref, grad_ref = refs[:9]
    q_buf, do_buf, sems = refs[9:12]
    count = grad_ref.shape[2] // HEAD_SIZE
    heads = range(part * count, (part + 1) * count)
    width = GROUP * HEAD_SIZE
    k_ref, v_ref = k_in, v_in
    small = []
    if first:
        k_ref, v_ref, small_sems = refs[12:]
        small = [
            pltpu.make_async_copy(k_in, k_ref, small_sems.at[0]),
            pltpu.make_async_copy(v_in, v_ref, small_sems.at[1]),
        ]
        for copy in small:
            copy.start()
    copies = []
    for at, g in enumerate(heads):
        cut = slice(g * width, (g + 1) * width)
        copies.append(
            [
                pltpu.make_async_copy(q_hbm.at[:, cut], q_buf.at[at], sems.at[0, at]),
                pltpu.make_async_copy(do_hbm.at[:, cut], do_buf.at[at], sems.at[1, at]),
            ]
        )
        for copy in copies[-1]:
            copy.start()
    rank = lax.axis_index("ctx")
    owner = lax.rem(rank + ctx_count - step, ctx_count)
    rows = q_hbm.shape[0]
    keys = k_in.shape[0]
    allowed = allowed_mask(lengths_ref, ctx_count, rank, owner, keys, rows)
    for copy in small:
        copy.wait()
    for at, g in enumerate(heads):
        for copy in copies[at]:
            copy.wait()
        q = rows_of_heads(q_buf[at])
        do = rows_of_heads(do_buf[at])
        group = slice(g * GROUP, (g + 1) * GROUP)
        delta = delta_ref[group, :]
        lse = lse_ref[group, :]
        columns = slice(g * HEAD_SIZE, (g + 1) * HEAD_SIZE)
        scores = dot(k_ref[:, columns], q, NT)
        grad_probs = dot(v_ref[:, columns], do, NT)
        probs_low = []
        grad_scores = []
        for h in range(GROUP):
            cut = slice(h * rows, (h + 1) * rows)
            probs = jnp.where(allowed, jnp.exp(scores[:, cut] * SCALE - lse[h : h + 1, :]), 0.0)
            grad_scores.append(
                (probs * (grad_probs[:, cut] - delta[h : h + 1, :])).astype(jnp.bfloat16)
            )
            probs_low.append(probs.astype(jnp.bfloat16))
        probs_low = jnp.concatenate(probs_low, axis=1)
        grad_scores = jnp.concatenate(grad_scores, axis=1)
        ds_ref[:, at * GROUP * rows : (at + 1) * GROUP * rows] = grad_scores
        columns = slice(at * HEAD_SIZE, (at + 1) * HEAD_SIZE)
        grad_ref[0, :, columns] = (dot(grad_scores, q, NN) * SCALE).astype(grad_ref.dtype)
        grad_ref[1, :, columns] = dot(probs_low, do, NN).astype(grad_ref.dtype)


def block_call(
    first, part, step, ctx_count, lengths, queries, output_gradient, keys, values, lse, delta
):
    rows = queries.shape[0]
    key_rows, half = keys.shape
    count = KEY_VALUE_HEADS if first else PART_HEADS
    buffer = pltpu.VMEM((count, rows, GROUP * HEAD_SIZE), jnp.bfloat16)
    small = pltpu.VMEM((key_rows, half), jnp.bfloat16)
    near = FAR if first else WHOLE
    return pl.pallas_call(
        functools.partial(block_kernel, first, part, ctx_count, step),
        in_specs=[SCALARS, FAR, FAR, near, near, WHOLE, WHOLE],
        out_specs=[WHOLE] * 2,
        out_shape=[
            shape((key_rows, count * GROUP * rows), jnp.bfloat16),
            shape((2, key_rows, count * HEAD_SIZE), jnp.float32 if first else jnp.bfloat16),
        ],
        scratch_shapes=[buffer, buffer, pltpu.SemaphoreType.DMA((2, count))]
        + ([small, small, pltpu.SemaphoreType.DMA((2,))] if first else []),
        compiler_params=limit(OWN_MIB if first else VISITING_MIB),
        cost_estimate=COST,
        name="own_keys" if first else "visiting_keys",
    )(lengths, queries, output_gradient, keys, values, lse, delta)


def query_kernel(steps, *refs):
    own_ref, k_refs, out_ref = refs[0], refs[-2 - steps : -1], refs[-1]
    visiting = refs[1 : 1 + steps * PARTS]
    rows = out_ref.shape[0]
    for g in range(KEY_VALUE_HEADS):
        columns = slice(g * HEAD_SIZE, (g + 1) * HEAD_SIZE)
        keys = jnp.concatenate([k[:, columns] for k in k_refs], axis=0)
        part, at = divmod(g, PART_HEADS)
        for h in range(GROUP):
            head = g * GROUP + h
            scores = [own_ref[:, head * rows : (head + 1) * rows]]
            for ref in visiting[part * steps : (part + 1) * steps]:
                inner = at * GROUP + h
                scores.append(ref[:, inner * rows : (inner + 1) * rows])
            out_ref[:, head * HEAD_SIZE : (head + 1) * HEAD_SIZE] = (
                dot(jnp.concatenate(scores, axis=0), keys, TN) * SCALE
            ).astype(out_ref.dtype)


def query_call(own_scores, visiting_scores, keys, rows):
    steps = len(keys) - 1
    operands = [own_scores] + visiting_scores + keys
    return pl.pallas_call(
        functools.partial(query_kernel, steps),
        in_specs=[WHOLE] * len(operands),
        out_specs=WHOLE,
        out_shape=shape((rows, QUERY_HEADS * HEAD_SIZE), jnp.bfloat16),
        compiler_params=PARAMS,
        cost_estimate=COST,
        name="query_gradient",
    )(*operands)


def group_place():
    dp_rank = lax.axis_index("dp")
    return lax.rem(lax.div(dp_rank, CORES), MIDDLE), lax.rem(lax.div(dp_rank, CORES * MIDDLE), NEAR)


def prepare_kernel(far, ctx_count, turn, *refs):
    do_hbm, out_hbm = refs[:2]
    if turn:
        in_hbm, piece_refs, refs = refs[2], refs[3:-6], refs[-6:]
        buf, buf_sems = refs[-2:]
        refs = refs[:-2]
    else:
        refs = refs[2:]
    delta_ref, do_buf, out_buf, sems = refs
    width = GROUP * HEAD_SIZE
    piece_copies = []
    if turn:
        for z in range(far):
            chunk = in_hbm.shape[1] // far
            copy = pltpu.make_async_copy(
                in_hbm.at[:, z * chunk : (z + 1) * chunk], buf.at[z], buf_sems.at[z]
            )
            copy.start()
            piece_copies.append(copy)
    copies = []
    for g in range(KEY_VALUE_HEADS):
        cut = slice(g * width, (g + 1) * width)
        pair = [
            pltpu.make_async_copy(do_hbm.at[:, cut], do_buf.at[g], sems.at[0, g]),
            pltpu.make_async_copy(out_hbm.at[:, cut], out_buf.at[g], sems.at[1, g]),
        ]
        for copy in pair:
            copy.start()
        copies.append(pair)
    if turn:
        y_rank, z_rank = group_place()
        block = piece_refs[0].shape[0] // (CORES * far * ctx_count)
        for zh in range(far):
            piece_copies[zh].wait()
            for index, piece_ref in enumerate(piece_refs):
                y = lax.rem(y_rank + index // NEAR, MIDDLE)
                zl = lax.rem(z_rank + index % NEAR, NEAR)
                for core in range(CORES):
                    column = ((zl * MIDDLE + y) * CORES + core) * ctx_count
                    for x in range(ctx_count):
                        start = pl.multiple_of((column + x) * block, block)
                        row = ((core * far + zh) * ctx_count + x) * block
                        piece_ref[row : row + block, :] = buf[zh, :, pl.ds(start, block)].T
    for g in range(KEY_VALUE_HEADS):
        for copy in copies[g]:
            copy.wait()
        delta_ref[g * GROUP : (g + 1) * GROUP, :] = delta_rows(do_buf[g], out_buf[g])


def prepare_call(normed, output_gradient, attention_output, far, ctx_count):
    rows, width = normed.shape
    count = MIDDLE * NEAR
    block = width // (count * CORES * far * ctx_count)
    turn = block % 128 == 0
    piece = shape((width // count, rows), normed.dtype)
    buffer = pltpu.VMEM((KEY_VALUE_HEADS, rows, GROUP * HEAD_SIZE), jnp.bfloat16)
    operands = [output_gradient, attention_output] + ([pinned(normed)] if turn else [])
    *pieces, delta = pl.pallas_call(
        functools.partial(prepare_kernel, far, ctx_count, turn),
        in_specs=[FAR] * len(operands),
        out_specs=[WHOLE] * (1 + count * turn),
        out_shape=[piece] * (count * turn) + [shape((QUERY_HEADS, rows), jnp.float32)],
        scratch_shapes=[buffer, buffer, pltpu.SemaphoreType.DMA((2, KEY_VALUE_HEADS))]
        + (
            [
                pltpu.VMEM((far, rows, width // far), normed.dtype),
                pltpu.SemaphoreType.DMA((far,)),
            ]
            if turn
            else []
        ),
        compiler_params=limit(PREPARE_MIB),
        cost_estimate=COST,
        name="prepare",
    )(*operands)
    if not turn:
        y_rank, z_rank = group_place()
        turned = normed.T.reshape(far, NEAR, MIDDLE, CORES, ctx_count, block, rows)
        for index in range(count):
            cut = lax.dynamic_index_in_dim(turned, (z_rank + index % NEAR) % NEAR, 1, False)
            cut = lax.dynamic_index_in_dim(cut, (y_rank + index // NEAR) % MIDDLE, 1, False)
            pieces.append(cut.transpose(1, 0, 2, 3, 4).reshape(piece.shape))
    return pieces, delta


def add_kernel(part, own_ref, *refs):
    cut = slice(part * PART_WIDTH, (part + 1) * PART_WIDTH)
    total = own_ref[:, :, cut]
    for back_ref in refs[:-1]:
        total = total + back_ref[...].astype(jnp.float32)
    refs[-1][...] = total.astype(refs[-1].dtype)


def add_call(part, own, back):
    return pl.pallas_call(
        functools.partial(add_kernel, part),
        in_specs=[WHOLE] * (1 + len(back)),
        out_specs=WHOLE,
        out_shape=shape(back[0].shape, jnp.bfloat16),
        compiler_params=PARAMS,
        cost_estimate=COST,
        name="grads_total",
    )(own, *back)


def weight_kernel(other, count, *refs):
    n_refs, g_refs, out_ref = refs[:count], refs[count:-1], refs[-1]
    height, columns = out_ref.shape
    width = columns // 2
    core = lax.rem(lax.axis_index("dp"), CORES)
    if other:
        core = 1 - core
    start = pl.multiple_of(core * height, height)
    block = height if height < 256 else 256
    grads = [
        jnp.concatenate([g[j] for g in g_refs], axis=0) for j in range(2)
    ]
    for row in range(0, height, block):
        tokens = jnp.concatenate([n[pl.ds(start + row, block), :] for n in n_refs], axis=1)
        for j in range(2):
            out_ref[row : row + block, j * width : (j + 1) * width] = dot(
                tokens, grads[j], NN
            ).astype(out_ref.dtype)


def weight_call(other, tokens, grads, dtype):
    operands = list(tokens) + list(grads)
    return pl.pallas_call(
        functools.partial(weight_kernel, other, len(tokens)),
        in_specs=[WHOLE] * len(operands),
        out_specs=WHOLE,
        out_shape=shape((tokens[0].shape[0] // CORES, 2 * grads[0].shape[-1]), dtype),
        compiler_params=PARAMS,
        cost_estimate=COST,
        name="weight_other_core" if other else "weight_this_core",
    )(*operands)


def chip_kernel(far, ctx_count, mine_ref, theirs_ref, own_ref, far_ref, *out_refs):
    block = own_ref.shape[0]
    z_rank = lax.div(lax.axis_index("dp"), CORES * MIDDLE * NEAR)
    x_rank = lax.axis_index("ctx")

    def total(z_steps, x_steps):
        z = lax.rem(z_rank + z_steps, far)
        x = lax.rem(x_rank + x_steps, ctx_count)
        at = pl.ds(pl.multiple_of((z * ctx_count + x) * block, block), block)
        return mine_ref[at, :] + theirs_ref[at, :].astype(jnp.float32)

    for x in range(1, ctx_count):
        near_out, far_out = out_refs[2 * x - 2 : 2 * x]
        for z in range(1, far):
            far_out[(z - 1) * block : z * block, :] = total(z, x).astype(far_out.dtype)
        near_out[...] = total(0, x).astype(near_out.dtype)
    for z in range(1, far):
        far_ref[(z - 1) * block : z * block, :] = total(z, 0)
    own_ref[...] = total(0, 0)


def chip_call(far, ctx_count, mine, theirs):
    height, columns = mine.shape
    block = height // (far * ctx_count)
    near = (block, columns)
    away = ((far - 1) * block, columns)
    return pl.pallas_call(
        functools.partial(chip_kernel, far, ctx_count),
        in_specs=[WHOLE] * 2,
        out_specs=[WHOLE] * (2 * ctx_count),
        out_shape=[shape(near, jnp.float32), shape(away, jnp.float32)]
        + [shape(near, jnp.bfloat16), shape(away, jnp.bfloat16)] * (ctx_count - 1),
        compiler_params=PARAMS,
        cost_estimate=COST,
        name="chip_total",
    )(mine, theirs)


def relay_kernel(far, far_ref, *refs):
    in_refs, out_refs = refs[: 1 - far], refs[1 - far :]
    block = out_refs[0].shape[0]
    for z, out_ref in enumerate(out_refs):
        at = slice(z * block, (z + 1) * block)
        total = far_ref[at, :]
        for in_ref in in_refs:
            total = total + in_ref[at, :].astype(jnp.float32)
        out_ref[...] = total.astype(out_ref.dtype)


def relay_call(far, away, arrived):
    height, columns = away.shape
    return pl.pallas_call(
        functools.partial(relay_kernel, far),
        in_specs=[WHOLE] * (1 + len(arrived)),
        out_specs=[WHOLE] * (far - 1),
        out_shape=[shape((height // (far - 1), columns), jnp.bfloat16)] * (far - 1),
        compiler_params=PARAMS,
        cost_estimate=COST,
        name="relay_total",
    )(away, *arrived)


def final_kernel(*refs):
    key_ref, value_ref = refs[-2:]
    count = (len(refs) - 2) // PARTS
    for part in range(PARTS):
        pieces = refs[part * count : (part + 1) * count]
        total = pieces[0][...]
        for piece in pieces[1:]:
            total = total + piece[...].astype(jnp.float32)
        at = slice(part * PART_WIDTH, (part + 1) * PART_WIDTH)
        key_ref[:, at] = total[:, :PART_WIDTH]
        value_ref[:, at] = total[:, PART_WIDTH:]


def final_call(pieces):
    block = pieces[0].shape[0]
    return pl.pallas_call(
        final_kernel,
        in_specs=[WHOLE] * len(pieces),
        out_specs=[WHOLE] * 2,
        out_shape=[shape((block, KEY_VALUE_HEADS * HEAD_SIZE), jnp.float32)] * 2,
        compiler_params=PARAMS,
        cost_estimate=COST,
        name="weight_total",
    )(*pieces)


def local(
    normed_input,
    queries,
    saved_keys,
    saved_values,
    attention_output,
    saved_log_totals,
    output_gradient,
    document_lengths,
):
    rows = queries.shape[0]
    ctx_count = lax.axis_size("ctx")
    dp_count = lax.axis_size("dp")
    far = dp_count // (CORES * MIDDLE * NEAR)

    def over_ctx(value, steps):
        pairs = [(s, (s + steps) % ctx_count) for s in range(ctx_count)]
        return lax.ppermute(value, "ctx", pairs)

    def over_far(value, steps):
        stride = dp_count // far
        pairs = [(s, (s + steps * stride) % dp_count) for s in range(dp_count)]
        return lax.ppermute(value, "dp", pairs)

    def over_cores(value):
        return lax.ppermute(value, "dp", [(s, s ^ 1) for s in range(dp_count)])

    def over_group(value, index):
        flip = index // NEAR * CORES + index % NEAR * CORES * MIDDLE
        return lax.ppermute(value, "dp", [(s, s ^ flip) for s in range(dp_count)])

    far_keys, far_values, queries, attention_output, output_gradient = (
        pinned(value)
        for value in (saved_keys, saved_values, queries, attention_output, output_gradient)
    )
    visiting = [
        (over_ctx(saved_keys, step), over_ctx(saved_values, step)) for step in range(1, ctx_count)
    ]
    pieces, delta = prepare_call(
        normed_input, output_gradient, attention_output, far, ctx_count
    )
    tokens = [over_group(piece, index) if index else piece for index, piece in enumerate(pieces)]
    lse = saved_log_totals.T

    def block(first, part, step, keys, values, sums):
        return block_call(
            first,
            part,
            step,
            ctx_count,
            document_lengths,
            queries,
            output_gradient,
            keys,
            values,
            lse,
            sums,
        )

    visiting_scores = []
    sent = []
    for part in range(PARTS):
        for step in range(1, ctx_count):
            scores, grads = block(False, part, step, *visiting[step - 1], delta)
            visiting_scores.append(scores)
            sent.append(grads)
    back = [over_ctx(grads, -1 - i % (ctx_count - 1)) for i, grads in enumerate(sent)]
    delta, sent = lax.optimization_barrier((delta, sent))
    own_scores, own = block(True, 0, 0, far_keys, far_values, delta)
    summands = []
    for part in range(PARTS):
        grads = add_call(part, own, back[part * (ctx_count - 1) : (part + 1) * (ctx_count - 1)])
        group_grads = [over_group(grads, i) if i else grads for i in range(len(tokens))]
        theirs = weight_call(True, tokens, group_grads, jnp.bfloat16)
        arriving = over_cores(theirs)
        mine = weight_call(False, tokens, group_grads, jnp.float32)
        total, away, *blocks = chip_call(far, ctx_count, mine, arriving)
        away_arrived = [over_ctx(value, s) for s, value in enumerate(blocks[1::2], 1)]
        near_arrived = [over_ctx(value, s) for s, value in enumerate(blocks[0::2], 1)]
        relayed = relay_call(far, away, away_arrived)
        summands += [total] + near_arrived
        summands += [over_far(value, s) for s, value in enumerate(relayed, 1)]
    query_gradient = query_call(
        own_scores, visiting_scores, [saved_keys] + [pair[0] for pair in visiting], rows
    )
    key_weight_grad, value_weight_grad = final_call(summands)
    return query_gradient, key_weight_grad, value_weight_grad


def solution(mesh):
    both = P(("dp", "ctx"), None)
    return jax.shard_map(
        local,
        mesh=mesh,
        in_specs=(both,) * 7 + (P("dp", None),),
        out_specs=(both,) * 3,
        check_vma=False,
    )
```

time: 82.8 us -> 68 us (0.82)
  the two profiles are of different devices: /device:TPU:9 before, /device:TPU:0 now
where the time goes in v3:
time: 68 us; the launch traced here: 67.8 us
  waiting for transfers between devices  34.4 us (51%)
  starting transfers between devices  16.8 us (25%)
  Pallas kernels  15.9 us (23%)
  between operations  0.73 us (1%)
    ppermute x6, waiting for transfers between devices, over_group(): return lax.ppermute(value, 'dp', [(s, s ^ flip) for s in range(dp_count)])  13.7 us
    ppermute x5, waiting for transfers between devices, over_ctx(): return lax.ppermute(value, 'ctx', pairs)  10.3 us
    ppermute x1, waiting for transfers between devices, over_far(): return lax.ppermute(value, 'dp', pairs)  8.5 us
    pallas_call x2, Pallas kernels, block_call(): pl.pallas_call(functools.partial(block_kernel, first, part, ctx_count, st...  8.03 us
    ppermute x6, starting transfers between devices, over_group(): return lax.ppermute(value, 'dp', [(s, s ^ flip) for s in range(dp_count)])  7.04 us
    ppermute x5, starting transfers between devices, over_ctx(): return lax.ppermute(value, 'ctx', pairs)  7.01 us
    pallas_call x1, Pallas kernels, prepare_call(): pl.pallas_call(functools.partial(prepare_kernel, far, ctx_count, turn), i...  3.62 us
    ppermute x1, starting transfers between devices, over_far(): return lax.ppermute(value, 'dp', pairs)  2.65 us
  transfers between devices with their start and end apart: 13, of which 9 were waited for; matrix products, arithmetic and copies ran while one was open for 0% of the time, Pallas kernels for 15%

profile of v3, /device:TPU:0, one launch (start us, length us, event | category | flops | bytes accessed | tf_op | source)
XLA Modules:
  0.0 67.8 jit_solution(16253489248241741642)
XLA Ops:
  0.6 0.0 copy-start.2
  0.6 0.0 copy-start.1
  0.7 3.0 %collective-permute-start.1 = (bf16[128,512]{1,0:T(8,128)(2,1)}, bf16[128,512]{1,0:T(8,128)(2,1)S(1)}, u32[]{:S(2)}, u32[]{:S(2)}) collective-permute-start(bf16[128,512]{1,0:T(8,128)(2,1)} %refs_4_.1), channel_id=1, source_target_pairs={{0,1},{1,0},{2,3},{3,2},{4,5},{5,4},{6,7},{7,6},{8,9},{9,8},{10,11... | collective-permute-start | bytes 393224 | tf_op jit(solution)/shard_map/ppermute | solution.py:449
  3.7 0.1 collective-permute-start
  3.7 3.6 %prepare.1 = (bf16[1024,128]{1,0:T(8,128)(2,1)S(1)}, bf16[1024,128]{1,0:T(8,128)(2,1)S(1)}, bf16[1024,128]{1,0:T(8,128)(2,1)S(1)}, bf16[1024,128]{1,0:T(8,128)(2,1)S(1)}, f32[32,128]{1,0:T(8,128)S(1)}) custom-call(bf16[128,4096]{1,0:T(8,128)(2,1)} %refs_2_.6, bf16[128,4096]{1,0:T(8,128)(2,1)} %refs_1_.3, bf16[128,4096]{1,0:T(8,128)(2,1)} %refs_2_.4), custom_call_target="tpu_custom_call" | custom-call | flops 1024 | bytes 1024 | tf_op jit(solution)/shard_map/prepare/pallas_call | solution.py:263
  7.4 0.8 %collective-permute-done.1.refs_4_ = bf16[128,512]{1,0:T(8,128)(2,1)S(1)} collective-permute-done((bf16[128,512]{1,0:T(8,128)(2,1)}, bf16[128,512]{1,0:T(8,128)(2,1)S(1)}, u32[]{:S(2)}, u32[]{:S(2)}) %collective-permute-start.1) | collective-permute-done | bytes 131104 | tf_op jit(solution)/shard_map/ppermute | solution.py:449
  8.2 2.0 %collective-permute-done.refs_3_ = bf16[128,512]{1,0:T(8,128)(2,1)S(1)} collective-permute-done((bf16[128,512]{1,0:T(8,128)(2,1)}, bf16[128,512]{1,0:T(8,128)(2,1)S(1)}, u32[]{:S(2)}, u32[]{:S(2)}) %collective-permute-start) | collective-permute-done | bytes 131104 | tf_op jit(solution)/shard_map/ppermute | solution.py:449
  10.2 0.0 copy-done.2
  10.2 0.0 copy-done.1
  10.2 3.8 %visiting_keys.1 = (bf16[128,4096]{1,0:T(8,128)(2,1)S(1)}, bf16[2,128,512]{2,1,0:T(8,128)(2,1)S(1)}) custom-call(s32[1,4]{1,0:T(1,128)S(1)} %copy-done.2, bf16[128,4096]{1,0:T(8,128)(2,1)} %refs_1_.5, bf16[128,4096]{1,0:T(8,128)(2,1)} %refs_2_.6, bf16[128,512]{1,0:T(8,128)(2,1)S(1)} %collective-permute-done.refs_3_, ...), custom_call_target="tpu_custom_call" | custom-call | flops 1024 | bytes 1024 | tf_op jit(solution)/shard_map/visiting_keys/pallas_call | solution.py:152
  14.0 1.8 %collective-permute-start.5 = (bf16[2,128,512]{2,1,0:T(8,128)(2,1)S(1)}, bf16[2,128,512]{2,1,0:T(8,128)(2,1)S(1)}, u32[]{:S(2)}, u32[]{:S(2)}) collective-permute-start(bf16[2,128,512]{2,1,0:T(8,128)(2,1)S(1)} %get-tuple-element.20), channel_id=1, source_target_pairs={{0,1},{1,0},{2,3},{3,2},{4,5},{5,4},{6,7},{7,6},{8,9},{9,8},{10,11... | collective-permute-start | bytes 786440 | tf_op jit(solution)/shard_map/ppermute | solution.py:449
  15.8 1.6 %collective-permute-start.2 = (bf16[1024,128]{1,0:T(8,128)(2,1)S(1)}, bf16[1024,128]{1,0:T(8,128)(2,1)S(1)}, u32[]{:S(2)}, u32[]{:S(2)}) collective-permute-start(bf16[1024,128]{1,0:T(8,128)(2,1)S(1)} %get-tuple-element.25), channel_id=1, source_target_pairs={{0,8},{2,10},{4,12},{6,14},{8,0},{10,2},{12,4},{14,6},{16,24},{18,... | collective-permute-start | bytes 786440 | tf_op jit(solution)/shard_map/ppermute | solution.py:461
  17.3 1.5 %collective-permute-start.3 = (bf16[1024,128]{1,0:T(8,128)(2,1)S(1)}, bf16[1024,128]{1,0:T(8,128)(2,1)S(1)}, u32[]{:S(2)}, u32[]{:S(2)}) collective-permute-start(bf16[1024,128]{1,0:T(8,128)(2,1)S(1)} %get-tuple-element.26), channel_id=1, source_target_pairs={{0,4},{2,6},{4,0},{6,2},{8,12},{10,14},{12,8},{14,10},{16,20},{18,... | collective-permute-start | bytes 786440 | tf_op jit(solution)/shard_map/ppermute | solution.py:461
  18.9 0.4 collective-permute-start.4
  19.3 4.3 %own_keys.1 = (bf16[128,4096]{1,0:T(8,128)(2,1)S(1)}, f32[2,128,512]{2,1,0:T(8,128)S(1)}) custom-call(s32[1,4]{1,0:T(1,128)S(1)} %copy-done.2, bf16[128,4096]{1,0:T(8,128)(2,1)} %refs_1_.5, bf16[128,4096]{1,0:T(8,128)(2,1)} %refs_2_.6, bf16[128,512]{1,0:T(8,128)(2,1)} %refs_2_.7, bf16[128,512]{1,0:T(8,128)(2,1)} %refs_4_.1, f32[32,128]{1,0:T(8,128)S(1)} %bitcast.2, ...), custom_call_target="tpu_custom_call" | custom-call | flops 1024 | bytes 1024 | tf_op jit(solution)/shard_map/own_keys/pallas_call | solution.py:152
  23.5 0.0 collective-permute-done.5.refs_0_
  23.5 0.1 grads_total.1.refs_4_
  23.6 2.6 %collective-permute-start.8 = (bf16[2,128,512]{2,1,0:T(8,128)(2,1)S(1)}, bf16[2,128,512]{2,1,0:T(8,128)(2,1)S(1)}, u32[]{:S(2)}, u32[]{:S(2)}) collective-permute-start(bf16[2,128,512]{2,1,0:T(8,128)(2,1)S(1)} %grads_total.1.refs_4_), channel_id=1, source_target_pairs={{0,12},{2,14},{4,8},{6,10},{8,4},{10,6},{12,0},{14,2},{16,28},{18,... | collective-permute-start | bytes 786440 | tf_op jit(solution)/shard_map/ppermute | solution.py:461
  26.2 0.5 collective-permute-start.7
  26.7 0.0 collective-permute-done.2.refs_1_
  26.7 0.4 collective-permute-start.6
  27.2 7.9 %collective-permute-done.3.refs_2_ = bf16[1024,128]{1,0:T(8,128)(2,1)S(1)} collective-permute-done((bf16[1024,128]{1,0:T(8,128)(2,1)S(1)}, bf16[1024,128]{1,0:T(8,128)(2,1)S(1)}, u32[]{:S(2)}, u32[]{:S(2)}) %collective-permute-start.3) | collective-permute-done | bytes 262176 | tf_op jit(solution)/shard_map/ppermute | solution.py:461
  35.1 0.0 collective-permute-done.4.refs_3_
  35.1 2.2 %collective-permute-done.8.refs_7_ = bf16[2,128,512]{2,1,0:T(8,128)(2,1)S(1)} collective-permute-done((bf16[2,128,512]{2,1,0:T(8,128)(2,1)S(1)}, bf16[2,128,512]{2,1,0:T(8,128)(2,1)S(1)}, u32[]{:S(2)}, u32[]{:S(2)}) %collective-permute-start.8) | collective-permute-done | bytes 262176 | tf_op jit(solution)/shard_map/ppermute | solution.py:461
  37.3 3.6 %collective-permute-done.7.refs_6_ = bf16[2,128,512]{2,1,0:T(8,128)(2,1)S(1)} collective-permute-done((bf16[2,128,512]{2,1,0:T(8,128)(2,1)S(1)}, bf16[2,128,512]{2,1,0:T(8,128)(2,1)S(1)}, u32[]{:S(2)}, u32[]{:S(2)}) %collective-permute-start.7) | collective-permute-done | bytes 262176 | tf_op jit(solution)/shard_map/ppermute | solution.py:461
  40.8 0.0 collective-permute-done.6.refs_5_
  40.8 0.7 %weight_other_core.1 = bf16[512,1024]{1,0:T(8,128)(2,1)S(1)} custom-call(bf16[1024,128]{1,0:T(8,128)(2,1)S(1)} %get-tuple-element.24.refs_0_, bf16[1024,128]{1,0:T(8,128)(2,1)S(1)} %collective-permute-done.2.refs_1_, bf16[1024,128]{1,0:T(8,128)(2,1)S(1)} %collective-permute-done.3.refs_2_, bf16[1024,128]{1,0:T(8,128)(2,1)S(1)} %collective-permute-done.4.refs_3_, ...), custom_call_target="tpu_custom_call" | custom-call | flops 1024 | bytes 1024 | tf_op jit(solution)/shard_map/weight_other_core/pallas_call | solution.py:333
  41.5 0.1 collective-permute-start.9
  41.6 0.7 %weight_this_core.1.mine_ref = f32[512,1024]{1,0:T(8,128)S(1)} custom-call(bf16[1024,128]{1,0:T(8,128)(2,1)S(1)} %get-tuple-element.24.refs_0_, bf16[1024,128]{1,0:T(8,128)(2,1)S(1)} %collective-permute-done.2.refs_1_, bf16[1024,128]{1,0:T(8,128)(2,1)S(1)} %collective-permute-done.3.refs_2_, bf16[1024,128]{1,0:T(8,128)(2,1)S(1)} %collective-permute-done.4.refs_3_, ...), custom_call_target="tpu_custom_call" | custom-call | flops 1024 | bytes 1024 | tf_op jit(solution)/shard_map/weight_this_core/pallas_call | solution.py:333
  42.3 0.0 copy-start
  42.3 1.9 %collective-permute-done.9.theirs_ref = bf16[512,1024]{1,0:T(8,128)(2,1)S(1)} collective-permute-done((bf16[512,1024]{1,0:T(8,128)(2,1)S(1)}, bf16[512,1024]{1,0:T(8,128)(2,1)S(1)}, u32[]{:S(2)}, u32[]{:S(2)}) %collective-permute-start.9) | collective-permute-done | bytes 1048608 | tf_op jit(solution)/shard_map/ppermute | solution.py:457
  44.3 0.2 chip_total.1
  44.4 0.6 collective-permute-start.11
  45.0 1.5 %collective-permute-start.10 = (bf16[128,1024]{1,0:T(8,128)(2,1)S(1)}, bf16[128,1024]{1,0:T(8,128)(2,1)S(1)}, u32[]{:S(2)}, u32[]{:S(2)}) collective-permute-start(bf16[128,1024]{1,0:T(8,128)(2,1)S(1)} %get-tuple-element.30), channel_id=1, source_target_pairs={{0,1},{1,0},{2,3},{3,2},{4,5},{5,4},{6,7},{7,6},{8,9},{9,8},{10,11... | collective-permute-start | bytes 786440 | tf_op jit(solution)/shard_map/ppermute | solution.py:449
  46.6 7.1 %collective-permute-done.11.refs_0_ = bf16[128,1024]{1,0:T(8,128)(2,1)S(1)} collective-permute-done((bf16[128,1024]{1,0:T(8,128)(2,1)S(1)}, bf16[128,1024]{1,0:T(8,128)(2,1)S(1)}, u32[]{:S(2)}, u32[]{:S(2)}) %collective-permute-start.11) | collective-permute-done | bytes 262176 | tf_op jit(solution)/shard_map/ppermute | solution.py:449
  53.7 2.6 %collective-permute-start.12 = (bf16[128,1024]{1,0:T(8,128)(2,1)S(1)}, bf16[128,1024]{1,0:T(8,128)(2,1)S(1)}, u32[]{:S(2)}, u32[]{:S(2)}) collective-permute-start(bf16[128,1024]{1,0:T(8,128)(2,1)S(1)} %relay_total.1), channel_id=1, source_target_pairs={{0,16},{2,18},{4,20},{6,22},{8,24},{10,26},{12,28},{14,30},{16,0},... | collective-permute-start | bytes 786440 | tf_op jit(solution)/shard_map/ppermute | solution.py:454
  56.4 0.0 copy-done
  56.4 1.7 %query_gradient.1 = bf16[128,4096]{1,0:T(8,128)(2,1)} custom-call(bf16[128,4096]{1,0:T(8,128)(2,1)S(1)} %get-tuple-element.22.refs_0_, bf16[128,4096]{1,0:T(8,128)(2,1)S(1)} %get-tuple-element.23.refs_1_, bf16[128,512]{1,0:T(8,128)(2,1)S(1)} %copy-done, bf16[128,512]{1,0:T(8,128)(2,1)S(1)} %collective-permute-done.refs_3_), custom_call_target="tpu_custom_call" | custom-call | flops 1024 | bytes 1024 | tf_op jit(solution)/shard_map/query_gradient/pallas_call | solution.py:190
  58.1 0.3 collective-permute-done.10.refs_1_
  58.5 8.5 %collective-permute-done.12.refs_2_ = bf16[128,1024]{1,0:T(8,128)(2,1)S(1)} collective-permute-done((bf16[128,1024]{1,0:T(8,128)(2,1)S(1)}, bf16[128,1024]{1,0:T(8,128)(2,1)S(1)}, u32[]{:S(2)}, u32[]{:S(2)}) %collective-permute-start.12) | collective-permute-done | bytes 262176 | tf_op jit(solution)/shard_map/ppermute | solution.py:454
  67.0 0.8 %weight_total.1 = (f32[128,512]{1,0:T(8,128)}, f32[128,512]{1,0:T(8,128)}) custom-call(f32[128,1024]{1,0:T(8,128)S(1)} %get-tuple-element.29.refs_0_, bf16[128,1024]{1,0:T(8,128)(2,1)S(1)} %collective-permute-done.10.refs_1_, bf16[128,1024]{1,0:T(8,128)(2,1)S(1)} %collective-permute-done.12.refs_2_), custom_call_target="tpu_custom_call" | custom-call | flops 1024 | bytes 1024 | tf_op jit(solution)/shard_map/weight_total/pallas_call | solution.py:421
  (1 shorter events, 0.0 us)
Async XLA Ops:
  0.6 9.5 %copy-start.2 = (s32[1,4]{1,0:T(1,128)S(1)}, s32[1,4]{1,0:T(1,128)}, u32[]{:S(2)}) copy-start(s32[1,4]{1,0:T(1,128)} %refs_0_.5) | copy-start | bytes 52
  0.6 9.5 %copy-start.1 = (f32[128,32]{0,1:T(8,128)S(1)}, f32[128,32]{0,1:T(8,128)}, u32[]{:S(2)}) copy-start(f32[128,32]{0,1:T(8,128)} %param.13) | copy-start | bytes 49156
  0.7 7.5 %collective-permute-start.1 = (bf16[128,512]{1,0:T(8,128)(2,1)}, bf16[128,512]{1,0:T(8,128)(2,1)S(1)}, u32[]{:S(2)}, u32[]{:S(2)}) collective-permute-start(bf16[128,512]{1,0:T(8,128)(2,1)} %refs_4_.1), channel_id=1, source_target_pairs={{0,1},{1,0},{2,3},{3,2},{4,5},{5,4},{6,7},{7,6},{8,9},{9,8},{10,11... | collective-permute-start | bytes 393224 | tf_op jit(solution)/shard_map/ppermute | solution.py:449
  3.7 6.5 %collective-permute-start = (bf16[128,512]{1,0:T(8,128)(2,1)}, bf16[128,512]{1,0:T(8,128)(2,1)S(1)}, u32[]{:S(2)}, u32[]{:S(2)}) collective-permute-start(bf16[128,512]{1,0:T(8,128)(2,1)} %refs_2_.7), channel_id=1, source_target_pairs={{0,1},{1,0},{2,3},{3,2},{4,5},{5,4},{6,7},{7,6},{8,9},{9,8},{10,11... | collective-permute-start | bytes 393224 | tf_op jit(solution)/shard_map/ppermute | solution.py:449
  14.0 9.6 %collective-permute-start.5 = (bf16[2,128,512]{2,1,0:T(8,128)(2,1)S(1)}, bf16[2,128,512]{2,1,0:T(8,128)(2,1)S(1)}, u32[]{:S(2)}, u32[]{:S(2)}) collective-permute-start(bf16[2,128,512]{2,1,0:T(8,128)(2,1)S(1)} %get-tuple-element.20), channel_id=1, source_target_pairs={{0,1},{1,0},{2,3},{3,2},{4,5},{5,4},{6,7},{7,6},{8,9},{9,8},{10,11... | collective-permute-start | bytes 786440 | tf_op jit(solution)/shard_map/ppermute | solution.py:449
  15.8 11.0 %collective-permute-start.2 = (bf16[1024,128]{1,0:T(8,128)(2,1)S(1)}, bf16[1024,128]{1,0:T(8,128)(2,1)S(1)}, u32[]{:S(2)}, u32[]{:S(2)}) collective-permute-start(bf16[1024,128]{1,0:T(8,128)(2,1)S(1)} %get-tuple-element.25), channel_id=1, source_target_pairs={{0,8},{2,10},{4,12},{6,14},{8,0},{10,2},{12,4},{14,6},{16,24},{18,... | collective-permute-start | bytes 786440 | tf_op jit(solution)/shard_map/ppermute | solution.py:461
  17.3 17.7 %collective-permute-start.3 = (bf16[1024,128]{1,0:T(8,128)(2,1)S(1)}, bf16[1024,128]{1,0:T(8,128)(2,1)S(1)}, u32[]{:S(2)}, u32[]{:S(2)}) collective-permute-start(bf16[1024,128]{1,0:T(8,128)(2,1)S(1)} %get-tuple-element.26), channel_id=1, source_target_pairs={{0,4},{2,6},{4,0},{6,2},{8,12},{10,14},{12,8},{14,10},{16,20},{18,... | collective-permute-start | bytes 786440 | tf_op jit(solution)/shard_map/ppermute | solution.py:461
  18.9 16.2 %collective-permute-start.4 = (bf16[1024,128]{1,0:T(8,128)(2,1)S(1)}, bf16[1024,128]{1,0:T(8,128)(2,1)S(1)}, u32[]{:S(2)}, u32[]{:S(2)}) collective-permute-start(bf16[1024,128]{1,0:T(8,128)(2,1)S(1)} %get-tuple-element.27), channel_id=1, source_target_pairs={{0,12},{2,14},{4,8},{6,10},{8,4},{10,6},{12,0},{14,2},{16,28},{18,... | collective-permute-start | bytes 786440 | tf_op jit(solution)/shard_map/ppermute | solution.py:461
  23.6 13.6 %collective-permute-start.8 = (bf16[2,128,512]{2,1,0:T(8,128)(2,1)S(1)}, bf16[2,128,512]{2,1,0:T(8,128)(2,1)S(1)}, u32[]{:S(2)}, u32[]{:S(2)}) collective-permute-start(bf16[2,128,512]{2,1,0:T(8,128)(2,1)S(1)} %grads_total.1.refs_4_), channel_id=1, source_target_pairs={{0,12},{2,14},{4,8},{6,10},{8,4},{10,6},{12,0},{14,2},{16,28},{18,... | collective-permute-start | bytes 786440 | tf_op jit(solution)/shard_map/ppermute | solution.py:461
  26.2 14.6 %collective-permute-start.7 = (bf16[2,128,512]{2,1,0:T(8,128)(2,1)S(1)}, bf16[2,128,512]{2,1,0:T(8,128)(2,1)S(1)}, u32[]{:S(2)}, u32[]{:S(2)}) collective-permute-start(bf16[2,128,512]{2,1,0:T(8,128)(2,1)S(1)} %grads_total.1.refs_4_), channel_id=1, source_target_pairs={{0,4},{2,6},{4,0},{6,2},{8,12},{10,14},{12,8},{14,10},{16,20},{18,... | collective-permute-start | bytes 786440 | tf_op jit(solution)/shard_map/ppermute | solution.py:461
  26.7 14.1 %collective-permute-start.6 = (bf16[2,128,512]{2,1,0:T(8,128)(2,1)S(1)}, bf16[2,128,512]{2,1,0:T(8,128)(2,1)S(1)}, u32[]{:S(2)}, u32[]{:S(2)}) collective-permute-start(bf16[2,128,512]{2,1,0:T(8,128)(2,1)S(1)} %grads_total.1.refs_4_), channel_id=1, source_target_pairs={{0,8},{2,10},{4,12},{6,14},{8,0},{10,2},{12,4},{14,6},{16,24},{18,... | collective-permute-start | bytes 786440 | tf_op jit(solution)/shard_map/ppermute | solution.py:461
  41.5 2.7 %collective-permute-start.9 = (bf16[512,1024]{1,0:T(8,128)(2,1)S(1)}, bf16[512,1024]{1,0:T(8,128)(2,1)S(1)}, u32[]{:S(2)}, u32[]{:S(2)}) collective-permute-start(bf16[512,1024]{1,0:T(8,128)(2,1)S(1)} %weight_other_core.1), channel_id=1, source_target_pairs={{0,2},{2,0},{4,6},{6,4},{8,10},{10,8},{12,14},{14,12},{16,18},{18,... | collective-permute-start | bytes 3145736 | tf_op jit(solution)/shard_map/ppermute | solution.py:457
  42.3 14.1 %copy-start = (bf16[128,512]{1,0:T(8,128)(2,1)S(1)}, bf16[128,512]{1,0:T(8,128)(2,1)}, u32[]{:S(2)}) copy-start(bf16[128,512]{1,0:T(8,128)(2,1)} %refs_2_.7) | copy-start | bytes 393220
  44.4 9.3 %collective-permute-start.11 = (bf16[128,1024]{1,0:T(8,128)(2,1)S(1)}, bf16[128,1024]{1,0:T(8,128)(2,1)S(1)}, u32[]{:S(2)}, u32[]{:S(2)}) collective-permute-start(bf16[128,1024]{1,0:T(8,128)(2,1)S(1)} %get-tuple-element.32), channel_id=1, source_target_pairs={{0,1},{1,0},{2,3},{3,2},{4,5},{5,4},{6,7},{7,6},{8,9},{9,8},{10,11... | collective-permute-start | bytes 786440 | tf_op jit(solution)/shard_map/ppermute | solution.py:449
  45.0 13.4 %collective-permute-start.10 = (bf16[128,1024]{1,0:T(8,128)(2,1)S(1)}, bf16[128,1024]{1,0:T(8,128)(2,1)S(1)}, u32[]{:S(2)}, u32[]{:S(2)}) collective-permute-start(bf16[128,1024]{1,0:T(8,128)(2,1)S(1)} %get-tuple-element.30), channel_id=1, source_target_pairs={{0,1},{1,0},{2,3},{3,2},{4,5},{5,4},{6,7},{7,6},{8,9},{9,8},{10,11... | collective-permute-start | bytes 786440 | tf_op jit(solution)/shard_map/ppermute | solution.py:449
  53.7 13.2 %collective-permute-start.12 = (bf16[128,1024]{1,0:T(8,128)(2,1)S(1)}, bf16[128,1024]{1,0:T(8,128)(2,1)S(1)}, u32[]{:S(2)}, u32[]{:S(2)}) collective-permute-start(bf16[128,1024]{1,0:T(8,128)(2,1)S(1)} %relay_total.1), channel_id=1, source_target_pairs={{0,16},{2,18},{4,20},{6,22},{8,24},{10,26},{12,28},{14,30},{16,0},... | collective-permute-start | bytes 786440 | tf_op jit(solution)/shard_map/ppermute | solution.py:454

commit v4 on v3

--- a/solution.py
+++ b/solution.py
@@ -16,18 +16,18 @@
 CORES = 2
 MIDDLE = 2
 NEAR = 2
-PARTS = 1
+PARTS = 2
 PART_HEADS = KEY_VALUE_HEADS // PARTS
 PART_WIDTH = PART_HEADS * HEAD_SIZE
-OWN_MIB, VISITING_MIB, PREPARE_MIB = 32, 32, 32
-
-
-def limit(mib):
-    return pltpu.CompilerParams(vmem_limit_bytes=mib * 2**20)
-
-
-PARAMS = limit(32)
+PARAMS = pltpu.CompilerParams(vmem_limit_bytes=32 * 2**20)
 COST = pl.CostEstimate(flops=1024, bytes_accessed=1024, transcendentals=0)
+PART_TOTAL_WEIGHT = 10
+
+
+def weighed(amount):
+    return pl.CostEstimate(flops=amount * 10**9, bytes_accessed=amount * 2**20, transcendentals=0)
+
+
 WHOLE = pl.BlockSpec(memory_space=pltpu.VMEM)
 FAR = pl.BlockSpec(memory_space=pltpu.HBM)
 SCALARS = pl.BlockSpec(memory_space=pltpu.SMEM)
@@ -81,8 +81,7 @@
 def block_kernel(first, part, ctx_count, step, *refs):
     lengths_ref, q_hbm, do_hbm, k_in, v_in, lse_ref, delta_ref, ds_ref, grad_ref = refs[:9]
     q_buf, do_buf, sems = refs[9:12]
-    count = grad_ref.shape[2] // HEAD_SIZE
-    heads = range(part * count, (part + 1) * count)
+    heads = range(part * PART_HEADS, (part + 1) * PART_HEADS)
     width = GROUP * HEAD_SIZE
     k_ref, v_ref = k_in, v_in
     small = []
@@ -145,7 +144,7 @@
 ):
     rows = queries.shape[0]
     key_rows, half = keys.shape
-    count = KEY_VALUE_HEADS if first else PART_HEADS
+    count = PART_HEADS
     buffer = pltpu.VMEM((count, rows, GROUP * HEAD_SIZE), jnp.bfloat16)
     small = pltpu.VMEM((key_rows, half), jnp.bfloat16)
     near = FAR if first else WHOLE
@@ -159,15 +158,14 @@
         ],
         scratch_shapes=[buffer, buffer, pltpu.SemaphoreType.DMA((2, count))]
         + ([small, small, pltpu.SemaphoreType.DMA((2,))] if first else []),
-        compiler_params=limit(OWN_MIB if first else VISITING_MIB),
+        compiler_params=PARAMS,
         cost_estimate=COST,
         name="own_keys" if first else "visiting_keys",
     )(lengths, queries, output_gradient, keys, values, lse, delta)
 
 
-def query_kernel(steps, *refs):
-    own_ref, k_refs, out_ref = refs[0], refs[-2 - steps : -1], refs[-1]
-    visiting = refs[1 : 1 + steps * PARTS]
+def query_kernel(count, *refs):
+    ds_refs, k_refs, out_ref = refs[: -1 - count], refs[-1 - count : -1], refs[-1]
     rows = out_ref.shape[0]
     for g in range(KEY_VALUE_HEADS):
         columns = slice(g * HEAD_SIZE, (g + 1) * HEAD_SIZE)
@@ -175,20 +173,20 @@
         part, at = divmod(g, PART_HEADS)
         for h in range(GROUP):
             head = g * GROUP + h
-            scores = [own_ref[:, head * rows : (head + 1) * rows]]
-            for ref in visiting[part * steps : (part + 1) * steps]:
-                inner = at * GROUP + h
-                scores.append(ref[:, inner * rows : (inner + 1) * rows])
+            inner = at * GROUP + h
+            scores = [
+                ref[:, inner * rows : (inner + 1) * rows]
+                for ref in ds_refs[part * count : (part + 1) * count]
+            ]
             out_ref[:, head * HEAD_SIZE : (head + 1) * HEAD_SIZE] = (
                 dot(jnp.concatenate(scores, axis=0), keys, TN) * SCALE
             ).astype(out_ref.dtype)
 
 
-def query_call(own_scores, visiting_scores, keys, rows):
-    steps = len(keys) - 1
-    operands = [own_scores] + visiting_scores + keys
-    return pl.pallas_call(
-        functools.partial(query_kernel, steps),
+def query_call(scores, keys, rows):
+    operands = [value for part in scores for value in part] + keys
+    return pl.pallas_call(
+        functools.partial(query_kernel, len(keys)),
         in_specs=[WHOLE] * len(operands),
         out_specs=WHOLE,
         out_shape=shape((rows, QUERY_HEADS * HEAD_SIZE), jnp.bfloat16),
@@ -201,6 +199,10 @@
 def group_place():
     dp_rank = lax.axis_index("dp")
     return lax.rem(lax.div(dp_rank, CORES), MIDDLE), lax.rem(lax.div(dp_rank, CORES * MIDDLE), NEAR)
+
+
+def after(values, others):
+    return lax.optimization_barrier((values, others))[0]
 
 
 def prepare_kernel(far, ctx_count, turn, *refs):
@@ -274,7 +276,7 @@
             if turn
             else []
         ),
-        compiler_params=limit(PREPARE_MIB),
+        compiler_params=PARAMS,
         cost_estimate=COST,
         name="prepare",
     )(*operands)
@@ -288,20 +290,19 @@
     return pieces, delta
 
 
-def add_kernel(part, own_ref, *refs):
-    cut = slice(part * PART_WIDTH, (part + 1) * PART_WIDTH)
-    total = own_ref[:, :, cut]
+def add_kernel(own_ref, *refs):
+    total = own_ref[...]
     for back_ref in refs[:-1]:
         total = total + back_ref[...].astype(jnp.float32)
     refs[-1][...] = total.astype(refs[-1].dtype)
 
 
-def add_call(part, own, back):
-    return pl.pallas_call(
-        functools.partial(add_kernel, part),
+def add_call(own, back):
+    return pl.pallas_call(
+        add_kernel,
         in_specs=[WHOLE] * (1 + len(back)),
         out_specs=WHOLE,
-        out_shape=shape(back[0].shape, jnp.bfloat16),
+        out_shape=shape(own.shape, jnp.bfloat16),
         compiler_params=PARAMS,
         cost_estimate=COST,
         name="grads_total",
@@ -403,30 +404,53 @@
     )(away, *arrived)
 
 
-def final_kernel(*refs):
+def part_total_kernel(*refs):
+    total = refs[0][...]
+    for piece in refs[1:-1]:
+        total = total + piece[...].astype(jnp.float32)
+    refs[-1][...] = total
+
+
+def part_total_call(own, arrived):
+    return pl.pallas_call(
+        part_total_kernel,
+        in_specs=[WHOLE] * (1 + len(arrived)),
+        out_specs=WHOLE,
+        out_shape=shape(own.shape, jnp.float32),
+        compiler_params=PARAMS,
+        cost_estimate=weighed(PART_TOTAL_WEIGHT),
+        name="part_total",
+    )(own, *arrived)
+
+
+def final_kernel(near_count, counts, *refs):
     key_ref, value_ref = refs[-2:]
-    count = (len(refs) - 2) // PARTS
-    for part in range(PARTS):
-        pieces = refs[part * count : (part + 1) * count]
-        total = pieces[0][...]
-        for piece in pieces[1:]:
+    near_refs, rest = refs[:near_count], refs[near_count:-2]
+    width = 2 * PART_WIDTH
+    for part, count in enumerate(counts):
+        total = rest[0][...]
+        for piece in rest[1:count]:
             total = total + piece[...].astype(jnp.float32)
+        rest = rest[count:]
+        for near in near_refs:
+            total = total + near[:, part * width : (part + 1) * width].astype(jnp.float32)
         at = slice(part * PART_WIDTH, (part + 1) * PART_WIDTH)
         key_ref[:, at] = total[:, :PART_WIDTH]
         value_ref[:, at] = total[:, PART_WIDTH:]
 
 
-def final_call(pieces):
-    block = pieces[0].shape[0]
-    return pl.pallas_call(
-        final_kernel,
-        in_specs=[WHOLE] * len(pieces),
+def final_call(near, pieces):
+    operands = list(near) + [value for part in pieces for value in part]
+    block = operands[0].shape[0]
+    return pl.pallas_call(
+        functools.partial(final_kernel, len(near), tuple(len(part) for part in pieces)),
+        in_specs=[WHOLE] * len(operands),
         out_specs=[WHOLE] * 2,
         out_shape=[shape((block, KEY_VALUE_HEADS * HEAD_SIZE), jnp.float32)] * 2,
         compiler_params=PARAMS,
         cost_estimate=COST,
         name="weight_total",
-    )(*pieces)
+    )(*operands)
 
 
 def local(
@@ -488,33 +512,53 @@
             sums,
         )
 
-    visiting_scores = []
-    sent = []
+    own_scores, own, back, part_scores = [], [], [], []
+    scores, grads = block(True, 0, 0, far_keys, far_values, delta)
+    own_scores.append(scores)
+    own.append(grads)
+    delta = after(delta, grads)
     for part in range(PARTS):
+        part_scores.append([])
+        back.append([])
         for step in range(1, ctx_count):
             scores, grads = block(False, part, step, *visiting[step - 1], delta)
-            visiting_scores.append(scores)
-            sent.append(grads)
-    back = [over_ctx(grads, -1 - i % (ctx_count - 1)) for i, grads in enumerate(sent)]
-    delta, sent = lax.optimization_barrier((delta, sent))
-    own_scores, own = block(True, 0, 0, far_keys, far_values, delta)
-    summands = []
+            part_scores[part].append(scores)
+            back[part].append(over_ctx(grads, -step))
+        delta = after(delta, grads)
+    for part in range(1, PARTS):
+        scores, grads = block(True, part, 0, far_keys, far_values, delta)
+        own_scores.append(scores)
+        own.append(grads)
+    back[0], tokens = lax.optimization_barrier((back[0], tokens))
+    totals, gathered = [], []
     for part in range(PARTS):
-        grads = add_call(part, own, back[part * (ctx_count - 1) : (part + 1) * (ctx_count - 1)])
-        group_grads = [over_group(grads, i) if i else grads for i in range(len(tokens))]
+        totals.append(add_call(own[part], back[part]))
+        gathered.append([over_group(totals[part], i) for i in range(1, len(tokens))])
+    near, summands = [], []
+    for part in range(PARTS):
+        group_grads = [totals[part]] + gathered[part]
         theirs = weight_call(True, tokens, group_grads, jnp.bfloat16)
         arriving = over_cores(theirs)
         mine = weight_call(False, tokens, group_grads, jnp.float32)
         total, away, *blocks = chip_call(far, ctx_count, mine, arriving)
         away_arrived = [over_ctx(value, s) for s, value in enumerate(blocks[1::2], 1)]
-        near_arrived = [over_ctx(value, s) for s, value in enumerate(blocks[0::2], 1)]
+        near.append(blocks[0::2])
         relayed = relay_call(far, away, away_arrived)
-        summands += [total] + near_arrived
-        summands += [over_far(value, s) for s, value in enumerate(relayed, 1)]
+        arrived = [over_far(value, s) for s, value in enumerate(relayed, 1)]
+        if part < PARTS - 1:
+            summands.append([part_total_call(total, arrived)])
+        else:
+            summands.append([total] + arrived)
+    near = after(near, relayed)
+    near = [
+        over_ctx(jnp.concatenate(values, axis=1), s) for s, values in enumerate(zip(*near), 1)
+    ]
     query_gradient = query_call(
-        own_scores, visiting_scores, [saved_keys] + [pair[0] for pair in visiting], rows
+        [[value] + values for value, values in zip(own_scores, part_scores)],
+        [saved_keys] + [pair[0] for pair in visiting],
+        rows,
     )
-    key_weight_grad, value_weight_grad = final_call(summands)
+    key_weight_grad, value_weight_grad = final_call(near, summands)
     return query_gradient, key_weight_grad, value_weight_grad
 
 

time: 68 us -> 61.6 us (0.906)
  waiting for transfers between devices: 34.4 us -> 15.5 us
  starting transfers between devices: 16.8 us -> 25 us
  Pallas kernels: 15.9 us -> 19.3 us
    ppermute x6 -> x9, waiting for transfers between devices: 13.7 us -> 4.85 us  [over_group(): return lax.ppermute(value, 'dp', [(s, s ^ flip) for s in range(dp_count)])]
    ppermute x5 -> x7, waiting for transfers between devices: 10.3 us -> 3.65 us  [over_ctx(): return lax.ppermute(value, 'ctx', pairs)]
    ppermute x6 -> x9, starting transfers between devices: 7.04 us -> 10.7 us  [over_group(): return lax.ppermute(value, 'dp', [(s, s ^ flip) for s in range(dp_count)])]
    ppermute x5 -> x7, starting transfers between devices: 7.01 us -> 10.6 us  [over_ctx(): return lax.ppermute(value, 'ctx', pairs)]
    pallas_call x2 -> x4, Pallas kernels: 8.03 us -> 11 us  [block_call(): pl.pallas_call(functools.partial(block_kernel, first, part, ctx_count, st...]
    ppermute x1 -> x2, waiting for transfers between devices: 1.92 us -> 0.01 us  [over_cores(): return lax.ppermute(value, 'dp', [(s, s ^ 1) for s in range(dp_count)])]
    ppermute x1 -> x2, waiting for transfers between devices: 8.5 us -> 7.03 us  [over_far(): return lax.ppermute(value, 'dp', pairs)]
    ppermute x1 -> x2, starting transfers between devices: 2.65 us -> 3.51 us  [over_far(): return lax.ppermute(value, 'dp', pairs)]
  transfers between devices with their start and end apart: 13 -> 20, of which waited for: 9 -> 7; matrix products, arithmetic and copies ran while one was open for 0% -> 0% of each run, Pallas kernels for 15% -> 30%
where the time goes in v4:
time: 61.6 us; the launch traced here: 61.4 us
  starting transfers between devices  25 us (41%)
  Pallas kernels  19.3 us (31%)
  waiting for transfers between devices  15.5 us (25%)
  between operations  0.83 us (1%)
  local copies, waits for them, and re-layouts  0.66 us (1%)
    pallas_call x4, Pallas kernels, block_call(): pl.pallas_call(functools.partial(block_kernel, first, part, ctx_count, st...  11 us
    ppermute x9, starting transfers between devices, over_group(): return lax.ppermute(value, 'dp', [(s, s ^ flip) for s in range(dp_count)])  10.7 us
    ppermute x7, starting transfers between devices, over_ctx(): return lax.ppermute(value, 'ctx', pairs)  10.6 us
    ppermute x2, waiting for transfers between devices, over_far(): return lax.ppermute(value, 'dp', pairs)  7.03 us
    ppermute x9, waiting for transfers between devices, over_group(): return lax.ppermute(value, 'dp', [(s, s ^ flip) for s in range(dp_count)])  4.85 us
    ppermute x7, waiting for transfers between devices, over_ctx(): return lax.ppermute(value, 'ctx', pairs)  3.65 us
    pallas_call x1, Pallas kernels, prepare_call(): pl.pallas_call(functools.partial(prepare_kernel, far, ctx_count, turn), i...  3.63 us
    ppermute x2, starting transfers between devices, over_far(): return lax.ppermute(value, 'dp', pairs)  3.51 us
  transfers between devices with their start and end apart: 20, of which 7 were waited for; matrix products, arithmetic and copies ran while one was open for 0% of the time, Pallas kernels for 30%

profile of v4, /device:TPU:0, one launch (start us, length us, event | category | flops | bytes accessed | tf_op | source)
XLA Modules:
  0.0 61.4 jit_solution(14087565907078749859)
XLA Ops:
  0.6 3.0 %collective-permute-start = (bf16[128,512]{1,0:T(8,128)(2,1)}, bf16[128,512]{1,0:T(8,128)(2,1)S(1)}, u32[]{:S(2)}, u32[]{:S(2)}) collective-permute-start(bf16[128,512]{1,0:T(8,128)(2,1)} %refs_4_.5), channel_id=1, source_target_pairs={{0,1},{1,0},{2,3},{3,2},{4,5},{5,4},{6,7},{7,6},{8,9},{9,8},{10,11... | collective-permute-start | bytes 393224 | tf_op jit(solution)/shard_map/ppermute | solution.py:473
  3.6 0.1 collective-permute-start.1
  3.7 3.6 %prepare.1 = (bf16[1024,128]{1,0:T(8,128)(2,1)S(1)}, bf16[1024,128]{1,0:T(8,128)(2,1)S(1)}, bf16[1024,128]{1,0:T(8,128)(2,1)S(1)}, bf16[1024,128]{1,0:T(8,128)(2,1)S(1)}, f32[32,128]{1,0:T(8,128)S(1)}) custom-call(bf16[128,4096]{1,0:T(8,128)(2,1)} %refs_2_.9, bf16[128,4096]{1,0:T(8,128)(2,1)} %refs_1_.5, bf16[128,4096]{1,0:T(8,128)(2,1)} %refs_2_.5), custom_call_target="tpu_custom_call" | custom-call | flops 1024 | bytes 1024 | tf_op jit(solution)/shard_map/prepare/pallas_call | solution.py:265
  7.4 2.1 %collective-permute-start.3 = (bf16[1024,128]{1,0:T(8,128)(2,1)S(1)}, bf16[1024,128]{1,0:T(8,128)(2,1)S(1)}, u32[]{:S(2)}, u32[]{:S(2)}) collective-permute-start(bf16[1024,128]{1,0:T(8,128)(2,1)S(1)} %get-tuple-element.48), channel_id=1, source_target_pairs={{0,8},{2,10},{4,12},{6,14},{8,0},{10,2},{12,4},{14,6},{16,24},{18,... | collective-permute-start | bytes 786440 | tf_op jit(solution)/shard_map/ppermute | solution.py:485
  9.4 1.5 %collective-permute-start.4 = (bf16[1024,128]{1,0:T(8,128)(2,1)S(1)}, bf16[1024,128]{1,0:T(8,128)(2,1)S(1)}, u32[]{:S(2)}, u32[]{:S(2)}) collective-permute-start(bf16[1024,128]{1,0:T(8,128)(2,1)S(1)} %get-tuple-element.49), channel_id=1, source_target_pairs={{0,4},{2,6},{4,0},{6,2},{8,12},{10,14},{12,8},{14,10},{16,20},{18,... | collective-permute-start | bytes 786440 | tf_op jit(solution)/shard_map/ppermute | solution.py:485
  11.0 0.0 collective-permute-start.5
  11.0 0.7 %copy-done.2 = s32[1,4]{1,0:T(1,128)S(1)} copy-done((s32[1,4]{1,0:T(1,128)S(1)}, s32[1,4]{1,0:T(1,128)}, u32[]{:S(2)}) %copy-start.2) | copy-done | bytes 40
  11.6 2.8 %own_keys.2 = (bf16[128,2048]{1,0:T(8,128)(2,1)S(1)}, f32[2,128,256]{2,1,0:T(8,128)S(1)}) custom-call(s32[1,4]{1,0:T(1,128)S(1)} %copy-done.2, bf16[128,4096]{1,0:T(8,128)(2,1)} %refs_1_.9, bf16[128,4096]{1,0:T(8,128)(2,1)} %refs_2_.9, bf16[128,512]{1,0:T(8,128)(2,1)} %refs_4_.5, bf16[128,512]{1,0:T(8,128)(2,1)} %refs_4_.4, f32[32,128]{1,0:T(8,128)S(1)} %bitcast.1, ...), custom_call_target="tpu_custom_call" | custom-call | flops 1024 | bytes 1024 | tf_op jit(solution)/shard_map/own_keys/pallas_call | solution.py:151
  14.5 0.0 collective-permute-done.refs_3_.refs_5_
  14.5 0.0 collective-permute-done.1.refs_4_
  14.5 2.7 %visiting_keys.2 = (bf16[128,2048]{1,0:T(8,128)(2,1)S(1)}, bf16[2,128,256]{2,1,0:T(8,128)(2,1)S(1)}) custom-call(s32[1,4]{1,0:T(1,128)S(1)} %copy-done.2, bf16[128,4096]{1,0:T(8,128)(2,1)} %refs_1_.9, bf16[128,4096]{1,0:T(8,128)(2,1)} %refs_2_.9, bf16[128,512]{1,0:T(8,128)(2,1)S(1)} %collective-permute-done.refs_3_.refs_5_, ...), custom_call_target="tpu_custom_call" | custom-call | flops 1024 | bytes 1024 | tf_op jit(solution)/shard_map/visiting_keys/pallas_call | solution.py:151
  17.2 1.9 %collective-permute-start.2 = (bf16[2,128,256]{2,1,0:T(8,128)(2,1)S(1)}, bf16[2,128,256]{2,1,0:T(8,128)(2,1)S(1)}, u32[]{:S(2)}, u32[]{:S(2)}) collective-permute-start(bf16[2,128,256]{2,1,0:T(8,128)(2,1)S(1)} %get-tuple-element.41), channel_id=1, source_target_pairs={{0,1},{1,0},{2,3},{3,2},{4,5},{5,4},{6,7},{7,6},{8,9},{9,8},{10,11... | collective-permute-start | bytes 393224 | tf_op jit(solution)/shard_map/ppermute | solution.py:473
  19.1 2.7 %visiting_keys.3 = (bf16[128,2048]{1,0:T(8,128)(2,1)S(1)}, bf16[2,128,256]{2,1,0:T(8,128)(2,1)S(1)}) custom-call(s32[1,4]{1,0:T(1,128)S(1)} %copy-done.2, bf16[128,4096]{1,0:T(8,128)(2,1)} %refs_1_.9, bf16[128,4096]{1,0:T(8,128)(2,1)} %refs_2_.9, bf16[128,512]{1,0:T(8,128)(2,1)S(1)} %collective-permute-done.refs_3_.refs_5_, ...), custom_call_target="tpu_custom_call" | custom-call | flops 1024 | bytes 1024 | tf_op jit(solution)/shard_map/visiting_keys/pallas_call | solution.py:151
  21.8 0.2 collective-permute-start.10
  22.0 0.7 %collective-permute-done.2.refs_0_ = bf16[2,128,256]{2,1,0:T(8,128)(2,1)S(1)} collective-permute-done((bf16[2,128,256]{2,1,0:T(8,128)(2,1)S(1)}, bf16[2,128,256]{2,1,0:T(8,128)(2,1)S(1)}, u32[]{:S(2)}, u32[]{:S(2)}) %collective-permute-start.2) | collective-permute-done | bytes 131104 | tf_op jit(solution)/shard_map/ppermute | solution.py:473
  22.8 0.0 collective-permute-done.3.refs_1_
  22.8 0.0 collective-permute-done.4.refs_2_
  22.8 0.0 collective-permute-done.5.refs_3_
  22.8 1.5 %collective-permute-start.6 = (bf16[2,128,256]{2,1,0:T(8,128)(2,1)S(1)}, bf16[2,128,256]{2,1,0:T(8,128)(2,1)S(1)}, u32[]{:S(2)}, u32[]{:S(2)}) collective-permute-start(bf16[2,128,256]{2,1,0:T(8,128)(2,1)S(1)} %grads_total.2.refs_4_), channel_id=1, source_target_pairs={{0,8},{2,10},{4,12},{6,14},{8,0},{10,2},{12,4},{14,6},{16,24},{18,... | collective-permute-start | bytes 393224 | tf_op jit(solution)/shard_map/ppermute | solution.py:485
  24.3 1.5 %collective-permute-start.7 = (bf16[2,128,256]{2,1,0:T(8,128)(2,1)S(1)}, bf16[2,128,256]{2,1,0:T(8,128)(2,1)S(1)}, u32[]{:S(2)}, u32[]{:S(2)}) collective-permute-start(bf16[2,128,256]{2,1,0:T(8,128)(2,1)S(1)} %grads_total.2.refs_4_), channel_id=1, source_target_pairs={{0,4},{2,6},{4,0},{6,2},{8,12},{10,14},{12,8},{14,10},{16,20},{18,... | collective-permute-start | bytes 393224 | tf_op jit(solution)/shard_map/ppermute | solution.py:485
  25.8 0.5 collective-permute-start.8
  26.4 2.8 %own_keys.3 = (bf16[128,2048]{1,0:T(8,128)(2,1)S(1)}, f32[2,128,256]{2,1,0:T(8,128)S(1)}) custom-call(s32[1,4]{1,0:T(1,128)S(1)} %copy-done.2, bf16[128,4096]{1,0:T(8,128)(2,1)} %refs_1_.9, bf16[128,4096]{1,0:T(8,128)(2,1)} %refs_2_.9, bf16[128,512]{1,0:T(8,128)(2,1)} %refs_4_.5, bf16[128,512]{1,0:T(8,128)(2,1)} %refs_4_.4, f32[32,128]{1,0:T(8,128)S(1)} %bitcast.4, ...), custom_call_target="tpu_custom_call" | custom-call | flops 1024 | bytes 1024 | tf_op jit(solution)/shard_map/own_keys/pallas_call | solution.py:151
  29.2 0.0 collective-permute-done.10.refs_0_
  29.3 1.5 %collective-permute-start.11 = (bf16[2,128,256]{2,1,0:T(8,128)(2,1)S(1)}, bf16[2,128,256]{2,1,0:T(8,128)(2,1)S(1)}, u32[]{:S(2)}, u32[]{:S(2)}) collective-permute-start(bf16[2,128,256]{2,1,0:T(8,128)(2,1)S(1)} %grads_total.3.refs_4_), channel_id=1, source_target_pairs={{0,8},{2,10},{4,12},{6,14},{8,0},{10,2},{12,4},{14,6},{16,24},{18,... | collective-permute-start | bytes 393224 | tf_op jit(solution)/shard_map/ppermute | solution.py:485
  30.8 1.5 %collective-permute-start.12 = (bf16[2,128,256]{2,1,0:T(8,128)(2,1)S(1)}, bf16[2,128,256]{2,1,0:T(8,128)(2,1)S(1)}, u32[]{:S(2)}, u32[]{:S(2)}) collective-permute-start(bf16[2,128,256]{2,1,0:T(8,128)(2,1)S(1)} %grads_total.3.refs_4_), channel_id=1, source_target_pairs={{0,4},{2,6},{4,0},{6,2},{8,12},{10,14},{12,8},{14,10},{16,20},{18,... | collective-permute-start | bytes 393224 | tf_op jit(solution)/shard_map/ppermute | solution.py:485
  32.3 0.5 collective-permute-start.13
  32.8 0.0 collective-permute-done.7.refs_6_
  32.8 0.4 weight_other_core.2
  33.3 0.1 collective-permute-start.9
  33.3 0.9 %collective-permute-done.11.refs_5_ = bf16[2,128,256]{2,1,0:T(8,128)(2,1)S(1)} collective-permute-done((bf16[2,128,256]{2,1,0:T(8,128)(2,1)S(1)}, bf16[2,128,256]{2,1,0:T(8,128)(2,1)S(1)}, u32[]{:S(2)}, u32[]{:S(2)}) %collective-permute-start.11) | collective-permute-done | bytes 131104 | tf_op jit(solution)/shard_map/ppermute | solution.py:485
  34.3 1.4 %collective-permute-done.12.refs_6_ = bf16[2,128,256]{2,1,0:T(8,128)(2,1)S(1)} collective-permute-done((bf16[2,128,256]{2,1,0:T(8,128)(2,1)S(1)}, bf16[2,128,256]{2,1,0:T(8,128)(2,1)S(1)}, u32[]{:S(2)}, u32[]{:S(2)}) %collective-permute-start.12) | collective-permute-done | bytes 131104 | tf_op jit(solution)/shard_map/ppermute | solution.py:485
  35.7 2.5 %collective-permute-done.13.refs_7_ = bf16[2,128,256]{2,1,0:T(8,128)(2,1)S(1)} collective-permute-done((bf16[2,128,256]{2,1,0:T(8,128)(2,1)S(1)}, bf16[2,128,256]{2,1,0:T(8,128)(2,1)S(1)}, u32[]{:S(2)}, u32[]{:S(2)}) %collective-permute-start.13) | collective-permute-done | bytes 131104 | tf_op jit(solution)/shard_map/ppermute | solution.py:485
  38.2 0.4 weight_other_core.3
  38.6 0.1 collective-permute-start.14
  38.7 0.4 weight_this_core.2.mine_ref
  39.2 0.1 chip_total.2
  39.3 2.5 %collective-permute-start.17 = (bf16[128,512]{1,0:T(8,128)(2,1)S(1)}, bf16[128,512]{1,0:T(8,128)(2,1)S(1)}, u32[]{:S(2)}, u32[]{:S(2)}) collective-permute-start(bf16[128,512]{1,0:T(8,128)(2,1)S(1)} %get-tuple-element.65), channel_id=1, source_target_pairs={{0,1},{1,0},{2,3},{3,2},{4,5},{5,4},{6,7},{7,6},{8,9},{9,8},{10,11... | collective-permute-start | bytes 393224 | tf_op jit(solution)/shard_map/ppermute | solution.py:473
  41.8 0.4 weight_this_core.3.mine_ref
  42.3 0.1 chip_total.3
  42.4 0.9 %collective-permute-start.15 = (bf16[128,512]{1,0:T(8,128)(2,1)S(1)}, bf16[128,512]{1,0:T(8,128)(2,1)S(1)}, u32[]{:S(2)}, u32[]{:S(2)}) collective-permute-start(bf16[128,512]{1,0:T(8,128)(2,1)S(1)} %get-tuple-element.60), channel_id=1, source_target_pairs={{0,1},{1,0},{2,3},{3,2},{4,5},{5,4},{6,7},{7,6},{8,9},{9,8},{10,11... | collective-permute-start | bytes 393224 | tf_op jit(solution)/shard_map/ppermute | solution.py:473
  43.2 2.9 %collective-permute-done.17.refs_0_ = bf16[128,512]{1,0:T(8,128)(2,1)S(1)} collective-permute-done((bf16[128,512]{1,0:T(8,128)(2,1)S(1)}, bf16[128,512]{1,0:T(8,128)(2,1)S(1)}, u32[]{:S(2)}, u32[]{:S(2)}) %collective-permute-start.17) | collective-permute-done | bytes 131104 | tf_op jit(solution)/shard_map/ppermute | solution.py:473
  46.2 2.6 %collective-permute-start.18 = (bf16[128,512]{1,0:T(8,128)(2,1)S(1)}, bf16[128,512]{1,0:T(8,128)(2,1)S(1)}, u32[]{:S(2)}, u32[]{:S(2)}) collective-permute-start(bf16[128,512]{1,0:T(8,128)(2,1)S(1)} %relay_total.3), channel_id=1, source_target_pairs={{0,16},{2,18},{4,20},{6,22},{8,24},{10,26},{12,28},{14,30},{16,0},... | collective-permute-start | bytes 393224 | tf_op jit(solution)/shard_map/ppermute | solution.py:478
  48.8 1.7 %query_gradient.1 = bf16[128,4096]{1,0:T(8,128)(2,1)} custom-call(bf16[128,2048]{1,0:T(8,128)(2,1)S(1)} %get-tuple-element.37.refs_0_, bf16[128,2048]{1,0:T(8,128)(2,1)S(1)} %get-tuple-element.40.refs_1_, bf16[128,2048]{1,0:T(8,128)(2,1)S(1)} %get-tuple-element.45.refs_2_, bf16[128,2048]{1,0:T(8,128)(2,1)S(1)} %get-tuple-element.46.refs_3_, ...), custom_call_target="tpu_custom_call" | custom-call | flops 1024 | bytes 1024 | tf_op jit(solution)/shard_map/query_gradient/pallas_call | solution.py:188
  50.6 0.9 %collective-permute-start.19 = (bf16[128,512]{1,0:T(8,128)(2,1)S(1)}, bf16[128,512]{1,0:T(8,128)(2,1)S(1)}, u32[]{:S(2)}, u32[]{:S(2)}) collective-permute-start(bf16[128,512]{1,0:T(8,128)(2,1)S(1)} %relay_total.2), channel_id=1, source_target_pairs={{0,16},{2,18},{4,20},{6,22},{8,24},{10,26},{12,28},{14,30},{16,0},... | collective-permute-start | bytes 393224 | tf_op jit(solution)/shard_map/ppermute | solution.py:478
  51.5 2.0 %collective-permute-start.16 = (bf16[128,1024]{1,0:T(8,128)(2,1)S(1)}, bf16[128,1024]{1,0:T(8,128)(2,1)S(1)}, u32[]{:S(2)}, u32[]{:S(2)}) collective-permute-start(bf16[128,1024]{1,0:T(8,128)(2,1)S(1)} %pad_maximum_fusion), channel_id=1, source_target_pairs={{0,1},{1,0},{2,3},{3,2},{4,5},{5,4},{6,7},{7,6},{8,9},{9,8},{10,11... | collective-permute-start | bytes 786440 | tf_op jit(solution)/shard_map/ppermute | solution.py:473
  53.5 4.3 %collective-permute-done.18.refs_1_ = bf16[128,512]{1,0:T(8,128)(2,1)S(1)} collective-permute-done((bf16[128,512]{1,0:T(8,128)(2,1)S(1)}, bf16[128,512]{1,0:T(8,128)(2,1)S(1)}, u32[]{:S(2)}, u32[]{:S(2)}) %collective-permute-start.18) | collective-permute-done | bytes 131104 | tf_op jit(solution)/shard_map/ppermute | solution.py:478
  57.9 2.7 %collective-permute-done.19.refs_3_ = bf16[128,512]{1,0:T(8,128)(2,1)S(1)} collective-permute-done((bf16[128,512]{1,0:T(8,128)(2,1)S(1)}, bf16[128,512]{1,0:T(8,128)(2,1)S(1)}, u32[]{:S(2)}, u32[]{:S(2)}) %collective-permute-start.19) | collective-permute-done | bytes 131104 | tf_op jit(solution)/shard_map/ppermute | solution.py:478
  60.6 0.8 %weight_total.1 = (f32[128,512]{1,0:T(8,128)}, f32[128,512]{1,0:T(8,128)}) custom-call(bf16[128,1024]{1,0:T(8,128)(2,1)S(1)} %collective-permute-done.16.refs_0_, f32[128,512]{1,0:T(8,128)S(1)} %part_total.1.refs_1_, f32[128,512]{1,0:T(8,128)S(1)} %get-tuple-element.66.refs_2_, bf16[128,512]{1,0:T(8,128)(2,1)S(1)} %collective-permute-done.19.refs_3_), custom_call_target="tpu_custom_call" | custom-call | flops 1024 | bytes 1024 | tf_op jit(solution)/shard_map/weight_total/pallas_call | solution.py:445
  (17 shorter events, 0.2 us)
Async XLA Ops:
  0.6 13.9 %collective-permute-start = (bf16[128,512]{1,0:T(8,128)(2,1)}, bf16[128,512]{1,0:T(8,128)(2,1)S(1)}, u32[]{:S(2)}, u32[]{:S(2)}) collective-permute-start(bf16[128,512]{1,0:T(8,128)(2,1)} %refs_4_.5), channel_id=1, source_target_pairs={{0,1},{1,0},{2,3},{3,2},{4,5},{5,4},{6,7},{7,6},{8,9},{9,8},{10,11... | collective-permute-start | bytes 393224 | tf_op jit(solution)/shard_map/ppermute | solution.py:473
  3.6 10.9 %collective-permute-start.1 = (bf16[128,512]{1,0:T(8,128)(2,1)}, bf16[128,512]{1,0:T(8,128)(2,1)S(1)}, u32[]{:S(2)}, u32[]{:S(2)}) collective-permute-start(bf16[128,512]{1,0:T(8,128)(2,1)} %refs_4_.4), channel_id=1, source_target_pairs={{0,1},{1,0},{2,3},{3,2},{4,5},{5,4},{6,7},{7,6},{8,9},{9,8},{10,11... | collective-permute-start | bytes 393224 | tf_op jit(solution)/shard_map/ppermute | solution.py:473
  3.7 7.3 %copy-start.1 = (f32[128,32]{0,1:T(8,128)S(1)}, f32[128,32]{0,1:T(8,128)}, u32[]{:S(2)}) copy-start(f32[128,32]{0,1:T(8,128)} %param.13) | copy-start | bytes 49156
  7.4 15.4 %collective-permute-start.3 = (bf16[1024,128]{1,0:T(8,128)(2,1)S(1)}, bf16[1024,128]{1,0:T(8,128)(2,1)S(1)}, u32[]{:S(2)}, u32[]{:S(2)}) collective-permute-start(bf16[1024,128]{1,0:T(8,128)(2,1)S(1)} %get-tuple-element.48), channel_id=1, source_target_pairs={{0,8},{2,10},{4,12},{6,14},{8,0},{10,2},{12,4},{14,6},{16,24},{18,... | collective-permute-start | bytes 786440 | tf_op jit(solution)/shard_map/ppermute | solution.py:485
  9.4 13.3 %collective-permute-start.4 = (bf16[1024,128]{1,0:T(8,128)(2,1)S(1)}, bf16[1024,128]{1,0:T(8,128)(2,1)S(1)}, u32[]{:S(2)}, u32[]{:S(2)}) collective-permute-start(bf16[1024,128]{1,0:T(8,128)(2,1)S(1)} %get-tuple-element.49), channel_id=1, source_target_pairs={{0,4},{2,6},{4,0},{6,2},{8,12},{10,14},{12,8},{14,10},{16,20},{18,... | collective-permute-start | bytes 786440 | tf_op jit(solution)/shard_map/ppermute | solution.py:485
  11.0 11.8 %collective-permute-start.5 = (bf16[1024,128]{1,0:T(8,128)(2,1)S(1)}, bf16[1024,128]{1,0:T(8,128)(2,1)S(1)}, u32[]{:S(2)}, u32[]{:S(2)}) collective-permute-start(bf16[1024,128]{1,0:T(8,128)(2,1)S(1)} %get-tuple-element.50), channel_id=1, source_target_pairs={{0,12},{2,14},{4,8},{6,10},{8,4},{10,6},{12,0},{14,2},{16,28},{18,... | collective-permute-start | bytes 786440 | tf_op jit(solution)/shard_map/ppermute | solution.py:485
  11.0 0.7 %copy-start.2 = (s32[1,4]{1,0:T(1,128)S(1)}, s32[1,4]{1,0:T(1,128)}, u32[]{:S(2)}) copy-start(s32[1,4]{1,0:T(1,128)} %refs_0_.9) | copy-start | bytes 52
  17.2 5.5 %collective-permute-start.2 = (bf16[2,128,256]{2,1,0:T(8,128)(2,1)S(1)}, bf16[2,128,256]{2,1,0:T(8,128)(2,1)S(1)}, u32[]{:S(2)}, u32[]{:S(2)}) collective-permute-start(bf16[2,128,256]{2,1,0:T(8,128)(2,1)S(1)} %get-tuple-element.41), channel_id=1, source_target_pairs={{0,1},{1,0},{2,3},{3,2},{4,5},{5,4},{6,7},{7,6},{8,9},{9,8},{10,11... | collective-permute-start | bytes 393224 | tf_op jit(solution)/shard_map/ppermute | solution.py:473
  21.8 7.4 %collective-permute-start.10 = (bf16[2,128,256]{2,1,0:T(8,128)(2,1)S(1)}, bf16[2,128,256]{2,1,0:T(8,128)(2,1)S(1)}, u32[]{:S(2)}, u32[]{:S(2)}) collective-permute-start(bf16[2,128,256]{2,1,0:T(8,128)(2,1)S(1)} %get-tuple-element.43), channel_id=1, source_target_pairs={{0,1},{1,0},{2,3},{3,2},{4,5},{5,4},{6,7},{7,6},{8,9},{9,8},{10,11... | collective-permute-start | bytes 393224 | tf_op jit(solution)/shard_map/ppermute | solution.py:473
  22.8 9.5 %collective-permute-start.6 = (bf16[2,128,256]{2,1,0:T(8,128)(2,1)S(1)}, bf16[2,128,256]{2,1,0:T(8,128)(2,1)S(1)}, u32[]{:S(2)}, u32[]{:S(2)}) collective-permute-start(bf16[2,128,256]{2,1,0:T(8,128)(2,1)S(1)} %grads_total.2.refs_4_), channel_id=1, source_target_pairs={{0,8},{2,10},{4,12},{6,14},{8,0},{10,2},{12,4},{14,6},{16,24},{18,... | collective-permute-start | bytes 393224 | tf_op jit(solution)/shard_map/ppermute | solution.py:485
  24.3 8.5 %collective-permute-start.7 = (bf16[2,128,256]{2,1,0:T(8,128)(2,1)S(1)}, bf16[2,128,256]{2,1,0:T(8,128)(2,1)S(1)}, u32[]{:S(2)}, u32[]{:S(2)}) collective-permute-start(bf16[2,128,256]{2,1,0:T(8,128)(2,1)S(1)} %grads_total.2.refs_4_), channel_id=1, source_target_pairs={{0,4},{2,6},{4,0},{6,2},{8,12},{10,14},{12,8},{14,10},{16,20},{18,... | collective-permute-start | bytes 393224 | tf_op jit(solution)/shard_map/ppermute | solution.py:485
  25.8 7.0 %collective-permute-start.8 = (bf16[2,128,256]{2,1,0:T(8,128)(2,1)S(1)}, bf16[2,128,256]{2,1,0:T(8,128)(2,1)S(1)}, u32[]{:S(2)}, u32[]{:S(2)}) collective-permute-start(bf16[2,128,256]{2,1,0:T(8,128)(2,1)S(1)} %grads_total.2.refs_4_), channel_id=1, source_target_pairs={{0,12},{2,14},{4,8},{6,10},{8,4},{10,6},{12,0},{14,2},{16,28},{18,... | collective-permute-start | bytes 393224 | tf_op jit(solution)/shard_map/ppermute | solution.py:485
  29.3 5.0 %collective-permute-start.11 = (bf16[2,128,256]{2,1,0:T(8,128)(2,1)S(1)}, bf16[2,128,256]{2,1,0:T(8,128)(2,1)S(1)}, u32[]{:S(2)}, u32[]{:S(2)}) collective-permute-start(bf16[2,128,256]{2,1,0:T(8,128)(2,1)S(1)} %grads_total.3.refs_4_), channel_id=1, source_target_pairs={{0,8},{2,10},{4,12},{6,14},{8,0},{10,2},{12,4},{14,6},{16,24},{18,... | collective-permute-start | bytes 393224 | tf_op jit(solution)/shard_map/ppermute | solution.py:485
  30.8 5.0 %collective-permute-start.12 = (bf16[2,128,256]{2,1,0:T(8,128)(2,1)S(1)}, bf16[2,128,256]{2,1,0:T(8,128)(2,1)S(1)}, u32[]{:S(2)}, u32[]{:S(2)}) collective-permute-start(bf16[2,128,256]{2,1,0:T(8,128)(2,1)S(1)} %grads_total.3.refs_4_), channel_id=1, source_target_pairs={{0,4},{2,6},{4,0},{6,2},{8,12},{10,14},{12,8},{14,10},{16,20},{18,... | collective-permute-start | bytes 393224 | tf_op jit(solution)/shard_map/ppermute | solution.py:485
  32.3 5.9 %collective-permute-start.13 = (bf16[2,128,256]{2,1,0:T(8,128)(2,1)S(1)}, bf16[2,128,256]{2,1,0:T(8,128)(2,1)S(1)}, u32[]{:S(2)}, u32[]{:S(2)}) collective-permute-start(bf16[2,128,256]{2,1,0:T(8,128)(2,1)S(1)} %grads_total.3.refs_4_), channel_id=1, source_target_pairs={{0,12},{2,14},{4,8},{6,10},{8,4},{10,6},{12,0},{14,2},{16,28},{18,... | collective-permute-start | bytes 393224 | tf_op jit(solution)/shard_map/ppermute | solution.py:485
  33.3 5.9 %collective-permute-start.9 = (bf16[512,512]{1,0:T(8,128)(2,1)S(1)}, bf16[512,512]{1,0:T(8,128)(2,1)S(1)}, u32[]{:S(2)}, u32[]{:S(2)}) collective-permute-start(bf16[512,512]{1,0:T(8,128)(2,1)S(1)} %weight_other_core.2), channel_id=1, source_target_pairs={{0,2},{2,0},{4,6},{6,4},{8,10},{10,8},{12,14},{14,12},{16,18},{18,... | collective-permute-start | bytes 1572872 | tf_op jit(solution)/shard_map/ppermute | solution.py:481
  38.6 3.6 %collective-permute-start.14 = (bf16[512,512]{1,0:T(8,128)(2,1)S(1)}, bf16[512,512]{1,0:T(8,128)(2,1)S(1)}, u32[]{:S(2)}, u32[]{:S(2)}) collective-permute-start(bf16[512,512]{1,0:T(8,128)(2,1)S(1)} %weight_other_core.3), channel_id=1, source_target_pairs={{0,2},{2,0},{4,6},{6,4},{8,10},{10,8},{12,14},{14,12},{16,18},{18,... | collective-permute-start | bytes 1572872 | tf_op jit(solution)/shard_map/ppermute | solution.py:481
  39.3 6.9 %collective-permute-start.17 = (bf16[128,512]{1,0:T(8,128)(2,1)S(1)}, bf16[128,512]{1,0:T(8,128)(2,1)S(1)}, u32[]{:S(2)}, u32[]{:S(2)}) collective-permute-start(bf16[128,512]{1,0:T(8,128)(2,1)S(1)} %get-tuple-element.65), channel_id=1, source_target_pairs={{0,1},{1,0},{2,3},{3,2},{4,5},{5,4},{6,7},{7,6},{8,9},{9,8},{10,11... | collective-permute-start | bytes 393224 | tf_op jit(solution)/shard_map/ppermute | solution.py:473
  42.4 8.2 %collective-permute-start.15 = (bf16[128,512]{1,0:T(8,128)(2,1)S(1)}, bf16[128,512]{1,0:T(8,128)(2,1)S(1)}, u32[]{:S(2)}, u32[]{:S(2)}) collective-permute-start(bf16[128,512]{1,0:T(8,128)(2,1)S(1)} %get-tuple-element.60), channel_id=1, source_target_pairs={{0,1},{1,0},{2,3},{3,2},{4,5},{5,4},{6,7},{7,6},{8,9},{9,8},{10,11... | collective-permute-start | bytes 393224 | tf_op jit(solution)/shard_map/ppermute | solution.py:473
  46.2 2.7 %copy-start = (bf16[128,512]{1,0:T(8,128)(2,1)S(1)}, bf16[128,512]{1,0:T(8,128)(2,1)}, u32[]{:S(2)}) copy-start(bf16[128,512]{1,0:T(8,128)(2,1)} %refs_4_.5) | copy-start | bytes 393220
  46.2 11.7 %collective-permute-start.18 = (bf16[128,512]{1,0:T(8,128)(2,1)S(1)}, bf16[128,512]{1,0:T(8,128)(2,1)S(1)}, u32[]{:S(2)}, u32[]{:S(2)}) collective-permute-start(bf16[128,512]{1,0:T(8,128)(2,1)S(1)} %relay_total.3), channel_id=1, source_target_pairs={{0,16},{2,18},{4,20},{6,22},{8,24},{10,26},{12,28},{14,30},{16,0},... | collective-permute-start | bytes 393224 | tf_op jit(solution)/shard_map/ppermute | solution.py:478
  50.6 10.0 %collective-permute-start.19 = (bf16[128,512]{1,0:T(8,128)(2,1)S(1)}, bf16[128,512]{1,0:T(8,128)(2,1)S(1)}, u32[]{:S(2)}, u32[]{:S(2)}) collective-permute-start(bf16[128,512]{1,0:T(8,128)(2,1)S(1)} %relay_total.2), channel_id=1, source_target_pairs={{0,16},{2,18},{4,20},{6,22},{8,24},{10,26},{12,28},{14,30},{16,0},... | collective-permute-start | bytes 393224 | tf_op jit(solution)/shard_map/ppermute | solution.py:478
  51.5 9.1 %collective-permute-start.16 = (bf16[128,1024]{1,0:T(8,128)(2,1)S(1)}, bf16[128,1024]{1,0:T(8,128)(2,1)S(1)}, u32[]{:S(2)}, u32[]{:S(2)}) collective-permute-start(bf16[128,1024]{1,0:T(8,128)(2,1)S(1)} %pad_maximum_fusion), channel_id=1, source_target_pairs={{0,1},{1,0},{2,3},{3,2},{4,5},{5,4},{6,7},{7,6},{8,9},{9,8},{10,11... | collective-permute-start | bytes 786440 | tf_op jit(solution)/shard_map/ppermute | solution.py:473

commit v5 on v4

v5 whole, which is shorter than its diff:
```python
import functools
import math

import jax
import jax.numpy as jnp
from jax import lax
from jax.experimental import pallas as pl
from jax.experimental.pallas import tpu as pltpu
from jax.sharding import PartitionSpec as P

QUERY_HEADS = 32
KEY_VALUE_HEADS = 4
HEAD_SIZE = 128
GROUP = QUERY_HEADS // KEY_VALUE_HEADS
SCALE = 1.0 / math.sqrt(HEAD_SIZE)
CORES = 2
MIDDLE = 2
NEAR = 2
PARTS = 2
PARAMS = pltpu.CompilerParams(vmem_limit_bytes=32 * 2**20)
COST = pl.CostEstimate(flops=1024, bytes_accessed=1024, transcendentals=0)
EARLY = pl.CostEstimate(flops=10**10, bytes_accessed=1024, transcendentals=0)
WHOLE = pl.BlockSpec(memory_space=pltpu.VMEM)
FAR = pl.BlockSpec(memory_space=pltpu.HBM)
SCALARS = pl.BlockSpec(memory_space=pltpu.SMEM)

NT = (((1,), (1,)), ((), ()))
TN = (((0,), (0,)), ((), ()))
NN = (((1,), (0,)), ((), ()))


def dot(a, b, dims):
    return lax.dot_general(a, b, dims, preferred_element_type=jnp.float32)


def pinned(value):
    return pltpu.with_memory_space_constraint(value, pltpu.HBM)


def shape(dims, dtype):
    return jax.ShapeDtypeStruct(dims, dtype)


def rows_of_heads(block):
    return jnp.concatenate(
        [block[:, h * HEAD_SIZE : (h + 1) * HEAD_SIZE] for h in range(GROUP)], axis=0
    )


def allowed_mask(lengths_ref, ctx_count, rank, owner, keys, rows):
    key_pos = lax.broadcasted_iota(jnp.int32, (keys, rows), 0) * ctx_count + owner
    query_pos = lax.broadcasted_iota(jnp.int32, (keys, rows), 1) * ctx_count + rank
    allowed = key_pos <= query_pos
    end = jnp.int32(0)
    for j in range(lengths_ref.shape[1]):
        end = end + lengths_ref[0, j]
        allowed = allowed & ((end <= key_pos) == (end <= query_pos))
    return allowed


def delta_kernel(do_ref, out_hbm, delta_ref, buf, sems):
    width = GROUP * HEAD_SIZE
    copies = [
        pltpu.make_async_copy(out_hbm.at[:, g * width : (g + 1) * width], buf.at[g], sems.at[g])
        for g in range(KEY_VALUE_HEADS)
    ]
    for copy in copies:
        copy.start()
    pick = (
        lax.broadcasted_iota(jnp.int32, (GROUP, width), 1) // HEAD_SIZE
        == lax.broadcasted_iota(jnp.int32, (GROUP, width), 0)
    ).astype(jnp.bfloat16)
    for g in range(KEY_VALUE_HEADS):
        copies[g].wait()
        columns = slice(g * width, (g + 1) * width)
        product = do_ref[:, columns].astype(jnp.float32) * buf[g].astype(jnp.float32)
        high = product.astype(jnp.bfloat16)
        low = (product - high.astype(jnp.float32)).astype(jnp.bfloat16)
        delta_ref[g * GROUP : (g + 1) * GROUP, :] = dot(pick, high, NT) + dot(pick, low, NT)


def delta_call(output_gradient, attention_output):
    return pl.pallas_call(
        delta_kernel,
        in_specs=[WHOLE, FAR],
        out_specs=WHOLE,
        out_shape=shape((QUERY_HEADS, output_gradient.shape[0]), jnp.float32),
        scratch_shapes=[
            pltpu.VMEM(
                (KEY_VALUE_HEADS, output_gradient.shape[0], GROUP * HEAD_SIZE), jnp.bfloat16
            ),
            pltpu.SemaphoreType.DMA((KEY_VALUE_HEADS,)),
        ],
        compiler_params=PARAMS,
        cost_estimate=COST,
        name="delta",
    )(output_gradient, pinned(attention_output))


def block_kernel(ctx_count, step, *refs):
    lengths_ref, q_ref, do_ref, k_ref, v_ref, lse_ref, delta_ref, ds_ref, grad_ref = refs
    width = GROUP * HEAD_SIZE
    rank = lax.axis_index("ctx")
    owner = lax.rem(rank + ctx_count - step, ctx_count)
    rows = q_ref.shape[0]
    keys = k_ref.shape[0]
    allowed = allowed_mask(lengths_ref, ctx_count, rank, owner, keys, rows)
    for g in range(KEY_VALUE_HEADS):
        wide = slice(g * width, (g + 1) * width)
        q = rows_of_heads(q_ref[:, wide])
        do = rows_of_heads(do_ref[:, wide])
        group = slice(g * GROUP, (g + 1) * GROUP)
        delta = delta_ref[group, :]
        lse = lse_ref[group, :]
        columns = slice(g * HEAD_SIZE, (g + 1) * HEAD_SIZE)
        scores = dot(k_ref[:, columns], q, NT)
        grad_probs = dot(v_ref[:, columns], do, NT)
        probs_low = []
        grad_scores = []
        for h in range(GROUP):
            cut = slice(h * rows, (h + 1) * rows)
            probs = jnp.where(allowed, jnp.exp(scores[:, cut] * SCALE - lse[h : h + 1, :]), 0.0)
            grad_scores.append(
                (probs * (grad_probs[:, cut] - delta[h : h + 1, :])).astype(jnp.bfloat16)
            )
            probs_low.append(probs.astype(jnp.bfloat16))
        probs_low = jnp.concatenate(probs_low, axis=1)
        grad_scores = jnp.concatenate(grad_scores, axis=1)
        ds_ref[:, g * GROUP * rows : (g + 1) * GROUP * rows] = grad_scores
        grad_ref[0, :, columns] = (dot(grad_scores, q, NN) * SCALE).astype(grad_ref.dtype)
        grad_ref[1, :, columns] = dot(probs_low, do, NN).astype(grad_ref.dtype)


def block_call(step, ctx_count, lengths, queries, output_gradient, keys, values, lse, delta):
    rows = queries.shape[0]
    key_rows, half = keys.shape
    return pl.pallas_call(
        functools.partial(block_kernel, ctx_count, step),
        in_specs=[SCALARS] + [WHOLE] * 6,
        out_specs=[WHOLE] * 2,
        out_shape=[
            shape((key_rows, QUERY_HEADS * rows), jnp.bfloat16),
            shape((2, key_rows, half), jnp.bfloat16 if step else jnp.float32),
        ],
        compiler_params=PARAMS,
        cost_estimate=COST,
        name="visiting_keys" if step else "own_keys",
    )(lengths, queries, output_gradient, keys, values, lse, delta)


def query_kernel(count, *refs):
    ds_refs, k_refs, out_ref = refs[:count], refs[count:-1], refs[-1]
    rows = out_ref.shape[0]
    for g in range(KEY_VALUE_HEADS):
        columns = slice(g * HEAD_SIZE, (g + 1) * HEAD_SIZE)
        keys = jnp.concatenate([k[:, columns] for k in k_refs], axis=0)
        for head in range(g * GROUP, (g + 1) * GROUP):
            scores = jnp.concatenate(
                [ref[:, head * rows : (head + 1) * rows] for ref in ds_refs], axis=0
            )
            out_ref[:, head * HEAD_SIZE : (head + 1) * HEAD_SIZE] = (
                dot(scores, keys, TN) * SCALE
            ).astype(out_ref.dtype)


def query_call(scores, keys, rows):
    return pl.pallas_call(
        functools.partial(query_kernel, len(keys)),
        in_specs=[WHOLE] * (2 * len(keys)),
        out_specs=WHOLE,
        out_shape=shape((rows, QUERY_HEADS * HEAD_SIZE), jnp.bfloat16),
        compiler_params=PARAMS,
        cost_estimate=COST,
        name="query_gradient",
    )(*scores, *keys)


def after(values, others):
    return lax.optimization_barrier((values, others))[0]


def pieces_kernel(far, in_hbm, *refs):
    piece_refs, sems = refs[:-1], refs[-1]
    dp_rank = lax.axis_index("dp")
    y_rank = lax.rem(lax.div(dp_rank, CORES), MIDDLE)
    z_rank = lax.rem(lax.div(dp_rank, CORES * MIDDLE), NEAR)
    width = piece_refs[0].shape[1] // (CORES * far)
    copies = []
    for index, piece_ref in enumerate(piece_refs):
        y = lax.rem(y_rank + index // NEAR, MIDDLE)
        zl = lax.rem(z_rank + index % NEAR, NEAR)
        for core in range(CORES):
            for zh in range(far):
                start = (((zh * NEAR + zl) * MIDDLE + y) * CORES + core) * width
                to = (core * far + zh) * width
                copies.append(
                    pltpu.make_async_copy(
                        in_hbm.at[:, pl.ds(pl.multiple_of(start, width), width)],
                        piece_ref.at[:, to : to + width],
                        sems.at[len(copies)],
                    )
                )
    for copy in copies:
        copy.start()
    for copy in copies:
        copy.wait()


def pieces_call(normed, far):
    rows, width = normed.shape
    count = MIDDLE * NEAR
    return pl.pallas_call(
        functools.partial(pieces_kernel, far),
        in_specs=[FAR],
        out_specs=[WHOLE] * count,
        out_shape=[shape((rows, width // count), normed.dtype)] * count,
        scratch_shapes=[pltpu.SemaphoreType.DMA((count * CORES * far,))],
        compiler_params=PARAMS,
        cost_estimate=COST,
        name="pieces",
    )(pinned(normed))


def turn_kernel(*refs):
    out_ref = refs[-1]
    for at, ref in enumerate(refs[:-1]):
        rows = ref.shape[0]
        out_ref[:, at * rows : (at + 1) * rows] = ref[...].T


def turn_call(pieces):
    rows, width = pieces[0].shape
    return pl.pallas_call(
        turn_kernel,
        in_specs=[WHOLE] * len(pieces),
        out_specs=WHOLE,
        out_shape=shape((width, rows * len(pieces)), pieces[0].dtype),
        compiler_params=PARAMS,
        cost_estimate=COST,
        name="turn_pieces",
    )(*pieces)


def add_kernel(own_ref, *refs):
    out_refs = refs[-PARTS:]
    for part, out_ref in enumerate(out_refs):
        total = own_ref[part]
        for back_ref in refs[:-PARTS]:
            total = total + back_ref[part].astype(jnp.float32)
        out_ref[...] = total.astype(out_ref.dtype)


def add_call(own, back):
    return pl.pallas_call(
        add_kernel,
        in_specs=[WHOLE] * (1 + len(back)),
        out_specs=[WHOLE] * PARTS,
        out_shape=[shape(own.shape[1:], jnp.bfloat16)] * PARTS,
        compiler_params=PARAMS,
        cost_estimate=COST,
        name="grads_total",
    )(own, *back)


def weight_kernel(other, tokens_ref, *refs):
    g_refs, out_ref = refs[:-1], refs[-1]
    height = out_ref.shape[0]
    core = lax.rem(lax.axis_index("dp"), CORES)
    if other:
        core = 1 - core
    start = pl.multiple_of(core * height, height)
    block = min(height, 256)
    grads = jnp.concatenate([g[...] for g in g_refs], axis=0)
    for row in range(0, height, block):
        out_ref[row : row + block, :] = dot(
            tokens_ref[pl.ds(start + row, block), :], grads, NN
        ).astype(out_ref.dtype)


def weight_call(other, tokens, grads, dtype):
    return pl.pallas_call(
        functools.partial(weight_kernel, other),
        in_specs=[WHOLE] * (1 + len(grads)),
        out_specs=WHOLE,
        out_shape=shape((tokens.shape[0] // CORES, grads[0].shape[1]), dtype),
        compiler_params=PARAMS,
        cost_estimate=COST,
        name="weight_other_core" if other else "weight_this_core",
    )(tokens, *grads)


def chip_kernel(far, ctx_count, mine_ref, theirs_ref, own_ref, far_ref, *out_refs):
    block = own_ref.shape[0]
    z_rank = lax.div(lax.axis_index("dp"), CORES * MIDDLE * NEAR)
    x_rank = lax.axis_index("ctx")

    def total(z_steps, x_steps):
        z = lax.rem(z_rank + z_steps, far)
        x = lax.rem(x_rank + x_steps, ctx_count)
        at = pl.ds(pl.multiple_of((z * ctx_count + x) * block, block), block)
        return mine_ref[at, :] + theirs_ref[at, :].astype(jnp.float32)

    for x in range(1, ctx_count):
        near_out, far_out = out_refs[2 * x - 2 : 2 * x]
        for z in range(1, far):
            far_out[(z - 1) * block : z * block, :] = total(z, x).astype(far_out.dtype)
        near_out[...] = total(0, x).astype(near_out.dtype)
    for z in range(1, far):
        far_ref[(z - 1) * block : z * block, :] = total(z, 0)
    own_ref[...] = total(0, 0)


def chip_call(far, ctx_count, mine, theirs):
    height, columns = mine.shape
    block = height // (far * ctx_count)
    near = (block, columns)
    away = ((far - 1) * block, columns)
    return pl.pallas_call(
        functools.partial(chip_kernel, far, ctx_count),
        in_specs=[WHOLE] * 2,
        out_specs=[WHOLE] * (2 * ctx_count),
        out_shape=[shape(near, jnp.float32), shape(away, jnp.float32)]
        + [shape(near, jnp.bfloat16), shape(away, jnp.bfloat16)] * (ctx_count - 1),
        compiler_params=PARAMS,
        cost_estimate=COST,
        name="chip_total",
    )(mine, theirs)


def relay_kernel(far, far_ref, *refs):
    in_refs, out_refs = refs[: 1 - far], refs[1 - far :]
    block = out_refs[0].shape[0]
    for z, out_ref in enumerate(out_refs):
        at = slice(z * block, (z + 1) * block)
        total = far_ref[at, :]
        for in_ref in in_refs:
            total = total + in_ref[at, :].astype(jnp.float32)
        out_ref[...] = total.astype(out_ref.dtype)


def relay_call(far, away, arrived):
    height, columns = away.shape
    return pl.pallas_call(
        functools.partial(relay_kernel, far),
        in_specs=[WHOLE] * (1 + len(arrived)),
        out_specs=[WHOLE] * (far - 1),
        out_shape=[shape((height // (far - 1), columns), jnp.bfloat16)] * (far - 1),
        compiler_params=PARAMS,
        cost_estimate=COST,
        name="relay_total",
    )(away, *arrived)


def part_total_kernel(*refs):
    total = refs[0][...]
    for ref in refs[1:-1]:
        total = total + ref[...].astype(jnp.float32)
    refs[-1][...] = total


def part_total_call(own, arrived):
    return pl.pallas_call(
        part_total_kernel,
        in_specs=[WHOLE] * (1 + len(arrived)),
        out_specs=WHOLE,
        out_shape=shape(own.shape, jnp.float32),
        compiler_params=PARAMS,
        cost_estimate=EARLY,
        name="key_part_total",
    )(own, *arrived)


def final_kernel(near_count, key_in, *refs):
    key_ref, value_ref = refs[-2:]
    near_refs, value_refs = refs[:near_count], refs[near_count:-2]
    block = key_ref.shape[0]
    key, value = key_in[...], value_refs[0][...]
    for ref in value_refs[1:]:
        value = value + ref[...].astype(jnp.float32)
    for ref in near_refs:
        key = key + ref[:block, :].astype(jnp.float32)
        value = value + ref[block:, :].astype(jnp.float32)
    key_ref[...] = key
    value_ref[...] = value


def final_call(key, near, values):
    return pl.pallas_call(
        functools.partial(final_kernel, len(near)),
        in_specs=[WHOLE] * (1 + len(near) + len(values)),
        out_specs=[WHOLE] * 2,
        out_shape=[shape(key.shape, jnp.float32)] * 2,
        compiler_params=PARAMS,
        cost_estimate=COST,
        name="weight_total",
    )(key, *near, *values)


def local(
    normed_input,
    queries,
    saved_keys,
    saved_values,
    attention_output,
    saved_log_totals,
    output_gradient,
    document_lengths,
):
    rows = queries.shape[0]
    ctx_count = lax.axis_size("ctx")
    dp_count = lax.axis_size("dp")
    far = dp_count // (CORES * MIDDLE * NEAR)

    def over_ctx(value, steps):
        pairs = [(s, (s + steps) % ctx_count) for s in range(ctx_count)]
        return lax.ppermute(value, "ctx", pairs)

    def over_far(value, steps):
        stride = dp_count // far
        pairs = [(s, (s + steps * stride) % dp_count) for s in range(dp_count)]
        return lax.ppermute(value, "dp", pairs)

    def over_cores(value):
        return lax.ppermute(value, "dp", [(s, s ^ 1) for s in range(dp_count)])

    def over_group(value, index):
        flip = index // NEAR * CORES + index % NEAR * CORES * MIDDLE
        return lax.ppermute(value, "dp", [(s, s ^ flip) for s in range(dp_count)])

    visiting = [
        (over_ctx(saved_keys, step), over_ctx(saved_values, step)) for step in range(1, ctx_count)
    ]
    pieces = pieces_call(normed_input, far)
    pieces = [over_group(piece, index) if index else piece for index, piece in enumerate(pieces)]
    delta = delta_call(output_gradient, attention_output)
    lse = saved_log_totals.T
    block = functools.partial(
        block_call, ctx_count=ctx_count, lengths=document_lengths, queries=queries, lse=lse
    )
    scores, back = [], []
    for step in range(1, ctx_count):
        keys, values = visiting[step - 1]
        part_scores, grads = block(
            step, output_gradient=output_gradient, keys=keys, values=values, delta=delta
        )
        scores.append(part_scores)
        back.append(over_ctx(grads, -step))
    delta = after(delta, grads)
    own_scores, own = block(
        0, output_gradient=output_gradient, keys=saved_keys, values=saved_values, delta=delta
    )
    back, pieces = lax.optimization_barrier((back, pieces))
    totals = add_call(own, back)
    gathered = [
        [total if i == 0 else over_group(total, i) for i in range(len(pieces))] for total in totals
    ]
    own_scores = after(own_scores, totals)
    query_gradient = query_call(
        [own_scores] + scores, [saved_keys] + [pair[0] for pair in visiting], rows
    )
    tokens = turn_call(after(pieces, query_gradient))
    near, sums = [], []
    for group_grads in gathered:
        theirs = weight_call(True, tokens, group_grads, jnp.bfloat16)
        arriving = over_cores(theirs)
        mine = weight_call(False, tokens, group_grads, jnp.float32)
        total, away, *blocks = chip_call(far, ctx_count, mine, arriving)
        away_arrived = [over_ctx(value, s) for s, value in enumerate(blocks[1::2], 1)]
        near.append(blocks[0::2])
        relayed = relay_call(far, away, away_arrived)
        sums.append([total] + [over_far(value, s) for s, value in enumerate(relayed, 1)])
    near = after(near, relayed)
    near = [
        over_ctx(jnp.concatenate(values, axis=0), s) for s, values in enumerate(zip(*near), 1)
    ]
    key_part = part_total_call(sums[0][0], sums[0][1:])
    key_weight_grad, value_weight_grad = final_call(key_part, near, sums[1])
    return query_gradient, key_weight_grad, value_weight_grad


def solution(mesh):
    both = P(("dp", "ctx"), None)
    return jax.shard_map(
        local,
        mesh=mesh,
        in_specs=(both,) * 7 + (P("dp", None),),
        out_specs=(both,) * 3,
        check_vma=False,
    )
```

time: 61.6 us -> 57.4 us (0.932)
  Pallas kernels: 19.3 us -> 13.5 us
  starting transfers between devices: 25 us -> 26.7 us
    pallas_call x10, Pallas kernels: 17.3 us -> 11.4 us  [the longest x2 4.48 us: block_call(): pl.pallas_call(functools.partial(block_kernel, ctx_count, step), in_specs...]
    ppermute x9, starting transfers between devices: 10.7 us -> 12.7 us  [over_group(): return lax.ppermute(value, 'dp', [(s, s ^ flip) for s in range(dp_count)])]
    ppermute x7 -> x6, starting transfers between devices: 10.6 us -> 8.88 us  [over_ctx(): return lax.ppermute(value, 'ctx', pairs)]
    ppermute x2, starting transfers between devices: 3.51 us -> 5.04 us  [over_far(): return lax.ppermute(value, 'dp', pairs)]
    ppermute x9, waiting for transfers between devices: 4.85 us -> 3.43 us  [over_group(): return lax.ppermute(value, 'dp', [(s, s ^ flip) for s in range(dp_count)])]
    ppermute x7 -> x6, waiting for transfers between devices: 3.65 us -> 4.68 us  [over_ctx(): return lax.ppermute(value, 'ctx', pairs)]
  transfers between devices with their start and end apart: 20 -> 19, of which waited for: 7 -> 7; matrix products, arithmetic and copies ran while one was open for 0% -> 0% of each run, Pallas kernels for 30% -> 22%
where the time goes in v5:
time: 57.4 us; the launch traced here: 57.2 us
  starting transfers between devices  26.7 us (47%)
  waiting for transfers between devices  15.5 us (27%)
  Pallas kernels  13.5 us (24%)
  between operations  0.86 us (1%)
  local copies, waits for them, and re-layouts  0.63 us (1%)
    ppermute x9, starting transfers between devices, over_group(): return lax.ppermute(value, 'dp', [(s, s ^ flip) for s in range(dp_count)])  12.7 us
    ppermute x6, starting transfers between devices, over_ctx(): return lax.ppermute(value, 'ctx', pairs)  8.88 us
    ppermute x2, waiting for transfers between devices, over_far(): return lax.ppermute(value, 'dp', pairs)  7.39 us
    ppermute x2, starting transfers between devices, over_far(): return lax.ppermute(value, 'dp', pairs)  5.04 us
    ppermute x6, waiting for transfers between devices, over_ctx(): return lax.ppermute(value, 'ctx', pairs)  4.68 us
    pallas_call x2, Pallas kernels, block_call(): pl.pallas_call(functools.partial(block_kernel, ctx_count, step), in_specs...  4.48 us
    ppermute x9, waiting for transfers between devices, over_group(): return lax.ppermute(value, 'dp', [(s, s ^ flip) for s in range(dp_count)])  3.43 us
    pallas_call x1, Pallas kernels, delta_call(): pl.pallas_call(delta_kernel, in_specs=[WHOLE, FAR], out_specs=WHOLE, out_...  2.65 us
  transfers between devices with their start and end apart: 19, of which 7 were waited for; matrix products, arithmetic and copies ran while one was open for 0% of the time, Pallas kernels for 22%

profile of v5, /device:TPU:0, one launch (start us, length us, event | category | flops | bytes accessed | tf_op | source)
XLA Modules:
  0.0 57.2 jit_solution(10631565265386825601)
XLA Ops:
  0.6 3.0 %collective-permute-start = (bf16[128,512]{1,0:T(8,128)(2,1)}, bf16[128,512]{1,0:T(8,128)(2,1)S(1)}, u32[]{:S(2)}, u32[]{:S(2)}) collective-permute-start(bf16[128,512]{1,0:T(8,128)(2,1)} %refs_2_.5), channel_id=1, source_target_pairs={{0,1},{1,0},{2,3},{3,2},{4,5},{5,4},{6,7},{7,6},{8,9},{9,8},{10,11... | collective-permute-start | bytes 393224 | tf_op jit(solution)/shard_map/ppermute | solution.py:416
  3.6 0.1 collective-permute-start.1
  3.7 1.4 %pieces.1 = (bf16[128,1024]{1,0:T(8,128)(2,1)S(1)}, bf16[128,1024]{1,0:T(8,128)(2,1)S(1)}, bf16[128,1024]{1,0:T(8,128)(2,1)S(1)}, bf16[128,1024]{1,0:T(8,128)(2,1)S(1)}) custom-call(bf16[128,4096]{1,0:T(8,128)(2,1)} %in_hbm.1), custom_call_target="tpu_custom_call" | custom-call | flops 1024 | bytes 1024 | tf_op jit(solution)/shard_map/pieces/pallas_call | solution.py:212
  5.1 2.1 %collective-permute-start.3 = (bf16[128,1024]{1,0:T(8,128)(2,1)S(1)}, bf16[128,1024]{1,0:T(8,128)(2,1)S(1)}, u32[]{:S(2)}, u32[]{:S(2)}) collective-permute-start(bf16[128,1024]{1,0:T(8,128)(2,1)S(1)} %get-tuple-element.41), channel_id=1, source_target_pairs={{0,8},{2,10},{4,12},{6,14},{8,0},{10,2},{12,4},{14,6},{16,24},{18,... | collective-permute-start | bytes 786440 | tf_op jit(solution)/shard_map/ppermute | solution.py:428
  7.2 1.5 %collective-permute-start.4 = (bf16[128,1024]{1,0:T(8,128)(2,1)S(1)}, bf16[128,1024]{1,0:T(8,128)(2,1)S(1)}, u32[]{:S(2)}, u32[]{:S(2)}) collective-permute-start(bf16[128,1024]{1,0:T(8,128)(2,1)S(1)} %get-tuple-element.42), channel_id=1, source_target_pairs={{0,4},{2,6},{4,0},{6,2},{8,12},{10,14},{12,8},{14,10},{16,20},{18,... | collective-permute-start | bytes 786440 | tf_op jit(solution)/shard_map/ppermute | solution.py:428
  8.7 0.0 collective-permute-start.5
  8.8 2.6 %delta.1.refs_6_ = f32[32,128]{1,0:T(8,128)S(1)} custom-call(bf16[128,4096]{1,0:T(8,128)(2,1)S(1)} %copy-done, bf16[128,4096]{1,0:T(8,128)(2,1)} %out_hbm.1), custom_call_target="tpu_custom_call" | custom-call | flops 1024 | bytes 1024 | tf_op jit(solution)/shard_map/delta/pallas_call | solution.py:83
  11.4 0.0 copy-start.5
  11.4 0.0 collective-permute-done.refs_3_
  11.4 0.0 collective-permute-done.1.refs_4_
  11.5 0.6 %copy-done.5 = s32[1,4]{1,0:T(1,128)S(1)} copy-done((s32[1,4]{1,0:T(1,128)S(1)}, s32[1,4]{1,0:T(1,128)}, u32[]{:S(2)}) %copy-start.5) | copy-done | bytes 40
  12.1 2.2 %visiting_keys.1 = (bf16[128,4096]{1,0:T(8,128)(2,1)S(1)}, bf16[2,128,512]{2,1,0:T(8,128)(2,1)S(1)}) custom-call(s32[1,4]{1,0:T(1,128)S(1)} %copy-done.5, bf16[128,4096]{1,0:T(8,128)(2,1)S(1)} %copy-done.1, bf16[128,4096]{1,0:T(8,128)(2,1)S(1)} %copy-done, bf16[128,512]{1,0:T(8,128)(2,1)S(1)} %collective-permute-done.refs_3_, ...), custom_call_target="tpu_custom_call" | custom-call | flops 1024 | bytes 1024 | tf_op jit(solution)/shard_map/visiting_keys/pallas_call | solution.py:137
  14.3 1.8 %collective-permute-start.2 = (bf16[2,128,512]{2,1,0:T(8,128)(2,1)S(1)}, bf16[2,128,512]{2,1,0:T(8,128)(2,1)S(1)}, u32[]{:S(2)}, u32[]{:S(2)}) collective-permute-start(bf16[2,128,512]{2,1,0:T(8,128)(2,1)S(1)} %get-tuple-element.36), channel_id=1, source_target_pairs={{0,1},{1,0},{2,3},{3,2},{4,5},{5,4},{6,7},{7,6},{8,9},{9,8},{10,11... | collective-permute-start | bytes 786440 | tf_op jit(solution)/shard_map/ppermute | solution.py:416
  16.2 2.2 %own_keys.1 = (bf16[128,4096]{1,0:T(8,128)(2,1)S(1)}, f32[2,128,512]{2,1,0:T(8,128)S(1)}) custom-call(s32[1,4]{1,0:T(1,128)S(1)} %copy-done.5, bf16[128,4096]{1,0:T(8,128)(2,1)S(1)} %copy-done.1, bf16[128,4096]{1,0:T(8,128)(2,1)S(1)} %copy-done, bf16[128,512]{1,0:T(8,128)(2,1)S(1)} %copy-done.2, bf16[128,512]{1,0:T(8,128)(2,1)S(1)} %copy-done.3, ...), custom_call_target="tpu_custom_call" | custom-call | flops 1024 | bytes 1024 | tf_op jit(solution)/shard_map/own_keys/pallas_call | solution.py:137
  18.4 0.0 collective-permute-done.3.refs_1_
  18.4 1.6 %collective-permute-done.4.refs_2_ = bf16[128,1024]{1,0:T(8,128)(2,1)S(1)} collective-permute-done((bf16[128,1024]{1,0:T(8,128)(2,1)S(1)}, bf16[128,1024]{1,0:T(8,128)(2,1)S(1)}, u32[]{:S(2)}, u32[]{:S(2)}) %collective-permute-start.4) | collective-permute-done | bytes 262176 | tf_op jit(solution)/shard_map/ppermute | solution.py:428
  20.0 1.3 %collective-permute-done.2.refs_0_ = bf16[2,128,512]{2,1,0:T(8,128)(2,1)S(1)} collective-permute-done((bf16[2,128,512]{2,1,0:T(8,128)(2,1)S(1)}, bf16[2,128,512]{2,1,0:T(8,128)(2,1)S(1)}, u32[]{:S(2)}, u32[]{:S(2)}) %collective-permute-start.2) | collective-permute-done | bytes 262176 | tf_op jit(solution)/shard_map/ppermute | solution.py:416
  21.4 1.7 %collective-permute-start.6 = (bf16[128,512]{1,0:T(8,128)(2,1)S(1)}, bf16[128,512]{1,0:T(8,128)(2,1)S(1)}, u32[]{:S(2)}, u32[]{:S(2)}) collective-permute-start(bf16[128,512]{1,0:T(8,128)(2,1)S(1)} %get-tuple-element.45.refs_0_), channel_id=1, source_target_pairs={{0,8},{2,10},{4,12},{6,14},{8,0},{10,2},{12,4},{14,6},{16,24},{18,... | collective-permute-start | bytes 393224 | tf_op jit(solution)/shard_map/ppermute | solution.py:428
  23.0 1.5 %collective-permute-start.7 = (bf16[128,512]{1,0:T(8,128)(2,1)S(1)}, bf16[128,512]{1,0:T(8,128)(2,1)S(1)}, u32[]{:S(2)}, u32[]{:S(2)}) collective-permute-start(bf16[128,512]{1,0:T(8,128)(2,1)S(1)} %get-tuple-element.45.refs_0_), channel_id=1, source_target_pairs={{0,4},{2,6},{4,0},{6,2},{8,12},{10,14},{12,8},{14,10},{16,20},{18,... | collective-permute-start | bytes 393224 | tf_op jit(solution)/shard_map/ppermute | solution.py:428
  24.5 0.4 collective-permute-start.8
  24.9 1.6 %collective-permute-start.12 = (bf16[128,512]{1,0:T(8,128)(2,1)S(1)}, bf16[128,512]{1,0:T(8,128)(2,1)S(1)}, u32[]{:S(2)}, u32[]{:S(2)}) collective-permute-start(bf16[128,512]{1,0:T(8,128)(2,1)S(1)} %get-tuple-element.46.refs_0_), channel_id=1, source_target_pairs={{0,8},{2,10},{4,12},{6,14},{8,0},{10,2},{12,4},{14,6},{16,24},{18,... | collective-permute-start | bytes 393224 | tf_op jit(solution)/shard_map/ppermute | solution.py:428
  26.5 1.5 %collective-permute-start.13 = (bf16[128,512]{1,0:T(8,128)(2,1)S(1)}, bf16[128,512]{1,0:T(8,128)(2,1)S(1)}, u32[]{:S(2)}, u32[]{:S(2)}) collective-permute-start(bf16[128,512]{1,0:T(8,128)(2,1)S(1)} %get-tuple-element.46.refs_0_), channel_id=1, source_target_pairs={{0,4},{2,6},{4,0},{6,2},{8,12},{10,14},{12,8},{14,10},{16,20},{18,... | collective-permute-start | bytes 393224 | tf_op jit(solution)/shard_map/ppermute | solution.py:428
  28.0 0.0 collective-permute-done.6.refs_1_
  28.0 2.4 %collective-permute-start.14 = (bf16[128,512]{1,0:T(8,128)(2,1)S(1)}, bf16[128,512]{1,0:T(8,128)(2,1)S(1)}, u32[]{:S(2)}, u32[]{:S(2)}) collective-permute-start(bf16[128,512]{1,0:T(8,128)(2,1)S(1)} %get-tuple-element.46.refs_0_), channel_id=1, source_target_pairs={{0,12},{2,14},{4,8},{6,10},{8,4},{10,6},{12,0},{14,2},{16,28},{18,... | collective-permute-start | bytes 393224 | tf_op jit(solution)/shard_map/ppermute | solution.py:428
  30.4 1.7 %query_gradient.1 = bf16[128,4096]{1,0:T(8,128)(2,1)} custom-call(bf16[128,4096]{1,0:T(8,128)(2,1)S(1)} %get-tuple-element.47.refs_0_, bf16[128,4096]{1,0:T(8,128)(2,1)S(1)} %get-tuple-element.48.refs_1_, bf16[128,512]{1,0:T(8,128)(2,1)S(1)} %copy-done.2, bf16[128,512]{1,0:T(8,128)(2,1)S(1)} %collective-permute-done.refs_3_), custom_call_target="tpu_custom_call" | custom-call | flops 1024 | bytes 1024 | tf_op jit(solution)/shard_map/query_gradient/pallas_call | solution.py:167
  32.2 0.3 turn_pieces.1.tokens_ref
  32.5 0.0 collective-permute-done.7.refs_2_
  32.5 0.0 collective-permute-done.8.refs_3_
  32.5 0.4 weight_other_core.2
  33.0 0.1 collective-permute-start.9
  33.0 0.0 collective-permute-done.12.refs_1_
  33.0 0.4 collective-permute-done.13.refs_2_
  33.4 1.4 %collective-permute-done.14.refs_3_ = bf16[128,512]{1,0:T(8,128)(2,1)S(1)} collective-permute-done((bf16[128,512]{1,0:T(8,128)(2,1)S(1)}, bf16[128,512]{1,0:T(8,128)(2,1)S(1)}, u32[]{:S(2)}, u32[]{:S(2)}) %collective-permute-start.14) | collective-permute-done | bytes 131104 | tf_op jit(solution)/shard_map/ppermute | solution.py:428
  34.9 0.4 weight_other_core.3
  35.3 0.1 collective-permute-start.15
  35.4 0.4 weight_this_core.2.mine_ref
  35.8 0.1 chip_total.2
  35.9 1.5 %collective-permute-start.10 = (bf16[128,512]{1,0:T(8,128)(2,1)S(1)}, bf16[128,512]{1,0:T(8,128)(2,1)S(1)}, u32[]{:S(2)}, u32[]{:S(2)}) collective-permute-start(bf16[128,512]{1,0:T(8,128)(2,1)S(1)} %get-tuple-element.59), channel_id=1, source_target_pairs={{0,1},{1,0},{2,3},{3,2},{4,5},{5,4},{6,7},{7,6},{8,9},{9,8},{10,11... | collective-permute-start | bytes 393224 | tf_op jit(solution)/shard_map/ppermute | solution.py:416
  37.5 0.4 weight_this_core.3.mine_ref
  37.9 0.1 chip_total.3
  38.0 0.9 %collective-permute-start.16 = (bf16[128,512]{1,0:T(8,128)(2,1)S(1)}, bf16[128,512]{1,0:T(8,128)(2,1)S(1)}, u32[]{:S(2)}, u32[]{:S(2)}) collective-permute-start(bf16[128,512]{1,0:T(8,128)(2,1)S(1)} %get-tuple-element.63), channel_id=1, source_target_pairs={{0,1},{1,0},{2,3},{3,2},{4,5},{5,4},{6,7},{7,6},{8,9},{9,8},{10,11... | collective-permute-start | bytes 393224 | tf_op jit(solution)/shard_map/ppermute | solution.py:416
  38.9 3.4 %collective-permute-done.10.refs_0_ = bf16[128,512]{1,0:T(8,128)(2,1)S(1)} collective-permute-done((bf16[128,512]{1,0:T(8,128)(2,1)S(1)}, bf16[128,512]{1,0:T(8,128)(2,1)S(1)}, u32[]{:S(2)}, u32[]{:S(2)}) %collective-permute-start.10) | collective-permute-done | bytes 131104 | tf_op jit(solution)/shard_map/ppermute | solution.py:416
  42.3 2.7 %collective-permute-start.11 = (bf16[128,512]{1,0:T(8,128)(2,1)S(1)}, bf16[128,512]{1,0:T(8,128)(2,1)S(1)}, u32[]{:S(2)}, u32[]{:S(2)}) collective-permute-start(bf16[128,512]{1,0:T(8,128)(2,1)S(1)} %relay_total.2), channel_id=1, source_target_pairs={{0,16},{2,18},{4,20},{6,22},{8,24},{10,26},{12,28},{14,30},{16,0},... | collective-permute-start | bytes 393224 | tf_op jit(solution)/shard_map/ppermute | solution.py:421
  45.0 2.4 %collective-permute-start.18 = (bf16[128,512]{1,0:T(8,128)(2,1)S(1)}, bf16[128,512]{1,0:T(8,128)(2,1)S(1)}, u32[]{:S(2)}, u32[]{:S(2)}) collective-permute-start(bf16[128,512]{1,0:T(8,128)(2,1)S(1)} %relay_total.3), channel_id=1, source_target_pairs={{0,16},{2,18},{4,20},{6,22},{8,24},{10,26},{12,28},{14,30},{16,0},... | collective-permute-start | bytes 393224 | tf_op jit(solution)/shard_map/ppermute | solution.py:421
  47.4 1.5 %collective-permute-start.17 = (bf16[256,512]{1,0:T(8,128)(2,1)S(1)}, bf16[256,512]{1,0:T(8,128)(2,1)S(1)}, u32[]{:S(2)}, u32[]{:S(2)}) collective-permute-start(bf16[256,512]{1,0:T(8,128)(2,1)S(1)} %pad_maximum_fusion), channel_id=1, source_target_pairs={{0,1},{1,0},{2,3},{3,2},{4,5},{5,4},{6,7},{7,6},{8,9},{9,8},{10,11... | collective-permute-start | bytes 786440 | tf_op jit(solution)/shard_map/ppermute | solution.py:416
  49.0 4.8 %collective-permute-done.11.refs_1_ = bf16[128,512]{1,0:T(8,128)(2,1)S(1)} collective-permute-done((bf16[128,512]{1,0:T(8,128)(2,1)S(1)}, bf16[128,512]{1,0:T(8,128)(2,1)S(1)}, u32[]{:S(2)}, u32[]{:S(2)}) %collective-permute-start.11) | collective-permute-done | bytes 131104 | tf_op jit(solution)/shard_map/ppermute | solution.py:421
  53.8 2.5 %collective-permute-done.18.refs_2_ = bf16[128,512]{1,0:T(8,128)(2,1)S(1)} collective-permute-done((bf16[128,512]{1,0:T(8,128)(2,1)S(1)}, bf16[128,512]{1,0:T(8,128)(2,1)S(1)}, u32[]{:S(2)}, u32[]{:S(2)}) %collective-permute-start.18) | collective-permute-done | bytes 131104 | tf_op jit(solution)/shard_map/ppermute | solution.py:421
  56.4 0.8 %weight_total.1 = (f32[128,512]{1,0:T(8,128)}, f32[128,512]{1,0:T(8,128)}) custom-call(f32[128,512]{1,0:T(8,128)S(1)} %key_part_total.1.key_in, bf16[256,512]{1,0:T(8,128)(2,1)S(1)} %collective-permute-done.17.refs_0_, f32[128,512]{1,0:T(8,128)S(1)} %get-tuple-element.66.refs_1_, bf16[128,512]{1,0:T(8,128)(2,1)S(1)} %collective-permute-done.18.refs_2_), custom_call_target="tpu_custom_call" | custom-call | flops 1024 | bytes 1024 | tf_op jit(solution)/shard_map/weight_total/pallas_call | solution.py:388
  (20 shorter events, 0.2 us)
Async XLA Ops:
  0.6 8.1 %copy-start = (bf16[128,4096]{1,0:T(8,128)(2,1)S(1)}, bf16[128,4096]{1,0:T(8,128)(2,1)}, u32[]{:S(2)}) copy-start(bf16[128,4096]{1,0:T(8,128)(2,1)} %refs_2_.4) | copy-start | bytes 3145732
  0.6 10.8 %collective-permute-start = (bf16[128,512]{1,0:T(8,128)(2,1)}, bf16[128,512]{1,0:T(8,128)(2,1)S(1)}, u32[]{:S(2)}, u32[]{:S(2)}) collective-permute-start(bf16[128,512]{1,0:T(8,128)(2,1)} %refs_2_.5), channel_id=1, source_target_pairs={{0,1},{1,0},{2,3},{3,2},{4,5},{5,4},{6,7},{7,6},{8,9},{9,8},{10,11... | collective-permute-start | bytes 393224 | tf_op jit(solution)/shard_map/ppermute | solution.py:416
  3.6 7.8 %collective-permute-start.1 = (bf16[128,512]{1,0:T(8,128)(2,1)}, bf16[128,512]{1,0:T(8,128)(2,1)S(1)}, u32[]{:S(2)}, u32[]{:S(2)}) collective-permute-start(bf16[128,512]{1,0:T(8,128)(2,1)} %refs_4_.1), channel_id=1, source_target_pairs={{0,1},{1,0},{2,3},{3,2},{4,5},{5,4},{6,7},{7,6},{8,9},{9,8},{10,11... | collective-permute-start | bytes 393224 | tf_op jit(solution)/shard_map/ppermute | solution.py:416
  5.1 13.3 %collective-permute-start.3 = (bf16[128,1024]{1,0:T(8,128)(2,1)S(1)}, bf16[128,1024]{1,0:T(8,128)(2,1)S(1)}, u32[]{:S(2)}, u32[]{:S(2)}) collective-permute-start(bf16[128,1024]{1,0:T(8,128)(2,1)S(1)} %get-tuple-element.41), channel_id=1, source_target_pairs={{0,8},{2,10},{4,12},{6,14},{8,0},{10,2},{12,4},{14,6},{16,24},{18,... | collective-permute-start | bytes 786440 | tf_op jit(solution)/shard_map/ppermute | solution.py:428
  7.2 12.8 %collective-permute-start.4 = (bf16[128,1024]{1,0:T(8,128)(2,1)S(1)}, bf16[128,1024]{1,0:T(8,128)(2,1)S(1)}, u32[]{:S(2)}, u32[]{:S(2)}) collective-permute-start(bf16[128,1024]{1,0:T(8,128)(2,1)S(1)} %get-tuple-element.42), channel_id=1, source_target_pairs={{0,4},{2,6},{4,0},{6,2},{8,12},{10,14},{12,8},{14,10},{16,20},{18,... | collective-permute-start | bytes 786440 | tf_op jit(solution)/shard_map/ppermute | solution.py:428
  8.7 2.7 %copy-start.1 = (bf16[128,4096]{1,0:T(8,128)(2,1)S(1)}, bf16[128,4096]{1,0:T(8,128)(2,1)}, u32[]{:S(2)}) copy-start(bf16[128,4096]{1,0:T(8,128)(2,1)} %refs_1_.3) | copy-start | bytes 3145732
  8.7 2.7 %copy-start.4 = (f32[128,32]{0,1:T(8,128)S(1)}, f32[128,32]{0,1:T(8,128)}, u32[]{:S(2)}) copy-start(f32[128,32]{0,1:T(8,128)} %param.13) | copy-start | bytes 49156
  8.7 11.3 %collective-permute-start.5 = (bf16[128,1024]{1,0:T(8,128)(2,1)S(1)}, bf16[128,1024]{1,0:T(8,128)(2,1)S(1)}, u32[]{:S(2)}, u32[]{:S(2)}) collective-permute-start(bf16[128,1024]{1,0:T(8,128)(2,1)S(1)} %get-tuple-element.43), channel_id=1, source_target_pairs={{0,12},{2,14},{4,8},{6,10},{8,4},{10,6},{12,0},{14,2},{16,28},{18,... | collective-permute-start | bytes 786440 | tf_op jit(solution)/shard_map/ppermute | solution.py:428
  11.4 0.7 %copy-start.5 = (s32[1,4]{1,0:T(1,128)S(1)}, s32[1,4]{1,0:T(1,128)}, u32[]{:S(2)}) copy-start(s32[1,4]{1,0:T(1,128)} %refs_0_.3) | copy-start | bytes 52
  12.1 4.1 %copy-start.2 = (bf16[128,512]{1,0:T(8,128)(2,1)S(1)}, bf16[128,512]{1,0:T(8,128)(2,1)}, u32[]{:S(2)}) copy-start(bf16[128,512]{1,0:T(8,128)(2,1)} %refs_2_.5) | copy-start | bytes 393220
  12.1 4.1 %copy-start.3 = (bf16[128,512]{1,0:T(8,128)(2,1)S(1)}, bf16[128,512]{1,0:T(8,128)(2,1)}, u32[]{:S(2)}) copy-start(bf16[128,512]{1,0:T(8,128)(2,1)} %refs_4_.1) | copy-start | bytes 393220
  14.3 7.0 %collective-permute-start.2 = (bf16[2,128,512]{2,1,0:T(8,128)(2,1)S(1)}, bf16[2,128,512]{2,1,0:T(8,128)(2,1)S(1)}, u32[]{:S(2)}, u32[]{:S(2)}) collective-permute-start(bf16[2,128,512]{2,1,0:T(8,128)(2,1)S(1)} %get-tuple-element.36), channel_id=1, source_target_pairs={{0,1},{1,0},{2,3},{3,2},{4,5},{5,4},{6,7},{7,6},{8,9},{9,8},{10,11... | collective-permute-start | bytes 786440 | tf_op jit(solution)/shard_map/ppermute | solution.py:416
  21.4 6.7 %collective-permute-start.6 = (bf16[128,512]{1,0:T(8,128)(2,1)S(1)}, bf16[128,512]{1,0:T(8,128)(2,1)S(1)}, u32[]{:S(2)}, u32[]{:S(2)}) collective-permute-start(bf16[128,512]{1,0:T(8,128)(2,1)S(1)} %get-tuple-element.45.refs_0_), channel_id=1, source_target_pairs={{0,8},{2,10},{4,12},{6,14},{8,0},{10,2},{12,4},{14,6},{16,24},{18,... | collective-permute-start | bytes 393224 | tf_op jit(solution)/shard_map/ppermute | solution.py:428
  23.0 9.5 %collective-permute-start.7 = (bf16[128,512]{1,0:T(8,128)(2,1)S(1)}, bf16[128,512]{1,0:T(8,128)(2,1)S(1)}, u32[]{:S(2)}, u32[]{:S(2)}) collective-permute-start(bf16[128,512]{1,0:T(8,128)(2,1)S(1)} %get-tuple-element.45.refs_0_), channel_id=1, source_target_pairs={{0,4},{2,6},{4,0},{6,2},{8,12},{10,14},{12,8},{14,10},{16,20},{18,... | collective-permute-start | bytes 393224 | tf_op jit(solution)/shard_map/ppermute | solution.py:428
  24.5 8.0 %collective-permute-start.8 = (bf16[128,512]{1,0:T(8,128)(2,1)S(1)}, bf16[128,512]{1,0:T(8,128)(2,1)S(1)}, u32[]{:S(2)}, u32[]{:S(2)}) collective-permute-start(bf16[128,512]{1,0:T(8,128)(2,1)S(1)} %get-tuple-element.45.refs_0_), channel_id=1, source_target_pairs={{0,12},{2,14},{4,8},{6,10},{8,4},{10,6},{12,0},{14,2},{16,28},{18,... | collective-permute-start | bytes 393224 | tf_op jit(solution)/shard_map/ppermute | solution.py:428
  24.9 8.1 %collective-permute-start.12 = (bf16[128,512]{1,0:T(8,128)(2,1)S(1)}, bf16[128,512]{1,0:T(8,128)(2,1)S(1)}, u32[]{:S(2)}, u32[]{:S(2)}) collective-permute-start(bf16[128,512]{1,0:T(8,128)(2,1)S(1)} %get-tuple-element.46.refs_0_), channel_id=1, source_target_pairs={{0,8},{2,10},{4,12},{6,14},{8,0},{10,2},{12,4},{14,6},{16,24},{18,... | collective-permute-start | bytes 393224 | tf_op jit(solution)/shard_map/ppermute | solution.py:428
  26.5 6.9 %collective-permute-start.13 = (bf16[128,512]{1,0:T(8,128)(2,1)S(1)}, bf16[128,512]{1,0:T(8,128)(2,1)S(1)}, u32[]{:S(2)}, u32[]{:S(2)}) collective-permute-start(bf16[128,512]{1,0:T(8,128)(2,1)S(1)} %get-tuple-element.46.refs_0_), channel_id=1, source_target_pairs={{0,4},{2,6},{4,0},{6,2},{8,12},{10,14},{12,8},{14,10},{16,20},{18,... | collective-permute-start | bytes 393224 | tf_op jit(solution)/shard_map/ppermute | solution.py:428
  28.0 6.8 %collective-permute-start.14 = (bf16[128,512]{1,0:T(8,128)(2,1)S(1)}, bf16[128,512]{1,0:T(8,128)(2,1)S(1)}, u32[]{:S(2)}, u32[]{:S(2)}) collective-permute-start(bf16[128,512]{1,0:T(8,128)(2,1)S(1)} %get-tuple-element.46.refs_0_), channel_id=1, source_target_pairs={{0,12},{2,14},{4,8},{6,10},{8,4},{10,6},{12,0},{14,2},{16,28},{18,... | collective-permute-start | bytes 393224 | tf_op jit(solution)/shard_map/ppermute | solution.py:428
  33.0 2.9 %collective-permute-start.9 = (bf16[512,512]{1,0:T(8,128)(2,1)S(1)}, bf16[512,512]{1,0:T(8,128)(2,1)S(1)}, u32[]{:S(2)}, u32[]{:S(2)}) collective-permute-start(bf16[512,512]{1,0:T(8,128)(2,1)S(1)} %weight_other_core.2), channel_id=1, source_target_pairs={{0,2},{2,0},{4,6},{6,4},{8,10},{10,8},{12,14},{14,12},{16,18},{18,... | collective-permute-start | bytes 1572872 | tf_op jit(solution)/shard_map/ppermute | solution.py:424
  35.3 2.6 %collective-permute-start.15 = (bf16[512,512]{1,0:T(8,128)(2,1)S(1)}, bf16[512,512]{1,0:T(8,128)(2,1)S(1)}, u32[]{:S(2)}, u32[]{:S(2)}) collective-permute-start(bf16[512,512]{1,0:T(8,128)(2,1)S(1)} %weight_other_core.3), channel_id=1, source_target_pairs={{0,2},{2,0},{4,6},{6,4},{8,10},{10,8},{12,14},{14,12},{16,18},{18,... | collective-permute-start | bytes 1572872 | tf_op jit(solution)/shard_map/ppermute | solution.py:424
  35.9 6.4 %collective-permute-start.10 = (bf16[128,512]{1,0:T(8,128)(2,1)S(1)}, bf16[128,512]{1,0:T(8,128)(2,1)S(1)}, u32[]{:S(2)}, u32[]{:S(2)}) collective-permute-start(bf16[128,512]{1,0:T(8,128)(2,1)S(1)} %get-tuple-element.59), channel_id=1, source_target_pairs={{0,1},{1,0},{2,3},{3,2},{4,5},{5,4},{6,7},{7,6},{8,9},{9,8},{10,11... | collective-permute-start | bytes 393224 | tf_op jit(solution)/shard_map/ppermute | solution.py:416
  38.0 7.0 %collective-permute-start.16 = (bf16[128,512]{1,0:T(8,128)(2,1)S(1)}, bf16[128,512]{1,0:T(8,128)(2,1)S(1)}, u32[]{:S(2)}, u32[]{:S(2)}) collective-permute-start(bf16[128,512]{1,0:T(8,128)(2,1)S(1)} %get-tuple-element.63), channel_id=1, source_target_pairs={{0,1},{1,0},{2,3},{3,2},{4,5},{5,4},{6,7},{7,6},{8,9},{9,8},{10,11... | collective-permute-start | bytes 393224 | tf_op jit(solution)/shard_map/ppermute | solution.py:416
  42.3 11.5 %collective-permute-start.11 = (bf16[128,512]{1,0:T(8,128)(2,1)S(1)}, bf16[128,512]{1,0:T(8,128)(2,1)S(1)}, u32[]{:S(2)}, u32[]{:S(2)}) collective-permute-start(bf16[128,512]{1,0:T(8,128)(2,1)S(1)} %relay_total.2), channel_id=1, source_target_pairs={{0,16},{2,18},{4,20},{6,22},{8,24},{10,26},{12,28},{14,30},{16,0},... | collective-permute-start | bytes 393224 | tf_op jit(solution)/shard_map/ppermute | solution.py:421
  45.0 11.4 %collective-permute-start.18 = (bf16[128,512]{1,0:T(8,128)(2,1)S(1)}, bf16[128,512]{1,0:T(8,128)(2,1)S(1)}, u32[]{:S(2)}, u32[]{:S(2)}) collective-permute-start(bf16[128,512]{1,0:T(8,128)(2,1)S(1)} %relay_total.3), channel_id=1, source_target_pairs={{0,16},{2,18},{4,20},{6,22},{8,24},{10,26},{12,28},{14,30},{16,0},... | collective-permute-start | bytes 393224 | tf_op jit(solution)/shard_map/ppermute | solution.py:421
  47.4 9.0 %collective-permute-start.17 = (bf16[256,512]{1,0:T(8,128)(2,1)S(1)}, bf16[256,512]{1,0:T(8,128)(2,1)S(1)}, u32[]{:S(2)}, u32[]{:S(2)}) collective-permute-start(bf16[256,512]{1,0:T(8,128)(2,1)S(1)} %pad_maximum_fusion), channel_id=1, source_target_pairs={{0,1},{1,0},{2,3},{3,2},{4,5},{5,4},{6,7},{7,6},{8,9},{9,8},{10,11... | collective-permute-start | bytes 786440 | tf_op jit(solution)/shard_map/ppermute | solution.py:416

commit v6 on v5

--- a/solution.py
+++ b/solution.py
@@ -56,45 +56,6 @@
         end = end + lengths_ref[0, j]
         allowed = allowed & ((end <= key_pos) == (end <= query_pos))
     return allowed
-
-
-def delta_kernel(do_ref, out_hbm, delta_ref, buf, sems):
-    width = GROUP * HEAD_SIZE
-    copies = [
-        pltpu.make_async_copy(out_hbm.at[:, g * width : (g + 1) * width], buf.at[g], sems.at[g])
-        for g in range(KEY_VALUE_HEADS)
-    ]
-    for copy in copies:
-        copy.start()
-    pick = (
-        lax.broadcasted_iota(jnp.int32, (GROUP, width), 1) // HEAD_SIZE
-        == lax.broadcasted_iota(jnp.int32, (GROUP, width), 0)
-    ).astype(jnp.bfloat16)
-    for g in range(KEY_VALUE_HEADS):
-        copies[g].wait()
-        columns = slice(g * width, (g + 1) * width)
-        product = do_ref[:, columns].astype(jnp.float32) * buf[g].astype(jnp.float32)
-        high = product.astype(jnp.bfloat16)
-        low = (product - high.astype(jnp.float32)).astype(jnp.bfloat16)
-        delta_ref[g * GROUP : (g + 1) * GROUP, :] = dot(pick, high, NT) + dot(pick, low, NT)
-
-
-def delta_call(output_gradient, attention_output):
-    return pl.pallas_call(
-        delta_kernel,
-        in_specs=[WHOLE, FAR],
-        out_specs=WHOLE,
-        out_shape=shape((QUERY_HEADS, output_gradient.shape[0]), jnp.float32),
-        scratch_shapes=[
-            pltpu.VMEM(
-                (KEY_VALUE_HEADS, output_gradient.shape[0], GROUP * HEAD_SIZE), jnp.bfloat16
-            ),
-            pltpu.SemaphoreType.DMA((KEY_VALUE_HEADS,)),
-        ],
-        compiler_params=PARAMS,
-        cost_estimate=COST,
-        name="delta",
-    )(output_gradient, pinned(attention_output))
 
 
 def block_kernel(ctx_count, step, *refs):
@@ -179,8 +140,18 @@
     return lax.optimization_barrier((values, others))[0]
 
 
-def pieces_kernel(far, in_hbm, *refs):
-    piece_refs, sems = refs[:-1], refs[-1]
+def prepare_kernel(far, in_hbm, do_hbm, out_hbm, *refs):
+    *piece_refs, delta_ref, do_buf, out_buf, delta_sems, sems = refs
+    head_width = GROUP * HEAD_SIZE
+    pairs = []
+    for g in range(KEY_VALUE_HEADS):
+        cut = slice(g * head_width, (g + 1) * head_width)
+        pairs.append(
+            [
+                pltpu.make_async_copy(do_hbm.at[:, cut], do_buf.at[g], delta_sems.at[0, g]),
+                pltpu.make_async_copy(out_hbm.at[:, cut], out_buf.at[g], delta_sems.at[1, g]),
+            ]
+        )
     dp_rank = lax.axis_index("dp")
     y_rank = lax.rem(lax.div(dp_rank, CORES), MIDDLE)
     z_rank = lax.rem(lax.div(dp_rank, CORES * MIDDLE), NEAR)
@@ -200,25 +171,47 @@
                         sems.at[len(copies)],
                     )
                 )
-    for copy in copies:
+    for copy in pairs[0] + copies:
         copy.start()
+    for pair in pairs[1:]:
+        for copy in pair:
+            copy.start()
+    pick = (
+        lax.broadcasted_iota(jnp.int32, (GROUP, head_width), 1) // HEAD_SIZE
+        == lax.broadcasted_iota(jnp.int32, (GROUP, head_width), 0)
+    ).astype(jnp.bfloat16)
+    for g, pair in enumerate(pairs):
+        for copy in pair:
+            copy.wait()
+        product = do_buf[g].astype(jnp.float32) * out_buf[g].astype(jnp.float32)
+        high = product.astype(jnp.bfloat16)
+        low = (product - high.astype(jnp.float32)).astype(jnp.bfloat16)
+        delta_ref[g * GROUP : (g + 1) * GROUP, :] = dot(pick, high, NT) + dot(pick, low, NT)
     for copy in copies:
         copy.wait()
 
 
-def pieces_call(normed, far):
+def prepare_call(normed, output_gradient, attention_output, far):
     rows, width = normed.shape
     count = MIDDLE * NEAR
-    return pl.pallas_call(
-        functools.partial(pieces_kernel, far),
-        in_specs=[FAR],
-        out_specs=[WHOLE] * count,
-        out_shape=[shape((rows, width // count), normed.dtype)] * count,
-        scratch_shapes=[pltpu.SemaphoreType.DMA((count * CORES * far,))],
-        compiler_params=PARAMS,
-        cost_estimate=COST,
-        name="pieces",
-    )(pinned(normed))
+    buffer = pltpu.VMEM((KEY_VALUE_HEADS, rows, GROUP * HEAD_SIZE), jnp.bfloat16)
+    *pieces, delta = pl.pallas_call(
+        functools.partial(prepare_kernel, far),
+        in_specs=[FAR] * 3,
+        out_specs=[WHOLE] * (count + 1),
+        out_shape=[shape((rows, width // count), normed.dtype)] * count
+        + [shape((QUERY_HEADS, rows), jnp.float32)],
+        scratch_shapes=[
+            buffer,
+            buffer,
+            pltpu.SemaphoreType.DMA((2, KEY_VALUE_HEADS)),
+            pltpu.SemaphoreType.DMA((count * CORES * far,)),
+        ],
+        compiler_params=PARAMS,
+        cost_estimate=COST,
+        name="prepare",
+    )(pinned(normed), pinned(output_gradient), pinned(attention_output))
+    return pieces, delta
 
 
 def turn_kernel(*refs):
@@ -430,12 +423,11 @@
     visiting = [
         (over_ctx(saved_keys, step), over_ctx(saved_values, step)) for step in range(1, ctx_count)
     ]
-    pieces = pieces_call(normed_input, far)
+    pieces, delta = prepare_call(normed_input, output_gradient, attention_output, far)
     pieces = [over_group(piece, index) if index else piece for index, piece in enumerate(pieces)]
-    delta = delta_call(output_gradient, attention_output)
     lse = saved_log_totals.T
     block = functools.partial(
-        block_call, ctx_count=ctx_count, lengths=document_lengths, queries=queries, lse=lse
+        block_call, ctx_count=ctx_count, lengths=pinned(document_lengths), queries=queries, lse=lse
     )
     scores, back = [], []
     for step in range(1, ctx_count):
@@ -454,11 +446,7 @@
     gathered = [
         [total if i == 0 else over_group(total, i) for i in range(len(pieces))] for total in totals
     ]
-    own_scores = after(own_scores, totals)
-    query_gradient = query_call(
-        [own_scores] + scores, [saved_keys] + [pair[0] for pair in visiting], rows
-    )
-    tokens = turn_call(after(pieces, query_gradient))
+    tokens = turn_call(after(pieces, totals))
     near, sums = [], []
     for group_grads in gathered:
         theirs = weight_call(True, tokens, group_grads, jnp.bfloat16)
@@ -473,6 +461,10 @@
     near = [
         over_ctx(jnp.concatenate(values, axis=0), s) for s, values in enumerate(zip(*near), 1)
     ]
+    own_scores = after(own_scores, near)
+    query_gradient = query_call(
+        [own_scores] + scores, [saved_keys] + [pair[0] for pair in visiting], rows
+    )
     key_part = part_total_call(sums[0][0], sums[0][1:])
     key_weight_grad, value_weight_grad = final_call(key_part, near, sums[1])
     return query_gradient, key_weight_grad, value_weight_grad

time: 57.4 us -> 58.1 us (1.012)
  waiting for transfers between devices: 15.5 us -> 19.2 us
  starting transfers between devices: 26.7 us -> 24.8 us
  local copies, waits for them, and re-layouts: 0.63 us -> 0.02 us
  Pallas kernels: 13.5 us -> 12.9 us
    ppermute x9, waiting for transfers between devices: 3.43 us -> 9.73 us  [over_group(): return lax.ppermute(value, 'dp', [(s, s ^ flip) for s in range(dp_count)])]
    ppermute x2, waiting for transfers between devices: 7.39 us -> 4.83 us  [over_far(): return lax.ppermute(value, 'dp', pairs)]
    ppermute x9, starting transfers between devices: 12.7 us -> 10.7 us  [over_group(): return lax.ppermute(value, 'dp', [(s, s ^ flip) for s in range(dp_count)])]
    pallas_call x2 -> x1, Pallas kernels: 4.03 us -> 3.14 us  [prepare_call(): pl.pallas_call(functools.partial(prepare_kernel, far), in_specs=[FAR] * 3...]
    unnamed x12 -> x10, local copies, waits for them, and re-layouts: 0.63 us -> 0.02 us
  transfers between devices with their start and end apart: 19 -> 19, of which waited for: 7 -> 8; matrix products, arithmetic and copies ran while one was open for 0% -> 0% of each run, Pallas kernels for 22% -> 21%
where the time goes in v6:
time: 58.1 us; the launch traced here: 57.9 us
  starting transfers between devices  24.8 us (43%)
  waiting for transfers between devices  19.2 us (33%)
  Pallas kernels  12.9 us (22%)
  between operations  0.83 us (1%)
    ppermute x9, starting transfers between devices, over_group(): return lax.ppermute(value, 'dp', [(s, s ^ flip) for s in range(dp_count)])  10.7 us
    ppermute x9, waiting for transfers between devices, over_group(): return lax.ppermute(value, 'dp', [(s, s ^ flip) for s in range(dp_count)])  9.73 us
    ppermute x6, starting transfers between devices, over_ctx(): return lax.ppermute(value, 'ctx', pairs)  8.97 us
    ppermute x2, starting transfers between devices, over_far(): return lax.ppermute(value, 'dp', pairs)  5.04 us
    pallas_call x2, Pallas kernels, block_call(): pl.pallas_call(functools.partial(block_kernel, ctx_count, step), in_specs...  4.86 us
    ppermute x2, waiting for transfers between devices, over_far(): return lax.ppermute(value, 'dp', pairs)  4.83 us
    ppermute x6, waiting for transfers between devices, over_ctx(): return lax.ppermute(value, 'ctx', pairs)  4.69 us
    pallas_call x1, Pallas kernels, prepare_call(): pl.pallas_call(functools.partial(prepare_kernel, far), in_specs=[FAR] * 3...  3.14 us
  transfers between devices with their start and end apart: 19, of which 8 were waited for; matrix products, arithmetic and copies ran while one was open for 0% of the time, Pallas kernels for 21%

profile of v6, /device:TPU:0, one launch (start us, length us, event | category | flops | bytes accessed | tf_op | source)
XLA Modules:
  0.0 57.9 jit_solution(5137999470151778853)
XLA Ops:
  0.7 3.0 %collective-permute-start = (bf16[128,512]{1,0:T(8,128)(2,1)}, bf16[128,512]{1,0:T(8,128)(2,1)S(1)}, u32[]{:S(2)}, u32[]{:S(2)}) collective-permute-start(bf16[128,512]{1,0:T(8,128)(2,1)} %refs_2_.5), channel_id=1, source_target_pairs={{0,1},{1,0},{2,3},{3,2},{4,5},{5,4},{6,7},{7,6},{8,9},{9,8},{10,11... | collective-permute-start | bytes 393224 | tf_op jit(solution)/shard_map/ppermute | solution.py:409
  3.7 0.1 collective-permute-start.1
  3.7 3.1 %prepare.1 = (bf16[128,1024]{1,0:T(8,128)(2,1)S(1)}, bf16[128,1024]{1,0:T(8,128)(2,1)S(1)}, bf16[128,1024]{1,0:T(8,128)(2,1)S(1)}, bf16[128,1024]{1,0:T(8,128)(2,1)S(1)}, f32[32,128]{1,0:T(8,128)S(1)}) custom-call(bf16[128,4096]{1,0:T(8,128)(2,1)} %in_hbm.1, bf16[128,4096]{1,0:T(8,128)(2,1)} %refs_2_.4, bf16[128,4096]{1,0:T(8,128)(2,1)} %out_hbm.1), custom_call_target="tpu_custom_call" | custom-call | flops 1024 | bytes 1024 | tf_op jit(solution)/shard_map/prepare/pallas_call | solution.py:198
  6.9 2.1 %collective-permute-start.3 = (bf16[128,1024]{1,0:T(8,128)(2,1)S(1)}, bf16[128,1024]{1,0:T(8,128)(2,1)S(1)}, u32[]{:S(2)}, u32[]{:S(2)}) collective-permute-start(bf16[128,1024]{1,0:T(8,128)(2,1)S(1)} %get-tuple-element.42), channel_id=1, source_target_pairs={{0,8},{2,10},{4,12},{6,14},{8,0},{10,2},{12,4},{14,6},{16,24},{18,... | collective-permute-start | bytes 786440 | tf_op jit(solution)/shard_map/ppermute | solution.py:421
  9.0 1.5 %collective-permute-start.4 = (bf16[128,1024]{1,0:T(8,128)(2,1)S(1)}, bf16[128,1024]{1,0:T(8,128)(2,1)S(1)}, u32[]{:S(2)}, u32[]{:S(2)}) collective-permute-start(bf16[128,1024]{1,0:T(8,128)(2,1)S(1)} %get-tuple-element.43), channel_id=1, source_target_pairs={{0,4},{2,6},{4,0},{6,2},{8,12},{10,14},{12,8},{14,10},{16,20},{18,... | collective-permute-start | bytes 786440 | tf_op jit(solution)/shard_map/ppermute | solution.py:421
  10.5 0.0 collective-permute-start.5
  10.6 0.0 copy-start.2
  10.6 0.0 copy-start.3
  10.6 2.5 %visiting_keys.1 = (bf16[128,4096]{1,0:T(8,128)(2,1)S(1)}, bf16[2,128,512]{2,1,0:T(8,128)(2,1)S(1)}) custom-call(s32[1,4]{1,0:T(1,128)} %refs_0_.3, bf16[128,4096]{1,0:T(8,128)(2,1)S(1)} %copy-done.1, bf16[128,4096]{1,0:T(8,128)(2,1)S(1)} %copy-done, bf16[128,512]{1,0:T(8,128)(2,1)S(1)} %collective-permute-done.refs_3_, ...), custom_call_target="tpu_custom_call" | custom-call | flops 1024 | bytes 1024 | tf_op jit(solution)/shard_map/visiting_keys/pallas_call | solution.py:98
  13.1 1.9 %collective-permute-start.2 = (bf16[2,128,512]{2,1,0:T(8,128)(2,1)S(1)}, bf16[2,128,512]{2,1,0:T(8,128)(2,1)S(1)}, u32[]{:S(2)}, u32[]{:S(2)}) collective-permute-start(bf16[2,128,512]{2,1,0:T(8,128)(2,1)S(1)} %get-tuple-element.38), channel_id=1, source_target_pairs={{0,1},{1,0},{2,3},{3,2},{4,5},{5,4},{6,7},{7,6},{8,9},{9,8},{10,11... | collective-permute-start | bytes 786440 | tf_op jit(solution)/shard_map/ppermute | solution.py:409
  15.0 2.4 %own_keys.1 = (bf16[128,4096]{1,0:T(8,128)(2,1)S(1)}, f32[2,128,512]{2,1,0:T(8,128)S(1)}) custom-call(s32[1,4]{1,0:T(1,128)} %refs_0_.3, bf16[128,4096]{1,0:T(8,128)(2,1)S(1)} %copy-done.1, bf16[128,4096]{1,0:T(8,128)(2,1)S(1)} %copy-done, bf16[128,512]{1,0:T(8,128)(2,1)S(1)} %copy-done.2, bf16[128,512]{1,0:T(8,128)(2,1)S(1)} %copy-done.3, ...), custom_call_target="tpu_custom_call" | custom-call | flops 1024 | bytes 1024 | tf_op jit(solution)/shard_map/own_keys/pallas_call | solution.py:98
  17.4 0.0 collective-permute-done.3.refs_1_
  17.4 4.4 %collective-permute-done.4.refs_2_ = bf16[128,1024]{1,0:T(8,128)(2,1)S(1)} collective-permute-done((bf16[128,1024]{1,0:T(8,128)(2,1)S(1)}, bf16[128,1024]{1,0:T(8,128)(2,1)S(1)}, u32[]{:S(2)}, u32[]{:S(2)}) %collective-permute-start.4) | collective-permute-done | bytes 262176 | tf_op jit(solution)/shard_map/ppermute | solution.py:421
  21.8 0.0 collective-permute-done.5.refs_3_
  21.8 0.0 collective-permute-done.2.refs_0_
  21.9 1.3 %collective-permute-start.6 = (bf16[128,512]{1,0:T(8,128)(2,1)S(1)}, bf16[128,512]{1,0:T(8,128)(2,1)S(1)}, u32[]{:S(2)}, u32[]{:S(2)}) collective-permute-start(bf16[128,512]{1,0:T(8,128)(2,1)S(1)} %get-tuple-element.51.refs_0_), channel_id=1, source_target_pairs={{0,8},{2,10},{4,12},{6,14},{8,0},{10,2},{12,4},{14,6},{16,24},{18,... | collective-permute-start | bytes 393224 | tf_op jit(solution)/shard_map/ppermute | solution.py:421
  23.2 0.7 %collective-permute-start.7 = (bf16[128,512]{1,0:T(8,128)(2,1)S(1)}, bf16[128,512]{1,0:T(8,128)(2,1)S(1)}, u32[]{:S(2)}, u32[]{:S(2)}) collective-permute-start(bf16[128,512]{1,0:T(8,128)(2,1)S(1)} %get-tuple-element.51.refs_0_), channel_id=1, source_target_pairs={{0,4},{2,6},{4,0},{6,2},{8,12},{10,14},{12,8},{14,10},{16,20},{18,... | collective-permute-start | bytes 393224 | tf_op jit(solution)/shard_map/ppermute | solution.py:421
  23.9 1.5 %collective-permute-start.8 = (bf16[128,512]{1,0:T(8,128)(2,1)S(1)}, bf16[128,512]{1,0:T(8,128)(2,1)S(1)}, u32[]{:S(2)}, u32[]{:S(2)}) collective-permute-start(bf16[128,512]{1,0:T(8,128)(2,1)S(1)} %get-tuple-element.51.refs_0_), channel_id=1, source_target_pairs={{0,12},{2,14},{4,8},{6,10},{8,4},{10,6},{12,0},{14,2},{16,28},{18,... | collective-permute-start | bytes 393224 | tf_op jit(solution)/shard_map/ppermute | solution.py:421
  25.4 1.2 %collective-permute-start.10 = (bf16[128,512]{1,0:T(8,128)(2,1)S(1)}, bf16[128,512]{1,0:T(8,128)(2,1)S(1)}, u32[]{:S(2)}, u32[]{:S(2)}) collective-permute-start(bf16[128,512]{1,0:T(8,128)(2,1)S(1)} %get-tuple-element.52.refs_0_), channel_id=1, source_target_pairs={{0,8},{2,10},{4,12},{6,14},{8,0},{10,2},{12,4},{14,6},{16,24},{18,... | collective-permute-start | bytes 393224 | tf_op jit(solution)/shard_map/ppermute | solution.py:421
  26.7 0.7 %collective-permute-start.11 = (bf16[128,512]{1,0:T(8,128)(2,1)S(1)}, bf16[128,512]{1,0:T(8,128)(2,1)S(1)}, u32[]{:S(2)}, u32[]{:S(2)}) collective-permute-start(bf16[128,512]{1,0:T(8,128)(2,1)S(1)} %get-tuple-element.52.refs_0_), channel_id=1, source_target_pairs={{0,4},{2,6},{4,0},{6,2},{8,12},{10,14},{12,8},{14,10},{16,20},{18,... | collective-permute-start | bytes 393224 | tf_op jit(solution)/shard_map/ppermute | solution.py:421
  27.4 0.8 %collective-permute-done.6.refs_1_ = bf16[128,512]{1,0:T(8,128)(2,1)S(1)} collective-permute-done((bf16[128,512]{1,0:T(8,128)(2,1)S(1)}, bf16[128,512]{1,0:T(8,128)(2,1)S(1)}, u32[]{:S(2)}, u32[]{:S(2)}) %collective-permute-start.6) | collective-permute-done | bytes 131104 | tf_op jit(solution)/shard_map/ppermute | solution.py:421
  28.2 1.5 %collective-permute-start.12 = (bf16[128,512]{1,0:T(8,128)(2,1)S(1)}, bf16[128,512]{1,0:T(8,128)(2,1)S(1)}, u32[]{:S(2)}, u32[]{:S(2)}) collective-permute-start(bf16[128,512]{1,0:T(8,128)(2,1)S(1)} %get-tuple-element.52.refs_0_), channel_id=1, source_target_pairs={{0,12},{2,14},{4,8},{6,10},{8,4},{10,6},{12,0},{14,2},{16,28},{18,... | collective-permute-start | bytes 393224 | tf_op jit(solution)/shard_map/ppermute | solution.py:421
  29.8 0.3 turn_pieces.1.tokens_ref
  30.1 2.2 %collective-permute-done.7.refs_2_ = bf16[128,512]{1,0:T(8,128)(2,1)S(1)} collective-permute-done((bf16[128,512]{1,0:T(8,128)(2,1)S(1)}, bf16[128,512]{1,0:T(8,128)(2,1)S(1)}, u32[]{:S(2)}, u32[]{:S(2)}) %collective-permute-start.7) | collective-permute-done | bytes 131104 | tf_op jit(solution)/shard_map/ppermute | solution.py:421
  32.3 0.4 weight_other_core.2
  32.7 0.1 collective-permute-start.9
  32.8 0.7 %collective-permute-done.10.refs_1_ = bf16[128,512]{1,0:T(8,128)(2,1)S(1)} collective-permute-done((bf16[128,512]{1,0:T(8,128)(2,1)S(1)}, bf16[128,512]{1,0:T(8,128)(2,1)S(1)}, u32[]{:S(2)}, u32[]{:S(2)}) %collective-permute-start.10) | collective-permute-done | bytes 131104 | tf_op jit(solution)/shard_map/ppermute | solution.py:421
  33.4 1.6 %collective-permute-done.11.refs_2_ = bf16[128,512]{1,0:T(8,128)(2,1)S(1)} collective-permute-done((bf16[128,512]{1,0:T(8,128)(2,1)S(1)}, bf16[128,512]{1,0:T(8,128)(2,1)S(1)}, u32[]{:S(2)}, u32[]{:S(2)}) %collective-permute-start.11) | collective-permute-done | bytes 131104 | tf_op jit(solution)/shard_map/ppermute | solution.py:421
  35.1 0.0 collective-permute-done.12.refs_3_
  35.1 0.4 weight_other_core.3
  35.5 0.1 collective-permute-start.13
  35.6 0.4 weight_this_core.2.mine_ref
  36.0 0.0 collective-permute-done.9.theirs_ref
  36.0 0.1 chip_total.2
  36.1 1.6 %collective-permute-start.16 = (bf16[128,512]{1,0:T(8,128)(2,1)S(1)}, bf16[128,512]{1,0:T(8,128)(2,1)S(1)}, u32[]{:S(2)}, u32[]{:S(2)}) collective-permute-start(bf16[128,512]{1,0:T(8,128)(2,1)S(1)} %get-tuple-element.67), channel_id=1, source_target_pairs={{0,1},{1,0},{2,3},{3,2},{4,5},{5,4},{6,7},{7,6},{8,9},{9,8},{10,11... | collective-permute-start | bytes 393224 | tf_op jit(solution)/shard_map/ppermute | solution.py:409
  37.7 0.4 weight_this_core.3.mine_ref
  38.1 0.0 collective-permute-done.13.theirs_ref
  38.1 0.1 chip_total.3
  38.3 0.9 %collective-permute-start.14 = (bf16[128,512]{1,0:T(8,128)(2,1)S(1)}, bf16[128,512]{1,0:T(8,128)(2,1)S(1)}, u32[]{:S(2)}, u32[]{:S(2)}) collective-permute-start(bf16[128,512]{1,0:T(8,128)(2,1)S(1)} %get-tuple-element.60), channel_id=1, source_target_pairs={{0,1},{1,0},{2,3},{3,2},{4,5},{5,4},{6,7},{7,6},{8,9},{9,8},{10,11... | collective-permute-start | bytes 393224 | tf_op jit(solution)/shard_map/ppermute | solution.py:409
  39.1 3.4 %collective-permute-done.16.refs_0_ = bf16[128,512]{1,0:T(8,128)(2,1)S(1)} collective-permute-done((bf16[128,512]{1,0:T(8,128)(2,1)S(1)}, bf16[128,512]{1,0:T(8,128)(2,1)S(1)}, u32[]{:S(2)}, u32[]{:S(2)}) %collective-permute-start.16) | collective-permute-done | bytes 131104 | tf_op jit(solution)/shard_map/ppermute | solution.py:409
  42.5 2.7 %collective-permute-start.17 = (bf16[128,512]{1,0:T(8,128)(2,1)S(1)}, bf16[128,512]{1,0:T(8,128)(2,1)S(1)}, u32[]{:S(2)}, u32[]{:S(2)}) collective-permute-start(bf16[128,512]{1,0:T(8,128)(2,1)S(1)} %relay_total.3), channel_id=1, source_target_pairs={{0,16},{2,18},{4,20},{6,22},{8,24},{10,26},{12,28},{14,30},{16,0},... | collective-permute-start | bytes 393224 | tf_op jit(solution)/shard_map/ppermute | solution.py:414
  45.2 2.4 %collective-permute-start.18 = (bf16[128,512]{1,0:T(8,128)(2,1)S(1)}, bf16[128,512]{1,0:T(8,128)(2,1)S(1)}, u32[]{:S(2)}, u32[]{:S(2)}) collective-permute-start(bf16[128,512]{1,0:T(8,128)(2,1)S(1)} %relay_total.2), channel_id=1, source_target_pairs={{0,16},{2,18},{4,20},{6,22},{8,24},{10,26},{12,28},{14,30},{16,0},... | collective-permute-start | bytes 393224 | tf_op jit(solution)/shard_map/ppermute | solution.py:414
  47.6 1.6 %collective-permute-start.15 = (bf16[256,512]{1,0:T(8,128)(2,1)S(1)}, bf16[256,512]{1,0:T(8,128)(2,1)S(1)}, u32[]{:S(2)}, u32[]{:S(2)}) collective-permute-start(bf16[256,512]{1,0:T(8,128)(2,1)S(1)} %pad_maximum_fusion), channel_id=1, source_target_pairs={{0,1},{1,0},{2,3},{3,2},{4,5},{5,4},{6,7},{7,6},{8,9},{9,8},{10,11... | collective-permute-start | bytes 786440 | tf_op jit(solution)/shard_map/ppermute | solution.py:409
  49.2 4.8 %collective-permute-done.17.refs_1_ = bf16[128,512]{1,0:T(8,128)(2,1)S(1)} collective-permute-done((bf16[128,512]{1,0:T(8,128)(2,1)S(1)}, bf16[128,512]{1,0:T(8,128)(2,1)S(1)}, u32[]{:S(2)}, u32[]{:S(2)}) %collective-permute-start.17) | collective-permute-done | bytes 131104 | tf_op jit(solution)/shard_map/ppermute | solution.py:414
  54.0 1.3 %collective-permute-done.15.refs_0_ = bf16[256,512]{1,0:T(8,128)(2,1)S(1)} collective-permute-done((bf16[256,512]{1,0:T(8,128)(2,1)S(1)}, bf16[256,512]{1,0:T(8,128)(2,1)S(1)}, u32[]{:S(2)}, u32[]{:S(2)}) %collective-permute-start.15) | collective-permute-done | bytes 262176 | tf_op jit(solution)/shard_map/ppermute | solution.py:409
  55.3 1.7 %query_gradient.1 = bf16[128,4096]{1,0:T(8,128)(2,1)} custom-call(bf16[128,4096]{1,0:T(8,128)(2,1)S(1)} %get-tuple-element.63.refs_0_, bf16[128,4096]{1,0:T(8,128)(2,1)S(1)} %get-tuple-element.64.refs_1_, bf16[128,512]{1,0:T(8,128)(2,1)S(1)} %copy-done.2, bf16[128,512]{1,0:T(8,128)(2,1)S(1)} %collective-permute-done.refs_3_), custom_call_target="tpu_custom_call" | custom-call | flops 1024 | bytes 1024 | tf_op jit(solution)/shard_map/query_gradient/pallas_call | solution.py:128
  57.1 0.0 collective-permute-done.18.refs_2_
  57.1 0.8 %weight_total.1 = (f32[128,512]{1,0:T(8,128)}, f32[128,512]{1,0:T(8,128)}) custom-call(f32[128,512]{1,0:T(8,128)S(1)} %key_part_total.1.key_in, bf16[256,512]{1,0:T(8,128)(2,1)S(1)} %collective-permute-done.15.refs_0_, f32[128,512]{1,0:T(8,128)S(1)} %get-tuple-element.68.refs_1_, bf16[128,512]{1,0:T(8,128)(2,1)S(1)} %collective-permute-done.18.refs_2_), custom_call_target="tpu_custom_call" | custom-call | flops 1024 | bytes 1024 | tf_op jit(solution)/shard_map/weight_total/pallas_call | solution.py:381
  (17 shorter events, 0.2 us)
Async XLA Ops:
  0.6 9.9 %copy-start = (bf16[128,4096]{1,0:T(8,128)(2,1)S(1)}, bf16[128,4096]{1,0:T(8,128)(2,1)}, u32[]{:S(2)}) copy-start(bf16[128,4096]{1,0:T(8,128)(2,1)} %refs_2_.4) | copy-start | bytes 3145732
  0.6 9.9 %copy-start.1 = (bf16[128,4096]{1,0:T(8,128)(2,1)S(1)}, bf16[128,4096]{1,0:T(8,128)(2,1)}, u32[]{:S(2)}) copy-start(bf16[128,4096]{1,0:T(8,128)(2,1)} %refs_1_.3) | copy-start | bytes 3145732
  0.7 9.9 %collective-permute-start = (bf16[128,512]{1,0:T(8,128)(2,1)}, bf16[128,512]{1,0:T(8,128)(2,1)S(1)}, u32[]{:S(2)}, u32[]{:S(2)}) collective-permute-start(bf16[128,512]{1,0:T(8,128)(2,1)} %refs_2_.5), channel_id=1, source_target_pairs={{0,1},{1,0},{2,3},{3,2},{4,5},{5,4},{6,7},{7,6},{8,9},{9,8},{10,11... | collective-permute-start | bytes 393224 | tf_op jit(solution)/shard_map/ppermute | solution.py:409
  3.7 6.9 %collective-permute-start.1 = (bf16[128,512]{1,0:T(8,128)(2,1)}, bf16[128,512]{1,0:T(8,128)(2,1)S(1)}, u32[]{:S(2)}, u32[]{:S(2)}) collective-permute-start(bf16[128,512]{1,0:T(8,128)(2,1)} %refs_4_.1), channel_id=1, source_target_pairs={{0,1},{1,0},{2,3},{3,2},{4,5},{5,4},{6,7},{7,6},{8,9},{9,8},{10,11... | collective-permute-start | bytes 393224 | tf_op jit(solution)/shard_map/ppermute | solution.py:409
  3.7 6.8 %copy-start.4 = (f32[128,32]{0,1:T(8,128)S(1)}, f32[128,32]{0,1:T(8,128)}, u32[]{:S(2)}) copy-start(f32[128,32]{0,1:T(8,128)} %param.13) | copy-start | bytes 49156
  6.9 10.5 %collective-permute-start.3 = (bf16[128,1024]{1,0:T(8,128)(2,1)S(1)}, bf16[128,1024]{1,0:T(8,128)(2,1)S(1)}, u32[]{:S(2)}, u32[]{:S(2)}) collective-permute-start(bf16[128,1024]{1,0:T(8,128)(2,1)S(1)} %get-tuple-element.42), channel_id=1, source_target_pairs={{0,8},{2,10},{4,12},{6,14},{8,0},{10,2},{12,4},{14,6},{16,24},{18,... | collective-permute-start | bytes 786440 | tf_op jit(solution)/shard_map/ppermute | solution.py:421
  9.0 12.8 %collective-permute-start.4 = (bf16[128,1024]{1,0:T(8,128)(2,1)S(1)}, bf16[128,1024]{1,0:T(8,128)(2,1)S(1)}, u32[]{:S(2)}, u32[]{:S(2)}) collective-permute-start(bf16[128,1024]{1,0:T(8,128)(2,1)S(1)} %get-tuple-element.43), channel_id=1, source_target_pairs={{0,4},{2,6},{4,0},{6,2},{8,12},{10,14},{12,8},{14,10},{16,20},{18,... | collective-permute-start | bytes 786440 | tf_op jit(solution)/shard_map/ppermute | solution.py:421
  10.5 11.3 %collective-permute-start.5 = (bf16[128,1024]{1,0:T(8,128)(2,1)S(1)}, bf16[128,1024]{1,0:T(8,128)(2,1)S(1)}, u32[]{:S(2)}, u32[]{:S(2)}) collective-permute-start(bf16[128,1024]{1,0:T(8,128)(2,1)S(1)} %get-tuple-element.44), channel_id=1, source_target_pairs={{0,12},{2,14},{4,8},{6,10},{8,4},{10,6},{12,0},{14,2},{16,28},{18,... | collective-permute-start | bytes 786440 | tf_op jit(solution)/shard_map/ppermute | solution.py:421
  10.6 4.4 %copy-start.2 = (bf16[128,512]{1,0:T(8,128)(2,1)S(1)}, bf16[128,512]{1,0:T(8,128)(2,1)}, u32[]{:S(2)}) copy-start(bf16[128,512]{1,0:T(8,128)(2,1)} %refs_2_.5) | copy-start | bytes 393220
  10.6 4.4 %copy-start.3 = (bf16[128,512]{1,0:T(8,128)(2,1)S(1)}, bf16[128,512]{1,0:T(8,128)(2,1)}, u32[]{:S(2)}) copy-start(bf16[128,512]{1,0:T(8,128)(2,1)} %refs_4_.1) | copy-start | bytes 393220
  13.1 8.7 %collective-permute-start.2 = (bf16[2,128,512]{2,1,0:T(8,128)(2,1)S(1)}, bf16[2,128,512]{2,1,0:T(8,128)(2,1)S(1)}, u32[]{:S(2)}, u32[]{:S(2)}) collective-permute-start(bf16[2,128,512]{2,1,0:T(8,128)(2,1)S(1)} %get-tuple-element.38), channel_id=1, source_target_pairs={{0,1},{1,0},{2,3},{3,2},{4,5},{5,4},{6,7},{7,6},{8,9},{9,8},{10,11... | collective-permute-start | bytes 786440 | tf_op jit(solution)/shard_map/ppermute | solution.py:409
  21.9 6.4 %collective-permute-start.6 = (bf16[128,512]{1,0:T(8,128)(2,1)S(1)}, bf16[128,512]{1,0:T(8,128)(2,1)S(1)}, u32[]{:S(2)}, u32[]{:S(2)}) collective-permute-start(bf16[128,512]{1,0:T(8,128)(2,1)S(1)} %get-tuple-element.51.refs_0_), channel_id=1, source_target_pairs={{0,8},{2,10},{4,12},{6,14},{8,0},{10,2},{12,4},{14,6},{16,24},{18,... | collective-permute-start | bytes 393224 | tf_op jit(solution)/shard_map/ppermute | solution.py:421
  23.2 9.1 %collective-permute-start.7 = (bf16[128,512]{1,0:T(8,128)(2,1)S(1)}, bf16[128,512]{1,0:T(8,128)(2,1)S(1)}, u32[]{:S(2)}, u32[]{:S(2)}) collective-permute-start(bf16[128,512]{1,0:T(8,128)(2,1)S(1)} %get-tuple-element.51.refs_0_), channel_id=1, source_target_pairs={{0,4},{2,6},{4,0},{6,2},{8,12},{10,14},{12,8},{14,10},{16,20},{18,... | collective-permute-start | bytes 393224 | tf_op jit(solution)/shard_map/ppermute | solution.py:421
  23.9 8.4 %collective-permute-start.8 = (bf16[128,512]{1,0:T(8,128)(2,1)S(1)}, bf16[128,512]{1,0:T(8,128)(2,1)S(1)}, u32[]{:S(2)}, u32[]{:S(2)}) collective-permute-start(bf16[128,512]{1,0:T(8,128)(2,1)S(1)} %get-tuple-element.51.refs_0_), channel_id=1, source_target_pairs={{0,12},{2,14},{4,8},{6,10},{8,4},{10,6},{12,0},{14,2},{16,28},{18,... | collective-permute-start | bytes 393224 | tf_op jit(solution)/shard_map/ppermute | solution.py:421
  25.4 8.0 %collective-permute-start.10 = (bf16[128,512]{1,0:T(8,128)(2,1)S(1)}, bf16[128,512]{1,0:T(8,128)(2,1)S(1)}, u32[]{:S(2)}, u32[]{:S(2)}) collective-permute-start(bf16[128,512]{1,0:T(8,128)(2,1)S(1)} %get-tuple-element.52.refs_0_), channel_id=1, source_target_pairs={{0,8},{2,10},{4,12},{6,14},{8,0},{10,2},{12,4},{14,6},{16,24},{18,... | collective-permute-start | bytes 393224 | tf_op jit(solution)/shard_map/ppermute | solution.py:421
  26.7 8.4 %collective-permute-start.11 = (bf16[128,512]{1,0:T(8,128)(2,1)S(1)}, bf16[128,512]{1,0:T(8,128)(2,1)S(1)}, u32[]{:S(2)}, u32[]{:S(2)}) collective-permute-start(bf16[128,512]{1,0:T(8,128)(2,1)S(1)} %get-tuple-element.52.refs_0_), channel_id=1, source_target_pairs={{0,4},{2,6},{4,0},{6,2},{8,12},{10,14},{12,8},{14,10},{16,20},{18,... | collective-permute-start | bytes 393224 | tf_op jit(solution)/shard_map/ppermute | solution.py:421
  28.2 6.8 %collective-permute-start.12 = (bf16[128,512]{1,0:T(8,128)(2,1)S(1)}, bf16[128,512]{1,0:T(8,128)(2,1)S(1)}, u32[]{:S(2)}, u32[]{:S(2)}) collective-permute-start(bf16[128,512]{1,0:T(8,128)(2,1)S(1)} %get-tuple-element.52.refs_0_), channel_id=1, source_target_pairs={{0,12},{2,14},{4,8},{6,10},{8,4},{10,6},{12,0},{14,2},{16,28},{18,... | collective-permute-start | bytes 393224 | tf_op jit(solution)/shard_map/ppermute | solution.py:421
  32.7 3.3 %collective-permute-start.9 = (bf16[512,512]{1,0:T(8,128)(2,1)S(1)}, bf16[512,512]{1,0:T(8,128)(2,1)S(1)}, u32[]{:S(2)}, u32[]{:S(2)}) collective-permute-start(bf16[512,512]{1,0:T(8,128)(2,1)S(1)} %weight_other_core.2), channel_id=1, source_target_pairs={{0,2},{2,0},{4,6},{6,4},{8,10},{10,8},{12,14},{14,12},{16,18},{18,... | collective-permute-start | bytes 1572872 | tf_op jit(solution)/shard_map/ppermute | solution.py:417
  35.5 2.6 %collective-permute-start.13 = (bf16[512,512]{1,0:T(8,128)(2,1)S(1)}, bf16[512,512]{1,0:T(8,128)(2,1)S(1)}, u32[]{:S(2)}, u32[]{:S(2)}) collective-permute-start(bf16[512,512]{1,0:T(8,128)(2,1)S(1)} %weight_other_core.3), channel_id=1, source_target_pairs={{0,2},{2,0},{4,6},{6,4},{8,10},{10,8},{12,14},{14,12},{16,18},{18,... | collective-permute-start | bytes 1572872 | tf_op jit(solution)/shard_map/ppermute | solution.py:417
  36.1 6.4 %collective-permute-start.16 = (bf16[128,512]{1,0:T(8,128)(2,1)S(1)}, bf16[128,512]{1,0:T(8,128)(2,1)S(1)}, u32[]{:S(2)}, u32[]{:S(2)}) collective-permute-start(bf16[128,512]{1,0:T(8,128)(2,1)S(1)} %get-tuple-element.67), channel_id=1, source_target_pairs={{0,1},{1,0},{2,3},{3,2},{4,5},{5,4},{6,7},{7,6},{8,9},{9,8},{10,11... | collective-permute-start | bytes 393224 | tf_op jit(solution)/shard_map/ppermute | solution.py:409
  38.3 6.9 %collective-permute-start.14 = (bf16[128,512]{1,0:T(8,128)(2,1)S(1)}, bf16[128,512]{1,0:T(8,128)(2,1)S(1)}, u32[]{:S(2)}, u32[]{:S(2)}) collective-permute-start(bf16[128,512]{1,0:T(8,128)(2,1)S(1)} %get-tuple-element.60), channel_id=1, source_target_pairs={{0,1},{1,0},{2,3},{3,2},{4,5},{5,4},{6,7},{7,6},{8,9},{9,8},{10,11... | collective-permute-start | bytes 393224 | tf_op jit(solution)/shard_map/ppermute | solution.py:409
  42.5 11.5 %collective-permute-start.17 = (bf16[128,512]{1,0:T(8,128)(2,1)S(1)}, bf16[128,512]{1,0:T(8,128)(2,1)S(1)}, u32[]{:S(2)}, u32[]{:S(2)}) collective-permute-start(bf16[128,512]{1,0:T(8,128)(2,1)S(1)} %relay_total.3), channel_id=1, source_target_pairs={{0,16},{2,18},{4,20},{6,22},{8,24},{10,26},{12,28},{14,30},{16,0},... | collective-permute-start | bytes 393224 | tf_op jit(solution)/shard_map/ppermute | solution.py:414
  45.2 11.8 %collective-permute-start.18 = (bf16[128,512]{1,0:T(8,128)(2,1)S(1)}, bf16[128,512]{1,0:T(8,128)(2,1)S(1)}, u32[]{:S(2)}, u32[]{:S(2)}) collective-permute-start(bf16[128,512]{1,0:T(8,128)(2,1)S(1)} %relay_total.2), channel_id=1, source_target_pairs={{0,16},{2,18},{4,20},{6,22},{8,24},{10,26},{12,28},{14,30},{16,0},... | collective-permute-start | bytes 393224 | tf_op jit(solution)/shard_map/ppermute | solution.py:414
  47.6 7.7 %collective-permute-start.15 = (bf16[256,512]{1,0:T(8,128)(2,1)S(1)}, bf16[256,512]{1,0:T(8,128)(2,1)S(1)}, u32[]{:S(2)}, u32[]{:S(2)}) collective-permute-start(bf16[256,512]{1,0:T(8,128)(2,1)S(1)} %pad_maximum_fusion), channel_id=1, source_target_pairs={{0,1},{1,0},{2,3},{3,2},{4,5},{5,4},{6,7},{7,6},{8,9},{9,8},{10,11... | collective-permute-start | bytes 786440 | tf_op jit(solution)/shard_map/ppermute | solution.py:409

commit v7 on v5

--- a/solution.py
+++ b/solution.py
@@ -56,45 +56,6 @@
         end = end + lengths_ref[0, j]
         allowed = allowed & ((end <= key_pos) == (end <= query_pos))
     return allowed
-
-
-def delta_kernel(do_ref, out_hbm, delta_ref, buf, sems):
-    width = GROUP * HEAD_SIZE
-    copies = [
-        pltpu.make_async_copy(out_hbm.at[:, g * width : (g + 1) * width], buf.at[g], sems.at[g])
-        for g in range(KEY_VALUE_HEADS)
-    ]
-    for copy in copies:
-        copy.start()
-    pick = (
-        lax.broadcasted_iota(jnp.int32, (GROUP, width), 1) // HEAD_SIZE
-        == lax.broadcasted_iota(jnp.int32, (GROUP, width), 0)
-    ).astype(jnp.bfloat16)
-    for g in range(KEY_VALUE_HEADS):
-        copies[g].wait()
-        columns = slice(g * width, (g + 1) * width)
-        product = do_ref[:, columns].astype(jnp.float32) * buf[g].astype(jnp.float32)
-        high = product.astype(jnp.bfloat16)
-        low = (product - high.astype(jnp.float32)).astype(jnp.bfloat16)
-        delta_ref[g * GROUP : (g + 1) * GROUP, :] = dot(pick, high, NT) + dot(pick, low, NT)
-
-
-def delta_call(output_gradient, attention_output):
-    return pl.pallas_call(
-        delta_kernel,
-        in_specs=[WHOLE, FAR],
-        out_specs=WHOLE,
-        out_shape=shape((QUERY_HEADS, output_gradient.shape[0]), jnp.float32),
-        scratch_shapes=[
-            pltpu.VMEM(
-                (KEY_VALUE_HEADS, output_gradient.shape[0], GROUP * HEAD_SIZE), jnp.bfloat16
-            ),
-            pltpu.SemaphoreType.DMA((KEY_VALUE_HEADS,)),
-        ],
-        compiler_params=PARAMS,
-        cost_estimate=COST,
-        name="delta",
-    )(output_gradient, pinned(attention_output))
 
 
 def block_kernel(ctx_count, step, *refs):
@@ -221,6 +182,44 @@
     )(pinned(normed))
 
 
+def delta_kernel(do_ref, out_hbm, delta_ref, buf, sems):
+    width = GROUP * HEAD_SIZE
+    copies = [
+        pltpu.make_async_copy(out_hbm.at[:, g * width : (g + 1) * width], buf.at[g], sems.at[g])
+        for g in range(KEY_VALUE_HEADS)
+    ]
+    for copy in copies:
+        copy.start()
+    pick = (
+        lax.broadcasted_iota(jnp.int32, (GROUP, width), 1) // HEAD_SIZE
+        == lax.broadcasted_iota(jnp.int32, (GROUP, width), 0)
+    ).astype(jnp.bfloat16)
+    for g in range(KEY_VALUE_HEADS):
+        copies[g].wait()
+        columns = slice(g * width, (g + 1) * width)
+        product = do_ref[:, columns].astype(jnp.float32) * buf[g].astype(jnp.float32)
+        high = product.astype(jnp.bfloat16)
+        low = (product - high.astype(jnp.float32)).astype(jnp.bfloat16)
+        delta_ref[g * GROUP : (g + 1) * GROUP, :] = dot(pick, high, NT) + dot(pick, low, NT)
+
+
+def delta_call(output_gradient, attention_output):
+    rows = output_gradient.shape[0]
+    return pl.pallas_call(
+        delta_kernel,
+        in_specs=[WHOLE, FAR],
+        out_specs=WHOLE,
+        out_shape=shape((QUERY_HEADS, rows), jnp.float32),
+        scratch_shapes=[
+            pltpu.VMEM((KEY_VALUE_HEADS, rows, GROUP * HEAD_SIZE), jnp.bfloat16),
+            pltpu.SemaphoreType.DMA((KEY_VALUE_HEADS,)),
+        ],
+        compiler_params=PARAMS,
+        cost_estimate=COST,
+        name="delta",
+    )(output_gradient, pinned(attention_output))
+
+
 def turn_kernel(*refs):
     out_ref = refs[-1]
     for at, ref in enumerate(refs[:-1]):
@@ -242,27 +241,25 @@
 
 
 def add_kernel(own_ref, *refs):
-    out_refs = refs[-PARTS:]
-    for part, out_ref in enumerate(out_refs):
-        total = own_ref[part]
-        for back_ref in refs[:-PARTS]:
-            total = total + back_ref[part].astype(jnp.float32)
-        out_ref[...] = total.astype(out_ref.dtype)
+    total = own_ref[...]
+    for back_ref in refs[:-1]:
+        total = total + back_ref[...].astype(jnp.float32)
+    refs[-1][...] = total.astype(refs[-1].dtype)
 
 
 def add_call(own, back):
     return pl.pallas_call(
         add_kernel,
         in_specs=[WHOLE] * (1 + len(back)),
-        out_specs=[WHOLE] * PARTS,
-        out_shape=[shape(own.shape[1:], jnp.bfloat16)] * PARTS,
+        out_specs=WHOLE,
+        out_shape=shape(own.shape, jnp.bfloat16),
         compiler_params=PARAMS,
         cost_estimate=COST,
         name="grads_total",
     )(own, *back)
 
 
-def weight_kernel(other, tokens_ref, *refs):
+def weight_kernel(other, part, tokens_ref, *refs):
     g_refs, out_ref = refs[:-1], refs[-1]
     height = out_ref.shape[0]
     core = lax.rem(lax.axis_index("dp"), CORES)
@@ -270,19 +267,19 @@
         core = 1 - core
     start = pl.multiple_of(core * height, height)
     block = min(height, 256)
-    grads = jnp.concatenate([g[...] for g in g_refs], axis=0)
+    grads = jnp.concatenate([g[part] for g in g_refs], axis=0)
     for row in range(0, height, block):
         out_ref[row : row + block, :] = dot(
             tokens_ref[pl.ds(start + row, block), :], grads, NN
         ).astype(out_ref.dtype)
 
 
-def weight_call(other, tokens, grads, dtype):
-    return pl.pallas_call(
-        functools.partial(weight_kernel, other),
+def weight_call(other, part, tokens, grads, dtype):
+    return pl.pallas_call(
+        functools.partial(weight_kernel, other, part),
         in_specs=[WHOLE] * (1 + len(grads)),
         out_specs=WHOLE,
-        out_shape=shape((tokens.shape[0] // CORES, grads[0].shape[1]), dtype),
+        out_shape=shape((tokens.shape[0] // CORES, grads[0].shape[2]), dtype),
         compiler_params=PARAMS,
         cost_estimate=COST,
         name="weight_other_core" if other else "weight_this_core",
@@ -435,7 +432,7 @@
     delta = delta_call(output_gradient, attention_output)
     lse = saved_log_totals.T
     block = functools.partial(
-        block_call, ctx_count=ctx_count, lengths=document_lengths, queries=queries, lse=lse
+        block_call, ctx_count=ctx_count, lengths=pinned(document_lengths), queries=queries, lse=lse
     )
     scores, back = [], []
     for step in range(1, ctx_count):
@@ -450,25 +447,25 @@
         0, output_gradient=output_gradient, keys=saved_keys, values=saved_values, delta=delta
     )
     back, pieces = lax.optimization_barrier((back, pieces))
-    totals = add_call(own, back)
-    gathered = [
-        [total if i == 0 else over_group(total, i) for i in range(len(pieces))] for total in totals
-    ]
-    own_scores = after(own_scores, totals)
+    total = add_call(own, back)
+    grads = [over_group(total, i) if i else total for i in range(len(pieces))]
+    own_scores, pieces = after((own_scores, pieces), total)
     query_gradient = query_call(
         [own_scores] + scores, [saved_keys] + [pair[0] for pair in visiting], rows
     )
     tokens = turn_call(after(pieces, query_gradient))
     near, sums = [], []
-    for group_grads in gathered:
-        theirs = weight_call(True, tokens, group_grads, jnp.bfloat16)
+    for part in range(PARTS):
+        theirs = weight_call(True, part, tokens, grads, jnp.bfloat16)
         arriving = over_cores(theirs)
-        mine = weight_call(False, tokens, group_grads, jnp.float32)
-        total, away, *blocks = chip_call(far, ctx_count, mine, arriving)
+        mine = weight_call(False, part, tokens, grads, jnp.float32)
+        own_block, away, *blocks = chip_call(far, ctx_count, mine, arriving)
+        if part:
+            blocks = after(blocks, relayed)
         away_arrived = [over_ctx(value, s) for s, value in enumerate(blocks[1::2], 1)]
         near.append(blocks[0::2])
         relayed = relay_call(far, away, away_arrived)
-        sums.append([total] + [over_far(value, s) for s, value in enumerate(relayed, 1)])
+        sums.append([own_block] + [over_far(value, s) for s, value in enumerate(relayed, 1)])
     near = after(near, relayed)
     near = [
         over_ctx(jnp.concatenate(values, axis=0), s) for s, values in enumerate(zip(*near), 1)

time: 57.4 us -> 58.3 us (1.016)
  waiting for transfers between devices: 15.5 us -> 20.7 us
  starting transfers between devices: 26.7 us -> 22.7 us
  local copies, waits for them, and re-layouts: 0.63 us -> 0.02 us
    ppermute x9 -> x6, waiting for transfers between devices: 3.43 us -> 8.94 us  [over_group(): return lax.ppermute(value, 'dp', [(s, s ^ flip) for s in range(dp_count)])]
    ppermute x9 -> x6, starting transfers between devices: 12.7 us -> 7.19 us  [over_group(): return lax.ppermute(value, 'dp', [(s, s ^ flip) for s in range(dp_count)])]
    ppermute x2, waiting for transfers between devices: 7.39 us -> 6 us  [over_far(): return lax.ppermute(value, 'dp', pairs)]
    ppermute x6, starting transfers between devices: 8.88 us -> 9.63 us  [over_ctx(): return lax.ppermute(value, 'ctx', pairs)]
    ppermute x6, waiting for transfers between devices: 4.68 us -> 5.31 us  [over_ctx(): return lax.ppermute(value, 'ctx', pairs)]
    unnamed x12 -> x10, local copies, waits for them, and re-layouts: 0.63 us -> 0.02 us
  transfers between devices with their start and end apart: 19 -> 16, of which waited for: 7 -> 9; matrix products, arithmetic and copies ran while one was open for 0% -> 0% of each run, Pallas kernels for 22% -> 21%
where the time goes in v7:
time: 58.3 us; the launch traced here: 58 us
  starting transfers between devices  22.7 us (39%)
  waiting for transfers between devices  20.7 us (36%)
  Pallas kernels  13.8 us (24%)
  between operations  0.82 us (1%)
    ppermute x6, starting transfers between devices, over_ctx(): return lax.ppermute(value, 'ctx', pairs)  9.63 us
    ppermute x6, waiting for transfers between devices, over_group(): return lax.ppermute(value, 'dp', [(s, s ^ flip) for s in range(dp_count)])  8.94 us
    ppermute x6, starting transfers between devices, over_group(): return lax.ppermute(value, 'dp', [(s, s ^ flip) for s in range(dp_count)])  7.19 us
    ppermute x2, waiting for transfers between devices, over_far(): return lax.ppermute(value, 'dp', pairs)  6 us
    ppermute x6, waiting for transfers between devices, over_ctx(): return lax.ppermute(value, 'ctx', pairs)  5.31 us
    ppermute x2, starting transfers between devices, over_far(): return lax.ppermute(value, 'dp', pairs)  5.21 us
    pallas_call x2, Pallas kernels, block_call(): pl.pallas_call(functools.partial(block_kernel, ctx_count, step), in_specs...  4.85 us
    pallas_call x1, Pallas kernels, delta_call(): pl.pallas_call(delta_kernel, in_specs=[WHOLE, FAR], out_specs=WHOLE, out_...  2.65 us
  transfers between devices with their start and end apart: 16, of which 9 were waited for; matrix products, arithmetic and copies ran while one was open for 0% of the time, Pallas kernels for 21%

profile of v7, /device:TPU:0, one launch (start us, length us, event | category | flops | bytes accessed | tf_op | source)
XLA Modules:
  0.0 58.0 jit_solution(14582056926137680454)
XLA Ops:
  0.6 3.0 %collective-permute-start = (bf16[128,512]{1,0:T(8,128)(2,1)}, bf16[128,512]{1,0:T(8,128)(2,1)S(1)}, u32[]{:S(2)}, u32[]{:S(2)}) collective-permute-start(bf16[128,512]{1,0:T(8,128)(2,1)} %refs_2_.5), channel_id=1, source_target_pairs={{0,1},{1,0},{2,3},{3,2},{4,5},{5,4},{6,7},{7,6},{8,9},{9,8},{10,11... | collective-permute-start | bytes 393224 | tf_op jit(solution)/shard_map/ppermute | solution.py:413
  3.6 0.1 collective-permute-start.1
  3.7 1.4 %pieces.1 = (bf16[128,1024]{1,0:T(8,128)(2,1)S(1)}, bf16[128,1024]{1,0:T(8,128)(2,1)S(1)}, bf16[128,1024]{1,0:T(8,128)(2,1)S(1)}, bf16[128,1024]{1,0:T(8,128)(2,1)S(1)}) custom-call(bf16[128,4096]{1,0:T(8,128)(2,1)} %in_hbm.1), custom_call_target="tpu_custom_call" | custom-call | flops 1024 | bytes 1024 | tf_op jit(solution)/shard_map/pieces/pallas_call | solution.py:173
  5.1 2.1 %collective-permute-start.3 = (bf16[128,1024]{1,0:T(8,128)(2,1)S(1)}, bf16[128,1024]{1,0:T(8,128)(2,1)S(1)}, u32[]{:S(2)}, u32[]{:S(2)}) collective-permute-start(bf16[128,1024]{1,0:T(8,128)(2,1)S(1)} %get-tuple-element.44), channel_id=1, source_target_pairs={{0,8},{2,10},{4,12},{6,14},{8,0},{10,2},{12,4},{14,6},{16,24},{18,... | collective-permute-start | bytes 786440 | tf_op jit(solution)/shard_map/ppermute | solution.py:425
  7.2 1.5 %collective-permute-start.4 = (bf16[128,1024]{1,0:T(8,128)(2,1)S(1)}, bf16[128,1024]{1,0:T(8,128)(2,1)S(1)}, u32[]{:S(2)}, u32[]{:S(2)}) collective-permute-start(bf16[128,1024]{1,0:T(8,128)(2,1)S(1)} %get-tuple-element.45), channel_id=1, source_target_pairs={{0,4},{2,6},{4,0},{6,2},{8,12},{10,14},{12,8},{14,10},{16,20},{18,... | collective-permute-start | bytes 786440 | tf_op jit(solution)/shard_map/ppermute | solution.py:425
  8.7 0.0 collective-permute-start.5
  8.8 2.6 %delta.1.refs_6_ = f32[32,128]{1,0:T(8,128)S(1)} custom-call(bf16[128,4096]{1,0:T(8,128)(2,1)S(1)} %copy-done, bf16[128,4096]{1,0:T(8,128)(2,1)} %out_hbm.1), custom_call_target="tpu_custom_call" | custom-call | flops 1024 | bytes 1024 | tf_op jit(solution)/shard_map/delta/pallas_call | solution.py:208
  11.4 0.0 collective-permute-done.refs_3_
  11.4 0.0 collective-permute-done.1.refs_4_
  11.5 0.0 copy-start.2
  11.5 0.0 copy-start.3
  11.5 2.5 %visiting_keys.1 = (bf16[128,4096]{1,0:T(8,128)(2,1)S(1)}, bf16[2,128,512]{2,1,0:T(8,128)(2,1)S(1)}) custom-call(s32[1,4]{1,0:T(1,128)} %refs_0_.3, bf16[128,4096]{1,0:T(8,128)(2,1)S(1)} %copy-done.1, bf16[128,4096]{1,0:T(8,128)(2,1)S(1)} %copy-done, bf16[128,512]{1,0:T(8,128)(2,1)S(1)} %collective-permute-done.refs_3_, ...), custom_call_target="tpu_custom_call" | custom-call | flops 1024 | bytes 1024 | tf_op jit(solution)/shard_map/visiting_keys/pallas_call | solution.py:98
  14.0 1.8 %collective-permute-start.2 = (bf16[2,128,512]{2,1,0:T(8,128)(2,1)S(1)}, bf16[2,128,512]{2,1,0:T(8,128)(2,1)S(1)}, u32[]{:S(2)}, u32[]{:S(2)}) collective-permute-start(bf16[2,128,512]{2,1,0:T(8,128)(2,1)S(1)} %get-tuple-element.40), channel_id=1, source_target_pairs={{0,1},{1,0},{2,3},{3,2},{4,5},{5,4},{6,7},{7,6},{8,9},{9,8},{10,11... | collective-permute-start | bytes 786440 | tf_op jit(solution)/shard_map/ppermute | solution.py:413
  15.8 0.0 copy-done.3
  15.8 2.3 %own_keys.1 = (bf16[128,4096]{1,0:T(8,128)(2,1)S(1)}, f32[2,128,512]{2,1,0:T(8,128)S(1)}) custom-call(s32[1,4]{1,0:T(1,128)} %refs_0_.3, bf16[128,4096]{1,0:T(8,128)(2,1)S(1)} %copy-done.1, bf16[128,4096]{1,0:T(8,128)(2,1)S(1)} %copy-done, bf16[128,512]{1,0:T(8,128)(2,1)S(1)} %copy-done.2, bf16[128,512]{1,0:T(8,128)(2,1)S(1)} %copy-done.3, ...), custom_call_target="tpu_custom_call" | custom-call | flops 1024 | bytes 1024 | tf_op jit(solution)/shard_map/own_keys/pallas_call | solution.py:98
  18.2 0.0 collective-permute-done.3.refs_1_
  18.2 1.8 %collective-permute-done.4.refs_2_ = bf16[128,1024]{1,0:T(8,128)(2,1)S(1)} collective-permute-done((bf16[128,1024]{1,0:T(8,128)(2,1)S(1)}, bf16[128,1024]{1,0:T(8,128)(2,1)S(1)}, u32[]{:S(2)}, u32[]{:S(2)}) %collective-permute-start.4) | collective-permute-done | bytes 262176 | tf_op jit(solution)/shard_map/ppermute | solution.py:425
  20.0 0.0 collective-permute-done.5.refs_3_
  20.0 0.9 %collective-permute-done.2.refs_0_ = bf16[2,128,512]{2,1,0:T(8,128)(2,1)S(1)} collective-permute-done((bf16[2,128,512]{2,1,0:T(8,128)(2,1)S(1)}, bf16[2,128,512]{2,1,0:T(8,128)(2,1)S(1)}, u32[]{:S(2)}, u32[]{:S(2)}) %collective-permute-start.2) | collective-permute-done | bytes 262176 | tf_op jit(solution)/shard_map/ppermute | solution.py:413
  21.0 1.7 %collective-permute-start.6 = (bf16[2,128,512]{2,1,0:T(8,128)(2,1)S(1)}, bf16[2,128,512]{2,1,0:T(8,128)(2,1)S(1)}, u32[]{:S(2)}, u32[]{:S(2)}) collective-permute-start(bf16[2,128,512]{2,1,0:T(8,128)(2,1)S(1)} %grads_total.1.refs_0_), channel_id=1, source_target_pairs={{0,8},{2,10},{4,12},{6,14},{8,0},{10,2},{12,4},{14,6},{16,24},{18,... | collective-permute-start | bytes 786440 | tf_op jit(solution)/shard_map/ppermute | solution.py:425
  22.7 1.5 %collective-permute-start.7 = (bf16[2,128,512]{2,1,0:T(8,128)(2,1)S(1)}, bf16[2,128,512]{2,1,0:T(8,128)(2,1)S(1)}, u32[]{:S(2)}, u32[]{:S(2)}) collective-permute-start(bf16[2,128,512]{2,1,0:T(8,128)(2,1)S(1)} %grads_total.1.refs_0_), channel_id=1, source_target_pairs={{0,4},{2,6},{4,0},{6,2},{8,12},{10,14},{12,8},{14,10},{16,20},{18,... | collective-permute-start | bytes 786440 | tf_op jit(solution)/shard_map/ppermute | solution.py:425
  24.2 0.4 collective-permute-start.8
  24.6 1.7 %query_gradient.1 = bf16[128,4096]{1,0:T(8,128)(2,1)} custom-call(bf16[128,4096]{1,0:T(8,128)(2,1)S(1)} %get-tuple-element.53.refs_0_, bf16[128,4096]{1,0:T(8,128)(2,1)S(1)} %get-tuple-element.54.refs_1_, bf16[128,512]{1,0:T(8,128)(2,1)S(1)} %copy-done.2, bf16[128,512]{1,0:T(8,128)(2,1)S(1)} %collective-permute-done.refs_3_), custom_call_target="tpu_custom_call" | custom-call | flops 1024 | bytes 1024 | tf_op jit(solution)/shard_map/query_gradient/pallas_call | solution.py:128
  26.3 0.3 turn_pieces.1.tokens_ref
  26.6 3.3 %collective-permute-done.6.refs_1_ = bf16[2,128,512]{2,1,0:T(8,128)(2,1)S(1)} collective-permute-done((bf16[2,128,512]{2,1,0:T(8,128)(2,1)S(1)}, bf16[2,128,512]{2,1,0:T(8,128)(2,1)S(1)}, u32[]{:S(2)}, u32[]{:S(2)}) %collective-permute-start.6) | collective-permute-done | bytes 262176 | tf_op jit(solution)/shard_map/ppermute | solution.py:425
  29.9 3.8 %collective-permute-done.7.refs_2_ = bf16[2,128,512]{2,1,0:T(8,128)(2,1)S(1)} collective-permute-done((bf16[2,128,512]{2,1,0:T(8,128)(2,1)S(1)}, bf16[2,128,512]{2,1,0:T(8,128)(2,1)S(1)}, u32[]{:S(2)}, u32[]{:S(2)}) %collective-permute-start.7) | collective-permute-done | bytes 262176 | tf_op jit(solution)/shard_map/ppermute | solution.py:425
  33.7 0.0 collective-permute-done.8.refs_3_
  33.7 0.4 weight_other_core.2
  34.2 0.1 collective-permute-start.9
  34.3 0.4 weight_other_core.3
  34.7 0.6 collective-permute-start.12
  35.3 0.4 weight_this_core.2.mine_ref
  35.7 0.5 collective-permute-done.9.theirs_ref
  36.2 0.1 chip_total.2
  36.3 1.6 %collective-permute-start.10 = (bf16[128,512]{1,0:T(8,128)(2,1)S(1)}, bf16[128,512]{1,0:T(8,128)(2,1)S(1)}, u32[]{:S(2)}, u32[]{:S(2)}) collective-permute-start(bf16[128,512]{1,0:T(8,128)(2,1)S(1)} %get-tuple-element.65), channel_id=1, source_target_pairs={{0,1},{1,0},{2,3},{3,2},{4,5},{5,4},{6,7},{7,6},{8,9},{9,8},{10,11... | collective-permute-start | bytes 393224 | tf_op jit(solution)/shard_map/ppermute | solution.py:413
  37.8 0.4 weight_this_core.3.mine_ref
  38.3 0.0 collective-permute-done.12.theirs_ref
  38.3 0.1 chip_total.3
  38.4 3.5 %collective-permute-done.10.refs_0_ = bf16[128,512]{1,0:T(8,128)(2,1)S(1)} collective-permute-done((bf16[128,512]{1,0:T(8,128)(2,1)S(1)}, bf16[128,512]{1,0:T(8,128)(2,1)S(1)}, u32[]{:S(2)}, u32[]{:S(2)}) %collective-permute-start.10) | collective-permute-done | bytes 131104 | tf_op jit(solution)/shard_map/ppermute | solution.py:413
  41.9 1.6 %collective-permute-start.13 = (bf16[128,512]{1,0:T(8,128)(2,1)S(1)}, bf16[128,512]{1,0:T(8,128)(2,1)S(1)}, u32[]{:S(2)}, u32[]{:S(2)}) collective-permute-start(bf16[128,512]{1,0:T(8,128)(2,1)S(1)} %get-tuple-element.71), channel_id=1, source_target_pairs={{0,1},{1,0},{2,3},{3,2},{4,5},{5,4},{6,7},{7,6},{8,9},{9,8},{10,11... | collective-permute-start | bytes 393224 | tf_op jit(solution)/shard_map/ppermute | solution.py:413
  43.5 2.6 %collective-permute-start.11 = (bf16[128,512]{1,0:T(8,128)(2,1)S(1)}, bf16[128,512]{1,0:T(8,128)(2,1)S(1)}, u32[]{:S(2)}, u32[]{:S(2)}) collective-permute-start(bf16[128,512]{1,0:T(8,128)(2,1)S(1)} %relay_total.2), channel_id=1, source_target_pairs={{0,16},{2,18},{4,20},{6,22},{8,24},{10,26},{12,28},{14,30},{16,0},... | collective-permute-start | bytes 393224 | tf_op jit(solution)/shard_map/ppermute | solution.py:418
  46.0 0.9 %collective-permute-done.13.refs_0_ = bf16[128,512]{1,0:T(8,128)(2,1)S(1)} collective-permute-done((bf16[128,512]{1,0:T(8,128)(2,1)S(1)}, bf16[128,512]{1,0:T(8,128)(2,1)S(1)}, u32[]{:S(2)}, u32[]{:S(2)}) %collective-permute-start.13) | collective-permute-done | bytes 131104 | tf_op jit(solution)/shard_map/ppermute | solution.py:413
  46.9 2.6 %collective-permute-start.15 = (bf16[128,512]{1,0:T(8,128)(2,1)S(1)}, bf16[128,512]{1,0:T(8,128)(2,1)S(1)}, u32[]{:S(2)}, u32[]{:S(2)}) collective-permute-start(bf16[128,512]{1,0:T(8,128)(2,1)S(1)} %relay_total.3), channel_id=1, source_target_pairs={{0,16},{2,18},{4,20},{6,22},{8,24},{10,26},{12,28},{14,30},{16,0},... | collective-permute-start | bytes 393224 | tf_op jit(solution)/shard_map/ppermute | solution.py:418
  49.6 1.6 %collective-permute-start.14 = (bf16[256,512]{1,0:T(8,128)(2,1)S(1)}, bf16[256,512]{1,0:T(8,128)(2,1)S(1)}, u32[]{:S(2)}, u32[]{:S(2)}) collective-permute-start(bf16[256,512]{1,0:T(8,128)(2,1)S(1)} %pad_maximum_fusion), channel_id=1, source_target_pairs={{0,1},{1,0},{2,3},{3,2},{4,5},{5,4},{6,7},{7,6},{8,9},{9,8},{10,11... | collective-permute-start | bytes 786440 | tf_op jit(solution)/shard_map/ppermute | solution.py:413
  51.2 4.1 %collective-permute-done.11.refs_1_ = bf16[128,512]{1,0:T(8,128)(2,1)S(1)} collective-permute-done((bf16[128,512]{1,0:T(8,128)(2,1)S(1)}, bf16[128,512]{1,0:T(8,128)(2,1)S(1)}, u32[]{:S(2)}, u32[]{:S(2)}) %collective-permute-start.11) | collective-permute-done | bytes 131104 | tf_op jit(solution)/shard_map/ppermute | solution.py:418
  55.3 1.9 %collective-permute-done.15.refs_2_ = bf16[128,512]{1,0:T(8,128)(2,1)S(1)} collective-permute-done((bf16[128,512]{1,0:T(8,128)(2,1)S(1)}, bf16[128,512]{1,0:T(8,128)(2,1)S(1)}, u32[]{:S(2)}, u32[]{:S(2)}) %collective-permute-start.15) | collective-permute-done | bytes 131104 | tf_op jit(solution)/shard_map/ppermute | solution.py:418
  57.2 0.0 collective-permute-done.14.refs_0_
  57.2 0.8 %weight_total.1 = (f32[128,512]{1,0:T(8,128)}, f32[128,512]{1,0:T(8,128)}) custom-call(f32[128,512]{1,0:T(8,128)S(1)} %key_part_total.1.key_in, bf16[256,512]{1,0:T(8,128)(2,1)S(1)} %collective-permute-done.14.refs_0_, f32[128,512]{1,0:T(8,128)S(1)} %get-tuple-element.74.refs_1_, bf16[128,512]{1,0:T(8,128)(2,1)S(1)} %collective-permute-done.15.refs_2_), custom_call_target="tpu_custom_call" | custom-call | flops 1024 | bytes 1024 | tf_op jit(solution)/shard_map/weight_total/pallas_call | solution.py:385
  (12 shorter events, 0.2 us)
Async XLA Ops:
  0.6 8.1 %copy-start = (bf16[128,4096]{1,0:T(8,128)(2,1)S(1)}, bf16[128,4096]{1,0:T(8,128)(2,1)}, u32[]{:S(2)}) copy-start(bf16[128,4096]{1,0:T(8,128)(2,1)} %refs_2_.4) | copy-start | bytes 3145732
  0.6 10.8 %collective-permute-start = (bf16[128,512]{1,0:T(8,128)(2,1)}, bf16[128,512]{1,0:T(8,128)(2,1)S(1)}, u32[]{:S(2)}, u32[]{:S(2)}) collective-permute-start(bf16[128,512]{1,0:T(8,128)(2,1)} %refs_2_.5), channel_id=1, source_target_pairs={{0,1},{1,0},{2,3},{3,2},{4,5},{5,4},{6,7},{7,6},{8,9},{9,8},{10,11... | collective-permute-start | bytes 393224 | tf_op jit(solution)/shard_map/ppermute | solution.py:413
  3.6 7.8 %collective-permute-start.1 = (bf16[128,512]{1,0:T(8,128)(2,1)}, bf16[128,512]{1,0:T(8,128)(2,1)S(1)}, u32[]{:S(2)}, u32[]{:S(2)}) collective-permute-start(bf16[128,512]{1,0:T(8,128)(2,1)} %refs_4_.1), channel_id=1, source_target_pairs={{0,1},{1,0},{2,3},{3,2},{4,5},{5,4},{6,7},{7,6},{8,9},{9,8},{10,11... | collective-permute-start | bytes 393224 | tf_op jit(solution)/shard_map/ppermute | solution.py:413
  5.1 13.1 %collective-permute-start.3 = (bf16[128,1024]{1,0:T(8,128)(2,1)S(1)}, bf16[128,1024]{1,0:T(8,128)(2,1)S(1)}, u32[]{:S(2)}, u32[]{:S(2)}) collective-permute-start(bf16[128,1024]{1,0:T(8,128)(2,1)S(1)} %get-tuple-element.44), channel_id=1, source_target_pairs={{0,8},{2,10},{4,12},{6,14},{8,0},{10,2},{12,4},{14,6},{16,24},{18,... | collective-permute-start | bytes 786440 | tf_op jit(solution)/shard_map/ppermute | solution.py:425
  7.2 12.8 %collective-permute-start.4 = (bf16[128,1024]{1,0:T(8,128)(2,1)S(1)}, bf16[128,1024]{1,0:T(8,128)(2,1)S(1)}, u32[]{:S(2)}, u32[]{:S(2)}) collective-permute-start(bf16[128,1024]{1,0:T(8,128)(2,1)S(1)} %get-tuple-element.45), channel_id=1, source_target_pairs={{0,4},{2,6},{4,0},{6,2},{8,12},{10,14},{12,8},{14,10},{16,20},{18,... | collective-permute-start | bytes 786440 | tf_op jit(solution)/shard_map/ppermute | solution.py:425
  8.7 2.7 %copy-start.1 = (bf16[128,4096]{1,0:T(8,128)(2,1)S(1)}, bf16[128,4096]{1,0:T(8,128)(2,1)}, u32[]{:S(2)}) copy-start(bf16[128,4096]{1,0:T(8,128)(2,1)} %refs_1_.3) | copy-start | bytes 3145732
  8.7 2.7 %copy-start.4 = (f32[128,32]{0,1:T(8,128)S(1)}, f32[128,32]{0,1:T(8,128)}, u32[]{:S(2)}) copy-start(f32[128,32]{0,1:T(8,128)} %param.13) | copy-start | bytes 49156
  8.7 11.3 %collective-permute-start.5 = (bf16[128,1024]{1,0:T(8,128)(2,1)S(1)}, bf16[128,1024]{1,0:T(8,128)(2,1)S(1)}, u32[]{:S(2)}, u32[]{:S(2)}) collective-permute-start(bf16[128,1024]{1,0:T(8,128)(2,1)S(1)} %get-tuple-element.46), channel_id=1, source_target_pairs={{0,12},{2,14},{4,8},{6,10},{8,4},{10,6},{12,0},{14,2},{16,28},{18,... | collective-permute-start | bytes 786440 | tf_op jit(solution)/shard_map/ppermute | solution.py:425
  11.5 4.4 %copy-start.2 = (bf16[128,512]{1,0:T(8,128)(2,1)S(1)}, bf16[128,512]{1,0:T(8,128)(2,1)}, u32[]{:S(2)}) copy-start(bf16[128,512]{1,0:T(8,128)(2,1)} %refs_2_.5) | copy-start | bytes 393220
  11.5 4.4 %copy-start.3 = (bf16[128,512]{1,0:T(8,128)(2,1)S(1)}, bf16[128,512]{1,0:T(8,128)(2,1)}, u32[]{:S(2)}) copy-start(bf16[128,512]{1,0:T(8,128)(2,1)} %refs_4_.1) | copy-start | bytes 393220
  14.0 7.0 %collective-permute-start.2 = (bf16[2,128,512]{2,1,0:T(8,128)(2,1)S(1)}, bf16[2,128,512]{2,1,0:T(8,128)(2,1)S(1)}, u32[]{:S(2)}, u32[]{:S(2)}) collective-permute-start(bf16[2,128,512]{2,1,0:T(8,128)(2,1)S(1)} %get-tuple-element.40), channel_id=1, source_target_pairs={{0,1},{1,0},{2,3},{3,2},{4,5},{5,4},{6,7},{7,6},{8,9},{9,8},{10,11... | collective-permute-start | bytes 786440 | tf_op jit(solution)/shard_map/ppermute | solution.py:413
  21.0 8.9 %collective-permute-start.6 = (bf16[2,128,512]{2,1,0:T(8,128)(2,1)S(1)}, bf16[2,128,512]{2,1,0:T(8,128)(2,1)S(1)}, u32[]{:S(2)}, u32[]{:S(2)}) collective-permute-start(bf16[2,128,512]{2,1,0:T(8,128)(2,1)S(1)} %grads_total.1.refs_0_), channel_id=1, source_target_pairs={{0,8},{2,10},{4,12},{6,14},{8,0},{10,2},{12,4},{14,6},{16,24},{18,... | collective-permute-start | bytes 786440 | tf_op jit(solution)/shard_map/ppermute | solution.py:425
  22.7 11.1 %collective-permute-start.7 = (bf16[2,128,512]{2,1,0:T(8,128)(2,1)S(1)}, bf16[2,128,512]{2,1,0:T(8,128)(2,1)S(1)}, u32[]{:S(2)}, u32[]{:S(2)}) collective-permute-start(bf16[2,128,512]{2,1,0:T(8,128)(2,1)S(1)} %grads_total.1.refs_0_), channel_id=1, source_target_pairs={{0,4},{2,6},{4,0},{6,2},{8,12},{10,14},{12,8},{14,10},{16,20},{18,... | collective-permute-start | bytes 786440 | tf_op jit(solution)/shard_map/ppermute | solution.py:425
  24.2 9.5 %collective-permute-start.8 = (bf16[2,128,512]{2,1,0:T(8,128)(2,1)S(1)}, bf16[2,128,512]{2,1,0:T(8,128)(2,1)S(1)}, u32[]{:S(2)}, u32[]{:S(2)}) collective-permute-start(bf16[2,128,512]{2,1,0:T(8,128)(2,1)S(1)} %grads_total.1.refs_0_), channel_id=1, source_target_pairs={{0,12},{2,14},{4,8},{6,10},{8,4},{10,6},{12,0},{14,2},{16,28},{18,... | collective-permute-start | bytes 786440 | tf_op jit(solution)/shard_map/ppermute | solution.py:425
  34.2 2.0 %collective-permute-start.9 = (bf16[512,512]{1,0:T(8,128)(2,1)S(1)}, bf16[512,512]{1,0:T(8,128)(2,1)S(1)}, u32[]{:S(2)}, u32[]{:S(2)}) collective-permute-start(bf16[512,512]{1,0:T(8,128)(2,1)S(1)} %weight_other_core.2), channel_id=1, source_target_pairs={{0,2},{2,0},{4,6},{6,4},{8,10},{10,8},{12,14},{14,12},{16,18},{18,... | collective-permute-start | bytes 1572872 | tf_op jit(solution)/shard_map/ppermute | solution.py:421
  34.7 3.5 %collective-permute-start.12 = (bf16[512,512]{1,0:T(8,128)(2,1)S(1)}, bf16[512,512]{1,0:T(8,128)(2,1)S(1)}, u32[]{:S(2)}, u32[]{:S(2)}) collective-permute-start(bf16[512,512]{1,0:T(8,128)(2,1)S(1)} %weight_other_core.3), channel_id=1, source_target_pairs={{0,2},{2,0},{4,6},{6,4},{8,10},{10,8},{12,14},{14,12},{16,18},{18,... | collective-permute-start | bytes 1572872 | tf_op jit(solution)/shard_map/ppermute | solution.py:421
  36.3 5.6 %collective-permute-start.10 = (bf16[128,512]{1,0:T(8,128)(2,1)S(1)}, bf16[128,512]{1,0:T(8,128)(2,1)S(1)}, u32[]{:S(2)}, u32[]{:S(2)}) collective-permute-start(bf16[128,512]{1,0:T(8,128)(2,1)S(1)} %get-tuple-element.65), channel_id=1, source_target_pairs={{0,1},{1,0},{2,3},{3,2},{4,5},{5,4},{6,7},{7,6},{8,9},{9,8},{10,11... | collective-permute-start | bytes 393224 | tf_op jit(solution)/shard_map/ppermute | solution.py:413
  41.9 5.0 %collective-permute-start.13 = (bf16[128,512]{1,0:T(8,128)(2,1)S(1)}, bf16[128,512]{1,0:T(8,128)(2,1)S(1)}, u32[]{:S(2)}, u32[]{:S(2)}) collective-permute-start(bf16[128,512]{1,0:T(8,128)(2,1)S(1)} %get-tuple-element.71), channel_id=1, source_target_pairs={{0,1},{1,0},{2,3},{3,2},{4,5},{5,4},{6,7},{7,6},{8,9},{9,8},{10,11... | collective-permute-start | bytes 393224 | tf_op jit(solution)/shard_map/ppermute | solution.py:413
  43.5 11.8 %collective-permute-start.11 = (bf16[128,512]{1,0:T(8,128)(2,1)S(1)}, bf16[128,512]{1,0:T(8,128)(2,1)S(1)}, u32[]{:S(2)}, u32[]{:S(2)}) collective-permute-start(bf16[128,512]{1,0:T(8,128)(2,1)S(1)} %relay_total.2), channel_id=1, source_target_pairs={{0,16},{2,18},{4,20},{6,22},{8,24},{10,26},{12,28},{14,30},{16,0},... | collective-permute-start | bytes 393224 | tf_op jit(solution)/shard_map/ppermute | solution.py:418
  46.9 10.3 %collective-permute-start.15 = (bf16[128,512]{1,0:T(8,128)(2,1)S(1)}, bf16[128,512]{1,0:T(8,128)(2,1)S(1)}, u32[]{:S(2)}, u32[]{:S(2)}) collective-permute-start(bf16[128,512]{1,0:T(8,128)(2,1)S(1)} %relay_total.3), channel_id=1, source_target_pairs={{0,16},{2,18},{4,20},{6,22},{8,24},{10,26},{12,28},{14,30},{16,0},... | collective-permute-start | bytes 393224 | tf_op jit(solution)/shard_map/ppermute | solution.py:418
  49.6 7.6 %collective-permute-start.14 = (bf16[256,512]{1,0:T(8,128)(2,1)S(1)}, bf16[256,512]{1,0:T(8,128)(2,1)S(1)}, u32[]{:S(2)}, u32[]{:S(2)}) collective-permute-start(bf16[256,512]{1,0:T(8,128)(2,1)S(1)} %pad_maximum_fusion), channel_id=1, source_target_pairs={{0,1},{1,0},{2,3},{3,2},{4,5},{5,4},{6,7},{7,6},{8,9},{9,8},{10,11... | collective-permute-start | bytes 786440 | tf_op jit(solution)/shard_map/ppermute | solution.py:413

commit v8 on v7

v8 whole, which is shorter than its diff:
```python
import functools
import math

import jax
import jax.numpy as jnp
from jax import lax
from jax.experimental import pallas as pl
from jax.experimental.pallas import tpu as pltpu
from jax.sharding import PartitionSpec as P

QUERY_HEADS = 32
KEY_VALUE_HEADS = 4
HEAD_SIZE = 128
GROUP = QUERY_HEADS // KEY_VALUE_HEADS
SCALE = 1.0 / math.sqrt(HEAD_SIZE)
CORES = 2
MIDDLE = 2
NEAR = 2
PARAMS = pltpu.CompilerParams(vmem_limit_bytes=32 * 2**20)
COST = pl.CostEstimate(flops=1024, bytes_accessed=1024, transcendentals=0)
NEAR_COST = pl.CostEstimate(flops=10**10, bytes_accessed=1024, transcendentals=0)
EARLY = pl.CostEstimate(flops=10**10, bytes_accessed=1024, transcendentals=0)
WHOLE = pl.BlockSpec(memory_space=pltpu.VMEM)
FAR = pl.BlockSpec(memory_space=pltpu.HBM)
SCALARS = pl.BlockSpec(memory_space=pltpu.SMEM)

NT = (((1,), (1,)), ((), ()))
TN = (((0,), (0,)), ((), ()))
NN = (((1,), (0,)), ((), ()))


def dot(a, b, dims):
    return lax.dot_general(a, b, dims, preferred_element_type=jnp.float32)


def pinned(value):
    return pltpu.with_memory_space_constraint(value, pltpu.HBM)


def shape(dims, dtype):
    return jax.ShapeDtypeStruct(dims, dtype)


def rows_of_heads(block):
    return jnp.concatenate(
        [block[:, h * HEAD_SIZE : (h + 1) * HEAD_SIZE] for h in range(GROUP)], axis=0
    )


def allowed_mask(lengths_ref, ctx_count, rank, owner, keys, rows):
    key_pos = lax.broadcasted_iota(jnp.int32, (keys, rows), 0) * ctx_count + owner
    query_pos = lax.broadcasted_iota(jnp.int32, (keys, rows), 1) * ctx_count + rank
    allowed = key_pos <= query_pos
    end = jnp.int32(0)
    for j in range(lengths_ref.shape[1]):
        end = end + lengths_ref[0, j]
        allowed = allowed & ((end <= key_pos) == (end <= query_pos))
    return allowed


def delta_rows(do, out):
    width = do.shape[1]
    pick = (
        lax.broadcasted_iota(jnp.int32, (GROUP, width), 1) // HEAD_SIZE
        == lax.broadcasted_iota(jnp.int32, (GROUP, width), 0)
    ).astype(jnp.bfloat16)
    product = do.astype(jnp.float32) * out.astype(jnp.float32)
    high = product.astype(jnp.bfloat16)
    low = (product - high.astype(jnp.float32)).astype(jnp.bfloat16)
    return dot(pick, high, NT) + dot(pick, low, NT)


def block_kernel(ctx_count, step, *refs):
    lengths_ref, q_ref, do_ref, k_ref, v_ref, lse_ref, other_ref, ds_ref, grad_ref = refs[:9]
    width = GROUP * HEAD_SIZE
    rank = lax.axis_index("ctx")
    owner = lax.rem(rank + ctx_count - step, ctx_count)
    rows = q_ref.shape[0]
    keys = k_ref.shape[0]
    allowed = allowed_mask(lengths_ref, ctx_count, rank, owner, keys, rows)
    for g in range(KEY_VALUE_HEADS):
        wide = slice(g * width, (g + 1) * width)
        q = rows_of_heads(q_ref[:, wide])
        do = rows_of_heads(do_ref[:, wide])
        group = slice(g * GROUP, (g + 1) * GROUP)
        if step == 1:
            delta = delta_rows(do_ref[:, wide], other_ref[:, wide])
            refs[9][group, :] = delta
        else:
            delta = other_ref[group, :]
        lse = lse_ref[group, :]
        columns = slice(g * HEAD_SIZE, (g + 1) * HEAD_SIZE)
        scores = dot(k_ref[:, columns], q, NT)
        grad_probs = dot(v_ref[:, columns], do, NT)
        probs_low = []
        grad_scores = []
        for h in range(GROUP):
            cut = slice(h * rows, (h + 1) * rows)
            probs = jnp.where(allowed, jnp.exp(scores[:, cut] * SCALE - lse[h : h + 1, :]), 0.0)
            grad_scores.append(
                (probs * (grad_probs[:, cut] - delta[h : h + 1, :])).astype(jnp.bfloat16)
            )
            probs_low.append(probs.astype(jnp.bfloat16))
        probs_low = jnp.concatenate(probs_low, axis=1)
        grad_scores = jnp.concatenate(grad_scores, axis=1)
        ds_ref[:, g * GROUP * rows : (g + 1) * GROUP * rows] = grad_scores
        grad_ref[0, :, columns] = (dot(grad_scores, q, NN) * SCALE).astype(grad_ref.dtype)
        grad_ref[1, :, columns] = dot(probs_low, do, NN).astype(grad_ref.dtype)


def block_call(step, ctx_count, lengths, queries, output_gradient, keys, values, lse, other):
    rows = queries.shape[0]
    key_rows, half = keys.shape
    out_shape = [
        shape((key_rows, QUERY_HEADS * rows), jnp.bfloat16),
        shape((2, key_rows, half), jnp.bfloat16 if step else jnp.float32),
    ]
    if step == 1:
        out_shape.append(shape((QUERY_HEADS, rows), jnp.float32))
    return pl.pallas_call(
        functools.partial(block_kernel, ctx_count, step),
        in_specs=[SCALARS] + [WHOLE] * 6,
        out_specs=[WHOLE] * len(out_shape),
        out_shape=out_shape,
        compiler_params=PARAMS,
        cost_estimate=COST,
        name="visiting_keys" if step else "own_keys",
    )(lengths, queries, output_gradient, keys, values, lse, other)


def query_kernel(count, *refs):
    ds_refs, k_refs, out_ref = refs[:count], refs[count:-1], refs[-1]
    rows = out_ref.shape[0]
    for g in range(KEY_VALUE_HEADS):
        columns = slice(g * HEAD_SIZE, (g + 1) * HEAD_SIZE)
        keys = jnp.concatenate([k[:, columns] for k in k_refs], axis=0)
        for head in range(g * GROUP, (g + 1) * GROUP):
            scores = jnp.concatenate(
                [ref[:, head * rows : (head + 1) * rows] for ref in ds_refs], axis=0
            )
            out_ref[:, head * HEAD_SIZE : (head + 1) * HEAD_SIZE] = (
                dot(scores, keys, TN) * SCALE
            ).astype(out_ref.dtype)


def query_call(scores, keys, rows):
    return pl.pallas_call(
        functools.partial(query_kernel, len(keys)),
        in_specs=[WHOLE] * (2 * len(keys)),
        out_specs=WHOLE,
        out_shape=shape((rows, QUERY_HEADS * HEAD_SIZE), jnp.bfloat16),
        compiler_params=PARAMS,
        cost_estimate=COST,
        name="query_gradient",
    )(*scores, *keys)


def after(values, others):
    return lax.optimization_barrier((values, others))[0]


def pieces_kernel(far, count, in_hbm, *refs):
    far_refs, piece_refs = refs[:count], refs[count : count + MIDDLE * NEAR]
    near_refs, (sems, near_sems) = refs[count + MIDDLE * NEAR : -2], refs[-2:]
    dp_rank = lax.axis_index("dp")
    y_rank = lax.rem(lax.div(dp_rank, CORES), MIDDLE)
    z_rank = lax.rem(lax.div(dp_rank, CORES * MIDDLE), NEAR)
    width = piece_refs[0].shape[1] // (CORES * far)
    copies = []
    for index, piece_ref in enumerate(piece_refs):
        y = lax.rem(y_rank + index // NEAR, MIDDLE)
        zl = lax.rem(z_rank + index % NEAR, NEAR)
        for core in range(CORES):
            for zh in range(far):
                start = (((zh * NEAR + zl) * MIDDLE + y) * CORES + core) * width
                to = (core * far + zh) * width
                copies.append(
                    pltpu.make_async_copy(
                        in_hbm.at[:, pl.ds(pl.multiple_of(start, width), width)],
                        piece_ref.at[:, to : to + width],
                        sems.at[len(copies)],
                    )
                )
    for i, (far_ref, near_ref) in enumerate(zip(far_refs, near_refs)):
        copies.append(pltpu.make_async_copy(far_ref, near_ref, near_sems.at[i]))
    for copy in copies:
        copy.start()
    for copy in copies:
        copy.wait()


def pieces_call(normed, wanted, far):
    rows, width = normed.shape
    count = MIDDLE * NEAR
    return pl.pallas_call(
        functools.partial(pieces_kernel, far, len(wanted)),
        in_specs=[FAR] * (1 + len(wanted)),
        out_specs=[WHOLE] * (count + len(wanted)),
        out_shape=[shape((rows, width // count), normed.dtype)] * count
        + [shape(value.shape, value.dtype) for value in wanted],
        scratch_shapes=[
            pltpu.SemaphoreType.DMA((count * CORES * far,)),
            pltpu.SemaphoreType.DMA((len(wanted),)),
        ],
        compiler_params=PARAMS,
        cost_estimate=COST,
        name="pieces",
    )(pinned(normed), *(pinned(value) for value in wanted))


def turn_kernel(*refs):
    out_ref = refs[-1]
    for at, ref in enumerate(refs[:-1]):
        rows = ref.shape[0]
        out_ref[:, at * rows : (at + 1) * rows] = ref[...].T


def turn_call(pieces):
    rows, width = pieces[0].shape
    return pl.pallas_call(
        turn_kernel,
        in_specs=[WHOLE] * len(pieces),
        out_specs=WHOLE,
        out_shape=shape((width, rows * len(pieces)), pieces[0].dtype),
        compiler_params=PARAMS,
        cost_estimate=COST,
        name="turn_pieces",
    )(*pieces)


def add_kernel(own_ref, *refs):
    total = own_ref[...]
    for back_ref in refs[:-1]:
        total = total + back_ref[...].astype(jnp.float32)
    refs[-1][...] = total.astype(refs[-1].dtype)


def add_call(own, back):
    return pl.pallas_call(
        add_kernel,
        in_specs=[WHOLE] * (1 + len(back)),
        out_specs=WHOLE,
        out_shape=shape(own.shape, jnp.bfloat16),
        compiler_params=PARAMS,
        cost_estimate=COST,
        name="grads_total",
    )(own, *back)


def weight_kernel(other, steps, far, tokens_ref, *refs):
    g_refs, out_ref = refs[:-1], refs[-1]
    half = out_ref.shape[1] // 2
    block = out_ref.shape[0] // len(steps)
    dp_rank = lax.axis_index("dp")
    core = lax.rem(dp_rank, CORES)
    z_rank = lax.div(dp_rank, CORES * MIDDLE * NEAR)
    if other:
        core = 1 - core
    grads = [jnp.concatenate([g[part] for g in g_refs], axis=0) for part in range(2)]
    for at, step in enumerate(steps):
        start = (core * far + lax.rem(z_rank + step, far)) * block
        tokens = tokens_ref[pl.ds(pl.multiple_of(start, block), block), :]
        for part in range(2):
            out_ref[at * block : (at + 1) * block, part * half : (part + 1) * half] = dot(
                tokens, grads[part], NN
            ).astype(out_ref.dtype)


def weight_call(other, steps, far, tokens, grads, dtype, cost=COST):
    height = tokens.shape[0] // (CORES * far) * len(steps)
    return pl.pallas_call(
        functools.partial(weight_kernel, other, steps, far),
        in_specs=[WHOLE] * (1 + len(grads)),
        out_specs=WHOLE,
        out_shape=shape((height, 2 * grads[0].shape[2]), dtype),
        compiler_params=PARAMS,
        cost_estimate=cost,
        name="weight_other_core" if other else "weight_this_core",
    )(tokens, *grads)


def chip_kernel(ctx_count, count, mine_ref, theirs_ref, *out_refs):
    block = out_refs[0].shape[0] // count
    x_rank = lax.axis_index("ctx")
    cuts = (len(out_refs) - 1) // (ctx_count - 1)
    for x in range(ctx_count):
        outs = out_refs[1 + (x - 1) * cuts : 1 + x * cuts] if x else out_refs[:1]
        for z in range(count):
            start = (z * ctx_count + lax.rem(x_rank + x, ctx_count)) * block
            at = pl.ds(pl.multiple_of(start, block), block)
            total = mine_ref[at, :] + theirs_ref[at, :].astype(jnp.float32)
            width = total.shape[1] // len(outs)
            for i, out in enumerate(outs):
                out[z * block : (z + 1) * block, :] = total[:, i * width : (i + 1) * width].astype(
                    out.dtype
                )


def chip_call(ctx_count, count, cuts, mine, theirs):
    height, columns = mine.shape
    rows = height // ctx_count
    return pl.pallas_call(
        functools.partial(chip_kernel, ctx_count, count),
        in_specs=[WHOLE] * 2,
        out_specs=[WHOLE] * (1 + cuts * (ctx_count - 1)),
        out_shape=[shape((rows, columns), jnp.float32)]
        + [shape((rows, columns // cuts), jnp.bfloat16)] * (cuts * (ctx_count - 1)),
        compiler_params=PARAMS,
        cost_estimate=COST,
        name="chip_far" if cuts > 1 else "chip_near",
    )(mine, theirs)


def relay_kernel(part, count, away_ref, *refs):
    in_refs, out_refs = refs[:-count], refs[-count:]
    block, width = out_refs[0].shape
    columns = slice(part * width, (part + 1) * width)
    for z, out_ref in enumerate(out_refs):
        at = slice(z * block, (z + 1) * block)
        total = away_ref[at, columns]
        for in_ref in in_refs:
            total = total + in_ref[at, :].astype(jnp.float32)
        out_ref[...] = total.astype(out_ref.dtype)


def relay_call(part, count, away, arrived):
    height, width = arrived[0].shape
    return pl.pallas_call(
        functools.partial(relay_kernel, part, count),
        in_specs=[WHOLE] * (1 + len(arrived)),
        out_specs=[WHOLE] * count,
        out_shape=[shape((height // count, width), jnp.bfloat16)] * count,
        compiler_params=PARAMS,
        cost_estimate=COST,
        name="relay_total",
    )(away, *arrived)


def early_kernel(*refs):
    total = refs[0][...].astype(jnp.float32)
    for ref in refs[1:-1]:
        total = total + ref[...].astype(jnp.float32)
    refs[-1][...] = total


def early_call(arrived):
    return pl.pallas_call(
        early_kernel,
        in_specs=[WHOLE] * len(arrived),
        out_specs=WHOLE,
        out_shape=shape(arrived[0].shape, jnp.float32),
        compiler_params=PARAMS,
        cost_estimate=EARLY,
        name="key_far_total",
    )(*arrived)


def final_kernel(near_count, own_ref, key_far_ref, *refs):
    key_ref, value_ref = refs[-2:]
    near_refs, value_refs = refs[:near_count], refs[near_count:-2]
    half = key_ref.shape[1]
    key = own_ref[:, :half] + key_far_ref[...]
    value = own_ref[:, half:]
    for ref in near_refs:
        key = key + ref[:, :half].astype(jnp.float32)
        value = value + ref[:, half:].astype(jnp.float32)
    for ref in value_refs:
        value = value + ref[...].astype(jnp.float32)
    key_ref[...] = key
    value_ref[...] = value


def final_call(own, key_far, near, values):
    return pl.pallas_call(
        functools.partial(final_kernel, len(near)),
        in_specs=[WHOLE] * (2 + len(near) + len(values)),
        out_specs=[WHOLE] * 2,
        out_shape=[shape(key_far.shape, jnp.float32)] * 2,
        compiler_params=PARAMS,
        cost_estimate=COST,
        name="weight_total",
    )(own, key_far, *near, *values)


def local(
    normed_input,
    queries,
    saved_keys,
    saved_values,
    attention_output,
    saved_log_totals,
    output_gradient,
    document_lengths,
):
    rows = queries.shape[0]
    ctx_count = lax.axis_size("ctx")
    dp_count = lax.axis_size("dp")
    far = dp_count // (CORES * MIDDLE * NEAR)

    def over_ctx(value, steps):
        pairs = [(s, (s + steps) % ctx_count) for s in range(ctx_count)]
        return lax.ppermute(value, "ctx", pairs)

    def over_far(value, steps):
        stride = dp_count // far
        pairs = [(s, (s + steps * stride) % dp_count) for s in range(dp_count)]
        return lax.ppermute(value, "dp", pairs)

    def over_cores(value):
        return lax.ppermute(value, "dp", [(s, s ^ 1) for s in range(dp_count)])

    def over_group(value, index):
        flip = index // NEAR * CORES + index % NEAR * CORES * MIDDLE
        return lax.ppermute(value, "dp", [(s, s ^ flip) for s in range(dp_count)])

    visiting = [
        (over_ctx(saved_keys, step), over_ctx(saved_values, step)) for step in range(1, ctx_count)
    ]
    *pieces, other, lse = pieces_call(normed_input, (attention_output, saved_log_totals.T), far)
    pieces = [over_group(piece, index) if index else piece for index, piece in enumerate(pieces)]
    block = functools.partial(
        block_call,
        ctx_count=ctx_count,
        lengths=pinned(document_lengths),
        queries=queries,
        output_gradient=output_gradient,
        lse=lse,
    )
    scores, back = [], []
    for step in range(1, ctx_count):
        keys, values = visiting[step - 1]
        part_scores, grads, *delta = block(step, keys=keys, values=values, other=other)
        other = delta[0] if delta else other
        scores.append(part_scores)
        back.append(over_ctx(grads, -step))
    other = after(other, grads)
    own_scores, own = block(0, keys=saved_keys, values=saved_values, other=other)
    back, pieces = lax.optimization_barrier((back, pieces))
    total = add_call(own, back)
    grads = [over_group(total, i) if i else total for i in range(len(pieces))]
    own_scores, pieces = after((own_scores, pieces), total)
    query_gradient = query_call(
        [own_scores] + scores, [saved_keys] + [pair[0] for pair in visiting], rows
    )
    tokens = turn_call(after(pieces, query_gradient))

    def chip_sums(steps, cuts, grads):
        theirs = weight_call(True, steps, far, tokens, grads, jnp.bfloat16)
        arriving = over_cores(theirs)
        cost = COST if cuts > 1 else NEAR_COST
        mine = weight_call(False, steps, far, tokens, grads, jnp.float32, cost)
        return chip_call(ctx_count, len(steps), cuts, mine, arriving)

    away, *blocks = chip_sums(tuple(range(1, far)), 2, grads)
    arrived = [over_ctx(value, 1 + i // 2) for i, value in enumerate(blocks)]
    from_far = []
    for part in range(2):
        relayed = relay_call(part, far - 1, away, arrived[part::2])
        from_far.append([over_far(value, s) for s, value in enumerate(relayed, 1)])
    own_block, *near = chip_sums((0,), 1, after(grads, blocks))
    near = after(near, relayed)
    near = [over_ctx(value, s) for s, value in enumerate(near, 1)]
    key_weight_grad, value_weight_grad = final_call(
        own_block, early_call(from_far[0]), near, from_far[1]
    )
    return query_gradient, key_weight_grad, value_weight_grad


def solution(mesh):
    both = P(("dp", "ctx"), None)
    return jax.shard_map(
        local,
        mesh=mesh,
        in_specs=(both,) * 7 + (P("dp", None),),
        out_specs=(both,) * 3,
        check_vma=False,
    )
```

time: 58.3 us -> 57.3 us (0.983)
  waiting for transfers between devices: 20.7 us -> 24.3 us
  starting transfers between devices: 22.7 us -> 19.8 us
  Pallas kernels: 13.8 us -> 12.4 us
    pallas_call x11 -> x10, Pallas kernels: 6.02 us -> 3.91 us  [the longest x1 1.94 us: pieces_call(): pl.pallas_call(functools.partial(pieces_kernel, far, len(wanted)), in_spe...]
    ppermute x6, waiting for transfers between devices: 8.94 us -> 10.6 us  [over_group(): return lax.ppermute(value, 'dp', [(s, s ^ flip) for s in range(dp_count)])]
    ppermute x2, starting transfers between devices: 5.21 us -> 3.89 us  [over_far(): return lax.ppermute(value, 'dp', pairs)]
    ppermute x2, waiting for transfers between devices: 6 us -> 7.26 us  [over_far(): return lax.ppermute(value, 'dp', pairs)]
    ppermute x6, starting transfers between devices: 9.63 us -> 8.53 us  [over_ctx(): return lax.ppermute(value, 'ctx', pairs)]
    ppermute x2, waiting for transfers between devices: 0.46 us -> 1.46 us  [over_cores(): return lax.ppermute(value, 'dp', [(s, s ^ 1) for s in range(dp_count)])]
    pallas_call x2, Pallas kernels: 4.85 us -> 5.51 us  [block_call(): pl.pallas_call(functools.partial(block_kernel, ctx_count, step), in_specs...]
  transfers between devices with their start and end apart: 16 -> 16, of which waited for: 9 -> 9; matrix products, arithmetic and copies ran while one was open for 0% -> 0% of each run, Pallas kernels for 21% -> 19%
where the time goes in v8:
time: 57.3 us; the launch traced here: 57.2 us
  waiting for transfers between devices  24.3 us (42%)
  starting transfers between devices  19.8 us (35%)
  Pallas kernels  12.4 us (22%)
  between operations  0.77 us (1%)
    ppermute x6, waiting for transfers between devices, over_group(): return lax.ppermute(value, 'dp', [(s, s ^ flip) for s in range(dp_count)])  10.6 us
    ppermute x6, starting transfers between devices, over_ctx(): return lax.ppermute(value, 'ctx', pairs)  8.53 us
    ppermute x2, waiting for transfers between devices, over_far(): return lax.ppermute(value, 'dp', pairs)  7.26 us
    ppermute x6, starting transfers between devices, over_group(): return lax.ppermute(value, 'dp', [(s, s ^ flip) for s in range(dp_count)])  7.19 us
    pallas_call x2, Pallas kernels, block_call(): pl.pallas_call(functools.partial(block_kernel, ctx_count, step), in_specs...  5.51 us
    ppermute x6, waiting for transfers between devices, over_ctx(): return lax.ppermute(value, 'ctx', pairs)  4.94 us
    ppermute x2, starting transfers between devices, over_far(): return lax.ppermute(value, 'dp', pairs)  3.89 us
    pallas_call x1, Pallas kernels, pieces_call(): pl.pallas_call(functools.partial(pieces_kernel, far, len(wanted)), in_spe...  1.94 us
  transfers between devices with their start and end apart: 16, of which 9 were waited for; matrix products, arithmetic and copies ran while one was open for 0% of the time, Pallas kernels for 19%

profile of v8, /device:TPU:0, one launch (start us, length us, event | category | flops | bytes accessed | tf_op | source)
XLA Modules:
  0.0 57.2 jit_solution(8748183862514103140)
XLA Ops:
  0.6 3.0 %collective-permute-start.1 = (bf16[128,512]{1,0:T(8,128)(2,1)}, bf16[128,512]{1,0:T(8,128)(2,1)S(1)}, u32[]{:S(2)}, u32[]{:S(2)}) collective-permute-start(bf16[128,512]{1,0:T(8,128)(2,1)} %refs_4_.1), channel_id=1, source_target_pairs={{0,1},{1,0},{2,3},{3,2},{4,5},{5,4},{6,7},{7,6},{8,9},{9,8},{10,11... | collective-permute-start | bytes 393224 | tf_op jit(solution)/shard_map/ppermute | solution.py:402
  3.6 0.1 collective-permute-start
  3.7 1.9 %pieces.1 = (bf16[128,1024]{1,0:T(8,128)(2,1)S(1)}, bf16[128,1024]{1,0:T(8,128)(2,1)S(1)}, bf16[128,1024]{1,0:T(8,128)(2,1)S(1)}, bf16[128,1024]{1,0:T(8,128)(2,...) custom-call(bf16[128,4096]{1,0:T(8,128)(2,1)} %in_hbm.1, bf16[128,4096]{1,0:T(8,128)(2,1)} %refs_0_.3, ...), custom_call_target="tpu_custom_call" | custom-call | flops 1024 | bytes 1024 | tf_op jit(solution)/shard_map/pieces/pallas_call | solution.py:195
  5.7 2.1 %collective-permute-start.3 = (bf16[128,1024]{1,0:T(8,128)(2,1)S(1)}, bf16[128,1024]{1,0:T(8,128)(2,1)S(1)}, u32[]{:S(2)}, u32[]{:S(2)}) collective-permute-start(bf16[128,1024]{1,0:T(8,128)(2,1)S(1)} %get-tuple-element.48), channel_id=1, source_target_pairs={{0,8},{2,10},{4,12},{6,14},{8,0},{10,2},{12,4},{14,6},{16,24},{18,... | collective-permute-start | bytes 786440 | tf_op jit(solution)/shard_map/ppermute | solution.py:414
  7.8 1.5 %collective-permute-start.4 = (bf16[128,1024]{1,0:T(8,128)(2,1)S(1)}, bf16[128,1024]{1,0:T(8,128)(2,1)S(1)}, u32[]{:S(2)}, u32[]{:S(2)}) collective-permute-start(bf16[128,1024]{1,0:T(8,128)(2,1)S(1)} %get-tuple-element.49), channel_id=1, source_target_pairs={{0,4},{2,6},{4,0},{6,2},{8,12},{10,14},{12,8},{14,10},{16,20},{18,... | collective-permute-start | bytes 786440 | tf_op jit(solution)/shard_map/ppermute | solution.py:414
  9.3 0.0 collective-permute-start.5
  9.3 0.0 collective-permute-done.1.refs_4_
  9.3 0.8 %collective-permute-done.refs_3_ = bf16[128,512]{1,0:T(8,128)(2,1)S(1)} collective-permute-done((bf16[128,512]{1,0:T(8,128)(2,1)}, bf16[128,512]{1,0:T(8,128)(2,1)S(1)}, u32[]{:S(2)}, u32[]{:S(2)}) %collective-permute-start) | collective-permute-done | bytes 131104 | tf_op jit(solution)/shard_map/ppermute | solution.py:402
  10.2 0.0 copy-done
  10.2 0.0 copy-done.1
  10.2 3.1 %visiting_keys.1 = (bf16[128,4096]{1,0:T(8,128)(2,1)S(1)}, bf16[2,128,512]{2,1,0:T(8,128)(2,1)S(1)}, f32[32,128]{1,0:T(8,128)S(1)}) custom-call(s32[1,4]{1,0:T(1,128)} %refs_0_.5, bf16[128,4096]{1,0:T(8,128)(2,1)S(1)} %copy-done, bf16[128,4096]{1,0:T(8,128)(2,1)S(1)} %copy-done.1, bf16[128,512]{1,0:T(8,128)(2,1)S(1)} %collective-permute-done.refs_3_, ...), custom_call_target="tpu_custom_call" | custom-call | flops 1024 | bytes 1024 | tf_op jit(solution)/shard_map/visiting_keys/pallas_call | solution.py:120
  13.3 1.8 %collective-permute-start.2 = (bf16[2,128,512]{2,1,0:T(8,128)(2,1)S(1)}, bf16[2,128,512]{2,1,0:T(8,128)(2,1)S(1)}, u32[]{:S(2)}, u32[]{:S(2)}) collective-permute-start(bf16[2,128,512]{2,1,0:T(8,128)(2,1)S(1)} %get-tuple-element.44), channel_id=1, source_target_pairs={{0,1},{1,0},{2,3},{3,2},{4,5},{5,4},{6,7},{7,6},{8,9},{9,8},{10,11... | collective-permute-start | bytes 786440 | tf_op jit(solution)/shard_map/ppermute | solution.py:402
  15.1 0.0 copy-done.2
  15.1 0.0 copy-done.3
  15.1 2.4 %own_keys.1 = (bf16[128,4096]{1,0:T(8,128)(2,1)S(1)}, f32[2,128,512]{2,1,0:T(8,128)S(1)}) custom-call(s32[1,4]{1,0:T(1,128)} %refs_0_.5, bf16[128,4096]{1,0:T(8,128)(2,1)S(1)} %copy-done, bf16[128,4096]{1,0:T(8,128)(2,1)S(1)} %copy-done.1, bf16[128,512]{1,0:T(8,128)(2,1)S(1)} %copy-done.2, bf16[128,512]{1,0:T(8,128)(2,1)S(1)} %copy-done.3, ...), custom_call_target="tpu_custom_call" | custom-call | flops 1024 | bytes 1024 | tf_op jit(solution)/shard_map/own_keys/pallas_call | solution.py:120
  17.5 0.0 collective-permute-done.3.refs_1_
  17.5 3.1 %collective-permute-done.4.refs_2_ = bf16[128,1024]{1,0:T(8,128)(2,1)S(1)} collective-permute-done((bf16[128,1024]{1,0:T(8,128)(2,1)S(1)}, bf16[128,1024]{1,0:T(8,128)(2,1)S(1)}, u32[]{:S(2)}, u32[]{:S(2)}) %collective-permute-start.4) | collective-permute-done | bytes 262176 | tf_op jit(solution)/shard_map/ppermute | solution.py:414
  20.6 0.0 collective-permute-done.5.refs_3_
  20.6 0.3 collective-permute-done.2.refs_0_
  20.9 2.5 %collective-permute-start.8 = (bf16[2,128,512]{2,1,0:T(8,128)(2,1)S(1)}, bf16[2,128,512]{2,1,0:T(8,128)(2,1)S(1)}, u32[]{:S(2)}, u32[]{:S(2)}) collective-permute-start(bf16[2,128,512]{2,1,0:T(8,128)(2,1)S(1)} %grads_total.1.refs_0_), channel_id=1, source_target_pairs={{0,12},{2,14},{4,8},{6,10},{8,4},{10,6},{12,0},{14,2},{16,28},{18,... | collective-permute-start | bytes 786440 | tf_op jit(solution)/shard_map/ppermute | solution.py:414
  23.5 0.5 collective-permute-start.7
  24.0 0.5 collective-permute-start.6
  24.5 1.7 %query_gradient.1 = bf16[128,4096]{1,0:T(8,128)(2,1)} custom-call(bf16[128,4096]{1,0:T(8,128)(2,1)S(1)} %get-tuple-element.57.refs_0_, bf16[128,4096]{1,0:T(8,128)(2,1)S(1)} %get-tuple-element.58.refs_1_, bf16[128,512]{1,0:T(8,128)(2,1)S(1)} %copy-done.2, bf16[128,512]{1,0:T(8,128)(2,1)S(1)} %collective-permute-done.refs_3_), custom_call_target="tpu_custom_call" | custom-call | flops 1024 | bytes 1024 | tf_op jit(solution)/shard_map/query_gradient/pallas_call | solution.py:147
  26.2 0.3 turn_pieces.1.tokens_ref
  26.5 4.6 %collective-permute-done.8.refs_3_ = bf16[2,128,512]{2,1,0:T(8,128)(2,1)S(1)} collective-permute-done((bf16[2,128,512]{2,1,0:T(8,128)(2,1)S(1)}, bf16[2,128,512]{2,1,0:T(8,128)(2,1)S(1)}, u32[]{:S(2)}, u32[]{:S(2)}) %collective-permute-start.8) | collective-permute-done | bytes 262176 | tf_op jit(solution)/shard_map/ppermute | solution.py:414
  31.2 2.9 %collective-permute-done.7.refs_2_ = bf16[2,128,512]{2,1,0:T(8,128)(2,1)S(1)} collective-permute-done((bf16[2,128,512]{2,1,0:T(8,128)(2,1)S(1)}, bf16[2,128,512]{2,1,0:T(8,128)(2,1)S(1)}, u32[]{:S(2)}, u32[]{:S(2)}) %collective-permute-start.7) | collective-permute-done | bytes 262176 | tf_op jit(solution)/shard_map/ppermute | solution.py:414
  34.1 0.0 collective-permute-done.6.refs_1_
  34.1 0.4 weight_other_core.2
  34.5 0.1 collective-permute-start.9
  34.6 0.4 weight_this_core.2.mine_ref
  35.0 1.5 %collective-permute-done.9.theirs_ref = bf16[256,1024]{1,0:T(8,128)(2,1)S(1)} collective-permute-done((bf16[256,1024]{1,0:T(8,128)(2,1)S(1)}, bf16[256,1024]{1,0:T(8,128)(2,1)S(1)}, u32[]{:S(2)}, u32[]{:S(2)}) %collective-permute-start.9) | collective-permute-done | bytes 524320 | tf_op jit(solution)/shard_map/ppermute | solution.py:410
  36.5 0.1 chip_far.1
  36.6 1.3 %collective-permute-start.11 = (bf16[128,512]{1,0:T(8,128)(2,1)S(1)}, bf16[128,512]{1,0:T(8,128)(2,1)S(1)}, u32[]{:S(2)}, u32[]{:S(2)}) collective-permute-start(bf16[128,512]{1,0:T(8,128)(2,1)S(1)} %get-tuple-element.67), channel_id=1, source_target_pairs={{0,1},{1,0},{2,3},{3,2},{4,5},{5,4},{6,7},{7,6},{8,9},{9,8},{10,11... | collective-permute-start | bytes 393224 | tf_op jit(solution)/shard_map/ppermute | solution.py:402
  37.9 0.8 %collective-permute-start.13 = (bf16[128,512]{1,0:T(8,128)(2,1)S(1)}, bf16[128,512]{1,0:T(8,128)(2,1)S(1)}, u32[]{:S(2)}, u32[]{:S(2)}) collective-permute-start(bf16[128,512]{1,0:T(8,128)(2,1)S(1)} %get-tuple-element.68), channel_id=1, source_target_pairs={{0,1},{1,0},{2,3},{3,2},{4,5},{5,4},{6,7},{7,6},{8,9},{9,8},{10,11... | collective-permute-start | bytes 393224 | tf_op jit(solution)/shard_map/ppermute | solution.py:402
  38.7 0.4 weight_other_core.3
  39.1 0.1 collective-permute-start.10
  39.2 3.8 %collective-permute-done.11.refs_0_ = bf16[128,512]{1,0:T(8,128)(2,1)S(1)} collective-permute-done((bf16[128,512]{1,0:T(8,128)(2,1)S(1)}, bf16[128,512]{1,0:T(8,128)(2,1)S(1)}, u32[]{:S(2)}, u32[]{:S(2)}) %collective-permute-start.11) | collective-permute-done | bytes 131104 | tf_op jit(solution)/shard_map/ppermute | solution.py:402
  43.0 2.4 %collective-permute-start.12 = (bf16[128,512]{1,0:T(8,128)(2,1)S(1)}, bf16[128,512]{1,0:T(8,128)(2,1)S(1)}, u32[]{:S(2)}, u32[]{:S(2)}) collective-permute-start(bf16[128,512]{1,0:T(8,128)(2,1)S(1)} %relay_total.2), channel_id=1, source_target_pairs={{0,16},{2,18},{4,20},{6,22},{8,24},{10,26},{12,28},{14,30},{16,0},... | collective-permute-start | bytes 393224 | tf_op jit(solution)/shard_map/ppermute | solution.py:407
  45.4 0.4 weight_this_core.3.mine_ref
  45.8 0.0 collective-permute-done.13.refs_0_
  45.9 1.5 %collective-permute-start.15 = (bf16[128,512]{1,0:T(8,128)(2,1)S(1)}, bf16[128,512]{1,0:T(8,128)(2,1)S(1)}, u32[]{:S(2)}, u32[]{:S(2)}) collective-permute-start(bf16[128,512]{1,0:T(8,128)(2,1)S(1)} %relay_total.3), channel_id=1, source_target_pairs={{0,16},{2,18},{4,20},{6,22},{8,24},{10,26},{12,28},{14,30},{16,0},... | collective-permute-start | bytes 393224 | tf_op jit(solution)/shard_map/ppermute | solution.py:407
  47.4 0.0 collective-permute-done.10.theirs_ref
  47.4 0.1 chip_near.1
  47.5 1.5 %collective-permute-start.14 = (bf16[128,1024]{1,0:T(8,128)(2,1)S(1)}, bf16[128,1024]{1,0:T(8,128)(2,1)S(1)}, u32[]{:S(2)}, u32[]{:S(2)}) collective-permute-start(bf16[128,1024]{1,0:T(8,128)(2,1)S(1)} %get-tuple-element.76), channel_id=1, source_target_pairs={{0,1},{1,0},{2,3},{3,2},{4,5},{5,4},{6,7},{7,6},{8,9},{9,8},{10,11... | collective-permute-start | bytes 786440 | tf_op jit(solution)/shard_map/ppermute | solution.py:402
  49.0 5.6 %collective-permute-done.12.refs_0_ = bf16[128,512]{1,0:T(8,128)(2,1)S(1)} collective-permute-done((bf16[128,512]{1,0:T(8,128)(2,1)S(1)}, bf16[128,512]{1,0:T(8,128)(2,1)S(1)}, u32[]{:S(2)}, u32[]{:S(2)}) %collective-permute-start.12) | collective-permute-done | bytes 131104 | tf_op jit(solution)/shard_map/ppermute | solution.py:407
  54.7 1.7 %collective-permute-done.15.refs_1_ = bf16[128,512]{1,0:T(8,128)(2,1)S(1)} collective-permute-done((bf16[128,512]{1,0:T(8,128)(2,1)S(1)}, bf16[128,512]{1,0:T(8,128)(2,1)S(1)}, u32[]{:S(2)}, u32[]{:S(2)}) %collective-permute-start.15) | collective-permute-done | bytes 131104 | tf_op jit(solution)/shard_map/ppermute | solution.py:407
  56.3 0.0 collective-permute-done.14.refs_0_
  56.3 0.8 %weight_total.1 = (f32[128,512]{1,0:T(8,128)}, f32[128,512]{1,0:T(8,128)}) custom-call(f32[128,1024]{1,0:T(8,128)S(1)} %get-tuple-element.73.own_ref, f32[128,512]{1,0:T(8,128)S(1)} %key_far_total.1.key_far_ref, bf16[128,1024]{1,0:T(8,128)(2,1)S(1)} %collective-permute-done.14.refs_0_, bf16[128,512]{1,0:T(8,128)(2,1)S(1)} %collective-permute-done.15.refs_1_), custom_call_target="tpu_custom_call" | custom-call | flops 1024 | bytes 1024 | tf_op jit(solution)/shard_map/weight_total/pallas_call | solution.py:374
  (8 shorter events, 0.1 us)
Async XLA Ops:
  0.6 8.7 %collective-permute-start.1 = (bf16[128,512]{1,0:T(8,128)(2,1)}, bf16[128,512]{1,0:T(8,128)(2,1)S(1)}, u32[]{:S(2)}, u32[]{:S(2)}) collective-permute-start(bf16[128,512]{1,0:T(8,128)(2,1)} %refs_4_.1), channel_id=1, source_target_pairs={{0,1},{1,0},{2,3},{3,2},{4,5},{5,4},{6,7},{7,6},{8,9},{9,8},{10,11... | collective-permute-start | bytes 393224 | tf_op jit(solution)/shard_map/ppermute | solution.py:402
  3.6 6.5 %collective-permute-start = (bf16[128,512]{1,0:T(8,128)(2,1)}, bf16[128,512]{1,0:T(8,128)(2,1)S(1)}, u32[]{:S(2)}, u32[]{:S(2)}) collective-permute-start(bf16[128,512]{1,0:T(8,128)(2,1)} %refs_2_.5), channel_id=1, source_target_pairs={{0,1},{1,0},{2,3},{3,2},{4,5},{5,4},{6,7},{7,6},{8,9},{9,8},{10,11... | collective-permute-start | bytes 393224 | tf_op jit(solution)/shard_map/ppermute | solution.py:402
  3.7 6.4 %copy-start = (bf16[128,4096]{1,0:T(8,128)(2,1)S(1)}, bf16[128,4096]{1,0:T(8,128)(2,1)}, u32[]{:S(2)}) copy-start(bf16[128,4096]{1,0:T(8,128)(2,1)} %refs_1_.3) | copy-start | bytes 3145732
  3.7 6.4 %copy-start.1 = (bf16[128,4096]{1,0:T(8,128)(2,1)S(1)}, bf16[128,4096]{1,0:T(8,128)(2,1)}, u32[]{:S(2)}) copy-start(bf16[128,4096]{1,0:T(8,128)(2,1)} %refs_2_.4) | copy-start | bytes 3145732
  5.7 11.8 %collective-permute-start.3 = (bf16[128,1024]{1,0:T(8,128)(2,1)S(1)}, bf16[128,1024]{1,0:T(8,128)(2,1)S(1)}, u32[]{:S(2)}, u32[]{:S(2)}) collective-permute-start(bf16[128,1024]{1,0:T(8,128)(2,1)S(1)} %get-tuple-element.48), channel_id=1, source_target_pairs={{0,8},{2,10},{4,12},{6,14},{8,0},{10,2},{12,4},{14,6},{16,24},{18,... | collective-permute-start | bytes 786440 | tf_op jit(solution)/shard_map/ppermute | solution.py:414
  7.8 12.8 %collective-permute-start.4 = (bf16[128,1024]{1,0:T(8,128)(2,1)S(1)}, bf16[128,1024]{1,0:T(8,128)(2,1)S(1)}, u32[]{:S(2)}, u32[]{:S(2)}) collective-permute-start(bf16[128,1024]{1,0:T(8,128)(2,1)S(1)} %get-tuple-element.49), channel_id=1, source_target_pairs={{0,4},{2,6},{4,0},{6,2},{8,12},{10,14},{12,8},{14,10},{16,20},{18,... | collective-permute-start | bytes 786440 | tf_op jit(solution)/shard_map/ppermute | solution.py:414
  9.3 11.3 %collective-permute-start.5 = (bf16[128,1024]{1,0:T(8,128)(2,1)S(1)}, bf16[128,1024]{1,0:T(8,128)(2,1)S(1)}, u32[]{:S(2)}, u32[]{:S(2)}) collective-permute-start(bf16[128,1024]{1,0:T(8,128)(2,1)S(1)} %get-tuple-element.50), channel_id=1, source_target_pairs={{0,12},{2,14},{4,8},{6,10},{8,4},{10,6},{12,0},{14,2},{16,28},{18,... | collective-permute-start | bytes 786440 | tf_op jit(solution)/shard_map/ppermute | solution.py:414
  10.2 5.0 %copy-start.2 = (bf16[128,512]{1,0:T(8,128)(2,1)S(1)}, bf16[128,512]{1,0:T(8,128)(2,1)}, u32[]{:S(2)}) copy-start(bf16[128,512]{1,0:T(8,128)(2,1)} %refs_2_.5) | copy-start | bytes 393220
  10.2 5.0 %copy-start.3 = (bf16[128,512]{1,0:T(8,128)(2,1)S(1)}, bf16[128,512]{1,0:T(8,128)(2,1)}, u32[]{:S(2)}) copy-start(bf16[128,512]{1,0:T(8,128)(2,1)} %refs_4_.1) | copy-start | bytes 393220
  13.3 7.6 %collective-permute-start.2 = (bf16[2,128,512]{2,1,0:T(8,128)(2,1)S(1)}, bf16[2,128,512]{2,1,0:T(8,128)(2,1)S(1)}, u32[]{:S(2)}, u32[]{:S(2)}) collective-permute-start(bf16[2,128,512]{2,1,0:T(8,128)(2,1)S(1)} %get-tuple-element.44), channel_id=1, source_target_pairs={{0,1},{1,0},{2,3},{3,2},{4,5},{5,4},{6,7},{7,6},{8,9},{9,8},{10,11... | collective-permute-start | bytes 786440 | tf_op jit(solution)/shard_map/ppermute | solution.py:402
  20.9 10.2 %collective-permute-start.8 = (bf16[2,128,512]{2,1,0:T(8,128)(2,1)S(1)}, bf16[2,128,512]{2,1,0:T(8,128)(2,1)S(1)}, u32[]{:S(2)}, u32[]{:S(2)}) collective-permute-start(bf16[2,128,512]{2,1,0:T(8,128)(2,1)S(1)} %grads_total.1.refs_0_), channel_id=1, source_target_pairs={{0,12},{2,14},{4,8},{6,10},{8,4},{10,6},{12,0},{14,2},{16,28},{18,... | collective-permute-start | bytes 786440 | tf_op jit(solution)/shard_map/ppermute | solution.py:414
  23.5 10.6 %collective-permute-start.7 = (bf16[2,128,512]{2,1,0:T(8,128)(2,1)S(1)}, bf16[2,128,512]{2,1,0:T(8,128)(2,1)S(1)}, u32[]{:S(2)}, u32[]{:S(2)}) collective-permute-start(bf16[2,128,512]{2,1,0:T(8,128)(2,1)S(1)} %grads_total.1.refs_0_), channel_id=1, source_target_pairs={{0,4},{2,6},{4,0},{6,2},{8,12},{10,14},{12,8},{14,10},{16,20},{18,... | collective-permute-start | bytes 786440 | tf_op jit(solution)/shard_map/ppermute | solution.py:414
  24.0 10.1 %collective-permute-start.6 = (bf16[2,128,512]{2,1,0:T(8,128)(2,1)S(1)}, bf16[2,128,512]{2,1,0:T(8,128)(2,1)S(1)}, u32[]{:S(2)}, u32[]{:S(2)}) collective-permute-start(bf16[2,128,512]{2,1,0:T(8,128)(2,1)S(1)} %grads_total.1.refs_0_), channel_id=1, source_target_pairs={{0,8},{2,10},{4,12},{6,14},{8,0},{10,2},{12,4},{14,6},{16,24},{18,... | collective-permute-start | bytes 786440 | tf_op jit(solution)/shard_map/ppermute | solution.py:414
  34.5 2.0 %collective-permute-start.9 = (bf16[256,1024]{1,0:T(8,128)(2,1)S(1)}, bf16[256,1024]{1,0:T(8,128)(2,1)S(1)}, u32[]{:S(2)}, u32[]{:S(2)}) collective-permute-start(bf16[256,1024]{1,0:T(8,128)(2,1)S(1)} %weight_other_core.2), channel_id=1, source_target_pairs={{0,2},{2,0},{4,6},{6,4},{8,10},{10,8},{12,14},{14,12},{16,18},{18,... | collective-permute-start | bytes 1572872 | tf_op jit(solution)/shard_map/ppermute | solution.py:410
  36.6 6.4 %collective-permute-start.11 = (bf16[128,512]{1,0:T(8,128)(2,1)S(1)}, bf16[128,512]{1,0:T(8,128)(2,1)S(1)}, u32[]{:S(2)}, u32[]{:S(2)}) collective-permute-start(bf16[128,512]{1,0:T(8,128)(2,1)S(1)} %get-tuple-element.67), channel_id=1, source_target_pairs={{0,1},{1,0},{2,3},{3,2},{4,5},{5,4},{6,7},{7,6},{8,9},{9,8},{10,11... | collective-permute-start | bytes 393224 | tf_op jit(solution)/shard_map/ppermute | solution.py:402
  37.9 8.0 %collective-permute-start.13 = (bf16[128,512]{1,0:T(8,128)(2,1)S(1)}, bf16[128,512]{1,0:T(8,128)(2,1)S(1)}, u32[]{:S(2)}, u32[]{:S(2)}) collective-permute-start(bf16[128,512]{1,0:T(8,128)(2,1)S(1)} %get-tuple-element.68), channel_id=1, source_target_pairs={{0,1},{1,0},{2,3},{3,2},{4,5},{5,4},{6,7},{7,6},{8,9},{9,8},{10,11... | collective-permute-start | bytes 393224 | tf_op jit(solution)/shard_map/ppermute | solution.py:402
  39.1 8.3 %collective-permute-start.10 = (bf16[256,1024]{1,0:T(8,128)(2,1)S(1)}, bf16[256,1024]{1,0:T(8,128)(2,1)S(1)}, u32[]{:S(2)}, u32[]{:S(2)}) collective-permute-start(bf16[256,1024]{1,0:T(8,128)(2,1)S(1)} %weight_other_core.3), channel_id=1, source_target_pairs={{0,2},{2,0},{4,6},{6,4},{8,10},{10,8},{12,14},{14,12},{16,18},{18,... | collective-permute-start | bytes 1572872 | tf_op jit(solution)/shard_map/ppermute | solution.py:410
  43.0 11.6 %collective-permute-start.12 = (bf16[128,512]{1,0:T(8,128)(2,1)S(1)}, bf16[128,512]{1,0:T(8,128)(2,1)S(1)}, u32[]{:S(2)}, u32[]{:S(2)}) collective-permute-start(bf16[128,512]{1,0:T(8,128)(2,1)S(1)} %relay_total.2), channel_id=1, source_target_pairs={{0,16},{2,18},{4,20},{6,22},{8,24},{10,26},{12,28},{14,30},{16,0},... | collective-permute-start | bytes 393224 | tf_op jit(solution)/shard_map/ppermute | solution.py:407
  45.9 10.5 %collective-permute-start.15 = (bf16[128,512]{1,0:T(8,128)(2,1)S(1)}, bf16[128,512]{1,0:T(8,128)(2,1)S(1)}, u32[]{:S(2)}, u32[]{:S(2)}) collective-permute-start(bf16[128,512]{1,0:T(8,128)(2,1)S(1)} %relay_total.3), channel_id=1, source_target_pairs={{0,16},{2,18},{4,20},{6,22},{8,24},{10,26},{12,28},{14,30},{16,0},... | collective-permute-start | bytes 393224 | tf_op jit(solution)/shard_map/ppermute | solution.py:407
  47.5 8.8 %collective-permute-start.14 = (bf16[128,1024]{1,0:T(8,128)(2,1)S(1)}, bf16[128,1024]{1,0:T(8,128)(2,1)S(1)}, u32[]{:S(2)}, u32[]{:S(2)}) collective-permute-start(bf16[128,1024]{1,0:T(8,128)(2,1)S(1)} %get-tuple-element.76), channel_id=1, source_target_pairs={{0,1},{1,0},{2,3},{3,2},{4,5},{5,4},{6,7},{7,6},{8,9},{9,8},{10,11... | collective-permute-start | bytes 786440 | tf_op jit(solution)/shard_map/ppermute | solution.py:402

commit v9 on v8

--- a/solution.py
+++ b/solution.py
@@ -16,6 +16,7 @@
 CORES = 2
 MIDDLE = 2
 NEAR = 2
+ORDER = (0, 3, 2, 1)
 PARAMS = pltpu.CompilerParams(vmem_limit_bytes=32 * 2**20)
 COST = pl.CostEstimate(flops=1024, bytes_accessed=1024, transcendentals=0)
 NEAR_COST = pl.CostEstimate(flops=10**10, bytes_accessed=1024, transcendentals=0)
@@ -437,12 +438,12 @@
     own_scores, own = block(0, keys=saved_keys, values=saved_values, other=other)
     back, pieces = lax.optimization_barrier((back, pieces))
     total = add_call(own, back)
-    grads = [over_group(total, i) if i else total for i in range(len(pieces))]
+    grads = [over_group(total, i) if i else total for i in ORDER]
     own_scores, pieces = after((own_scores, pieces), total)
     query_gradient = query_call(
         [own_scores] + scores, [saved_keys] + [pair[0] for pair in visiting], rows
     )
-    tokens = turn_call(after(pieces, query_gradient))
+    tokens = turn_call(after([pieces[i] for i in ORDER], query_gradient))
 
     def chip_sums(steps, cuts, grads):
         theirs = weight_call(True, steps, far, tokens, grads, jnp.bfloat16)

time: 57.3 us -> 57.4 us (level)
  no operation moved by 1% of the time
where the time goes in v9:
time: 57.4 us; the launch traced here: 57.2 us
  waiting for transfers between devices  24 us (42%)
  starting transfers between devices  20 us (35%)
  Pallas kernels  12.4 us (22%)
  between operations  0.77 us (1%)
    ppermute x6, waiting for transfers between devices, over_group(): return lax.ppermute(value, 'dp', [(s, s ^ flip) for s in range(dp_count)])  10.6 us
    ppermute x6, starting transfers between devices, over_ctx(): return lax.ppermute(value, 'ctx', pairs)  8.54 us
    ppermute x6, starting transfers between devices, over_group(): return lax.ppermute(value, 'dp', [(s, s ^ flip) for s in range(dp_count)])  7.19 us
    ppermute x2, waiting for transfers between devices, over_far(): return lax.ppermute(value, 'dp', pairs)  6.96 us
    pallas_call x2, Pallas kernels, block_call(): pl.pallas_call(functools.partial(block_kernel, ctx_count, step), in_specs...  5.51 us
    ppermute x6, waiting for transfers between devices, over_ctx(): return lax.ppermute(value, 'ctx', pairs)  4.94 us
    ppermute x2, starting transfers between devices, over_far(): return lax.ppermute(value, 'dp', pairs)  4.18 us
    pallas_call x1, Pallas kernels, pieces_call(): pl.pallas_call(functools.partial(pieces_kernel, far, len(wanted)), in_spe...  1.94 us
  transfers between devices with their start and end apart: 16, of which 9 were waited for; matrix products, arithmetic and copies ran while one was open for 0% of the time, Pallas kernels for 19%

profile of v9, /device:TPU:0, one launch (start us, length us, event | category | flops | bytes accessed | tf_op | source)
XLA Modules:
  0.0 57.2 jit_solution(5634392901624616094)
XLA Ops:
  0.6 3.0 %collective-permute-start.1 = (bf16[128,512]{1,0:T(8,128)(2,1)}, bf16[128,512]{1,0:T(8,128)(2,1)S(1)}, u32[]{:S(2)}, u32[]{:S(2)}) collective-permute-start(bf16[128,512]{1,0:T(8,128)(2,1)} %refs_4_.1), channel_id=1, source_target_pairs={{0,1},{1,0},{2,3},{3,2},{4,5},{5,4},{6,7},{7,6},{8,9},{9,8},{10,11... | collective-permute-start | bytes 393224 | tf_op jit(solution)/shard_map/ppermute | solution.py:403
  3.6 0.1 collective-permute-start
  3.7 1.9 %pieces.1 = (bf16[128,1024]{1,0:T(8,128)(2,1)S(1)}, bf16[128,1024]{1,0:T(8,128)(2,1)S(1)}, bf16[128,1024]{1,0:T(8,128)(2,1)S(1)}, bf16[128,1024]{1,0:T(8,128)(2,...) custom-call(bf16[128,4096]{1,0:T(8,128)(2,1)} %in_hbm.1, bf16[128,4096]{1,0:T(8,128)(2,1)} %refs_0_.3, ...), custom_call_target="tpu_custom_call" | custom-call | flops 1024 | bytes 1024 | tf_op jit(solution)/shard_map/pieces/pallas_call | solution.py:196
  5.7 2.1 %collective-permute-start.3 = (bf16[128,1024]{1,0:T(8,128)(2,1)S(1)}, bf16[128,1024]{1,0:T(8,128)(2,1)S(1)}, u32[]{:S(2)}, u32[]{:S(2)}) collective-permute-start(bf16[128,1024]{1,0:T(8,128)(2,1)S(1)} %get-tuple-element.48), channel_id=1, source_target_pairs={{0,8},{2,10},{4,12},{6,14},{8,0},{10,2},{12,4},{14,6},{16,24},{18,... | collective-permute-start | bytes 786440 | tf_op jit(solution)/shard_map/ppermute | solution.py:415
  7.8 1.5 %collective-permute-start.4 = (bf16[128,1024]{1,0:T(8,128)(2,1)S(1)}, bf16[128,1024]{1,0:T(8,128)(2,1)S(1)}, u32[]{:S(2)}, u32[]{:S(2)}) collective-permute-start(bf16[128,1024]{1,0:T(8,128)(2,1)S(1)} %get-tuple-element.49), channel_id=1, source_target_pairs={{0,4},{2,6},{4,0},{6,2},{8,12},{10,14},{12,8},{14,10},{16,20},{18,... | collective-permute-start | bytes 786440 | tf_op jit(solution)/shard_map/ppermute | solution.py:415
  9.3 0.0 collective-permute-start.5
  9.3 0.0 collective-permute-done.1.refs_4_
  9.3 0.8 %collective-permute-done.refs_3_ = bf16[128,512]{1,0:T(8,128)(2,1)S(1)} collective-permute-done((bf16[128,512]{1,0:T(8,128)(2,1)}, bf16[128,512]{1,0:T(8,128)(2,1)S(1)}, u32[]{:S(2)}, u32[]{:S(2)}) %collective-permute-start) | collective-permute-done | bytes 131104 | tf_op jit(solution)/shard_map/ppermute | solution.py:403
  10.2 0.0 copy-done
  10.2 0.0 copy-done.1
  10.2 3.1 %visiting_keys.1 = (bf16[128,4096]{1,0:T(8,128)(2,1)S(1)}, bf16[2,128,512]{2,1,0:T(8,128)(2,1)S(1)}, f32[32,128]{1,0:T(8,128)S(1)}) custom-call(s32[1,4]{1,0:T(1,128)} %refs_0_.5, bf16[128,4096]{1,0:T(8,128)(2,1)S(1)} %copy-done, bf16[128,4096]{1,0:T(8,128)(2,1)S(1)} %copy-done.1, bf16[128,512]{1,0:T(8,128)(2,1)S(1)} %collective-permute-done.refs_3_, ...), custom_call_target="tpu_custom_call" | custom-call | flops 1024 | bytes 1024 | tf_op jit(solution)/shard_map/visiting_keys/pallas_call | solution.py:121
  13.3 1.8 %collective-permute-start.2 = (bf16[2,128,512]{2,1,0:T(8,128)(2,1)S(1)}, bf16[2,128,512]{2,1,0:T(8,128)(2,1)S(1)}, u32[]{:S(2)}, u32[]{:S(2)}) collective-permute-start(bf16[2,128,512]{2,1,0:T(8,128)(2,1)S(1)} %get-tuple-element.44), channel_id=1, source_target_pairs={{0,1},{1,0},{2,3},{3,2},{4,5},{5,4},{6,7},{7,6},{8,9},{9,8},{10,11... | collective-permute-start | bytes 786440 | tf_op jit(solution)/shard_map/ppermute | solution.py:403
  15.1 0.0 copy-done.2
  15.1 0.0 copy-done.3
  15.1 2.4 %own_keys.1 = (bf16[128,4096]{1,0:T(8,128)(2,1)S(1)}, f32[2,128,512]{2,1,0:T(8,128)S(1)}) custom-call(s32[1,4]{1,0:T(1,128)} %refs_0_.5, bf16[128,4096]{1,0:T(8,128)(2,1)S(1)} %copy-done, bf16[128,4096]{1,0:T(8,128)(2,1)S(1)} %copy-done.1, bf16[128,512]{1,0:T(8,128)(2,1)S(1)} %copy-done.2, bf16[128,512]{1,0:T(8,128)(2,1)S(1)} %copy-done.3, ...), custom_call_target="tpu_custom_call" | custom-call | flops 1024 | bytes 1024 | tf_op jit(solution)/shard_map/own_keys/pallas_call | solution.py:121
  17.5 0.0 collective-permute-done.3.refs_3_
  17.5 3.1 %collective-permute-done.4.refs_2_ = bf16[128,1024]{1,0:T(8,128)(2,1)S(1)} collective-permute-done((bf16[128,1024]{1,0:T(8,128)(2,1)S(1)}, bf16[128,1024]{1,0:T(8,128)(2,1)S(1)}, u32[]{:S(2)}, u32[]{:S(2)}) %collective-permute-start.4) | collective-permute-done | bytes 262176 | tf_op jit(solution)/shard_map/ppermute | solution.py:415
  20.6 0.0 collective-permute-done.5.refs_1_
  20.6 0.3 collective-permute-done.2.refs_0_
  20.9 1.6 %collective-permute-start.8 = (bf16[2,128,512]{2,1,0:T(8,128)(2,1)S(1)}, bf16[2,128,512]{2,1,0:T(8,128)(2,1)S(1)}, u32[]{:S(2)}, u32[]{:S(2)}) collective-permute-start(bf16[2,128,512]{2,1,0:T(8,128)(2,1)S(1)} %grads_total.1.refs_0_), channel_id=1, source_target_pairs={{0,8},{2,10},{4,12},{6,14},{8,0},{10,2},{12,4},{14,6},{16,24},{18,... | collective-permute-start | bytes 786440 | tf_op jit(solution)/shard_map/ppermute | solution.py:415
  22.5 1.5 %collective-permute-start.7 = (bf16[2,128,512]{2,1,0:T(8,128)(2,1)S(1)}, bf16[2,128,512]{2,1,0:T(8,128)(2,1)S(1)}, u32[]{:S(2)}, u32[]{:S(2)}) collective-permute-start(bf16[2,128,512]{2,1,0:T(8,128)(2,1)S(1)} %grads_total.1.refs_0_), channel_id=1, source_target_pairs={{0,4},{2,6},{4,0},{6,2},{8,12},{10,14},{12,8},{14,10},{16,20},{18,... | collective-permute-start | bytes 786440 | tf_op jit(solution)/shard_map/ppermute | solution.py:415
  24.0 0.5 collective-permute-start.6
  24.5 1.7 %query_gradient.1 = bf16[128,4096]{1,0:T(8,128)(2,1)} custom-call(bf16[128,4096]{1,0:T(8,128)(2,1)S(1)} %get-tuple-element.57.refs_0_, bf16[128,4096]{1,0:T(8,128)(2,1)S(1)} %get-tuple-element.58.refs_1_, bf16[128,512]{1,0:T(8,128)(2,1)S(1)} %copy-done.2, bf16[128,512]{1,0:T(8,128)(2,1)S(1)} %collective-permute-done.refs_3_), custom_call_target="tpu_custom_call" | custom-call | flops 1024 | bytes 1024 | tf_op jit(solution)/shard_map/query_gradient/pallas_call | solution.py:148
  26.2 0.3 turn_pieces.1.tokens_ref
  26.5 3.7 %collective-permute-done.8.refs_3_ = bf16[2,128,512]{2,1,0:T(8,128)(2,1)S(1)} collective-permute-done((bf16[2,128,512]{2,1,0:T(8,128)(2,1)S(1)}, bf16[2,128,512]{2,1,0:T(8,128)(2,1)S(1)}, u32[]{:S(2)}, u32[]{:S(2)}) %collective-permute-start.8) | collective-permute-done | bytes 262176 | tf_op jit(solution)/shard_map/ppermute | solution.py:415
  30.2 3.9 %collective-permute-done.7.refs_2_ = bf16[2,128,512]{2,1,0:T(8,128)(2,1)S(1)} collective-permute-done((bf16[2,128,512]{2,1,0:T(8,128)(2,1)S(1)}, bf16[2,128,512]{2,1,0:T(8,128)(2,1)S(1)}, u32[]{:S(2)}, u32[]{:S(2)}) %collective-permute-start.7) | collective-permute-done | bytes 262176 | tf_op jit(solution)/shard_map/ppermute | solution.py:415
  34.1 0.0 collective-permute-done.6.refs_1_
  34.1 0.4 weight_other_core.2
  34.5 0.1 collective-permute-start.9
  34.6 0.4 weight_this_core.2.mine_ref
  35.1 1.5 %collective-permute-done.9.theirs_ref = bf16[256,1024]{1,0:T(8,128)(2,1)S(1)} collective-permute-done((bf16[256,1024]{1,0:T(8,128)(2,1)S(1)}, bf16[256,1024]{1,0:T(8,128)(2,1)S(1)}, u32[]{:S(2)}, u32[]{:S(2)}) %collective-permute-start.9) | collective-permute-done | bytes 524320 | tf_op jit(solution)/shard_map/ppermute | solution.py:411
  36.5 0.1 chip_far.1
  36.6 1.5 %collective-permute-start.11 = (bf16[128,512]{1,0:T(8,128)(2,1)S(1)}, bf16[128,512]{1,0:T(8,128)(2,1)S(1)}, u32[]{:S(2)}, u32[]{:S(2)}) collective-permute-start(bf16[128,512]{1,0:T(8,128)(2,1)S(1)} %get-tuple-element.67), channel_id=1, source_target_pairs={{0,1},{1,0},{2,3},{3,2},{4,5},{5,4},{6,7},{7,6},{8,9},{9,8},{10,11... | collective-permute-start | bytes 393224 | tf_op jit(solution)/shard_map/ppermute | solution.py:403
  38.2 0.5 collective-permute-start.13
  38.7 0.4 weight_other_core.3
  39.1 0.1 collective-permute-start.10
  39.2 3.8 %collective-permute-done.11.refs_0_ = bf16[128,512]{1,0:T(8,128)(2,1)S(1)} collective-permute-done((bf16[128,512]{1,0:T(8,128)(2,1)S(1)}, bf16[128,512]{1,0:T(8,128)(2,1)S(1)}, u32[]{:S(2)}, u32[]{:S(2)}) %collective-permute-start.11) | collective-permute-done | bytes 131104 | tf_op jit(solution)/shard_map/ppermute | solution.py:403
  43.0 2.7 %collective-permute-start.12 = (bf16[128,512]{1,0:T(8,128)(2,1)S(1)}, bf16[128,512]{1,0:T(8,128)(2,1)S(1)}, u32[]{:S(2)}, u32[]{:S(2)}) collective-permute-start(bf16[128,512]{1,0:T(8,128)(2,1)S(1)} %relay_total.2), channel_id=1, source_target_pairs={{0,16},{2,18},{4,20},{6,22},{8,24},{10,26},{12,28},{14,30},{16,0},... | collective-permute-start | bytes 393224 | tf_op jit(solution)/shard_map/ppermute | solution.py:408
  45.7 0.4 weight_this_core.3.mine_ref
  46.1 0.0 collective-permute-done.13.refs_0_
  46.2 1.5 %collective-permute-start.15 = (bf16[128,512]{1,0:T(8,128)(2,1)S(1)}, bf16[128,512]{1,0:T(8,128)(2,1)S(1)}, u32[]{:S(2)}, u32[]{:S(2)}) collective-permute-start(bf16[128,512]{1,0:T(8,128)(2,1)S(1)} %relay_total.3), channel_id=1, source_target_pairs={{0,16},{2,18},{4,20},{6,22},{8,24},{10,26},{12,28},{14,30},{16,0},... | collective-permute-start | bytes 393224 | tf_op jit(solution)/shard_map/ppermute | solution.py:408
  47.7 0.0 collective-permute-done.10.theirs_ref
  47.7 0.1 chip_near.1
  47.8 1.6 %collective-permute-start.14 = (bf16[128,1024]{1,0:T(8,128)(2,1)S(1)}, bf16[128,1024]{1,0:T(8,128)(2,1)S(1)}, u32[]{:S(2)}, u32[]{:S(2)}) collective-permute-start(bf16[128,1024]{1,0:T(8,128)(2,1)S(1)} %get-tuple-element.76), channel_id=1, source_target_pairs={{0,1},{1,0},{2,3},{3,2},{4,5},{5,4},{6,7},{7,6},{8,9},{9,8},{10,11... | collective-permute-start | bytes 786440 | tf_op jit(solution)/shard_map/ppermute | solution.py:403
  49.4 5.3 %collective-permute-done.12.refs_0_ = bf16[128,512]{1,0:T(8,128)(2,1)S(1)} collective-permute-done((bf16[128,512]{1,0:T(8,128)(2,1)S(1)}, bf16[128,512]{1,0:T(8,128)(2,1)S(1)}, u32[]{:S(2)}, u32[]{:S(2)}) %collective-permute-start.12) | collective-permute-done | bytes 131104 | tf_op jit(solution)/shard_map/ppermute | solution.py:408
  54.7 1.7 %collective-permute-done.15.refs_1_ = bf16[128,512]{1,0:T(8,128)(2,1)S(1)} collective-permute-done((bf16[128,512]{1,0:T(8,128)(2,1)S(1)}, bf16[128,512]{1,0:T(8,128)(2,1)S(1)}, u32[]{:S(2)}, u32[]{:S(2)}) %collective-permute-start.15) | collective-permute-done | bytes 131104 | tf_op jit(solution)/shard_map/ppermute | solution.py:408
  56.3 0.0 collective-permute-done.14.refs_0_
  56.3 0.8 %weight_total.1 = (f32[128,512]{1,0:T(8,128)}, f32[128,512]{1,0:T(8,128)}) custom-call(f32[128,1024]{1,0:T(8,128)S(1)} %get-tuple-element.73.own_ref, f32[128,512]{1,0:T(8,128)S(1)} %key_far_total.1.key_far_ref, bf16[128,1024]{1,0:T(8,128)(2,1)S(1)} %collective-permute-done.14.refs_0_, bf16[128,512]{1,0:T(8,128)(2,1)S(1)} %collective-permute-done.15.refs_1_), custom_call_target="tpu_custom_call" | custom-call | flops 1024 | bytes 1024 | tf_op jit(solution)/shard_map/weight_total/pallas_call | solution.py:375
  (8 shorter events, 0.1 us)
Async XLA Ops:
  0.6 8.7 %collective-permute-start.1 = (bf16[128,512]{1,0:T(8,128)(2,1)}, bf16[128,512]{1,0:T(8,128)(2,1)S(1)}, u32[]{:S(2)}, u32[]{:S(2)}) collective-permute-start(bf16[128,512]{1,0:T(8,128)(2,1)} %refs_4_.1), channel_id=1, source_target_pairs={{0,1},{1,0},{2,3},{3,2},{4,5},{5,4},{6,7},{7,6},{8,9},{9,8},{10,11... | collective-permute-start | bytes 393224 | tf_op jit(solution)/shard_map/ppermute | solution.py:403
  3.6 6.5 %collective-permute-start = (bf16[128,512]{1,0:T(8,128)(2,1)}, bf16[128,512]{1,0:T(8,128)(2,1)S(1)}, u32[]{:S(2)}, u32[]{:S(2)}) collective-permute-start(bf16[128,512]{1,0:T(8,128)(2,1)} %refs_2_.5), channel_id=1, source_target_pairs={{0,1},{1,0},{2,3},{3,2},{4,5},{5,4},{6,7},{7,6},{8,9},{9,8},{10,11... | collective-permute-start | bytes 393224 | tf_op jit(solution)/shard_map/ppermute | solution.py:403
  3.7 6.4 %copy-start = (bf16[128,4096]{1,0:T(8,128)(2,1)S(1)}, bf16[128,4096]{1,0:T(8,128)(2,1)}, u32[]{:S(2)}) copy-start(bf16[128,4096]{1,0:T(8,128)(2,1)} %refs_1_.3) | copy-start | bytes 3145732
  3.7 6.4 %copy-start.1 = (bf16[128,4096]{1,0:T(8,128)(2,1)S(1)}, bf16[128,4096]{1,0:T(8,128)(2,1)}, u32[]{:S(2)}) copy-start(bf16[128,4096]{1,0:T(8,128)(2,1)} %refs_2_.4) | copy-start | bytes 3145732
  5.7 11.8 %collective-permute-start.3 = (bf16[128,1024]{1,0:T(8,128)(2,1)S(1)}, bf16[128,1024]{1,0:T(8,128)(2,1)S(1)}, u32[]{:S(2)}, u32[]{:S(2)}) collective-permute-start(bf16[128,1024]{1,0:T(8,128)(2,1)S(1)} %get-tuple-element.48), channel_id=1, source_target_pairs={{0,8},{2,10},{4,12},{6,14},{8,0},{10,2},{12,4},{14,6},{16,24},{18,... | collective-permute-start | bytes 786440 | tf_op jit(solution)/shard_map/ppermute | solution.py:415
  7.8 12.8 %collective-permute-start.4 = (bf16[128,1024]{1,0:T(8,128)(2,1)S(1)}, bf16[128,1024]{1,0:T(8,128)(2,1)S(1)}, u32[]{:S(2)}, u32[]{:S(2)}) collective-permute-start(bf16[128,1024]{1,0:T(8,128)(2,1)S(1)} %get-tuple-element.49), channel_id=1, source_target_pairs={{0,4},{2,6},{4,0},{6,2},{8,12},{10,14},{12,8},{14,10},{16,20},{18,... | collective-permute-start | bytes 786440 | tf_op jit(solution)/shard_map/ppermute | solution.py:415
  9.3 11.3 %collective-permute-start.5 = (bf16[128,1024]{1,0:T(8,128)(2,1)S(1)}, bf16[128,1024]{1,0:T(8,128)(2,1)S(1)}, u32[]{:S(2)}, u32[]{:S(2)}) collective-permute-start(bf16[128,1024]{1,0:T(8,128)(2,1)S(1)} %get-tuple-element.50), channel_id=1, source_target_pairs={{0,12},{2,14},{4,8},{6,10},{8,4},{10,6},{12,0},{14,2},{16,28},{18,... | collective-permute-start | bytes 786440 | tf_op jit(solution)/shard_map/ppermute | solution.py:415
  10.2 5.0 %copy-start.2 = (bf16[128,512]{1,0:T(8,128)(2,1)S(1)}, bf16[128,512]{1,0:T(8,128)(2,1)}, u32[]{:S(2)}) copy-start(bf16[128,512]{1,0:T(8,128)(2,1)} %refs_2_.5) | copy-start | bytes 393220
  10.2 5.0 %copy-start.3 = (bf16[128,512]{1,0:T(8,128)(2,1)S(1)}, bf16[128,512]{1,0:T(8,128)(2,1)}, u32[]{:S(2)}) copy-start(bf16[128,512]{1,0:T(8,128)(2,1)} %refs_4_.1) | copy-start | bytes 393220
  13.3 7.6 %collective-permute-start.2 = (bf16[2,128,512]{2,1,0:T(8,128)(2,1)S(1)}, bf16[2,128,512]{2,1,0:T(8,128)(2,1)S(1)}, u32[]{:S(2)}, u32[]{:S(2)}) collective-permute-start(bf16[2,128,512]{2,1,0:T(8,128)(2,1)S(1)} %get-tuple-element.44), channel_id=1, source_target_pairs={{0,1},{1,0},{2,3},{3,2},{4,5},{5,4},{6,7},{7,6},{8,9},{9,8},{10,11... | collective-permute-start | bytes 786440 | tf_op jit(solution)/shard_map/ppermute | solution.py:403
  20.9 9.3 %collective-permute-start.8 = (bf16[2,128,512]{2,1,0:T(8,128)(2,1)S(1)}, bf16[2,128,512]{2,1,0:T(8,128)(2,1)S(1)}, u32[]{:S(2)}, u32[]{:S(2)}) collective-permute-start(bf16[2,128,512]{2,1,0:T(8,128)(2,1)S(1)} %grads_total.1.refs_0_), channel_id=1, source_target_pairs={{0,8},{2,10},{4,12},{6,14},{8,0},{10,2},{12,4},{14,6},{16,24},{18,... | collective-permute-start | bytes 786440 | tf_op jit(solution)/shard_map/ppermute | solution.py:415
  22.5 11.6 %collective-permute-start.7 = (bf16[2,128,512]{2,1,0:T(8,128)(2,1)S(1)}, bf16[2,128,512]{2,1,0:T(8,128)(2,1)S(1)}, u32[]{:S(2)}, u32[]{:S(2)}) collective-permute-start(bf16[2,128,512]{2,1,0:T(8,128)(2,1)S(1)} %grads_total.1.refs_0_), channel_id=1, source_target_pairs={{0,4},{2,6},{4,0},{6,2},{8,12},{10,14},{12,8},{14,10},{16,20},{18,... | collective-permute-start | bytes 786440 | tf_op jit(solution)/shard_map/ppermute | solution.py:415
  24.0 10.1 %collective-permute-start.6 = (bf16[2,128,512]{2,1,0:T(8,128)(2,1)S(1)}, bf16[2,128,512]{2,1,0:T(8,128)(2,1)S(1)}, u32[]{:S(2)}, u32[]{:S(2)}) collective-permute-start(bf16[2,128,512]{2,1,0:T(8,128)(2,1)S(1)} %grads_total.1.refs_0_), channel_id=1, source_target_pairs={{0,12},{2,14},{4,8},{6,10},{8,4},{10,6},{12,0},{14,2},{16,28},{18,... | collective-permute-start | bytes 786440 | tf_op jit(solution)/shard_map/ppermute | solution.py:415
  34.5 2.0 %collective-permute-start.9 = (bf16[256,1024]{1,0:T(8,128)(2,1)S(1)}, bf16[256,1024]{1,0:T(8,128)(2,1)S(1)}, u32[]{:S(2)}, u32[]{:S(2)}) collective-permute-start(bf16[256,1024]{1,0:T(8,128)(2,1)S(1)} %weight_other_core.2), channel_id=1, source_target_pairs={{0,2},{2,0},{4,6},{6,4},{8,10},{10,8},{12,14},{14,12},{16,18},{18,... | collective-permute-start | bytes 1572872 | tf_op jit(solution)/shard_map/ppermute | solution.py:411
  36.6 6.4 %collective-permute-start.11 = (bf16[128,512]{1,0:T(8,128)(2,1)S(1)}, bf16[128,512]{1,0:T(8,128)(2,1)S(1)}, u32[]{:S(2)}, u32[]{:S(2)}) collective-permute-start(bf16[128,512]{1,0:T(8,128)(2,1)S(1)} %get-tuple-element.67), channel_id=1, source_target_pairs={{0,1},{1,0},{2,3},{3,2},{4,5},{5,4},{6,7},{7,6},{8,9},{9,8},{10,11... | collective-permute-start | bytes 393224 | tf_op jit(solution)/shard_map/ppermute | solution.py:403
  38.2 8.0 %collective-permute-start.13 = (bf16[128,512]{1,0:T(8,128)(2,1)S(1)}, bf16[128,512]{1,0:T(8,128)(2,1)S(1)}, u32[]{:S(2)}, u32[]{:S(2)}) collective-permute-start(bf16[128,512]{1,0:T(8,128)(2,1)S(1)} %get-tuple-element.68), channel_id=1, source_target_pairs={{0,1},{1,0},{2,3},{3,2},{4,5},{5,4},{6,7},{7,6},{8,9},{9,8},{10,11... | collective-permute-start | bytes 393224 | tf_op jit(solution)/shard_map/ppermute | solution.py:403
  39.1 8.6 %collective-permute-start.10 = (bf16[256,1024]{1,0:T(8,128)(2,1)S(1)}, bf16[256,1024]{1,0:T(8,128)(2,1)S(1)}, u32[]{:S(2)}, u32[]{:S(2)}) collective-permute-start(bf16[256,1024]{1,0:T(8,128)(2,1)S(1)} %weight_other_core.3), channel_id=1, source_target_pairs={{0,2},{2,0},{4,6},{6,4},{8,10},{10,8},{12,14},{14,12},{16,18},{18,... | collective-permute-start | bytes 1572872 | tf_op jit(solution)/shard_map/ppermute | solution.py:411
  43.0 11.6 %collective-permute-start.12 = (bf16[128,512]{1,0:T(8,128)(2,1)S(1)}, bf16[128,512]{1,0:T(8,128)(2,1)S(1)}, u32[]{:S(2)}, u32[]{:S(2)}) collective-permute-start(bf16[128,512]{1,0:T(8,128)(2,1)S(1)} %relay_total.2), channel_id=1, source_target_pairs={{0,16},{2,18},{4,20},{6,22},{8,24},{10,26},{12,28},{14,30},{16,0},... | collective-permute-start | bytes 393224 | tf_op jit(solution)/shard_map/ppermute | solution.py:408
  46.2 10.2 %collective-permute-start.15 = (bf16[128,512]{1,0:T(8,128)(2,1)S(1)}, bf16[128,512]{1,0:T(8,128)(2,1)S(1)}, u32[]{:S(2)}, u32[]{:S(2)}) collective-permute-start(bf16[128,512]{1,0:T(8,128)(2,1)S(1)} %relay_total.3), channel_id=1, source_target_pairs={{0,16},{2,18},{4,20},{6,22},{8,24},{10,26},{12,28},{14,30},{16,0},... | collective-permute-start | bytes 393224 | tf_op jit(solution)/shard_map/ppermute | solution.py:408
  47.8 8.5 %collective-permute-start.14 = (bf16[128,1024]{1,0:T(8,128)(2,1)S(1)}, bf16[128,1024]{1,0:T(8,128)(2,1)S(1)}, u32[]{:S(2)}, u32[]{:S(2)}) collective-permute-start(bf16[128,1024]{1,0:T(8,128)(2,1)S(1)} %get-tuple-element.76), channel_id=1, source_target_pairs={{0,1},{1,0},{2,3},{3,2},{4,5},{5,4},{6,7},{7,6},{8,9},{9,8},{10,11... | collective-permute-start | bytes 786440 | tf_op jit(solution)/shard_map/ppermute | solution.py:403

commit v10 on v9

--- a/solution.py
+++ b/solution.py
@@ -17,6 +17,7 @@
 MIDDLE = 2
 NEAR = 2
 ORDER = (0, 3, 2, 1)
+VISITS = 2
 PARAMS = pltpu.CompilerParams(vmem_limit_bytes=32 * 2**20)
 COST = pl.CostEstimate(flops=1024, bytes_accessed=1024, transcendentals=0)
 NEAR_COST = pl.CostEstimate(flops=10**10, bytes_accessed=1024, transcendentals=0)
@@ -71,25 +72,31 @@
     return dot(pick, high, NT) + dot(pick, low, NT)
 
 
-def block_kernel(ctx_count, step, *refs):
-    lengths_ref, q_ref, do_ref, k_ref, v_ref, lse_ref, other_ref, ds_ref, grad_ref = refs[:9]
+def block_kernel(ctx_count, step, heads, *refs):
+    lengths_ref, q_ref, do_ref, k_ref, v_ref, lse_ref = refs[:6]
+    if step == 1:
+        others, (ds_ref, grad_ref, delta_out) = refs[6:-3], refs[-3:]
+    else:
+        others, (ds_ref, grad_ref) = refs[6:-2], refs[-2:]
     width = GROUP * HEAD_SIZE
     rank = lax.axis_index("ctx")
     owner = lax.rem(rank + ctx_count - step, ctx_count)
     rows = q_ref.shape[0]
     keys = k_ref.shape[0]
     allowed = allowed_mask(lengths_ref, ctx_count, rank, owner, keys, rows)
-    for g in range(KEY_VALUE_HEADS):
+    for at, g in enumerate(heads):
         wide = slice(g * width, (g + 1) * width)
         q = rows_of_heads(q_ref[:, wide])
         do = rows_of_heads(do_ref[:, wide])
-        group = slice(g * GROUP, (g + 1) * GROUP)
+        group = slice(at * GROUP, (at + 1) * GROUP)
         if step == 1:
-            delta = delta_rows(do_ref[:, wide], other_ref[:, wide])
-            refs[9][group, :] = delta
+            delta = delta_rows(do_ref[:, wide], others[0][:, wide])
+            delta_out[group, :] = delta
         else:
-            delta = other_ref[group, :]
-        lse = lse_ref[group, :]
+            count = KEY_VALUE_HEADS // len(others)
+            start = g % count * GROUP
+            delta = others[g // count][start : start + GROUP, :]
+        lse = lse_ref[g * GROUP : (g + 1) * GROUP, :]
         columns = slice(g * HEAD_SIZE, (g + 1) * HEAD_SIZE)
         scores = dot(k_ref[:, columns], q, NT)
         grad_probs = dot(v_ref[:, columns], do, NT)
@@ -104,56 +111,67 @@
             probs_low.append(probs.astype(jnp.bfloat16))
         probs_low = jnp.concatenate(probs_low, axis=1)
         grad_scores = jnp.concatenate(grad_scores, axis=1)
-        ds_ref[:, g * GROUP * rows : (g + 1) * GROUP * rows] = grad_scores
+        ds_ref[:, at * GROUP * rows : (at + 1) * GROUP * rows] = grad_scores
+        columns = slice(at * HEAD_SIZE, (at + 1) * HEAD_SIZE)
         grad_ref[0, :, columns] = (dot(grad_scores, q, NN) * SCALE).astype(grad_ref.dtype)
         grad_ref[1, :, columns] = dot(probs_low, do, NN).astype(grad_ref.dtype)
 
 
-def block_call(step, ctx_count, lengths, queries, output_gradient, keys, values, lse, other):
+def block_call(
+    step, heads, ctx_count, lengths, queries, output_gradient, keys, values, lse, others
+):
     rows = queries.shape[0]
-    key_rows, half = keys.shape
+    key_rows = keys.shape[0]
+    count = len(heads)
     out_shape = [
-        shape((key_rows, QUERY_HEADS * rows), jnp.bfloat16),
-        shape((2, key_rows, half), jnp.bfloat16 if step else jnp.float32),
+        shape((key_rows, count * GROUP * rows), jnp.bfloat16),
+        shape((2, key_rows, count * HEAD_SIZE), jnp.bfloat16 if step else jnp.float32),
     ]
     if step == 1:
-        out_shape.append(shape((QUERY_HEADS, rows), jnp.float32))
-    return pl.pallas_call(
-        functools.partial(block_kernel, ctx_count, step),
-        in_specs=[SCALARS] + [WHOLE] * 6,
+        out_shape.append(shape((count * GROUP, rows), jnp.float32))
+    return pl.pallas_call(
+        functools.partial(block_kernel, ctx_count, step, heads),
+        in_specs=[SCALARS] + [WHOLE] * (5 + len(others)),
         out_specs=[WHOLE] * len(out_shape),
         out_shape=out_shape,
         compiler_params=PARAMS,
         cost_estimate=COST,
         name="visiting_keys" if step else "own_keys",
-    )(lengths, queries, output_gradient, keys, values, lse, other)
-
-
-def query_kernel(count, *refs):
-    ds_refs, k_refs, out_ref = refs[:count], refs[count:-1], refs[-1]
+    )(lengths, queries, output_gradient, keys, values, lse, *others)
+
+
+def query_kernel(counts, *refs):
+    k_refs, out_ref = refs[-1 - len(counts) : -1], refs[-1]
     rows = out_ref.shape[0]
+    owners = []
+    for count in counts:
+        owners.append(refs[:count])
+        refs = refs[count:]
     for g in range(KEY_VALUE_HEADS):
         columns = slice(g * HEAD_SIZE, (g + 1) * HEAD_SIZE)
         keys = jnp.concatenate([k[:, columns] for k in k_refs], axis=0)
         for head in range(g * GROUP, (g + 1) * GROUP):
-            scores = jnp.concatenate(
-                [ref[:, head * rows : (head + 1) * rows] for ref in ds_refs], axis=0
-            )
+            scores = []
+            for parts in owners:
+                count = QUERY_HEADS // len(parts)
+                start = head % count * rows
+                scores.append(parts[head // count][:, start : start + rows])
             out_ref[:, head * HEAD_SIZE : (head + 1) * HEAD_SIZE] = (
-                dot(scores, keys, TN) * SCALE
+                dot(jnp.concatenate(scores, axis=0), keys, TN) * SCALE
             ).astype(out_ref.dtype)
 
 
 def query_call(scores, keys, rows):
-    return pl.pallas_call(
-        functools.partial(query_kernel, len(keys)),
-        in_specs=[WHOLE] * (2 * len(keys)),
+    operands = [part for parts in scores for part in parts] + keys
+    return pl.pallas_call(
+        functools.partial(query_kernel, tuple(len(parts) for parts in scores)),
+        in_specs=[WHOLE] * len(operands),
         out_specs=WHOLE,
         out_shape=shape((rows, QUERY_HEADS * HEAD_SIZE), jnp.bfloat16),
         compiler_params=PARAMS,
         cost_estimate=COST,
         name="query_gradient",
-    )(*scores, *keys)
+    )(*operands)
 
 
 def after(values, others):
@@ -229,23 +247,32 @@
     )(*pieces)
 
 
-def add_kernel(own_ref, *refs):
-    total = own_ref[...]
-    for back_ref in refs[:-1]:
+def add_kernel(part, done, own_ref, *refs):
+    out_ref = refs[-1]
+    width = own_ref.shape[2] // VISITS
+    start = part * width
+    total = own_ref[:, :, start : start + width]
+    for back_ref in refs[done:-1]:
         total = total + back_ref[...].astype(jnp.float32)
-    refs[-1][...] = total.astype(refs[-1].dtype)
-
-
-def add_call(own, back):
-    return pl.pallas_call(
-        add_kernel,
-        in_specs=[WHOLE] * (1 + len(back)),
+    if done:
+        out_ref[:, :, :start] = refs[0][...]
+    else:
+        start = 0
+    out_ref[:, :, start : start + width] = total.astype(out_ref.dtype)
+
+
+def add_call(part, own, back, so_far):
+    earlier = [] if so_far is None else [so_far]
+    dims = own.shape[:2] + (own.shape[2] // VISITS * (1 + part),)
+    return pl.pallas_call(
+        functools.partial(add_kernel, part, len(earlier)),
+        in_specs=[WHOLE] * (1 + len(earlier) + len(back)),
         out_specs=WHOLE,
-        out_shape=shape(own.shape, jnp.bfloat16),
+        out_shape=shape(dims, jnp.bfloat16),
         compiler_params=PARAMS,
         cost_estimate=COST,
         name="grads_total",
-    )(own, *back)
+    )(own, *earlier, *back)
 
 
 def weight_kernel(other, steps, far, tokens_ref, *refs):
@@ -427,21 +454,36 @@
         output_gradient=output_gradient,
         lse=lse,
     )
-    scores, back = [], []
-    for step in range(1, ctx_count):
-        keys, values = visiting[step - 1]
-        part_scores, grads, *delta = block(step, keys=keys, values=values, other=other)
-        other = delta[0] if delta else other
-        scores.append(part_scores)
-        back.append(over_ctx(grads, -step))
-    other = after(other, grads)
-    own_scores, own = block(0, keys=saved_keys, values=saved_values, other=other)
-    back, pieces = lax.optimization_barrier((back, pieces))
-    total = add_call(own, back)
+    count = KEY_VALUE_HEADS // VISITS
+    scores, back, delta = [[] for _ in visiting], [[] for _ in range(VISITS)], []
+    for part in range(VISITS):
+        heads = range(part * count, (part + 1) * count)
+        others = [other]
+        for step in range(1, ctx_count):
+            keys, values = visiting[step - 1]
+            part_scores, grads, *sums = block(
+                step, heads, keys=keys, values=values, others=others if step == 1 else delta
+            )
+            delta += sums
+            scores[step - 1].append(part_scores)
+            back[part].append(over_ctx(grads, -step))
+        other = after(other, grads)
+    delta = after(delta, grads)
+    own_scores, own = block(
+        0,
+        range(KEY_VALUE_HEADS),
+        keys=saved_keys,
+        values=saved_values,
+        others=delta,
+    )
+    back[0], pieces = lax.optimization_barrier((back[0], pieces))
+    total = None
+    for part in range(VISITS):
+        total = add_call(part, own, back[part], total)
     grads = [over_group(total, i) if i else total for i in ORDER]
     own_scores, pieces = after((own_scores, pieces), total)
     query_gradient = query_call(
-        [own_scores] + scores, [saved_keys] + [pair[0] for pair in visiting], rows
+        [[own_scores]] + scores, [saved_keys] + [pair[0] for pair in visiting], rows
     )
     tokens = turn_call(after([pieces[i] for i in ORDER], query_gradient))
 

time: 57.4 us -> 57.4 us (level)
  waiting for transfers between devices: 24 us -> 22.7 us
  Pallas kernels: 12.4 us -> 13.1 us
  starting transfers between devices: 20 us -> 20.6 us
    ppermute x6, waiting for transfers between devices: 10.6 us -> 9.57 us  [over_group(): return lax.ppermute(value, 'dp', [(s, s ^ flip) for s in range(dp_count)])]
    pallas_call x4 -> x6, Pallas kernels: 7.29 us -> 8.04 us  [the longest x3 6.24 us: block_call(): pl.pallas_call(functools.partial(block_kernel, ctx_count, step, heads), i...]
    ppermute x6 -> x7, starting transfers between devices: 8.54 us -> 9.08 us  [over_ctx(): return lax.ppermute(value, 'ctx', pairs)]
    ppermute x6 -> x7, waiting for transfers between devices: 4.94 us -> 4.95 us  [over_ctx(): return lax.ppermute(value, 'ctx', pairs)]
  transfers between devices with their start and end apart: 16 -> 17, of which waited for: 9 -> 9; matrix products, arithmetic and copies ran while one was open for 0% -> 0% of each run, Pallas kernels for 19% -> 20%
where the time goes in v10:
time: 57.4 us; the launch traced here: 57.3 us
  waiting for transfers between devices  22.7 us (40%)
  starting transfers between devices  20.6 us (36%)
  Pallas kernels  13.1 us (23%)
  between operations  0.79 us (1%)
    ppermute x6, waiting for transfers between devices, over_group(): return lax.ppermute(value, 'dp', [(s, s ^ flip) for s in range(dp_count)])  9.57 us
    ppermute x7, starting transfers between devices, over_ctx(): return lax.ppermute(value, 'ctx', pairs)  9.08 us
    ppermute x6, starting transfers between devices, over_group(): return lax.ppermute(value, 'dp', [(s, s ^ flip) for s in range(dp_count)])  7.19 us
    ppermute x2, waiting for transfers between devices, over_far(): return lax.ppermute(value, 'dp', pairs)  6.77 us
    pallas_call x3, Pallas kernels, block_call(): pl.pallas_call(functools.partial(block_kernel, ctx_count, step, heads), i...  6.24 us
    ppermute x7, waiting for transfers between devices, over_ctx(): return lax.ppermute(value, 'ctx', pairs)  4.95 us
    ppermute x2, starting transfers between devices, over_far(): return lax.ppermute(value, 'dp', pairs)  4.18 us
    pallas_call x1, Pallas kernels, pieces_call(): pl.pallas_call(functools.partial(pieces_kernel, far, len(wanted)), in_spe...  1.94 us
  transfers between devices with their start and end apart: 17, of which 9 were waited for; matrix products, arithmetic and copies ran while one was open for 0% of the time, Pallas kernels for 20%

profile of v10, /device:TPU:0, one launch (start us, length us, event | category | flops | bytes accessed | tf_op | source)
XLA Modules:
  0.0 57.3 jit_solution(1157362987147883442)
XLA Ops:
  0.6 3.0 %collective-permute-start.1 = (bf16[128,512]{1,0:T(8,128)(2,1)}, bf16[128,512]{1,0:T(8,128)(2,1)S(1)}, u32[]{:S(2)}, u32[]{:S(2)}) collective-permute-start(bf16[128,512]{1,0:T(8,128)(2,1)} %refs_4_.1), channel_id=1, source_target_pairs={{0,1},{1,0},{2,3},{3,2},{4,5},{5,4},{6,7},{7,6},{8,9},{9,8},{10,11... | collective-permute-start | bytes 393224 | tf_op jit(solution)/shard_map/ppermute | solution.py:430
  3.6 0.1 collective-permute-start
  3.7 1.9 %pieces.1 = (bf16[128,1024]{1,0:T(8,128)(2,1)S(1)}, bf16[128,1024]{1,0:T(8,128)(2,1)S(1)}, bf16[128,1024]{1,0:T(8,128)(2,1)S(1)}, bf16[128,1024]{1,0:T(8,128)(2,...) custom-call(bf16[128,4096]{1,0:T(8,128)(2,1)} %in_hbm.1, bf16[128,4096]{1,0:T(8,128)(2,1)} %refs_0_.4, ...), custom_call_target="tpu_custom_call" | custom-call | flops 1024 | bytes 1024 | tf_op jit(solution)/shard_map/pieces/pallas_call | solution.py:214
  5.7 2.1 %collective-permute-start.3 = (bf16[128,1024]{1,0:T(8,128)(2,1)S(1)}, bf16[128,1024]{1,0:T(8,128)(2,1)S(1)}, u32[]{:S(2)}, u32[]{:S(2)}) collective-permute-start(bf16[128,1024]{1,0:T(8,128)(2,1)S(1)} %get-tuple-element.57), channel_id=1, source_target_pairs={{0,8},{2,10},{4,12},{6,14},{8,0},{10,2},{12,4},{14,6},{16,24},{18,... | collective-permute-start | bytes 786440 | tf_op jit(solution)/shard_map/ppermute | solution.py:442
  7.8 1.5 %collective-permute-start.4 = (bf16[128,1024]{1,0:T(8,128)(2,1)S(1)}, bf16[128,1024]{1,0:T(8,128)(2,1)S(1)}, u32[]{:S(2)}, u32[]{:S(2)}) collective-permute-start(bf16[128,1024]{1,0:T(8,128)(2,1)S(1)} %get-tuple-element.58), channel_id=1, source_target_pairs={{0,4},{2,6},{4,0},{6,2},{8,12},{10,14},{12,8},{14,10},{16,20},{18,... | collective-permute-start | bytes 786440 | tf_op jit(solution)/shard_map/ppermute | solution.py:442
  9.3 0.0 collective-permute-start.5
  9.3 0.0 collective-permute-done.1.refs_4_
  9.3 0.8 %collective-permute-done.refs_3_.refs_4_ = bf16[128,512]{1,0:T(8,128)(2,1)S(1)} collective-permute-done((bf16[128,512]{1,0:T(8,128)(2,1)}, bf16[128,512]{1,0:T(8,128)(2,1)S(1)}, u32[]{:S(2)}, u32[]{:S(2)}) %collective-permute-start) | collective-permute-done | bytes 131104 | tf_op jit(solution)/shard_map/ppermute | solution.py:430
  10.2 1.9 %visiting_keys.2 = (bf16[128,2048]{1,0:T(8,128)(2,1)S(1)}, bf16[2,128,256]{2,1,0:T(8,128)(2,1)S(1)}, f32[16,128]{1,0:T(8,128)S(1)}) custom-call(s32[1,4]{1,0:T(1,128)} %refs_0_.7, bf16[128,4096]{1,0:T(8,128)(2,1)S(1)} %copy-done, bf16[128,4096]{1,0:T(8,128)(2,1)S(1)} %copy-done.1, bf16[128,512]{1,0:T(8,128)(2,1)S(1)} %collective-permute-done.refs_3_.refs_4_, ...), custom_call_target="tpu_custom_call" | custom-call | flops 1024 | bytes 1024 | tf_op jit(solution)/shard_map/visiting_keys/pallas_call | solution.py:132
  12.1 0.0 copy-start.2
  12.1 0.0 copy-start.3
  12.1 1.8 %collective-permute-start.2 = (bf16[2,128,256]{2,1,0:T(8,128)(2,1)S(1)}, bf16[2,128,256]{2,1,0:T(8,128)(2,1)S(1)}, u32[]{:S(2)}, u32[]{:S(2)}) collective-permute-start(bf16[2,128,256]{2,1,0:T(8,128)(2,1)S(1)} %get-tuple-element.49), channel_id=1, source_target_pairs={{0,1},{1,0},{2,3},{3,2},{4,5},{5,4},{6,7},{7,6},{8,9},{9,8},{10,11... | collective-permute-start | bytes 393224 | tf_op jit(solution)/shard_map/ppermute | solution.py:430
  13.9 1.9 %visiting_keys.3 = (bf16[128,2048]{1,0:T(8,128)(2,1)S(1)}, bf16[2,128,256]{2,1,0:T(8,128)(2,1)S(1)}, f32[16,128]{1,0:T(8,128)S(1)}) custom-call(s32[1,4]{1,0:T(1,128)} %refs_0_.7, bf16[128,4096]{1,0:T(8,128)(2,1)S(1)} %copy-done, bf16[128,4096]{1,0:T(8,128)(2,1)S(1)} %copy-done.1, bf16[128,512]{1,0:T(8,128)(2,1)S(1)} %collective-permute-done.refs_3_.refs_4_, ...), custom_call_target="tpu_custom_call" | custom-call | flops 1024 | bytes 1024 | tf_op jit(solution)/shard_map/visiting_keys/pallas_call | solution.py:132
  15.9 0.4 collective-permute-start.6
  16.2 2.4 %own_keys.1 = (bf16[128,4096]{1,0:T(8,128)(2,1)S(1)}, f32[2,128,512]{2,1,0:T(8,128)S(1)}) custom-call(s32[1,4]{1,0:T(1,128)} %refs_0_.7, bf16[128,4096]{1,0:T(8,128)(2,1)S(1)} %copy-done, bf16[128,4096]{1,0:T(8,128)(2,1)S(1)} %copy-done.1, bf16[128,512]{1,0:T(8,128)(2,1)S(1)} %copy-done.2, bf16[128,512]{1,0:T(8,128)(2,1)S(1)} %copy-done.3, ...), custom_call_target="tpu_custom_call" | custom-call | flops 1024 | bytes 1024 | tf_op jit(solution)/shard_map/own_keys/pallas_call | solution.py:132
  18.6 0.0 collective-permute-done.3.refs_3_
  18.6 2.0 %collective-permute-done.4.refs_2_ = bf16[128,1024]{1,0:T(8,128)(2,1)S(1)} collective-permute-done((bf16[128,1024]{1,0:T(8,128)(2,1)S(1)}, bf16[128,1024]{1,0:T(8,128)(2,1)S(1)}, u32[]{:S(2)}, u32[]{:S(2)}) %collective-permute-start.4) | collective-permute-done | bytes 262176 | tf_op jit(solution)/shard_map/ppermute | solution.py:442
  20.6 0.0 collective-permute-done.5.refs_1_
  20.6 0.0 collective-permute-done.2.refs_0_
  20.6 0.3 collective-permute-done.6.refs_1_
  21.0 1.6 %collective-permute-start.9 = (bf16[2,128,512]{2,1,0:T(8,128)(2,1)S(1)}, bf16[2,128,512]{2,1,0:T(8,128)(2,1)S(1)}, u32[]{:S(2)}, u32[]{:S(2)}) collective-permute-start(bf16[2,128,512]{2,1,0:T(8,128)(2,1)S(1)} %grads_total.3.refs_0_), channel_id=1, source_target_pairs={{0,8},{2,10},{4,12},{6,14},{8,0},{10,2},{12,4},{14,6},{16,24},{18,... | collective-permute-start | bytes 786440 | tf_op jit(solution)/shard_map/ppermute | solution.py:442
  22.6 1.5 %collective-permute-start.8 = (bf16[2,128,512]{2,1,0:T(8,128)(2,1)S(1)}, bf16[2,128,512]{2,1,0:T(8,128)(2,1)S(1)}, u32[]{:S(2)}, u32[]{:S(2)}) collective-permute-start(bf16[2,128,512]{2,1,0:T(8,128)(2,1)S(1)} %grads_total.3.refs_0_), channel_id=1, source_target_pairs={{0,4},{2,6},{4,0},{6,2},{8,12},{10,14},{12,8},{14,10},{16,20},{18,... | collective-permute-start | bytes 786440 | tf_op jit(solution)/shard_map/ppermute | solution.py:442
  24.1 0.4 collective-permute-start.7
  24.5 1.7 %query_gradient.1 = bf16[128,4096]{1,0:T(8,128)(2,1)} custom-call(bf16[128,4096]{1,0:T(8,128)(2,1)S(1)} %get-tuple-element.66.refs_0_, bf16[128,2048]{1,0:T(8,128)(2,1)S(1)} %get-tuple-element.67.refs_1_, bf16[128,2048]{1,0:T(8,128)(2,1)S(1)} %get-tuple-element.68.refs_2_, bf16[128,512]{1,0:T(8,128)(2,1)S(1)} %copy-done.2, ...), custom_call_target="tpu_custom_call" | custom-call | flops 1024 | bytes 1024 | tf_op jit(solution)/shard_map/query_gradient/pallas_call | solution.py:166
  26.2 0.3 turn_pieces.1.tokens_ref
  26.6 3.3 %collective-permute-done.9.refs_3_ = bf16[2,128,512]{2,1,0:T(8,128)(2,1)S(1)} collective-permute-done((bf16[2,128,512]{2,1,0:T(8,128)(2,1)S(1)}, bf16[2,128,512]{2,1,0:T(8,128)(2,1)S(1)}, u32[]{:S(2)}, u32[]{:S(2)}) %collective-permute-start.9) | collective-permute-done | bytes 262176 | tf_op jit(solution)/shard_map/ppermute | solution.py:442
  29.9 4.3 %collective-permute-done.8.refs_2_ = bf16[2,128,512]{2,1,0:T(8,128)(2,1)S(1)} collective-permute-done((bf16[2,128,512]{2,1,0:T(8,128)(2,1)S(1)}, bf16[2,128,512]{2,1,0:T(8,128)(2,1)S(1)}, u32[]{:S(2)}, u32[]{:S(2)}) %collective-permute-start.8) | collective-permute-done | bytes 262176 | tf_op jit(solution)/shard_map/ppermute | solution.py:442
  34.2 0.0 collective-permute-done.7.refs_1_
  34.2 0.4 weight_other_core.2
  34.6 0.1 collective-permute-start.10
  34.7 0.4 weight_this_core.2.mine_ref
  35.1 1.5 %collective-permute-done.10.theirs_ref = bf16[256,1024]{1,0:T(8,128)(2,1)S(1)} collective-permute-done((bf16[256,1024]{1,0:T(8,128)(2,1)S(1)}, bf16[256,1024]{1,0:T(8,128)(2,1)S(1)}, u32[]{:S(2)}, u32[]{:S(2)}) %collective-permute-start.10) | collective-permute-done | bytes 524320 | tf_op jit(solution)/shard_map/ppermute | solution.py:438
  36.6 0.1 chip_far.1
  36.7 1.7 %collective-permute-start.12 = (bf16[128,512]{1,0:T(8,128)(2,1)S(1)}, bf16[128,512]{1,0:T(8,128)(2,1)S(1)}, u32[]{:S(2)}, u32[]{:S(2)}) collective-permute-start(bf16[128,512]{1,0:T(8,128)(2,1)S(1)} %get-tuple-element.77), channel_id=1, source_target_pairs={{0,1},{1,0},{2,3},{3,2},{4,5},{5,4},{6,7},{7,6},{8,9},{9,8},{10,11... | collective-permute-start | bytes 393224 | tf_op jit(solution)/shard_map/ppermute | solution.py:430
  38.4 0.3 collective-permute-start.14
  38.8 0.4 weight_other_core.3
  39.2 0.1 collective-permute-start.11
  39.3 3.8 %collective-permute-done.12.refs_0_ = bf16[128,512]{1,0:T(8,128)(2,1)S(1)} collective-permute-done((bf16[128,512]{1,0:T(8,128)(2,1)S(1)}, bf16[128,512]{1,0:T(8,128)(2,1)S(1)}, u32[]{:S(2)}, u32[]{:S(2)}) %collective-permute-start.12) | collective-permute-done | bytes 131104 | tf_op jit(solution)/shard_map/ppermute | solution.py:430
  43.1 2.7 %collective-permute-start.13 = (bf16[128,512]{1,0:T(8,128)(2,1)S(1)}, bf16[128,512]{1,0:T(8,128)(2,1)S(1)}, u32[]{:S(2)}, u32[]{:S(2)}) collective-permute-start(bf16[128,512]{1,0:T(8,128)(2,1)S(1)} %relay_total.2), channel_id=1, source_target_pairs={{0,16},{2,18},{4,20},{6,22},{8,24},{10,26},{12,28},{14,30},{16,0},... | collective-permute-start | bytes 393224 | tf_op jit(solution)/shard_map/ppermute | solution.py:435
  45.8 0.4 weight_this_core.3.mine_ref
  46.2 0.0 collective-permute-done.14.refs_0_
  46.2 1.5 %collective-permute-start.16 = (bf16[128,512]{1,0:T(8,128)(2,1)S(1)}, bf16[128,512]{1,0:T(8,128)(2,1)S(1)}, u32[]{:S(2)}, u32[]{:S(2)}) collective-permute-start(bf16[128,512]{1,0:T(8,128)(2,1)S(1)} %relay_total.3), channel_id=1, source_target_pairs={{0,16},{2,18},{4,20},{6,22},{8,24},{10,26},{12,28},{14,30},{16,0},... | collective-permute-start | bytes 393224 | tf_op jit(solution)/shard_map/ppermute | solution.py:435
  47.8 0.0 collective-permute-done.11.theirs_ref
  47.8 0.1 chip_near.1
  47.9 1.8 %collective-permute-start.15 = (bf16[128,1024]{1,0:T(8,128)(2,1)S(1)}, bf16[128,1024]{1,0:T(8,128)(2,1)S(1)}, u32[]{:S(2)}, u32[]{:S(2)}) collective-permute-start(bf16[128,1024]{1,0:T(8,128)(2,1)S(1)} %get-tuple-element.86), channel_id=1, source_target_pairs={{0,1},{1,0},{2,3},{3,2},{4,5},{5,4},{6,7},{7,6},{8,9},{9,8},{10,11... | collective-permute-start | bytes 786440 | tf_op jit(solution)/shard_map/ppermute | solution.py:430
  49.6 5.1 %collective-permute-done.13.refs_0_ = bf16[128,512]{1,0:T(8,128)(2,1)S(1)} collective-permute-done((bf16[128,512]{1,0:T(8,128)(2,1)S(1)}, bf16[128,512]{1,0:T(8,128)(2,1)S(1)}, u32[]{:S(2)}, u32[]{:S(2)}) %collective-permute-start.13) | collective-permute-done | bytes 131104 | tf_op jit(solution)/shard_map/ppermute | solution.py:435
  54.7 1.7 %collective-permute-done.16.refs_1_ = bf16[128,512]{1,0:T(8,128)(2,1)S(1)} collective-permute-done((bf16[128,512]{1,0:T(8,128)(2,1)S(1)}, bf16[128,512]{1,0:T(8,128)(2,1)S(1)}, u32[]{:S(2)}, u32[]{:S(2)}) %collective-permute-start.16) | collective-permute-done | bytes 131104 | tf_op jit(solution)/shard_map/ppermute | solution.py:435
  56.4 0.8 %weight_total.1 = (f32[128,512]{1,0:T(8,128)}, f32[128,512]{1,0:T(8,128)}) custom-call(f32[128,1024]{1,0:T(8,128)S(1)} %get-tuple-element.83.own_ref, f32[128,512]{1,0:T(8,128)S(1)} %key_far_total.1.key_far_ref, bf16[128,1024]{1,0:T(8,128)(2,1)S(1)} %collective-permute-done.15.refs_0_, bf16[128,512]{1,0:T(8,128)(2,1)S(1)} %collective-permute-done.16.refs_1_), custom_call_target="tpu_custom_call" | custom-call | flops 1024 | bytes 1024 | tf_op jit(solution)/shard_map/weight_total/pallas_call | solution.py:402
  (12 shorter events, 0.1 us)
Async XLA Ops:
  0.6 8.7 %collective-permute-start.1 = (bf16[128,512]{1,0:T(8,128)(2,1)}, bf16[128,512]{1,0:T(8,128)(2,1)S(1)}, u32[]{:S(2)}, u32[]{:S(2)}) collective-permute-start(bf16[128,512]{1,0:T(8,128)(2,1)} %refs_4_.1), channel_id=1, source_target_pairs={{0,1},{1,0},{2,3},{3,2},{4,5},{5,4},{6,7},{7,6},{8,9},{9,8},{10,11... | collective-permute-start | bytes 393224 | tf_op jit(solution)/shard_map/ppermute | solution.py:430
  3.6 6.5 %collective-permute-start = (bf16[128,512]{1,0:T(8,128)(2,1)}, bf16[128,512]{1,0:T(8,128)(2,1)S(1)}, u32[]{:S(2)}, u32[]{:S(2)}) collective-permute-start(bf16[128,512]{1,0:T(8,128)(2,1)} %refs_3_.3), channel_id=1, source_target_pairs={{0,1},{1,0},{2,3},{3,2},{4,5},{5,4},{6,7},{7,6},{8,9},{9,8},{10,11... | collective-permute-start | bytes 393224 | tf_op jit(solution)/shard_map/ppermute | solution.py:430
  3.7 6.4 %copy-start = (bf16[128,4096]{1,0:T(8,128)(2,1)S(1)}, bf16[128,4096]{1,0:T(8,128)(2,1)}, u32[]{:S(2)}) copy-start(bf16[128,4096]{1,0:T(8,128)(2,1)} %refs_1_.5) | copy-start | bytes 3145732
  3.7 6.4 %copy-start.1 = (bf16[128,4096]{1,0:T(8,128)(2,1)S(1)}, bf16[128,4096]{1,0:T(8,128)(2,1)}, u32[]{:S(2)}) copy-start(bf16[128,4096]{1,0:T(8,128)(2,1)} %refs_2_.5) | copy-start | bytes 3145732
  5.7 12.9 %collective-permute-start.3 = (bf16[128,1024]{1,0:T(8,128)(2,1)S(1)}, bf16[128,1024]{1,0:T(8,128)(2,1)S(1)}, u32[]{:S(2)}, u32[]{:S(2)}) collective-permute-start(bf16[128,1024]{1,0:T(8,128)(2,1)S(1)} %get-tuple-element.57), channel_id=1, source_target_pairs={{0,8},{2,10},{4,12},{6,14},{8,0},{10,2},{12,4},{14,6},{16,24},{18,... | collective-permute-start | bytes 786440 | tf_op jit(solution)/shard_map/ppermute | solution.py:442
  7.8 12.8 %collective-permute-start.4 = (bf16[128,1024]{1,0:T(8,128)(2,1)S(1)}, bf16[128,1024]{1,0:T(8,128)(2,1)S(1)}, u32[]{:S(2)}, u32[]{:S(2)}) collective-permute-start(bf16[128,1024]{1,0:T(8,128)(2,1)S(1)} %get-tuple-element.58), channel_id=1, source_target_pairs={{0,4},{2,6},{4,0},{6,2},{8,12},{10,14},{12,8},{14,10},{16,20},{18,... | collective-permute-start | bytes 786440 | tf_op jit(solution)/shard_map/ppermute | solution.py:442
  9.3 11.3 %collective-permute-start.5 = (bf16[128,1024]{1,0:T(8,128)(2,1)S(1)}, bf16[128,1024]{1,0:T(8,128)(2,1)S(1)}, u32[]{:S(2)}, u32[]{:S(2)}) collective-permute-start(bf16[128,1024]{1,0:T(8,128)(2,1)S(1)} %get-tuple-element.59), channel_id=1, source_target_pairs={{0,12},{2,14},{4,8},{6,10},{8,4},{10,6},{12,0},{14,2},{16,28},{18,... | collective-permute-start | bytes 786440 | tf_op jit(solution)/shard_map/ppermute | solution.py:442
  12.1 4.1 %copy-start.2 = (bf16[128,512]{1,0:T(8,128)(2,1)S(1)}, bf16[128,512]{1,0:T(8,128)(2,1)}, u32[]{:S(2)}) copy-start(bf16[128,512]{1,0:T(8,128)(2,1)} %refs_3_.3) | copy-start | bytes 393220
  12.1 4.1 %copy-start.3 = (bf16[128,512]{1,0:T(8,128)(2,1)S(1)}, bf16[128,512]{1,0:T(8,128)(2,1)}, u32[]{:S(2)}) copy-start(bf16[128,512]{1,0:T(8,128)(2,1)} %refs_4_.1) | copy-start | bytes 393220
  12.1 8.5 %collective-permute-start.2 = (bf16[2,128,256]{2,1,0:T(8,128)(2,1)S(1)}, bf16[2,128,256]{2,1,0:T(8,128)(2,1)S(1)}, u32[]{:S(2)}, u32[]{:S(2)}) collective-permute-start(bf16[2,128,256]{2,1,0:T(8,128)(2,1)S(1)} %get-tuple-element.49), channel_id=1, source_target_pairs={{0,1},{1,0},{2,3},{3,2},{4,5},{5,4},{6,7},{7,6},{8,9},{9,8},{10,11... | collective-permute-start | bytes 393224 | tf_op jit(solution)/shard_map/ppermute | solution.py:430
  15.9 5.0 %collective-permute-start.6 = (bf16[2,128,256]{2,1,0:T(8,128)(2,1)S(1)}, bf16[2,128,256]{2,1,0:T(8,128)(2,1)S(1)}, u32[]{:S(2)}, u32[]{:S(2)}) collective-permute-start(bf16[2,128,256]{2,1,0:T(8,128)(2,1)S(1)} %get-tuple-element.52), channel_id=1, source_target_pairs={{0,1},{1,0},{2,3},{3,2},{4,5},{5,4},{6,7},{7,6},{8,9},{9,8},{10,11... | collective-permute-start | bytes 393224 | tf_op jit(solution)/shard_map/ppermute | solution.py:430
  21.0 8.9 %collective-permute-start.9 = (bf16[2,128,512]{2,1,0:T(8,128)(2,1)S(1)}, bf16[2,128,512]{2,1,0:T(8,128)(2,1)S(1)}, u32[]{:S(2)}, u32[]{:S(2)}) collective-permute-start(bf16[2,128,512]{2,1,0:T(8,128)(2,1)S(1)} %grads_total.3.refs_0_), channel_id=1, source_target_pairs={{0,8},{2,10},{4,12},{6,14},{8,0},{10,2},{12,4},{14,6},{16,24},{18,... | collective-permute-start | bytes 786440 | tf_op jit(solution)/shard_map/ppermute | solution.py:442
  22.6 11.6 %collective-permute-start.8 = (bf16[2,128,512]{2,1,0:T(8,128)(2,1)S(1)}, bf16[2,128,512]{2,1,0:T(8,128)(2,1)S(1)}, u32[]{:S(2)}, u32[]{:S(2)}) collective-permute-start(bf16[2,128,512]{2,1,0:T(8,128)(2,1)S(1)} %grads_total.3.refs_0_), channel_id=1, source_target_pairs={{0,4},{2,6},{4,0},{6,2},{8,12},{10,14},{12,8},{14,10},{16,20},{18,... | collective-permute-start | bytes 786440 | tf_op jit(solution)/shard_map/ppermute | solution.py:442
  24.1 10.0 %collective-permute-start.7 = (bf16[2,128,512]{2,1,0:T(8,128)(2,1)S(1)}, bf16[2,128,512]{2,1,0:T(8,128)(2,1)S(1)}, u32[]{:S(2)}, u32[]{:S(2)}) collective-permute-start(bf16[2,128,512]{2,1,0:T(8,128)(2,1)S(1)} %grads_total.3.refs_0_), channel_id=1, source_target_pairs={{0,12},{2,14},{4,8},{6,10},{8,4},{10,6},{12,0},{14,2},{16,28},{18,... | collective-permute-start | bytes 786440 | tf_op jit(solution)/shard_map/ppermute | solution.py:442
  34.6 2.0 %collective-permute-start.10 = (bf16[256,1024]{1,0:T(8,128)(2,1)S(1)}, bf16[256,1024]{1,0:T(8,128)(2,1)S(1)}, u32[]{:S(2)}, u32[]{:S(2)}) collective-permute-start(bf16[256,1024]{1,0:T(8,128)(2,1)S(1)} %weight_other_core.2), channel_id=1, source_target_pairs={{0,2},{2,0},{4,6},{6,4},{8,10},{10,8},{12,14},{14,12},{16,18},{18,... | collective-permute-start | bytes 1572872 | tf_op jit(solution)/shard_map/ppermute | solution.py:438
  36.7 6.4 %collective-permute-start.12 = (bf16[128,512]{1,0:T(8,128)(2,1)S(1)}, bf16[128,512]{1,0:T(8,128)(2,1)S(1)}, u32[]{:S(2)}, u32[]{:S(2)}) collective-permute-start(bf16[128,512]{1,0:T(8,128)(2,1)S(1)} %get-tuple-element.77), channel_id=1, source_target_pairs={{0,1},{1,0},{2,3},{3,2},{4,5},{5,4},{6,7},{7,6},{8,9},{9,8},{10,11... | collective-permute-start | bytes 393224 | tf_op jit(solution)/shard_map/ppermute | solution.py:430
  38.4 7.8 %collective-permute-start.14 = (bf16[128,512]{1,0:T(8,128)(2,1)S(1)}, bf16[128,512]{1,0:T(8,128)(2,1)S(1)}, u32[]{:S(2)}, u32[]{:S(2)}) collective-permute-start(bf16[128,512]{1,0:T(8,128)(2,1)S(1)} %get-tuple-element.78), channel_id=1, source_target_pairs={{0,1},{1,0},{2,3},{3,2},{4,5},{5,4},{6,7},{7,6},{8,9},{9,8},{10,11... | collective-permute-start | bytes 393224 | tf_op jit(solution)/shard_map/ppermute | solution.py:430
  39.2 8.6 %collective-permute-start.11 = (bf16[256,1024]{1,0:T(8,128)(2,1)S(1)}, bf16[256,1024]{1,0:T(8,128)(2,1)S(1)}, u32[]{:S(2)}, u32[]{:S(2)}) collective-permute-start(bf16[256,1024]{1,0:T(8,128)(2,1)S(1)} %weight_other_core.3), channel_id=1, source_target_pairs={{0,2},{2,0},{4,6},{6,4},{8,10},{10,8},{12,14},{14,12},{16,18},{18,... | collective-permute-start | bytes 1572872 | tf_op jit(solution)/shard_map/ppermute | solution.py:438
  43.1 11.6 %collective-permute-start.13 = (bf16[128,512]{1,0:T(8,128)(2,1)S(1)}, bf16[128,512]{1,0:T(8,128)(2,1)S(1)}, u32[]{:S(2)}, u32[]{:S(2)}) collective-permute-start(bf16[128,512]{1,0:T(8,128)(2,1)S(1)} %relay_total.2), channel_id=1, source_target_pairs={{0,16},{2,18},{4,20},{6,22},{8,24},{10,26},{12,28},{14,30},{16,0},... | collective-permute-start | bytes 393224 | tf_op jit(solution)/shard_map/ppermute | solution.py:435
  46.2 10.2 %collective-permute-start.16 = (bf16[128,512]{1,0:T(8,128)(2,1)S(1)}, bf16[128,512]{1,0:T(8,128)(2,1)S(1)}, u32[]{:S(2)}, u32[]{:S(2)}) collective-permute-start(bf16[128,512]{1,0:T(8,128)(2,1)S(1)} %relay_total.3), channel_id=1, source_target_pairs={{0,16},{2,18},{4,20},{6,22},{8,24},{10,26},{12,28},{14,30},{16,0},... | collective-permute-start | bytes 393224 | tf_op jit(solution)/shard_map/ppermute | solution.py:435
  47.9 8.5 %collective-permute-start.15 = (bf16[128,1024]{1,0:T(8,128)(2,1)S(1)}, bf16[128,1024]{1,0:T(8,128)(2,1)S(1)}, u32[]{:S(2)}, u32[]{:S(2)}) collective-permute-start(bf16[128,1024]{1,0:T(8,128)(2,1)S(1)} %get-tuple-element.86), channel_id=1, source_target_pairs={{0,1},{1,0},{2,3},{3,2},{4,5},{5,4},{6,7},{7,6},{8,9},{9,8},{10,11... | collective-permute-start | bytes 786440 | tf_op jit(solution)/shard_map/ppermute | solution.py:430

commit v11 on v9

--- a/solution.py
+++ b/solution.py
@@ -20,6 +20,7 @@
 PARAMS = pltpu.CompilerParams(vmem_limit_bytes=32 * 2**20)
 COST = pl.CostEstimate(flops=1024, bytes_accessed=1024, transcendentals=0)
 NEAR_COST = pl.CostEstimate(flops=10**10, bytes_accessed=1024, transcendentals=0)
+KEY_COST = pl.CostEstimate(flops=2 * 10**9, bytes_accessed=1024, transcendentals=0)
 EARLY = pl.CostEstimate(flops=10**10, bytes_accessed=1024, transcendentals=0)
 WHOLE = pl.BlockSpec(memory_space=pltpu.VMEM)
 FAR = pl.BlockSpec(memory_space=pltpu.HBM)
@@ -230,104 +231,101 @@
 
 
 def add_kernel(own_ref, *refs):
-    total = own_ref[...]
-    for back_ref in refs[:-1]:
-        total = total + back_ref[...].astype(jnp.float32)
-    refs[-1][...] = total.astype(refs[-1].dtype)
+    for part, out_ref in enumerate(refs[-2:]):
+        total = own_ref[part]
+        for back_ref in refs[:-2]:
+            total = total + back_ref[part].astype(jnp.float32)
+        out_ref[...] = total.astype(out_ref.dtype)
 
 
 def add_call(own, back):
     return pl.pallas_call(
         add_kernel,
         in_specs=[WHOLE] * (1 + len(back)),
-        out_specs=WHOLE,
-        out_shape=shape(own.shape, jnp.bfloat16),
+        out_specs=[WHOLE] * 2,
+        out_shape=[shape(own.shape[1:], jnp.bfloat16)] * 2,
         compiler_params=PARAMS,
         cost_estimate=COST,
         name="grads_total",
     )(own, *back)
 
 
-def weight_kernel(other, steps, far, tokens_ref, *refs):
+def weight_kernel(other, steps, far, counts, tokens_ref, *refs):
     g_refs, out_ref = refs[:-1], refs[-1]
-    half = out_ref.shape[1] // 2
     block = out_ref.shape[0] // len(steps)
     dp_rank = lax.axis_index("dp")
     core = lax.rem(dp_rank, CORES)
     z_rank = lax.div(dp_rank, CORES * MIDDLE * NEAR)
     if other:
         core = 1 - core
-    grads = [jnp.concatenate([g[part] for g in g_refs], axis=0) for part in range(2)]
+    grads = []
+    for count in counts:
+        grads.append(jnp.concatenate([g[...] for g in g_refs[:count]], axis=0))
+        g_refs = g_refs[count:]
     for at, step in enumerate(steps):
         start = (core * far + lax.rem(z_rank + step, far)) * block
         tokens = tokens_ref[pl.ds(pl.multiple_of(start, block), block), :]
-        for part in range(2):
-            out_ref[at * block : (at + 1) * block, part * half : (part + 1) * half] = dot(
-                tokens, grads[part], NN
+        for part, value in enumerate(grads):
+            width = value.shape[1]
+            out_ref[at * block : (at + 1) * block, part * width : (part + 1) * width] = dot(
+                tokens, value, NN
             ).astype(out_ref.dtype)
 
 
-def weight_call(other, steps, far, tokens, grads, dtype, cost=COST):
+def weight_call(other, steps, far, tokens, grads, dtype, cost):
+    operands = [value for part in grads for value in part]
     height = tokens.shape[0] // (CORES * far) * len(steps)
     return pl.pallas_call(
-        functools.partial(weight_kernel, other, steps, far),
-        in_specs=[WHOLE] * (1 + len(grads)),
+        functools.partial(weight_kernel, other, steps, far, tuple(len(part) for part in grads)),
+        in_specs=[WHOLE] * (1 + len(operands)),
         out_specs=WHOLE,
-        out_shape=shape((height, 2 * grads[0].shape[2]), dtype),
+        out_shape=shape((height, sum(part[0].shape[1] for part in grads)), dtype),
         compiler_params=PARAMS,
         cost_estimate=cost,
         name="weight_other_core" if other else "weight_this_core",
-    )(tokens, *grads)
+    )(tokens, *operands)
 
 
 def chip_kernel(ctx_count, count, mine_ref, theirs_ref, *out_refs):
     block = out_refs[0].shape[0] // count
     x_rank = lax.axis_index("ctx")
-    cuts = (len(out_refs) - 1) // (ctx_count - 1)
-    for x in range(ctx_count):
-        outs = out_refs[1 + (x - 1) * cuts : 1 + x * cuts] if x else out_refs[:1]
+    for x, out_ref in enumerate(out_refs):
         for z in range(count):
             start = (z * ctx_count + lax.rem(x_rank + x, ctx_count)) * block
             at = pl.ds(pl.multiple_of(start, block), block)
             total = mine_ref[at, :] + theirs_ref[at, :].astype(jnp.float32)
-            width = total.shape[1] // len(outs)
-            for i, out in enumerate(outs):
-                out[z * block : (z + 1) * block, :] = total[:, i * width : (i + 1) * width].astype(
-                    out.dtype
-                )
-
-
-def chip_call(ctx_count, count, cuts, mine, theirs):
+            out_ref[z * block : (z + 1) * block, :] = total.astype(out_ref.dtype)
+
+
+def chip_call(ctx_count, count, mine, theirs):
     height, columns = mine.shape
-    rows = height // ctx_count
+    dims = (height // ctx_count, columns)
     return pl.pallas_call(
         functools.partial(chip_kernel, ctx_count, count),
         in_specs=[WHOLE] * 2,
-        out_specs=[WHOLE] * (1 + cuts * (ctx_count - 1)),
-        out_shape=[shape((rows, columns), jnp.float32)]
-        + [shape((rows, columns // cuts), jnp.bfloat16)] * (cuts * (ctx_count - 1)),
-        compiler_params=PARAMS,
-        cost_estimate=COST,
-        name="chip_far" if cuts > 1 else "chip_near",
+        out_specs=[WHOLE] * ctx_count,
+        out_shape=[shape(dims, jnp.float32)] + [shape(dims, jnp.bfloat16)] * (ctx_count - 1),
+        compiler_params=PARAMS,
+        cost_estimate=COST,
+        name="chip_total",
     )(mine, theirs)
 
 
-def relay_kernel(part, count, away_ref, *refs):
+def relay_kernel(count, away_ref, *refs):
     in_refs, out_refs = refs[:-count], refs[-count:]
-    block, width = out_refs[0].shape
-    columns = slice(part * width, (part + 1) * width)
+    block = out_refs[0].shape[0]
     for z, out_ref in enumerate(out_refs):
         at = slice(z * block, (z + 1) * block)
-        total = away_ref[at, columns]
+        total = away_ref[at, :]
         for in_ref in in_refs:
             total = total + in_ref[at, :].astype(jnp.float32)
         out_ref[...] = total.astype(out_ref.dtype)
 
 
-def relay_call(part, count, away, arrived):
-    height, width = arrived[0].shape
-    return pl.pallas_call(
-        functools.partial(relay_kernel, part, count),
+def relay_call(count, away, arrived):
+    height, width = away.shape
+    return pl.pallas_call(
+        functools.partial(relay_kernel, count),
         in_specs=[WHOLE] * (1 + len(arrived)),
         out_specs=[WHOLE] * count,
         out_shape=[shape((height // count, width), jnp.bfloat16)] * count,
@@ -437,28 +435,35 @@
     other = after(other, grads)
     own_scores, own = block(0, keys=saved_keys, values=saved_values, other=other)
     back, pieces = lax.optimization_barrier((back, pieces))
-    total = add_call(own, back)
-    grads = [over_group(total, i) if i else total for i in ORDER]
-    own_scores, pieces = after((own_scores, pieces), total)
+    totals = add_call(own, back)
+    grads = [[over_group(total, i) if i else total for i in ORDER] for total in totals]
+    tokens = turn_call(after([pieces[i] for i in ORDER], totals))
+
+    def chip_sums(steps, grads, cost):
+        theirs = weight_call(True, steps, far, tokens, grads, jnp.bfloat16, COST)
+        arriving = over_cores(theirs)
+        if cost is KEY_COST:
+            grads = after(grads, values_there)
+        mine = weight_call(False, steps, far, tokens, grads, jnp.float32, cost)
+        return chip_call(ctx_count, len(steps), mine, arriving)
+
+    values_there = grads[1]
+    steps = tuple(range(1, far))
+    away, arrived, from_far, blocks = [], [], [], []
+    for part in range(2):
+        part_grads = after(grads[part], blocks) if part else grads[0]
+        sums, *blocks = chip_sums(steps, [part_grads], COST if part else KEY_COST)
+        away.append(sums)
+        arrived.append([over_ctx(value, s) for s, value in enumerate(blocks, 1)])
+    own_block, *near = chip_sums((0,), after(grads, blocks), NEAR_COST)
+    arrived[0] = after(arrived[0], blocks)
+    for part in range(2):
+        relayed = relay_call(far - 1, away[part], arrived[part])
+        from_far.append([over_far(value, s) for s, value in enumerate(relayed, 1)])
+    own_scores = after(own_scores, relayed)
     query_gradient = query_call(
         [own_scores] + scores, [saved_keys] + [pair[0] for pair in visiting], rows
     )
-    tokens = turn_call(after([pieces[i] for i in ORDER], query_gradient))
-
-    def chip_sums(steps, cuts, grads):
-        theirs = weight_call(True, steps, far, tokens, grads, jnp.bfloat16)
-        arriving = over_cores(theirs)
-        cost = COST if cuts > 1 else NEAR_COST
-        mine = weight_call(False, steps, far, tokens, grads, jnp.float32, cost)
-        return chip_call(ctx_count, len(steps), cuts, mine, arriving)
-
-    away, *blocks = chip_sums(tuple(range(1, far)), 2, grads)
-    arrived = [over_ctx(value, 1 + i // 2) for i, value in enumerate(blocks)]
-    from_far = []
-    for part in range(2):
-        relayed = relay_call(part, far - 1, away, arrived[part::2])
-        from_far.append([over_far(value, s) for s, value in enumerate(relayed, 1)])
-    own_block, *near = chip_sums((0,), 1, after(grads, blocks))
     near = after(near, relayed)
     near = [over_ctx(value, s) for s, value in enumerate(near, 1)]
     key_weight_grad, value_weight_grad = final_call(

time: 57.4 us -> 57 us (level)
  waiting for transfers between devices: 24 us -> 17.2 us
  starting transfers between devices: 20 us -> 26 us
    ppermute x6 -> x9, starting transfers between devices: 7.19 us -> 12.6 us  [over_group(): return lax.ppermute(value, 'dp', [(s, s ^ flip) for s in range(dp_count)])]
    ppermute x6 -> x9, waiting for transfers between devices: 10.6 us -> 7.37 us  [over_group(): return lax.ppermute(value, 'dp', [(s, s ^ flip) for s in range(dp_count)])]
    ppermute x2, waiting for transfers between devices: 6.96 us -> 5.43 us  [over_far(): return lax.ppermute(value, 'dp', pairs)]
    ppermute x2 -> x3, waiting for transfers between devices: 1.46 us -> 0.06 us  [over_cores(): return lax.ppermute(value, 'dp', [(s, s ^ 1) for s in range(dp_count)])]
    ppermute x6, starting transfers between devices: 8.54 us -> 9.19 us  [over_ctx(): return lax.ppermute(value, 'ctx', pairs)]
    pallas_call x6 -> x8, Pallas kernels: 1.78 us -> 2.09 us  [the longest x6 2.04 us: weight_call(): pl.pallas_call(functools.partial(weight_kernel, other, steps, far, tuple(...]
  transfers between devices with their start and end apart: 16 -> 20, of which waited for: 9 -> 12; matrix products, arithmetic and copies ran while one was open for 0% -> 0% of each run, Pallas kernels for 19% -> 20%
where the time goes in v11:
time: 57 us; the launch traced here: 56.8 us
  starting transfers between devices  26 us (46%)
  waiting for transfers between devices  17.2 us (30%)
  Pallas kernels  12.7 us (22%)
  between operations  0.82 us (1%)
    ppermute x9, starting transfers between devices, over_group(): return lax.ppermute(value, 'dp', [(s, s ^ flip) for s in range(dp_count)])  12.6 us
    ppermute x6, starting transfers between devices, over_ctx(): return lax.ppermute(value, 'ctx', pairs)  9.19 us
    ppermute x9, waiting for transfers between devices, over_group(): return lax.ppermute(value, 'dp', [(s, s ^ flip) for s in range(dp_count)])  7.37 us
    pallas_call x2, Pallas kernels, block_call(): pl.pallas_call(functools.partial(block_kernel, ctx_count, step), in_specs...  5.51 us
    ppermute x2, waiting for transfers between devices, over_far(): return lax.ppermute(value, 'dp', pairs)  5.43 us
    ppermute x6, waiting for transfers between devices, over_ctx(): return lax.ppermute(value, 'ctx', pairs)  4.38 us
    ppermute x2, starting transfers between devices, over_far(): return lax.ppermute(value, 'dp', pairs)  4.02 us
    pallas_call x6, Pallas kernels, weight_call(): pl.pallas_call(functools.partial(weight_kernel, other, steps, far, tuple(...  2.04 us
  transfers between devices with their start and end apart: 20, of which 12 were waited for; matrix products, arithmetic and copies ran while one was open for 0% of the time, Pallas kernels for 20%

profile of v11, /device:TPU:0, one launch (start us, length us, event | category | flops | bytes accessed | tf_op | source)
XLA Modules:
  0.0 56.8 jit_solution(8706866308835725376)
XLA Ops:
  0.6 3.0 %collective-permute-start.1 = (bf16[128,512]{1,0:T(8,128)(2,1)}, bf16[128,512]{1,0:T(8,128)(2,1)S(1)}, u32[]{:S(2)}, u32[]{:S(2)}) collective-permute-start(bf16[128,512]{1,0:T(8,128)(2,1)} %refs_4_.1), channel_id=1, source_target_pairs={{0,1},{1,0},{2,3},{3,2},{4,5},{5,4},{6,7},{7,6},{8,9},{9,8},{10,11... | collective-permute-start | bytes 393224 | tf_op jit(solution)/shard_map/ppermute | solution.py:401
  3.6 0.1 collective-permute-start
  3.7 1.9 %pieces.1 = (bf16[128,1024]{1,0:T(8,128)(2,1)S(1)}, bf16[128,1024]{1,0:T(8,128)(2,1)S(1)}, bf16[128,1024]{1,0:T(8,128)(2,1)S(1)}, bf16[128,1024]{1,0:T(8,128)(2,...) custom-call(bf16[128,4096]{1,0:T(8,128)(2,1)} %in_hbm.1, bf16[128,4096]{1,0:T(8,128)(2,1)} %refs_0_.3, ...), custom_call_target="tpu_custom_call" | custom-call | flops 1024 | bytes 1024 | tf_op jit(solution)/shard_map/pieces/pallas_call | solution.py:197
  5.7 2.1 %collective-permute-start.3 = (bf16[128,1024]{1,0:T(8,128)(2,1)S(1)}, bf16[128,1024]{1,0:T(8,128)(2,1)S(1)}, u32[]{:S(2)}, u32[]{:S(2)}) collective-permute-start(bf16[128,1024]{1,0:T(8,128)(2,1)S(1)} %get-tuple-element.60), channel_id=1, source_target_pairs={{0,8},{2,10},{4,12},{6,14},{8,0},{10,2},{12,4},{14,6},{16,24},{18,... | collective-permute-start | bytes 786440 | tf_op jit(solution)/shard_map/ppermute | solution.py:413
  7.8 1.5 %collective-permute-start.4 = (bf16[128,1024]{1,0:T(8,128)(2,1)S(1)}, bf16[128,1024]{1,0:T(8,128)(2,1)S(1)}, u32[]{:S(2)}, u32[]{:S(2)}) collective-permute-start(bf16[128,1024]{1,0:T(8,128)(2,1)S(1)} %get-tuple-element.61), channel_id=1, source_target_pairs={{0,4},{2,6},{4,0},{6,2},{8,12},{10,14},{12,8},{14,10},{16,20},{18,... | collective-permute-start | bytes 786440 | tf_op jit(solution)/shard_map/ppermute | solution.py:413
  9.3 0.0 collective-permute-start.5
  9.3 0.8 %collective-permute-done.refs_3_ = bf16[128,512]{1,0:T(8,128)(2,1)S(1)} collective-permute-done((bf16[128,512]{1,0:T(8,128)(2,1)}, bf16[128,512]{1,0:T(8,128)(2,1)S(1)}, u32[]{:S(2)}, u32[]{:S(2)}) %collective-permute-start) | collective-permute-done | bytes 131104 | tf_op jit(solution)/shard_map/ppermute | solution.py:401
  10.2 3.1 %visiting_keys.1 = (bf16[128,4096]{1,0:T(8,128)(2,1)S(1)}, bf16[2,128,512]{2,1,0:T(8,128)(2,1)S(1)}, f32[32,128]{1,0:T(8,128)S(1)}) custom-call(s32[1,4]{1,0:T(1,128)} %refs_0_.5, bf16[128,4096]{1,0:T(8,128)(2,1)S(1)} %copy-done, bf16[128,4096]{1,0:T(8,128)(2,1)S(1)} %copy-done.1, bf16[128,512]{1,0:T(8,128)(2,1)S(1)} %collective-permute-done.refs_3_, ...), custom_call_target="tpu_custom_call" | custom-call | flops 1024 | bytes 1024 | tf_op jit(solution)/shard_map/visiting_keys/pallas_call | solution.py:122
  13.3 1.8 %collective-permute-start.2 = (bf16[2,128,512]{2,1,0:T(8,128)(2,1)S(1)}, bf16[2,128,512]{2,1,0:T(8,128)(2,1)S(1)}, u32[]{:S(2)}, u32[]{:S(2)}) collective-permute-start(bf16[2,128,512]{2,1,0:T(8,128)(2,1)S(1)} %get-tuple-element.56), channel_id=1, source_target_pairs={{0,1},{1,0},{2,3},{3,2},{4,5},{5,4},{6,7},{7,6},{8,9},{9,8},{10,11... | collective-permute-start | bytes 786440 | tf_op jit(solution)/shard_map/ppermute | solution.py:401
  15.1 2.4 %own_keys.1 = (bf16[128,4096]{1,0:T(8,128)(2,1)S(1)}, f32[2,128,512]{2,1,0:T(8,128)S(1)}) custom-call(s32[1,4]{1,0:T(1,128)} %refs_0_.5, bf16[128,4096]{1,0:T(8,128)(2,1)S(1)} %copy-done, bf16[128,4096]{1,0:T(8,128)(2,1)S(1)} %copy-done.1, bf16[128,512]{1,0:T(8,128)(2,1)S(1)} %copy-done.2, bf16[128,512]{1,0:T(8,128)(2,1)S(1)} %copy-done.3, ...), custom_call_target="tpu_custom_call" | custom-call | flops 1024 | bytes 1024 | tf_op jit(solution)/shard_map/own_keys/pallas_call | solution.py:122
  17.5 3.1 %collective-permute-done.4.refs_2_ = bf16[128,1024]{1,0:T(8,128)(2,1)S(1)} collective-permute-done((bf16[128,1024]{1,0:T(8,128)(2,1)S(1)}, bf16[128,1024]{1,0:T(8,128)(2,1)S(1)}, u32[]{:S(2)}, u32[]{:S(2)}) %collective-permute-start.4) | collective-permute-done | bytes 262176 | tf_op jit(solution)/shard_map/ppermute | solution.py:413
  20.6 0.0 collective-permute-done.5.refs_1_
  20.6 0.3 collective-permute-done.2.refs_0_
  20.9 1.6 %collective-permute-start.11 = (bf16[128,512]{1,0:T(8,128)(2,1)S(1)}, bf16[128,512]{1,0:T(8,128)(2,1)S(1)}, u32[]{:S(2)}, u32[]{:S(2)}) collective-permute-start(bf16[128,512]{1,0:T(8,128)(2,1)S(1)} %get-tuple-element.88.refs_0_), channel_id=1, source_target_pairs={{0,8},{2,10},{4,12},{6,14},{8,0},{10,2},{12,4},{14,6},{16,24},{18,... | collective-permute-start | bytes 393224 | tf_op jit(solution)/shard_map/ppermute | solution.py:413
  22.5 1.5 %collective-permute-start.10 = (bf16[128,512]{1,0:T(8,128)(2,1)S(1)}, bf16[128,512]{1,0:T(8,128)(2,1)S(1)}, u32[]{:S(2)}, u32[]{:S(2)}) collective-permute-start(bf16[128,512]{1,0:T(8,128)(2,1)S(1)} %get-tuple-element.88.refs_0_), channel_id=1, source_target_pairs={{0,4},{2,6},{4,0},{6,2},{8,12},{10,14},{12,8},{14,10},{16,20},{18,... | collective-permute-start | bytes 393224 | tf_op jit(solution)/shard_map/ppermute | solution.py:413
  24.0 0.5 collective-permute-start.9
  24.5 1.5 %collective-permute-start.8 = (bf16[128,512]{1,0:T(8,128)(2,1)S(1)}, bf16[128,512]{1,0:T(8,128)(2,1)S(1)}, u32[]{:S(2)}, u32[]{:S(2)}) collective-permute-start(bf16[128,512]{1,0:T(8,128)(2,1)S(1)} %get-tuple-element.92.refs_0_.refs_4_), channel_id=1, source_target_pairs={{0,8},{2,10},{4,12},{6,14},{8,0},{10,2},{12,4},{14,6},{16,24},{18,... | collective-permute-start | bytes 393224 | tf_op jit(solution)/shard_map/ppermute | solution.py:413
  26.0 1.5 %collective-permute-start.7 = (bf16[128,512]{1,0:T(8,128)(2,1)S(1)}, bf16[128,512]{1,0:T(8,128)(2,1)S(1)}, u32[]{:S(2)}, u32[]{:S(2)}) collective-permute-start(bf16[128,512]{1,0:T(8,128)(2,1)S(1)} %get-tuple-element.92.refs_0_.refs_4_), channel_id=1, source_target_pairs={{0,4},{2,6},{4,0},{6,2},{8,12},{10,14},{12,8},{14,10},{16,20},{18,... | collective-permute-start | bytes 393224 | tf_op jit(solution)/shard_map/ppermute | solution.py:413
  27.5 2.4 %collective-permute-start.6 = (bf16[128,512]{1,0:T(8,128)(2,1)S(1)}, bf16[128,512]{1,0:T(8,128)(2,1)S(1)}, u32[]{:S(2)}, u32[]{:S(2)}) collective-permute-start(bf16[128,512]{1,0:T(8,128)(2,1)S(1)} %get-tuple-element.92.refs_0_.refs_4_), channel_id=1, source_target_pairs={{0,12},{2,14},{4,8},{6,10},{8,4},{10,6},{12,0},{14,2},{16,28},{18,... | collective-permute-start | bytes 393224 | tf_op jit(solution)/shard_map/ppermute | solution.py:413
  29.9 0.3 turn_pieces.1.tokens_ref
  30.2 0.1 collective-permute-done.10.refs_2_
  30.3 1.2 %collective-permute-done.9.refs_1_ = bf16[128,512]{1,0:T(8,128)(2,1)S(1)} collective-permute-done((bf16[128,512]{1,0:T(8,128)(2,1)S(1)}, bf16[128,512]{1,0:T(8,128)(2,1)S(1)}, u32[]{:S(2)}, u32[]{:S(2)}) %collective-permute-start.9) | collective-permute-done | bytes 131104 | tf_op jit(solution)/shard_map/ppermute | solution.py:413
  31.5 0.3 weight_other_core.3
  31.8 0.1 collective-permute-start.12
  31.8 0.7 %collective-permute-done.8.refs_3_.refs_7_ = bf16[128,512]{1,0:T(8,128)(2,1)S(1)} collective-permute-done((bf16[128,512]{1,0:T(8,128)(2,1)S(1)}, bf16[128,512]{1,0:T(8,128)(2,1)S(1)}, u32[]{:S(2)}, u32[]{:S(2)}) %collective-permute-start.8) | collective-permute-done | bytes 131104 | tf_op jit(solution)/shard_map/ppermute | solution.py:413
  32.5 1.0 %collective-permute-done.7.refs_2_.refs_6_ = bf16[128,512]{1,0:T(8,128)(2,1)S(1)} collective-permute-done((bf16[128,512]{1,0:T(8,128)(2,1)S(1)}, bf16[128,512]{1,0:T(8,128)(2,1)S(1)}, u32[]{:S(2)}, u32[]{:S(2)}) %collective-permute-start.7) | collective-permute-done | bytes 131104 | tf_op jit(solution)/shard_map/ppermute | solution.py:413
  33.5 1.4 %collective-permute-done.6.refs_1_.refs_5_ = bf16[128,512]{1,0:T(8,128)(2,1)S(1)} collective-permute-done((bf16[128,512]{1,0:T(8,128)(2,1)S(1)}, bf16[128,512]{1,0:T(8,128)(2,1)S(1)}, u32[]{:S(2)}, u32[]{:S(2)}) %collective-permute-start.6) | collective-permute-done | bytes 131104 | tf_op jit(solution)/shard_map/ppermute | solution.py:413
  34.9 0.3 weight_this_core.3.mine_ref
  35.2 0.1 chip_total.3
  35.3 0.3 weight_other_core.4
  35.6 0.1 collective-permute-start.13
  35.7 1.6 %collective-permute-start.16 = (bf16[128,512]{1,0:T(8,128)(2,1)S(1)}, bf16[128,512]{1,0:T(8,128)(2,1)S(1)}, u32[]{:S(2)}, u32[]{:S(2)}) collective-permute-start(bf16[128,512]{1,0:T(8,128)(2,1)S(1)} %get-tuple-element.79), channel_id=1, source_target_pairs={{0,1},{1,0},{2,3},{3,2},{4,5},{5,4},{6,7},{7,6},{8,9},{9,8},{10,11... | collective-permute-start | bytes 393224 | tf_op jit(solution)/shard_map/ppermute | solution.py:401
  37.2 0.3 weight_this_core.4.mine_ref
  37.5 0.1 chip_total.4
  37.6 1.2 %collective-permute-start.14 = (bf16[128,512]{1,0:T(8,128)(2,1)S(1)}, bf16[128,512]{1,0:T(8,128)(2,1)S(1)}, u32[]{:S(2)}, u32[]{:S(2)}) collective-permute-start(bf16[128,512]{1,0:T(8,128)(2,1)S(1)} %get-tuple-element.85), channel_id=1, source_target_pairs={{0,1},{1,0},{2,3},{3,2},{4,5},{5,4},{6,7},{7,6},{8,9},{9,8},{10,11... | collective-permute-start | bytes 393224 | tf_op jit(solution)/shard_map/ppermute | solution.py:401
  38.8 3.2 %collective-permute-done.16.refs_0_ = bf16[128,512]{1,0:T(8,128)(2,1)S(1)} collective-permute-done((bf16[128,512]{1,0:T(8,128)(2,1)S(1)}, bf16[128,512]{1,0:T(8,128)(2,1)S(1)}, u32[]{:S(2)}, u32[]{:S(2)}) %collective-permute-start.16) | collective-permute-done | bytes 131104 | tf_op jit(solution)/shard_map/ppermute | solution.py:401
  42.0 2.7 %collective-permute-start.17 = (bf16[128,512]{1,0:T(8,128)(2,1)S(1)}, bf16[128,512]{1,0:T(8,128)(2,1)S(1)}, u32[]{:S(2)}, u32[]{:S(2)}) collective-permute-start(bf16[128,512]{1,0:T(8,128)(2,1)S(1)} %relay_total.3), channel_id=1, source_target_pairs={{0,16},{2,18},{4,20},{6,22},{8,24},{10,26},{12,28},{14,30},{16,0},... | collective-permute-start | bytes 393224 | tf_op jit(solution)/shard_map/ppermute | solution.py:406
  44.7 0.4 weight_other_core.5
  45.2 0.1 collective-permute-start.15
  45.2 0.4 weight_this_core.5.mine_ref
  45.7 1.4 %collective-permute-start.19 = (bf16[128,512]{1,0:T(8,128)(2,1)S(1)}, bf16[128,512]{1,0:T(8,128)(2,1)S(1)}, u32[]{:S(2)}, u32[]{:S(2)}) collective-permute-start(bf16[128,512]{1,0:T(8,128)(2,1)S(1)} %relay_total.2), channel_id=1, source_target_pairs={{0,16},{2,18},{4,20},{6,22},{8,24},{10,26},{12,28},{14,30},{16,0},... | collective-permute-start | bytes 393224 | tf_op jit(solution)/shard_map/ppermute | solution.py:406
  47.1 0.1 collective-permute-done.15.theirs_ref
  47.1 0.1 chip_total.5
  47.2 1.5 %collective-permute-start.18 = (bf16[128,1024]{1,0:T(8,128)(2,1)S(1)}, bf16[128,1024]{1,0:T(8,128)(2,1)S(1)}, u32[]{:S(2)}, u32[]{:S(2)}) collective-permute-start(bf16[128,1024]{1,0:T(8,128)(2,1)S(1)} %get-tuple-element.100), channel_id=1, source_target_pairs={{0,1},{1,0},{2,3},{3,2},{4,5},{5,4},{6,7},{7,6},{8,9},{9,8},{10,11... | collective-permute-start | bytes 786440 | tf_op jit(solution)/shard_map/ppermute | solution.py:401
  48.8 4.8 %collective-permute-done.17.refs_0_ = bf16[128,512]{1,0:T(8,128)(2,1)S(1)} collective-permute-done((bf16[128,512]{1,0:T(8,128)(2,1)S(1)}, bf16[128,512]{1,0:T(8,128)(2,1)S(1)}, u32[]{:S(2)}, u32[]{:S(2)}) %collective-permute-start.17) | collective-permute-done | bytes 131104 | tf_op jit(solution)/shard_map/ppermute | solution.py:406
  53.6 1.7 %query_gradient.1 = bf16[128,4096]{1,0:T(8,128)(2,1)} custom-call(bf16[128,4096]{1,0:T(8,128)(2,1)S(1)} %get-tuple-element.86.refs_0_, bf16[128,4096]{1,0:T(8,128)(2,1)S(1)} %get-tuple-element.87.refs_1_, bf16[128,512]{1,0:T(8,128)(2,1)S(1)} %copy-done.2, bf16[128,512]{1,0:T(8,128)(2,1)S(1)} %collective-permute-done.refs_3_), custom_call_target="tpu_custom_call" | custom-call | flops 1024 | bytes 1024 | tf_op jit(solution)/shard_map/query_gradient/pallas_call | solution.py:149
  55.3 0.6 %collective-permute-done.19.refs_1_ = bf16[128,512]{1,0:T(8,128)(2,1)S(1)} collective-permute-done((bf16[128,512]{1,0:T(8,128)(2,1)S(1)}, bf16[128,512]{1,0:T(8,128)(2,1)S(1)}, u32[]{:S(2)}, u32[]{:S(2)}) %collective-permute-start.19) | collective-permute-done | bytes 131104 | tf_op jit(solution)/shard_map/ppermute | solution.py:406
  56.0 0.8 %weight_total.1 = (f32[128,512]{1,0:T(8,128)}, f32[128,512]{1,0:T(8,128)}) custom-call(f32[128,1024]{1,0:T(8,128)S(1)} %get-tuple-element.96.own_ref, f32[128,512]{1,0:T(8,128)S(1)} %key_far_total.1.key_far_ref, bf16[128,1024]{1,0:T(8,128)(2,1)S(1)} %collective-permute-done.18.refs_0_, bf16[128,512]{1,0:T(8,128)(2,1)S(1)} %collective-permute-done.19.refs_1_), custom_call_target="tpu_custom_call" | custom-call | flops 1024 | bytes 1024 | tf_op jit(solution)/shard_map/weight_total/pallas_call | solution.py:373
  (19 shorter events, 0.2 us)
Async XLA Ops:
  0.6 8.7 %collective-permute-start.1 = (bf16[128,512]{1,0:T(8,128)(2,1)}, bf16[128,512]{1,0:T(8,128)(2,1)S(1)}, u32[]{:S(2)}, u32[]{:S(2)}) collective-permute-start(bf16[128,512]{1,0:T(8,128)(2,1)} %refs_4_.1), channel_id=1, source_target_pairs={{0,1},{1,0},{2,3},{3,2},{4,5},{5,4},{6,7},{7,6},{8,9},{9,8},{10,11... | collective-permute-start | bytes 393224 | tf_op jit(solution)/shard_map/ppermute | solution.py:401
  3.6 6.5 %collective-permute-start = (bf16[128,512]{1,0:T(8,128)(2,1)}, bf16[128,512]{1,0:T(8,128)(2,1)S(1)}, u32[]{:S(2)}, u32[]{:S(2)}) collective-permute-start(bf16[128,512]{1,0:T(8,128)(2,1)} %refs_2_.5), channel_id=1, source_target_pairs={{0,1},{1,0},{2,3},{3,2},{4,5},{5,4},{6,7},{7,6},{8,9},{9,8},{10,11... | collective-permute-start | bytes 393224 | tf_op jit(solution)/shard_map/ppermute | solution.py:401
  3.7 6.4 %copy-start = (bf16[128,4096]{1,0:T(8,128)(2,1)S(1)}, bf16[128,4096]{1,0:T(8,128)(2,1)}, u32[]{:S(2)}) copy-start(bf16[128,4096]{1,0:T(8,128)(2,1)} %refs_1_.3) | copy-start | bytes 3145732
  3.7 6.4 %copy-start.1 = (bf16[128,4096]{1,0:T(8,128)(2,1)S(1)}, bf16[128,4096]{1,0:T(8,128)(2,1)}, u32[]{:S(2)}) copy-start(bf16[128,4096]{1,0:T(8,128)(2,1)} %refs_2_.4) | copy-start | bytes 3145732
  5.7 11.8 %collective-permute-start.3 = (bf16[128,1024]{1,0:T(8,128)(2,1)S(1)}, bf16[128,1024]{1,0:T(8,128)(2,1)S(1)}, u32[]{:S(2)}, u32[]{:S(2)}) collective-permute-start(bf16[128,1024]{1,0:T(8,128)(2,1)S(1)} %get-tuple-element.60), channel_id=1, source_target_pairs={{0,8},{2,10},{4,12},{6,14},{8,0},{10,2},{12,4},{14,6},{16,24},{18,... | collective-permute-start | bytes 786440 | tf_op jit(solution)/shard_map/ppermute | solution.py:413
  7.8 12.8 %collective-permute-start.4 = (bf16[128,1024]{1,0:T(8,128)(2,1)S(1)}, bf16[128,1024]{1,0:T(8,128)(2,1)S(1)}, u32[]{:S(2)}, u32[]{:S(2)}) collective-permute-start(bf16[128,1024]{1,0:T(8,128)(2,1)S(1)} %get-tuple-element.61), channel_id=1, source_target_pairs={{0,4},{2,6},{4,0},{6,2},{8,12},{10,14},{12,8},{14,10},{16,20},{18,... | collective-permute-start | bytes 786440 | tf_op jit(solution)/shard_map/ppermute | solution.py:413
  9.3 11.3 %collective-permute-start.5 = (bf16[128,1024]{1,0:T(8,128)(2,1)S(1)}, bf16[128,1024]{1,0:T(8,128)(2,1)S(1)}, u32[]{:S(2)}, u32[]{:S(2)}) collective-permute-start(bf16[128,1024]{1,0:T(8,128)(2,1)S(1)} %get-tuple-element.62), channel_id=1, source_target_pairs={{0,12},{2,14},{4,8},{6,10},{8,4},{10,6},{12,0},{14,2},{16,28},{18,... | collective-permute-start | bytes 786440 | tf_op jit(solution)/shard_map/ppermute | solution.py:413
  10.2 5.0 %copy-start.2 = (bf16[128,512]{1,0:T(8,128)(2,1)S(1)}, bf16[128,512]{1,0:T(8,128)(2,1)}, u32[]{:S(2)}) copy-start(bf16[128,512]{1,0:T(8,128)(2,1)} %refs_2_.5) | copy-start | bytes 393220
  10.2 5.0 %copy-start.3 = (bf16[128,512]{1,0:T(8,128)(2,1)S(1)}, bf16[128,512]{1,0:T(8,128)(2,1)}, u32[]{:S(2)}) copy-start(bf16[128,512]{1,0:T(8,128)(2,1)} %refs_4_.1) | copy-start | bytes 393220
  13.3 7.6 %collective-permute-start.2 = (bf16[2,128,512]{2,1,0:T(8,128)(2,1)S(1)}, bf16[2,128,512]{2,1,0:T(8,128)(2,1)S(1)}, u32[]{:S(2)}, u32[]{:S(2)}) collective-permute-start(bf16[2,128,512]{2,1,0:T(8,128)(2,1)S(1)} %get-tuple-element.56), channel_id=1, source_target_pairs={{0,1},{1,0},{2,3},{3,2},{4,5},{5,4},{6,7},{7,6},{8,9},{9,8},{10,11... | collective-permute-start | bytes 786440 | tf_op jit(solution)/shard_map/ppermute | solution.py:401
  20.9 6.6 %collective-permute-start.11 = (bf16[128,512]{1,0:T(8,128)(2,1)S(1)}, bf16[128,512]{1,0:T(8,128)(2,1)S(1)}, u32[]{:S(2)}, u32[]{:S(2)}) collective-permute-start(bf16[128,512]{1,0:T(8,128)(2,1)S(1)} %get-tuple-element.88.refs_0_), channel_id=1, source_target_pairs={{0,8},{2,10},{4,12},{6,14},{8,0},{10,2},{12,4},{14,6},{16,24},{18,... | collective-permute-start | bytes 393224 | tf_op jit(solution)/shard_map/ppermute | solution.py:413
  22.5 7.8 %collective-permute-start.10 = (bf16[128,512]{1,0:T(8,128)(2,1)S(1)}, bf16[128,512]{1,0:T(8,128)(2,1)S(1)}, u32[]{:S(2)}, u32[]{:S(2)}) collective-permute-start(bf16[128,512]{1,0:T(8,128)(2,1)S(1)} %get-tuple-element.88.refs_0_), channel_id=1, source_target_pairs={{0,4},{2,6},{4,0},{6,2},{8,12},{10,14},{12,8},{14,10},{16,20},{18,... | collective-permute-start | bytes 393224 | tf_op jit(solution)/shard_map/ppermute | solution.py:413
  24.0 7.4 %collective-permute-start.9 = (bf16[128,512]{1,0:T(8,128)(2,1)S(1)}, bf16[128,512]{1,0:T(8,128)(2,1)S(1)}, u32[]{:S(2)}, u32[]{:S(2)}) collective-permute-start(bf16[128,512]{1,0:T(8,128)(2,1)S(1)} %get-tuple-element.88.refs_0_), channel_id=1, source_target_pairs={{0,12},{2,14},{4,8},{6,10},{8,4},{10,6},{12,0},{14,2},{16,28},{18,... | collective-permute-start | bytes 393224 | tf_op jit(solution)/shard_map/ppermute | solution.py:413
  24.5 8.0 %collective-permute-start.8 = (bf16[128,512]{1,0:T(8,128)(2,1)S(1)}, bf16[128,512]{1,0:T(8,128)(2,1)S(1)}, u32[]{:S(2)}, u32[]{:S(2)}) collective-permute-start(bf16[128,512]{1,0:T(8,128)(2,1)S(1)} %get-tuple-element.92.refs_0_.refs_4_), channel_id=1, source_target_pairs={{0,8},{2,10},{4,12},{6,14},{8,0},{10,2},{12,4},{14,6},{16,24},{18,... | collective-permute-start | bytes 393224 | tf_op jit(solution)/shard_map/ppermute | solution.py:413
  26.0 7.5 %collective-permute-start.7 = (bf16[128,512]{1,0:T(8,128)(2,1)S(1)}, bf16[128,512]{1,0:T(8,128)(2,1)S(1)}, u32[]{:S(2)}, u32[]{:S(2)}) collective-permute-start(bf16[128,512]{1,0:T(8,128)(2,1)S(1)} %get-tuple-element.92.refs_0_.refs_4_), channel_id=1, source_target_pairs={{0,4},{2,6},{4,0},{6,2},{8,12},{10,14},{12,8},{14,10},{16,20},{18,... | collective-permute-start | bytes 393224 | tf_op jit(solution)/shard_map/ppermute | solution.py:413
  27.5 7.4 %collective-permute-start.6 = (bf16[128,512]{1,0:T(8,128)(2,1)S(1)}, bf16[128,512]{1,0:T(8,128)(2,1)S(1)}, u32[]{:S(2)}, u32[]{:S(2)}) collective-permute-start(bf16[128,512]{1,0:T(8,128)(2,1)S(1)} %get-tuple-element.92.refs_0_.refs_4_), channel_id=1, source_target_pairs={{0,12},{2,14},{4,8},{6,10},{8,4},{10,6},{12,0},{14,2},{16,28},{18,... | collective-permute-start | bytes 393224 | tf_op jit(solution)/shard_map/ppermute | solution.py:413
  31.8 3.4 %collective-permute-start.12 = (bf16[256,512]{1,0:T(8,128)(2,1)S(1)}, bf16[256,512]{1,0:T(8,128)(2,1)S(1)}, u32[]{:S(2)}, u32[]{:S(2)}) collective-permute-start(bf16[256,512]{1,0:T(8,128)(2,1)S(1)} %weight_other_core.3), channel_id=1, source_target_pairs={{0,2},{2,0},{4,6},{6,4},{8,10},{10,8},{12,14},{14,12},{16,18},{18,... | collective-permute-start | bytes 786440 | tf_op jit(solution)/shard_map/ppermute | solution.py:409
  35.6 1.9 %collective-permute-start.13 = (bf16[256,512]{1,0:T(8,128)(2,1)S(1)}, bf16[256,512]{1,0:T(8,128)(2,1)S(1)}, u32[]{:S(2)}, u32[]{:S(2)}) collective-permute-start(bf16[256,512]{1,0:T(8,128)(2,1)S(1)} %weight_other_core.4), channel_id=1, source_target_pairs={{0,2},{2,0},{4,6},{6,4},{8,10},{10,8},{12,14},{14,12},{16,18},{18,... | collective-permute-start | bytes 786440 | tf_op jit(solution)/shard_map/ppermute | solution.py:409
  35.7 6.4 %collective-permute-start.16 = (bf16[128,512]{1,0:T(8,128)(2,1)S(1)}, bf16[128,512]{1,0:T(8,128)(2,1)S(1)}, u32[]{:S(2)}, u32[]{:S(2)}) collective-permute-start(bf16[128,512]{1,0:T(8,128)(2,1)S(1)} %get-tuple-element.79), channel_id=1, source_target_pairs={{0,1},{1,0},{2,3},{3,2},{4,5},{5,4},{6,7},{7,6},{8,9},{9,8},{10,11... | collective-permute-start | bytes 393224 | tf_op jit(solution)/shard_map/ppermute | solution.py:401
  37.6 8.1 %collective-permute-start.14 = (bf16[128,512]{1,0:T(8,128)(2,1)S(1)}, bf16[128,512]{1,0:T(8,128)(2,1)S(1)}, u32[]{:S(2)}, u32[]{:S(2)}) collective-permute-start(bf16[128,512]{1,0:T(8,128)(2,1)S(1)} %get-tuple-element.85), channel_id=1, source_target_pairs={{0,1},{1,0},{2,3},{3,2},{4,5},{5,4},{6,7},{7,6},{8,9},{9,8},{10,11... | collective-permute-start | bytes 393224 | tf_op jit(solution)/shard_map/ppermute | solution.py:401
  42.0 11.5 %collective-permute-start.17 = (bf16[128,512]{1,0:T(8,128)(2,1)S(1)}, bf16[128,512]{1,0:T(8,128)(2,1)S(1)}, u32[]{:S(2)}, u32[]{:S(2)}) collective-permute-start(bf16[128,512]{1,0:T(8,128)(2,1)S(1)} %relay_total.3), channel_id=1, source_target_pairs={{0,16},{2,18},{4,20},{6,22},{8,24},{10,26},{12,28},{14,30},{16,0},... | collective-permute-start | bytes 393224 | tf_op jit(solution)/shard_map/ppermute | solution.py:406
  45.2 2.0 %collective-permute-start.15 = (bf16[256,1024]{1,0:T(8,128)(2,1)S(1)}, bf16[256,1024]{1,0:T(8,128)(2,1)S(1)}, u32[]{:S(2)}, u32[]{:S(2)}) collective-permute-start(bf16[256,1024]{1,0:T(8,128)(2,1)S(1)} %weight_other_core.5), channel_id=1, source_target_pairs={{0,2},{2,0},{4,6},{6,4},{8,10},{10,8},{12,14},{14,12},{16,18},{18,... | collective-permute-start | bytes 1572872 | tf_op jit(solution)/shard_map/ppermute | solution.py:409
  45.7 10.2 %collective-permute-start.19 = (bf16[128,512]{1,0:T(8,128)(2,1)S(1)}, bf16[128,512]{1,0:T(8,128)(2,1)S(1)}, u32[]{:S(2)}, u32[]{:S(2)}) collective-permute-start(bf16[128,512]{1,0:T(8,128)(2,1)S(1)} %relay_total.2), channel_id=1, source_target_pairs={{0,16},{2,18},{4,20},{6,22},{8,24},{10,26},{12,28},{14,30},{16,0},... | collective-permute-start | bytes 393224 | tf_op jit(solution)/shard_map/ppermute | solution.py:406
  47.2 8.7 %collective-permute-start.18 = (bf16[128,1024]{1,0:T(8,128)(2,1)S(1)}, bf16[128,1024]{1,0:T(8,128)(2,1)S(1)}, u32[]{:S(2)}, u32[]{:S(2)}) collective-permute-start(bf16[128,1024]{1,0:T(8,128)(2,1)S(1)} %get-tuple-element.100), channel_id=1, source_target_pairs={{0,1},{1,0},{2,3},{3,2},{4,5},{5,4},{6,7},{7,6},{8,9},{9,8},{10,11... | collective-permute-start | bytes 786440 | tf_op jit(solution)/shard_map/ppermute | solution.py:401

commit v12 on v11

--- a/solution.py
+++ b/solution.py
@@ -19,8 +19,8 @@
 ORDER = (0, 3, 2, 1)
 PARAMS = pltpu.CompilerParams(vmem_limit_bytes=32 * 2**20)
 COST = pl.CostEstimate(flops=1024, bytes_accessed=1024, transcendentals=0)
-NEAR_COST = pl.CostEstimate(flops=10**10, bytes_accessed=1024, transcendentals=0)
-KEY_COST = pl.CostEstimate(flops=2 * 10**9, bytes_accessed=1024, transcendentals=0)
+VISIT_COST = pl.CostEstimate(flops=5*10**9, bytes_accessed=1024, transcendentals=0)
+ADD_COST = pl.CostEstimate(flops=1*10**9, bytes_accessed=1024, transcendentals=0)
 EARLY = pl.CostEstimate(flops=10**10, bytes_accessed=1024, transcendentals=0)
 WHOLE = pl.BlockSpec(memory_space=pltpu.VMEM)
 FAR = pl.BlockSpec(memory_space=pltpu.HBM)
@@ -73,7 +73,9 @@
 
 
 def block_kernel(ctx_count, step, *refs):
-    lengths_ref, q_ref, do_ref, k_ref, v_ref, lse_ref, other_ref, ds_ref, grad_ref = refs[:9]
+    lengths_ref, q_ref, do_ref, k_ref, v_ref, lse_ref, other_ref, ds_ref = refs[:8]
+    same_ref, cross_ref = refs[8:10]
+    core = lax.rem(lax.axis_index("dp"), CORES)
     width = GROUP * HEAD_SIZE
     rank = lax.axis_index("ctx")
     owner = lax.rem(rank + ctx_count - step, ctx_count)
@@ -87,7 +89,7 @@
         group = slice(g * GROUP, (g + 1) * GROUP)
         if step == 1:
             delta = delta_rows(do_ref[:, wide], other_ref[:, wide])
-            refs[9][group, :] = delta
+            refs[10][group, :] = delta
         else:
             delta = other_ref[group, :]
         lse = lse_ref[group, :]
@@ -106,8 +108,10 @@
         probs_low = jnp.concatenate(probs_low, axis=1)
         grad_scores = jnp.concatenate(grad_scores, axis=1)
         ds_ref[:, g * GROUP * rows : (g + 1) * GROUP * rows] = grad_scores
-        grad_ref[0, :, columns] = (dot(grad_scores, q, NN) * SCALE).astype(grad_ref.dtype)
-        grad_ref[1, :, columns] = dot(probs_low, do, NN).astype(grad_ref.dtype)
+        key_grad = dot(grad_scores, q, NN) * SCALE
+        value_grad = dot(probs_low, do, NN)
+        same_ref[:, columns] = jnp.where(core == 0, key_grad, value_grad).astype(same_ref.dtype)
+        cross_ref[:, columns] = jnp.where(core == 0, value_grad, key_grad).astype(cross_ref.dtype)
 
 
 def block_call(step, ctx_count, lengths, queries, output_gradient, keys, values, lse, other):
@@ -115,7 +119,8 @@
     key_rows, half = keys.shape
     out_shape = [
         shape((key_rows, QUERY_HEADS * rows), jnp.bfloat16),
-        shape((2, key_rows, half), jnp.bfloat16 if step else jnp.float32),
+        shape((key_rows, half), jnp.bfloat16 if step else jnp.float32),
+        shape((key_rows, half), jnp.bfloat16),
     ]
     if step == 1:
         out_shape.append(shape((QUERY_HEADS, rows), jnp.float32))
@@ -125,7 +130,7 @@
         out_specs=[WHOLE] * len(out_shape),
         out_shape=out_shape,
         compiler_params=PARAMS,
-        cost_estimate=COST,
+        cost_estimate=VISIT_COST if step else COST,
         name="visiting_keys" if step else "own_keys",
     )(lengths, queries, output_gradient, keys, values, lse, other)
 
@@ -230,85 +235,107 @@
     )(*pieces)
 
 
-def add_kernel(own_ref, *refs):
-    for part, out_ref in enumerate(refs[-2:]):
-        total = own_ref[part]
-        for back_ref in refs[:-2]:
-            total = total + back_ref[part].astype(jnp.float32)
+def add_kernel(count, *refs):
+    same_ref, cross_ref = refs[-2:]
+    for ref, out_ref in ((refs[:count], same_ref), (refs[count:-2], cross_ref)):
+        total = ref[0][...].astype(jnp.float32)
+        for value in ref[1:]:
+            total = total + value[...].astype(jnp.float32)
         out_ref[...] = total.astype(out_ref.dtype)
 
 
-def add_call(own, back):
-    return pl.pallas_call(
-        add_kernel,
-        in_specs=[WHOLE] * (1 + len(back)),
+def add_call(same, cross):
+    dims = same[0].shape
+    return pl.pallas_call(
+        functools.partial(add_kernel, len(same)),
+        in_specs=[WHOLE] * (len(same) + len(cross)),
         out_specs=[WHOLE] * 2,
-        out_shape=[shape(own.shape[1:], jnp.bfloat16)] * 2,
+        out_shape=[shape(dims, jnp.bfloat16), shape(dims, jnp.float32)],
+        compiler_params=PARAMS,
+        cost_estimate=ADD_COST,
+        name="returned_grads",
+    )(*same, *cross)
+
+
+def total_kernel(same_ref, cross_ref, sibling_ref, out_ref):
+    rows = same_ref.shape[0]
+    out_ref[:rows, :] = same_ref[...]
+    out_ref[rows:, :] = (cross_ref[...] + sibling_ref[...].astype(jnp.float32)).astype(
+        out_ref.dtype
+    )
+
+
+def total_call(same, cross, sibling):
+    rows, width = same.shape
+    return pl.pallas_call(
+        total_kernel,
+        in_specs=[WHOLE] * 3,
+        out_specs=WHOLE,
+        out_shape=shape((2 * rows, width), jnp.bfloat16),
         compiler_params=PARAMS,
         cost_estimate=COST,
         name="grads_total",
-    )(own, *back)
-
-
-def weight_kernel(other, steps, far, counts, tokens_ref, *refs):
-    g_refs, out_ref = refs[:-1], refs[-1]
-    block = out_ref.shape[0] // len(steps)
+    )(same, cross, sibling)
+
+
+def stack_kernel(*refs):
+    own_ref, sibling_ref = refs[-2:]
+    rows = refs[0].shape[0] // 2
+    for at, ref in enumerate(refs[:-2]):
+        here = slice(at * rows, (at + 1) * rows)
+        own_ref[here, :] = ref[:rows, :]
+        sibling_ref[here, :] = ref[rows:, :]
+
+
+def stack_call(grads):
+    height, width = grads[0].shape
+    return pl.pallas_call(
+        stack_kernel,
+        in_specs=[WHOLE] * len(grads),
+        out_specs=[WHOLE] * 2,
+        out_shape=[shape((height // 2 * len(grads), width), grads[0].dtype)] * 2,
+        compiler_params=PARAMS,
+        cost_estimate=EARLY,
+        name="stack_grads",
+    )(*grads)
+
+
+def weight_kernel(core_steps, z_steps, far, ctx_count, *refs):
+    own_ref, sibling_ref, own_grads, sibling_grads = refs[:4]
+    out_refs, buf = refs[4:-1], refs[-1]
+    block = out_refs[0].shape[0] // len(z_steps)
     dp_rank = lax.axis_index("dp")
-    core = lax.rem(dp_rank, CORES)
+    x_rank = lax.axis_index("ctx")
+    core = lax.rem(dp_rank + core_steps, CORES)
     z_rank = lax.div(dp_rank, CORES * MIDDLE * NEAR)
-    if other:
-        core = 1 - core
-    grads = []
-    for count in counts:
-        grads.append(jnp.concatenate([g[...] for g in g_refs[:count]], axis=0))
-        g_refs = g_refs[count:]
-    for at, step in enumerate(steps):
-        start = (core * far + lax.rem(z_rank + step, far)) * block
-        tokens = tokens_ref[pl.ds(pl.multiple_of(start, block), block), :]
-        for part, value in enumerate(grads):
-            width = value.shape[1]
-            out_ref[at * block : (at + 1) * block, part * width : (part + 1) * width] = dot(
-                tokens, value, NN
-            ).astype(out_ref.dtype)
-
-
-def weight_call(other, steps, far, tokens, grads, dtype, cost):
-    operands = [value for part in grads for value in part]
-    height = tokens.shape[0] // (CORES * far) * len(steps)
-    return pl.pallas_call(
-        functools.partial(weight_kernel, other, steps, far, tuple(len(part) for part in grads)),
-        in_specs=[WHOLE] * (1 + len(operands)),
-        out_specs=WHOLE,
-        out_shape=shape((height, sum(part[0].shape[1] for part in grads)), dtype),
-        compiler_params=PARAMS,
-        cost_estimate=cost,
-        name="weight_other_core" if other else "weight_this_core",
-    )(tokens, *operands)
-
-
-def chip_kernel(ctx_count, count, mine_ref, theirs_ref, *out_refs):
-    block = out_refs[0].shape[0] // count
-    x_rank = lax.axis_index("ctx")
-    for x, out_ref in enumerate(out_refs):
-        for z in range(count):
-            start = (z * ctx_count + lax.rem(x_rank + x, ctx_count)) * block
-            at = pl.ds(pl.multiple_of(start, block), block)
-            total = mine_ref[at, :] + theirs_ref[at, :].astype(jnp.float32)
-            out_ref[z * block : (z + 1) * block, :] = total.astype(out_ref.dtype)
-
-
-def chip_call(ctx_count, count, mine, theirs):
-    height, columns = mine.shape
-    dims = (height // ctx_count, columns)
-    return pl.pallas_call(
-        functools.partial(chip_kernel, ctx_count, count),
-        in_specs=[WHOLE] * 2,
+    size = ctx_count * block
+    for at, step in enumerate(z_steps):
+        start = (core * far + lax.rem(z_rank + step, far)) * size
+        here = pl.ds(pl.multiple_of(start, size), size)
+        buf[...] = dot(own_ref[here, :], own_grads[...], NN) + dot(
+            sibling_ref[here, :], sibling_grads[...], NN
+        )
+        for x, out_ref in enumerate(out_refs):
+            start = lax.rem(x_rank + x, ctx_count) * block
+            out_ref[at * block : (at + 1) * block, :] = buf[
+                pl.ds(pl.multiple_of(start, block), block), :
+            ].astype(out_ref.dtype)
+
+
+def weight_call(core_steps, z_steps, far, ctx_count, tokens, grads, kept):
+    height = tokens[0].shape[0] // (CORES * far)
+    width = grads[0].shape[1]
+    dims = (height // ctx_count * len(z_steps), width)
+    return pl.pallas_call(
+        functools.partial(weight_kernel, core_steps, z_steps, far, ctx_count),
+        in_specs=[WHOLE] * 4,
         out_specs=[WHOLE] * ctx_count,
-        out_shape=[shape(dims, jnp.float32)] + [shape(dims, jnp.bfloat16)] * (ctx_count - 1),
-        compiler_params=PARAMS,
-        cost_estimate=COST,
-        name="chip_total",
-    )(mine, theirs)
+        out_shape=[shape(dims, kept)] + [shape(dims, jnp.bfloat16)] * (ctx_count - 1),
+        scratch_shapes=[pltpu.VMEM((height, width), jnp.float32)],
+        compiler_params=PARAMS,
+        cost_estimate=COST,
+        name="weight_far" if z_steps[0] else "weight_near",
+    )(*tokens, *grads)
 
 
 def relay_kernel(count, away_ref, *refs):
@@ -350,35 +377,33 @@
         out_shape=shape(arrived[0].shape, jnp.float32),
         compiler_params=PARAMS,
         cost_estimate=EARLY,
-        name="key_far_total",
+        name="early_total",
     )(*arrived)
 
 
-def final_kernel(near_count, own_ref, key_far_ref, *refs):
+def final_kernel(count, *refs):
     key_ref, value_ref = refs[-2:]
-    near_refs, value_refs = refs[:near_count], refs[near_count:-2]
-    half = key_ref.shape[1]
-    key = own_ref[:, :half] + key_far_ref[...]
-    value = own_ref[:, half:]
-    for ref in near_refs:
-        key = key + ref[:, :half].astype(jnp.float32)
-        value = value + ref[:, half:].astype(jnp.float32)
-    for ref in value_refs:
-        value = value + ref[...].astype(jnp.float32)
-    key_ref[...] = key
-    value_ref[...] = value
-
-
-def final_call(own, key_far, near, values):
-    return pl.pallas_call(
-        functools.partial(final_kernel, len(near)),
-        in_specs=[WHOLE] * (2 + len(near) + len(values)),
+    core = lax.rem(lax.axis_index("dp"), CORES)
+    totals = []
+    for part in (refs[:count], refs[count:-2]):
+        total = part[0][...].astype(jnp.float32)
+        for ref in part[1:]:
+            total = total + ref[...].astype(jnp.float32)
+        totals.append(total)
+    key_ref[...] = jnp.where(core == 0, totals[0], totals[1])
+    value_ref[...] = jnp.where(core == 0, totals[1], totals[0])
+
+
+def final_call(same, cross):
+    return pl.pallas_call(
+        functools.partial(final_kernel, len(same)),
+        in_specs=[WHOLE] * (len(same) + len(cross)),
         out_specs=[WHOLE] * 2,
-        out_shape=[shape(key_far.shape, jnp.float32)] * 2,
+        out_shape=[shape(same[0].shape, jnp.float32)] * 2,
         compiler_params=PARAMS,
         cost_estimate=COST,
         name="weight_total",
-    )(own, key_far, *near, *values)
+    )(*same, *cross)
 
 
 def local(
@@ -396,27 +421,20 @@
     dp_count = lax.axis_size("dp")
     far = dp_count // (CORES * MIDDLE * NEAR)
 
-    def over_ctx(value, steps):
-        pairs = [(s, (s + steps) % ctx_count) for s in range(ctx_count)]
-        return lax.ppermute(value, "ctx", pairs)
-
-    def over_far(value, steps):
-        stride = dp_count // far
-        pairs = [(s, (s + steps * stride) % dp_count) for s in range(dp_count)]
-        return lax.ppermute(value, "dp", pairs)
-
-    def over_cores(value):
-        return lax.ppermute(value, "dp", [(s, s ^ 1) for s in range(dp_count)])
-
-    def over_group(value, index):
-        flip = index // NEAR * CORES + index % NEAR * CORES * MIDDLE
-        return lax.ppermute(value, "dp", [(s, s ^ flip) for s in range(dp_count)])
+    def send(value, x_steps=0, core_steps=0, far_steps=0, member=0):
+        flip = core_steps + member // NEAR * CORES + member % NEAR * CORES * MIDDLE
+        pairs = []
+        for d in range(dp_count):
+            to = ((d ^ flip) + far_steps * CORES * MIDDLE * NEAR) % dp_count
+            for x in range(ctx_count):
+                pairs.append((d * ctx_count + x, to * ctx_count + (x + x_steps) % ctx_count))
+        return lax.ppermute(value, ("dp", "ctx"), pairs)
 
     visiting = [
-        (over_ctx(saved_keys, step), over_ctx(saved_values, step)) for step in range(1, ctx_count)
+        (send(saved_keys, step), send(saved_values, step)) for step in range(1, ctx_count)
     ]
     *pieces, other, lse = pieces_call(normed_input, (attention_output, saved_log_totals.T), far)
-    pieces = [over_group(piece, index) if index else piece for index, piece in enumerate(pieces)]
+    pieces = [send(piece, member=i) if i else piece for i, piece in enumerate(pieces)]
     block = functools.partial(
         block_call,
         ctx_count=ctx_count,
@@ -425,50 +443,49 @@
         output_gradient=output_gradient,
         lse=lse,
     )
-    scores, back = [], []
+    scores, same, cross = [], [], []
     for step in range(1, ctx_count):
         keys, values = visiting[step - 1]
-        part_scores, grads, *delta = block(step, keys=keys, values=values, other=other)
+        part_scores, same_grads, cross_grads, *delta = block(
+            step, keys=keys, values=values, other=other
+        )
         other = delta[0] if delta else other
         scores.append(part_scores)
-        back.append(over_ctx(grads, -step))
-    other = after(other, grads)
-    own_scores, own = block(0, keys=saved_keys, values=saved_values, other=other)
-    back, pieces = lax.optimization_barrier((back, pieces))
-    totals = add_call(own, back)
-    grads = [[over_group(total, i) if i else total for i in ORDER] for total in totals]
-    tokens = turn_call(after([pieces[i] for i in ORDER], totals))
-
-    def chip_sums(steps, grads, cost):
-        theirs = weight_call(True, steps, far, tokens, grads, jnp.bfloat16, COST)
-        arriving = over_cores(theirs)
-        if cost is KEY_COST:
-            grads = after(grads, values_there)
-        mine = weight_call(False, steps, far, tokens, grads, jnp.float32, cost)
-        return chip_call(ctx_count, len(steps), mine, arriving)
-
-    values_there = grads[1]
+        same.append(send(same_grads, -step))
+        cross.append(send(cross_grads, -step, 1))
+    other = after(other, same_grads)
+    own_scores, own_same, own_cross = block(0, keys=saved_keys, values=saved_values, other=other)
+    own_cross, pieces[1] = lax.optimization_barrier((own_cross, pieces[1]))
+    sibling = send(own_cross, core_steps=1)
+    same, pieces = lax.optimization_barrier((same, pieces))
+    total = total_call(*add_call([own_same] + same, cross), sibling)
+    grads = [send(total, member=i) if i else total for i in ORDER]
+    tokens = turn_call(after([pieces[i] for i in ORDER], total))
+    grads = stack_call(grads)
+    tokens = [tokens, after(send(tokens, core_steps=1), grads)]
+    weights = functools.partial(
+        weight_call, far=far, ctx_count=ctx_count, tokens=tokens, kept=jnp.float32
+    )
     steps = tuple(range(1, far))
-    away, arrived, from_far, blocks = [], [], [], []
-    for part in range(2):
-        part_grads = after(grads[part], blocks) if part else grads[0]
-        sums, *blocks = chip_sums(steps, [part_grads], COST if part else KEY_COST)
-        away.append(sums)
-        arrived.append([over_ctx(value, s) for s, value in enumerate(blocks, 1)])
-    own_block, *near = chip_sums((0,), after(grads, blocks), NEAR_COST)
-    arrived[0] = after(arrived[0], blocks)
-    for part in range(2):
-        relayed = relay_call(far - 1, away[part], arrived[part])
-        from_far.append([over_far(value, s) for s, value in enumerate(relayed, 1)])
-    own_scores = after(own_scores, relayed)
+    away, arrived, from_far = [], [], []
+    for core in range(CORES):
+        kept, *blocks = weights(core, steps, grads=grads)
+        grads = after(grads, kept)
+        away.append(kept)
+        arrived.append([send(value, s) for s, value in enumerate(blocks, 1)])
+    own_block, *near = weights(0, (0,), grads=grads)
+    cross_block, *cross_near = weights(1, (0,), grads=grads, kept=jnp.bfloat16)
+    for core in range(CORES):
+        relayed = relay_call(far - 1, away[core], arrived[core])
+        from_far.append([send(value, 0, core, s) for s, value in enumerate(relayed, 1)])
+    near, cross_near, own_scores = after((near, cross_near, own_scores), relayed)
+    same = [own_block, early_call(from_far[0])] + [send(v, s) for s, v in enumerate(near, 1)]
+    cross = [send(cross_block, core_steps=1)] + from_far[1]
+    cross += [send(value, s, 1) for s, value in enumerate(cross_near, 1)]
     query_gradient = query_call(
         [own_scores] + scores, [saved_keys] + [pair[0] for pair in visiting], rows
     )
-    near = after(near, relayed)
-    near = [over_ctx(value, s) for s, value in enumerate(near, 1)]
-    key_weight_grad, value_weight_grad = final_call(
-        own_block, early_call(from_far[0]), near, from_far[1]
-    )
+    key_weight_grad, value_weight_grad = final_call(same, cross)
     return query_gradient, key_weight_grad, value_weight_grad
 
 

time: 57 us -> 56.9 us (level)
  waiting for transfers between devices: 17.2 us -> 23.9 us
  starting transfers between devices: 26 us -> 19.5 us
    ppermute x20 -> x19, waiting for transfers between devices: 17.2 us -> 23.9 us  [send(): return lax.ppermute(value, ('dp', 'ctx'), pairs)]
    ppermute x20 -> x19, starting transfers between devices: 26 us -> 19.5 us  [send(): return lax.ppermute(value, ('dp', 'ctx'), pairs)]
    pallas_call x11 -> x8, Pallas kernels: 3.13 us -> 2.97 us  [the longest x4 1.95 us: weight_call(): pl.pallas_call(functools.partial(weight_kernel, core_steps, z_steps, far,...]
  transfers between devices with their start and end apart: 20 -> 19, of which waited for: 12 -> 11; matrix products, arithmetic and copies ran while one was open for 0% -> 0% of each run, Pallas kernels for 20% -> 20%
where the time goes in v12:
time: 56.9 us; the launch traced here: 56.8 us
  waiting for transfers between devices  23.9 us (42%)
  starting transfers between devices  19.5 us (34%)
  Pallas kernels  12.5 us (22%)
  between operations  0.8 us (1%)
    ppermute x19, waiting for transfers between devices, send(): return lax.ppermute(value, ('dp', 'ctx'), pairs)  23.9 us
    ppermute x19, starting transfers between devices, send(): return lax.ppermute(value, ('dp', 'ctx'), pairs)  19.5 us
    pallas_call x2, Pallas kernels, block_call(): pl.pallas_call(functools.partial(block_kernel, ctx_count, step), in_specs...  5.5 us
    pallas_call x4, Pallas kernels, weight_call(): pl.pallas_call(functools.partial(weight_kernel, core_steps, z_steps, far,...  1.95 us
    pallas_call x1, Pallas kernels, pieces_call(): pl.pallas_call(functools.partial(pieces_kernel, far, len(wanted)), in_spe...  1.94 us
    pallas_call x1, Pallas kernels, query_call(): pl.pallas_call(functools.partial(query_kernel, len(keys)), in_specs=[WHOL...  1.73 us
  transfers between devices with their start and end apart: 19, of which 11 were waited for; matrix products, arithmetic and copies ran while one was open for 0% of the time, Pallas kernels for 20%

profile of v12, /device:TPU:0, one launch (start us, length us, event | category | flops | bytes accessed | tf_op | source)
XLA Modules:
  0.0 56.8 jit_solution(860805450543754059)
XLA Ops:
  0.6 3.0 %collective-permute-start = (bf16[128,512]{1,0:T(8,128)(2,1)}, bf16[128,512]{1,0:T(8,128)(2,1)S(1)}, u32[]{:S(2)}, u32[]{:S(2)}) collective-permute-start(bf16[128,512]{1,0:T(8,128)(2,1)} %refs_2_.5), channel_id=1, source_target_pairs={{0,1},{1,0},{2,3},{3,2},{4,5},{5,4},{6,7},{7,6},{8,9},{9,8},{10,11... | collective-permute-start | bytes 393224 | tf_op jit(solution)/shard_map/ppermute | solution.py:431
  3.6 0.1 collective-permute-start.1
  3.7 1.9 %pieces.1 = (bf16[128,1024]{1,0:T(8,128)(2,1)S(1)}, bf16[128,1024]{1,0:T(8,128)(2,1)S(1)}, bf16[128,1024]{1,0:T(8,128)(2,1)S(1)}, bf16[128,1024]{1,0:T(8,128)(2,...) custom-call(bf16[128,4096]{1,0:T(8,128)(2,1)} %in_hbm.1, bf16[128,4096]{1,0:T(8,128)(2,1)} %refs_0_.3, ...), custom_call_target="tpu_custom_call" | custom-call | flops 1024 | bytes 1024 | tf_op jit(solution)/shard_map/pieces/pallas_call | solution.py:202
  5.7 2.1 %collective-permute-start.3 = (bf16[128,1024]{1,0:T(8,128)(2,1)S(1)}, bf16[128,1024]{1,0:T(8,128)(2,1)S(1)}, u32[]{:S(2)}, u32[]{:S(2)}) collective-permute-start(bf16[128,1024]{1,0:T(8,128)(2,1)S(1)} %get-tuple-element.57), channel_id=1, source_target_pairs={{0,8},{1,9},{2,10},{3,11},{4,12},{5,13},{6,14},{7,15},{8,0},{9,1},... | collective-permute-start | bytes 786440 | tf_op jit(solution)/shard_map/ppermute | solution.py:431
  7.8 1.5 %collective-permute-start.4 = (bf16[128,1024]{1,0:T(8,128)(2,1)S(1)}, bf16[128,1024]{1,0:T(8,128)(2,1)S(1)}, u32[]{:S(2)}, u32[]{:S(2)}) collective-permute-start(bf16[128,1024]{1,0:T(8,128)(2,1)S(1)} %get-tuple-element.59), channel_id=1, source_target_pairs={{0,4},{1,5},{2,6},{3,7},{4,0},{5,1},{6,2},{7,3},{8,12},{9,13},{10,... | collective-permute-start | bytes 786440 | tf_op jit(solution)/shard_map/ppermute | solution.py:431
  9.3 0.0 collective-permute-start.5
  9.3 0.0 collective-permute-done.refs_3_
  9.3 0.8 %collective-permute-done.1.refs_4_ = bf16[128,512]{1,0:T(8,128)(2,1)S(1)} collective-permute-done((bf16[128,512]{1,0:T(8,128)(2,1)}, bf16[128,512]{1,0:T(8,128)(2,1)S(1)}, u32[]{:S(2)}, u32[]{:S(2)}) %collective-permute-start.1) | collective-permute-done | bytes 131104 | tf_op jit(solution)/shard_map/ppermute | solution.py:431
  10.2 3.1 %visiting_keys.1 = (bf16[128,4096]{1,0:T(8,128)(2,1)S(1)}, bf16[128,512]{1,0:T(8,128)(2,1)S(1)}, bf16[128,512]{1,0:T(8,128)(2,1)S(1)}, f32[32,128]{1,0:T(8,128)S(1)}) custom-call(s32[1,4]{1,0:T(1,128)} %refs_0_.5, bf16[128,4096]{1,0:T(8,128)(2,1)S(1)} %copy-done, bf16[128,4096]{1,0:T(8,128)(2,1)S(1)} %copy-done.1, ...), custom_call_target="tpu_custom_call" | custom-call | flops 5000000000 | bytes 1024 | tf_op jit(solution)/shard_map/visiting_keys/pallas_call | solution.py:127
  13.3 1.8 %collective-permute-start.2 = (bf16[128,512]{1,0:T(8,128)(2,1)S(1)}, bf16[128,512]{1,0:T(8,128)(2,1)S(1)}, u32[]{:S(2)}, u32[]{:S(2)}) collective-permute-start(bf16[128,512]{1,0:T(8,128)(2,1)S(1)} %get-tuple-element.52), channel_id=1, source_target_pairs={{0,1},{1,0},{2,3},{3,2},{4,5},{5,4},{6,7},{7,6},{8,9},{9,8},{10,11... | collective-permute-start | bytes 393224 | tf_op jit(solution)/shard_map/ppermute | solution.py:431
  15.1 0.0 collective-permute-start.6
  15.1 2.4 %own_keys.1 = (bf16[128,4096]{1,0:T(8,128)(2,1)S(1)}, f32[128,512]{1,0:T(8,128)S(1)}, bf16[128,512]{1,0:T(8,128)(2,1)S(1)}) custom-call(s32[1,4]{1,0:T(1,128)} %refs_0_.5, bf16[128,4096]{1,0:T(8,128)(2,1)S(1)} %copy-done, bf16[128,4096]{1,0:T(8,128)(2,1)S(1)} %copy-done.1, bf16[128,512]{1,0:T(8,128)(2,1)S(1)} %copy-done.2, bf16[128,512]{1,0:T(8,128)(2,1)S(1)} %copy-done.3, ...), custom_call_target="tpu_custom_call" | custom-call | flops 1024 | bytes 1024 | tf_op jit(solution)/shard_map/own_keys/pallas_call | solution.py:127
  17.5 0.0 collective-permute-done.3.refs_3_
  17.5 0.5 collective-permute-start.7
  18.0 0.7 %collective-permute-done.2.refs_1_ = bf16[128,512]{1,0:T(8,128)(2,1)S(1)} collective-permute-done((bf16[128,512]{1,0:T(8,128)(2,1)S(1)}, bf16[128,512]{1,0:T(8,128)(2,1)S(1)}, u32[]{:S(2)}, u32[]{:S(2)}) %collective-permute-start.2) | collective-permute-done | bytes 131104 | tf_op jit(solution)/shard_map/ppermute | solution.py:431
  18.7 1.9 %collective-permute-done.4.refs_2_ = bf16[128,1024]{1,0:T(8,128)(2,1)S(1)} collective-permute-done((bf16[128,1024]{1,0:T(8,128)(2,1)S(1)}, bf16[128,1024]{1,0:T(8,128)(2,1)S(1)}, u32[]{:S(2)}, u32[]{:S(2)}) %collective-permute-start.4) | collective-permute-done | bytes 262176 | tf_op jit(solution)/shard_map/ppermute | solution.py:431
  20.6 0.0 collective-permute-done.5.refs_1_
  20.6 0.4 collective-permute-done.6.refs_2_
  21.0 0.0 collective-permute-done.7.sibling_ref
  21.0 1.5 %collective-permute-start.10 = (bf16[256,512]{1,0:T(8,128)(2,1)S(1)}, bf16[256,512]{1,0:T(8,128)(2,1)S(1)}, u32[]{:S(2)}, u32[]{:S(2)}) collective-permute-start(bf16[256,512]{1,0:T(8,128)(2,1)S(1)} %grads_total.1.refs_0_), channel_id=1, source_target_pairs={{0,4},{1,5},{2,6},{3,7},{4,0},{5,1},{6,2},{7,3},{8,12},{9,13},{10,... | collective-permute-start | bytes 786440 | tf_op jit(solution)/shard_map/ppermute | solution.py:431
  22.6 1.6 %collective-permute-start.11 = (bf16[256,512]{1,0:T(8,128)(2,1)S(1)}, bf16[256,512]{1,0:T(8,128)(2,1)S(1)}, u32[]{:S(2)}, u32[]{:S(2)}) collective-permute-start(bf16[256,512]{1,0:T(8,128)(2,1)S(1)} %grads_total.1.refs_0_), channel_id=1, source_target_pairs={{0,8},{1,9},{2,10},{3,11},{4,12},{5,13},{6,14},{7,15},{8,0},{9,1},... | collective-permute-start | bytes 786440 | tf_op jit(solution)/shard_map/ppermute | solution.py:431
  24.2 0.4 collective-permute-start.9
  24.6 0.3 turn_pieces.1.refs_0_
  24.9 0.1 collective-permute-start.8
  25.0 4.4 %collective-permute-done.10.refs_2_ = bf16[256,512]{1,0:T(8,128)(2,1)S(1)} collective-permute-done((bf16[256,512]{1,0:T(8,128)(2,1)S(1)}, bf16[256,512]{1,0:T(8,128)(2,1)S(1)}, u32[]{:S(2)}, u32[]{:S(2)}) %collective-permute-start.10) | collective-permute-done | bytes 262176 | tf_op jit(solution)/shard_map/ppermute | solution.py:431
  29.4 2.3 %collective-permute-done.11.refs_3_ = bf16[256,512]{1,0:T(8,128)(2,1)S(1)} collective-permute-done((bf16[256,512]{1,0:T(8,128)(2,1)S(1)}, bf16[256,512]{1,0:T(8,128)(2,1)S(1)}, u32[]{:S(2)}, u32[]{:S(2)}) %collective-permute-start.11) | collective-permute-done | bytes 262176 | tf_op jit(solution)/shard_map/ppermute | solution.py:431
  31.8 4.5 %collective-permute-done.9.refs_1_ = bf16[256,512]{1,0:T(8,128)(2,1)S(1)} collective-permute-done((bf16[256,512]{1,0:T(8,128)(2,1)S(1)}, bf16[256,512]{1,0:T(8,128)(2,1)S(1)}, u32[]{:S(2)}, u32[]{:S(2)}) %collective-permute-start.9) | collective-permute-done | bytes 262176 | tf_op jit(solution)/shard_map/ppermute | solution.py:431
  36.3 0.1 stack_grads.1
  36.3 0.0 collective-permute-done.8.refs_1_
  36.3 0.5 weight_far.2
  36.8 1.5 %collective-permute-start.13 = (bf16[128,512]{1,0:T(8,128)(2,1)S(1)}, bf16[128,512]{1,0:T(8,128)(2,1)S(1)}, u32[]{:S(2)}, u32[]{:S(2)}) collective-permute-start(bf16[128,512]{1,0:T(8,128)(2,1)S(1)} %get-tuple-element.91), channel_id=1, source_target_pairs={{0,1},{1,0},{2,3},{3,2},{4,5},{5,4},{6,7},{7,6},{8,9},{9,8},{10,11... | collective-permute-start | bytes 393224 | tf_op jit(solution)/shard_map/ppermute | solution.py:431
  38.4 0.5 weight_far.3
  38.9 0.6 %collective-permute-start.12 = (bf16[128,512]{1,0:T(8,128)(2,1)S(1)}, bf16[128,512]{1,0:T(8,128)(2,1)S(1)}, u32[]{:S(2)}, u32[]{:S(2)}) collective-permute-start(bf16[128,512]{1,0:T(8,128)(2,1)S(1)} %get-tuple-element.87), channel_id=1, source_target_pairs={{0,1},{1,0},{2,3},{3,2},{4,5},{5,4},{6,7},{7,6},{8,9},{9,8},{10,11... | collective-permute-start | bytes 393224 | tf_op jit(solution)/shard_map/ppermute | solution.py:431
  39.5 3.7 %collective-permute-done.13.refs_0_ = bf16[128,512]{1,0:T(8,128)(2,1)S(1)} collective-permute-done((bf16[128,512]{1,0:T(8,128)(2,1)S(1)}, bf16[128,512]{1,0:T(8,128)(2,1)S(1)}, u32[]{:S(2)}, u32[]{:S(2)}) %collective-permute-start.13) | collective-permute-done | bytes 131104 | tf_op jit(solution)/shard_map/ppermute | solution.py:431
  43.2 2.7 %collective-permute-start.14 = (bf16[128,512]{1,0:T(8,128)(2,1)S(1)}, bf16[128,512]{1,0:T(8,128)(2,1)S(1)}, u32[]{:S(2)}, u32[]{:S(2)}) collective-permute-start(bf16[128,512]{1,0:T(8,128)(2,1)S(1)} %relay_total.3), channel_id=1, source_target_pairs={{0,16},{1,17},{2,18},{3,19},{4,20},{5,21},{6,22},{7,23},{8,24},{9,... | collective-permute-start | bytes 393224 | tf_op jit(solution)/shard_map/ppermute | solution.py:431
  45.8 0.5 weight_near.3
  46.3 0.5 weight_near.2
  46.8 0.1 collective-permute-start.16
  46.9 0.0 collective-permute-done.12.refs_0_
  46.9 0.5 collective-permute-start.17
  47.4 1.4 %collective-permute-start.15 = (bf16[128,512]{1,0:T(8,128)(2,1)S(1)}, bf16[128,512]{1,0:T(8,128)(2,1)S(1)}, u32[]{:S(2)}, u32[]{:S(2)}) collective-permute-start(bf16[128,512]{1,0:T(8,128)(2,1)S(1)} %get-tuple-element.92), channel_id=1, source_target_pairs={{0,1},{1,0},{2,3},{3,2},{4,5},{5,4},{6,7},{7,6},{8,9},{9,8},{10,11... | collective-permute-start | bytes 393224 | tf_op jit(solution)/shard_map/ppermute | solution.py:431
  48.8 0.2 collective-permute-start.18
  49.0 1.7 %query_gradient.1 = bf16[128,4096]{1,0:T(8,128)(2,1)} custom-call(bf16[128,4096]{1,0:T(8,128)(2,1)S(1)} %get-tuple-element.88.refs_0_, bf16[128,4096]{1,0:T(8,128)(2,1)S(1)} %get-tuple-element.89.refs_1_, bf16[128,512]{1,0:T(8,128)(2,1)S(1)} %copy-done.2, bf16[128,512]{1,0:T(8,128)(2,1)S(1)} %collective-permute-done.refs_3_), custom_call_target="tpu_custom_call" | custom-call | flops 1024 | bytes 1024 | tf_op jit(solution)/shard_map/query_gradient/pallas_call | solution.py:154
  50.7 0.0 collective-permute-done.14.refs_0_
  50.7 3.0 %collective-permute-done.15.refs_2_ = bf16[128,512]{1,0:T(8,128)(2,1)S(1)} collective-permute-done((bf16[128,512]{1,0:T(8,128)(2,1)S(1)}, bf16[128,512]{1,0:T(8,128)(2,1)S(1)}, u32[]{:S(2)}, u32[]{:S(2)}) %collective-permute-start.15) | collective-permute-done | bytes 131104 | tf_op jit(solution)/shard_map/ppermute | solution.py:431
  53.8 1.3 %collective-permute-done.18.refs_5_ = bf16[128,512]{1,0:T(8,128)(2,1)S(1)} collective-permute-done((bf16[128,512]{1,0:T(8,128)(2,1)S(1)}, bf16[128,512]{1,0:T(8,128)(2,1)S(1)}, u32[]{:S(2)}, u32[]{:S(2)}) %collective-permute-start.18) | collective-permute-done | bytes 131104 | tf_op jit(solution)/shard_map/ppermute | solution.py:431
  55.1 0.8 %collective-permute-done.17.refs_4_ = bf16[128,512]{1,0:T(8,128)(2,1)S(1)} collective-permute-done((bf16[128,512]{1,0:T(8,128)(2,1)S(1)}, bf16[128,512]{1,0:T(8,128)(2,1)S(1)}, u32[]{:S(2)}, u32[]{:S(2)}) %collective-permute-start.17) | collective-permute-done | bytes 131104 | tf_op jit(solution)/shard_map/ppermute | solution.py:431
  55.9 0.9 %weight_total.1 = (f32[128,512]{1,0:T(8,128)}, f32[128,512]{1,0:T(8,128)}) custom-call(f32[128,512]{1,0:T(8,128)S(1)} %get-tuple-element.90.refs_0_, f32[128,512]{1,0:T(8,128)S(1)} %early_total.1.refs_1_, bf16[128,512]{1,0:T(8,128)(2,1)S(1)} %collective-permute-done.15.refs_2_, bf16[128,512]{1,0:T(8,128)(2,1)S(1)} %collective-permute-done.16.refs_3_, ...), custom_call_target="tpu_custom_call" | custom-call | flops 1024 | bytes 1024 | tf_op jit(solution)/shard_map/weight_total/pallas_call | solution.py:398
  (14 shorter events, 0.2 us)
Async XLA Ops:
  0.6 8.7 %collective-permute-start = (bf16[128,512]{1,0:T(8,128)(2,1)}, bf16[128,512]{1,0:T(8,128)(2,1)S(1)}, u32[]{:S(2)}, u32[]{:S(2)}) collective-permute-start(bf16[128,512]{1,0:T(8,128)(2,1)} %refs_2_.5), channel_id=1, source_target_pairs={{0,1},{1,0},{2,3},{3,2},{4,5},{5,4},{6,7},{7,6},{8,9},{9,8},{10,11... | collective-permute-start | bytes 393224 | tf_op jit(solution)/shard_map/ppermute | solution.py:431
  3.6 6.5 %collective-permute-start.1 = (bf16[128,512]{1,0:T(8,128)(2,1)}, bf16[128,512]{1,0:T(8,128)(2,1)S(1)}, u32[]{:S(2)}, u32[]{:S(2)}) collective-permute-start(bf16[128,512]{1,0:T(8,128)(2,1)} %refs_4_.1), channel_id=1, source_target_pairs={{0,1},{1,0},{2,3},{3,2},{4,5},{5,4},{6,7},{7,6},{8,9},{9,8},{10,11... | collective-permute-start | bytes 393224 | tf_op jit(solution)/shard_map/ppermute | solution.py:431
  3.7 6.4 %copy-start = (bf16[128,4096]{1,0:T(8,128)(2,1)S(1)}, bf16[128,4096]{1,0:T(8,128)(2,1)}, u32[]{:S(2)}) copy-start(bf16[128,4096]{1,0:T(8,128)(2,1)} %refs_1_.3) | copy-start | bytes 3145732
  3.7 6.4 %copy-start.1 = (bf16[128,4096]{1,0:T(8,128)(2,1)S(1)}, bf16[128,4096]{1,0:T(8,128)(2,1)}, u32[]{:S(2)}) copy-start(bf16[128,4096]{1,0:T(8,128)(2,1)} %refs_2_.4) | copy-start | bytes 3145732
  5.7 11.8 %collective-permute-start.3 = (bf16[128,1024]{1,0:T(8,128)(2,1)S(1)}, bf16[128,1024]{1,0:T(8,128)(2,1)S(1)}, u32[]{:S(2)}, u32[]{:S(2)}) collective-permute-start(bf16[128,1024]{1,0:T(8,128)(2,1)S(1)} %get-tuple-element.57), channel_id=1, source_target_pairs={{0,8},{1,9},{2,10},{3,11},{4,12},{5,13},{6,14},{7,15},{8,0},{9,1},... | collective-permute-start | bytes 786440 | tf_op jit(solution)/shard_map/ppermute | solution.py:431
  7.8 12.8 %collective-permute-start.4 = (bf16[128,1024]{1,0:T(8,128)(2,1)S(1)}, bf16[128,1024]{1,0:T(8,128)(2,1)S(1)}, u32[]{:S(2)}, u32[]{:S(2)}) collective-permute-start(bf16[128,1024]{1,0:T(8,128)(2,1)S(1)} %get-tuple-element.59), channel_id=1, source_target_pairs={{0,4},{1,5},{2,6},{3,7},{4,0},{5,1},{6,2},{7,3},{8,12},{9,13},{10,... | collective-permute-start | bytes 786440 | tf_op jit(solution)/shard_map/ppermute | solution.py:431
  9.3 11.3 %collective-permute-start.5 = (bf16[128,1024]{1,0:T(8,128)(2,1)S(1)}, bf16[128,1024]{1,0:T(8,128)(2,1)S(1)}, u32[]{:S(2)}, u32[]{:S(2)}) collective-permute-start(bf16[128,1024]{1,0:T(8,128)(2,1)S(1)} %get-tuple-element.60), channel_id=1, source_target_pairs={{0,12},{1,13},{2,14},{3,15},{4,8},{5,9},{6,10},{7,11},{8,4},{9,5},... | collective-permute-start | bytes 786440 | tf_op jit(solution)/shard_map/ppermute | solution.py:431
  10.2 5.0 %copy-start.2 = (bf16[128,512]{1,0:T(8,128)(2,1)S(1)}, bf16[128,512]{1,0:T(8,128)(2,1)}, u32[]{:S(2)}) copy-start(bf16[128,512]{1,0:T(8,128)(2,1)} %refs_2_.5) | copy-start | bytes 393220
  10.2 5.0 %copy-start.3 = (bf16[128,512]{1,0:T(8,128)(2,1)S(1)}, bf16[128,512]{1,0:T(8,128)(2,1)}, u32[]{:S(2)}) copy-start(bf16[128,512]{1,0:T(8,128)(2,1)} %refs_4_.1) | copy-start | bytes 393220
  13.3 5.4 %collective-permute-start.2 = (bf16[128,512]{1,0:T(8,128)(2,1)S(1)}, bf16[128,512]{1,0:T(8,128)(2,1)S(1)}, u32[]{:S(2)}, u32[]{:S(2)}) collective-permute-start(bf16[128,512]{1,0:T(8,128)(2,1)S(1)} %get-tuple-element.52), channel_id=1, source_target_pairs={{0,1},{1,0},{2,3},{3,2},{4,5},{5,4},{6,7},{7,6},{8,9},{9,8},{10,11... | collective-permute-start | bytes 393224 | tf_op jit(solution)/shard_map/ppermute | solution.py:431
  15.1 5.8 %collective-permute-start.6 = (bf16[128,512]{1,0:T(8,128)(2,1)S(1)}, bf16[128,512]{1,0:T(8,128)(2,1)S(1)}, u32[]{:S(2)}, u32[]{:S(2)}) collective-permute-start(bf16[128,512]{1,0:T(8,128)(2,1)S(1)} %get-tuple-element.67), channel_id=1, source_target_pairs={{0,3},{1,2},{2,1},{3,0},{4,7},{5,6},{6,5},{7,4},{8,11},{9,10},{10,... | collective-permute-start | bytes 393224 | tf_op jit(solution)/shard_map/ppermute | solution.py:431
  17.5 3.5 %collective-permute-start.7 = (bf16[128,512]{1,0:T(8,128)(2,1)S(1)}, bf16[128,512]{1,0:T(8,128)(2,1)S(1)}, u32[]{:S(2)}, u32[]{:S(2)}) collective-permute-start(bf16[128,512]{1,0:T(8,128)(2,1)S(1)} %get-tuple-element.70), channel_id=1, source_target_pairs={{0,2},{1,3},{2,0},{3,1},{4,6},{5,7},{6,4},{7,5},{8,10},{9,11},{10,... | collective-permute-start | bytes 393224 | tf_op jit(solution)/shard_map/ppermute | solution.py:431
  21.0 8.4 %collective-permute-start.10 = (bf16[256,512]{1,0:T(8,128)(2,1)S(1)}, bf16[256,512]{1,0:T(8,128)(2,1)S(1)}, u32[]{:S(2)}, u32[]{:S(2)}) collective-permute-start(bf16[256,512]{1,0:T(8,128)(2,1)S(1)} %grads_total.1.refs_0_), channel_id=1, source_target_pairs={{0,4},{1,5},{2,6},{3,7},{4,0},{5,1},{6,2},{7,3},{8,12},{9,13},{10,... | collective-permute-start | bytes 786440 | tf_op jit(solution)/shard_map/ppermute | solution.py:431
  22.6 9.2 %collective-permute-start.11 = (bf16[256,512]{1,0:T(8,128)(2,1)S(1)}, bf16[256,512]{1,0:T(8,128)(2,1)S(1)}, u32[]{:S(2)}, u32[]{:S(2)}) collective-permute-start(bf16[256,512]{1,0:T(8,128)(2,1)S(1)} %grads_total.1.refs_0_), channel_id=1, source_target_pairs={{0,8},{1,9},{2,10},{3,11},{4,12},{5,13},{6,14},{7,15},{8,0},{9,1},... | collective-permute-start | bytes 786440 | tf_op jit(solution)/shard_map/ppermute | solution.py:431
  24.2 12.1 %collective-permute-start.9 = (bf16[256,512]{1,0:T(8,128)(2,1)S(1)}, bf16[256,512]{1,0:T(8,128)(2,1)S(1)}, u32[]{:S(2)}, u32[]{:S(2)}) collective-permute-start(bf16[256,512]{1,0:T(8,128)(2,1)S(1)} %grads_total.1.refs_0_), channel_id=1, source_target_pairs={{0,12},{1,13},{2,14},{3,15},{4,8},{5,9},{6,10},{7,11},{8,4},{9,5},... | collective-permute-start | bytes 786440 | tf_op jit(solution)/shard_map/ppermute | solution.py:431
  24.9 11.4 %collective-permute-start.8 = (bf16[1024,512]{1,0:T(8,128)(2,1)S(1)}, bf16[1024,512]{1,0:T(8,128)(2,1)S(1)}, u32[]{:S(2)}, u32[]{:S(2)}) collective-permute-start(bf16[1024,512]{1,0:T(8,128)(2,1)S(1)} %turn_pieces.1.refs_0_), channel_id=1, source_target_pairs={{0,2},{1,3},{2,0},{3,1},{4,6},{5,7},{6,4},{7,5},{8,10},{9,11},{10,... | collective-permute-start | bytes 3145736 | tf_op jit(solution)/shard_map/ppermute | solution.py:431
  36.8 6.3 %collective-permute-start.13 = (bf16[128,512]{1,0:T(8,128)(2,1)S(1)}, bf16[128,512]{1,0:T(8,128)(2,1)S(1)}, u32[]{:S(2)}, u32[]{:S(2)}) collective-permute-start(bf16[128,512]{1,0:T(8,128)(2,1)S(1)} %get-tuple-element.91), channel_id=1, source_target_pairs={{0,1},{1,0},{2,3},{3,2},{4,5},{5,4},{6,7},{7,6},{8,9},{9,8},{10,11... | collective-permute-start | bytes 393224 | tf_op jit(solution)/shard_map/ppermute | solution.py:431
  38.9 8.1 %collective-permute-start.12 = (bf16[128,512]{1,0:T(8,128)(2,1)S(1)}, bf16[128,512]{1,0:T(8,128)(2,1)S(1)}, u32[]{:S(2)}, u32[]{:S(2)}) collective-permute-start(bf16[128,512]{1,0:T(8,128)(2,1)S(1)} %get-tuple-element.87), channel_id=1, source_target_pairs={{0,1},{1,0},{2,3},{3,2},{4,5},{5,4},{6,7},{7,6},{8,9},{9,8},{10,11... | collective-permute-start | bytes 393224 | tf_op jit(solution)/shard_map/ppermute | solution.py:431
  43.2 7.5 %collective-permute-start.14 = (bf16[128,512]{1,0:T(8,128)(2,1)S(1)}, bf16[128,512]{1,0:T(8,128)(2,1)S(1)}, u32[]{:S(2)}, u32[]{:S(2)}) collective-permute-start(bf16[128,512]{1,0:T(8,128)(2,1)S(1)} %relay_total.3), channel_id=1, source_target_pairs={{0,16},{1,17},{2,18},{3,19},{4,20},{5,21},{6,22},{7,23},{8,24},{9,... | collective-permute-start | bytes 393224 | tf_op jit(solution)/shard_map/ppermute | solution.py:431
  46.8 3.9 %collective-permute-start.16 = (bf16[128,512]{1,0:T(8,128)(2,1)S(1)}, bf16[128,512]{1,0:T(8,128)(2,1)S(1)}, u32[]{:S(2)}, u32[]{:S(2)}) collective-permute-start(bf16[128,512]{1,0:T(8,128)(2,1)S(1)} %get-tuple-element.93), channel_id=1, source_target_pairs={{0,2},{1,3},{2,0},{3,1},{4,6},{5,7},{6,4},{7,5},{8,10},{9,11},{10,... | collective-permute-start | bytes 393224 | tf_op jit(solution)/shard_map/ppermute | solution.py:431
  46.9 9.0 %collective-permute-start.17 = (bf16[128,512]{1,0:T(8,128)(2,1)S(1)}, bf16[128,512]{1,0:T(8,128)(2,1)S(1)}, u32[]{:S(2)}, u32[]{:S(2)}) collective-permute-start(bf16[128,512]{1,0:T(8,128)(2,1)S(1)} %relay_total.2), channel_id=1, source_target_pairs={{0,18},{1,19},{2,16},{3,17},{4,22},{5,23},{6,20},{7,21},{8,26},{9,... | collective-permute-start | bytes 393224 | tf_op jit(solution)/shard_map/ppermute | solution.py:431
  47.4 6.3 %collective-permute-start.15 = (bf16[128,512]{1,0:T(8,128)(2,1)S(1)}, bf16[128,512]{1,0:T(8,128)(2,1)S(1)}, u32[]{:S(2)}, u32[]{:S(2)}) collective-permute-start(bf16[128,512]{1,0:T(8,128)(2,1)S(1)} %get-tuple-element.92), channel_id=1, source_target_pairs={{0,1},{1,0},{2,3},{3,2},{4,5},{5,4},{6,7},{7,6},{8,9},{9,8},{10,11... | collective-permute-start | bytes 393224 | tf_op jit(solution)/shard_map/ppermute | solution.py:431
  48.8 6.3 %collective-permute-start.18 = (bf16[128,512]{1,0:T(8,128)(2,1)S(1)}, bf16[128,512]{1,0:T(8,128)(2,1)S(1)}, u32[]{:S(2)}, u32[]{:S(2)}) collective-permute-start(bf16[128,512]{1,0:T(8,128)(2,1)S(1)} %get-tuple-element.94), channel_id=1, source_target_pairs={{0,3},{1,2},{2,1},{3,0},{4,7},{5,6},{6,5},{7,4},{8,11},{9,10},{10,... | collective-permute-start | bytes 393224 | tf_op jit(solution)/shard_map/ppermute | solution.py:431

commit v13 on v12

--- a/solution.py
+++ b/solution.py
@@ -16,11 +16,12 @@
 CORES = 2
 MIDDLE = 2
 NEAR = 2
-ORDER = (0, 3, 2, 1)
+ORDER = (0, 2, 1, 3)
 PARAMS = pltpu.CompilerParams(vmem_limit_bytes=32 * 2**20)
 COST = pl.CostEstimate(flops=1024, bytes_accessed=1024, transcendentals=0)
 VISIT_COST = pl.CostEstimate(flops=5*10**9, bytes_accessed=1024, transcendentals=0)
 ADD_COST = pl.CostEstimate(flops=1*10**9, bytes_accessed=1024, transcendentals=0)
+STACK_COST = pl.CostEstimate(flops=2*10**9, bytes_accessed=1024, transcendentals=0)
 EARLY = pl.CostEstimate(flops=10**10, bytes_accessed=1024, transcendentals=0)
 WHOLE = pl.BlockSpec(memory_space=pltpu.VMEM)
 FAR = pl.BlockSpec(memory_space=pltpu.HBM)
@@ -257,12 +258,15 @@
     )(*same, *cross)
 
 
-def total_kernel(same_ref, cross_ref, sibling_ref, out_ref):
+def total_kernel(same_ref, cross_ref, sibling_ref, *out_refs):
     rows = same_ref.shape[0]
-    out_ref[:rows, :] = same_ref[...]
-    out_ref[rows:, :] = (cross_ref[...] + sibling_ref[...].astype(jnp.float32)).astype(
-        out_ref.dtype
-    )
+    for half, out_ref in enumerate(out_refs):
+        width = out_ref.shape[1]
+        columns = slice(half * width, (half + 1) * width)
+        out_ref[:rows, :] = same_ref[:, columns]
+        out_ref[rows:, :] = (
+            cross_ref[:, columns] + sibling_ref[:, columns].astype(jnp.float32)
+        ).astype(out_ref.dtype)
 
 
 def total_call(same, cross, sibling):
@@ -270,8 +274,8 @@
     return pl.pallas_call(
         total_kernel,
         in_specs=[WHOLE] * 3,
-        out_specs=WHOLE,
-        out_shape=shape((2 * rows, width), jnp.bfloat16),
+        out_specs=[WHOLE] * 2,
+        out_shape=[shape((2 * rows, width // 2), jnp.bfloat16)] * 2,
         compiler_params=PARAMS,
         cost_estimate=COST,
         name="grads_total",
@@ -281,28 +285,33 @@
 def stack_kernel(*refs):
     own_ref, sibling_ref = refs[-2:]
     rows = refs[0].shape[0] // 2
-    for at, ref in enumerate(refs[:-2]):
+    width = refs[0].shape[1]
+    for at in range(len(refs) // 2 - 1):
         here = slice(at * rows, (at + 1) * rows)
-        own_ref[here, :] = ref[:rows, :]
-        sibling_ref[here, :] = ref[rows:, :]
-
-
-def stack_call(grads):
-    height, width = grads[0].shape
+        for half in range(2):
+            ref = refs[2 * at + half]
+            columns = slice(half * width, (half + 1) * width)
+            own_ref[here, columns] = ref[:rows, :]
+            sibling_ref[here, columns] = ref[rows:, :]
+
+
+def stack_call(grads, cost):
+    height, width = grads[0][0].shape
+    operands = [half for halves in grads for half in halves]
     return pl.pallas_call(
         stack_kernel,
-        in_specs=[WHOLE] * len(grads),
+        in_specs=[WHOLE] * len(operands),
         out_specs=[WHOLE] * 2,
-        out_shape=[shape((height // 2 * len(grads), width), grads[0].dtype)] * 2,
-        compiler_params=PARAMS,
-        cost_estimate=EARLY,
+        out_shape=[shape((height // 2 * len(grads), 2 * width), jnp.bfloat16)] * 2,
+        compiler_params=PARAMS,
+        cost_estimate=cost,
         name="stack_grads",
-    )(*grads)
+    )(*operands)
 
 
 def weight_kernel(core_steps, z_steps, far, ctx_count, *refs):
-    own_ref, sibling_ref, own_grads, sibling_grads = refs[:4]
-    out_refs, buf = refs[4:-1], refs[-1]
+    own_ref, sibling_ref, *g_refs = refs[:6]
+    out_refs, buf = refs[6:-1], refs[-1]
     block = out_refs[0].shape[0] // len(z_steps)
     dp_rank = lax.axis_index("dp")
     x_rank = lax.axis_index("ctx")
@@ -312,9 +321,11 @@
     for at, step in enumerate(z_steps):
         start = (core * far + lax.rem(z_rank + step, far)) * size
         here = pl.ds(pl.multiple_of(start, size), size)
-        buf[...] = dot(own_ref[here, :], own_grads[...], NN) + dot(
-            sibling_ref[here, :], sibling_grads[...], NN
-        )
+        cut = g_refs[0].shape[0]
+        total = dot(own_ref[here, :cut], g_refs[0][...], NN)
+        total = total + dot(sibling_ref[here, :cut], g_refs[1][...], NN)
+        total = total + dot(own_ref[here, cut:], g_refs[2][...], NN)
+        buf[...] = total + dot(sibling_ref[here, cut:], g_refs[3][...], NN)
         for x, out_ref in enumerate(out_refs):
             start = lax.rem(x_rank + x, ctx_count) * block
             out_ref[at * block : (at + 1) * block, :] = buf[
@@ -328,7 +339,7 @@
     dims = (height // ctx_count * len(z_steps), width)
     return pl.pallas_call(
         functools.partial(weight_kernel, core_steps, z_steps, far, ctx_count),
-        in_specs=[WHOLE] * 4,
+        in_specs=[WHOLE] * 6,
         out_specs=[WHOLE] * ctx_count,
         out_shape=[shape(dims, kept)] + [shape(dims, jnp.bfloat16)] * (ctx_count - 1),
         scratch_shapes=[pltpu.VMEM((height, width), jnp.float32)],
@@ -458,11 +469,15 @@
     own_cross, pieces[1] = lax.optimization_barrier((own_cross, pieces[1]))
     sibling = send(own_cross, core_steps=1)
     same, pieces = lax.optimization_barrier((same, pieces))
-    total = total_call(*add_call([own_same] + same, cross), sibling)
-    grads = [send(total, member=i) if i else total for i in ORDER]
-    tokens = turn_call(after([pieces[i] for i in ORDER], total))
-    grads = stack_call(grads)
-    tokens = [tokens, after(send(tokens, core_steps=1), grads)]
+    halves = total_call(*add_call([own_same] + same, cross), sibling)
+    over_y = [send(value, member=2) for value in halves]
+    over_z = [send(value, member=1) for value in halves[::-1]][::-1]
+    over_both = [send(over_y[0], member=1), send(over_z[1], member=2)]
+    tokens = turn_call(after([pieces[i] for i in ORDER], halves))
+    grads = stack_call([halves, over_y, over_z], STACK_COST)
+    last = stack_call([after(over_both, grads)], EARLY)
+    grads = grads + last
+    tokens = [tokens, after(send(tokens, core_steps=1), last)]
     weights = functools.partial(
         weight_call, far=far, ctx_count=ctx_count, tokens=tokens, kept=jnp.float32
     )
@@ -475,10 +490,11 @@
         arrived.append([send(value, s) for s, value in enumerate(blocks, 1)])
     own_block, *near = weights(0, (0,), grads=grads)
     cross_block, *cross_near = weights(1, (0,), grads=grads, kept=jnp.bfloat16)
+    arrived[0] = after(arrived[0], (own_block, cross_block))
     for core in range(CORES):
         relayed = relay_call(far - 1, away[core], arrived[core])
         from_far.append([send(value, 0, core, s) for s, value in enumerate(relayed, 1)])
-    near, cross_near, own_scores = after((near, cross_near, own_scores), relayed)
+    own_scores = after(own_scores, relayed)
     same = [own_block, early_call(from_far[0])] + [send(v, s) for s, v in enumerate(near, 1)]
     cross = [send(cross_block, core_steps=1)] + from_far[1]
     cross += [send(value, s, 1) for s, value in enumerate(cross_near, 1)]

time: 56.9 us -> 56.3 us (0.989)
  waiting for transfers between devices: 23.9 us -> 18.2 us
  starting transfers between devices: 19.5 us -> 24.1 us
    ppermute x19 -> x22, waiting for transfers between devices: 23.9 us -> 18.2 us  [send(): return lax.ppermute(value, ('dp', 'ctx'), pairs)]
    ppermute x19 -> x22, starting transfers between devices: 19.5 us -> 24.1 us  [send(): return lax.ppermute(value, ('dp', 'ctx'), pairs)]
  transfers between devices with their start and end apart: 19 -> 22, of which waited for: 11 -> 13; matrix products, arithmetic and copies ran while one was open for 0% -> 0% of each run, Pallas kernels for 20% -> 21%
where the time goes in v13:
time: 56.3 us; the launch traced here: 56.1 us
  starting transfers between devices  24.1 us (43%)
  waiting for transfers between devices  18.2 us (32%)
  Pallas kernels  13 us (23%)
  between operations  0.8 us (1%)
    ppermute x22, starting transfers between devices, send(): return lax.ppermute(value, ('dp', 'ctx'), pairs)  24.1 us
    ppermute x22, waiting for transfers between devices, send(): return lax.ppermute(value, ('dp', 'ctx'), pairs)  18.2 us
    pallas_call x2, Pallas kernels, block_call(): pl.pallas_call(functools.partial(block_kernel, ctx_count, step), in_specs...  5.5 us
    pallas_call x4, Pallas kernels, weight_call(): pl.pallas_call(functools.partial(weight_kernel, core_steps, z_steps, far,...  2.47 us
    pallas_call x1, Pallas kernels, pieces_call(): pl.pallas_call(functools.partial(pieces_kernel, far, len(wanted)), in_spe...  1.94 us
    pallas_call x1, Pallas kernels, query_call(): pl.pallas_call(functools.partial(query_kernel, len(keys)), in_specs=[WHOL...  1.74 us
  transfers between devices with their start and end apart: 22, of which 13 were waited for; matrix products, arithmetic and copies ran while one was open for 0% of the time, Pallas kernels for 21%

profile of v13, /device:TPU:0, one launch (start us, length us, event | category | flops | bytes accessed | tf_op | source)
XLA Modules:
  0.0 56.1 jit_solution(18216406079374652342)
XLA Ops:
  0.6 3.0 %collective-permute-start = (bf16[128,512]{1,0:T(8,128)(2,1)}, bf16[128,512]{1,0:T(8,128)(2,1)S(1)}, u32[]{:S(2)}, u32[]{:S(2)}) collective-permute-start(bf16[128,512]{1,0:T(8,128)(2,1)} %refs_2_.5), channel_id=1, source_target_pairs={{0,1},{1,0},{2,3},{3,2},{4,5},{5,4},{6,7},{7,6},{8,9},{9,8},{10,11... | collective-permute-start | bytes 393224 | tf_op jit(solution)/shard_map/ppermute | solution.py:442
  3.6 0.1 collective-permute-start.1
  3.7 1.9 %pieces.1 = (bf16[128,1024]{1,0:T(8,128)(2,1)S(1)}, bf16[128,1024]{1,0:T(8,128)(2,1)S(1)}, bf16[128,1024]{1,0:T(8,128)(2,1)S(1)}, bf16[128,1024]{1,0:T(8,128)(2,...) custom-call(bf16[128,4096]{1,0:T(8,128)(2,1)} %in_hbm.1, bf16[128,4096]{1,0:T(8,128)(2,1)} %refs_0_.3, ...), custom_call_target="tpu_custom_call" | custom-call | flops 1024 | bytes 1024 | tf_op jit(solution)/shard_map/pieces/pallas_call | solution.py:203
  5.7 2.1 %collective-permute-start.3 = (bf16[128,1024]{1,0:T(8,128)(2,1)S(1)}, bf16[128,1024]{1,0:T(8,128)(2,1)S(1)}, u32[]{:S(2)}, u32[]{:S(2)}) collective-permute-start(bf16[128,1024]{1,0:T(8,128)(2,1)S(1)} %get-tuple-element.67), channel_id=1, source_target_pairs={{0,8},{1,9},{2,10},{3,11},{4,12},{5,13},{6,14},{7,15},{8,0},{9,1},... | collective-permute-start | bytes 786440 | tf_op jit(solution)/shard_map/ppermute | solution.py:442
  7.8 1.5 %collective-permute-start.4 = (bf16[128,1024]{1,0:T(8,128)(2,1)S(1)}, bf16[128,1024]{1,0:T(8,128)(2,1)S(1)}, u32[]{:S(2)}, u32[]{:S(2)}) collective-permute-start(bf16[128,1024]{1,0:T(8,128)(2,1)S(1)} %get-tuple-element.69), channel_id=1, source_target_pairs={{0,4},{1,5},{2,6},{3,7},{4,0},{5,1},{6,2},{7,3},{8,12},{9,13},{10,... | collective-permute-start | bytes 786440 | tf_op jit(solution)/shard_map/ppermute | solution.py:442
  9.3 0.0 collective-permute-start.5
  9.3 0.0 collective-permute-done.refs_3_
  9.3 0.8 %collective-permute-done.1.refs_4_ = bf16[128,512]{1,0:T(8,128)(2,1)S(1)} collective-permute-done((bf16[128,512]{1,0:T(8,128)(2,1)}, bf16[128,512]{1,0:T(8,128)(2,1)S(1)}, u32[]{:S(2)}, u32[]{:S(2)}) %collective-permute-start.1) | collective-permute-done | bytes 131104 | tf_op jit(solution)/shard_map/ppermute | solution.py:442
  10.2 3.1 %visiting_keys.1 = (bf16[128,4096]{1,0:T(8,128)(2,1)S(1)}, bf16[128,512]{1,0:T(8,128)(2,1)S(1)}, bf16[128,512]{1,0:T(8,128)(2,1)S(1)}, f32[32,128]{1,0:T(8,128)S(1)}) custom-call(s32[1,4]{1,0:T(1,128)} %refs_0_.5, bf16[128,4096]{1,0:T(8,128)(2,1)S(1)} %copy-done, bf16[128,4096]{1,0:T(8,128)(2,1)S(1)} %copy-done.1, ...), custom_call_target="tpu_custom_call" | custom-call | flops 5000000000 | bytes 1024 | tf_op jit(solution)/shard_map/visiting_keys/pallas_call | solution.py:128
  13.3 1.8 %collective-permute-start.2 = (bf16[128,512]{1,0:T(8,128)(2,1)S(1)}, bf16[128,512]{1,0:T(8,128)(2,1)S(1)}, u32[]{:S(2)}, u32[]{:S(2)}) collective-permute-start(bf16[128,512]{1,0:T(8,128)(2,1)S(1)} %get-tuple-element.62), channel_id=1, source_target_pairs={{0,1},{1,0},{2,3},{3,2},{4,5},{5,4},{6,7},{7,6},{8,9},{9,8},{10,11... | collective-permute-start | bytes 393224 | tf_op jit(solution)/shard_map/ppermute | solution.py:442
  15.1 2.4 %own_keys.1 = (bf16[128,4096]{1,0:T(8,128)(2,1)S(1)}, f32[128,512]{1,0:T(8,128)S(1)}, bf16[128,512]{1,0:T(8,128)(2,1)S(1)}) custom-call(s32[1,4]{1,0:T(1,128)} %refs_0_.5, bf16[128,4096]{1,0:T(8,128)(2,1)S(1)} %copy-done, bf16[128,4096]{1,0:T(8,128)(2,1)S(1)} %copy-done.1, bf16[128,512]{1,0:T(8,128)(2,1)S(1)} %copy-done.2, bf16[128,512]{1,0:T(8,128)(2,1)S(1)} %copy-done.3, ...), custom_call_target="tpu_custom_call" | custom-call | flops 1024 | bytes 1024 | tf_op jit(solution)/shard_map/own_keys/pallas_call | solution.py:128
  17.5 0.0 collective-permute-done.3.refs_2_
  17.5 0.5 collective-permute-start.7
  18.0 0.7 %collective-permute-done.2.refs_1_ = bf16[128,512]{1,0:T(8,128)(2,1)S(1)} collective-permute-done((bf16[128,512]{1,0:T(8,128)(2,1)S(1)}, bf16[128,512]{1,0:T(8,128)(2,1)S(1)}, u32[]{:S(2)}, u32[]{:S(2)}) %collective-permute-start.2) | collective-permute-done | bytes 131104 | tf_op jit(solution)/shard_map/ppermute | solution.py:442
  18.7 1.9 %collective-permute-done.4.refs_1_ = bf16[128,1024]{1,0:T(8,128)(2,1)S(1)} collective-permute-done((bf16[128,1024]{1,0:T(8,128)(2,1)S(1)}, bf16[128,1024]{1,0:T(8,128)(2,1)S(1)}, u32[]{:S(2)}, u32[]{:S(2)}) %collective-permute-start.4) | collective-permute-done | bytes 262176 | tf_op jit(solution)/shard_map/ppermute | solution.py:442
  20.6 0.4 collective-permute-done.6.refs_2_
  21.0 1.5 %collective-permute-start.9 = (bf16[256,256]{1,0:T(8,128)(2,1)S(1)}, bf16[256,256]{1,0:T(8,128)(2,1)S(1)}, u32[]{:S(2)}, u32[]{:S(2)}) collective-permute-start(bf16[256,256]{1,0:T(8,128)(2,1)S(1)} %get-tuple-element.81.refs_0_), channel_id=1, source_target_pairs={{0,4},{1,5},{2,6},{3,7},{4,0},{5,1},{6,2},{7,3},{8,12},{9,13},{10,... | collective-permute-start | bytes 393224 | tf_op jit(solution)/shard_map/ppermute | solution.py:442
  22.6 1.6 %collective-permute-start.11 = (bf16[256,256]{1,0:T(8,128)(2,1)S(1)}, bf16[256,256]{1,0:T(8,128)(2,1)S(1)}, u32[]{:S(2)}, u32[]{:S(2)}) collective-permute-start(bf16[256,256]{1,0:T(8,128)(2,1)S(1)} %get-tuple-element.82.refs_1_), channel_id=1, source_target_pairs={{0,8},{1,9},{2,10},{3,11},{4,12},{5,13},{6,14},{7,15},{8,0},{9,1},... | collective-permute-start | bytes 393224 | tf_op jit(solution)/shard_map/ppermute | solution.py:442
  24.2 0.5 collective-permute-start.13
  24.7 0.5 collective-permute-start.14
  25.2 0.3 turn_pieces.1.refs_0_
  25.5 0.1 collective-permute-start.8
  25.6 1.1 %collective-permute-done.9.refs_2_ = bf16[256,256]{1,0:T(8,128)(2,1)S(1)} collective-permute-done((bf16[256,256]{1,0:T(8,128)(2,1)S(1)}, bf16[256,256]{1,0:T(8,128)(2,1)S(1)}, u32[]{:S(2)}, u32[]{:S(2)}) %collective-permute-start.9) | collective-permute-done | bytes 131104 | tf_op jit(solution)/shard_map/ppermute | solution.py:442
  26.7 2.3 %collective-permute-start.10 = (bf16[256,256]{1,0:T(8,128)(2,1)S(1)}, bf16[256,256]{1,0:T(8,128)(2,1)S(1)}, u32[]{:S(2)}, u32[]{:S(2)}) collective-permute-start(bf16[256,256]{1,0:T(8,128)(2,1)S(1)} %collective-permute-done.9.refs_2_), channel_id=1, source_target_pairs={{0,8},{1,9},{2,10},{3,11},{4,12},{5,13},{6,14},{7,15},{8,0},{9,1},... | collective-permute-start | bytes 393224 | tf_op jit(solution)/shard_map/ppermute | solution.py:442
  29.0 0.0 collective-permute-done.11.refs_5_
  29.0 1.5 %collective-permute-start.12 = (bf16[256,256]{1,0:T(8,128)(2,1)S(1)}, bf16[256,256]{1,0:T(8,128)(2,1)S(1)}, u32[]{:S(2)}, u32[]{:S(2)}) collective-permute-start(bf16[256,256]{1,0:T(8,128)(2,1)S(1)} %collective-permute-done.11.refs_5_), channel_id=1, source_target_pairs={{0,4},{1,5},{2,6},{3,7},{4,0},{5,1},{6,2},{7,3},{8,12},{9,13},{10,... | collective-permute-start | bytes 393224 | tf_op jit(solution)/shard_map/ppermute | solution.py:442
  30.5 0.0 collective-permute-done.13.refs_3_
  30.5 1.3 %collective-permute-done.14.refs_4_ = bf16[256,256]{1,0:T(8,128)(2,1)S(1)} collective-permute-done((bf16[256,256]{1,0:T(8,128)(2,1)S(1)}, bf16[256,256]{1,0:T(8,128)(2,1)S(1)}, u32[]{:S(2)}, u32[]{:S(2)}) %collective-permute-start.14) | collective-permute-done | bytes 131104 | tf_op jit(solution)/shard_map/ppermute | solution.py:442
  31.8 0.1 stack_grads.2
  31.8 1.8 %collective-permute-done.10.refs_0_ = bf16[256,256]{1,0:T(8,128)(2,1)S(1)} collective-permute-done((bf16[256,256]{1,0:T(8,128)(2,1)S(1)}, bf16[256,256]{1,0:T(8,128)(2,1)S(1)}, u32[]{:S(2)}, u32[]{:S(2)}) %collective-permute-start.10) | collective-permute-done | bytes 131104 | tf_op jit(solution)/shard_map/ppermute | solution.py:442
  33.7 0.3 collective-permute-done.12.refs_1_
  34.0 0.6 %weight_far.2 = (f32[128,512]{1,0:T(8,128)S(1)}, bf16[128,512]{1,0:T(8,128)(2,1)S(1)}) custom-call(bf16[1024,512]{1,0:T(8,128)(2,1)S(1)} %turn_pieces.1.refs_0_, bf16[1024,512]{1,0:T(8,128)(2,1)S(1)} %collective-permute-done.8.refs_1_, bf16[384,512]{1,0:T(8,128)(2,1)S(1)} %get-tuple-element.103.refs_2_, bf16[384,512]{1,0:T(8,128)(2,1)S(1)} %get-tuple-element.104.refs_3_, ...), custom_call_target="tpu_custom_call" | custom-call | flops 1024 | bytes 1024 | tf_op jit(solution)/shard_map/weight_far/pallas_call | solution.py:340
  34.6 1.2 %collective-permute-start.16 = (bf16[128,512]{1,0:T(8,128)(2,1)S(1)}, bf16[128,512]{1,0:T(8,128)(2,1)S(1)}, u32[]{:S(2)}, u32[]{:S(2)}) collective-permute-start(bf16[128,512]{1,0:T(8,128)(2,1)S(1)} %get-tuple-element.108), channel_id=1, source_target_pairs={{0,1},{1,0},{2,3},{3,2},{4,5},{5,4},{6,7},{7,6},{8,9},{9,8},{10,11... | collective-permute-start | bytes 393224 | tf_op jit(solution)/shard_map/ppermute | solution.py:442
  35.8 0.6 %weight_far.3 = (f32[128,512]{1,0:T(8,128)S(1)}, bf16[128,512]{1,0:T(8,128)(2,1)S(1)}) custom-call(bf16[1024,512]{1,0:T(8,128)(2,1)S(1)} %turn_pieces.1.refs_0_, bf16[1024,512]{1,0:T(8,128)(2,1)S(1)} %collective-permute-done.8.refs_1_, bf16[384,512]{1,0:T(8,128)(2,1)S(1)} %get-tuple-element.103.refs_2_, bf16[384,512]{1,0:T(8,128)(2,1)S(1)} %get-tuple-element.104.refs_3_, ...), custom_call_target="tpu_custom_call" | custom-call | flops 1024 | bytes 1024 | tf_op jit(solution)/shard_map/weight_far/pallas_call | solution.py:340
  36.5 0.9 %collective-permute-start.15 = (bf16[128,512]{1,0:T(8,128)(2,1)S(1)}, bf16[128,512]{1,0:T(8,128)(2,1)S(1)}, u32[]{:S(2)}, u32[]{:S(2)}) collective-permute-start(bf16[128,512]{1,0:T(8,128)(2,1)S(1)} %get-tuple-element.100), channel_id=1, source_target_pairs={{0,1},{1,0},{2,3},{3,2},{4,5},{5,4},{6,7},{7,6},{8,9},{9,8},{10,11... | collective-permute-start | bytes 393224 | tf_op jit(solution)/shard_map/ppermute | solution.py:442
  37.4 0.6 %weight_near.3 = (bf16[128,512]{1,0:T(8,128)(2,1)S(1)}, bf16[128,512]{1,0:T(8,128)(2,1)S(1)}) custom-call(bf16[1024,512]{1,0:T(8,128)(2,1)S(1)} %turn_pieces.1.refs_0_, bf16[1024,512]{1,0:T(8,128)(2,1)S(1)} %collective-permute-done.8.refs_1_, bf16[384,512]{1,0:T(8,128)(2,1)S(1)} %get-tuple-element.103.refs_2_, ...), custom_call_target="tpu_custom_call" | custom-call | flops 1024 | bytes 1024 | tf_op jit(solution)/shard_map/weight_near/pallas_call | solution.py:340
  38.0 0.6 %weight_near.2 = (f32[128,512]{1,0:T(8,128)S(1)}, bf16[128,512]{1,0:T(8,128)(2,1)S(1)}) custom-call(bf16[1024,512]{1,0:T(8,128)(2,1)S(1)} %turn_pieces.1.refs_0_, bf16[1024,512]{1,0:T(8,128)(2,1)S(1)} %collective-permute-done.8.refs_1_, bf16[384,512]{1,0:T(8,128)(2,1)S(1)} %get-tuple-element.103.refs_2_, bf16[384,512]{1,0:T(8,128)(2,1)S(1)} %get-tuple-element.104.refs_3_, ...), custom_call_target="tpu_custom_call" | custom-call | flops 1024 | bytes 1024 | tf_op jit(solution)/shard_map/weight_near/pallas_call | solution.py:340
  38.6 2.3 %collective-permute-done.16.refs_0_ = bf16[128,512]{1,0:T(8,128)(2,1)S(1)} collective-permute-done((bf16[128,512]{1,0:T(8,128)(2,1)S(1)}, bf16[128,512]{1,0:T(8,128)(2,1)S(1)}, u32[]{:S(2)}, u32[]{:S(2)}) %collective-permute-start.16) | collective-permute-done | bytes 131104 | tf_op jit(solution)/shard_map/ppermute | solution.py:442
  40.9 2.7 %collective-permute-start.17 = (bf16[128,512]{1,0:T(8,128)(2,1)S(1)}, bf16[128,512]{1,0:T(8,128)(2,1)S(1)}, u32[]{:S(2)}, u32[]{:S(2)}) collective-permute-start(bf16[128,512]{1,0:T(8,128)(2,1)S(1)} %relay_total.3), channel_id=1, source_target_pairs={{0,16},{1,17},{2,18},{3,19},{4,20},{5,21},{6,22},{7,23},{8,24},{9,... | collective-permute-start | bytes 393224 | tf_op jit(solution)/shard_map/ppermute | solution.py:442
  43.6 1.4 %collective-permute-start.21 = (bf16[128,512]{1,0:T(8,128)(2,1)S(1)}, bf16[128,512]{1,0:T(8,128)(2,1)S(1)}, u32[]{:S(2)}, u32[]{:S(2)}) collective-permute-start(bf16[128,512]{1,0:T(8,128)(2,1)S(1)} %get-tuple-element.112), channel_id=1, source_target_pairs={{0,3},{1,2},{2,1},{3,0},{4,7},{5,6},{6,5},{7,4},{8,11},{9,10},{10,... | collective-permute-start | bytes 393224 | tf_op jit(solution)/shard_map/ppermute | solution.py:442
  45.0 0.8 %collective-permute-start.18 = (bf16[128,512]{1,0:T(8,128)(2,1)S(1)}, bf16[128,512]{1,0:T(8,128)(2,1)S(1)}, u32[]{:S(2)}, u32[]{:S(2)}) collective-permute-start(bf16[128,512]{1,0:T(8,128)(2,1)S(1)} %get-tuple-element.111), channel_id=1, source_target_pairs={{0,1},{1,0},{2,3},{3,2},{4,5},{5,4},{6,7},{7,6},{8,9},{9,8},{10,11... | collective-permute-start | bytes 393224 | tf_op jit(solution)/shard_map/ppermute | solution.py:442
  45.8 0.1 collective-permute-start.20
  45.9 1.7 %query_gradient.1 = bf16[128,4096]{1,0:T(8,128)(2,1)} custom-call(bf16[128,4096]{1,0:T(8,128)(2,1)S(1)} %get-tuple-element.101.refs_0_, bf16[128,4096]{1,0:T(8,128)(2,1)S(1)} %get-tuple-element.102.refs_1_, bf16[128,512]{1,0:T(8,128)(2,1)S(1)} %copy-done.2, bf16[128,512]{1,0:T(8,128)(2,1)S(1)} %collective-permute-done.refs_3_), custom_call_target="tpu_custom_call" | custom-call | flops 1024 | bytes 1024 | tf_op jit(solution)/shard_map/query_gradient/pallas_call | solution.py:155
  47.6 0.7 %collective-permute-done.17.refs_0_ = bf16[128,512]{1,0:T(8,128)(2,1)S(1)} collective-permute-done((bf16[128,512]{1,0:T(8,128)(2,1)S(1)}, bf16[128,512]{1,0:T(8,128)(2,1)S(1)}, u32[]{:S(2)}, u32[]{:S(2)}) %collective-permute-start.17) | collective-permute-done | bytes 131104 | tf_op jit(solution)/shard_map/ppermute | solution.py:442
  48.3 0.5 collective-permute-done.21.refs_5_
  48.8 3.4 %collective-permute-done.18.refs_2_ = bf16[128,512]{1,0:T(8,128)(2,1)S(1)} collective-permute-done((bf16[128,512]{1,0:T(8,128)(2,1)S(1)}, bf16[128,512]{1,0:T(8,128)(2,1)S(1)}, u32[]{:S(2)}, u32[]{:S(2)}) %collective-permute-start.18) | collective-permute-done | bytes 131104 | tf_op jit(solution)/shard_map/ppermute | solution.py:442
  52.2 3.0 %collective-permute-done.20.refs_4_ = bf16[128,512]{1,0:T(8,128)(2,1)S(1)} collective-permute-done((bf16[128,512]{1,0:T(8,128)(2,1)S(1)}, bf16[128,512]{1,0:T(8,128)(2,1)S(1)}, u32[]{:S(2)}, u32[]{:S(2)}) %collective-permute-start.20) | collective-permute-done | bytes 131104 | tf_op jit(solution)/shard_map/ppermute | solution.py:442
  55.2 0.9 %weight_total.1 = (f32[128,512]{1,0:T(8,128)}, f32[128,512]{1,0:T(8,128)}) custom-call(f32[128,512]{1,0:T(8,128)S(1)} %get-tuple-element.107.refs_0_, f32[128,512]{1,0:T(8,128)S(1)} %early_total.1.refs_1_, bf16[128,512]{1,0:T(8,128)(2,1)S(1)} %collective-permute-done.18.refs_2_, bf16[128,512]{1,0:T(8,128)(2,1)S(1)} %collective-permute-done.19.refs_3_, ...), custom_call_target="tpu_custom_call" | custom-call | flops 1024 | bytes 1024 | tf_op jit(solution)/shard_map/weight_total/pallas_call | solution.py:409
  (21 shorter events, 0.2 us)
Async XLA Ops:
  0.6 8.7 %collective-permute-start = (bf16[128,512]{1,0:T(8,128)(2,1)}, bf16[128,512]{1,0:T(8,128)(2,1)S(1)}, u32[]{:S(2)}, u32[]{:S(2)}) collective-permute-start(bf16[128,512]{1,0:T(8,128)(2,1)} %refs_2_.5), channel_id=1, source_target_pairs={{0,1},{1,0},{2,3},{3,2},{4,5},{5,4},{6,7},{7,6},{8,9},{9,8},{10,11... | collective-permute-start | bytes 393224 | tf_op jit(solution)/shard_map/ppermute | solution.py:442
  3.6 6.5 %collective-permute-start.1 = (bf16[128,512]{1,0:T(8,128)(2,1)}, bf16[128,512]{1,0:T(8,128)(2,1)S(1)}, u32[]{:S(2)}, u32[]{:S(2)}) collective-permute-start(bf16[128,512]{1,0:T(8,128)(2,1)} %refs_4_.1), channel_id=1, source_target_pairs={{0,1},{1,0},{2,3},{3,2},{4,5},{5,4},{6,7},{7,6},{8,9},{9,8},{10,11... | collective-permute-start | bytes 393224 | tf_op jit(solution)/shard_map/ppermute | solution.py:442
  3.7 6.4 %copy-start = (bf16[128,4096]{1,0:T(8,128)(2,1)S(1)}, bf16[128,4096]{1,0:T(8,128)(2,1)}, u32[]{:S(2)}) copy-start(bf16[128,4096]{1,0:T(8,128)(2,1)} %refs_1_.3) | copy-start | bytes 3145732
  3.7 6.4 %copy-start.1 = (bf16[128,4096]{1,0:T(8,128)(2,1)S(1)}, bf16[128,4096]{1,0:T(8,128)(2,1)}, u32[]{:S(2)}) copy-start(bf16[128,4096]{1,0:T(8,128)(2,1)} %refs_2_.4) | copy-start | bytes 3145732
  5.7 11.8 %collective-permute-start.3 = (bf16[128,1024]{1,0:T(8,128)(2,1)S(1)}, bf16[128,1024]{1,0:T(8,128)(2,1)S(1)}, u32[]{:S(2)}, u32[]{:S(2)}) collective-permute-start(bf16[128,1024]{1,0:T(8,128)(2,1)S(1)} %get-tuple-element.67), channel_id=1, source_target_pairs={{0,8},{1,9},{2,10},{3,11},{4,12},{5,13},{6,14},{7,15},{8,0},{9,1},... | collective-permute-start | bytes 786440 | tf_op jit(solution)/shard_map/ppermute | solution.py:442
  7.8 12.8 %collective-permute-start.4 = (bf16[128,1024]{1,0:T(8,128)(2,1)S(1)}, bf16[128,1024]{1,0:T(8,128)(2,1)S(1)}, u32[]{:S(2)}, u32[]{:S(2)}) collective-permute-start(bf16[128,1024]{1,0:T(8,128)(2,1)S(1)} %get-tuple-element.69), channel_id=1, source_target_pairs={{0,4},{1,5},{2,6},{3,7},{4,0},{5,1},{6,2},{7,3},{8,12},{9,13},{10,... | collective-permute-start | bytes 786440 | tf_op jit(solution)/shard_map/ppermute | solution.py:442
  9.3 11.3 %collective-permute-start.5 = (bf16[128,1024]{1,0:T(8,128)(2,1)S(1)}, bf16[128,1024]{1,0:T(8,128)(2,1)S(1)}, u32[]{:S(2)}, u32[]{:S(2)}) collective-permute-start(bf16[128,1024]{1,0:T(8,128)(2,1)S(1)} %get-tuple-element.70), channel_id=1, source_target_pairs={{0,12},{1,13},{2,14},{3,15},{4,8},{5,9},{6,10},{7,11},{8,4},{9,5},... | collective-permute-start | bytes 786440 | tf_op jit(solution)/shard_map/ppermute | solution.py:442
  10.2 5.0 %copy-start.2 = (bf16[128,512]{1,0:T(8,128)(2,1)S(1)}, bf16[128,512]{1,0:T(8,128)(2,1)}, u32[]{:S(2)}) copy-start(bf16[128,512]{1,0:T(8,128)(2,1)} %refs_2_.5) | copy-start | bytes 393220
  10.2 5.0 %copy-start.3 = (bf16[128,512]{1,0:T(8,128)(2,1)S(1)}, bf16[128,512]{1,0:T(8,128)(2,1)}, u32[]{:S(2)}) copy-start(bf16[128,512]{1,0:T(8,128)(2,1)} %refs_4_.1) | copy-start | bytes 393220
  13.3 5.4 %collective-permute-start.2 = (bf16[128,512]{1,0:T(8,128)(2,1)S(1)}, bf16[128,512]{1,0:T(8,128)(2,1)S(1)}, u32[]{:S(2)}, u32[]{:S(2)}) collective-permute-start(bf16[128,512]{1,0:T(8,128)(2,1)S(1)} %get-tuple-element.62), channel_id=1, source_target_pairs={{0,1},{1,0},{2,3},{3,2},{4,5},{5,4},{6,7},{7,6},{8,9},{9,8},{10,11... | collective-permute-start | bytes 393224 | tf_op jit(solution)/shard_map/ppermute | solution.py:442
  15.1 5.8 %collective-permute-start.6 = (bf16[128,512]{1,0:T(8,128)(2,1)S(1)}, bf16[128,512]{1,0:T(8,128)(2,1)S(1)}, u32[]{:S(2)}, u32[]{:S(2)}) collective-permute-start(bf16[128,512]{1,0:T(8,128)(2,1)S(1)} %get-tuple-element.77), channel_id=1, source_target_pairs={{0,3},{1,2},{2,1},{3,0},{4,7},{5,6},{6,5},{7,4},{8,11},{9,10},{10,... | collective-permute-start | bytes 393224 | tf_op jit(solution)/shard_map/ppermute | solution.py:442
  17.5 3.5 %collective-permute-start.7 = (bf16[128,512]{1,0:T(8,128)(2,1)S(1)}, bf16[128,512]{1,0:T(8,128)(2,1)S(1)}, u32[]{:S(2)}, u32[]{:S(2)}) collective-permute-start(bf16[128,512]{1,0:T(8,128)(2,1)S(1)} %get-tuple-element.80), channel_id=1, source_target_pairs={{0,2},{1,3},{2,0},{3,1},{4,6},{5,7},{6,4},{7,5},{8,10},{9,11},{10,... | collective-permute-start | bytes 393224 | tf_op jit(solution)/shard_map/ppermute | solution.py:442
  21.0 5.6 %collective-permute-start.9 = (bf16[256,256]{1,0:T(8,128)(2,1)S(1)}, bf16[256,256]{1,0:T(8,128)(2,1)S(1)}, u32[]{:S(2)}, u32[]{:S(2)}) collective-permute-start(bf16[256,256]{1,0:T(8,128)(2,1)S(1)} %get-tuple-element.81.refs_0_), channel_id=1, source_target_pairs={{0,4},{1,5},{2,6},{3,7},{4,0},{5,1},{6,2},{7,3},{8,12},{9,13},{10,... | collective-permute-start | bytes 393224 | tf_op jit(solution)/shard_map/ppermute | solution.py:442
  22.6 6.4 %collective-permute-start.11 = (bf16[256,256]{1,0:T(8,128)(2,1)S(1)}, bf16[256,256]{1,0:T(8,128)(2,1)S(1)}, u32[]{:S(2)}, u32[]{:S(2)}) collective-permute-start(bf16[256,256]{1,0:T(8,128)(2,1)S(1)} %get-tuple-element.82.refs_1_), channel_id=1, source_target_pairs={{0,8},{1,9},{2,10},{3,11},{4,12},{5,13},{6,14},{7,15},{8,0},{9,1},... | collective-permute-start | bytes 393224 | tf_op jit(solution)/shard_map/ppermute | solution.py:442
  24.2 6.3 %collective-permute-start.13 = (bf16[256,256]{1,0:T(8,128)(2,1)S(1)}, bf16[256,256]{1,0:T(8,128)(2,1)S(1)}, u32[]{:S(2)}, u32[]{:S(2)}) collective-permute-start(bf16[256,256]{1,0:T(8,128)(2,1)S(1)} %get-tuple-element.82.refs_1_), channel_id=1, source_target_pairs={{0,4},{1,5},{2,6},{3,7},{4,0},{5,1},{6,2},{7,3},{8,12},{9,13},{10,... | collective-permute-start | bytes 393224 | tf_op jit(solution)/shard_map/ppermute | solution.py:442
  24.7 7.1 %collective-permute-start.14 = (bf16[256,256]{1,0:T(8,128)(2,1)S(1)}, bf16[256,256]{1,0:T(8,128)(2,1)S(1)}, u32[]{:S(2)}, u32[]{:S(2)}) collective-permute-start(bf16[256,256]{1,0:T(8,128)(2,1)S(1)} %get-tuple-element.81.refs_0_), channel_id=1, source_target_pairs={{0,8},{1,9},{2,10},{3,11},{4,12},{5,13},{6,14},{7,15},{8,0},{9,1},... | collective-permute-start | bytes 393224 | tf_op jit(solution)/shard_map/ppermute | solution.py:442
  25.5 8.5 %collective-permute-start.8 = (bf16[1024,512]{1,0:T(8,128)(2,1)S(1)}, bf16[1024,512]{1,0:T(8,128)(2,1)S(1)}, u32[]{:S(2)}, u32[]{:S(2)}) collective-permute-start(bf16[1024,512]{1,0:T(8,128)(2,1)S(1)} %turn_pieces.1.refs_0_), channel_id=1, source_target_pairs={{0,2},{1,3},{2,0},{3,1},{4,6},{5,7},{6,4},{7,5},{8,10},{9,11},{10,... | collective-permute-start | bytes 3145736 | tf_op jit(solution)/shard_map/ppermute | solution.py:442
  26.7 7.0 %collective-permute-start.10 = (bf16[256,256]{1,0:T(8,128)(2,1)S(1)}, bf16[256,256]{1,0:T(8,128)(2,1)S(1)}, u32[]{:S(2)}, u32[]{:S(2)}) collective-permute-start(bf16[256,256]{1,0:T(8,128)(2,1)S(1)} %collective-permute-done.9.refs_2_), channel_id=1, source_target_pairs={{0,8},{1,9},{2,10},{3,11},{4,12},{5,13},{6,14},{7,15},{8,0},{9,1},... | collective-permute-start | bytes 393224 | tf_op jit(solution)/shard_map/ppermute | solution.py:442
  29.0 5.0 %collective-permute-start.12 = (bf16[256,256]{1,0:T(8,128)(2,1)S(1)}, bf16[256,256]{1,0:T(8,128)(2,1)S(1)}, u32[]{:S(2)}, u32[]{:S(2)}) collective-permute-start(bf16[256,256]{1,0:T(8,128)(2,1)S(1)} %collective-permute-done.11.refs_5_), channel_id=1, source_target_pairs={{0,4},{1,5},{2,6},{3,7},{4,0},{5,1},{6,2},{7,3},{8,12},{9,13},{10,... | collective-permute-start | bytes 393224 | tf_op jit(solution)/shard_map/ppermute | solution.py:442
  34.6 6.3 %collective-permute-start.16 = (bf16[128,512]{1,0:T(8,128)(2,1)S(1)}, bf16[128,512]{1,0:T(8,128)(2,1)S(1)}, u32[]{:S(2)}, u32[]{:S(2)}) collective-permute-start(bf16[128,512]{1,0:T(8,128)(2,1)S(1)} %get-tuple-element.108), channel_id=1, source_target_pairs={{0,1},{1,0},{2,3},{3,2},{4,5},{5,4},{6,7},{7,6},{8,9},{9,8},{10,11... | collective-permute-start | bytes 393224 | tf_op jit(solution)/shard_map/ppermute | solution.py:442
  36.5 9.3 %collective-permute-start.15 = (bf16[128,512]{1,0:T(8,128)(2,1)S(1)}, bf16[128,512]{1,0:T(8,128)(2,1)S(1)}, u32[]{:S(2)}, u32[]{:S(2)}) collective-permute-start(bf16[128,512]{1,0:T(8,128)(2,1)S(1)} %get-tuple-element.100), channel_id=1, source_target_pairs={{0,1},{1,0},{2,3},{3,2},{4,5},{5,4},{6,7},{7,6},{8,9},{9,8},{10,11... | collective-permute-start | bytes 393224 | tf_op jit(solution)/shard_map/ppermute | solution.py:442
  40.9 7.3 %collective-permute-start.17 = (bf16[128,512]{1,0:T(8,128)(2,1)S(1)}, bf16[128,512]{1,0:T(8,128)(2,1)S(1)}, u32[]{:S(2)}, u32[]{:S(2)}) collective-permute-start(bf16[128,512]{1,0:T(8,128)(2,1)S(1)} %relay_total.3), channel_id=1, source_target_pairs={{0,16},{1,17},{2,18},{3,19},{4,20},{5,21},{6,22},{7,23},{8,24},{9,... | collective-permute-start | bytes 393224 | tf_op jit(solution)/shard_map/ppermute | solution.py:442
  43.6 4.7 %collective-permute-start.19 = (bf16[128,512]{1,0:T(8,128)(2,1)S(1)}, bf16[128,512]{1,0:T(8,128)(2,1)S(1)}, u32[]{:S(2)}, u32[]{:S(2)}) collective-permute-start(bf16[128,512]{1,0:T(8,128)(2,1)S(1)} %get-tuple-element.109), channel_id=1, source_target_pairs={{0,2},{1,3},{2,0},{3,1},{4,6},{5,7},{6,4},{7,5},{8,10},{9,11},{10,... | collective-permute-start | bytes 393224 | tf_op jit(solution)/shard_map/ppermute | solution.py:442
  43.6 5.2 %collective-permute-start.21 = (bf16[128,512]{1,0:T(8,128)(2,1)S(1)}, bf16[128,512]{1,0:T(8,128)(2,1)S(1)}, u32[]{:S(2)}, u32[]{:S(2)}) collective-permute-start(bf16[128,512]{1,0:T(8,128)(2,1)S(1)} %get-tuple-element.112), channel_id=1, source_target_pairs={{0,3},{1,2},{2,1},{3,0},{4,7},{5,6},{6,5},{7,4},{8,11},{9,10},{10,... | collective-permute-start | bytes 393224 | tf_op jit(solution)/shard_map/ppermute | solution.py:442
  45.0 7.3 %collective-permute-start.18 = (bf16[128,512]{1,0:T(8,128)(2,1)S(1)}, bf16[128,512]{1,0:T(8,128)(2,1)S(1)}, u32[]{:S(2)}, u32[]{:S(2)}) collective-permute-start(bf16[128,512]{1,0:T(8,128)(2,1)S(1)} %get-tuple-element.111), channel_id=1, source_target_pairs={{0,1},{1,0},{2,3},{3,2},{4,5},{5,4},{6,7},{7,6},{8,9},{9,8},{10,11... | collective-permute-start | bytes 393224 | tf_op jit(solution)/shard_map/ppermute | solution.py:442
  45.8 9.5 %collective-permute-start.20 = (bf16[128,512]{1,0:T(8,128)(2,1)S(1)}, bf16[128,512]{1,0:T(8,128)(2,1)S(1)}, u32[]{:S(2)}, u32[]{:S(2)}) collective-permute-start(bf16[128,512]{1,0:T(8,128)(2,1)S(1)} %relay_total.2), channel_id=1, source_target_pairs={{0,18},{1,19},{2,16},{3,17},{4,22},{5,23},{6,20},{7,21},{8,26},{9,... | collective-permute-start | bytes 393224 | tf_op jit(solution)/shard_map/ppermute | solution.py:442

commit v14 on v13

--- a/solution.py
+++ b/solution.py
@@ -315,33 +315,37 @@
     block = out_refs[0].shape[0] // len(z_steps)
     dp_rank = lax.axis_index("dp")
     x_rank = lax.axis_index("ctx")
-    core = lax.rem(dp_rank + core_steps, CORES)
     z_rank = lax.div(dp_rank, CORES * MIDDLE * NEAR)
     size = ctx_count * block
-    for at, step in enumerate(z_steps):
-        start = (core * far + lax.rem(z_rank + step, far)) * size
-        here = pl.ds(pl.multiple_of(start, size), size)
-        cut = g_refs[0].shape[0]
-        total = dot(own_ref[here, :cut], g_refs[0][...], NN)
-        total = total + dot(sibling_ref[here, :cut], g_refs[1][...], NN)
-        total = total + dot(own_ref[here, cut:], g_refs[2][...], NN)
-        buf[...] = total + dot(sibling_ref[here, cut:], g_refs[3][...], NN)
-        for x, out_ref in enumerate(out_refs):
-            start = lax.rem(x_rank + x, ctx_count) * block
-            out_ref[at * block : (at + 1) * block, :] = buf[
-                pl.ds(pl.multiple_of(start, block), block), :
-            ].astype(out_ref.dtype)
-
-
-def weight_call(core_steps, z_steps, far, ctx_count, tokens, grads, kept):
+    cut = g_refs[0].shape[0]
+    for i, core_step in enumerate(core_steps):
+        core = lax.rem(dp_rank + core_step, CORES)
+        for at, step in enumerate(z_steps):
+            start = (core * far + lax.rem(z_rank + step, far)) * size
+            here = pl.ds(pl.multiple_of(start, size), size)
+            total = dot(own_ref[here, :cut], g_refs[0][...], NN)
+            total = total + dot(sibling_ref[here, :cut], g_refs[1][...], NN)
+            total = total + dot(own_ref[here, cut:], g_refs[2][...], NN)
+            buf[...] = total + dot(sibling_ref[here, cut:], g_refs[3][...], NN)
+            for x in range(ctx_count):
+                out_ref = out_refs[i * ctx_count + x]
+                start = lax.rem(x_rank + x, ctx_count) * block
+                out_ref[at * block : (at + 1) * block, :] = buf[
+                    pl.ds(pl.multiple_of(start, block), block), :
+                ].astype(out_ref.dtype)
+
+
+def weight_call(core_steps, z_steps, far, ctx_count, tokens, grads):
     height = tokens[0].shape[0] // (CORES * far)
     width = grads[0].shape[1]
     dims = (height // ctx_count * len(z_steps), width)
+    out_shape = [shape(dims, jnp.float32)] + [shape(dims, jnp.bfloat16)] * (ctx_count - 1)
+    out_shape += [shape(dims, jnp.bfloat16)] * (ctx_count * (len(core_steps) - 1))
     return pl.pallas_call(
         functools.partial(weight_kernel, core_steps, z_steps, far, ctx_count),
         in_specs=[WHOLE] * 6,
-        out_specs=[WHOLE] * ctx_count,
-        out_shape=[shape(dims, kept)] + [shape(dims, jnp.bfloat16)] * (ctx_count - 1),
+        out_specs=[WHOLE] * len(out_shape),
+        out_shape=out_shape,
         scratch_shapes=[pltpu.VMEM((height, width), jnp.float32)],
         compiler_params=PARAMS,
         cost_estimate=COST,
@@ -478,24 +482,24 @@
     last = stack_call([after(over_both, grads)], EARLY)
     grads = grads + last
     tokens = [tokens, after(send(tokens, core_steps=1), last)]
-    weights = functools.partial(
-        weight_call, far=far, ctx_count=ctx_count, tokens=tokens, kept=jnp.float32
-    )
+    weights = functools.partial(weight_call, far=far, ctx_count=ctx_count, tokens=tokens)
     steps = tuple(range(1, far))
     away, arrived, from_far = [], [], []
     for core in range(CORES):
-        kept, *blocks = weights(core, steps, grads=grads)
+        kept, *blocks = weights((core,), steps, grads=grads)
         grads = after(grads, kept)
         away.append(kept)
         arrived.append([send(value, s) for s, value in enumerate(blocks, 1)])
-    own_block, *near = weights(0, (0,), grads=grads)
-    cross_block, *cross_near = weights(1, (0,), grads=grads, kept=jnp.bfloat16)
-    arrived[0] = after(arrived[0], (own_block, cross_block))
+    blocks = weights(tuple(range(CORES)), (0,), grads=grads)
+    own_block, near = blocks[0], blocks[1:ctx_count]
+    cross_block, cross_near = blocks[ctx_count], blocks[ctx_count + 1 :]
+    arrived[0] = after(arrived[0], own_block)
+    near_arrived = [send(v, s) for s, v in enumerate(near, 1)]
     for core in range(CORES):
         relayed = relay_call(far - 1, away[core], arrived[core])
         from_far.append([send(value, 0, core, s) for s, value in enumerate(relayed, 1)])
-    own_scores = after(own_scores, relayed)
-    same = [own_block, early_call(from_far[0])] + [send(v, s) for s, v in enumerate(near, 1)]
+    cross_block, cross_near, own_scores = after((cross_block, cross_near, own_scores), relayed)
+    same = [early_call([own_block] + near_arrived + from_far[0])]
     cross = [send(cross_block, core_steps=1)] + from_far[1]
     cross += [send(value, s, 1) for s, value in enumerate(cross_near, 1)]
     query_gradient = query_call(

time: 56.3 us -> 54.4 us (0.966)
  waiting for transfers between devices: 18.2 us -> 14.2 us
  starting transfers between devices: 24.1 us -> 26.3 us
    ppermute x22, waiting for transfers between devices: 18.2 us -> 14.2 us  [send(): return lax.ppermute(value, ('dp', 'ctx'), pairs)]
    ppermute x22, starting transfers between devices: 24.1 us -> 26.3 us  [send(): return lax.ppermute(value, ('dp', 'ctx'), pairs)]
    pallas_call x4 -> x3, Pallas kernels: 2.47 us -> 2.29 us  [weight_call(): pl.pallas_call(functools.partial(weight_kernel, core_steps, z_steps, far,...]
  transfers between devices with their start and end apart: 22 -> 22, of which waited for: 13 -> 14; matrix products, arithmetic and copies ran while one was open for 0% -> 0% of each run, Pallas kernels for 21% -> 21%
where the time goes in v14:
time: 54.4 us; the launch traced here: 54.2 us
  starting transfers between devices  26.3 us (48%)
  waiting for transfers between devices  14.2 us (26%)
  Pallas kernels  12.9 us (24%)
  between operations  0.79 us (1%)
    ppermute x22, starting transfers between devices, send(): return lax.ppermute(value, ('dp', 'ctx'), pairs)  26.3 us
    ppermute x22, waiting for transfers between devices, send(): return lax.ppermute(value, ('dp', 'ctx'), pairs)  14.2 us
    pallas_call x2, Pallas kernels, block_call(): pl.pallas_call(functools.partial(block_kernel, ctx_count, step), in_specs...  5.5 us
    pallas_call x3, Pallas kernels, weight_call(): pl.pallas_call(functools.partial(weight_kernel, core_steps, z_steps, far,...  2.29 us
    pallas_call x1, Pallas kernels, pieces_call(): pl.pallas_call(functools.partial(pieces_kernel, far, len(wanted)), in_spe...  1.94 us
    pallas_call x1, Pallas kernels, query_call(): pl.pallas_call(functools.partial(query_kernel, len(keys)), in_specs=[WHOL...  1.73 us
  transfers between devices with their start and end apart: 22, of which 14 were waited for; matrix products, arithmetic and copies ran while one was open for 0% of the time, Pallas kernels for 21%

profile of v14, /device:TPU:0, one launch (start us, length us, event | category | flops | bytes accessed | tf_op | source)
XLA Modules:
  0.0 54.2 jit_solution(9363588429381069928)
XLA Ops:
  0.6 3.0 %collective-permute-start.1 = (bf16[128,512]{1,0:T(8,128)(2,1)}, bf16[128,512]{1,0:T(8,128)(2,1)S(1)}, u32[]{:S(2)}, u32[]{:S(2)}) collective-permute-start(bf16[128,512]{1,0:T(8,128)(2,1)} %refs_4_.1), channel_id=1, source_target_pairs={{0,1},{1,0},{2,3},{3,2},{4,5},{5,4},{6,7},{7,6},{8,9},{9,8},{10,11... | collective-permute-start | bytes 393224 | tf_op jit(solution)/shard_map/ppermute | solution.py:446
  3.6 0.1 collective-permute-start
  3.7 1.9 %pieces.1 = (bf16[128,1024]{1,0:T(8,128)(2,1)S(1)}, bf16[128,1024]{1,0:T(8,128)(2,1)S(1)}, bf16[128,1024]{1,0:T(8,128)(2,1)S(1)}, bf16[128,1024]{1,0:T(8,128)(2,...) custom-call(bf16[128,4096]{1,0:T(8,128)(2,1)} %in_hbm.1, bf16[128,4096]{1,0:T(8,128)(2,1)} %refs_0_.3, ...), custom_call_target="tpu_custom_call" | custom-call | flops 1024 | bytes 1024 | tf_op jit(solution)/shard_map/pieces/pallas_call | solution.py:203
  5.7 2.1 %collective-permute-start.3 = (bf16[128,1024]{1,0:T(8,128)(2,1)S(1)}, bf16[128,1024]{1,0:T(8,128)(2,1)S(1)}, u32[]{:S(2)}, u32[]{:S(2)}) collective-permute-start(bf16[128,1024]{1,0:T(8,128)(2,1)S(1)} %get-tuple-element.68), channel_id=1, source_target_pairs={{0,8},{1,9},{2,10},{3,11},{4,12},{5,13},{6,14},{7,15},{8,0},{9,1},... | collective-permute-start | bytes 786440 | tf_op jit(solution)/shard_map/ppermute | solution.py:446
  7.8 1.5 %collective-permute-start.4 = (bf16[128,1024]{1,0:T(8,128)(2,1)S(1)}, bf16[128,1024]{1,0:T(8,128)(2,1)S(1)}, u32[]{:S(2)}, u32[]{:S(2)}) collective-permute-start(bf16[128,1024]{1,0:T(8,128)(2,1)S(1)} %get-tuple-element.70), channel_id=1, source_target_pairs={{0,4},{1,5},{2,6},{3,7},{4,0},{5,1},{6,2},{7,3},{8,12},{9,13},{10,... | collective-permute-start | bytes 786440 | tf_op jit(solution)/shard_map/ppermute | solution.py:446
  9.3 0.0 collective-permute-start.5
  9.3 0.0 collective-permute-done.1.refs_4_
  9.3 0.8 %collective-permute-done.refs_3_ = bf16[128,512]{1,0:T(8,128)(2,1)S(1)} collective-permute-done((bf16[128,512]{1,0:T(8,128)(2,1)}, bf16[128,512]{1,0:T(8,128)(2,1)S(1)}, u32[]{:S(2)}, u32[]{:S(2)}) %collective-permute-start) | collective-permute-done | bytes 131104 | tf_op jit(solution)/shard_map/ppermute | solution.py:446
  10.2 3.1 %visiting_keys.1 = (bf16[128,4096]{1,0:T(8,128)(2,1)S(1)}, bf16[128,512]{1,0:T(8,128)(2,1)S(1)}, bf16[128,512]{1,0:T(8,128)(2,1)S(1)}, f32[32,128]{1,0:T(8,128)S(1)}) custom-call(s32[1,4]{1,0:T(1,128)} %refs_0_.5, bf16[128,4096]{1,0:T(8,128)(2,1)S(1)} %copy-done, bf16[128,4096]{1,0:T(8,128)(2,1)S(1)} %copy-done.1, ...), custom_call_target="tpu_custom_call" | custom-call | flops 5000000000 | bytes 1024 | tf_op jit(solution)/shard_map/visiting_keys/pallas_call | solution.py:128
  13.3 1.8 %collective-permute-start.2 = (bf16[128,512]{1,0:T(8,128)(2,1)S(1)}, bf16[128,512]{1,0:T(8,128)(2,1)S(1)}, u32[]{:S(2)}, u32[]{:S(2)}) collective-permute-start(bf16[128,512]{1,0:T(8,128)(2,1)S(1)} %get-tuple-element.63), channel_id=1, source_target_pairs={{0,1},{1,0},{2,3},{3,2},{4,5},{5,4},{6,7},{7,6},{8,9},{9,8},{10,11... | collective-permute-start | bytes 393224 | tf_op jit(solution)/shard_map/ppermute | solution.py:446
  15.1 2.4 %own_keys.1 = (bf16[128,4096]{1,0:T(8,128)(2,1)S(1)}, f32[128,512]{1,0:T(8,128)S(1)}, bf16[128,512]{1,0:T(8,128)(2,1)S(1)}) custom-call(s32[1,4]{1,0:T(1,128)} %refs_0_.5, bf16[128,4096]{1,0:T(8,128)(2,1)S(1)} %copy-done, bf16[128,4096]{1,0:T(8,128)(2,1)S(1)} %copy-done.1, bf16[128,512]{1,0:T(8,128)(2,1)S(1)} %copy-done.2, bf16[128,512]{1,0:T(8,128)(2,1)S(1)} %copy-done.3, ...), custom_call_target="tpu_custom_call" | custom-call | flops 1024 | bytes 1024 | tf_op jit(solution)/shard_map/own_keys/pallas_call | solution.py:128
  17.5 0.0 collective-permute-done.3.refs_2_
  17.5 0.5 collective-permute-start.7
  18.0 0.7 %collective-permute-done.2.refs_1_ = bf16[128,512]{1,0:T(8,128)(2,1)S(1)} collective-permute-done((bf16[128,512]{1,0:T(8,128)(2,1)S(1)}, bf16[128,512]{1,0:T(8,128)(2,1)S(1)}, u32[]{:S(2)}, u32[]{:S(2)}) %collective-permute-start.2) | collective-permute-done | bytes 131104 | tf_op jit(solution)/shard_map/ppermute | solution.py:446
  18.7 1.9 %collective-permute-done.4.refs_1_ = bf16[128,1024]{1,0:T(8,128)(2,1)S(1)} collective-permute-done((bf16[128,1024]{1,0:T(8,128)(2,1)S(1)}, bf16[128,1024]{1,0:T(8,128)(2,1)S(1)}, u32[]{:S(2)}, u32[]{:S(2)}) %collective-permute-start.4) | collective-permute-done | bytes 262176 | tf_op jit(solution)/shard_map/ppermute | solution.py:446
  20.6 0.4 collective-permute-done.6.refs_2_
  21.0 1.5 %collective-permute-start.9 = (bf16[256,256]{1,0:T(8,128)(2,1)S(1)}, bf16[256,256]{1,0:T(8,128)(2,1)S(1)}, u32[]{:S(2)}, u32[]{:S(2)}) collective-permute-start(bf16[256,256]{1,0:T(8,128)(2,1)S(1)} %get-tuple-element.82.refs_0_), channel_id=1, source_target_pairs={{0,4},{1,5},{2,6},{3,7},{4,0},{5,1},{6,2},{7,3},{8,12},{9,13},{10,... | collective-permute-start | bytes 393224 | tf_op jit(solution)/shard_map/ppermute | solution.py:446
  22.6 1.6 %collective-permute-start.11 = (bf16[256,256]{1,0:T(8,128)(2,1)S(1)}, bf16[256,256]{1,0:T(8,128)(2,1)S(1)}, u32[]{:S(2)}, u32[]{:S(2)}) collective-permute-start(bf16[256,256]{1,0:T(8,128)(2,1)S(1)} %get-tuple-element.83.refs_1_), channel_id=1, source_target_pairs={{0,8},{1,9},{2,10},{3,11},{4,12},{5,13},{6,14},{7,15},{8,0},{9,1},... | collective-permute-start | bytes 393224 | tf_op jit(solution)/shard_map/ppermute | solution.py:446
  24.2 0.4 collective-permute-start.14
  24.6 0.5 %collective-permute-start.13 = (bf16[256,256]{1,0:T(8,128)(2,1)S(1)}, bf16[256,256]{1,0:T(8,128)(2,1)S(1)}, u32[]{:S(2)}, u32[]{:S(2)}) collective-permute-start(bf16[256,256]{1,0:T(8,128)(2,1)S(1)} %get-tuple-element.83.refs_1_), channel_id=1, source_target_pairs={{0,4},{1,5},{2,6},{3,7},{4,0},{5,1},{6,2},{7,3},{8,12},{9,13},{10,... | collective-permute-start | bytes 393224 | tf_op jit(solution)/shard_map/ppermute | solution.py:446
  25.2 0.3 turn_pieces.1.refs_0_
  25.5 0.1 collective-permute-start.8
  25.6 1.1 %collective-permute-done.9.refs_2_ = bf16[256,256]{1,0:T(8,128)(2,1)S(1)} collective-permute-done((bf16[256,256]{1,0:T(8,128)(2,1)S(1)}, bf16[256,256]{1,0:T(8,128)(2,1)S(1)}, u32[]{:S(2)}, u32[]{:S(2)}) %collective-permute-start.9) | collective-permute-done | bytes 131104 | tf_op jit(solution)/shard_map/ppermute | solution.py:446
  26.6 1.8 %collective-permute-start.10 = (bf16[256,256]{1,0:T(8,128)(2,1)S(1)}, bf16[256,256]{1,0:T(8,128)(2,1)S(1)}, u32[]{:S(2)}, u32[]{:S(2)}) collective-permute-start(bf16[256,256]{1,0:T(8,128)(2,1)S(1)} %collective-permute-done.9.refs_2_), channel_id=1, source_target_pairs={{0,8},{1,9},{2,10},{3,11},{4,12},{5,13},{6,14},{7,15},{8,0},{9,1},... | collective-permute-start | bytes 393224 | tf_op jit(solution)/shard_map/ppermute | solution.py:446
  28.4 0.5 collective-permute-done.11.refs_5_
  28.9 1.5 %collective-permute-start.12 = (bf16[256,256]{1,0:T(8,128)(2,1)S(1)}, bf16[256,256]{1,0:T(8,128)(2,1)S(1)}, u32[]{:S(2)}, u32[]{:S(2)}) collective-permute-start(bf16[256,256]{1,0:T(8,128)(2,1)S(1)} %collective-permute-done.11.refs_5_), channel_id=1, source_target_pairs={{0,4},{1,5},{2,6},{3,7},{4,0},{5,1},{6,2},{7,3},{8,12},{9,13},{10,... | collective-permute-start | bytes 393224 | tf_op jit(solution)/shard_map/ppermute | solution.py:446
  30.5 1.3 %collective-permute-done.14.refs_4_ = bf16[256,256]{1,0:T(8,128)(2,1)S(1)} collective-permute-done((bf16[256,256]{1,0:T(8,128)(2,1)S(1)}, bf16[256,256]{1,0:T(8,128)(2,1)S(1)}, u32[]{:S(2)}, u32[]{:S(2)}) %collective-permute-start.14) | collective-permute-done | bytes 131104 | tf_op jit(solution)/shard_map/ppermute | solution.py:446
  31.8 0.0 collective-permute-done.13.refs_3_
  31.8 0.1 stack_grads.2
  31.8 1.8 %collective-permute-done.10.refs_0_ = bf16[256,256]{1,0:T(8,128)(2,1)S(1)} collective-permute-done((bf16[256,256]{1,0:T(8,128)(2,1)S(1)}, bf16[256,256]{1,0:T(8,128)(2,1)S(1)}, u32[]{:S(2)}, u32[]{:S(2)}) %collective-permute-start.10) | collective-permute-done | bytes 131104 | tf_op jit(solution)/shard_map/ppermute | solution.py:446
  33.7 0.3 collective-permute-done.12.refs_1_
  33.9 0.6 %weight_far.2 = (f32[128,512]{1,0:T(8,128)S(1)}, bf16[128,512]{1,0:T(8,128)(2,1)S(1)}) custom-call(bf16[1024,512]{1,0:T(8,128)(2,1)S(1)} %turn_pieces.1.refs_0_, bf16[1024,512]{1,0:T(8,128)(2,1)S(1)} %collective-permute-done.8.refs_1_, bf16[384,512]{1,0:T(8,128)(2,1)S(1)} %get-tuple-element.101.refs_2_, bf16[384,512]{1,0:T(8,128)(2,1)S(1)} %get-tuple-element.102.refs_3_, ...), custom_call_target="tpu_custom_call" | custom-call | flops 1024 | bytes 1024 | tf_op jit(solution)/shard_map/weight_far/pallas_call | solution.py:344
  34.6 1.3 %collective-permute-start.17 = (bf16[128,512]{1,0:T(8,128)(2,1)S(1)}, bf16[128,512]{1,0:T(8,128)(2,1)S(1)}, u32[]{:S(2)}, u32[]{:S(2)}) collective-permute-start(bf16[128,512]{1,0:T(8,128)(2,1)S(1)} %get-tuple-element.113), channel_id=1, source_target_pairs={{0,1},{1,0},{2,3},{3,2},{4,5},{5,4},{6,7},{7,6},{8,9},{9,8},{10,11... | collective-permute-start | bytes 393224 | tf_op jit(solution)/shard_map/ppermute | solution.py:446
  35.8 0.6 %weight_far.3 = (f32[128,512]{1,0:T(8,128)S(1)}, bf16[128,512]{1,0:T(8,128)(2,1)S(1)}) custom-call(bf16[1024,512]{1,0:T(8,128)(2,1)S(1)} %turn_pieces.1.refs_0_, bf16[1024,512]{1,0:T(8,128)(2,1)S(1)} %collective-permute-done.8.refs_1_, bf16[384,512]{1,0:T(8,128)(2,1)S(1)} %get-tuple-element.101.refs_2_, bf16[384,512]{1,0:T(8,128)(2,1)S(1)} %get-tuple-element.102.refs_3_, ...), custom_call_target="tpu_custom_call" | custom-call | flops 1024 | bytes 1024 | tf_op jit(solution)/shard_map/weight_far/pallas_call | solution.py:344
  36.5 0.9 %collective-permute-start.15 = (bf16[128,512]{1,0:T(8,128)(2,1)S(1)}, bf16[128,512]{1,0:T(8,128)(2,1)S(1)}, u32[]{:S(2)}, u32[]{:S(2)}) collective-permute-start(bf16[128,512]{1,0:T(8,128)(2,1)S(1)} %get-tuple-element.108), channel_id=1, source_target_pairs={{0,1},{1,0},{2,3},{3,2},{4,5},{5,4},{6,7},{7,6},{8,9},{9,8},{10,11... | collective-permute-start | bytes 393224 | tf_op jit(solution)/shard_map/ppermute | solution.py:446
  37.4 1.1 %weight_near.1 = (f32[128,512]{1,0:T(8,128)S(1)}, bf16[128,512]{1,0:T(8,128)(2,1)S(1)}, bf16[128,512]{1,0:T(8,128)(2,1)S(1)}, bf16[128,512]{1,0:T(8,128)(2,1)S(1)}) custom-call(bf16[1024,512]{1,0:T(8,128)(2,1)S(1)} %turn_pieces.1.refs_0_, bf16[1024,512]{1,0:T(8,128)(2,1)S(1)} %collective-permute-done.8.refs_1_, ...), custom_call_target="tpu_custom_call" | custom-call | flops 1024 | bytes 1024 | tf_op jit(solution)/shard_map/weight_near/pallas_call | solution.py:344
  38.4 1.3 %collective-permute-start.16 = (bf16[128,512]{1,0:T(8,128)(2,1)S(1)}, bf16[128,512]{1,0:T(8,128)(2,1)S(1)}, u32[]{:S(2)}, u32[]{:S(2)}) collective-permute-start(bf16[128,512]{1,0:T(8,128)(2,1)S(1)} %get-tuple-element.112), channel_id=1, source_target_pairs={{0,1},{1,0},{2,3},{3,2},{4,5},{5,4},{6,7},{7,6},{8,9},{9,8},{10,11... | collective-permute-start | bytes 393224 | tf_op jit(solution)/shard_map/ppermute | solution.py:446
  39.7 1.2 %collective-permute-done.17.refs_0_ = bf16[128,512]{1,0:T(8,128)(2,1)S(1)} collective-permute-done((bf16[128,512]{1,0:T(8,128)(2,1)S(1)}, bf16[128,512]{1,0:T(8,128)(2,1)S(1)}, u32[]{:S(2)}, u32[]{:S(2)}) %collective-permute-start.17) | collective-permute-done | bytes 131104 | tf_op jit(solution)/shard_map/ppermute | solution.py:446
  40.9 2.7 %collective-permute-start.18 = (bf16[128,512]{1,0:T(8,128)(2,1)S(1)}, bf16[128,512]{1,0:T(8,128)(2,1)S(1)}, u32[]{:S(2)}, u32[]{:S(2)}) collective-permute-start(bf16[128,512]{1,0:T(8,128)(2,1)S(1)} %relay_total.3), channel_id=1, source_target_pairs={{0,16},{1,17},{2,18},{3,19},{4,20},{5,21},{6,22},{7,23},{8,24},{9,... | collective-permute-start | bytes 393224 | tf_op jit(solution)/shard_map/ppermute | solution.py:446
  43.6 0.1 collective-permute-done.15.refs_0_
  43.7 0.1 collective-permute-start.20
  43.8 2.7 %collective-permute-start.19 = (bf16[128,512]{1,0:T(8,128)(2,1)S(1)}, bf16[128,512]{1,0:T(8,128)(2,1)S(1)}, u32[]{:S(2)}, u32[]{:S(2)}) collective-permute-start(bf16[128,512]{1,0:T(8,128)(2,1)S(1)} %get-tuple-element.115), channel_id=1, source_target_pairs={{0,2},{1,3},{2,0},{3,1},{4,6},{5,7},{6,4},{7,5},{8,10},{9,11},{10,... | collective-permute-start | bytes 393224 | tf_op jit(solution)/shard_map/ppermute | solution.py:446
  46.5 0.9 %collective-permute-start.21 = (bf16[128,512]{1,0:T(8,128)(2,1)S(1)}, bf16[128,512]{1,0:T(8,128)(2,1)S(1)}, u32[]{:S(2)}, u32[]{:S(2)}) collective-permute-start(bf16[128,512]{1,0:T(8,128)(2,1)S(1)} %get-tuple-element.116), channel_id=1, source_target_pairs={{0,3},{1,2},{2,1},{3,0},{4,7},{5,6},{6,5},{7,4},{8,11},{9,10},{10,... | collective-permute-start | bytes 393224 | tf_op jit(solution)/shard_map/ppermute | solution.py:446
  47.4 1.7 %query_gradient.1 = bf16[128,4096]{1,0:T(8,128)(2,1)} custom-call(bf16[128,4096]{1,0:T(8,128)(2,1)S(1)} %get-tuple-element.109.refs_0_, bf16[128,4096]{1,0:T(8,128)(2,1)S(1)} %get-tuple-element.110.refs_1_, bf16[128,512]{1,0:T(8,128)(2,1)S(1)} %copy-done.2, bf16[128,512]{1,0:T(8,128)(2,1)S(1)} %collective-permute-done.refs_3_), custom_call_target="tpu_custom_call" | custom-call | flops 1024 | bytes 1024 | tf_op jit(solution)/shard_map/query_gradient/pallas_call | solution.py:155
  49.1 2.4 %collective-permute-done.18.refs_2_ = bf16[128,512]{1,0:T(8,128)(2,1)S(1)} collective-permute-done((bf16[128,512]{1,0:T(8,128)(2,1)S(1)}, bf16[128,512]{1,0:T(8,128)(2,1)S(1)}, u32[]{:S(2)}, u32[]{:S(2)}) %collective-permute-start.18) | collective-permute-done | bytes 131104 | tf_op jit(solution)/shard_map/ppermute | solution.py:446
  51.6 0.5 collective-permute-done.21.refs_3_
  52.1 1.2 %collective-permute-done.20.refs_2_ = bf16[128,512]{1,0:T(8,128)(2,1)S(1)} collective-permute-done((bf16[128,512]{1,0:T(8,128)(2,1)S(1)}, bf16[128,512]{1,0:T(8,128)(2,1)S(1)}, u32[]{:S(2)}, u32[]{:S(2)}) %collective-permute-start.20) | collective-permute-done | bytes 131104 | tf_op jit(solution)/shard_map/ppermute | solution.py:446
  53.3 0.8 %weight_total.1 = (f32[128,512]{1,0:T(8,128)}, f32[128,512]{1,0:T(8,128)}) custom-call(f32[128,512]{1,0:T(8,128)S(1)} %early_total.1.refs_0_, bf16[128,512]{1,0:T(8,128)(2,1)S(1)} %collective-permute-done.19.refs_1_, bf16[128,512]{1,0:T(8,128)(2,1)S(1)} %collective-permute-done.20.refs_2_, bf16[128,512]{1,0:T(8,128)(2,1)S(1)} %collective-permute-done.21.refs_3_), custom_call_target="tpu_custom_call" | custom-call | flops 1024 | bytes 1024 | tf_op jit(solution)/shard_map/weight_total/pallas_call | solution.py:413
  (20 shorter events, 0.2 us)
Async XLA Ops:
  0.6 8.7 %collective-permute-start.1 = (bf16[128,512]{1,0:T(8,128)(2,1)}, bf16[128,512]{1,0:T(8,128)(2,1)S(1)}, u32[]{:S(2)}, u32[]{:S(2)}) collective-permute-start(bf16[128,512]{1,0:T(8,128)(2,1)} %refs_4_.1), channel_id=1, source_target_pairs={{0,1},{1,0},{2,3},{3,2},{4,5},{5,4},{6,7},{7,6},{8,9},{9,8},{10,11... | collective-permute-start | bytes 393224 | tf_op jit(solution)/shard_map/ppermute | solution.py:446
  3.6 6.5 %collective-permute-start = (bf16[128,512]{1,0:T(8,128)(2,1)}, bf16[128,512]{1,0:T(8,128)(2,1)S(1)}, u32[]{:S(2)}, u32[]{:S(2)}) collective-permute-start(bf16[128,512]{1,0:T(8,128)(2,1)} %refs_2_.5), channel_id=1, source_target_pairs={{0,1},{1,0},{2,3},{3,2},{4,5},{5,4},{6,7},{7,6},{8,9},{9,8},{10,11... | collective-permute-start | bytes 393224 | tf_op jit(solution)/shard_map/ppermute | solution.py:446
  3.7 6.4 %copy-start = (bf16[128,4096]{1,0:T(8,128)(2,1)S(1)}, bf16[128,4096]{1,0:T(8,128)(2,1)}, u32[]{:S(2)}) copy-start(bf16[128,4096]{1,0:T(8,128)(2,1)} %refs_1_.3) | copy-start | bytes 3145732
  3.7 6.4 %copy-start.1 = (bf16[128,4096]{1,0:T(8,128)(2,1)S(1)}, bf16[128,4096]{1,0:T(8,128)(2,1)}, u32[]{:S(2)}) copy-start(bf16[128,4096]{1,0:T(8,128)(2,1)} %refs_2_.4) | copy-start | bytes 3145732
  5.7 11.8 %collective-permute-start.3 = (bf16[128,1024]{1,0:T(8,128)(2,1)S(1)}, bf16[128,1024]{1,0:T(8,128)(2,1)S(1)}, u32[]{:S(2)}, u32[]{:S(2)}) collective-permute-start(bf16[128,1024]{1,0:T(8,128)(2,1)S(1)} %get-tuple-element.68), channel_id=1, source_target_pairs={{0,8},{1,9},{2,10},{3,11},{4,12},{5,13},{6,14},{7,15},{8,0},{9,1},... | collective-permute-start | bytes 786440 | tf_op jit(solution)/shard_map/ppermute | solution.py:446
  7.8 12.8 %collective-permute-start.4 = (bf16[128,1024]{1,0:T(8,128)(2,1)S(1)}, bf16[128,1024]{1,0:T(8,128)(2,1)S(1)}, u32[]{:S(2)}, u32[]{:S(2)}) collective-permute-start(bf16[128,1024]{1,0:T(8,128)(2,1)S(1)} %get-tuple-element.70), channel_id=1, source_target_pairs={{0,4},{1,5},{2,6},{3,7},{4,0},{5,1},{6,2},{7,3},{8,12},{9,13},{10,... | collective-permute-start | bytes 786440 | tf_op jit(solution)/shard_map/ppermute | solution.py:446
  9.3 11.3 %collective-permute-start.5 = (bf16[128,1024]{1,0:T(8,128)(2,1)S(1)}, bf16[128,1024]{1,0:T(8,128)(2,1)S(1)}, u32[]{:S(2)}, u32[]{:S(2)}) collective-permute-start(bf16[128,1024]{1,0:T(8,128)(2,1)S(1)} %get-tuple-element.71), channel_id=1, source_target_pairs={{0,12},{1,13},{2,14},{3,15},{4,8},{5,9},{6,10},{7,11},{8,4},{9,5},... | collective-permute-start | bytes 786440 | tf_op jit(solution)/shard_map/ppermute | solution.py:446
  10.2 5.0 %copy-start.2 = (bf16[128,512]{1,0:T(8,128)(2,1)S(1)}, bf16[128,512]{1,0:T(8,128)(2,1)}, u32[]{:S(2)}) copy-start(bf16[128,512]{1,0:T(8,128)(2,1)} %refs_2_.5) | copy-start | bytes 393220
  10.2 5.0 %copy-start.3 = (bf16[128,512]{1,0:T(8,128)(2,1)S(1)}, bf16[128,512]{1,0:T(8,128)(2,1)}, u32[]{:S(2)}) copy-start(bf16[128,512]{1,0:T(8,128)(2,1)} %refs_4_.1) | copy-start | bytes 393220
  13.3 5.4 %collective-permute-start.2 = (bf16[128,512]{1,0:T(8,128)(2,1)S(1)}, bf16[128,512]{1,0:T(8,128)(2,1)S(1)}, u32[]{:S(2)}, u32[]{:S(2)}) collective-permute-start(bf16[128,512]{1,0:T(8,128)(2,1)S(1)} %get-tuple-element.63), channel_id=1, source_target_pairs={{0,1},{1,0},{2,3},{3,2},{4,5},{5,4},{6,7},{7,6},{8,9},{9,8},{10,11... | collective-permute-start | bytes 393224 | tf_op jit(solution)/shard_map/ppermute | solution.py:446
  15.1 5.8 %collective-permute-start.6 = (bf16[128,512]{1,0:T(8,128)(2,1)S(1)}, bf16[128,512]{1,0:T(8,128)(2,1)S(1)}, u32[]{:S(2)}, u32[]{:S(2)}) collective-permute-start(bf16[128,512]{1,0:T(8,128)(2,1)S(1)} %get-tuple-element.78), channel_id=1, source_target_pairs={{0,3},{1,2},{2,1},{3,0},{4,7},{5,6},{6,5},{7,4},{8,11},{9,10},{10,... | collective-permute-start | bytes 393224 | tf_op jit(solution)/shard_map/ppermute | solution.py:446
  17.5 3.5 %collective-permute-start.7 = (bf16[128,512]{1,0:T(8,128)(2,1)S(1)}, bf16[128,512]{1,0:T(8,128)(2,1)S(1)}, u32[]{:S(2)}, u32[]{:S(2)}) collective-permute-start(bf16[128,512]{1,0:T(8,128)(2,1)S(1)} %get-tuple-element.81), channel_id=1, source_target_pairs={{0,2},{1,3},{2,0},{3,1},{4,6},{5,7},{6,4},{7,5},{8,10},{9,11},{10,... | collective-permute-start | bytes 393224 | tf_op jit(solution)/shard_map/ppermute | solution.py:446
  21.0 5.6 %collective-permute-start.9 = (bf16[256,256]{1,0:T(8,128)(2,1)S(1)}, bf16[256,256]{1,0:T(8,128)(2,1)S(1)}, u32[]{:S(2)}, u32[]{:S(2)}) collective-permute-start(bf16[256,256]{1,0:T(8,128)(2,1)S(1)} %get-tuple-element.82.refs_0_), channel_id=1, source_target_pairs={{0,4},{1,5},{2,6},{3,7},{4,0},{5,1},{6,2},{7,3},{8,12},{9,13},{10,... | collective-permute-start | bytes 393224 | tf_op jit(solution)/shard_map/ppermute | solution.py:446
  22.6 6.4 %collective-permute-start.11 = (bf16[256,256]{1,0:T(8,128)(2,1)S(1)}, bf16[256,256]{1,0:T(8,128)(2,1)S(1)}, u32[]{:S(2)}, u32[]{:S(2)}) collective-permute-start(bf16[256,256]{1,0:T(8,128)(2,1)S(1)} %get-tuple-element.83.refs_1_), channel_id=1, source_target_pairs={{0,8},{1,9},{2,10},{3,11},{4,12},{5,13},{6,14},{7,15},{8,0},{9,1},... | collective-permute-start | bytes 393224 | tf_op jit(solution)/shard_map/ppermute | solution.py:446
  24.2 7.6 %collective-permute-start.14 = (bf16[256,256]{1,0:T(8,128)(2,1)S(1)}, bf16[256,256]{1,0:T(8,128)(2,1)S(1)}, u32[]{:S(2)}, u32[]{:S(2)}) collective-permute-start(bf16[256,256]{1,0:T(8,128)(2,1)S(1)} %get-tuple-element.82.refs_0_), channel_id=1, source_target_pairs={{0,8},{1,9},{2,10},{3,11},{4,12},{5,13},{6,14},{7,15},{8,0},{9,1},... | collective-permute-start | bytes 393224 | tf_op jit(solution)/shard_map/ppermute | solution.py:446
  24.6 7.1 %collective-permute-start.13 = (bf16[256,256]{1,0:T(8,128)(2,1)S(1)}, bf16[256,256]{1,0:T(8,128)(2,1)S(1)}, u32[]{:S(2)}, u32[]{:S(2)}) collective-permute-start(bf16[256,256]{1,0:T(8,128)(2,1)S(1)} %get-tuple-element.83.refs_1_), channel_id=1, source_target_pairs={{0,4},{1,5},{2,6},{3,7},{4,0},{5,1},{6,2},{7,3},{8,12},{9,13},{10,... | collective-permute-start | bytes 393224 | tf_op jit(solution)/shard_map/ppermute | solution.py:446
  25.5 8.5 %collective-permute-start.8 = (bf16[1024,512]{1,0:T(8,128)(2,1)S(1)}, bf16[1024,512]{1,0:T(8,128)(2,1)S(1)}, u32[]{:S(2)}, u32[]{:S(2)}) collective-permute-start(bf16[1024,512]{1,0:T(8,128)(2,1)S(1)} %turn_pieces.1.refs_0_), channel_id=1, source_target_pairs={{0,2},{1,3},{2,0},{3,1},{4,6},{5,7},{6,4},{7,5},{8,10},{9,11},{10,... | collective-permute-start | bytes 3145736 | tf_op jit(solution)/shard_map/ppermute | solution.py:446
  26.6 7.0 %collective-permute-start.10 = (bf16[256,256]{1,0:T(8,128)(2,1)S(1)}, bf16[256,256]{1,0:T(8,128)(2,1)S(1)}, u32[]{:S(2)}, u32[]{:S(2)}) collective-permute-start(bf16[256,256]{1,0:T(8,128)(2,1)S(1)} %collective-permute-done.9.refs_2_), channel_id=1, source_target_pairs={{0,8},{1,9},{2,10},{3,11},{4,12},{5,13},{6,14},{7,15},{8,0},{9,1},... | collective-permute-start | bytes 393224 | tf_op jit(solution)/shard_map/ppermute | solution.py:446
  28.9 5.0 %collective-permute-start.12 = (bf16[256,256]{1,0:T(8,128)(2,1)S(1)}, bf16[256,256]{1,0:T(8,128)(2,1)S(1)}, u32[]{:S(2)}, u32[]{:S(2)}) collective-permute-start(bf16[256,256]{1,0:T(8,128)(2,1)S(1)} %collective-permute-done.11.refs_5_), channel_id=1, source_target_pairs={{0,4},{1,5},{2,6},{3,7},{4,0},{5,1},{6,2},{7,3},{8,12},{9,13},{10,... | collective-permute-start | bytes 393224 | tf_op jit(solution)/shard_map/ppermute | solution.py:446
  34.6 6.3 %collective-permute-start.17 = (bf16[128,512]{1,0:T(8,128)(2,1)S(1)}, bf16[128,512]{1,0:T(8,128)(2,1)S(1)}, u32[]{:S(2)}, u32[]{:S(2)}) collective-permute-start(bf16[128,512]{1,0:T(8,128)(2,1)S(1)} %get-tuple-element.113), channel_id=1, source_target_pairs={{0,1},{1,0},{2,3},{3,2},{4,5},{5,4},{6,7},{7,6},{8,9},{9,8},{10,11... | collective-permute-start | bytes 393224 | tf_op jit(solution)/shard_map/ppermute | solution.py:446
  36.5 7.2 %collective-permute-start.15 = (bf16[128,512]{1,0:T(8,128)(2,1)S(1)}, bf16[128,512]{1,0:T(8,128)(2,1)S(1)}, u32[]{:S(2)}, u32[]{:S(2)}) collective-permute-start(bf16[128,512]{1,0:T(8,128)(2,1)S(1)} %get-tuple-element.108), channel_id=1, source_target_pairs={{0,1},{1,0},{2,3},{3,2},{4,5},{5,4},{6,7},{7,6},{8,9},{9,8},{10,11... | collective-permute-start | bytes 393224 | tf_op jit(solution)/shard_map/ppermute | solution.py:446
  38.4 10.7 %collective-permute-start.16 = (bf16[128,512]{1,0:T(8,128)(2,1)S(1)}, bf16[128,512]{1,0:T(8,128)(2,1)S(1)}, u32[]{:S(2)}, u32[]{:S(2)}) collective-permute-start(bf16[128,512]{1,0:T(8,128)(2,1)S(1)} %get-tuple-element.112), channel_id=1, source_target_pairs={{0,1},{1,0},{2,3},{3,2},{4,5},{5,4},{6,7},{7,6},{8,9},{9,8},{10,11... | collective-permute-start | bytes 393224 | tf_op jit(solution)/shard_map/ppermute | solution.py:446
  40.9 10.7 %collective-permute-start.18 = (bf16[128,512]{1,0:T(8,128)(2,1)S(1)}, bf16[128,512]{1,0:T(8,128)(2,1)S(1)}, u32[]{:S(2)}, u32[]{:S(2)}) collective-permute-start(bf16[128,512]{1,0:T(8,128)(2,1)S(1)} %relay_total.3), channel_id=1, source_target_pairs={{0,16},{1,17},{2,18},{3,19},{4,20},{5,21},{6,22},{7,23},{8,24},{9,... | collective-permute-start | bytes 393224 | tf_op jit(solution)/shard_map/ppermute | solution.py:446
  43.7 9.6 %collective-permute-start.20 = (bf16[128,512]{1,0:T(8,128)(2,1)S(1)}, bf16[128,512]{1,0:T(8,128)(2,1)S(1)}, u32[]{:S(2)}, u32[]{:S(2)}) collective-permute-start(bf16[128,512]{1,0:T(8,128)(2,1)S(1)} %relay_total.2), channel_id=1, source_target_pairs={{0,18},{1,19},{2,16},{3,17},{4,22},{5,23},{6,20},{7,21},{8,26},{9,... | collective-permute-start | bytes 393224 | tf_op jit(solution)/shard_map/ppermute | solution.py:446
  43.8 7.8 %collective-permute-start.19 = (bf16[128,512]{1,0:T(8,128)(2,1)S(1)}, bf16[128,512]{1,0:T(8,128)(2,1)S(1)}, u32[]{:S(2)}, u32[]{:S(2)}) collective-permute-start(bf16[128,512]{1,0:T(8,128)(2,1)S(1)} %get-tuple-element.115), channel_id=1, source_target_pairs={{0,2},{1,3},{2,0},{3,1},{4,6},{5,7},{6,4},{7,5},{8,10},{9,11},{10,... | collective-permute-start | bytes 393224 | tf_op jit(solution)/shard_map/ppermute | solution.py:446
  46.5 5.6 %collective-permute-start.21 = (bf16[128,512]{1,0:T(8,128)(2,1)S(1)}, bf16[128,512]{1,0:T(8,128)(2,1)S(1)}, u32[]{:S(2)}, u32[]{:S(2)}) collective-permute-start(bf16[128,512]{1,0:T(8,128)(2,1)S(1)} %get-tuple-element.116), channel_id=1, source_target_pairs={{0,3},{1,2},{2,1},{3,0},{4,7},{5,6},{6,5},{7,4},{8,11},{9,10},{10,... | collective-permute-start | bytes 393224 | tf_op jit(solution)/shard_map/ppermute | solution.py:446

commit v15 on v14

--- a/solution.py
+++ b/solution.py
@@ -167,9 +167,33 @@
     return lax.optimization_barrier((values, others))[0]
 
 
-def pieces_kernel(far, count, in_hbm, *refs):
-    far_refs, piece_refs = refs[:count], refs[count : count + MIDDLE * NEAR]
-    near_refs, (sems, near_sems) = refs[count + MIDDLE * NEAR : -2], refs[-2:]
+def near_kernel(*refs):
+    count = len(refs) // 2
+    sems = refs[-1]
+    copies = [
+        pltpu.make_async_copy(refs[i], refs[count + i], sems.at[i]) for i in range(count)
+    ]
+    for copy in copies:
+        copy.start()
+    for copy in copies:
+        copy.wait()
+
+
+def near_call(*values):
+    return pl.pallas_call(
+        near_kernel,
+        in_specs=[FAR] * len(values),
+        out_specs=[WHOLE] * len(values),
+        out_shape=[shape(value.shape, value.dtype) for value in values],
+        scratch_shapes=[pltpu.SemaphoreType.DMA((len(values),))],
+        compiler_params=PARAMS,
+        cost_estimate=COST,
+        name="bring_near",
+    )(*(pinned(value) for value in values))
+
+
+def pieces_kernel(far, in_hbm, *refs):
+    piece_refs, sems = refs[:-1], refs[-1]
     dp_rank = lax.axis_index("dp")
     y_rank = lax.rem(lax.div(dp_rank, CORES), MIDDLE)
     z_rank = lax.rem(lax.div(dp_rank, CORES * MIDDLE), NEAR)
@@ -189,31 +213,25 @@
                         sems.at[len(copies)],
                     )
                 )
-    for i, (far_ref, near_ref) in enumerate(zip(far_refs, near_refs)):
-        copies.append(pltpu.make_async_copy(far_ref, near_ref, near_sems.at[i]))
     for copy in copies:
         copy.start()
     for copy in copies:
         copy.wait()
 
 
-def pieces_call(normed, wanted, far):
+def pieces_call(normed, far):
     rows, width = normed.shape
     count = MIDDLE * NEAR
     return pl.pallas_call(
-        functools.partial(pieces_kernel, far, len(wanted)),
-        in_specs=[FAR] * (1 + len(wanted)),
-        out_specs=[WHOLE] * (count + len(wanted)),
-        out_shape=[shape((rows, width // count), normed.dtype)] * count
-        + [shape(value.shape, value.dtype) for value in wanted],
-        scratch_shapes=[
-            pltpu.SemaphoreType.DMA((count * CORES * far,)),
-            pltpu.SemaphoreType.DMA((len(wanted),)),
-        ],
+        functools.partial(pieces_kernel, far),
+        in_specs=[FAR],
+        out_specs=[WHOLE] * count,
+        out_shape=[shape((rows, width // count), normed.dtype)] * count,
+        scratch_shapes=[pltpu.SemaphoreType.DMA((count * CORES * far,))],
         compiler_params=PARAMS,
         cost_estimate=COST,
         name="pieces",
-    )(pinned(normed), *(pinned(value) for value in wanted))
+    )(pinned(normed))
 
 
 def turn_kernel(*refs):
@@ -448,7 +466,9 @@
     visiting = [
         (send(saved_keys, step), send(saved_values, step)) for step in range(1, ctx_count)
     ]
-    *pieces, other, lse = pieces_call(normed_input, (attention_output, saved_log_totals.T), far)
+    pieces = pieces_call(normed_input, far)
+    totals = after(saved_log_totals.T, pieces[0])
+    other, lse = near_call(attention_output, totals)
     pieces = [send(piece, member=i) if i else piece for i, piece in enumerate(pieces)]
     block = functools.partial(
         block_call,
@@ -490,16 +510,19 @@
         grads = after(grads, kept)
         away.append(kept)
         arrived.append([send(value, s) for s, value in enumerate(blocks, 1)])
-    blocks = weights(tuple(range(CORES)), (0,), grads=grads)
-    own_block, near = blocks[0], blocks[1:ctx_count]
-    cross_block, cross_near = blocks[ctx_count], blocks[ctx_count + 1 :]
-    arrived[0] = after(arrived[0], own_block)
-    near_arrived = [send(v, s) for s, v in enumerate(near, 1)]
     for core in range(CORES):
         relayed = relay_call(far - 1, away[core], arrived[core])
         from_far.append([send(value, 0, core, s) for s, value in enumerate(relayed, 1)])
-    cross_block, cross_near, own_scores = after((cross_block, cross_near, own_scores), relayed)
-    same = [early_call([own_block] + near_arrived + from_far[0])]
+        if core == 0:
+            grads = after(grads, relayed)
+            blocks = weights(tuple(range(CORES)), (0,), grads=grads)
+            own_block, near = blocks[0], blocks[1:ctx_count]
+            cross_block, cross_near = blocks[ctx_count], blocks[ctx_count + 1 :]
+            arrived[1] = after(arrived[1], own_block)
+    near, cross_block, cross_near, own_scores = after(
+        (near, cross_block, cross_near, own_scores), relayed
+    )
+    same = [early_call([own_block] + from_far[0])] + [send(v, s) for s, v in enumerate(near, 1)]
     cross = [send(cross_block, core_steps=1)] + from_far[1]
     cross += [send(value, s, 1) for s, value in enumerate(cross_near, 1)]
     query_gradient = query_call(

time: 54.4 us -> 54.5 us (level)
  starting transfers between devices: 26.3 us -> 23.7 us
  waiting for transfers between devices: 14.2 us -> 16.1 us
  Pallas kernels: 12.9 us -> 13.6 us
    ppermute x22, starting transfers between devices: 26.3 us -> 23.7 us  [send(): return lax.ppermute(value, ('dp', 'ctx'), pairs)]
    ppermute x22, waiting for transfers between devices: 14.2 us -> 16.1 us  [send(): return lax.ppermute(value, ('dp', 'ctx'), pairs)]
    pallas_call x1 -> x2, Pallas kernels: 1.94 us -> 2.63 us  [the longest x1 1.39 us: pieces_call(): pl.pallas_call(functools.partial(pieces_kernel, far), in_specs=[FAR], out...]
  transfers between devices with their start and end apart: 22 -> 22, of which waited for: 14 -> 11; matrix products, arithmetic and copies ran while one was open for 0% -> 0% of each run, Pallas kernels for 21% -> 22%
where the time goes in v15:
time: 54.5 us; the launch traced here: 54.2 us
  starting transfers between devices  23.7 us (43%)
  waiting for transfers between devices  16.1 us (30%)
  Pallas kernels  13.6 us (25%)
  between operations  0.82 us (2%)
    ppermute x22, starting transfers between devices, send(): return lax.ppermute(value, ('dp', 'ctx'), pairs)  23.7 us
    ppermute x22, waiting for transfers between devices, send(): return lax.ppermute(value, ('dp', 'ctx'), pairs)  16.1 us
    pallas_call x2, Pallas kernels, block_call(): pl.pallas_call(functools.partial(block_kernel, ctx_count, step), in_specs...  5.52 us
    pallas_call x3, Pallas kernels, weight_call(): pl.pallas_call(functools.partial(weight_kernel, core_steps, z_steps, far,...  2.29 us
    pallas_call x1, Pallas kernels, query_call(): pl.pallas_call(functools.partial(query_kernel, len(keys)), in_specs=[WHOL...  1.73 us
    pallas_call x1, Pallas kernels, pieces_call(): pl.pallas_call(functools.partial(pieces_kernel, far), in_specs=[FAR], out...  1.39 us
    pallas_call x1, Pallas kernels, near_call(): pl.pallas_call(near_kernel, in_specs=[FAR] * len(values), out_specs=[WHOL...  1.24 us
  transfers between devices with their start and end apart: 22, of which 11 were waited for; matrix products, arithmetic and copies ran while one was open for 0% of the time, Pallas kernels for 22%

profile of v15, /device:TPU:0, one launch (start us, length us, event | category | flops | bytes accessed | tf_op | source)
XLA Modules:
  0.0 54.2 jit_solution(557412796385362466)
XLA Ops:
  0.7 3.0 %collective-permute-start.1 = (bf16[128,512]{1,0:T(8,128)(2,1)}, bf16[128,512]{1,0:T(8,128)(2,1)S(1)}, u32[]{:S(2)}, u32[]{:S(2)}) collective-permute-start(bf16[128,512]{1,0:T(8,128)(2,1)} %refs_4_.1), channel_id=1, source_target_pairs={{0,1},{1,0},{2,3},{3,2},{4,5},{5,4},{6,7},{7,6},{8,9},{9,8},{10,11... | collective-permute-start | bytes 393224 | tf_op jit(solution)/shard_map/ppermute | solution.py:464
  3.7 0.1 collective-permute-start
  3.7 1.4 %pieces.1 = (bf16[128,1024]{1,0:T(8,128)(2,1)S(1)}, bf16[128,1024]{1,0:T(8,128)(2,1)S(1)}, bf16[128,1024]{1,0:T(8,128)(2,1)S(1)}, bf16[128,1024]{1,0:T(8,128)(2,1)S(1)}) custom-call(bf16[128,4096]{1,0:T(8,128)(2,1)} %in_hbm.1), custom_call_target="tpu_custom_call" | custom-call | flops 1024 | bytes 1024 | tf_op jit(solution)/shard_map/pieces/pallas_call | solution.py:225
  5.1 2.1 %collective-permute-start.3 = (bf16[128,1024]{1,0:T(8,128)(2,1)S(1)}, bf16[128,1024]{1,0:T(8,128)(2,1)S(1)}, u32[]{:S(2)}, u32[]{:S(2)}) collective-permute-start(bf16[128,1024]{1,0:T(8,128)(2,1)S(1)} %get-tuple-element.75), channel_id=1, source_target_pairs={{0,8},{1,9},{2,10},{3,11},{4,12},{5,13},{6,14},{7,15},{8,0},{9,1},... | collective-permute-start | bytes 786440 | tf_op jit(solution)/shard_map/ppermute | solution.py:464
  7.2 1.5 %collective-permute-start.4 = (bf16[128,1024]{1,0:T(8,128)(2,1)S(1)}, bf16[128,1024]{1,0:T(8,128)(2,1)S(1)}, u32[]{:S(2)}, u32[]{:S(2)}) collective-permute-start(bf16[128,1024]{1,0:T(8,128)(2,1)S(1)} %get-tuple-element.77), channel_id=1, source_target_pairs={{0,4},{1,5},{2,6},{3,7},{4,0},{5,1},{6,2},{7,3},{8,12},{9,13},{10,... | collective-permute-start | bytes 786440 | tf_op jit(solution)/shard_map/ppermute | solution.py:464
  8.7 0.0 collective-permute-start.5
  8.8 1.2 %bring_near.1 = (bf16[128,4096]{1,0:T(8,128)(2,1)S(1)}, f32[32,128]{1,0:T(8,128)S(1)}) custom-call(bf16[128,4096]{1,0:T(8,128)(2,1)} %refs_0_.3, f32[32,128]{1,0:T(8,128)} %bitcast.1), custom_call_target="tpu_custom_call" | custom-call | flops 1024 | bytes 1024 | tf_op jit(solution)/shard_map/bring_near/pallas_call | solution.py:183
  10.0 0.0 collective-permute-done.1.refs_4_
  10.0 0.1 collective-permute-done.refs_3_
  10.2 3.1 %visiting_keys.1 = (bf16[128,4096]{1,0:T(8,128)(2,1)S(1)}, bf16[128,512]{1,0:T(8,128)(2,1)S(1)}, bf16[128,512]{1,0:T(8,128)(2,1)S(1)}, f32[32,128]{1,0:T(8,128)S(1)}) custom-call(s32[1,4]{1,0:T(1,128)} %refs_0_.5, bf16[128,4096]{1,0:T(8,128)(2,1)S(1)} %copy-done, bf16[128,4096]{1,0:T(8,128)(2,1)S(1)} %copy-done.1, ...), custom_call_target="tpu_custom_call" | custom-call | flops 5000000000 | bytes 1024 | tf_op jit(solution)/shard_map/visiting_keys/pallas_call | solution.py:128
  13.3 1.8 %collective-permute-start.2 = (bf16[128,512]{1,0:T(8,128)(2,1)S(1)}, bf16[128,512]{1,0:T(8,128)(2,1)S(1)}, u32[]{:S(2)}, u32[]{:S(2)}) collective-permute-start(bf16[128,512]{1,0:T(8,128)(2,1)S(1)} %get-tuple-element.71), channel_id=1, source_target_pairs={{0,1},{1,0},{2,3},{3,2},{4,5},{5,4},{6,7},{7,6},{8,9},{9,8},{10,11... | collective-permute-start | bytes 393224 | tf_op jit(solution)/shard_map/ppermute | solution.py:464
  15.2 2.4 %own_keys.1 = (bf16[128,4096]{1,0:T(8,128)(2,1)S(1)}, f32[128,512]{1,0:T(8,128)S(1)}, bf16[128,512]{1,0:T(8,128)(2,1)S(1)}) custom-call(s32[1,4]{1,0:T(1,128)} %refs_0_.5, bf16[128,4096]{1,0:T(8,128)(2,1)S(1)} %copy-done, bf16[128,4096]{1,0:T(8,128)(2,1)S(1)} %copy-done.1, bf16[128,512]{1,0:T(8,128)(2,1)S(1)} %copy-done.2, bf16[128,512]{1,0:T(8,128)(2,1)S(1)} %copy-done.3, ...), custom_call_target="tpu_custom_call" | custom-call | flops 1024 | bytes 1024 | tf_op jit(solution)/shard_map/own_keys/pallas_call | solution.py:128
  17.6 0.4 collective-permute-start.7
  18.0 2.0 %collective-permute-done.4.refs_1_ = bf16[128,1024]{1,0:T(8,128)(2,1)S(1)} collective-permute-done((bf16[128,1024]{1,0:T(8,128)(2,1)S(1)}, bf16[128,1024]{1,0:T(8,128)(2,1)S(1)}, u32[]{:S(2)}, u32[]{:S(2)}) %collective-permute-start.4) | collective-permute-done | bytes 262176 | tf_op jit(solution)/shard_map/ppermute | solution.py:464
  20.0 0.0 collective-permute-done.5.refs_3_
  20.1 0.0 collective-permute-done.2.refs_1_
  20.1 0.9 %collective-permute-done.6.refs_2_ = bf16[128,512]{1,0:T(8,128)(2,1)S(1)} collective-permute-done((bf16[128,512]{1,0:T(8,128)(2,1)S(1)}, bf16[128,512]{1,0:T(8,128)(2,1)S(1)}, u32[]{:S(2)}, u32[]{:S(2)}) %collective-permute-start.6) | collective-permute-done | bytes 131104 | tf_op jit(solution)/shard_map/ppermute | solution.py:464
  21.0 0.0 collective-permute-done.7.sibling_ref
  21.1 1.5 %collective-permute-start.9 = (bf16[256,256]{1,0:T(8,128)(2,1)S(1)}, bf16[256,256]{1,0:T(8,128)(2,1)S(1)}, u32[]{:S(2)}, u32[]{:S(2)}) collective-permute-start(bf16[256,256]{1,0:T(8,128)(2,1)S(1)} %get-tuple-element.89.refs_0_), channel_id=1, source_target_pairs={{0,4},{1,5},{2,6},{3,7},{4,0},{5,1},{6,2},{7,3},{8,12},{9,13},{10,... | collective-permute-start | bytes 393224 | tf_op jit(solution)/shard_map/ppermute | solution.py:464
  22.6 1.6 %collective-permute-start.11 = (bf16[256,256]{1,0:T(8,128)(2,1)S(1)}, bf16[256,256]{1,0:T(8,128)(2,1)S(1)}, u32[]{:S(2)}, u32[]{:S(2)}) collective-permute-start(bf16[256,256]{1,0:T(8,128)(2,1)S(1)} %get-tuple-element.90.refs_1_), channel_id=1, source_target_pairs={{0,8},{1,9},{2,10},{3,11},{4,12},{5,13},{6,14},{7,15},{8,0},{9,1},... | collective-permute-start | bytes 393224 | tf_op jit(solution)/shard_map/ppermute | solution.py:464
  24.2 0.4 collective-permute-start.14
  24.7 0.5 collective-permute-start.13
  25.2 0.3 turn_pieces.1.refs_0_
  25.5 0.1 collective-permute-start.8
  25.6 1.1 %collective-permute-done.9.refs_2_ = bf16[256,256]{1,0:T(8,128)(2,1)S(1)} collective-permute-done((bf16[256,256]{1,0:T(8,128)(2,1)S(1)}, bf16[256,256]{1,0:T(8,128)(2,1)S(1)}, u32[]{:S(2)}, u32[]{:S(2)}) %collective-permute-start.9) | collective-permute-done | bytes 131104 | tf_op jit(solution)/shard_map/ppermute | solution.py:464
  26.7 1.8 %collective-permute-start.10 = (bf16[256,256]{1,0:T(8,128)(2,1)S(1)}, bf16[256,256]{1,0:T(8,128)(2,1)S(1)}, u32[]{:S(2)}, u32[]{:S(2)}) collective-permute-start(bf16[256,256]{1,0:T(8,128)(2,1)S(1)} %collective-permute-done.9.refs_2_), channel_id=1, source_target_pairs={{0,8},{1,9},{2,10},{3,11},{4,12},{5,13},{6,14},{7,15},{8,0},{9,1},... | collective-permute-start | bytes 393224 | tf_op jit(solution)/shard_map/ppermute | solution.py:464
  28.4 0.5 %collective-permute-done.11.refs_5_ = bf16[256,256]{1,0:T(8,128)(2,1)S(1)} collective-permute-done((bf16[256,256]{1,0:T(8,128)(2,1)S(1)}, bf16[256,256]{1,0:T(8,128)(2,1)S(1)}, u32[]{:S(2)}, u32[]{:S(2)}) %collective-permute-start.11) | collective-permute-done | bytes 131104 | tf_op jit(solution)/shard_map/ppermute | solution.py:464
  29.0 1.5 %collective-permute-start.12 = (bf16[256,256]{1,0:T(8,128)(2,1)S(1)}, bf16[256,256]{1,0:T(8,128)(2,1)S(1)}, u32[]{:S(2)}, u32[]{:S(2)}) collective-permute-start(bf16[256,256]{1,0:T(8,128)(2,1)S(1)} %collective-permute-done.11.refs_5_), channel_id=1, source_target_pairs={{0,4},{1,5},{2,6},{3,7},{4,0},{5,1},{6,2},{7,3},{8,12},{9,13},{10,... | collective-permute-start | bytes 393224 | tf_op jit(solution)/shard_map/ppermute | solution.py:464
  30.5 1.3 %collective-permute-done.14.refs_4_ = bf16[256,256]{1,0:T(8,128)(2,1)S(1)} collective-permute-done((bf16[256,256]{1,0:T(8,128)(2,1)S(1)}, bf16[256,256]{1,0:T(8,128)(2,1)S(1)}, u32[]{:S(2)}, u32[]{:S(2)}) %collective-permute-start.14) | collective-permute-done | bytes 131104 | tf_op jit(solution)/shard_map/ppermute | solution.py:464
  31.8 0.1 stack_grads.2
  31.9 1.8 %collective-permute-done.10.refs_0_ = bf16[256,256]{1,0:T(8,128)(2,1)S(1)} collective-permute-done((bf16[256,256]{1,0:T(8,128)(2,1)S(1)}, bf16[256,256]{1,0:T(8,128)(2,1)S(1)}, u32[]{:S(2)}, u32[]{:S(2)}) %collective-permute-start.10) | collective-permute-done | bytes 131104 | tf_op jit(solution)/shard_map/ppermute | solution.py:464
  33.7 0.3 collective-permute-done.12.refs_1_
  34.0 0.6 %weight_far.2 = (f32[128,512]{1,0:T(8,128)S(1)}, bf16[128,512]{1,0:T(8,128)(2,1)S(1)}) custom-call(bf16[1024,512]{1,0:T(8,128)(2,1)S(1)} %turn_pieces.1.refs_0_, bf16[1024,512]{1,0:T(8,128)(2,1)S(1)} %collective-permute-done.8.refs_1_, bf16[384,512]{1,0:T(8,128)(2,1)S(1)} %get-tuple-element.113.refs_2_, bf16[384,512]{1,0:T(8,128)(2,1)S(1)} %get-tuple-element.114.refs_3_, ...), custom_call_target="tpu_custom_call" | custom-call | flops 1024 | bytes 1024 | tf_op jit(solution)/shard_map/weight_far/pallas_call | solution.py:362
  34.6 1.3 %collective-permute-start.15 = (bf16[128,512]{1,0:T(8,128)(2,1)S(1)}, bf16[128,512]{1,0:T(8,128)(2,1)S(1)}, u32[]{:S(2)}, u32[]{:S(2)}) collective-permute-start(bf16[128,512]{1,0:T(8,128)(2,1)S(1)} %get-tuple-element.112), channel_id=1, source_target_pairs={{0,1},{1,0},{2,3},{3,2},{4,5},{5,4},{6,7},{7,6},{8,9},{9,8},{10,11... | collective-permute-start | bytes 393224 | tf_op jit(solution)/shard_map/ppermute | solution.py:464
  35.9 0.6 %weight_far.3 = (f32[128,512]{1,0:T(8,128)S(1)}, bf16[128,512]{1,0:T(8,128)(2,1)S(1)}) custom-call(bf16[1024,512]{1,0:T(8,128)(2,1)S(1)} %turn_pieces.1.refs_0_, bf16[1024,512]{1,0:T(8,128)(2,1)S(1)} %collective-permute-done.8.refs_1_, bf16[384,512]{1,0:T(8,128)(2,1)S(1)} %get-tuple-element.113.refs_2_, bf16[384,512]{1,0:T(8,128)(2,1)S(1)} %get-tuple-element.114.refs_3_, ...), custom_call_target="tpu_custom_call" | custom-call | flops 1024 | bytes 1024 | tf_op jit(solution)/shard_map/weight_far/pallas_call | solution.py:362
  36.5 0.9 %collective-permute-start.16 = (bf16[128,512]{1,0:T(8,128)(2,1)S(1)}, bf16[128,512]{1,0:T(8,128)(2,1)S(1)}, u32[]{:S(2)}, u32[]{:S(2)}) collective-permute-start(bf16[128,512]{1,0:T(8,128)(2,1)S(1)} %get-tuple-element.121), channel_id=1, source_target_pairs={{0,1},{1,0},{2,3},{3,2},{4,5},{5,4},{6,7},{7,6},{8,9},{9,8},{10,11... | collective-permute-start | bytes 393224 | tf_op jit(solution)/shard_map/ppermute | solution.py:464
  37.4 3.1 %collective-permute-done.15.refs_0_ = bf16[128,512]{1,0:T(8,128)(2,1)S(1)} collective-permute-done((bf16[128,512]{1,0:T(8,128)(2,1)S(1)}, bf16[128,512]{1,0:T(8,128)(2,1)S(1)}, u32[]{:S(2)}, u32[]{:S(2)}) %collective-permute-start.15) | collective-permute-done | bytes 131104 | tf_op jit(solution)/shard_map/ppermute | solution.py:464
  40.5 2.6 %collective-permute-start.17 = (bf16[128,512]{1,0:T(8,128)(2,1)S(1)}, bf16[128,512]{1,0:T(8,128)(2,1)S(1)}, u32[]{:S(2)}, u32[]{:S(2)}) collective-permute-start(bf16[128,512]{1,0:T(8,128)(2,1)S(1)} %relay_total.2), channel_id=1, source_target_pairs={{0,16},{1,17},{2,18},{3,19},{4,20},{5,21},{6,22},{7,23},{8,24},{9,... | collective-permute-start | bytes 393224 | tf_op jit(solution)/shard_map/ppermute | solution.py:464
  43.1 1.1 %weight_near.1 = (f32[128,512]{1,0:T(8,128)S(1)}, bf16[128,512]{1,0:T(8,128)(2,1)S(1)}, bf16[128,512]{1,0:T(8,128)(2,1)S(1)}, bf16[128,512]{1,0:T(8,128)(2,1)S(1)}) custom-call(bf16[1024,512]{1,0:T(8,128)(2,1)S(1)} %turn_pieces.1.refs_0_, bf16[1024,512]{1,0:T(8,128)(2,1)S(1)} %collective-permute-done.8.refs_1_, ...), custom_call_target="tpu_custom_call" | custom-call | flops 1024 | bytes 1024 | tf_op jit(solution)/shard_map/weight_near/pallas_call | solution.py:362
  44.2 0.1 collective-permute-start.20
  44.3 1.9 %collective-permute-start.18 = (bf16[128,512]{1,0:T(8,128)(2,1)S(1)}, bf16[128,512]{1,0:T(8,128)(2,1)S(1)}, u32[]{:S(2)}, u32[]{:S(2)}) collective-permute-start(bf16[128,512]{1,0:T(8,128)(2,1)S(1)} %get-tuple-element.126), channel_id=1, source_target_pairs={{0,1},{1,0},{2,3},{3,2},{4,5},{5,4},{6,7},{7,6},{8,9},{9,8},{10,11... | collective-permute-start | bytes 393224 | tf_op jit(solution)/shard_map/ppermute | solution.py:464
  46.2 0.5 collective-permute-start.19
  46.6 1.7 %query_gradient.1 = bf16[128,4096]{1,0:T(8,128)(2,1)} custom-call(bf16[128,4096]{1,0:T(8,128)(2,1)S(1)} %get-tuple-element.124.refs_0_, bf16[128,4096]{1,0:T(8,128)(2,1)S(1)} %get-tuple-element.125.refs_1_, bf16[128,512]{1,0:T(8,128)(2,1)S(1)} %copy-done.2, bf16[128,512]{1,0:T(8,128)(2,1)S(1)} %collective-permute-done.refs_3_), custom_call_target="tpu_custom_call" | custom-call | flops 1024 | bytes 1024 | tf_op jit(solution)/shard_map/query_gradient/pallas_call | solution.py:155
  48.4 2.3 %collective-permute-done.17.refs_1_ = bf16[128,512]{1,0:T(8,128)(2,1)S(1)} collective-permute-done((bf16[128,512]{1,0:T(8,128)(2,1)S(1)}, bf16[128,512]{1,0:T(8,128)(2,1)S(1)}, u32[]{:S(2)}, u32[]{:S(2)}) %collective-permute-start.17) | collective-permute-done | bytes 131104 | tf_op jit(solution)/shard_map/ppermute | solution.py:464
  50.7 0.0 collective-permute-done.18.refs_1_
  50.7 2.6 %collective-permute-done.21.refs_4_ = bf16[128,512]{1,0:T(8,128)(2,1)S(1)} collective-permute-done((bf16[128,512]{1,0:T(8,128)(2,1)S(1)}, bf16[128,512]{1,0:T(8,128)(2,1)S(1)}, u32[]{:S(2)}, u32[]{:S(2)}) %collective-permute-start.21) | collective-permute-done | bytes 131104 | tf_op jit(solution)/shard_map/ppermute | solution.py:464
  53.4 0.0 collective-permute-done.20.refs_3_
  53.4 0.9 %weight_total.1 = (f32[128,512]{1,0:T(8,128)}, f32[128,512]{1,0:T(8,128)}) custom-call(f32[128,512]{1,0:T(8,128)S(1)} %early_total.1.refs_0_, bf16[128,512]{1,0:T(8,128)(2,1)S(1)} %collective-permute-done.18.refs_1_, bf16[128,512]{1,0:T(8,128)(2,1)S(1)} %collective-permute-done.19.refs_2_, bf16[128,512]{1,0:T(8,128)(2,1)S(1)} %collective-permute-done.20.refs_3_, ...), custom_call_target="tpu_custom_call" | custom-call | flops 1024 | bytes 1024 | tf_op jit(solution)/shard_map/weight_total/pallas_call | solution.py:431
  (21 shorter events, 0.2 us)
Async XLA Ops:
  0.6 9.5 %copy-start.1 = (bf16[128,4096]{1,0:T(8,128)(2,1)S(1)}, bf16[128,4096]{1,0:T(8,128)(2,1)}, u32[]{:S(2)}) copy-start(bf16[128,4096]{1,0:T(8,128)(2,1)} %refs_2_.4) | copy-start | bytes 3145732
  0.6 9.5 %copy-start = (bf16[128,4096]{1,0:T(8,128)(2,1)S(1)}, bf16[128,4096]{1,0:T(8,128)(2,1)}, u32[]{:S(2)}) copy-start(bf16[128,4096]{1,0:T(8,128)(2,1)} %refs_1_.3) | copy-start | bytes 3145732
  0.7 9.4 %collective-permute-start.1 = (bf16[128,512]{1,0:T(8,128)(2,1)}, bf16[128,512]{1,0:T(8,128)(2,1)S(1)}, u32[]{:S(2)}, u32[]{:S(2)}) collective-permute-start(bf16[128,512]{1,0:T(8,128)(2,1)} %refs_4_.1), channel_id=1, source_target_pairs={{0,1},{1,0},{2,3},{3,2},{4,5},{5,4},{6,7},{7,6},{8,9},{9,8},{10,11... | collective-permute-start | bytes 393224 | tf_op jit(solution)/shard_map/ppermute | solution.py:464
  3.7 6.5 %collective-permute-start = (bf16[128,512]{1,0:T(8,128)(2,1)}, bf16[128,512]{1,0:T(8,128)(2,1)S(1)}, u32[]{:S(2)}, u32[]{:S(2)}) collective-permute-start(bf16[128,512]{1,0:T(8,128)(2,1)} %refs_2_.5), channel_id=1, source_target_pairs={{0,1},{1,0},{2,3},{3,2},{4,5},{5,4},{6,7},{7,6},{8,9},{9,8},{10,11... | collective-permute-start | bytes 393224 | tf_op jit(solution)/shard_map/ppermute | solution.py:464
  5.1 12.4 %collective-permute-start.3 = (bf16[128,1024]{1,0:T(8,128)(2,1)S(1)}, bf16[128,1024]{1,0:T(8,128)(2,1)S(1)}, u32[]{:S(2)}, u32[]{:S(2)}) collective-permute-start(bf16[128,1024]{1,0:T(8,128)(2,1)S(1)} %get-tuple-element.75), channel_id=1, source_target_pairs={{0,8},{1,9},{2,10},{3,11},{4,12},{5,13},{6,14},{7,15},{8,0},{9,1},... | collective-permute-start | bytes 786440 | tf_op jit(solution)/shard_map/ppermute | solution.py:464
  7.2 12.8 %collective-permute-start.4 = (bf16[128,1024]{1,0:T(8,128)(2,1)S(1)}, bf16[128,1024]{1,0:T(8,128)(2,1)S(1)}, u32[]{:S(2)}, u32[]{:S(2)}) collective-permute-start(bf16[128,1024]{1,0:T(8,128)(2,1)S(1)} %get-tuple-element.77), channel_id=1, source_target_pairs={{0,4},{1,5},{2,6},{3,7},{4,0},{5,1},{6,2},{7,3},{8,12},{9,13},{10,... | collective-permute-start | bytes 786440 | tf_op jit(solution)/shard_map/ppermute | solution.py:464
  8.7 11.3 %collective-permute-start.5 = (bf16[128,1024]{1,0:T(8,128)(2,1)S(1)}, bf16[128,1024]{1,0:T(8,128)(2,1)S(1)}, u32[]{:S(2)}, u32[]{:S(2)}) collective-permute-start(bf16[128,1024]{1,0:T(8,128)(2,1)S(1)} %get-tuple-element.78), channel_id=1, source_target_pairs={{0,12},{1,13},{2,14},{3,15},{4,8},{5,9},{6,10},{7,11},{8,4},{9,5},... | collective-permute-start | bytes 786440 | tf_op jit(solution)/shard_map/ppermute | solution.py:464
  10.2 5.0 %copy-start.2 = (bf16[128,512]{1,0:T(8,128)(2,1)S(1)}, bf16[128,512]{1,0:T(8,128)(2,1)}, u32[]{:S(2)}) copy-start(bf16[128,512]{1,0:T(8,128)(2,1)} %refs_2_.5) | copy-start | bytes 393220
  10.2 5.0 %copy-start.3 = (bf16[128,512]{1,0:T(8,128)(2,1)S(1)}, bf16[128,512]{1,0:T(8,128)(2,1)}, u32[]{:S(2)}) copy-start(bf16[128,512]{1,0:T(8,128)(2,1)} %refs_4_.1) | copy-start | bytes 393220
  13.3 6.7 %collective-permute-start.2 = (bf16[128,512]{1,0:T(8,128)(2,1)S(1)}, bf16[128,512]{1,0:T(8,128)(2,1)S(1)}, u32[]{:S(2)}, u32[]{:S(2)}) collective-permute-start(bf16[128,512]{1,0:T(8,128)(2,1)S(1)} %get-tuple-element.71), channel_id=1, source_target_pairs={{0,1},{1,0},{2,3},{3,2},{4,5},{5,4},{6,7},{7,6},{8,9},{9,8},{10,11... | collective-permute-start | bytes 393224 | tf_op jit(solution)/shard_map/ppermute | solution.py:464
  15.2 5.8 %collective-permute-start.6 = (bf16[128,512]{1,0:T(8,128)(2,1)S(1)}, bf16[128,512]{1,0:T(8,128)(2,1)S(1)}, u32[]{:S(2)}, u32[]{:S(2)}) collective-permute-start(bf16[128,512]{1,0:T(8,128)(2,1)S(1)} %get-tuple-element.85), channel_id=1, source_target_pairs={{0,3},{1,2},{2,1},{3,0},{4,7},{5,6},{6,5},{7,4},{8,11},{9,10},{10,... | collective-permute-start | bytes 393224 | tf_op jit(solution)/shard_map/ppermute | solution.py:464
  17.6 3.5 %collective-permute-start.7 = (bf16[128,512]{1,0:T(8,128)(2,1)S(1)}, bf16[128,512]{1,0:T(8,128)(2,1)S(1)}, u32[]{:S(2)}, u32[]{:S(2)}) collective-permute-start(bf16[128,512]{1,0:T(8,128)(2,1)S(1)} %get-tuple-element.88), channel_id=1, source_target_pairs={{0,2},{1,3},{2,0},{3,1},{4,6},{5,7},{6,4},{7,5},{8,10},{9,11},{10,... | collective-permute-start | bytes 393224 | tf_op jit(solution)/shard_map/ppermute | solution.py:464
  21.1 5.6 %collective-permute-start.9 = (bf16[256,256]{1,0:T(8,128)(2,1)S(1)}, bf16[256,256]{1,0:T(8,128)(2,1)S(1)}, u32[]{:S(2)}, u32[]{:S(2)}) collective-permute-start(bf16[256,256]{1,0:T(8,128)(2,1)S(1)} %get-tuple-element.89.refs_0_), channel_id=1, source_target_pairs={{0,4},{1,5},{2,6},{3,7},{4,0},{5,1},{6,2},{7,3},{8,12},{9,13},{10,... | collective-permute-start | bytes 393224 | tf_op jit(solution)/shard_map/ppermute | solution.py:464
  22.6 6.4 %collective-permute-start.11 = (bf16[256,256]{1,0:T(8,128)(2,1)S(1)}, bf16[256,256]{1,0:T(8,128)(2,1)S(1)}, u32[]{:S(2)}, u32[]{:S(2)}) collective-permute-start(bf16[256,256]{1,0:T(8,128)(2,1)S(1)} %get-tuple-element.90.refs_1_), channel_id=1, source_target_pairs={{0,8},{1,9},{2,10},{3,11},{4,12},{5,13},{6,14},{7,15},{8,0},{9,1},... | collective-permute-start | bytes 393224 | tf_op jit(solution)/shard_map/ppermute | solution.py:464
  24.2 7.6 %collective-permute-start.14 = (bf16[256,256]{1,0:T(8,128)(2,1)S(1)}, bf16[256,256]{1,0:T(8,128)(2,1)S(1)}, u32[]{:S(2)}, u32[]{:S(2)}) collective-permute-start(bf16[256,256]{1,0:T(8,128)(2,1)S(1)} %get-tuple-element.89.refs_0_), channel_id=1, source_target_pairs={{0,8},{1,9},{2,10},{3,11},{4,12},{5,13},{6,14},{7,15},{8,0},{9,1},... | collective-permute-start | bytes 393224 | tf_op jit(solution)/shard_map/ppermute | solution.py:464
  24.7 7.1 %collective-permute-start.13 = (bf16[256,256]{1,0:T(8,128)(2,1)S(1)}, bf16[256,256]{1,0:T(8,128)(2,1)S(1)}, u32[]{:S(2)}, u32[]{:S(2)}) collective-permute-start(bf16[256,256]{1,0:T(8,128)(2,1)S(1)} %get-tuple-element.90.refs_1_), channel_id=1, source_target_pairs={{0,4},{1,5},{2,6},{3,7},{4,0},{5,1},{6,2},{7,3},{8,12},{9,13},{10,... | collective-permute-start | bytes 393224 | tf_op jit(solution)/shard_map/ppermute | solution.py:464
  25.5 8.5 %collective-permute-start.8 = (bf16[1024,512]{1,0:T(8,128)(2,1)S(1)}, bf16[1024,512]{1,0:T(8,128)(2,1)S(1)}, u32[]{:S(2)}, u32[]{:S(2)}) collective-permute-start(bf16[1024,512]{1,0:T(8,128)(2,1)S(1)} %turn_pieces.1.refs_0_), channel_id=1, source_target_pairs={{0,2},{1,3},{2,0},{3,1},{4,6},{5,7},{6,4},{7,5},{8,10},{9,11},{10,... | collective-permute-start | bytes 3145736 | tf_op jit(solution)/shard_map/ppermute | solution.py:464
  26.7 7.0 %collective-permute-start.10 = (bf16[256,256]{1,0:T(8,128)(2,1)S(1)}, bf16[256,256]{1,0:T(8,128)(2,1)S(1)}, u32[]{:S(2)}, u32[]{:S(2)}) collective-permute-start(bf16[256,256]{1,0:T(8,128)(2,1)S(1)} %collective-permute-done.9.refs_2_), channel_id=1, source_target_pairs={{0,8},{1,9},{2,10},{3,11},{4,12},{5,13},{6,14},{7,15},{8,0},{9,1},... | collective-permute-start | bytes 393224 | tf_op jit(solution)/shard_map/ppermute | solution.py:464
  29.0 5.0 %collective-permute-start.12 = (bf16[256,256]{1,0:T(8,128)(2,1)S(1)}, bf16[256,256]{1,0:T(8,128)(2,1)S(1)}, u32[]{:S(2)}, u32[]{:S(2)}) collective-permute-start(bf16[256,256]{1,0:T(8,128)(2,1)S(1)} %collective-permute-done.11.refs_5_), channel_id=1, source_target_pairs={{0,4},{1,5},{2,6},{3,7},{4,0},{5,1},{6,2},{7,3},{8,12},{9,13},{10,... | collective-permute-start | bytes 393224 | tf_op jit(solution)/shard_map/ppermute | solution.py:464
  34.6 5.8 %collective-permute-start.15 = (bf16[128,512]{1,0:T(8,128)(2,1)S(1)}, bf16[128,512]{1,0:T(8,128)(2,1)S(1)}, u32[]{:S(2)}, u32[]{:S(2)}) collective-permute-start(bf16[128,512]{1,0:T(8,128)(2,1)S(1)} %get-tuple-element.112), channel_id=1, source_target_pairs={{0,1},{1,0},{2,3},{3,2},{4,5},{5,4},{6,7},{7,6},{8,9},{9,8},{10,11... | collective-permute-start | bytes 393224 | tf_op jit(solution)/shard_map/ppermute | solution.py:464
  36.5 7.7 %collective-permute-start.16 = (bf16[128,512]{1,0:T(8,128)(2,1)S(1)}, bf16[128,512]{1,0:T(8,128)(2,1)S(1)}, u32[]{:S(2)}, u32[]{:S(2)}) collective-permute-start(bf16[128,512]{1,0:T(8,128)(2,1)S(1)} %get-tuple-element.121), channel_id=1, source_target_pairs={{0,1},{1,0},{2,3},{3,2},{4,5},{5,4},{6,7},{7,6},{8,9},{9,8},{10,11... | collective-permute-start | bytes 393224 | tf_op jit(solution)/shard_map/ppermute | solution.py:464
  40.5 10.2 %collective-permute-start.17 = (bf16[128,512]{1,0:T(8,128)(2,1)S(1)}, bf16[128,512]{1,0:T(8,128)(2,1)S(1)}, u32[]{:S(2)}, u32[]{:S(2)}) collective-permute-start(bf16[128,512]{1,0:T(8,128)(2,1)S(1)} %relay_total.2), channel_id=1, source_target_pairs={{0,16},{1,17},{2,18},{3,19},{4,20},{5,21},{6,22},{7,23},{8,24},{9,... | collective-permute-start | bytes 393224 | tf_op jit(solution)/shard_map/ppermute | solution.py:464
  44.2 9.2 %collective-permute-start.20 = (bf16[128,512]{1,0:T(8,128)(2,1)S(1)}, bf16[128,512]{1,0:T(8,128)(2,1)S(1)}, u32[]{:S(2)}, u32[]{:S(2)}) collective-permute-start(bf16[128,512]{1,0:T(8,128)(2,1)S(1)} %relay_total.3), channel_id=1, source_target_pairs={{0,18},{1,19},{2,16},{3,17},{4,22},{5,23},{6,20},{7,21},{8,26},{9,... | collective-permute-start | bytes 393224 | tf_op jit(solution)/shard_map/ppermute | solution.py:464
  44.3 6.4 %collective-permute-start.18 = (bf16[128,512]{1,0:T(8,128)(2,1)S(1)}, bf16[128,512]{1,0:T(8,128)(2,1)S(1)}, u32[]{:S(2)}, u32[]{:S(2)}) collective-permute-start(bf16[128,512]{1,0:T(8,128)(2,1)S(1)} %get-tuple-element.126), channel_id=1, source_target_pairs={{0,1},{1,0},{2,3},{3,2},{4,5},{5,4},{6,7},{7,6},{8,9},{9,8},{10,11... | collective-permute-start | bytes 393224 | tf_op jit(solution)/shard_map/ppermute | solution.py:464
  46.2 4.6 %collective-permute-start.19 = (bf16[128,512]{1,0:T(8,128)(2,1)S(1)}, bf16[128,512]{1,0:T(8,128)(2,1)S(1)}, u32[]{:S(2)}, u32[]{:S(2)}) collective-permute-start(bf16[128,512]{1,0:T(8,128)(2,1)S(1)} %get-tuple-element.127), channel_id=1, source_target_pairs={{0,2},{1,3},{2,0},{3,1},{4,6},{5,7},{6,4},{7,5},{8,10},{9,11},{10,... | collective-permute-start | bytes 393224 | tf_op jit(solution)/shard_map/ppermute | solution.py:464
  46.6 6.7 %collective-permute-start.21 = (bf16[128,512]{1,0:T(8,128)(2,1)S(1)}, bf16[128,512]{1,0:T(8,128)(2,1)S(1)}, u32[]{:S(2)}, u32[]{:S(2)}) collective-permute-start(bf16[128,512]{1,0:T(8,128)(2,1)S(1)} %get-tuple-element.128), channel_id=1, source_target_pairs={{0,3},{1,2},{2,1},{3,0},{4,7},{5,6},{6,5},{7,4},{8,11},{9,10},{10,... | collective-permute-start | bytes 393224 | tf_op jit(solution)/shard_map/ppermute | solution.py:464

commit v16 on v15

--- a/solution.py
+++ b/solution.py
@@ -300,12 +300,12 @@
     )(same, cross, sibling)
 
 
-def stack_kernel(*refs):
+def stack_kernel(first, count, *refs):
     own_ref, sibling_ref = refs[-2:]
     rows = refs[0].shape[0] // 2
     width = refs[0].shape[1]
-    for at in range(len(refs) // 2 - 1):
-        here = slice(at * rows, (at + 1) * rows)
+    for at in range(count):
+        here = slice((first + at) * rows, (first + at + 1) * rows)
         for half in range(2):
             ref = refs[2 * at + half]
             columns = slice(half * width, (half + 1) * width)
@@ -313,14 +313,19 @@
             sibling_ref[here, columns] = ref[rows:, :]
 
 
-def stack_call(grads, cost):
+def stack_call(grads, so_far, cost):
     height, width = grads[0][0].shape
     operands = [half for halves in grads for half in halves]
-    return pl.pallas_call(
-        stack_kernel,
+    count = len(operands)
+    first = 0 if so_far is None else MIDDLE * NEAR - len(grads)
+    aliases = {} if so_far is None else {count: 0, count + 1: 1}
+    operands += so_far or []
+    return pl.pallas_call(
+        functools.partial(stack_kernel, first, len(grads)),
         in_specs=[WHOLE] * len(operands),
         out_specs=[WHOLE] * 2,
-        out_shape=[shape((height // 2 * len(grads), 2 * width), jnp.bfloat16)] * 2,
+        out_shape=[shape((height // 2 * MIDDLE * NEAR, 2 * width), jnp.bfloat16)] * 2,
+        input_output_aliases=aliases,
         compiler_params=PARAMS,
         cost_estimate=cost,
         name="stack_grads",
@@ -328,23 +333,21 @@
 
 
 def weight_kernel(core_steps, z_steps, far, ctx_count, *refs):
-    own_ref, sibling_ref, *g_refs = refs[:6]
-    out_refs, buf = refs[6:-1], refs[-1]
+    own_ref, sibling_ref, own_grads, sibling_grads = refs[:4]
+    out_refs, buf = refs[4:-1], refs[-1]
     block = out_refs[0].shape[0] // len(z_steps)
     dp_rank = lax.axis_index("dp")
     x_rank = lax.axis_index("ctx")
     z_rank = lax.div(dp_rank, CORES * MIDDLE * NEAR)
     size = ctx_count * block
-    cut = g_refs[0].shape[0]
     for i, core_step in enumerate(core_steps):
         core = lax.rem(dp_rank + core_step, CORES)
         for at, step in enumerate(z_steps):
             start = (core * far + lax.rem(z_rank + step, far)) * size
             here = pl.ds(pl.multiple_of(start, size), size)
-            total = dot(own_ref[here, :cut], g_refs[0][...], NN)
-            total = total + dot(sibling_ref[here, :cut], g_refs[1][...], NN)
-            total = total + dot(own_ref[here, cut:], g_refs[2][...], NN)
-            buf[...] = total + dot(sibling_ref[here, cut:], g_refs[3][...], NN)
+            buf[...] = dot(own_ref[here, :], own_grads[...], NN) + dot(
+                sibling_ref[here, :], sibling_grads[...], NN
+            )
             for x in range(ctx_count):
                 out_ref = out_refs[i * ctx_count + x]
                 start = lax.rem(x_rank + x, ctx_count) * block
@@ -361,7 +364,7 @@
     out_shape += [shape(dims, jnp.bfloat16)] * (ctx_count * (len(core_steps) - 1))
     return pl.pallas_call(
         functools.partial(weight_kernel, core_steps, z_steps, far, ctx_count),
-        in_specs=[WHOLE] * 6,
+        in_specs=[WHOLE] * 4,
         out_specs=[WHOLE] * len(out_shape),
         out_shape=out_shape,
         scratch_shapes=[pltpu.VMEM((height, width), jnp.float32)],
@@ -498,16 +501,17 @@
     over_z = [send(value, member=1) for value in halves[::-1]][::-1]
     over_both = [send(over_y[0], member=1), send(over_z[1], member=2)]
     tokens = turn_call(after([pieces[i] for i in ORDER], halves))
-    grads = stack_call([halves, over_y, over_z], STACK_COST)
-    last = stack_call([after(over_both, grads)], EARLY)
-    grads = grads + last
-    tokens = [tokens, after(send(tokens, core_steps=1), last)]
+    grads = stack_call([halves, over_y, over_z], None, STACK_COST)
+    grads = stack_call([after(over_both, grads)], list(grads), EARLY)
+    tokens = [tokens, after(send(tokens, core_steps=1), grads)]
     weights = functools.partial(weight_call, far=far, ctx_count=ctx_count, tokens=tokens)
     steps = tuple(range(1, far))
     away, arrived, from_far = [], [], []
     for core in range(CORES):
         kept, *blocks = weights((core,), steps, grads=grads)
         grads = after(grads, kept)
+        if core:
+            blocks = after(blocks, arrived[0])
         away.append(kept)
         arrived.append([send(value, s) for s, value in enumerate(blocks, 1)])
     for core in range(CORES):

time: 54.5 us -> 55.4 us (1.017)
  starting transfers between devices: 23.7 us -> 26 us
  waiting for transfers between devices: 16.1 us -> 15.3 us
    ppermute x22, starting transfers between devices: 23.7 us -> 26 us  [send(): return lax.ppermute(value, ('dp', 'ctx'), pairs)]
    ppermute x22, waiting for transfers between devices: 16.1 us -> 15.3 us  [send(): return lax.ppermute(value, ('dp', 'ctx'), pairs)]
  transfers between devices with their start and end apart: 22 -> 22, of which waited for: 11 -> 12; matrix products, arithmetic and copies ran while one was open for 0% -> 0% of each run, Pallas kernels for 22% -> 21%
where the time goes in v16:
time: 55.4 us; the launch traced here: 55.2 us
  starting transfers between devices  26 us (47%)
  waiting for transfers between devices  15.3 us (28%)
  Pallas kernels  13.1 us (24%)
  between operations  0.82 us (1%)
    ppermute x22, starting transfers between devices, send(): return lax.ppermute(value, ('dp', 'ctx'), pairs)  26 us
    ppermute x22, waiting for transfers between devices, send(): return lax.ppermute(value, ('dp', 'ctx'), pairs)  15.3 us
    pallas_call x2, Pallas kernels, block_call(): pl.pallas_call(functools.partial(block_kernel, ctx_count, step), in_specs...  5.52 us
    pallas_call x3, Pallas kernels, weight_call(): pl.pallas_call(functools.partial(weight_kernel, core_steps, z_steps, far,...  1.77 us
    pallas_call x1, Pallas kernels, query_call(): pl.pallas_call(functools.partial(query_kernel, len(keys)), in_specs=[WHOL...  1.74 us
    pallas_call x1, Pallas kernels, pieces_call(): pl.pallas_call(functools.partial(pieces_kernel, far), in_specs=[FAR], out...  1.39 us
    pallas_call x1, Pallas kernels, near_call(): pl.pallas_call(near_kernel, in_specs=[FAR] * len(values), out_specs=[WHOL...  1.24 us
  transfers between devices with their start and end apart: 22, of which 12 were waited for; matrix products, arithmetic and copies ran while one was open for 0% of the time, Pallas kernels for 21%

profile of v16, /device:TPU:0, one launch (start us, length us, event | category | flops | bytes accessed | tf_op | source)
XLA Modules:
  0.0 55.2 jit_solution(7120078167727532392)
XLA Ops:
  0.7 3.0 %collective-permute-start.1 = (bf16[128,512]{1,0:T(8,128)(2,1)}, bf16[128,512]{1,0:T(8,128)(2,1)S(1)}, u32[]{:S(2)}, u32[]{:S(2)}) collective-permute-start(bf16[128,512]{1,0:T(8,128)(2,1)} %refs_4_.1), channel_id=1, source_target_pairs={{0,1},{1,0},{2,3},{3,2},{4,5},{5,4},{6,7},{7,6},{8,9},{9,8},{10,11... | collective-permute-start | bytes 393224 | tf_op jit(solution)/shard_map/ppermute | solution.py:467
  3.7 0.1 collective-permute-start
  3.7 1.4 %pieces.1 = (bf16[128,1024]{1,0:T(8,128)(2,1)S(1)}, bf16[128,1024]{1,0:T(8,128)(2,1)S(1)}, bf16[128,1024]{1,0:T(8,128)(2,1)S(1)}, bf16[128,1024]{1,0:T(8,128)(2,1)S(1)}) custom-call(bf16[128,4096]{1,0:T(8,128)(2,1)} %in_hbm.1), custom_call_target="tpu_custom_call" | custom-call | flops 1024 | bytes 1024 | tf_op jit(solution)/shard_map/pieces/pallas_call | solution.py:225
  5.1 2.1 %collective-permute-start.3 = (bf16[128,1024]{1,0:T(8,128)(2,1)S(1)}, bf16[128,1024]{1,0:T(8,128)(2,1)S(1)}, u32[]{:S(2)}, u32[]{:S(2)}) collective-permute-start(bf16[128,1024]{1,0:T(8,128)(2,1)S(1)} %get-tuple-element.70), channel_id=1, source_target_pairs={{0,8},{1,9},{2,10},{3,11},{4,12},{5,13},{6,14},{7,15},{8,0},{9,1},... | collective-permute-start | bytes 786440 | tf_op jit(solution)/shard_map/ppermute | solution.py:467
  7.2 1.5 %collective-permute-start.4 = (bf16[128,1024]{1,0:T(8,128)(2,1)S(1)}, bf16[128,1024]{1,0:T(8,128)(2,1)S(1)}, u32[]{:S(2)}, u32[]{:S(2)}) collective-permute-start(bf16[128,1024]{1,0:T(8,128)(2,1)S(1)} %get-tuple-element.72), channel_id=1, source_target_pairs={{0,4},{1,5},{2,6},{3,7},{4,0},{5,1},{6,2},{7,3},{8,12},{9,13},{10,... | collective-permute-start | bytes 786440 | tf_op jit(solution)/shard_map/ppermute | solution.py:467
  8.7 0.0 collective-permute-start.5
  8.8 1.2 %bring_near.1 = (bf16[128,4096]{1,0:T(8,128)(2,1)S(1)}, f32[32,128]{1,0:T(8,128)S(1)}) custom-call(bf16[128,4096]{1,0:T(8,128)(2,1)} %refs_0_.3, f32[32,128]{1,0:T(8,128)} %bitcast.1), custom_call_target="tpu_custom_call" | custom-call | flops 1024 | bytes 1024 | tf_op jit(solution)/shard_map/bring_near/pallas_call | solution.py:183
  10.0 0.1 collective-permute-done.refs_3_
  10.2 3.1 %visiting_keys.1 = (bf16[128,4096]{1,0:T(8,128)(2,1)S(1)}, bf16[128,512]{1,0:T(8,128)(2,1)S(1)}, bf16[128,512]{1,0:T(8,128)(2,1)S(1)}, f32[32,128]{1,0:T(8,128)S(1)}) custom-call(s32[1,4]{1,0:T(1,128)} %refs_0_.5, bf16[128,4096]{1,0:T(8,128)(2,1)S(1)} %copy-done, bf16[128,4096]{1,0:T(8,128)(2,1)S(1)} %copy-done.1, ...), custom_call_target="tpu_custom_call" | custom-call | flops 5000000000 | bytes 1024 | tf_op jit(solution)/shard_map/visiting_keys/pallas_call | solution.py:128
  13.3 1.8 %collective-permute-start.2 = (bf16[128,512]{1,0:T(8,128)(2,1)S(1)}, bf16[128,512]{1,0:T(8,128)(2,1)S(1)}, u32[]{:S(2)}, u32[]{:S(2)}) collective-permute-start(bf16[128,512]{1,0:T(8,128)(2,1)S(1)} %get-tuple-element.66), channel_id=1, source_target_pairs={{0,1},{1,0},{2,3},{3,2},{4,5},{5,4},{6,7},{7,6},{8,9},{9,8},{10,11... | collective-permute-start | bytes 393224 | tf_op jit(solution)/shard_map/ppermute | solution.py:467
  15.2 0.0 collective-permute-start.6
  15.2 2.4 %own_keys.1 = (bf16[128,4096]{1,0:T(8,128)(2,1)S(1)}, f32[128,512]{1,0:T(8,128)S(1)}, bf16[128,512]{1,0:T(8,128)(2,1)S(1)}) custom-call(s32[1,4]{1,0:T(1,128)} %refs_0_.5, bf16[128,4096]{1,0:T(8,128)(2,1)S(1)} %copy-done, bf16[128,4096]{1,0:T(8,128)(2,1)S(1)} %copy-done.1, bf16[128,512]{1,0:T(8,128)(2,1)S(1)} %copy-done.2, bf16[128,512]{1,0:T(8,128)(2,1)S(1)} %copy-done.3, ...), custom_call_target="tpu_custom_call" | custom-call | flops 1024 | bytes 1024 | tf_op jit(solution)/shard_map/own_keys/pallas_call | solution.py:128
  17.6 0.0 collective-permute-done.3.refs_2_
  17.6 0.4 collective-permute-start.7
  18.0 2.0 %collective-permute-done.4.refs_1_ = bf16[128,1024]{1,0:T(8,128)(2,1)S(1)} collective-permute-done((bf16[128,1024]{1,0:T(8,128)(2,1)S(1)}, bf16[128,1024]{1,0:T(8,128)(2,1)S(1)}, u32[]{:S(2)}, u32[]{:S(2)}) %collective-permute-start.4) | collective-permute-done | bytes 262176 | tf_op jit(solution)/shard_map/ppermute | solution.py:467
  20.1 0.9 %collective-permute-done.6.refs_2_ = bf16[128,512]{1,0:T(8,128)(2,1)S(1)} collective-permute-done((bf16[128,512]{1,0:T(8,128)(2,1)S(1)}, bf16[128,512]{1,0:T(8,128)(2,1)S(1)}, u32[]{:S(2)}, u32[]{:S(2)}) %collective-permute-start.6) | collective-permute-done | bytes 131104 | tf_op jit(solution)/shard_map/ppermute | solution.py:467
  21.1 1.5 %collective-permute-start.9 = (bf16[256,256]{1,0:T(8,128)(2,1)S(1)}, bf16[256,256]{1,0:T(8,128)(2,1)S(1)}, u32[]{:S(2)}, u32[]{:S(2)}) collective-permute-start(bf16[256,256]{1,0:T(8,128)(2,1)S(1)} %get-tuple-element.84.refs_0_), channel_id=1, source_target_pairs={{0,4},{1,5},{2,6},{3,7},{4,0},{5,1},{6,2},{7,3},{8,12},{9,13},{10,... | collective-permute-start | bytes 393224 | tf_op jit(solution)/shard_map/ppermute | solution.py:467
  22.6 1.6 %collective-permute-start.11 = (bf16[256,256]{1,0:T(8,128)(2,1)S(1)}, bf16[256,256]{1,0:T(8,128)(2,1)S(1)}, u32[]{:S(2)}, u32[]{:S(2)}) collective-permute-start(bf16[256,256]{1,0:T(8,128)(2,1)S(1)} %get-tuple-element.85.refs_1_), channel_id=1, source_target_pairs={{0,8},{1,9},{2,10},{3,11},{4,12},{5,13},{6,14},{7,15},{8,0},{9,1},... | collective-permute-start | bytes 393224 | tf_op jit(solution)/shard_map/ppermute | solution.py:467
  24.2 0.4 collective-permute-start.14
  24.7 0.5 collective-permute-start.13
  25.2 0.3 turn_pieces.1.refs_0_
  25.5 0.1 collective-permute-start.8
  25.6 1.1 %collective-permute-done.9.refs_2_ = bf16[256,256]{1,0:T(8,128)(2,1)S(1)} collective-permute-done((bf16[256,256]{1,0:T(8,128)(2,1)S(1)}, bf16[256,256]{1,0:T(8,128)(2,1)S(1)}, u32[]{:S(2)}, u32[]{:S(2)}) %collective-permute-start.9) | collective-permute-done | bytes 131104 | tf_op jit(solution)/shard_map/ppermute | solution.py:467
  26.7 1.8 %collective-permute-start.10 = (bf16[256,256]{1,0:T(8,128)(2,1)S(1)}, bf16[256,256]{1,0:T(8,128)(2,1)S(1)}, u32[]{:S(2)}, u32[]{:S(2)}) collective-permute-start(bf16[256,256]{1,0:T(8,128)(2,1)S(1)} %collective-permute-done.9.refs_2_), channel_id=1, source_target_pairs={{0,8},{1,9},{2,10},{3,11},{4,12},{5,13},{6,14},{7,15},{8,0},{9,1},... | collective-permute-start | bytes 393224 | tf_op jit(solution)/shard_map/ppermute | solution.py:467
  28.4 0.5 collective-permute-done.11.refs_5_
  29.0 1.5 %collective-permute-start.12 = (bf16[256,256]{1,0:T(8,128)(2,1)S(1)}, bf16[256,256]{1,0:T(8,128)(2,1)S(1)}, u32[]{:S(2)}, u32[]{:S(2)}) collective-permute-start(bf16[256,256]{1,0:T(8,128)(2,1)S(1)} %collective-permute-done.11.refs_5_), channel_id=1, source_target_pairs={{0,4},{1,5},{2,6},{3,7},{4,0},{5,1},{6,2},{7,3},{8,12},{9,13},{10,... | collective-permute-start | bytes 393224 | tf_op jit(solution)/shard_map/ppermute | solution.py:467
  30.5 1.3 %collective-permute-done.14.refs_4_ = bf16[256,256]{1,0:T(8,128)(2,1)S(1)} collective-permute-done((bf16[256,256]{1,0:T(8,128)(2,1)S(1)}, bf16[256,256]{1,0:T(8,128)(2,1)S(1)}, u32[]{:S(2)}, u32[]{:S(2)}) %collective-permute-start.14) | collective-permute-done | bytes 131104 | tf_op jit(solution)/shard_map/ppermute | solution.py:467
  31.8 0.1 stack_grads.2
  31.9 1.8 %collective-permute-done.10.refs_0_ = bf16[256,256]{1,0:T(8,128)(2,1)S(1)} collective-permute-done((bf16[256,256]{1,0:T(8,128)(2,1)S(1)}, bf16[256,256]{1,0:T(8,128)(2,1)S(1)}, u32[]{:S(2)}, u32[]{:S(2)}) %collective-permute-start.10) | collective-permute-done | bytes 131104 | tf_op jit(solution)/shard_map/ppermute | solution.py:467
  33.7 0.3 collective-permute-done.12.refs_1_
  34.0 0.0 collective-permute-done.8.refs_1_
  34.0 0.5 weight_far.2
  34.5 1.3 %collective-permute-start.15 = (bf16[128,512]{1,0:T(8,128)(2,1)S(1)}, bf16[128,512]{1,0:T(8,128)(2,1)S(1)}, u32[]{:S(2)}, u32[]{:S(2)}) collective-permute-start(bf16[128,512]{1,0:T(8,128)(2,1)S(1)} %get-tuple-element.103), channel_id=1, source_target_pairs={{0,1},{1,0},{2,3},{3,2},{4,5},{5,4},{6,7},{7,6},{8,9},{9,8},{10,11... | collective-permute-start | bytes 393224 | tf_op jit(solution)/shard_map/ppermute | solution.py:467
  35.7 0.5 weight_far.3
  36.2 3.3 %collective-permute-done.15.refs_0_ = bf16[128,512]{1,0:T(8,128)(2,1)S(1)} collective-permute-done((bf16[128,512]{1,0:T(8,128)(2,1)S(1)}, bf16[128,512]{1,0:T(8,128)(2,1)S(1)}, u32[]{:S(2)}, u32[]{:S(2)}) %collective-permute-start.15) | collective-permute-done | bytes 131104 | tf_op jit(solution)/shard_map/ppermute | solution.py:467
  39.5 1.6 %collective-permute-start.16 = (bf16[128,512]{1,0:T(8,128)(2,1)S(1)}, bf16[128,512]{1,0:T(8,128)(2,1)S(1)}, u32[]{:S(2)}, u32[]{:S(2)}) collective-permute-start(bf16[128,512]{1,0:T(8,128)(2,1)S(1)} %get-tuple-element.111), channel_id=1, source_target_pairs={{0,1},{1,0},{2,3},{3,2},{4,5},{5,4},{6,7},{7,6},{8,9},{9,8},{10,11... | collective-permute-start | bytes 393224 | tf_op jit(solution)/shard_map/ppermute | solution.py:467
  41.2 2.7 %collective-permute-start.17 = (bf16[128,512]{1,0:T(8,128)(2,1)S(1)}, bf16[128,512]{1,0:T(8,128)(2,1)S(1)}, u32[]{:S(2)}, u32[]{:S(2)}) collective-permute-start(bf16[128,512]{1,0:T(8,128)(2,1)S(1)} %relay_total.2), channel_id=1, source_target_pairs={{0,16},{1,17},{2,18},{3,19},{4,20},{5,21},{6,22},{7,23},{8,24},{9,... | collective-permute-start | bytes 393224 | tf_op jit(solution)/shard_map/ppermute | solution.py:467
  43.9 0.8 %weight_near.1 = (f32[128,512]{1,0:T(8,128)S(1)}, bf16[128,512]{1,0:T(8,128)(2,1)S(1)}, bf16[128,512]{1,0:T(8,128)(2,1)S(1)}, bf16[128,512]{1,0:T(8,128)(2,1)S(1)}) custom-call(bf16[1024,512]{1,0:T(8,128)(2,1)S(1)} %turn_pieces.1.refs_0_, bf16[1024,512]{1,0:T(8,128)(2,1)S(1)} %collective-permute-done.8.refs_1_, ...), custom_call_target="tpu_custom_call" | custom-call | flops 1024 | bytes 1024 | tf_op jit(solution)/shard_map/weight_near/pallas_call | solution.py:365
  44.7 0.0 collective-permute-done.16.refs_0_
  44.7 0.1 collective-permute-start.20
  44.8 1.7 %collective-permute-start.18 = (bf16[128,512]{1,0:T(8,128)(2,1)S(1)}, bf16[128,512]{1,0:T(8,128)(2,1)S(1)}, u32[]{:S(2)}, u32[]{:S(2)}) collective-permute-start(bf16[128,512]{1,0:T(8,128)(2,1)S(1)} %get-tuple-element.116), channel_id=1, source_target_pairs={{0,1},{1,0},{2,3},{3,2},{4,5},{5,4},{6,7},{7,6},{8,9},{9,8},{10,11... | collective-permute-start | bytes 393224 | tf_op jit(solution)/shard_map/ppermute | solution.py:467
  46.5 2.2 %collective-permute-start.19 = (bf16[128,512]{1,0:T(8,128)(2,1)S(1)}, bf16[128,512]{1,0:T(8,128)(2,1)S(1)}, u32[]{:S(2)}, u32[]{:S(2)}) collective-permute-start(bf16[128,512]{1,0:T(8,128)(2,1)S(1)} %get-tuple-element.117), channel_id=1, source_target_pairs={{0,2},{1,3},{2,0},{3,1},{4,6},{5,7},{6,4},{7,5},{8,10},{9,11},{10,... | collective-permute-start | bytes 393224 | tf_op jit(solution)/shard_map/ppermute | solution.py:467
  48.7 0.0 collective-permute-start.21
  48.7 1.2 %collective-permute-done.17.refs_1_ = bf16[128,512]{1,0:T(8,128)(2,1)S(1)} collective-permute-done((bf16[128,512]{1,0:T(8,128)(2,1)S(1)}, bf16[128,512]{1,0:T(8,128)(2,1)S(1)}, u32[]{:S(2)}, u32[]{:S(2)}) %collective-permute-start.17) | collective-permute-done | bytes 131104 | tf_op jit(solution)/shard_map/ppermute | solution.py:467
  49.9 1.7 %query_gradient.1 = bf16[128,4096]{1,0:T(8,128)(2,1)} custom-call(bf16[128,4096]{1,0:T(8,128)(2,1)S(1)} %get-tuple-element.114.refs_0_, bf16[128,4096]{1,0:T(8,128)(2,1)S(1)} %get-tuple-element.115.refs_1_, bf16[128,512]{1,0:T(8,128)(2,1)S(1)} %copy-done.2, bf16[128,512]{1,0:T(8,128)(2,1)S(1)} %collective-permute-done.refs_3_), custom_call_target="tpu_custom_call" | custom-call | flops 1024 | bytes 1024 | tf_op jit(solution)/shard_map/query_gradient/pallas_call | solution.py:155
  51.6 2.7 %collective-permute-done.21.refs_4_ = bf16[128,512]{1,0:T(8,128)(2,1)S(1)} collective-permute-done((bf16[128,512]{1,0:T(8,128)(2,1)S(1)}, bf16[128,512]{1,0:T(8,128)(2,1)S(1)}, u32[]{:S(2)}, u32[]{:S(2)}) %collective-permute-start.21) | collective-permute-done | bytes 131104 | tf_op jit(solution)/shard_map/ppermute | solution.py:467
  54.3 0.1 collective-permute-done.20.refs_3_
  54.3 0.9 %weight_total.1 = (f32[128,512]{1,0:T(8,128)}, f32[128,512]{1,0:T(8,128)}) custom-call(f32[128,512]{1,0:T(8,128)S(1)} %early_total.1.refs_0_, bf16[128,512]{1,0:T(8,128)(2,1)S(1)} %collective-permute-done.18.refs_1_, bf16[128,512]{1,0:T(8,128)(2,1)S(1)} %collective-permute-done.19.refs_2_, bf16[128,512]{1,0:T(8,128)(2,1)S(1)} %collective-permute-done.20.refs_3_, ...), custom_call_target="tpu_custom_call" | custom-call | flops 1024 | bytes 1024 | tf_op jit(solution)/shard_map/weight_total/pallas_call | solution.py:434
  (21 shorter events, 0.2 us)
Async XLA Ops:
  0.6 9.5 %copy-start.1 = (bf16[128,4096]{1,0:T(8,128)(2,1)S(1)}, bf16[128,4096]{1,0:T(8,128)(2,1)}, u32[]{:S(2)}) copy-start(bf16[128,4096]{1,0:T(8,128)(2,1)} %refs_2_.4) | copy-start | bytes 3145732
  0.6 9.5 %copy-start = (bf16[128,4096]{1,0:T(8,128)(2,1)S(1)}, bf16[128,4096]{1,0:T(8,128)(2,1)}, u32[]{:S(2)}) copy-start(bf16[128,4096]{1,0:T(8,128)(2,1)} %refs_1_.3) | copy-start | bytes 3145732
  0.7 9.4 %collective-permute-start.1 = (bf16[128,512]{1,0:T(8,128)(2,1)}, bf16[128,512]{1,0:T(8,128)(2,1)S(1)}, u32[]{:S(2)}, u32[]{:S(2)}) collective-permute-start(bf16[128,512]{1,0:T(8,128)(2,1)} %refs_4_.1), channel_id=1, source_target_pairs={{0,1},{1,0},{2,3},{3,2},{4,5},{5,4},{6,7},{7,6},{8,9},{9,8},{10,11... | collective-permute-start | bytes 393224 | tf_op jit(solution)/shard_map/ppermute | solution.py:467
  3.7 6.5 %collective-permute-start = (bf16[128,512]{1,0:T(8,128)(2,1)}, bf16[128,512]{1,0:T(8,128)(2,1)S(1)}, u32[]{:S(2)}, u32[]{:S(2)}) collective-permute-start(bf16[128,512]{1,0:T(8,128)(2,1)} %refs_2_.5), channel_id=1, source_target_pairs={{0,1},{1,0},{2,3},{3,2},{4,5},{5,4},{6,7},{7,6},{8,9},{9,8},{10,11... | collective-permute-start | bytes 393224 | tf_op jit(solution)/shard_map/ppermute | solution.py:467
  5.1 12.4 %collective-permute-start.3 = (bf16[128,1024]{1,0:T(8,128)(2,1)S(1)}, bf16[128,1024]{1,0:T(8,128)(2,1)S(1)}, u32[]{:S(2)}, u32[]{:S(2)}) collective-permute-start(bf16[128,1024]{1,0:T(8,128)(2,1)S(1)} %get-tuple-element.70), channel_id=1, source_target_pairs={{0,8},{1,9},{2,10},{3,11},{4,12},{5,13},{6,14},{7,15},{8,0},{9,1},... | collective-permute-start | bytes 786440 | tf_op jit(solution)/shard_map/ppermute | solution.py:467
  7.2 12.8 %collective-permute-start.4 = (bf16[128,1024]{1,0:T(8,128)(2,1)S(1)}, bf16[128,1024]{1,0:T(8,128)(2,1)S(1)}, u32[]{:S(2)}, u32[]{:S(2)}) collective-permute-start(bf16[128,1024]{1,0:T(8,128)(2,1)S(1)} %get-tuple-element.72), channel_id=1, source_target_pairs={{0,4},{1,5},{2,6},{3,7},{4,0},{5,1},{6,2},{7,3},{8,12},{9,13},{10,... | collective-permute-start | bytes 786440 | tf_op jit(solution)/shard_map/ppermute | solution.py:467
  8.7 11.3 %collective-permute-start.5 = (bf16[128,1024]{1,0:T(8,128)(2,1)S(1)}, bf16[128,1024]{1,0:T(8,128)(2,1)S(1)}, u32[]{:S(2)}, u32[]{:S(2)}) collective-permute-start(bf16[128,1024]{1,0:T(8,128)(2,1)S(1)} %get-tuple-element.73), channel_id=1, source_target_pairs={{0,12},{1,13},{2,14},{3,15},{4,8},{5,9},{6,10},{7,11},{8,4},{9,5},... | collective-permute-start | bytes 786440 | tf_op jit(solution)/shard_map/ppermute | solution.py:467
  10.2 5.0 %copy-start.2 = (bf16[128,512]{1,0:T(8,128)(2,1)S(1)}, bf16[128,512]{1,0:T(8,128)(2,1)}, u32[]{:S(2)}) copy-start(bf16[128,512]{1,0:T(8,128)(2,1)} %refs_2_.5) | copy-start | bytes 393220
  10.2 5.0 %copy-start.3 = (bf16[128,512]{1,0:T(8,128)(2,1)S(1)}, bf16[128,512]{1,0:T(8,128)(2,1)}, u32[]{:S(2)}) copy-start(bf16[128,512]{1,0:T(8,128)(2,1)} %refs_4_.1) | copy-start | bytes 393220
  13.3 6.7 %collective-permute-start.2 = (bf16[128,512]{1,0:T(8,128)(2,1)S(1)}, bf16[128,512]{1,0:T(8,128)(2,1)S(1)}, u32[]{:S(2)}, u32[]{:S(2)}) collective-permute-start(bf16[128,512]{1,0:T(8,128)(2,1)S(1)} %get-tuple-element.66), channel_id=1, source_target_pairs={{0,1},{1,0},{2,3},{3,2},{4,5},{5,4},{6,7},{7,6},{8,9},{9,8},{10,11... | collective-permute-start | bytes 393224 | tf_op jit(solution)/shard_map/ppermute | solution.py:467
  15.2 5.8 %collective-permute-start.6 = (bf16[128,512]{1,0:T(8,128)(2,1)S(1)}, bf16[128,512]{1,0:T(8,128)(2,1)S(1)}, u32[]{:S(2)}, u32[]{:S(2)}) collective-permute-start(bf16[128,512]{1,0:T(8,128)(2,1)S(1)} %get-tuple-element.80), channel_id=1, source_target_pairs={{0,3},{1,2},{2,1},{3,0},{4,7},{5,6},{6,5},{7,4},{8,11},{9,10},{10,... | collective-permute-start | bytes 393224 | tf_op jit(solution)/shard_map/ppermute | solution.py:467
  17.6 3.5 %collective-permute-start.7 = (bf16[128,512]{1,0:T(8,128)(2,1)S(1)}, bf16[128,512]{1,0:T(8,128)(2,1)S(1)}, u32[]{:S(2)}, u32[]{:S(2)}) collective-permute-start(bf16[128,512]{1,0:T(8,128)(2,1)S(1)} %get-tuple-element.83), channel_id=1, source_target_pairs={{0,2},{1,3},{2,0},{3,1},{4,6},{5,7},{6,4},{7,5},{8,10},{9,11},{10,... | collective-permute-start | bytes 393224 | tf_op jit(solution)/shard_map/ppermute | solution.py:467
  21.1 5.6 %collective-permute-start.9 = (bf16[256,256]{1,0:T(8,128)(2,1)S(1)}, bf16[256,256]{1,0:T(8,128)(2,1)S(1)}, u32[]{:S(2)}, u32[]{:S(2)}) collective-permute-start(bf16[256,256]{1,0:T(8,128)(2,1)S(1)} %get-tuple-element.84.refs_0_), channel_id=1, source_target_pairs={{0,4},{1,5},{2,6},{3,7},{4,0},{5,1},{6,2},{7,3},{8,12},{9,13},{10,... | collective-permute-start | bytes 393224 | tf_op jit(solution)/shard_map/ppermute | solution.py:467
  22.6 6.4 %collective-permute-start.11 = (bf16[256,256]{1,0:T(8,128)(2,1)S(1)}, bf16[256,256]{1,0:T(8,128)(2,1)S(1)}, u32[]{:S(2)}, u32[]{:S(2)}) collective-permute-start(bf16[256,256]{1,0:T(8,128)(2,1)S(1)} %get-tuple-element.85.refs_1_), channel_id=1, source_target_pairs={{0,8},{1,9},{2,10},{3,11},{4,12},{5,13},{6,14},{7,15},{8,0},{9,1},... | collective-permute-start | bytes 393224 | tf_op jit(solution)/shard_map/ppermute | solution.py:467
  24.2 7.6 %collective-permute-start.14 = (bf16[256,256]{1,0:T(8,128)(2,1)S(1)}, bf16[256,256]{1,0:T(8,128)(2,1)S(1)}, u32[]{:S(2)}, u32[]{:S(2)}) collective-permute-start(bf16[256,256]{1,0:T(8,128)(2,1)S(1)} %get-tuple-element.84.refs_0_), channel_id=1, source_target_pairs={{0,8},{1,9},{2,10},{3,11},{4,12},{5,13},{6,14},{7,15},{8,0},{9,1},... | collective-permute-start | bytes 393224 | tf_op jit(solution)/shard_map/ppermute | solution.py:467
  24.7 7.1 %collective-permute-start.13 = (bf16[256,256]{1,0:T(8,128)(2,1)S(1)}, bf16[256,256]{1,0:T(8,128)(2,1)S(1)}, u32[]{:S(2)}, u32[]{:S(2)}) collective-permute-start(bf16[256,256]{1,0:T(8,128)(2,1)S(1)} %get-tuple-element.85.refs_1_), channel_id=1, source_target_pairs={{0,4},{1,5},{2,6},{3,7},{4,0},{5,1},{6,2},{7,3},{8,12},{9,13},{10,... | collective-permute-start | bytes 393224 | tf_op jit(solution)/shard_map/ppermute | solution.py:467
  25.5 8.5 %collective-permute-start.8 = (bf16[1024,512]{1,0:T(8,128)(2,1)S(1)}, bf16[1024,512]{1,0:T(8,128)(2,1)S(1)}, u32[]{:S(2)}, u32[]{:S(2)}) collective-permute-start(bf16[1024,512]{1,0:T(8,128)(2,1)S(1)} %turn_pieces.1.refs_0_), channel_id=1, source_target_pairs={{0,2},{1,3},{2,0},{3,1},{4,6},{5,7},{6,4},{7,5},{8,10},{9,11},{10,... | collective-permute-start | bytes 3145736 | tf_op jit(solution)/shard_map/ppermute | solution.py:467
  26.7 7.0 %collective-permute-start.10 = (bf16[256,256]{1,0:T(8,128)(2,1)S(1)}, bf16[256,256]{1,0:T(8,128)(2,1)S(1)}, u32[]{:S(2)}, u32[]{:S(2)}) collective-permute-start(bf16[256,256]{1,0:T(8,128)(2,1)S(1)} %collective-permute-done.9.refs_2_), channel_id=1, source_target_pairs={{0,8},{1,9},{2,10},{3,11},{4,12},{5,13},{6,14},{7,15},{8,0},{9,1},... | collective-permute-start | bytes 393224 | tf_op jit(solution)/shard_map/ppermute | solution.py:467
  29.0 5.0 %collective-permute-start.12 = (bf16[256,256]{1,0:T(8,128)(2,1)S(1)}, bf16[256,256]{1,0:T(8,128)(2,1)S(1)}, u32[]{:S(2)}, u32[]{:S(2)}) collective-permute-start(bf16[256,256]{1,0:T(8,128)(2,1)S(1)} %collective-permute-done.11.refs_5_), channel_id=1, source_target_pairs={{0,4},{1,5},{2,6},{3,7},{4,0},{5,1},{6,2},{7,3},{8,12},{9,13},{10,... | collective-permute-start | bytes 393224 | tf_op jit(solution)/shard_map/ppermute | solution.py:467
  34.5 5.0 %collective-permute-start.15 = (bf16[128,512]{1,0:T(8,128)(2,1)S(1)}, bf16[128,512]{1,0:T(8,128)(2,1)S(1)}, u32[]{:S(2)}, u32[]{:S(2)}) collective-permute-start(bf16[128,512]{1,0:T(8,128)(2,1)S(1)} %get-tuple-element.103), channel_id=1, source_target_pairs={{0,1},{1,0},{2,3},{3,2},{4,5},{5,4},{6,7},{7,6},{8,9},{9,8},{10,11... | collective-permute-start | bytes 393224 | tf_op jit(solution)/shard_map/ppermute | solution.py:467
  39.5 5.1 %collective-permute-start.16 = (bf16[128,512]{1,0:T(8,128)(2,1)S(1)}, bf16[128,512]{1,0:T(8,128)(2,1)S(1)}, u32[]{:S(2)}, u32[]{:S(2)}) collective-permute-start(bf16[128,512]{1,0:T(8,128)(2,1)S(1)} %get-tuple-element.111), channel_id=1, source_target_pairs={{0,1},{1,0},{2,3},{3,2},{4,5},{5,4},{6,7},{7,6},{8,9},{9,8},{10,11... | collective-permute-start | bytes 393224 | tf_op jit(solution)/shard_map/ppermute | solution.py:467
  41.2 8.6 %collective-permute-start.17 = (bf16[128,512]{1,0:T(8,128)(2,1)S(1)}, bf16[128,512]{1,0:T(8,128)(2,1)S(1)}, u32[]{:S(2)}, u32[]{:S(2)}) collective-permute-start(bf16[128,512]{1,0:T(8,128)(2,1)S(1)} %relay_total.2), channel_id=1, source_target_pairs={{0,16},{1,17},{2,18},{3,19},{4,20},{5,21},{6,22},{7,23},{8,24},{9,... | collective-permute-start | bytes 393224 | tf_op jit(solution)/shard_map/ppermute | solution.py:467
  44.7 9.6 %collective-permute-start.20 = (bf16[128,512]{1,0:T(8,128)(2,1)S(1)}, bf16[128,512]{1,0:T(8,128)(2,1)S(1)}, u32[]{:S(2)}, u32[]{:S(2)}) collective-permute-start(bf16[128,512]{1,0:T(8,128)(2,1)S(1)} %relay_total.3), channel_id=1, source_target_pairs={{0,18},{1,19},{2,16},{3,17},{4,22},{5,23},{6,20},{7,21},{8,26},{9,... | collective-permute-start | bytes 393224 | tf_op jit(solution)/shard_map/ppermute | solution.py:467
  44.8 6.8 %collective-permute-start.18 = (bf16[128,512]{1,0:T(8,128)(2,1)S(1)}, bf16[128,512]{1,0:T(8,128)(2,1)S(1)}, u32[]{:S(2)}, u32[]{:S(2)}) collective-permute-start(bf16[128,512]{1,0:T(8,128)(2,1)S(1)} %get-tuple-element.116), channel_id=1, source_target_pairs={{0,1},{1,0},{2,3},{3,2},{4,5},{5,4},{6,7},{7,6},{8,9},{9,8},{10,11... | collective-permute-start | bytes 393224 | tf_op jit(solution)/shard_map/ppermute | solution.py:467
  46.5 5.1 %collective-permute-start.19 = (bf16[128,512]{1,0:T(8,128)(2,1)S(1)}, bf16[128,512]{1,0:T(8,128)(2,1)S(1)}, u32[]{:S(2)}, u32[]{:S(2)}) collective-permute-start(bf16[128,512]{1,0:T(8,128)(2,1)S(1)} %get-tuple-element.117), channel_id=1, source_target_pairs={{0,2},{1,3},{2,0},{3,1},{4,6},{5,7},{6,4},{7,5},{8,10},{9,11},{10,... | collective-permute-start | bytes 393224 | tf_op jit(solution)/shard_map/ppermute | solution.py:467
  48.7 5.6 %collective-permute-start.21 = (bf16[128,512]{1,0:T(8,128)(2,1)S(1)}, bf16[128,512]{1,0:T(8,128)(2,1)S(1)}, u32[]{:S(2)}, u32[]{:S(2)}) collective-permute-start(bf16[128,512]{1,0:T(8,128)(2,1)S(1)} %get-tuple-element.118), channel_id=1, source_target_pairs={{0,3},{1,2},{2,1},{3,0},{4,7},{5,6},{6,5},{7,4},{8,11},{9,10},{10,... | collective-permute-start | bytes 393224 | tf_op jit(solution)/shard_map/ppermute | solution.py:467

commit v17 on v16

--- a/solution.py
+++ b/solution.py
@@ -510,23 +510,18 @@
     for core in range(CORES):
         kept, *blocks = weights((core,), steps, grads=grads)
         grads = after(grads, kept)
-        if core:
-            blocks = after(blocks, arrived[0])
         away.append(kept)
         arrived.append([send(value, s) for s, value in enumerate(blocks, 1)])
+    blocks = weights(tuple(range(CORES)), (0,), grads=grads)
+    own_block, near = blocks[0], blocks[1:ctx_count]
+    cross_block, cross_near = blocks[ctx_count], blocks[ctx_count + 1 :]
+    arrived[0] = after(arrived[0], own_block)
+    near_arrived = [send(value, s) for s, value in enumerate(near, 1)]
     for core in range(CORES):
         relayed = relay_call(far - 1, away[core], arrived[core])
         from_far.append([send(value, 0, core, s) for s, value in enumerate(relayed, 1)])
-        if core == 0:
-            grads = after(grads, relayed)
-            blocks = weights(tuple(range(CORES)), (0,), grads=grads)
-            own_block, near = blocks[0], blocks[1:ctx_count]
-            cross_block, cross_near = blocks[ctx_count], blocks[ctx_count + 1 :]
-            arrived[1] = after(arrived[1], own_block)
-    near, cross_block, cross_near, own_scores = after(
-        (near, cross_block, cross_near, own_scores), relayed
-    )
-    same = [early_call([own_block] + from_far[0])] + [send(v, s) for s, v in enumerate(near, 1)]
+    cross_block, cross_near, own_scores = after((cross_block, cross_near, own_scores), relayed)
+    same = [early_call([own_block] + near_arrived + from_far[0])]
     cross = [send(cross_block, core_steps=1)] + from_far[1]
     cross += [send(value, s, 1) for s, value in enumerate(cross_near, 1)]
     query_gradient = query_call(

time: 55.4 us -> 54.2 us (0.978)
  waiting for transfers between devices: 15.3 us -> 13.5 us
    ppermute x22, waiting for transfers between devices: 15.3 us -> 13.5 us  [send(): return lax.ppermute(value, ('dp', 'ctx'), pairs)]
  transfers between devices with their start and end apart: 22 -> 22, of which waited for: 12 -> 12; matrix products, arithmetic and copies ran while one was open for 0% -> 0% of each run, Pallas kernels for 21% -> 22%
where the time goes in v17:
time: 54.2 us; the launch traced here: 54 us
  starting transfers between devices  26.5 us (49%)
  waiting for transfers between devices  13.5 us (25%)
  Pallas kernels  13.1 us (24%)
  between operations  0.81 us (1%)
    ppermute x22, starting transfers between devices, send(): return lax.ppermute(value, ('dp', 'ctx'), pairs)  26.5 us
    ppermute x22, waiting for transfers between devices, send(): return lax.ppermute(value, ('dp', 'ctx'), pairs)  13.5 us
    pallas_call x2, Pallas kernels, block_call(): pl.pallas_call(functools.partial(block_kernel, ctx_count, step), in_specs...  5.52 us
    pallas_call x3, Pallas kernels, weight_call(): pl.pallas_call(functools.partial(weight_kernel, core_steps, z_steps, far,...  1.77 us
    pallas_call x1, Pallas kernels, query_call(): pl.pallas_call(functools.partial(query_kernel, len(keys)), in_specs=[WHOL...  1.73 us
    pallas_call x1, Pallas kernels, pieces_call(): pl.pallas_call(functools.partial(pieces_kernel, far), in_specs=[FAR], out...  1.39 us
    pallas_call x1, Pallas kernels, near_call(): pl.pallas_call(near_kernel, in_specs=[FAR] * len(values), out_specs=[WHOL...  1.24 us
  transfers between devices with their start and end apart: 22, of which 12 were waited for; matrix products, arithmetic and copies ran while one was open for 0% of the time, Pallas kernels for 22%

profile of v17, /device:TPU:0, one launch (start us, length us, event | category | flops | bytes accessed | tf_op | source)
XLA Modules:
  0.0 54.0 jit_solution(4135268462459215080)
XLA Ops:
  0.7 3.0 %collective-permute-start.1 = (bf16[128,512]{1,0:T(8,128)(2,1)}, bf16[128,512]{1,0:T(8,128)(2,1)S(1)}, u32[]{:S(2)}, u32[]{:S(2)}) collective-permute-start(bf16[128,512]{1,0:T(8,128)(2,1)} %refs_4_.1), channel_id=1, source_target_pairs={{0,1},{1,0},{2,3},{3,2},{4,5},{5,4},{6,7},{7,6},{8,9},{9,8},{10,11... | collective-permute-start | bytes 393224 | tf_op jit(solution)/shard_map/ppermute | solution.py:467
  3.7 0.1 collective-permute-start
  3.7 1.4 %pieces.1 = (bf16[128,1024]{1,0:T(8,128)(2,1)S(1)}, bf16[128,1024]{1,0:T(8,128)(2,1)S(1)}, bf16[128,1024]{1,0:T(8,128)(2,1)S(1)}, bf16[128,1024]{1,0:T(8,128)(2,1)S(1)}) custom-call(bf16[128,4096]{1,0:T(8,128)(2,1)} %in_hbm.1), custom_call_target="tpu_custom_call" | custom-call | flops 1024 | bytes 1024 | tf_op jit(solution)/shard_map/pieces/pallas_call | solution.py:225
  5.1 2.1 %collective-permute-start.3 = (bf16[128,1024]{1,0:T(8,128)(2,1)S(1)}, bf16[128,1024]{1,0:T(8,128)(2,1)S(1)}, u32[]{:S(2)}, u32[]{:S(2)}) collective-permute-start(bf16[128,1024]{1,0:T(8,128)(2,1)S(1)} %get-tuple-element.66), channel_id=1, source_target_pairs={{0,8},{1,9},{2,10},{3,11},{4,12},{5,13},{6,14},{7,15},{8,0},{9,1},... | collective-permute-start | bytes 786440 | tf_op jit(solution)/shard_map/ppermute | solution.py:467
  7.2 1.5 %collective-permute-start.4 = (bf16[128,1024]{1,0:T(8,128)(2,1)S(1)}, bf16[128,1024]{1,0:T(8,128)(2,1)S(1)}, u32[]{:S(2)}, u32[]{:S(2)}) collective-permute-start(bf16[128,1024]{1,0:T(8,128)(2,1)S(1)} %get-tuple-element.68), channel_id=1, source_target_pairs={{0,4},{1,5},{2,6},{3,7},{4,0},{5,1},{6,2},{7,3},{8,12},{9,13},{10,... | collective-permute-start | bytes 786440 | tf_op jit(solution)/shard_map/ppermute | solution.py:467
  8.7 0.0 collective-permute-start.5
  8.8 1.2 %bring_near.1 = (bf16[128,4096]{1,0:T(8,128)(2,1)S(1)}, f32[32,128]{1,0:T(8,128)S(1)}) custom-call(bf16[128,4096]{1,0:T(8,128)(2,1)} %refs_0_.3, f32[32,128]{1,0:T(8,128)} %bitcast.1), custom_call_target="tpu_custom_call" | custom-call | flops 1024 | bytes 1024 | tf_op jit(solution)/shard_map/bring_near/pallas_call | solution.py:183
  10.0 0.0 collective-permute-done.1.refs_4_
  10.0 0.1 collective-permute-done.refs_3_
  10.2 3.1 %visiting_keys.1 = (bf16[128,4096]{1,0:T(8,128)(2,1)S(1)}, bf16[128,512]{1,0:T(8,128)(2,1)S(1)}, bf16[128,512]{1,0:T(8,128)(2,1)S(1)}, f32[32,128]{1,0:T(8,128)S(1)}) custom-call(s32[1,4]{1,0:T(1,128)} %refs_0_.5, bf16[128,4096]{1,0:T(8,128)(2,1)S(1)} %copy-done, bf16[128,4096]{1,0:T(8,128)(2,1)S(1)} %copy-done.1, ...), custom_call_target="tpu_custom_call" | custom-call | flops 5000000000 | bytes 1024 | tf_op jit(solution)/shard_map/visiting_keys/pallas_call | solution.py:128
  13.3 1.8 %collective-permute-start.2 = (bf16[128,512]{1,0:T(8,128)(2,1)S(1)}, bf16[128,512]{1,0:T(8,128)(2,1)S(1)}, u32[]{:S(2)}, u32[]{:S(2)}) collective-permute-start(bf16[128,512]{1,0:T(8,128)(2,1)S(1)} %get-tuple-element.62), channel_id=1, source_target_pairs={{0,1},{1,0},{2,3},{3,2},{4,5},{5,4},{6,7},{7,6},{8,9},{9,8},{10,11... | collective-permute-start | bytes 393224 | tf_op jit(solution)/shard_map/ppermute | solution.py:467
  15.2 2.4 %own_keys.1 = (bf16[128,4096]{1,0:T(8,128)(2,1)S(1)}, f32[128,512]{1,0:T(8,128)S(1)}, bf16[128,512]{1,0:T(8,128)(2,1)S(1)}) custom-call(s32[1,4]{1,0:T(1,128)} %refs_0_.5, bf16[128,4096]{1,0:T(8,128)(2,1)S(1)} %copy-done, bf16[128,4096]{1,0:T(8,128)(2,1)S(1)} %copy-done.1, bf16[128,512]{1,0:T(8,128)(2,1)S(1)} %copy-done.2, bf16[128,512]{1,0:T(8,128)(2,1)S(1)} %copy-done.3, ...), custom_call_target="tpu_custom_call" | custom-call | flops 1024 | bytes 1024 | tf_op jit(solution)/shard_map/own_keys/pallas_call | solution.py:128
  17.6 0.4 collective-permute-start.7
  18.0 2.0 %collective-permute-done.4.refs_1_ = bf16[128,1024]{1,0:T(8,128)(2,1)S(1)} collective-permute-done((bf16[128,1024]{1,0:T(8,128)(2,1)S(1)}, bf16[128,1024]{1,0:T(8,128)(2,1)S(1)}, u32[]{:S(2)}, u32[]{:S(2)}) %collective-permute-start.4) | collective-permute-done | bytes 262176 | tf_op jit(solution)/shard_map/ppermute | solution.py:467
  20.1 0.9 %collective-permute-done.6.refs_2_ = bf16[128,512]{1,0:T(8,128)(2,1)S(1)} collective-permute-done((bf16[128,512]{1,0:T(8,128)(2,1)S(1)}, bf16[128,512]{1,0:T(8,128)(2,1)S(1)}, u32[]{:S(2)}, u32[]{:S(2)}) %collective-permute-start.6) | collective-permute-done | bytes 131104 | tf_op jit(solution)/shard_map/ppermute | solution.py:467
  21.0 0.0 collective-permute-done.7.sibling_ref
  21.1 1.5 %collective-permute-start.9 = (bf16[256,256]{1,0:T(8,128)(2,1)S(1)}, bf16[256,256]{1,0:T(8,128)(2,1)S(1)}, u32[]{:S(2)}, u32[]{:S(2)}) collective-permute-start(bf16[256,256]{1,0:T(8,128)(2,1)S(1)} %get-tuple-element.80.refs_0_), channel_id=1, source_target_pairs={{0,4},{1,5},{2,6},{3,7},{4,0},{5,1},{6,2},{7,3},{8,12},{9,13},{10,... | collective-permute-start | bytes 393224 | tf_op jit(solution)/shard_map/ppermute | solution.py:467
  22.6 1.6 %collective-permute-start.11 = (bf16[256,256]{1,0:T(8,128)(2,1)S(1)}, bf16[256,256]{1,0:T(8,128)(2,1)S(1)}, u32[]{:S(2)}, u32[]{:S(2)}) collective-permute-start(bf16[256,256]{1,0:T(8,128)(2,1)S(1)} %get-tuple-element.81.refs_1_), channel_id=1, source_target_pairs={{0,8},{1,9},{2,10},{3,11},{4,12},{5,13},{6,14},{7,15},{8,0},{9,1},... | collective-permute-start | bytes 393224 | tf_op jit(solution)/shard_map/ppermute | solution.py:467
  24.2 0.4 collective-permute-start.14
  24.7 0.5 %collective-permute-start.13 = (bf16[256,256]{1,0:T(8,128)(2,1)S(1)}, bf16[256,256]{1,0:T(8,128)(2,1)S(1)}, u32[]{:S(2)}, u32[]{:S(2)}) collective-permute-start(bf16[256,256]{1,0:T(8,128)(2,1)S(1)} %get-tuple-element.81.refs_1_), channel_id=1, source_target_pairs={{0,4},{1,5},{2,6},{3,7},{4,0},{5,1},{6,2},{7,3},{8,12},{9,13},{10,... | collective-permute-start | bytes 393224 | tf_op jit(solution)/shard_map/ppermute | solution.py:467
  25.2 0.3 turn_pieces.1.refs_0_
  25.5 0.1 collective-permute-start.8
  25.6 1.1 %collective-permute-done.9.refs_2_ = bf16[256,256]{1,0:T(8,128)(2,1)S(1)} collective-permute-done((bf16[256,256]{1,0:T(8,128)(2,1)S(1)}, bf16[256,256]{1,0:T(8,128)(2,1)S(1)}, u32[]{:S(2)}, u32[]{:S(2)}) %collective-permute-start.9) | collective-permute-done | bytes 131104 | tf_op jit(solution)/shard_map/ppermute | solution.py:467
  26.7 1.8 %collective-permute-start.10 = (bf16[256,256]{1,0:T(8,128)(2,1)S(1)}, bf16[256,256]{1,0:T(8,128)(2,1)S(1)}, u32[]{:S(2)}, u32[]{:S(2)}) collective-permute-start(bf16[256,256]{1,0:T(8,128)(2,1)S(1)} %collective-permute-done.9.refs_2_), channel_id=1, source_target_pairs={{0,8},{1,9},{2,10},{3,11},{4,12},{5,13},{6,14},{7,15},{8,0},{9,1},... | collective-permute-start | bytes 393224 | tf_op jit(solution)/shard_map/ppermute | solution.py:467
  28.4 0.5 %collective-permute-done.11.refs_5_ = bf16[256,256]{1,0:T(8,128)(2,1)S(1)} collective-permute-done((bf16[256,256]{1,0:T(8,128)(2,1)S(1)}, bf16[256,256]{1,0:T(8,128)(2,1)S(1)}, u32[]{:S(2)}, u32[]{:S(2)}) %collective-permute-start.11) | collective-permute-done | bytes 131104 | tf_op jit(solution)/shard_map/ppermute | solution.py:467
  29.0 1.5 %collective-permute-start.12 = (bf16[256,256]{1,0:T(8,128)(2,1)S(1)}, bf16[256,256]{1,0:T(8,128)(2,1)S(1)}, u32[]{:S(2)}, u32[]{:S(2)}) collective-permute-start(bf16[256,256]{1,0:T(8,128)(2,1)S(1)} %collective-permute-done.11.refs_5_), channel_id=1, source_target_pairs={{0,4},{1,5},{2,6},{3,7},{4,0},{5,1},{6,2},{7,3},{8,12},{9,13},{10,... | collective-permute-start | bytes 393224 | tf_op jit(solution)/shard_map/ppermute | solution.py:467
  30.5 1.3 %collective-permute-done.14.refs_4_ = bf16[256,256]{1,0:T(8,128)(2,1)S(1)} collective-permute-done((bf16[256,256]{1,0:T(8,128)(2,1)S(1)}, bf16[256,256]{1,0:T(8,128)(2,1)S(1)}, u32[]{:S(2)}, u32[]{:S(2)}) %collective-permute-start.14) | collective-permute-done | bytes 131104 | tf_op jit(solution)/shard_map/ppermute | solution.py:467
  31.8 0.0 collective-permute-done.13.refs_3_
  31.8 0.1 stack_grads.2
  31.9 1.8 %collective-permute-done.10.refs_0_ = bf16[256,256]{1,0:T(8,128)(2,1)S(1)} collective-permute-done((bf16[256,256]{1,0:T(8,128)(2,1)S(1)}, bf16[256,256]{1,0:T(8,128)(2,1)S(1)}, u32[]{:S(2)}, u32[]{:S(2)}) %collective-permute-start.10) | collective-permute-done | bytes 131104 | tf_op jit(solution)/shard_map/ppermute | solution.py:467
  33.7 0.3 collective-permute-done.12.refs_1_
  34.0 0.0 collective-permute-done.8.refs_1_
  34.0 0.5 weight_far.2
  34.5 1.3 %collective-permute-start.17 = (bf16[128,512]{1,0:T(8,128)(2,1)S(1)}, bf16[128,512]{1,0:T(8,128)(2,1)S(1)}, u32[]{:S(2)}, u32[]{:S(2)}) collective-permute-start(bf16[128,512]{1,0:T(8,128)(2,1)S(1)} %get-tuple-element.107), channel_id=1, source_target_pairs={{0,1},{1,0},{2,3},{3,2},{4,5},{5,4},{6,7},{7,6},{8,9},{9,8},{10,11... | collective-permute-start | bytes 393224 | tf_op jit(solution)/shard_map/ppermute | solution.py:467
  35.7 0.5 weight_far.3
  36.2 0.9 %collective-permute-start.15 = (bf16[128,512]{1,0:T(8,128)(2,1)S(1)}, bf16[128,512]{1,0:T(8,128)(2,1)S(1)}, u32[]{:S(2)}, u32[]{:S(2)}) collective-permute-start(bf16[128,512]{1,0:T(8,128)(2,1)S(1)} %get-tuple-element.102), channel_id=1, source_target_pairs={{0,1},{1,0},{2,3},{3,2},{4,5},{5,4},{6,7},{7,6},{8,9},{9,8},{10,11... | collective-permute-start | bytes 393224 | tf_op jit(solution)/shard_map/ppermute | solution.py:467
  37.1 0.8 %weight_near.1 = (f32[128,512]{1,0:T(8,128)S(1)}, bf16[128,512]{1,0:T(8,128)(2,1)S(1)}, bf16[128,512]{1,0:T(8,128)(2,1)S(1)}, bf16[128,512]{1,0:T(8,128)(2,1)S(1)}) custom-call(bf16[1024,512]{1,0:T(8,128)(2,1)S(1)} %turn_pieces.1.refs_0_, bf16[1024,512]{1,0:T(8,128)(2,1)S(1)} %collective-permute-done.8.refs_1_, ...), custom_call_target="tpu_custom_call" | custom-call | flops 1024 | bytes 1024 | tf_op jit(solution)/shard_map/weight_near/pallas_call | solution.py:365
  37.9 1.3 %collective-permute-start.16 = (bf16[128,512]{1,0:T(8,128)(2,1)S(1)}, bf16[128,512]{1,0:T(8,128)(2,1)S(1)}, u32[]{:S(2)}, u32[]{:S(2)}) collective-permute-start(bf16[128,512]{1,0:T(8,128)(2,1)S(1)} %get-tuple-element.106), channel_id=1, source_target_pairs={{0,1},{1,0},{2,3},{3,2},{4,5},{5,4},{6,7},{7,6},{8,9},{9,8},{10,11... | collective-permute-start | bytes 393224 | tf_op jit(solution)/shard_map/ppermute | solution.py:467
  39.2 1.3 %collective-permute-done.17.refs_0_ = bf16[128,512]{1,0:T(8,128)(2,1)S(1)} collective-permute-done((bf16[128,512]{1,0:T(8,128)(2,1)S(1)}, bf16[128,512]{1,0:T(8,128)(2,1)S(1)}, u32[]{:S(2)}, u32[]{:S(2)}) %collective-permute-start.17) | collective-permute-done | bytes 131104 | tf_op jit(solution)/shard_map/ppermute | solution.py:467
  40.5 2.6 %collective-permute-start.18 = (bf16[128,512]{1,0:T(8,128)(2,1)S(1)}, bf16[128,512]{1,0:T(8,128)(2,1)S(1)}, u32[]{:S(2)}, u32[]{:S(2)}) collective-permute-start(bf16[128,512]{1,0:T(8,128)(2,1)S(1)} %relay_total.3), channel_id=1, source_target_pairs={{0,16},{1,17},{2,18},{3,19},{4,20},{5,21},{6,22},{7,23},{8,24},{9,... | collective-permute-start | bytes 393224 | tf_op jit(solution)/shard_map/ppermute | solution.py:467
  43.1 0.1 collective-permute-done.15.refs_0_
  43.3 0.5 collective-permute-start.20
  43.8 2.3 %collective-permute-start.19 = (bf16[128,512]{1,0:T(8,128)(2,1)S(1)}, bf16[128,512]{1,0:T(8,128)(2,1)S(1)}, u32[]{:S(2)}, u32[]{:S(2)}) collective-permute-start(bf16[128,512]{1,0:T(8,128)(2,1)S(1)} %get-tuple-element.109), channel_id=1, source_target_pairs={{0,2},{1,3},{2,0},{3,1},{4,6},{5,7},{6,4},{7,5},{8,10},{9,11},{10,... | collective-permute-start | bytes 393224 | tf_op jit(solution)/shard_map/ppermute | solution.py:467
  46.1 1.3 %collective-permute-start.21 = (bf16[128,512]{1,0:T(8,128)(2,1)S(1)}, bf16[128,512]{1,0:T(8,128)(2,1)S(1)}, u32[]{:S(2)}, u32[]{:S(2)}) collective-permute-start(bf16[128,512]{1,0:T(8,128)(2,1)S(1)} %get-tuple-element.110), channel_id=1, source_target_pairs={{0,3},{1,2},{2,1},{3,0},{4,7},{5,6},{6,5},{7,4},{8,11},{9,10},{10,... | collective-permute-start | bytes 393224 | tf_op jit(solution)/shard_map/ppermute | solution.py:467
  47.3 1.7 %query_gradient.1 = bf16[128,4096]{1,0:T(8,128)(2,1)} custom-call(bf16[128,4096]{1,0:T(8,128)(2,1)S(1)} %get-tuple-element.103.refs_0_, bf16[128,4096]{1,0:T(8,128)(2,1)S(1)} %get-tuple-element.104.refs_1_, bf16[128,512]{1,0:T(8,128)(2,1)S(1)} %copy-done.2, bf16[128,512]{1,0:T(8,128)(2,1)S(1)} %collective-permute-done.refs_3_), custom_call_target="tpu_custom_call" | custom-call | flops 1024 | bytes 1024 | tf_op jit(solution)/shard_map/query_gradient/pallas_call | solution.py:155
  49.1 2.5 %collective-permute-done.21.refs_3_ = bf16[128,512]{1,0:T(8,128)(2,1)S(1)} collective-permute-done((bf16[128,512]{1,0:T(8,128)(2,1)S(1)}, bf16[128,512]{1,0:T(8,128)(2,1)S(1)}, u32[]{:S(2)}, u32[]{:S(2)}) %collective-permute-start.21) | collective-permute-done | bytes 131104 | tf_op jit(solution)/shard_map/ppermute | solution.py:467
  51.6 1.5 %collective-permute-done.20.refs_2_ = bf16[128,512]{1,0:T(8,128)(2,1)S(1)} collective-permute-done((bf16[128,512]{1,0:T(8,128)(2,1)S(1)}, bf16[128,512]{1,0:T(8,128)(2,1)S(1)}, u32[]{:S(2)}, u32[]{:S(2)}) %collective-permute-start.20) | collective-permute-done | bytes 131104 | tf_op jit(solution)/shard_map/ppermute | solution.py:467
  53.1 0.8 %weight_total.1 = (f32[128,512]{1,0:T(8,128)}, f32[128,512]{1,0:T(8,128)}) custom-call(f32[128,512]{1,0:T(8,128)S(1)} %early_total.1.refs_0_, bf16[128,512]{1,0:T(8,128)(2,1)S(1)} %collective-permute-done.19.refs_1_, bf16[128,512]{1,0:T(8,128)(2,1)S(1)} %collective-permute-done.20.refs_2_, bf16[128,512]{1,0:T(8,128)(2,1)S(1)} %collective-permute-done.21.refs_3_), custom_call_target="tpu_custom_call" | custom-call | flops 1024 | bytes 1024 | tf_op jit(solution)/shard_map/weight_total/pallas_call | solution.py:434
  (21 shorter events, 0.2 us)
Async XLA Ops:
  0.6 9.5 %copy-start.1 = (bf16[128,4096]{1,0:T(8,128)(2,1)S(1)}, bf16[128,4096]{1,0:T(8,128)(2,1)}, u32[]{:S(2)}) copy-start(bf16[128,4096]{1,0:T(8,128)(2,1)} %refs_2_.4) | copy-start | bytes 3145732
  0.6 9.5 %copy-start = (bf16[128,4096]{1,0:T(8,128)(2,1)S(1)}, bf16[128,4096]{1,0:T(8,128)(2,1)}, u32[]{:S(2)}) copy-start(bf16[128,4096]{1,0:T(8,128)(2,1)} %refs_1_.3) | copy-start | bytes 3145732
  0.7 9.4 %collective-permute-start.1 = (bf16[128,512]{1,0:T(8,128)(2,1)}, bf16[128,512]{1,0:T(8,128)(2,1)S(1)}, u32[]{:S(2)}, u32[]{:S(2)}) collective-permute-start(bf16[128,512]{1,0:T(8,128)(2,1)} %refs_4_.1), channel_id=1, source_target_pairs={{0,1},{1,0},{2,3},{3,2},{4,5},{5,4},{6,7},{7,6},{8,9},{9,8},{10,11... | collective-permute-start | bytes 393224 | tf_op jit(solution)/shard_map/ppermute | solution.py:467
  3.7 6.5 %collective-permute-start = (bf16[128,512]{1,0:T(8,128)(2,1)}, bf16[128,512]{1,0:T(8,128)(2,1)S(1)}, u32[]{:S(2)}, u32[]{:S(2)}) collective-permute-start(bf16[128,512]{1,0:T(8,128)(2,1)} %refs_2_.5), channel_id=1, source_target_pairs={{0,1},{1,0},{2,3},{3,2},{4,5},{5,4},{6,7},{7,6},{8,9},{9,8},{10,11... | collective-permute-start | bytes 393224 | tf_op jit(solution)/shard_map/ppermute | solution.py:467
  5.1 12.4 %collective-permute-start.3 = (bf16[128,1024]{1,0:T(8,128)(2,1)S(1)}, bf16[128,1024]{1,0:T(8,128)(2,1)S(1)}, u32[]{:S(2)}, u32[]{:S(2)}) collective-permute-start(bf16[128,1024]{1,0:T(8,128)(2,1)S(1)} %get-tuple-element.66), channel_id=1, source_target_pairs={{0,8},{1,9},{2,10},{3,11},{4,12},{5,13},{6,14},{7,15},{8,0},{9,1},... | collective-permute-start | bytes 786440 | tf_op jit(solution)/shard_map/ppermute | solution.py:467
  7.2 12.8 %collective-permute-start.4 = (bf16[128,1024]{1,0:T(8,128)(2,1)S(1)}, bf16[128,1024]{1,0:T(8,128)(2,1)S(1)}, u32[]{:S(2)}, u32[]{:S(2)}) collective-permute-start(bf16[128,1024]{1,0:T(8,128)(2,1)S(1)} %get-tuple-element.68), channel_id=1, source_target_pairs={{0,4},{1,5},{2,6},{3,7},{4,0},{5,1},{6,2},{7,3},{8,12},{9,13},{10,... | collective-permute-start | bytes 786440 | tf_op jit(solution)/shard_map/ppermute | solution.py:467
  8.7 11.3 %collective-permute-start.5 = (bf16[128,1024]{1,0:T(8,128)(2,1)S(1)}, bf16[128,1024]{1,0:T(8,128)(2,1)S(1)}, u32[]{:S(2)}, u32[]{:S(2)}) collective-permute-start(bf16[128,1024]{1,0:T(8,128)(2,1)S(1)} %get-tuple-element.69), channel_id=1, source_target_pairs={{0,12},{1,13},{2,14},{3,15},{4,8},{5,9},{6,10},{7,11},{8,4},{9,5},... | collective-permute-start | bytes 786440 | tf_op jit(solution)/shard_map/ppermute | solution.py:467
  10.2 5.0 %copy-start.2 = (bf16[128,512]{1,0:T(8,128)(2,1)S(1)}, bf16[128,512]{1,0:T(8,128)(2,1)}, u32[]{:S(2)}) copy-start(bf16[128,512]{1,0:T(8,128)(2,1)} %refs_2_.5) | copy-start | bytes 393220
  10.2 5.0 %copy-start.3 = (bf16[128,512]{1,0:T(8,128)(2,1)S(1)}, bf16[128,512]{1,0:T(8,128)(2,1)}, u32[]{:S(2)}) copy-start(bf16[128,512]{1,0:T(8,128)(2,1)} %refs_4_.1) | copy-start | bytes 393220
  13.3 6.7 %collective-permute-start.2 = (bf16[128,512]{1,0:T(8,128)(2,1)S(1)}, bf16[128,512]{1,0:T(8,128)(2,1)S(1)}, u32[]{:S(2)}, u32[]{:S(2)}) collective-permute-start(bf16[128,512]{1,0:T(8,128)(2,1)S(1)} %get-tuple-element.62), channel_id=1, source_target_pairs={{0,1},{1,0},{2,3},{3,2},{4,5},{5,4},{6,7},{7,6},{8,9},{9,8},{10,11... | collective-permute-start | bytes 393224 | tf_op jit(solution)/shard_map/ppermute | solution.py:467
  15.2 5.8 %collective-permute-start.6 = (bf16[128,512]{1,0:T(8,128)(2,1)S(1)}, bf16[128,512]{1,0:T(8,128)(2,1)S(1)}, u32[]{:S(2)}, u32[]{:S(2)}) collective-permute-start(bf16[128,512]{1,0:T(8,128)(2,1)S(1)} %get-tuple-element.76), channel_id=1, source_target_pairs={{0,3},{1,2},{2,1},{3,0},{4,7},{5,6},{6,5},{7,4},{8,11},{9,10},{10,... | collective-permute-start | bytes 393224 | tf_op jit(solution)/shard_map/ppermute | solution.py:467
  17.6 3.5 %collective-permute-start.7 = (bf16[128,512]{1,0:T(8,128)(2,1)S(1)}, bf16[128,512]{1,0:T(8,128)(2,1)S(1)}, u32[]{:S(2)}, u32[]{:S(2)}) collective-permute-start(bf16[128,512]{1,0:T(8,128)(2,1)S(1)} %get-tuple-element.79), channel_id=1, source_target_pairs={{0,2},{1,3},{2,0},{3,1},{4,6},{5,7},{6,4},{7,5},{8,10},{9,11},{10,... | collective-permute-start | bytes 393224 | tf_op jit(solution)/shard_map/ppermute | solution.py:467
  21.1 5.6 %collective-permute-start.9 = (bf16[256,256]{1,0:T(8,128)(2,1)S(1)}, bf16[256,256]{1,0:T(8,128)(2,1)S(1)}, u32[]{:S(2)}, u32[]{:S(2)}) collective-permute-start(bf16[256,256]{1,0:T(8,128)(2,1)S(1)} %get-tuple-element.80.refs_0_), channel_id=1, source_target_pairs={{0,4},{1,5},{2,6},{3,7},{4,0},{5,1},{6,2},{7,3},{8,12},{9,13},{10,... | collective-permute-start | bytes 393224 | tf_op jit(solution)/shard_map/ppermute | solution.py:467
  22.6 6.4 %collective-permute-start.11 = (bf16[256,256]{1,0:T(8,128)(2,1)S(1)}, bf16[256,256]{1,0:T(8,128)(2,1)S(1)}, u32[]{:S(2)}, u32[]{:S(2)}) collective-permute-start(bf16[256,256]{1,0:T(8,128)(2,1)S(1)} %get-tuple-element.81.refs_1_), channel_id=1, source_target_pairs={{0,8},{1,9},{2,10},{3,11},{4,12},{5,13},{6,14},{7,15},{8,0},{9,1},... | collective-permute-start | bytes 393224 | tf_op jit(solution)/shard_map/ppermute | solution.py:467
  24.2 7.6 %collective-permute-start.14 = (bf16[256,256]{1,0:T(8,128)(2,1)S(1)}, bf16[256,256]{1,0:T(8,128)(2,1)S(1)}, u32[]{:S(2)}, u32[]{:S(2)}) collective-permute-start(bf16[256,256]{1,0:T(8,128)(2,1)S(1)} %get-tuple-element.80.refs_0_), channel_id=1, source_target_pairs={{0,8},{1,9},{2,10},{3,11},{4,12},{5,13},{6,14},{7,15},{8,0},{9,1},... | collective-permute-start | bytes 393224 | tf_op jit(solution)/shard_map/ppermute | solution.py:467
  24.7 7.1 %collective-permute-start.13 = (bf16[256,256]{1,0:T(8,128)(2,1)S(1)}, bf16[256,256]{1,0:T(8,128)(2,1)S(1)}, u32[]{:S(2)}, u32[]{:S(2)}) collective-permute-start(bf16[256,256]{1,0:T(8,128)(2,1)S(1)} %get-tuple-element.81.refs_1_), channel_id=1, source_target_pairs={{0,4},{1,5},{2,6},{3,7},{4,0},{5,1},{6,2},{7,3},{8,12},{9,13},{10,... | collective-permute-start | bytes 393224 | tf_op jit(solution)/shard_map/ppermute | solution.py:467
  25.5 8.5 %collective-permute-start.8 = (bf16[1024,512]{1,0:T(8,128)(2,1)S(1)}, bf16[1024,512]{1,0:T(8,128)(2,1)S(1)}, u32[]{:S(2)}, u32[]{:S(2)}) collective-permute-start(bf16[1024,512]{1,0:T(8,128)(2,1)S(1)} %turn_pieces.1.refs_0_), channel_id=1, source_target_pairs={{0,2},{1,3},{2,0},{3,1},{4,6},{5,7},{6,4},{7,5},{8,10},{9,11},{10,... | collective-permute-start | bytes 3145736 | tf_op jit(solution)/shard_map/ppermute | solution.py:467
  26.7 7.0 %collective-permute-start.10 = (bf16[256,256]{1,0:T(8,128)(2,1)S(1)}, bf16[256,256]{1,0:T(8,128)(2,1)S(1)}, u32[]{:S(2)}, u32[]{:S(2)}) collective-permute-start(bf16[256,256]{1,0:T(8,128)(2,1)S(1)} %collective-permute-done.9.refs_2_), channel_id=1, source_target_pairs={{0,8},{1,9},{2,10},{3,11},{4,12},{5,13},{6,14},{7,15},{8,0},{9,1},... | collective-permute-start | bytes 393224 | tf_op jit(solution)/shard_map/ppermute | solution.py:467
  29.0 5.0 %collective-permute-start.12 = (bf16[256,256]{1,0:T(8,128)(2,1)S(1)}, bf16[256,256]{1,0:T(8,128)(2,1)S(1)}, u32[]{:S(2)}, u32[]{:S(2)}) collective-permute-start(bf16[256,256]{1,0:T(8,128)(2,1)S(1)} %collective-permute-done.11.refs_5_), channel_id=1, source_target_pairs={{0,4},{1,5},{2,6},{3,7},{4,0},{5,1},{6,2},{7,3},{8,12},{9,13},{10,... | collective-permute-start | bytes 393224 | tf_op jit(solution)/shard_map/ppermute | solution.py:467
  34.5 6.0 %collective-permute-start.17 = (bf16[128,512]{1,0:T(8,128)(2,1)S(1)}, bf16[128,512]{1,0:T(8,128)(2,1)S(1)}, u32[]{:S(2)}, u32[]{:S(2)}) collective-permute-start(bf16[128,512]{1,0:T(8,128)(2,1)S(1)} %get-tuple-element.107), channel_id=1, source_target_pairs={{0,1},{1,0},{2,3},{3,2},{4,5},{5,4},{6,7},{7,6},{8,9},{9,8},{10,11... | collective-permute-start | bytes 393224 | tf_op jit(solution)/shard_map/ppermute | solution.py:467
  36.2 7.0 %collective-permute-start.15 = (bf16[128,512]{1,0:T(8,128)(2,1)S(1)}, bf16[128,512]{1,0:T(8,128)(2,1)S(1)}, u32[]{:S(2)}, u32[]{:S(2)}) collective-permute-start(bf16[128,512]{1,0:T(8,128)(2,1)S(1)} %get-tuple-element.102), channel_id=1, source_target_pairs={{0,1},{1,0},{2,3},{3,2},{4,5},{5,4},{6,7},{7,6},{8,9},{9,8},{10,11... | collective-permute-start | bytes 393224 | tf_op jit(solution)/shard_map/ppermute | solution.py:467
  37.9 11.1 %collective-permute-start.16 = (bf16[128,512]{1,0:T(8,128)(2,1)S(1)}, bf16[128,512]{1,0:T(8,128)(2,1)S(1)}, u32[]{:S(2)}, u32[]{:S(2)}) collective-permute-start(bf16[128,512]{1,0:T(8,128)(2,1)S(1)} %get-tuple-element.106), channel_id=1, source_target_pairs={{0,1},{1,0},{2,3},{3,2},{4,5},{5,4},{6,7},{7,6},{8,9},{9,8},{10,11... | collective-permute-start | bytes 393224 | tf_op jit(solution)/shard_map/ppermute | solution.py:467
  40.5 8.6 %collective-permute-start.18 = (bf16[128,512]{1,0:T(8,128)(2,1)S(1)}, bf16[128,512]{1,0:T(8,128)(2,1)S(1)}, u32[]{:S(2)}, u32[]{:S(2)}) collective-permute-start(bf16[128,512]{1,0:T(8,128)(2,1)S(1)} %relay_total.3), channel_id=1, source_target_pairs={{0,16},{1,17},{2,18},{3,19},{4,20},{5,21},{6,22},{7,23},{8,24},{9,... | collective-permute-start | bytes 393224 | tf_op jit(solution)/shard_map/ppermute | solution.py:467
  43.3 9.8 %collective-permute-start.20 = (bf16[128,512]{1,0:T(8,128)(2,1)S(1)}, bf16[128,512]{1,0:T(8,128)(2,1)S(1)}, u32[]{:S(2)}, u32[]{:S(2)}) collective-permute-start(bf16[128,512]{1,0:T(8,128)(2,1)S(1)} %relay_total.2), channel_id=1, source_target_pairs={{0,18},{1,19},{2,16},{3,17},{4,22},{5,23},{6,20},{7,21},{8,26},{9,... | collective-permute-start | bytes 393224 | tf_op jit(solution)/shard_map/ppermute | solution.py:467
  43.8 5.3 %collective-permute-start.19 = (bf16[128,512]{1,0:T(8,128)(2,1)S(1)}, bf16[128,512]{1,0:T(8,128)(2,1)S(1)}, u32[]{:S(2)}, u32[]{:S(2)}) collective-permute-start(bf16[128,512]{1,0:T(8,128)(2,1)S(1)} %get-tuple-element.109), channel_id=1, source_target_pairs={{0,2},{1,3},{2,0},{3,1},{4,6},{5,7},{6,4},{7,5},{8,10},{9,11},{10,... | collective-permute-start | bytes 393224 | tf_op jit(solution)/shard_map/ppermute | solution.py:467
  46.1 5.6 %collective-permute-start.21 = (bf16[128,512]{1,0:T(8,128)(2,1)S(1)}, bf16[128,512]{1,0:T(8,128)(2,1)S(1)}, u32[]{:S(2)}, u32[]{:S(2)}) collective-permute-start(bf16[128,512]{1,0:T(8,128)(2,1)S(1)} %get-tuple-element.110), channel_id=1, source_target_pairs={{0,3},{1,2},{2,1},{3,0},{4,7},{5,6},{6,5},{7,4},{8,11},{9,10},{10,... | collective-permute-start | bytes 393224 | tf_op jit(solution)/shard_map/ppermute | solution.py:467

commit v18 on v17

--- a/solution.py
+++ b/solution.py
@@ -20,7 +20,8 @@
 PARAMS = pltpu.CompilerParams(vmem_limit_bytes=32 * 2**20)
 COST = pl.CostEstimate(flops=1024, bytes_accessed=1024, transcendentals=0)
 VISIT_COST = pl.CostEstimate(flops=5*10**9, bytes_accessed=1024, transcendentals=0)
-ADD_COST = pl.CostEstimate(flops=1*10**9, bytes_accessed=1024, transcendentals=0)
+SIBLING_COST = pl.CostEstimate(flops=0*10**9, bytes_accessed=1024, transcendentals=0)
+ADD_COST = pl.CostEstimate(flops=0*10**9, bytes_accessed=1024, transcendentals=0)
 STACK_COST = pl.CostEstimate(flops=2*10**9, bytes_accessed=1024, transcendentals=0)
 EARLY = pl.CostEstimate(flops=10**10, bytes_accessed=1024, transcendentals=0)
 WHOLE = pl.BlockSpec(memory_space=pltpu.VMEM)
@@ -254,63 +255,31 @@
     )(*pieces)
 
 
-def add_kernel(count, *refs):
-    same_ref, cross_ref = refs[-2:]
-    for ref, out_ref in ((refs[:count], same_ref), (refs[count:-2], cross_ref)):
-        total = ref[0][...].astype(jnp.float32)
-        for value in ref[1:]:
-            total = total + value[...].astype(jnp.float32)
-        out_ref[...] = total.astype(out_ref.dtype)
-
-
-def add_call(same, cross):
-    dims = same[0].shape
-    return pl.pallas_call(
-        functools.partial(add_kernel, len(same)),
-        in_specs=[WHOLE] * (len(same) + len(cross)),
-        out_specs=[WHOLE] * 2,
-        out_shape=[shape(dims, jnp.bfloat16), shape(dims, jnp.float32)],
-        compiler_params=PARAMS,
-        cost_estimate=ADD_COST,
-        name="returned_grads",
-    )(*same, *cross)
-
-
-def total_kernel(same_ref, cross_ref, sibling_ref, *out_refs):
-    rows = same_ref.shape[0]
-    for half, out_ref in enumerate(out_refs):
-        width = out_ref.shape[1]
-        columns = slice(half * width, (half + 1) * width)
-        out_ref[:rows, :] = same_ref[:, columns]
-        out_ref[rows:, :] = (
-            cross_ref[:, columns] + sibling_ref[:, columns].astype(jnp.float32)
-        ).astype(out_ref.dtype)
-
-
-def total_call(same, cross, sibling):
-    rows, width = same.shape
-    return pl.pallas_call(
-        total_kernel,
-        in_specs=[WHOLE] * 3,
-        out_specs=[WHOLE] * 2,
-        out_shape=[shape((2 * rows, width // 2), jnp.bfloat16)] * 2,
-        compiler_params=PARAMS,
-        cost_estimate=COST,
+def add_kernel(*refs):
+    total = refs[0][...].astype(jnp.float32)
+    for ref in refs[1:-1]:
+        total = total + ref[...].astype(jnp.float32)
+    refs[-1][...] = total.astype(refs[-1].dtype)
+
+
+def add_call(values, cost):
+    return pl.pallas_call(
+        add_kernel,
+        in_specs=[WHOLE] * len(values),
+        out_specs=WHOLE,
+        out_shape=shape(values[0].shape, jnp.bfloat16),
+        compiler_params=PARAMS,
+        cost_estimate=cost,
         name="grads_total",
-    )(same, cross, sibling)
+    )(*values)
 
 
 def stack_kernel(first, count, *refs):
-    own_ref, sibling_ref = refs[-2:]
-    rows = refs[0].shape[0] // 2
-    width = refs[0].shape[1]
+    rows = refs[0].shape[0]
     for at in range(count):
         here = slice((first + at) * rows, (first + at + 1) * rows)
-        for half in range(2):
-            ref = refs[2 * at + half]
-            columns = slice(half * width, (half + 1) * width)
-            own_ref[here, columns] = ref[:rows, :]
-            sibling_ref[here, columns] = ref[rows:, :]
+        for half, out_ref in enumerate(refs[-2:]):
+            out_ref[here, :] = refs[2 * at + half][...]
 
 
 def stack_call(grads, so_far, cost):
@@ -324,7 +293,7 @@
         functools.partial(stack_kernel, first, len(grads)),
         in_specs=[WHOLE] * len(operands),
         out_specs=[WHOLE] * 2,
-        out_shape=[shape((height // 2 * MIDDLE * NEAR, 2 * width), jnp.bfloat16)] * 2,
+        out_shape=[shape((height * MIDDLE * NEAR, width), jnp.bfloat16)] * 2,
         input_output_aliases=aliases,
         compiler_params=PARAMS,
         cost_estimate=cost,
@@ -495,11 +464,13 @@
     own_scores, own_same, own_cross = block(0, keys=saved_keys, values=saved_values, other=other)
     own_cross, pieces[1] = lax.optimization_barrier((own_cross, pieces[1]))
     sibling = send(own_cross, core_steps=1)
-    same, pieces = lax.optimization_barrier((same, pieces))
-    halves = total_call(*add_call([own_same] + same, cross), sibling)
+    same, pieces[2] = lax.optimization_barrier((same, pieces[2]))
+    sibling, pieces = lax.optimization_barrier((sibling, pieces))
+    halves = [add_call([own_same] + same, ADD_COST)]
+    halves.append(add_call([sibling] + after(cross, halves), SIBLING_COST))
     over_y = [send(value, member=2) for value in halves]
-    over_z = [send(value, member=1) for value in halves[::-1]][::-1]
-    over_both = [send(over_y[0], member=1), send(over_z[1], member=2)]
+    over_z = [send(value, member=1) for value in halves]
+    over_both = [send(after(over_y[0], over_z[0]), member=1), send(over_z[1], member=2)]
     tokens = turn_call(after([pieces[i] for i in ORDER], halves))
     grads = stack_call([halves, over_y, over_z], None, STACK_COST)
     grads = stack_call([after(over_both, grads)], list(grads), EARLY)

time: 54.2 us -> 55.2 us (1.018)
  waiting for transfers between devices: 13.5 us -> 14.5 us
    ppermute x22, waiting for transfers between devices: 13.5 us -> 14.5 us  [send(): return lax.ppermute(value, ('dp', 'ctx'), pairs)]
  transfers between devices with their start and end apart: 22 -> 22, of which waited for: 12 -> 10; matrix products, arithmetic and copies ran while one was open for 0% -> 0% of each run, Pallas kernels for 22% -> 21%
where the time goes in v18:
time: 55.2 us; the launch traced here: 55 us
  starting transfers between devices  26.6 us (48%)
  waiting for transfers between devices  14.5 us (26%)
  Pallas kernels  13 us (24%)
  between operations  0.81 us (1%)
    ppermute x22, starting transfers between devices, send(): return lax.ppermute(value, ('dp', 'ctx'), pairs)  26.6 us
    ppermute x22, waiting for transfers between devices, send(): return lax.ppermute(value, ('dp', 'ctx'), pairs)  14.5 us
    pallas_call x2, Pallas kernels, block_call(): pl.pallas_call(functools.partial(block_kernel, ctx_count, step), in_specs...  5.52 us
    pallas_call x3, Pallas kernels, weight_call(): pl.pallas_call(functools.partial(weight_kernel, core_steps, z_steps, far,...  1.77 us
    pallas_call x1, Pallas kernels, query_call(): pl.pallas_call(functools.partial(query_kernel, len(keys)), in_specs=[WHOL...  1.73 us
    pallas_call x1, Pallas kernels, pieces_call(): pl.pallas_call(functools.partial(pieces_kernel, far), in_specs=[FAR], out...  1.39 us
    pallas_call x1, Pallas kernels, near_call(): pl.pallas_call(near_kernel, in_specs=[FAR] * len(values), out_specs=[WHOL...  1.24 us
  transfers between devices with their start and end apart: 22, of which 10 were waited for; matrix products, arithmetic and copies ran while one was open for 0% of the time, Pallas kernels for 21%

profile of v18, /device:TPU:0, one launch (start us, length us, event | category | flops | bytes accessed | tf_op | source)
XLA Modules:
  0.0 55.0 jit_solution(196546419547856366)
XLA Ops:
  0.7 3.0 %collective-permute-start.1 = (bf16[128,512]{1,0:T(8,128)(2,1)}, bf16[128,512]{1,0:T(8,128)(2,1)S(1)}, u32[]{:S(2)}, u32[]{:S(2)}) collective-permute-start(bf16[128,512]{1,0:T(8,128)(2,1)} %refs_4_.1), channel_id=1, source_target_pairs={{0,1},{1,0},{2,3},{3,2},{4,5},{5,4},{6,7},{7,6},{8,9},{9,8},{10,11... | collective-permute-start | bytes 393224 | tf_op jit(solution)/shard_map/ppermute | solution.py:436
  3.7 0.1 collective-permute-start
  3.7 1.4 %pieces.1 = (bf16[128,1024]{1,0:T(8,128)(2,1)S(1)}, bf16[128,1024]{1,0:T(8,128)(2,1)S(1)}, bf16[128,1024]{1,0:T(8,128)(2,1)S(1)}, bf16[128,1024]{1,0:T(8,128)(2,1)S(1)}) custom-call(bf16[128,4096]{1,0:T(8,128)(2,1)} %in_hbm.1), custom_call_target="tpu_custom_call" | custom-call | flops 1024 | bytes 1024 | tf_op jit(solution)/shard_map/pieces/pallas_call | solution.py:226
  5.1 2.1 %collective-permute-start.2 = (bf16[128,1024]{1,0:T(8,128)(2,1)S(1)}, bf16[128,1024]{1,0:T(8,128)(2,1)S(1)}, u32[]{:S(2)}, u32[]{:S(2)}) collective-permute-start(bf16[128,1024]{1,0:T(8,128)(2,1)S(1)} %get-tuple-element.66), channel_id=1, source_target_pairs={{0,8},{1,9},{2,10},{3,11},{4,12},{5,13},{6,14},{7,15},{8,0},{9,1},... | collective-permute-start | bytes 786440 | tf_op jit(solution)/shard_map/ppermute | solution.py:436
  7.2 1.5 %collective-permute-start.5 = (bf16[128,1024]{1,0:T(8,128)(2,1)S(1)}, bf16[128,1024]{1,0:T(8,128)(2,1)S(1)}, u32[]{:S(2)}, u32[]{:S(2)}) collective-permute-start(bf16[128,1024]{1,0:T(8,128)(2,1)S(1)} %get-tuple-element.69), channel_id=1, source_target_pairs={{0,4},{1,5},{2,6},{3,7},{4,0},{5,1},{6,2},{7,3},{8,12},{9,13},{10,... | collective-permute-start | bytes 786440 | tf_op jit(solution)/shard_map/ppermute | solution.py:436
  8.7 0.0 collective-permute-start.6
  8.8 1.2 %bring_near.1 = (bf16[128,4096]{1,0:T(8,128)(2,1)S(1)}, f32[32,128]{1,0:T(8,128)S(1)}) custom-call(bf16[128,4096]{1,0:T(8,128)(2,1)} %refs_0_.3, f32[32,128]{1,0:T(8,128)} %bitcast.1), custom_call_target="tpu_custom_call" | custom-call | flops 1024 | bytes 1024 | tf_op jit(solution)/shard_map/bring_near/pallas_call | solution.py:184
  10.0 0.1 collective-permute-done.refs_3_
  10.2 3.1 %visiting_keys.1 = (bf16[128,4096]{1,0:T(8,128)(2,1)S(1)}, bf16[128,512]{1,0:T(8,128)(2,1)S(1)}, bf16[128,512]{1,0:T(8,128)(2,1)S(1)}, f32[32,128]{1,0:T(8,128)S(1)}) custom-call(s32[1,4]{1,0:T(1,128)} %refs_0_.5, bf16[128,4096]{1,0:T(8,128)(2,1)S(1)} %copy-done, bf16[128,4096]{1,0:T(8,128)(2,1)S(1)} %copy-done.1, ...), custom_call_target="tpu_custom_call" | custom-call | flops 5000000000 | bytes 1024 | tf_op jit(solution)/shard_map/visiting_keys/pallas_call | solution.py:129
  13.3 1.8 %collective-permute-start.4 = (bf16[128,512]{1,0:T(8,128)(2,1)S(1)}, bf16[128,512]{1,0:T(8,128)(2,1)S(1)}, u32[]{:S(2)}, u32[]{:S(2)}) collective-permute-start(bf16[128,512]{1,0:T(8,128)(2,1)S(1)} %get-tuple-element.63), channel_id=1, source_target_pairs={{0,1},{1,0},{2,3},{3,2},{4,5},{5,4},{6,7},{7,6},{8,9},{9,8},{10,11... | collective-permute-start | bytes 393224 | tf_op jit(solution)/shard_map/ppermute | solution.py:436
  15.2 0.0 collective-permute-start.7
  15.2 2.4 %own_keys.1 = (bf16[128,4096]{1,0:T(8,128)(2,1)S(1)}, f32[128,512]{1,0:T(8,128)S(1)}, bf16[128,512]{1,0:T(8,128)(2,1)S(1)}) custom-call(s32[1,4]{1,0:T(1,128)} %refs_0_.5, bf16[128,4096]{1,0:T(8,128)(2,1)S(1)} %copy-done, bf16[128,4096]{1,0:T(8,128)(2,1)S(1)} %copy-done.1, bf16[128,512]{1,0:T(8,128)(2,1)S(1)} %copy-done.2, bf16[128,512]{1,0:T(8,128)(2,1)S(1)} %copy-done.3, ...), custom_call_target="tpu_custom_call" | custom-call | flops 1024 | bytes 1024 | tf_op jit(solution)/shard_map/own_keys/pallas_call | solution.py:129
  17.6 0.0 collective-permute-done.2.refs_2_
  17.6 0.4 collective-permute-start.3
  18.0 2.0 %collective-permute-done.5.refs_1_ = bf16[128,1024]{1,0:T(8,128)(2,1)S(1)} collective-permute-done((bf16[128,1024]{1,0:T(8,128)(2,1)S(1)}, bf16[128,1024]{1,0:T(8,128)(2,1)S(1)}, u32[]{:S(2)}, u32[]{:S(2)}) %collective-permute-start.5) | collective-permute-done | bytes 262176 | tf_op jit(solution)/shard_map/ppermute | solution.py:436
  20.0 0.0 collective-permute-done.4.refs_1_
  20.1 0.7 %collective-permute-start.10 = (bf16[128,512]{1,0:T(8,128)(2,1)S(1)}, bf16[128,512]{1,0:T(8,128)(2,1)S(1)}, u32[]{:S(2)}, u32[]{:S(2)}) collective-permute-start(bf16[128,512]{1,0:T(8,128)(2,1)S(1)} %grads_total.2.refs_0_), channel_id=1, source_target_pairs={{0,8},{1,9},{2,10},{3,11},{4,12},{5,13},{6,14},{7,15},{8,0},{9,1},... | collective-permute-start | bytes 393224 | tf_op jit(solution)/shard_map/ppermute | solution.py:436
  20.8 1.5 %collective-permute-start.9 = (bf16[128,512]{1,0:T(8,128)(2,1)S(1)}, bf16[128,512]{1,0:T(8,128)(2,1)S(1)}, u32[]{:S(2)}, u32[]{:S(2)}) collective-permute-start(bf16[128,512]{1,0:T(8,128)(2,1)S(1)} %grads_total.2.refs_0_), channel_id=1, source_target_pairs={{0,4},{1,5},{2,6},{3,7},{4,0},{5,1},{6,2},{7,3},{8,12},{9,13},{10,... | collective-permute-start | bytes 393224 | tf_op jit(solution)/shard_map/ppermute | solution.py:436
  22.3 0.0 collective-permute-done.7.refs_1_
  22.3 0.0 collective-permute-done.6.refs_3_
  22.3 0.0 collective-permute-done.3.refs_0_
  22.4 1.4 %collective-permute-start.12 = (bf16[128,512]{1,0:T(8,128)(2,1)S(1)}, bf16[128,512]{1,0:T(8,128)(2,1)S(1)}, u32[]{:S(2)}, u32[]{:S(2)}) collective-permute-start(bf16[128,512]{1,0:T(8,128)(2,1)S(1)} %grads_total.3.refs_1_), channel_id=1, source_target_pairs={{0,8},{1,9},{2,10},{3,11},{4,12},{5,13},{6,14},{7,15},{8,0},{9,1},... | collective-permute-start | bytes 393224 | tf_op jit(solution)/shard_map/ppermute | solution.py:436
  23.8 0.5 collective-permute-start.14
  24.3 2.1 %collective-permute-done.10.refs_4_ = bf16[128,512]{1,0:T(8,128)(2,1)S(1)} collective-permute-done((bf16[128,512]{1,0:T(8,128)(2,1)S(1)}, bf16[128,512]{1,0:T(8,128)(2,1)S(1)}, u32[]{:S(2)}, u32[]{:S(2)}) %collective-permute-start.10) | collective-permute-done | bytes 131104 | tf_op jit(solution)/shard_map/ppermute | solution.py:436
  26.4 2.0 %collective-permute-start.11 = (bf16[128,512]{1,0:T(8,128)(2,1)S(1)}, bf16[128,512]{1,0:T(8,128)(2,1)S(1)}, u32[]{:S(2)}, u32[]{:S(2)}) collective-permute-start(bf16[128,512]{1,0:T(8,128)(2,1)S(1)} %collective-permute-done.9.refs_2_), channel_id=1, source_target_pairs={{0,8},{1,9},{2,10},{3,11},{4,12},{5,13},{6,14},{7,15},{8,0},{9,1},... | collective-permute-start | bytes 393224 | tf_op jit(solution)/shard_map/ppermute | solution.py:436
  28.4 0.3 turn_pieces.1.refs_0_
  28.8 0.1 collective-permute-start.8
  28.8 0.4 collective-permute-done.12.refs_5_
  29.2 1.4 %collective-permute-start.13 = (bf16[128,512]{1,0:T(8,128)(2,1)S(1)}, bf16[128,512]{1,0:T(8,128)(2,1)S(1)}, u32[]{:S(2)}, u32[]{:S(2)}) collective-permute-start(bf16[128,512]{1,0:T(8,128)(2,1)S(1)} %collective-permute-done.12.refs_5_), channel_id=1, source_target_pairs={{0,4},{1,5},{2,6},{3,7},{4,0},{5,1},{6,2},{7,3},{8,12},{9,13},{10,... | collective-permute-start | bytes 393224 | tf_op jit(solution)/shard_map/ppermute | solution.py:436
  30.6 0.1 stack_grads.2
  30.7 0.7 %collective-permute-done.11.refs_0_ = bf16[128,512]{1,0:T(8,128)(2,1)S(1)} collective-permute-done((bf16[128,512]{1,0:T(8,128)(2,1)S(1)}, bf16[128,512]{1,0:T(8,128)(2,1)S(1)}, u32[]{:S(2)}, u32[]{:S(2)}) %collective-permute-start.11) | collective-permute-done | bytes 131104 | tf_op jit(solution)/shard_map/ppermute | solution.py:436
  31.4 3.4 %collective-permute-done.13.refs_1_ = bf16[128,512]{1,0:T(8,128)(2,1)S(1)} collective-permute-done((bf16[128,512]{1,0:T(8,128)(2,1)S(1)}, bf16[128,512]{1,0:T(8,128)(2,1)S(1)}, u32[]{:S(2)}, u32[]{:S(2)}) %collective-permute-start.13) | collective-permute-done | bytes 131104 | tf_op jit(solution)/shard_map/ppermute | solution.py:436
  34.8 0.5 weight_far.2
  35.3 1.5 %collective-permute-start.17 = (bf16[128,512]{1,0:T(8,128)(2,1)S(1)}, bf16[128,512]{1,0:T(8,128)(2,1)S(1)}, u32[]{:S(2)}, u32[]{:S(2)}) collective-permute-start(bf16[128,512]{1,0:T(8,128)(2,1)S(1)} %get-tuple-element.107), channel_id=1, source_target_pairs={{0,1},{1,0},{2,3},{3,2},{4,5},{5,4},{6,7},{7,6},{8,9},{9,8},{10,11... | collective-permute-start | bytes 393224 | tf_op jit(solution)/shard_map/ppermute | solution.py:436
  36.8 0.5 weight_far.3
  37.3 0.6 %collective-permute-start.15 = (bf16[128,512]{1,0:T(8,128)(2,1)S(1)}, bf16[128,512]{1,0:T(8,128)(2,1)S(1)}, u32[]{:S(2)}, u32[]{:S(2)}) collective-permute-start(bf16[128,512]{1,0:T(8,128)(2,1)S(1)} %get-tuple-element.102), channel_id=1, source_target_pairs={{0,1},{1,0},{2,3},{3,2},{4,5},{5,4},{6,7},{7,6},{8,9},{9,8},{10,11... | collective-permute-start | bytes 393224 | tf_op jit(solution)/shard_map/ppermute | solution.py:436
  37.9 0.8 %weight_near.1 = (f32[128,512]{1,0:T(8,128)S(1)}, bf16[128,512]{1,0:T(8,128)(2,1)S(1)}, bf16[128,512]{1,0:T(8,128)(2,1)S(1)}, bf16[128,512]{1,0:T(8,128)(2,1)S(1)}) custom-call(bf16[1024,512]{1,0:T(8,128)(2,1)S(1)} %turn_pieces.1.refs_0_, bf16[1024,512]{1,0:T(8,128)(2,1)S(1)} %collective-permute-done.8.refs_1_, ...), custom_call_target="tpu_custom_call" | custom-call | flops 1024 | bytes 1024 | tf_op jit(solution)/shard_map/weight_near/pallas_call | solution.py:334
  38.7 1.5 %collective-permute-start.16 = (bf16[128,512]{1,0:T(8,128)(2,1)S(1)}, bf16[128,512]{1,0:T(8,128)(2,1)S(1)}, u32[]{:S(2)}, u32[]{:S(2)}) collective-permute-start(bf16[128,512]{1,0:T(8,128)(2,1)S(1)} %get-tuple-element.106), channel_id=1, source_target_pairs={{0,1},{1,0},{2,3},{3,2},{4,5},{5,4},{6,7},{7,6},{8,9},{9,8},{10,11... | collective-permute-start | bytes 393224 | tf_op jit(solution)/shard_map/ppermute | solution.py:436
  40.2 1.5 %collective-permute-done.17.refs_0_ = bf16[128,512]{1,0:T(8,128)(2,1)S(1)} collective-permute-done((bf16[128,512]{1,0:T(8,128)(2,1)S(1)}, bf16[128,512]{1,0:T(8,128)(2,1)S(1)}, u32[]{:S(2)}, u32[]{:S(2)}) %collective-permute-start.17) | collective-permute-done | bytes 131104 | tf_op jit(solution)/shard_map/ppermute | solution.py:436
  41.7 2.7 %collective-permute-start.18 = (bf16[128,512]{1,0:T(8,128)(2,1)S(1)}, bf16[128,512]{1,0:T(8,128)(2,1)S(1)}, u32[]{:S(2)}, u32[]{:S(2)}) collective-permute-start(bf16[128,512]{1,0:T(8,128)(2,1)S(1)} %relay_total.3), channel_id=1, source_target_pairs={{0,16},{1,17},{2,18},{3,19},{4,20},{5,21},{6,22},{7,23},{8,24},{9,... | collective-permute-start | bytes 393224 | tf_op jit(solution)/shard_map/ppermute | solution.py:436
  44.5 0.1 collective-permute-start.20
  44.6 2.8 %collective-permute-start.19 = (bf16[128,512]{1,0:T(8,128)(2,1)S(1)}, bf16[128,512]{1,0:T(8,128)(2,1)S(1)}, u32[]{:S(2)}, u32[]{:S(2)}) collective-permute-start(bf16[128,512]{1,0:T(8,128)(2,1)S(1)} %get-tuple-element.109), channel_id=1, source_target_pairs={{0,2},{1,3},{2,0},{3,1},{4,6},{5,7},{6,4},{7,5},{8,10},{9,11},{10,... | collective-permute-start | bytes 393224 | tf_op jit(solution)/shard_map/ppermute | solution.py:436
  47.4 0.7 %collective-permute-start.21 = (bf16[128,512]{1,0:T(8,128)(2,1)S(1)}, bf16[128,512]{1,0:T(8,128)(2,1)S(1)}, u32[]{:S(2)}, u32[]{:S(2)}) collective-permute-start(bf16[128,512]{1,0:T(8,128)(2,1)S(1)} %get-tuple-element.110), channel_id=1, source_target_pairs={{0,3},{1,2},{2,1},{3,0},{4,7},{5,6},{6,5},{7,4},{8,11},{9,10},{10,... | collective-permute-start | bytes 393224 | tf_op jit(solution)/shard_map/ppermute | solution.py:436
  48.1 1.7 %query_gradient.1 = bf16[128,4096]{1,0:T(8,128)(2,1)} custom-call(bf16[128,4096]{1,0:T(8,128)(2,1)S(1)} %get-tuple-element.103.refs_0_, bf16[128,4096]{1,0:T(8,128)(2,1)S(1)} %get-tuple-element.104.refs_1_, bf16[128,512]{1,0:T(8,128)(2,1)S(1)} %copy-done.2, bf16[128,512]{1,0:T(8,128)(2,1)S(1)} %collective-permute-done.refs_3_), custom_call_target="tpu_custom_call" | custom-call | flops 1024 | bytes 1024 | tf_op jit(solution)/shard_map/query_gradient/pallas_call | solution.py:156
  49.9 2.6 %collective-permute-done.18.refs_2_ = bf16[128,512]{1,0:T(8,128)(2,1)S(1)} collective-permute-done((bf16[128,512]{1,0:T(8,128)(2,1)S(1)}, bf16[128,512]{1,0:T(8,128)(2,1)S(1)}, u32[]{:S(2)}, u32[]{:S(2)}) %collective-permute-start.18) | collective-permute-done | bytes 131104 | tf_op jit(solution)/shard_map/ppermute | solution.py:436
  52.5 0.5 collective-permute-done.21.refs_3_
  53.0 1.1 %collective-permute-done.20.refs_2_ = bf16[128,512]{1,0:T(8,128)(2,1)S(1)} collective-permute-done((bf16[128,512]{1,0:T(8,128)(2,1)S(1)}, bf16[128,512]{1,0:T(8,128)(2,1)S(1)}, u32[]{:S(2)}, u32[]{:S(2)}) %collective-permute-start.20) | collective-permute-done | bytes 131104 | tf_op jit(solution)/shard_map/ppermute | solution.py:436
  54.2 0.8 %weight_total.1 = (f32[128,512]{1,0:T(8,128)}, f32[128,512]{1,0:T(8,128)}) custom-call(f32[128,512]{1,0:T(8,128)S(1)} %early_total.1.refs_0_, bf16[128,512]{1,0:T(8,128)(2,1)S(1)} %collective-permute-done.19.refs_1_, bf16[128,512]{1,0:T(8,128)(2,1)S(1)} %collective-permute-done.20.refs_2_, bf16[128,512]{1,0:T(8,128)(2,1)S(1)} %collective-permute-done.21.refs_3_), custom_call_target="tpu_custom_call" | custom-call | flops 1024 | bytes 1024 | tf_op jit(solution)/shard_map/weight_total/pallas_call | solution.py:403
  (21 shorter events, 0.2 us)
Async XLA Ops:
  0.6 9.5 %copy-start.1 = (bf16[128,4096]{1,0:T(8,128)(2,1)S(1)}, bf16[128,4096]{1,0:T(8,128)(2,1)}, u32[]{:S(2)}) copy-start(bf16[128,4096]{1,0:T(8,128)(2,1)} %refs_2_.4) | copy-start | bytes 3145732
  0.6 9.5 %copy-start = (bf16[128,4096]{1,0:T(8,128)(2,1)S(1)}, bf16[128,4096]{1,0:T(8,128)(2,1)}, u32[]{:S(2)}) copy-start(bf16[128,4096]{1,0:T(8,128)(2,1)} %refs_1_.3) | copy-start | bytes 3145732
  0.7 9.4 %collective-permute-start.1 = (bf16[128,512]{1,0:T(8,128)(2,1)}, bf16[128,512]{1,0:T(8,128)(2,1)S(1)}, u32[]{:S(2)}, u32[]{:S(2)}) collective-permute-start(bf16[128,512]{1,0:T(8,128)(2,1)} %refs_4_.1), channel_id=1, source_target_pairs={{0,1},{1,0},{2,3},{3,2},{4,5},{5,4},{6,7},{7,6},{8,9},{9,8},{10,11... | collective-permute-start | bytes 393224 | tf_op jit(solution)/shard_map/ppermute | solution.py:436
  3.7 6.5 %collective-permute-start = (bf16[128,512]{1,0:T(8,128)(2,1)}, bf16[128,512]{1,0:T(8,128)(2,1)S(1)}, u32[]{:S(2)}, u32[]{:S(2)}) collective-permute-start(bf16[128,512]{1,0:T(8,128)(2,1)} %refs_2_.5), channel_id=1, source_target_pairs={{0,1},{1,0},{2,3},{3,2},{4,5},{5,4},{6,7},{7,6},{8,9},{9,8},{10,11... | collective-permute-start | bytes 393224 | tf_op jit(solution)/shard_map/ppermute | solution.py:436
  5.1 12.4 %collective-permute-start.2 = (bf16[128,1024]{1,0:T(8,128)(2,1)S(1)}, bf16[128,1024]{1,0:T(8,128)(2,1)S(1)}, u32[]{:S(2)}, u32[]{:S(2)}) collective-permute-start(bf16[128,1024]{1,0:T(8,128)(2,1)S(1)} %get-tuple-element.66), channel_id=1, source_target_pairs={{0,8},{1,9},{2,10},{3,11},{4,12},{5,13},{6,14},{7,15},{8,0},{9,1},... | collective-permute-start | bytes 786440 | tf_op jit(solution)/shard_map/ppermute | solution.py:436
  7.2 12.8 %collective-permute-start.5 = (bf16[128,1024]{1,0:T(8,128)(2,1)S(1)}, bf16[128,1024]{1,0:T(8,128)(2,1)S(1)}, u32[]{:S(2)}, u32[]{:S(2)}) collective-permute-start(bf16[128,1024]{1,0:T(8,128)(2,1)S(1)} %get-tuple-element.69), channel_id=1, source_target_pairs={{0,4},{1,5},{2,6},{3,7},{4,0},{5,1},{6,2},{7,3},{8,12},{9,13},{10,... | collective-permute-start | bytes 786440 | tf_op jit(solution)/shard_map/ppermute | solution.py:436
  8.7 13.6 %collective-permute-start.6 = (bf16[128,1024]{1,0:T(8,128)(2,1)S(1)}, bf16[128,1024]{1,0:T(8,128)(2,1)S(1)}, u32[]{:S(2)}, u32[]{:S(2)}) collective-permute-start(bf16[128,1024]{1,0:T(8,128)(2,1)S(1)} %get-tuple-element.71), channel_id=1, source_target_pairs={{0,12},{1,13},{2,14},{3,15},{4,8},{5,9},{6,10},{7,11},{8,4},{9,5},... | collective-permute-start | bytes 786440 | tf_op jit(solution)/shard_map/ppermute | solution.py:436
  10.2 5.0 %copy-start.2 = (bf16[128,512]{1,0:T(8,128)(2,1)S(1)}, bf16[128,512]{1,0:T(8,128)(2,1)}, u32[]{:S(2)}) copy-start(bf16[128,512]{1,0:T(8,128)(2,1)} %refs_2_.5) | copy-start | bytes 393220
  10.2 5.0 %copy-start.3 = (bf16[128,512]{1,0:T(8,128)(2,1)S(1)}, bf16[128,512]{1,0:T(8,128)(2,1)}, u32[]{:S(2)}) copy-start(bf16[128,512]{1,0:T(8,128)(2,1)} %refs_4_.1) | copy-start | bytes 393220
  13.3 6.7 %collective-permute-start.4 = (bf16[128,512]{1,0:T(8,128)(2,1)S(1)}, bf16[128,512]{1,0:T(8,128)(2,1)S(1)}, u32[]{:S(2)}, u32[]{:S(2)}) collective-permute-start(bf16[128,512]{1,0:T(8,128)(2,1)S(1)} %get-tuple-element.63), channel_id=1, source_target_pairs={{0,1},{1,0},{2,3},{3,2},{4,5},{5,4},{6,7},{7,6},{8,9},{9,8},{10,11... | collective-permute-start | bytes 393224 | tf_op jit(solution)/shard_map/ppermute | solution.py:436
  15.2 7.2 %collective-permute-start.7 = (bf16[128,512]{1,0:T(8,128)(2,1)S(1)}, bf16[128,512]{1,0:T(8,128)(2,1)S(1)}, u32[]{:S(2)}, u32[]{:S(2)}) collective-permute-start(bf16[128,512]{1,0:T(8,128)(2,1)S(1)} %get-tuple-element.79), channel_id=1, source_target_pairs={{0,3},{1,2},{2,1},{3,0},{4,7},{5,6},{6,5},{7,4},{8,11},{9,10},{10,... | collective-permute-start | bytes 393224 | tf_op jit(solution)/shard_map/ppermute | solution.py:436
  17.6 4.8 %collective-permute-start.3 = (bf16[128,512]{1,0:T(8,128)(2,1)S(1)}, bf16[128,512]{1,0:T(8,128)(2,1)S(1)}, u32[]{:S(2)}, u32[]{:S(2)}) collective-permute-start(bf16[128,512]{1,0:T(8,128)(2,1)S(1)} %get-tuple-element.67), channel_id=1, source_target_pairs={{0,2},{1,3},{2,0},{3,1},{4,6},{5,7},{6,4},{7,5},{8,10},{9,11},{10,... | collective-permute-start | bytes 393224 | tf_op jit(solution)/shard_map/ppermute | solution.py:436
  20.1 6.3 %collective-permute-start.10 = (bf16[128,512]{1,0:T(8,128)(2,1)S(1)}, bf16[128,512]{1,0:T(8,128)(2,1)S(1)}, u32[]{:S(2)}, u32[]{:S(2)}) collective-permute-start(bf16[128,512]{1,0:T(8,128)(2,1)S(1)} %grads_total.2.refs_0_), channel_id=1, source_target_pairs={{0,8},{1,9},{2,10},{3,11},{4,12},{5,13},{6,14},{7,15},{8,0},{9,1},... | collective-permute-start | bytes 393224 | tf_op jit(solution)/shard_map/ppermute | solution.py:436
  20.8 5.6 %collective-permute-start.9 = (bf16[128,512]{1,0:T(8,128)(2,1)S(1)}, bf16[128,512]{1,0:T(8,128)(2,1)S(1)}, u32[]{:S(2)}, u32[]{:S(2)}) collective-permute-start(bf16[128,512]{1,0:T(8,128)(2,1)S(1)} %grads_total.2.refs_0_), channel_id=1, source_target_pairs={{0,4},{1,5},{2,6},{3,7},{4,0},{5,1},{6,2},{7,3},{8,12},{9,13},{10,... | collective-permute-start | bytes 393224 | tf_op jit(solution)/shard_map/ppermute | solution.py:436
  22.4 6.9 %collective-permute-start.12 = (bf16[128,512]{1,0:T(8,128)(2,1)S(1)}, bf16[128,512]{1,0:T(8,128)(2,1)S(1)}, u32[]{:S(2)}, u32[]{:S(2)}) collective-permute-start(bf16[128,512]{1,0:T(8,128)(2,1)S(1)} %grads_total.3.refs_1_), channel_id=1, source_target_pairs={{0,8},{1,9},{2,10},{3,11},{4,12},{5,13},{6,14},{7,15},{8,0},{9,1},... | collective-permute-start | bytes 393224 | tf_op jit(solution)/shard_map/ppermute | solution.py:436
  23.8 6.8 %collective-permute-start.14 = (bf16[128,512]{1,0:T(8,128)(2,1)S(1)}, bf16[128,512]{1,0:T(8,128)(2,1)S(1)}, u32[]{:S(2)}, u32[]{:S(2)}) collective-permute-start(bf16[128,512]{1,0:T(8,128)(2,1)S(1)} %grads_total.3.refs_1_), channel_id=1, source_target_pairs={{0,4},{1,5},{2,6},{3,7},{4,0},{5,1},{6,2},{7,3},{8,12},{9,13},{10,... | collective-permute-start | bytes 393224 | tf_op jit(solution)/shard_map/ppermute | solution.py:436
  26.4 5.0 %collective-permute-start.11 = (bf16[128,512]{1,0:T(8,128)(2,1)S(1)}, bf16[128,512]{1,0:T(8,128)(2,1)S(1)}, u32[]{:S(2)}, u32[]{:S(2)}) collective-permute-start(bf16[128,512]{1,0:T(8,128)(2,1)S(1)} %collective-permute-done.9.refs_2_), channel_id=1, source_target_pairs={{0,8},{1,9},{2,10},{3,11},{4,12},{5,13},{6,14},{7,15},{8,0},{9,1},... | collective-permute-start | bytes 393224 | tf_op jit(solution)/shard_map/ppermute | solution.py:436
  28.8 6.0 %collective-permute-start.8 = (bf16[1024,512]{1,0:T(8,128)(2,1)S(1)}, bf16[1024,512]{1,0:T(8,128)(2,1)S(1)}, u32[]{:S(2)}, u32[]{:S(2)}) collective-permute-start(bf16[1024,512]{1,0:T(8,128)(2,1)S(1)} %turn_pieces.1.refs_0_), channel_id=1, source_target_pairs={{0,2},{1,3},{2,0},{3,1},{4,6},{5,7},{6,4},{7,5},{8,10},{9,11},{10,... | collective-permute-start | bytes 3145736 | tf_op jit(solution)/shard_map/ppermute | solution.py:436
  29.2 5.5 %collective-permute-start.13 = (bf16[128,512]{1,0:T(8,128)(2,1)S(1)}, bf16[128,512]{1,0:T(8,128)(2,1)S(1)}, u32[]{:S(2)}, u32[]{:S(2)}) collective-permute-start(bf16[128,512]{1,0:T(8,128)(2,1)S(1)} %collective-permute-done.12.refs_5_), channel_id=1, source_target_pairs={{0,4},{1,5},{2,6},{3,7},{4,0},{5,1},{6,2},{7,3},{8,12},{9,13},{10,... | collective-permute-start | bytes 393224 | tf_op jit(solution)/shard_map/ppermute | solution.py:436
  35.3 6.4 %collective-permute-start.17 = (bf16[128,512]{1,0:T(8,128)(2,1)S(1)}, bf16[128,512]{1,0:T(8,128)(2,1)S(1)}, u32[]{:S(2)}, u32[]{:S(2)}) collective-permute-start(bf16[128,512]{1,0:T(8,128)(2,1)S(1)} %get-tuple-element.107), channel_id=1, source_target_pairs={{0,1},{1,0},{2,3},{3,2},{4,5},{5,4},{6,7},{7,6},{8,9},{9,8},{10,11... | collective-permute-start | bytes 393224 | tf_op jit(solution)/shard_map/ppermute | solution.py:436
  37.3 7.2 %collective-permute-start.15 = (bf16[128,512]{1,0:T(8,128)(2,1)S(1)}, bf16[128,512]{1,0:T(8,128)(2,1)S(1)}, u32[]{:S(2)}, u32[]{:S(2)}) collective-permute-start(bf16[128,512]{1,0:T(8,128)(2,1)S(1)} %get-tuple-element.102), channel_id=1, source_target_pairs={{0,1},{1,0},{2,3},{3,2},{4,5},{5,4},{6,7},{7,6},{8,9},{9,8},{10,11... | collective-permute-start | bytes 393224 | tf_op jit(solution)/shard_map/ppermute | solution.py:436
  38.7 11.1 %collective-permute-start.16 = (bf16[128,512]{1,0:T(8,128)(2,1)S(1)}, bf16[128,512]{1,0:T(8,128)(2,1)S(1)}, u32[]{:S(2)}, u32[]{:S(2)}) collective-permute-start(bf16[128,512]{1,0:T(8,128)(2,1)S(1)} %get-tuple-element.106), channel_id=1, source_target_pairs={{0,1},{1,0},{2,3},{3,2},{4,5},{5,4},{6,7},{7,6},{8,9},{9,8},{10,11... | collective-permute-start | bytes 393224 | tf_op jit(solution)/shard_map/ppermute | solution.py:436
  41.7 10.7 %collective-permute-start.18 = (bf16[128,512]{1,0:T(8,128)(2,1)S(1)}, bf16[128,512]{1,0:T(8,128)(2,1)S(1)}, u32[]{:S(2)}, u32[]{:S(2)}) collective-permute-start(bf16[128,512]{1,0:T(8,128)(2,1)S(1)} %relay_total.3), channel_id=1, source_target_pairs={{0,16},{1,17},{2,18},{3,19},{4,20},{5,21},{6,22},{7,23},{8,24},{9,... | collective-permute-start | bytes 393224 | tf_op jit(solution)/shard_map/ppermute | solution.py:436
  44.5 9.6 %collective-permute-start.20 = (bf16[128,512]{1,0:T(8,128)(2,1)S(1)}, bf16[128,512]{1,0:T(8,128)(2,1)S(1)}, u32[]{:S(2)}, u32[]{:S(2)}) collective-permute-start(bf16[128,512]{1,0:T(8,128)(2,1)S(1)} %relay_total.2), channel_id=1, source_target_pairs={{0,18},{1,19},{2,16},{3,17},{4,22},{5,23},{6,20},{7,21},{8,26},{9,... | collective-permute-start | bytes 393224 | tf_op jit(solution)/shard_map/ppermute | solution.py:436
  44.6 7.9 %collective-permute-start.19 = (bf16[128,512]{1,0:T(8,128)(2,1)S(1)}, bf16[128,512]{1,0:T(8,128)(2,1)S(1)}, u32[]{:S(2)}, u32[]{:S(2)}) collective-permute-start(bf16[128,512]{1,0:T(8,128)(2,1)S(1)} %get-tuple-element.109), channel_id=1, source_target_pairs={{0,2},{1,3},{2,0},{3,1},{4,6},{5,7},{6,4},{7,5},{8,10},{9,11},{10,... | collective-permute-start | bytes 393224 | tf_op jit(solution)/shard_map/ppermute | solution.py:436
  47.4 5.6 %collective-permute-start.21 = (bf16[128,512]{1,0:T(8,128)(2,1)S(1)}, bf16[128,512]{1,0:T(8,128)(2,1)S(1)}, u32[]{:S(2)}, u32[]{:S(2)}) collective-permute-start(bf16[128,512]{1,0:T(8,128)(2,1)S(1)} %get-tuple-element.110), channel_id=1, source_target_pairs={{0,3},{1,2},{2,1},{3,0},{4,7},{5,6},{6,5},{7,4},{8,11},{9,10},{10,... | collective-permute-start | bytes 393224 | tf_op jit(solution)/shard_map/ppermute | solution.py:436

commit v19 on v18

--- a/solution.py
+++ b/solution.py
@@ -23,6 +23,7 @@
 SIBLING_COST = pl.CostEstimate(flops=0*10**9, bytes_accessed=1024, transcendentals=0)
 ADD_COST = pl.CostEstimate(flops=0*10**9, bytes_accessed=1024, transcendentals=0)
 STACK_COST = pl.CostEstimate(flops=2*10**9, bytes_accessed=1024, transcendentals=0)
+LAST_COST = pl.CostEstimate(flops=10**10, bytes_accessed=1024, transcendentals=0)
 EARLY = pl.CostEstimate(flops=10**10, bytes_accessed=1024, transcendentals=0)
 WHOLE = pl.BlockSpec(memory_space=pltpu.VMEM)
 FAR = pl.BlockSpec(memory_space=pltpu.HBM)
@@ -465,15 +466,14 @@
     own_cross, pieces[1] = lax.optimization_barrier((own_cross, pieces[1]))
     sibling = send(own_cross, core_steps=1)
     same, pieces[2] = lax.optimization_barrier((same, pieces[2]))
-    sibling, pieces = lax.optimization_barrier((sibling, pieces))
     halves = [add_call([own_same] + same, ADD_COST)]
-    halves.append(add_call([sibling] + after(cross, halves), SIBLING_COST))
+    tokens = turn_call(after([pieces[i] for i in ORDER], halves))
+    halves.append(add_call([sibling] + after(cross, tokens), SIBLING_COST))
     over_y = [send(value, member=2) for value in halves]
     over_z = [send(value, member=1) for value in halves]
     over_both = [send(after(over_y[0], over_z[0]), member=1), send(over_z[1], member=2)]
-    tokens = turn_call(after([pieces[i] for i in ORDER], halves))
     grads = stack_call([halves, over_y, over_z], None, STACK_COST)
-    grads = stack_call([after(over_both, grads)], list(grads), EARLY)
+    grads = stack_call([after(over_both, grads)], list(grads), LAST_COST)
     tokens = [tokens, after(send(tokens, core_steps=1), grads)]
     weights = functools.partial(weight_call, far=far, ctx_count=ctx_count, tokens=tokens)
     steps = tuple(range(1, far))

time: 55.2 us -> 53.8 us (0.975)
  starting transfers between devices: 26.6 us -> 24.6 us
    ppermute x22, starting transfers between devices: 26.6 us -> 24.6 us  [send(): return lax.ppermute(value, ('dp', 'ctx'), pairs)]
  transfers between devices with their start and end apart: 22 -> 22, of which waited for: 10 -> 9; matrix products, arithmetic and copies ran while one was open for 0% -> 0% of each run, Pallas kernels for 21% -> 22%
where the time goes in v19:
time: 53.8 us; the launch traced here: 53.5 us
  starting transfers between devices  24.6 us (46%)
  waiting for transfers between devices  15 us (28%)
  Pallas kernels  13 us (24%)
  between operations  0.82 us (2%)
    ppermute x22, starting transfers between devices, send(): return lax.ppermute(value, ('dp', 'ctx'), pairs)  24.6 us
    ppermute x22, waiting for transfers between devices, send(): return lax.ppermute(value, ('dp', 'ctx'), pairs)  15 us
    pallas_call x2, Pallas kernels, block_call(): pl.pallas_call(functools.partial(block_kernel, ctx_count, step), in_specs...  5.52 us
    pallas_call x3, Pallas kernels, weight_call(): pl.pallas_call(functools.partial(weight_kernel, core_steps, z_steps, far,...  1.77 us
    pallas_call x1, Pallas kernels, query_call(): pl.pallas_call(functools.partial(query_kernel, len(keys)), in_specs=[WHOL...  1.73 us
    pallas_call x1, Pallas kernels, pieces_call(): pl.pallas_call(functools.partial(pieces_kernel, far), in_specs=[FAR], out...  1.39 us
    pallas_call x1, Pallas kernels, near_call(): pl.pallas_call(near_kernel, in_specs=[FAR] * len(values), out_specs=[WHOL...  1.24 us
  transfers between devices with their start and end apart: 22, of which 9 were waited for; matrix products, arithmetic and copies ran while one was open for 0% of the time, Pallas kernels for 22%

profile of v19, /device:TPU:0, one launch (start us, length us, event | category | flops | bytes accessed | tf_op | source)
XLA Modules:
  0.0 53.5 jit_solution(11819325241392573726)
XLA Ops:
  0.7 3.0 %collective-permute-start.1 = (bf16[128,512]{1,0:T(8,128)(2,1)}, bf16[128,512]{1,0:T(8,128)(2,1)S(1)}, u32[]{:S(2)}, u32[]{:S(2)}) collective-permute-start(bf16[128,512]{1,0:T(8,128)(2,1)} %refs_4_.1), channel_id=1, source_target_pairs={{0,1},{1,0},{2,3},{3,2},{4,5},{5,4},{6,7},{7,6},{8,9},{9,8},{10,11... | collective-permute-start | bytes 393224 | tf_op jit(solution)/shard_map/ppermute | solution.py:437
  3.7 0.1 collective-permute-start
  3.7 1.4 %pieces.1 = (bf16[128,1024]{1,0:T(8,128)(2,1)S(1)}, bf16[128,1024]{1,0:T(8,128)(2,1)S(1)}, bf16[128,1024]{1,0:T(8,128)(2,1)S(1)}, bf16[128,1024]{1,0:T(8,128)(2,1)S(1)}) custom-call(bf16[128,4096]{1,0:T(8,128)(2,1)} %in_hbm.1), custom_call_target="tpu_custom_call" | custom-call | flops 1024 | bytes 1024 | tf_op jit(solution)/shard_map/pieces/pallas_call | solution.py:227
  5.1 2.0 %collective-permute-start.3 = (bf16[128,1024]{1,0:T(8,128)(2,1)S(1)}, bf16[128,1024]{1,0:T(8,128)(2,1)S(1)}, u32[]{:S(2)}, u32[]{:S(2)}) collective-permute-start(bf16[128,1024]{1,0:T(8,128)(2,1)S(1)} %get-tuple-element.58), channel_id=1, source_target_pairs={{0,4},{1,5},{2,6},{3,7},{4,0},{5,1},{6,2},{7,3},{8,12},{9,13},{10,... | collective-permute-start | bytes 786440 | tf_op jit(solution)/shard_map/ppermute | solution.py:437
  7.2 1.6 %collective-permute-start.4 = (bf16[128,1024]{1,0:T(8,128)(2,1)S(1)}, bf16[128,1024]{1,0:T(8,128)(2,1)S(1)}, u32[]{:S(2)}, u32[]{:S(2)}) collective-permute-start(bf16[128,1024]{1,0:T(8,128)(2,1)S(1)} %get-tuple-element.63), channel_id=1, source_target_pairs={{0,8},{1,9},{2,10},{3,11},{4,12},{5,13},{6,14},{7,15},{8,0},{9,1},... | collective-permute-start | bytes 786440 | tf_op jit(solution)/shard_map/ppermute | solution.py:437
  8.7 0.0 collective-permute-start.5
  8.7 1.2 %bring_near.1 = (bf16[128,4096]{1,0:T(8,128)(2,1)S(1)}, f32[32,128]{1,0:T(8,128)S(1)}) custom-call(bf16[128,4096]{1,0:T(8,128)(2,1)} %refs_0_.3, f32[32,128]{1,0:T(8,128)} %bitcast.1), custom_call_target="tpu_custom_call" | custom-call | flops 1024 | bytes 1024 | tf_op jit(solution)/shard_map/bring_near/pallas_call | solution.py:185
  10.0 0.2 collective-permute-done.refs_3_
  10.2 3.1 %visiting_keys.1 = (bf16[128,4096]{1,0:T(8,128)(2,1)S(1)}, bf16[128,512]{1,0:T(8,128)(2,1)S(1)}, bf16[128,512]{1,0:T(8,128)(2,1)S(1)}, f32[32,128]{1,0:T(8,128)S(1)}) custom-call(s32[1,4]{1,0:T(1,128)} %refs_0_.5, bf16[128,4096]{1,0:T(8,128)(2,1)S(1)} %copy-done, bf16[128,4096]{1,0:T(8,128)(2,1)S(1)} %copy-done.1, ...), custom_call_target="tpu_custom_call" | custom-call | flops 5000000000 | bytes 1024 | tf_op jit(solution)/shard_map/visiting_keys/pallas_call | solution.py:130
  13.3 1.8 %collective-permute-start.2 = (bf16[128,512]{1,0:T(8,128)(2,1)S(1)}, bf16[128,512]{1,0:T(8,128)(2,1)S(1)}, u32[]{:S(2)}, u32[]{:S(2)}) collective-permute-start(bf16[128,512]{1,0:T(8,128)(2,1)S(1)} %get-tuple-element.57), channel_id=1, source_target_pairs={{0,1},{1,0},{2,3},{3,2},{4,5},{5,4},{6,7},{7,6},{8,9},{9,8},{10,11... | collective-permute-start | bytes 393224 | tf_op jit(solution)/shard_map/ppermute | solution.py:437
  15.2 0.0 collective-permute-start.11
  15.2 2.4 %own_keys.1 = (bf16[128,4096]{1,0:T(8,128)(2,1)S(1)}, f32[128,512]{1,0:T(8,128)S(1)}, bf16[128,512]{1,0:T(8,128)(2,1)S(1)}) custom-call(s32[1,4]{1,0:T(1,128)} %refs_0_.5, bf16[128,4096]{1,0:T(8,128)(2,1)S(1)} %copy-done, bf16[128,4096]{1,0:T(8,128)(2,1)S(1)} %copy-done.1, bf16[128,512]{1,0:T(8,128)(2,1)S(1)} %copy-done.2, bf16[128,512]{1,0:T(8,128)(2,1)S(1)} %copy-done.3, ...), custom_call_target="tpu_custom_call" | custom-call | flops 1024 | bytes 1024 | tf_op jit(solution)/shard_map/own_keys/pallas_call | solution.py:130
  17.6 0.4 collective-permute-start.10
  18.0 0.7 %collective-permute-done.2.refs_1_ = bf16[128,512]{1,0:T(8,128)(2,1)S(1)} collective-permute-done((bf16[128,512]{1,0:T(8,128)(2,1)S(1)}, bf16[128,512]{1,0:T(8,128)(2,1)S(1)}, u32[]{:S(2)}, u32[]{:S(2)}) %collective-permute-start.2) | collective-permute-done | bytes 131104 | tf_op jit(solution)/shard_map/ppermute | solution.py:437
  18.8 2.0 %collective-permute-start.8 = (bf16[128,512]{1,0:T(8,128)(2,1)S(1)}, bf16[128,512]{1,0:T(8,128)(2,1)S(1)}, u32[]{:S(2)}, u32[]{:S(2)}) collective-permute-start(bf16[128,512]{1,0:T(8,128)(2,1)S(1)} %grads_total.2.refs_0_), channel_id=1, source_target_pairs={{0,8},{1,9},{2,10},{3,11},{4,12},{5,13},{6,14},{7,15},{8,0},{9,1},... | collective-permute-start | bytes 393224 | tf_op jit(solution)/shard_map/ppermute | solution.py:437
  20.8 1.5 %collective-permute-start.7 = (bf16[128,512]{1,0:T(8,128)(2,1)S(1)}, bf16[128,512]{1,0:T(8,128)(2,1)S(1)}, u32[]{:S(2)}, u32[]{:S(2)}) collective-permute-start(bf16[128,512]{1,0:T(8,128)(2,1)S(1)} %grads_total.2.refs_0_), channel_id=1, source_target_pairs={{0,4},{1,5},{2,6},{3,7},{4,0},{5,1},{6,2},{7,3},{8,12},{9,13},{10,... | collective-permute-start | bytes 393224 | tf_op jit(solution)/shard_map/ppermute | solution.py:437
  22.3 0.0 collective-permute-done.5.refs_3_
  22.3 0.3 turn_pieces.1.refs_0_
  22.7 0.0 collective-permute-done.11.refs_1_
  22.7 0.5 collective-permute-start.12
  23.2 0.9 %collective-permute-start.14 = (bf16[128,512]{1,0:T(8,128)(2,1)S(1)}, bf16[128,512]{1,0:T(8,128)(2,1)S(1)}, u32[]{:S(2)}, u32[]{:S(2)}) collective-permute-start(bf16[128,512]{1,0:T(8,128)(2,1)S(1)} %grads_total.3.refs_1_), channel_id=1, source_target_pairs={{0,4},{1,5},{2,6},{3,7},{4,0},{5,1},{6,2},{7,3},{8,12},{9,13},{10,... | collective-permute-start | bytes 393224 | tf_op jit(solution)/shard_map/ppermute | solution.py:437
  24.2 0.0 collective-permute-start.6
  24.2 0.0 collective-permute-done.8.refs_4_
  24.2 2.2 %collective-permute-done.7.refs_2_ = bf16[128,512]{1,0:T(8,128)(2,1)S(1)} collective-permute-done((bf16[128,512]{1,0:T(8,128)(2,1)S(1)}, bf16[128,512]{1,0:T(8,128)(2,1)S(1)}, u32[]{:S(2)}, u32[]{:S(2)}) %collective-permute-start.7) | collective-permute-done | bytes 131104 | tf_op jit(solution)/shard_map/ppermute | solution.py:437
  26.3 1.9 %collective-permute-done.12.refs_5_ = bf16[128,512]{1,0:T(8,128)(2,1)S(1)} collective-permute-done((bf16[128,512]{1,0:T(8,128)(2,1)S(1)}, bf16[128,512]{1,0:T(8,128)(2,1)S(1)}, u32[]{:S(2)}, u32[]{:S(2)}) %collective-permute-start.12) | collective-permute-done | bytes 131104 | tf_op jit(solution)/shard_map/ppermute | solution.py:437
  28.3 0.4 collective-permute-start.13
  28.6 0.2 collective-permute-done.14.refs_3_
  28.8 0.1 stack_grads.2
  28.9 2.4 %collective-permute-done.9.refs_0_ = bf16[128,512]{1,0:T(8,128)(2,1)S(1)} collective-permute-done((bf16[128,512]{1,0:T(8,128)(2,1)S(1)}, bf16[128,512]{1,0:T(8,128)(2,1)S(1)}, u32[]{:S(2)}, u32[]{:S(2)}) %collective-permute-start.9) | collective-permute-done | bytes 131104 | tf_op jit(solution)/shard_map/ppermute | solution.py:437
  31.3 1.9 %collective-permute-done.13.refs_1_ = bf16[128,512]{1,0:T(8,128)(2,1)S(1)} collective-permute-done((bf16[128,512]{1,0:T(8,128)(2,1)S(1)}, bf16[128,512]{1,0:T(8,128)(2,1)S(1)}, u32[]{:S(2)}, u32[]{:S(2)}) %collective-permute-start.13) | collective-permute-done | bytes 131104 | tf_op jit(solution)/shard_map/ppermute | solution.py:437
  33.2 0.0 collective-permute-done.6.refs_1_
  33.3 0.5 weight_far.2
  33.7 3.0 %collective-permute-start.17 = (bf16[128,512]{1,0:T(8,128)(2,1)S(1)}, bf16[128,512]{1,0:T(8,128)(2,1)S(1)}, u32[]{:S(2)}, u32[]{:S(2)}) collective-permute-start(bf16[128,512]{1,0:T(8,128)(2,1)S(1)} %get-tuple-element.97), channel_id=1, source_target_pairs={{0,1},{1,0},{2,3},{3,2},{4,5},{5,4},{6,7},{7,6},{8,9},{9,8},{10,11... | collective-permute-start | bytes 393224 | tf_op jit(solution)/shard_map/ppermute | solution.py:437
  36.7 0.5 weight_far.3
  37.2 0.1 collective-permute-start.15
  37.3 0.8 %weight_near.1 = (f32[128,512]{1,0:T(8,128)S(1)}, bf16[128,512]{1,0:T(8,128)(2,1)S(1)}, bf16[128,512]{1,0:T(8,128)(2,1)S(1)}, bf16[128,512]{1,0:T(8,128)(2,1)S(1)}) custom-call(bf16[1024,512]{1,0:T(8,128)(2,1)S(1)} %turn_pieces.1.refs_0_, bf16[1024,512]{1,0:T(8,128)(2,1)S(1)} %collective-permute-done.6.refs_1_, ...), custom_call_target="tpu_custom_call" | custom-call | flops 1024 | bytes 1024 | tf_op jit(solution)/shard_map/weight_near/pallas_call | solution.py:335
  38.1 2.1 %collective-permute-start.16 = (bf16[128,512]{1,0:T(8,128)(2,1)S(1)}, bf16[128,512]{1,0:T(8,128)(2,1)S(1)}, u32[]{:S(2)}, u32[]{:S(2)}) collective-permute-start(bf16[128,512]{1,0:T(8,128)(2,1)S(1)} %get-tuple-element.96), channel_id=1, source_target_pairs={{0,1},{1,0},{2,3},{3,2},{4,5},{5,4},{6,7},{7,6},{8,9},{9,8},{10,11... | collective-permute-start | bytes 393224 | tf_op jit(solution)/shard_map/ppermute | solution.py:437
  40.2 0.0 collective-permute-done.17.refs_0_
  40.2 2.6 %collective-permute-start.18 = (bf16[128,512]{1,0:T(8,128)(2,1)S(1)}, bf16[128,512]{1,0:T(8,128)(2,1)S(1)}, u32[]{:S(2)}, u32[]{:S(2)}) collective-permute-start(bf16[128,512]{1,0:T(8,128)(2,1)S(1)} %relay_total.3), channel_id=1, source_target_pairs={{0,16},{1,17},{2,18},{3,19},{4,20},{5,21},{6,22},{7,23},{8,24},{9,... | collective-permute-start | bytes 393224 | tf_op jit(solution)/shard_map/ppermute | solution.py:437
  42.8 0.0 collective-permute-done.15.refs_0_
  42.8 0.1 collective-permute-start.20
  42.9 2.1 %collective-permute-start.19 = (bf16[128,512]{1,0:T(8,128)(2,1)S(1)}, bf16[128,512]{1,0:T(8,128)(2,1)S(1)}, u32[]{:S(2)}, u32[]{:S(2)}) collective-permute-start(bf16[128,512]{1,0:T(8,128)(2,1)S(1)} %get-tuple-element.99), channel_id=1, source_target_pairs={{0,2},{1,3},{2,0},{3,1},{4,6},{5,7},{6,4},{7,5},{8,10},{9,11},{10,... | collective-permute-start | bytes 393224 | tf_op jit(solution)/shard_map/ppermute | solution.py:437
  45.0 0.5 collective-permute-start.21
  45.4 1.7 %query_gradient.1 = bf16[128,4096]{1,0:T(8,128)(2,1)} custom-call(bf16[128,4096]{1,0:T(8,128)(2,1)S(1)} %get-tuple-element.93.refs_0_, bf16[128,4096]{1,0:T(8,128)(2,1)S(1)} %get-tuple-element.94.refs_1_, bf16[128,512]{1,0:T(8,128)(2,1)S(1)} %copy-done.2, bf16[128,512]{1,0:T(8,128)(2,1)S(1)} %collective-permute-done.refs_3_), custom_call_target="tpu_custom_call" | custom-call | flops 1024 | bytes 1024 | tf_op jit(solution)/shard_map/query_gradient/pallas_call | solution.py:157
  47.2 0.0 collective-permute-done.16.refs_1_
  47.2 3.7 %collective-permute-done.18.refs_2_ = bf16[128,512]{1,0:T(8,128)(2,1)S(1)} collective-permute-done((bf16[128,512]{1,0:T(8,128)(2,1)S(1)}, bf16[128,512]{1,0:T(8,128)(2,1)S(1)}, u32[]{:S(2)}, u32[]{:S(2)}) %collective-permute-start.18) | collective-permute-done | bytes 131104 | tf_op jit(solution)/shard_map/ppermute | solution.py:437
  50.9 1.7 %collective-permute-done.20.refs_2_ = bf16[128,512]{1,0:T(8,128)(2,1)S(1)} collective-permute-done((bf16[128,512]{1,0:T(8,128)(2,1)S(1)}, bf16[128,512]{1,0:T(8,128)(2,1)S(1)}, u32[]{:S(2)}, u32[]{:S(2)}) %collective-permute-start.20) | collective-permute-done | bytes 131104 | tf_op jit(solution)/shard_map/ppermute | solution.py:437
  52.7 0.8 %weight_total.1 = (f32[128,512]{1,0:T(8,128)}, f32[128,512]{1,0:T(8,128)}) custom-call(f32[128,512]{1,0:T(8,128)S(1)} %early_total.1.refs_0_, bf16[128,512]{1,0:T(8,128)(2,1)S(1)} %collective-permute-done.19.refs_1_, bf16[128,512]{1,0:T(8,128)(2,1)S(1)} %collective-permute-done.20.refs_2_, bf16[128,512]{1,0:T(8,128)(2,1)S(1)} %collective-permute-done.21.refs_3_), custom_call_target="tpu_custom_call" | custom-call | flops 1024 | bytes 1024 | tf_op jit(solution)/shard_map/weight_total/pallas_call | solution.py:404
  (21 shorter events, 0.2 us)
Async XLA Ops:
  0.6 9.5 %copy-start.1 = (bf16[128,4096]{1,0:T(8,128)(2,1)S(1)}, bf16[128,4096]{1,0:T(8,128)(2,1)}, u32[]{:S(2)}) copy-start(bf16[128,4096]{1,0:T(8,128)(2,1)} %refs_2_.4) | copy-start | bytes 3145732
  0.6 9.5 %copy-start = (bf16[128,4096]{1,0:T(8,128)(2,1)S(1)}, bf16[128,4096]{1,0:T(8,128)(2,1)}, u32[]{:S(2)}) copy-start(bf16[128,4096]{1,0:T(8,128)(2,1)} %refs_1_.3) | copy-start | bytes 3145732
  0.7 9.4 %collective-permute-start.1 = (bf16[128,512]{1,0:T(8,128)(2,1)}, bf16[128,512]{1,0:T(8,128)(2,1)S(1)}, u32[]{:S(2)}, u32[]{:S(2)}) collective-permute-start(bf16[128,512]{1,0:T(8,128)(2,1)} %refs_4_.1), channel_id=1, source_target_pairs={{0,1},{1,0},{2,3},{3,2},{4,5},{5,4},{6,7},{7,6},{8,9},{9,8},{10,11... | collective-permute-start | bytes 393224 | tf_op jit(solution)/shard_map/ppermute | solution.py:437
  3.7 6.5 %collective-permute-start = (bf16[128,512]{1,0:T(8,128)(2,1)}, bf16[128,512]{1,0:T(8,128)(2,1)S(1)}, u32[]{:S(2)}, u32[]{:S(2)}) collective-permute-start(bf16[128,512]{1,0:T(8,128)(2,1)} %refs_2_.5), channel_id=1, source_target_pairs={{0,1},{1,0},{2,3},{3,2},{4,5},{5,4},{6,7},{7,6},{8,9},{9,8},{10,11... | collective-permute-start | bytes 393224 | tf_op jit(solution)/shard_map/ppermute | solution.py:437
  5.1 12.9 %collective-permute-start.3 = (bf16[128,1024]{1,0:T(8,128)(2,1)S(1)}, bf16[128,1024]{1,0:T(8,128)(2,1)S(1)}, u32[]{:S(2)}, u32[]{:S(2)}) collective-permute-start(bf16[128,1024]{1,0:T(8,128)(2,1)S(1)} %get-tuple-element.58), channel_id=1, source_target_pairs={{0,4},{1,5},{2,6},{3,7},{4,0},{5,1},{6,2},{7,3},{8,12},{9,13},{10,... | collective-permute-start | bytes 786440 | tf_op jit(solution)/shard_map/ppermute | solution.py:437
  7.2 10.4 %collective-permute-start.4 = (bf16[128,1024]{1,0:T(8,128)(2,1)S(1)}, bf16[128,1024]{1,0:T(8,128)(2,1)S(1)}, u32[]{:S(2)}, u32[]{:S(2)}) collective-permute-start(bf16[128,1024]{1,0:T(8,128)(2,1)S(1)} %get-tuple-element.63), channel_id=1, source_target_pairs={{0,8},{1,9},{2,10},{3,11},{4,12},{5,13},{6,14},{7,15},{8,0},{9,1},... | collective-permute-start | bytes 786440 | tf_op jit(solution)/shard_map/ppermute | solution.py:437
  8.7 13.6 %collective-permute-start.5 = (bf16[128,1024]{1,0:T(8,128)(2,1)S(1)}, bf16[128,1024]{1,0:T(8,128)(2,1)S(1)}, u32[]{:S(2)}, u32[]{:S(2)}) collective-permute-start(bf16[128,1024]{1,0:T(8,128)(2,1)S(1)} %get-tuple-element.65), channel_id=1, source_target_pairs={{0,12},{1,13},{2,14},{3,15},{4,8},{5,9},{6,10},{7,11},{8,4},{9,5},... | collective-permute-start | bytes 786440 | tf_op jit(solution)/shard_map/ppermute | solution.py:437
  10.2 5.0 %copy-start.2 = (bf16[128,512]{1,0:T(8,128)(2,1)S(1)}, bf16[128,512]{1,0:T(8,128)(2,1)}, u32[]{:S(2)}) copy-start(bf16[128,512]{1,0:T(8,128)(2,1)} %refs_2_.5) | copy-start | bytes 393220
  10.2 5.0 %copy-start.3 = (bf16[128,512]{1,0:T(8,128)(2,1)S(1)}, bf16[128,512]{1,0:T(8,128)(2,1)}, u32[]{:S(2)}) copy-start(bf16[128,512]{1,0:T(8,128)(2,1)} %refs_4_.1) | copy-start | bytes 393220
  13.3 5.4 %collective-permute-start.2 = (bf16[128,512]{1,0:T(8,128)(2,1)S(1)}, bf16[128,512]{1,0:T(8,128)(2,1)S(1)}, u32[]{:S(2)}, u32[]{:S(2)}) collective-permute-start(bf16[128,512]{1,0:T(8,128)(2,1)S(1)} %get-tuple-element.57), channel_id=1, source_target_pairs={{0,1},{1,0},{2,3},{3,2},{4,5},{5,4},{6,7},{7,6},{8,9},{9,8},{10,11... | collective-permute-start | bytes 393224 | tf_op jit(solution)/shard_map/ppermute | solution.py:437
  15.2 7.5 %collective-permute-start.11 = (bf16[128,512]{1,0:T(8,128)(2,1)S(1)}, bf16[128,512]{1,0:T(8,128)(2,1)S(1)}, u32[]{:S(2)}, u32[]{:S(2)}) collective-permute-start(bf16[128,512]{1,0:T(8,128)(2,1)S(1)} %get-tuple-element.74), channel_id=1, source_target_pairs={{0,3},{1,2},{2,1},{3,0},{4,7},{5,6},{6,5},{7,4},{8,11},{9,10},{10,... | collective-permute-start | bytes 393224 | tf_op jit(solution)/shard_map/ppermute | solution.py:437
  17.6 5.1 %collective-permute-start.10 = (bf16[128,512]{1,0:T(8,128)(2,1)S(1)}, bf16[128,512]{1,0:T(8,128)(2,1)S(1)}, u32[]{:S(2)}, u32[]{:S(2)}) collective-permute-start(bf16[128,512]{1,0:T(8,128)(2,1)S(1)} %get-tuple-element.73), channel_id=1, source_target_pairs={{0,2},{1,3},{2,0},{3,1},{4,6},{5,7},{6,4},{7,5},{8,10},{9,11},{10,... | collective-permute-start | bytes 393224 | tf_op jit(solution)/shard_map/ppermute | solution.py:437
  18.8 5.4 %collective-permute-start.8 = (bf16[128,512]{1,0:T(8,128)(2,1)S(1)}, bf16[128,512]{1,0:T(8,128)(2,1)S(1)}, u32[]{:S(2)}, u32[]{:S(2)}) collective-permute-start(bf16[128,512]{1,0:T(8,128)(2,1)S(1)} %grads_total.2.refs_0_), channel_id=1, source_target_pairs={{0,8},{1,9},{2,10},{3,11},{4,12},{5,13},{6,14},{7,15},{8,0},{9,1},... | collective-permute-start | bytes 393224 | tf_op jit(solution)/shard_map/ppermute | solution.py:437
  20.8 5.5 %collective-permute-start.7 = (bf16[128,512]{1,0:T(8,128)(2,1)S(1)}, bf16[128,512]{1,0:T(8,128)(2,1)S(1)}, u32[]{:S(2)}, u32[]{:S(2)}) collective-permute-start(bf16[128,512]{1,0:T(8,128)(2,1)S(1)} %grads_total.2.refs_0_), channel_id=1, source_target_pairs={{0,4},{1,5},{2,6},{3,7},{4,0},{5,1},{6,2},{7,3},{8,12},{9,13},{10,... | collective-permute-start | bytes 393224 | tf_op jit(solution)/shard_map/ppermute | solution.py:437
  22.7 5.5 %collective-permute-start.12 = (bf16[128,512]{1,0:T(8,128)(2,1)S(1)}, bf16[128,512]{1,0:T(8,128)(2,1)S(1)}, u32[]{:S(2)}, u32[]{:S(2)}) collective-permute-start(bf16[128,512]{1,0:T(8,128)(2,1)S(1)} %grads_total.3.refs_1_), channel_id=1, source_target_pairs={{0,8},{1,9},{2,10},{3,11},{4,12},{5,13},{6,14},{7,15},{8,0},{9,1},... | collective-permute-start | bytes 393224 | tf_op jit(solution)/shard_map/ppermute | solution.py:437
  23.2 5.6 %collective-permute-start.14 = (bf16[128,512]{1,0:T(8,128)(2,1)S(1)}, bf16[128,512]{1,0:T(8,128)(2,1)S(1)}, u32[]{:S(2)}, u32[]{:S(2)}) collective-permute-start(bf16[128,512]{1,0:T(8,128)(2,1)S(1)} %grads_total.3.refs_1_), channel_id=1, source_target_pairs={{0,4},{1,5},{2,6},{3,7},{4,0},{5,1},{6,2},{7,3},{8,12},{9,13},{10,... | collective-permute-start | bytes 393224 | tf_op jit(solution)/shard_map/ppermute | solution.py:437
  24.2 9.1 %collective-permute-start.6 = (bf16[1024,512]{1,0:T(8,128)(2,1)S(1)}, bf16[1024,512]{1,0:T(8,128)(2,1)S(1)}, u32[]{:S(2)}, u32[]{:S(2)}) collective-permute-start(bf16[1024,512]{1,0:T(8,128)(2,1)S(1)} %turn_pieces.1.refs_0_), channel_id=1, source_target_pairs={{0,2},{1,3},{2,0},{3,1},{4,6},{5,7},{6,4},{7,5},{8,10},{9,11},{10,... | collective-permute-start | bytes 3145736 | tf_op jit(solution)/shard_map/ppermute | solution.py:437
  26.3 5.0 %collective-permute-start.9 = (bf16[128,512]{1,0:T(8,128)(2,1)S(1)}, bf16[128,512]{1,0:T(8,128)(2,1)S(1)}, u32[]{:S(2)}, u32[]{:S(2)}) collective-permute-start(bf16[128,512]{1,0:T(8,128)(2,1)S(1)} %collective-permute-done.7.refs_2_), channel_id=1, source_target_pairs={{0,8},{1,9},{2,10},{3,11},{4,12},{5,13},{6,14},{7,15},{8,0},{9,1},... | collective-permute-start | bytes 393224 | tf_op jit(solution)/shard_map/ppermute | solution.py:437
  28.3 5.0 %collective-permute-start.13 = (bf16[128,512]{1,0:T(8,128)(2,1)S(1)}, bf16[128,512]{1,0:T(8,128)(2,1)S(1)}, u32[]{:S(2)}, u32[]{:S(2)}) collective-permute-start(bf16[128,512]{1,0:T(8,128)(2,1)S(1)} %collective-permute-done.12.refs_5_), channel_id=1, source_target_pairs={{0,4},{1,5},{2,6},{3,7},{4,0},{5,1},{6,2},{7,3},{8,12},{9,13},{10,... | collective-permute-start | bytes 393224 | tf_op jit(solution)/shard_map/ppermute | solution.py:437
  33.7 6.4 %collective-permute-start.17 = (bf16[128,512]{1,0:T(8,128)(2,1)S(1)}, bf16[128,512]{1,0:T(8,128)(2,1)S(1)}, u32[]{:S(2)}, u32[]{:S(2)}) collective-permute-start(bf16[128,512]{1,0:T(8,128)(2,1)S(1)} %get-tuple-element.97), channel_id=1, source_target_pairs={{0,1},{1,0},{2,3},{3,2},{4,5},{5,4},{6,7},{7,6},{8,9},{9,8},{10,11... | collective-permute-start | bytes 393224 | tf_op jit(solution)/shard_map/ppermute | solution.py:437
  37.2 5.6 %collective-permute-start.15 = (bf16[128,512]{1,0:T(8,128)(2,1)S(1)}, bf16[128,512]{1,0:T(8,128)(2,1)S(1)}, u32[]{:S(2)}, u32[]{:S(2)}) collective-permute-start(bf16[128,512]{1,0:T(8,128)(2,1)S(1)} %get-tuple-element.92), channel_id=1, source_target_pairs={{0,1},{1,0},{2,3},{3,2},{4,5},{5,4},{6,7},{7,6},{8,9},{9,8},{10,11... | collective-permute-start | bytes 393224 | tf_op jit(solution)/shard_map/ppermute | solution.py:437
  38.1 9.0 %collective-permute-start.16 = (bf16[128,512]{1,0:T(8,128)(2,1)S(1)}, bf16[128,512]{1,0:T(8,128)(2,1)S(1)}, u32[]{:S(2)}, u32[]{:S(2)}) collective-permute-start(bf16[128,512]{1,0:T(8,128)(2,1)S(1)} %get-tuple-element.96), channel_id=1, source_target_pairs={{0,1},{1,0},{2,3},{3,2},{4,5},{5,4},{6,7},{7,6},{8,9},{9,8},{10,11... | collective-permute-start | bytes 393224 | tf_op jit(solution)/shard_map/ppermute | solution.py:437
  40.2 10.7 %collective-permute-start.18 = (bf16[128,512]{1,0:T(8,128)(2,1)S(1)}, bf16[128,512]{1,0:T(8,128)(2,1)S(1)}, u32[]{:S(2)}, u32[]{:S(2)}) collective-permute-start(bf16[128,512]{1,0:T(8,128)(2,1)S(1)} %relay_total.3), channel_id=1, source_target_pairs={{0,16},{1,17},{2,18},{3,19},{4,20},{5,21},{6,22},{7,23},{8,24},{9,... | collective-permute-start | bytes 393224 | tf_op jit(solution)/shard_map/ppermute | solution.py:437
  42.8 9.9 %collective-permute-start.20 = (bf16[128,512]{1,0:T(8,128)(2,1)S(1)}, bf16[128,512]{1,0:T(8,128)(2,1)S(1)}, u32[]{:S(2)}, u32[]{:S(2)}) collective-permute-start(bf16[128,512]{1,0:T(8,128)(2,1)S(1)} %relay_total.2), channel_id=1, source_target_pairs={{0,18},{1,19},{2,16},{3,17},{4,22},{5,23},{6,20},{7,21},{8,26},{9,... | collective-permute-start | bytes 393224 | tf_op jit(solution)/shard_map/ppermute | solution.py:437
  42.9 8.0 %collective-permute-start.19 = (bf16[128,512]{1,0:T(8,128)(2,1)S(1)}, bf16[128,512]{1,0:T(8,128)(2,1)S(1)}, u32[]{:S(2)}, u32[]{:S(2)}) collective-permute-start(bf16[128,512]{1,0:T(8,128)(2,1)S(1)} %get-tuple-element.99), channel_id=1, source_target_pairs={{0,2},{1,3},{2,0},{3,1},{4,6},{5,7},{6,4},{7,5},{8,10},{9,11},{10,... | collective-permute-start | bytes 393224 | tf_op jit(solution)/shard_map/ppermute | solution.py:437
  45.0 6.0 %collective-permute-start.21 = (bf16[128,512]{1,0:T(8,128)(2,1)S(1)}, bf16[128,512]{1,0:T(8,128)(2,1)S(1)}, u32[]{:S(2)}, u32[]{:S(2)}) collective-permute-start(bf16[128,512]{1,0:T(8,128)(2,1)S(1)} %get-tuple-element.100), channel_id=1, source_target_pairs={{0,3},{1,2},{2,1},{3,0},{4,7},{5,6},{6,5},{7,4},{8,11},{9,10},{10,... | collective-permute-start | bytes 393224 | tf_op jit(solution)/shard_map/ppermute | solution.py:437

commit v20 on v19

--- a/solution.py
+++ b/solution.py
@@ -319,7 +319,7 @@
                 sibling_ref[here, :], sibling_grads[...], NN
             )
             for x in range(ctx_count):
-                out_ref = out_refs[i * ctx_count + x]
+                out_ref = out_refs[x * len(core_steps) + i]
                 start = lax.rem(x_rank + x, ctx_count) * block
                 out_ref[at * block : (at + 1) * block, :] = buf[
                     pl.ds(pl.multiple_of(start, block), block), :
@@ -330,8 +330,8 @@
     height = tokens[0].shape[0] // (CORES * far)
     width = grads[0].shape[1]
     dims = (height // ctx_count * len(z_steps), width)
-    out_shape = [shape(dims, jnp.float32)] + [shape(dims, jnp.bfloat16)] * (ctx_count - 1)
-    out_shape += [shape(dims, jnp.bfloat16)] * (ctx_count * (len(core_steps) - 1))
+    out_shape = [shape(dims, jnp.float32)] * len(core_steps)
+    out_shape += [shape(dims, jnp.bfloat16)] * (len(core_steps) * (ctx_count - 1))
     return pl.pallas_call(
         functools.partial(weight_kernel, core_steps, z_steps, far, ctx_count),
         in_specs=[WHOLE] * 4,
@@ -368,48 +368,46 @@
     )(away, *arrived)
 
 
-def early_kernel(*refs):
-    total = refs[0][...].astype(jnp.float32)
+def cross_kernel(*refs):
+    total = refs[0][...]
     for ref in refs[1:-1]:
         total = total + ref[...].astype(jnp.float32)
-    refs[-1][...] = total
-
-
-def early_call(arrived):
-    return pl.pallas_call(
-        early_kernel,
-        in_specs=[WHOLE] * len(arrived),
+    refs[-1][...] = total.astype(refs[-1].dtype)
+
+
+def cross_call(block, near, from_far):
+    return pl.pallas_call(
+        cross_kernel,
+        in_specs=[WHOLE] * (1 + len(near) + len(from_far)),
         out_specs=WHOLE,
-        out_shape=shape(arrived[0].shape, jnp.float32),
+        out_shape=shape(block.shape, jnp.bfloat16),
         compiler_params=PARAMS,
         cost_estimate=EARLY,
-        name="early_total",
-    )(*arrived)
-
-
-def final_kernel(count, *refs):
+        name="sibling_total",
+    )(block, *near, *from_far)
+
+
+def final_kernel(block_ref, sibling_ref, *refs):
     key_ref, value_ref = refs[-2:]
     core = lax.rem(lax.axis_index("dp"), CORES)
-    totals = []
-    for part in (refs[:count], refs[count:-2]):
-        total = part[0][...].astype(jnp.float32)
-        for ref in part[1:]:
-            total = total + ref[...].astype(jnp.float32)
-        totals.append(total)
-    key_ref[...] = jnp.where(core == 0, totals[0], totals[1])
-    value_ref[...] = jnp.where(core == 0, totals[1], totals[0])
-
-
-def final_call(same, cross):
-    return pl.pallas_call(
-        functools.partial(final_kernel, len(same)),
-        in_specs=[WHOLE] * (len(same) + len(cross)),
+    total = block_ref[...]
+    for ref in refs[:-2]:
+        total = total + ref[...].astype(jnp.float32)
+    other = sibling_ref[...].astype(jnp.float32)
+    key_ref[...] = jnp.where(core == 0, total, other)
+    value_ref[...] = jnp.where(core == 0, other, total)
+
+
+def final_call(block, sibling, near, from_far):
+    return pl.pallas_call(
+        final_kernel,
+        in_specs=[WHOLE] * (2 + len(near) + len(from_far)),
         out_specs=[WHOLE] * 2,
-        out_shape=[shape(same[0].shape, jnp.float32)] * 2,
+        out_shape=[shape(block.shape, jnp.float32)] * 2,
         compiler_params=PARAMS,
         cost_estimate=COST,
         name="weight_total",
-    )(*same, *cross)
+    )(block, sibling, *near, *from_far)
 
 
 def local(
@@ -478,27 +476,25 @@
     weights = functools.partial(weight_call, far=far, ctx_count=ctx_count, tokens=tokens)
     steps = tuple(range(1, far))
     away, arrived, from_far = [], [], []
-    for core in range(CORES):
+    for core in (1, 0):
         kept, *blocks = weights((core,), steps, grads=grads)
         grads = after(grads, kept)
         away.append(kept)
         arrived.append([send(value, s) for s, value in enumerate(blocks, 1)])
-    blocks = weights(tuple(range(CORES)), (0,), grads=grads)
-    own_block, near = blocks[0], blocks[1:ctx_count]
-    cross_block, cross_near = blocks[ctx_count], blocks[ctx_count + 1 :]
+    own_block, cross_block, *near = weights((0, 1), (0,), grads=grads)
+    near, cross_near = near[0::2], near[1::2]
     arrived[0] = after(arrived[0], own_block)
-    near_arrived = [send(value, s) for s, value in enumerate(near, 1)]
-    for core in range(CORES):
-        relayed = relay_call(far - 1, away[core], arrived[core])
-        from_far.append([send(value, 0, core, s) for s, value in enumerate(relayed, 1)])
-    cross_block, cross_near, own_scores = after((cross_block, cross_near, own_scores), relayed)
-    same = [early_call([own_block] + near_arrived + from_far[0])]
-    cross = [send(cross_block, core_steps=1)] + from_far[1]
-    cross += [send(value, s, 1) for s, value in enumerate(cross_near, 1)]
+    cross_near = [send(value, s) for s, value in enumerate(cross_near, 1)]
+    for part in range(2):
+        relayed = relay_call(far - 1, away[part], arrived[part])
+        from_far.append([send(value, far_steps=s) for s, value in enumerate(relayed, 1)])
+    near, own_scores = after((near, own_scores), relayed)
+    near = [send(value, s) for s, value in enumerate(near, 1)]
+    sibling = send(cross_call(cross_block, cross_near, from_far[0]), core_steps=1)
     query_gradient = query_call(
         [own_scores] + scores, [saved_keys] + [pair[0] for pair in visiting], rows
     )
-    key_weight_grad, value_weight_grad = final_call(same, cross)
+    key_weight_grad, value_weight_grad = final_call(own_block, sibling, near, from_far[1])
     return query_gradient, key_weight_grad, value_weight_grad
 
 

time: 53.8 us -> 52.1 us (0.968)
  waiting for transfers between devices: 15 us -> 11.8 us
  starting transfers between devices: 24.6 us -> 26.2 us
    ppermute x22, waiting for transfers between devices: 15 us -> 11.8 us  [send(): return lax.ppermute(value, ('dp', 'ctx'), pairs)]
    ppermute x22, starting transfers between devices: 24.6 us -> 26.2 us  [send(): return lax.ppermute(value, ('dp', 'ctx'), pairs)]
  transfers between devices with their start and end apart: 22 -> 22, of which waited for: 9 -> 9; matrix products, arithmetic and copies ran while one was open for 0% -> 0% of each run, Pallas kernels for 22% -> 23%
where the time goes in v20:
time: 52.1 us; the launch traced here: 51.8 us
  starting transfers between devices  26.2 us (50%)
  Pallas kernels  13.1 us (25%)
  waiting for transfers between devices  11.8 us (23%)
  between operations  0.81 us (2%)
    ppermute x22, starting transfers between devices, send(): return lax.ppermute(value, ('dp', 'ctx'), pairs)  26.2 us
    ppermute x22, waiting for transfers between devices, send(): return lax.ppermute(value, ('dp', 'ctx'), pairs)  11.8 us
    pallas_call x2, Pallas kernels, block_call(): pl.pallas_call(functools.partial(block_kernel, ctx_count, step), in_specs...  5.52 us
    pallas_call x3, Pallas kernels, weight_call(): pl.pallas_call(functools.partial(weight_kernel, core_steps, z_steps, far,...  1.77 us
    pallas_call x1, Pallas kernels, query_call(): pl.pallas_call(functools.partial(query_kernel, len(keys)), in_specs=[WHOL...  1.74 us
    pallas_call x1, Pallas kernels, pieces_call(): pl.pallas_call(functools.partial(pieces_kernel, far), in_specs=[FAR], out...  1.39 us
    pallas_call x1, Pallas kernels, near_call(): pl.pallas_call(near_kernel, in_specs=[FAR] * len(values), out_specs=[WHOL...  1.24 us
  transfers between devices with their start and end apart: 22, of which 9 were waited for; matrix products, arithmetic and copies ran while one was open for 0% of the time, Pallas kernels for 23%

profile of v20, /device:TPU:0, one launch (start us, length us, event | category | flops | bytes accessed | tf_op | source)
XLA Modules:
  0.0 51.8 jit_solution(14854172118894701240)
XLA Ops:
  0.7 3.0 %collective-permute-start.1 = (bf16[128,512]{1,0:T(8,128)(2,1)}, bf16[128,512]{1,0:T(8,128)(2,1)S(1)}, u32[]{:S(2)}, u32[]{:S(2)}) collective-permute-start(bf16[128,512]{1,0:T(8,128)(2,1)} %refs_4_.1), channel_id=1, source_target_pairs={{0,1},{1,0},{2,3},{3,2},{4,5},{5,4},{6,7},{7,6},{8,9},{9,8},{10,11... | collective-permute-start | bytes 393224 | tf_op jit(solution)/shard_map/ppermute | solution.py:435
  3.7 0.1 collective-permute-start
  3.7 1.4 %pieces.1 = (bf16[128,1024]{1,0:T(8,128)(2,1)S(1)}, bf16[128,1024]{1,0:T(8,128)(2,1)S(1)}, bf16[128,1024]{1,0:T(8,128)(2,1)S(1)}, bf16[128,1024]{1,0:T(8,128)(2,1)S(1)}) custom-call(bf16[128,4096]{1,0:T(8,128)(2,1)} %in_hbm.1), custom_call_target="tpu_custom_call" | custom-call | flops 1024 | bytes 1024 | tf_op jit(solution)/shard_map/pieces/pallas_call | solution.py:227
  5.1 2.0 %collective-permute-start.3 = (bf16[128,1024]{1,0:T(8,128)(2,1)S(1)}, bf16[128,1024]{1,0:T(8,128)(2,1)S(1)}, u32[]{:S(2)}, u32[]{:S(2)}) collective-permute-start(bf16[128,1024]{1,0:T(8,128)(2,1)S(1)} %get-tuple-element.57), channel_id=1, source_target_pairs={{0,4},{1,5},{2,6},{3,7},{4,0},{5,1},{6,2},{7,3},{8,12},{9,13},{10,... | collective-permute-start | bytes 786440 | tf_op jit(solution)/shard_map/ppermute | solution.py:435
  7.2 1.6 %collective-permute-start.4 = (bf16[128,1024]{1,0:T(8,128)(2,1)S(1)}, bf16[128,1024]{1,0:T(8,128)(2,1)S(1)}, u32[]{:S(2)}, u32[]{:S(2)}) collective-permute-start(bf16[128,1024]{1,0:T(8,128)(2,1)S(1)} %get-tuple-element.62), channel_id=1, source_target_pairs={{0,8},{1,9},{2,10},{3,11},{4,12},{5,13},{6,14},{7,15},{8,0},{9,1},... | collective-permute-start | bytes 786440 | tf_op jit(solution)/shard_map/ppermute | solution.py:435
  8.7 0.0 collective-permute-start.5
  8.7 1.2 %bring_near.1 = (bf16[128,4096]{1,0:T(8,128)(2,1)S(1)}, f32[32,128]{1,0:T(8,128)S(1)}) custom-call(bf16[128,4096]{1,0:T(8,128)(2,1)} %refs_0_.3, f32[32,128]{1,0:T(8,128)} %bitcast.1), custom_call_target="tpu_custom_call" | custom-call | flops 1024 | bytes 1024 | tf_op jit(solution)/shard_map/bring_near/pallas_call | solution.py:185
  10.0 0.0 collective-permute-done.1.refs_4_
  10.0 0.2 collective-permute-done.refs_3_
  10.2 3.1 %visiting_keys.1 = (bf16[128,4096]{1,0:T(8,128)(2,1)S(1)}, bf16[128,512]{1,0:T(8,128)(2,1)S(1)}, bf16[128,512]{1,0:T(8,128)(2,1)S(1)}, f32[32,128]{1,0:T(8,128)S(1)}) custom-call(s32[1,4]{1,0:T(1,128)} %refs_0_.5, bf16[128,4096]{1,0:T(8,128)(2,1)S(1)} %copy-done, bf16[128,4096]{1,0:T(8,128)(2,1)S(1)} %copy-done.1, ...), custom_call_target="tpu_custom_call" | custom-call | flops 5000000000 | bytes 1024 | tf_op jit(solution)/shard_map/visiting_keys/pallas_call | solution.py:130
  13.3 1.8 %collective-permute-start.2 = (bf16[128,512]{1,0:T(8,128)(2,1)S(1)}, bf16[128,512]{1,0:T(8,128)(2,1)S(1)}, u32[]{:S(2)}, u32[]{:S(2)}) collective-permute-start(bf16[128,512]{1,0:T(8,128)(2,1)S(1)} %get-tuple-element.56), channel_id=1, source_target_pairs={{0,1},{1,0},{2,3},{3,2},{4,5},{5,4},{6,7},{7,6},{8,9},{9,8},{10,11... | collective-permute-start | bytes 393224 | tf_op jit(solution)/shard_map/ppermute | solution.py:435
  15.2 0.0 collective-permute-start.11
  15.2 2.4 %own_keys.1 = (bf16[128,4096]{1,0:T(8,128)(2,1)S(1)}, f32[128,512]{1,0:T(8,128)S(1)}, bf16[128,512]{1,0:T(8,128)(2,1)S(1)}) custom-call(s32[1,4]{1,0:T(1,128)} %refs_0_.5, bf16[128,4096]{1,0:T(8,128)(2,1)S(1)} %copy-done, bf16[128,4096]{1,0:T(8,128)(2,1)S(1)} %copy-done.1, bf16[128,512]{1,0:T(8,128)(2,1)S(1)} %copy-done.2, bf16[128,512]{1,0:T(8,128)(2,1)S(1)} %copy-done.3, ...), custom_call_target="tpu_custom_call" | custom-call | flops 1024 | bytes 1024 | tf_op jit(solution)/shard_map/own_keys/pallas_call | solution.py:130
  17.6 0.0 collective-permute-done.4.refs_2_
  17.6 0.4 collective-permute-start.10
  18.0 0.0 collective-permute-done.3.refs_1_
  18.0 0.7 %collective-permute-done.2.refs_1_ = bf16[128,512]{1,0:T(8,128)(2,1)S(1)} collective-permute-done((bf16[128,512]{1,0:T(8,128)(2,1)S(1)}, bf16[128,512]{1,0:T(8,128)(2,1)S(1)}, u32[]{:S(2)}, u32[]{:S(2)}) %collective-permute-start.2) | collective-permute-done | bytes 131104 | tf_op jit(solution)/shard_map/ppermute | solution.py:435
  18.8 2.0 %collective-permute-start.8 = (bf16[128,512]{1,0:T(8,128)(2,1)S(1)}, bf16[128,512]{1,0:T(8,128)(2,1)S(1)}, u32[]{:S(2)}, u32[]{:S(2)}) collective-permute-start(bf16[128,512]{1,0:T(8,128)(2,1)S(1)} %grads_total.2.refs_0_), channel_id=1, source_target_pairs={{0,8},{1,9},{2,10},{3,11},{4,12},{5,13},{6,14},{7,15},{8,0},{9,1},... | collective-permute-start | bytes 393224 | tf_op jit(solution)/shard_map/ppermute | solution.py:435
  20.8 1.5 %collective-permute-start.7 = (bf16[128,512]{1,0:T(8,128)(2,1)S(1)}, bf16[128,512]{1,0:T(8,128)(2,1)S(1)}, u32[]{:S(2)}, u32[]{:S(2)}) collective-permute-start(bf16[128,512]{1,0:T(8,128)(2,1)S(1)} %grads_total.2.refs_0_), channel_id=1, source_target_pairs={{0,4},{1,5},{2,6},{3,7},{4,0},{5,1},{6,2},{7,3},{8,12},{9,13},{10,... | collective-permute-start | bytes 393224 | tf_op jit(solution)/shard_map/ppermute | solution.py:435
  22.3 0.0 collective-permute-done.5.refs_3_
  22.3 0.3 turn_pieces.1.refs_0_
  22.7 0.0 collective-permute-done.11.refs_1_
  22.7 0.5 collective-permute-start.12
  23.2 0.9 %collective-permute-start.14 = (bf16[128,512]{1,0:T(8,128)(2,1)S(1)}, bf16[128,512]{1,0:T(8,128)(2,1)S(1)}, u32[]{:S(2)}, u32[]{:S(2)}) collective-permute-start(bf16[128,512]{1,0:T(8,128)(2,1)S(1)} %grads_total.3.refs_1_), channel_id=1, source_target_pairs={{0,4},{1,5},{2,6},{3,7},{4,0},{5,1},{6,2},{7,3},{8,12},{9,13},{10,... | collective-permute-start | bytes 393224 | tf_op jit(solution)/shard_map/ppermute | solution.py:435
  24.2 0.0 collective-permute-start.6
  24.2 0.0 collective-permute-done.8.refs_4_
  24.2 2.2 %collective-permute-done.7.refs_2_ = bf16[128,512]{1,0:T(8,128)(2,1)S(1)} collective-permute-done((bf16[128,512]{1,0:T(8,128)(2,1)S(1)}, bf16[128,512]{1,0:T(8,128)(2,1)S(1)}, u32[]{:S(2)}, u32[]{:S(2)}) %collective-permute-start.7) | collective-permute-done | bytes 131104 | tf_op jit(solution)/shard_map/ppermute | solution.py:435
  26.3 1.9 %collective-permute-done.12.refs_5_ = bf16[128,512]{1,0:T(8,128)(2,1)S(1)} collective-permute-done((bf16[128,512]{1,0:T(8,128)(2,1)S(1)}, bf16[128,512]{1,0:T(8,128)(2,1)S(1)}, u32[]{:S(2)}, u32[]{:S(2)}) %collective-permute-start.12) | collective-permute-done | bytes 131104 | tf_op jit(solution)/shard_map/ppermute | solution.py:435
  28.3 0.4 collective-permute-start.13
  28.6 0.2 collective-permute-done.14.refs_3_
  28.8 0.1 stack_grads.2
  28.9 2.4 %collective-permute-done.9.refs_0_ = bf16[128,512]{1,0:T(8,128)(2,1)S(1)} collective-permute-done((bf16[128,512]{1,0:T(8,128)(2,1)S(1)}, bf16[128,512]{1,0:T(8,128)(2,1)S(1)}, u32[]{:S(2)}, u32[]{:S(2)}) %collective-permute-start.9) | collective-permute-done | bytes 131104 | tf_op jit(solution)/shard_map/ppermute | solution.py:435
  31.3 1.9 %collective-permute-done.13.refs_1_ = bf16[128,512]{1,0:T(8,128)(2,1)S(1)} collective-permute-done((bf16[128,512]{1,0:T(8,128)(2,1)S(1)}, bf16[128,512]{1,0:T(8,128)(2,1)S(1)}, u32[]{:S(2)}, u32[]{:S(2)}) %collective-permute-start.13) | collective-permute-done | bytes 131104 | tf_op jit(solution)/shard_map/ppermute | solution.py:435
  33.3 0.5 weight_far.2
  33.7 3.0 %collective-permute-start.17 = (bf16[128,512]{1,0:T(8,128)(2,1)S(1)}, bf16[128,512]{1,0:T(8,128)(2,1)S(1)}, u32[]{:S(2)}, u32[]{:S(2)}) collective-permute-start(bf16[128,512]{1,0:T(8,128)(2,1)S(1)} %get-tuple-element.96), channel_id=1, source_target_pairs={{0,1},{1,0},{2,3},{3,2},{4,5},{5,4},{6,7},{7,6},{8,9},{9,8},{10,11... | collective-permute-start | bytes 393224 | tf_op jit(solution)/shard_map/ppermute | solution.py:435
  36.7 0.5 weight_far.3
  37.2 0.1 collective-permute-start.15
  37.3 0.8 %weight_near.1 = (f32[128,512]{1,0:T(8,128)S(1)}, f32[128,512]{1,0:T(8,128)S(1)}, bf16[128,512]{1,0:T(8,128)(2,1)S(1)}, bf16[128,512]{1,0:T(8,128)(2,1)S(1)}) custom-call(bf16[1024,512]{1,0:T(8,128)(2,1)S(1)} %turn_pieces.1.refs_0_, bf16[1024,512]{1,0:T(8,128)(2,1)S(1)} %collective-permute-done.6.refs_1_, bf16[512,512]{1,0:T(8,128)(2,1)S(1)} %get-tuple-element.86.refs_2_, ...), custom_call_target="tpu_custom_call" | custom-call | flops 1024 | bytes 1024 | tf_op jit(solution)/shard_map/weight_near/pallas_call | solution.py:335
  38.1 2.1 %collective-permute-start.16 = (bf16[128,512]{1,0:T(8,128)(2,1)S(1)}, bf16[128,512]{1,0:T(8,128)(2,1)S(1)}, u32[]{:S(2)}, u32[]{:S(2)}) collective-permute-start(bf16[128,512]{1,0:T(8,128)(2,1)S(1)} %get-tuple-element.95), channel_id=1, source_target_pairs={{0,1},{1,0},{2,3},{3,2},{4,5},{5,4},{6,7},{7,6},{8,9},{9,8},{10,11... | collective-permute-start | bytes 393224 | tf_op jit(solution)/shard_map/ppermute | solution.py:435
  40.2 0.0 collective-permute-done.17.refs_0_
  40.2 2.6 %collective-permute-start.18 = (bf16[128,512]{1,0:T(8,128)(2,1)S(1)}, bf16[128,512]{1,0:T(8,128)(2,1)S(1)}, u32[]{:S(2)}, u32[]{:S(2)}) collective-permute-start(bf16[128,512]{1,0:T(8,128)(2,1)S(1)} %relay_total.3), channel_id=1, source_target_pairs={{0,16},{1,17},{2,18},{3,19},{4,20},{5,21},{6,22},{7,23},{8,24},{9,... | collective-permute-start | bytes 393224 | tf_op jit(solution)/shard_map/ppermute | solution.py:435
  42.8 3.2 %collective-permute-start.21 = (bf16[128,512]{1,0:T(8,128)(2,1)S(1)}, bf16[128,512]{1,0:T(8,128)(2,1)S(1)}, u32[]{:S(2)}, u32[]{:S(2)}) collective-permute-start(bf16[128,512]{1,0:T(8,128)(2,1)S(1)} %relay_total.2), channel_id=1, source_target_pairs={{0,16},{1,17},{2,18},{3,19},{4,20},{5,21},{6,22},{7,23},{8,24},{9,... | collective-permute-start | bytes 393224 | tf_op jit(solution)/shard_map/ppermute | solution.py:435
  46.0 0.9 %collective-permute-start.20 = (bf16[128,512]{1,0:T(8,128)(2,1)S(1)}, bf16[128,512]{1,0:T(8,128)(2,1)S(1)}, u32[]{:S(2)}, u32[]{:S(2)}) collective-permute-start(bf16[128,512]{1,0:T(8,128)(2,1)S(1)} %get-tuple-element.98), channel_id=1, source_target_pairs={{0,1},{1,0},{2,3},{3,2},{4,5},{5,4},{6,7},{7,6},{8,9},{9,8},{10,11... | collective-permute-start | bytes 393224 | tf_op jit(solution)/shard_map/ppermute | solution.py:435
  46.9 0.6 %collective-permute-done.18.refs_2_ = bf16[128,512]{1,0:T(8,128)(2,1)S(1)} collective-permute-done((bf16[128,512]{1,0:T(8,128)(2,1)S(1)}, bf16[128,512]{1,0:T(8,128)(2,1)S(1)}, u32[]{:S(2)}, u32[]{:S(2)}) %collective-permute-start.18) | collective-permute-done | bytes 131104 | tf_op jit(solution)/shard_map/ppermute | solution.py:435
  47.6 0.1 collective-permute-start.19
  47.7 1.7 %query_gradient.1 = bf16[128,4096]{1,0:T(8,128)(2,1)} custom-call(bf16[128,4096]{1,0:T(8,128)(2,1)S(1)} %get-tuple-element.91.refs_0_, bf16[128,4096]{1,0:T(8,128)(2,1)S(1)} %get-tuple-element.92.refs_1_, bf16[128,512]{1,0:T(8,128)(2,1)S(1)} %copy-done.2, bf16[128,512]{1,0:T(8,128)(2,1)S(1)} %collective-permute-done.refs_3_), custom_call_target="tpu_custom_call" | custom-call | flops 1024 | bytes 1024 | tf_op jit(solution)/shard_map/query_gradient/pallas_call | solution.py:157
  49.4 1.6 %collective-permute-done.20.refs_0_ = bf16[128,512]{1,0:T(8,128)(2,1)S(1)} collective-permute-done((bf16[128,512]{1,0:T(8,128)(2,1)S(1)}, bf16[128,512]{1,0:T(8,128)(2,1)S(1)}, u32[]{:S(2)}, u32[]{:S(2)}) %collective-permute-start.20) | collective-permute-done | bytes 131104 | tf_op jit(solution)/shard_map/ppermute | solution.py:435
  51.0 0.8 %weight_total.1 = (f32[128,512]{1,0:T(8,128)}, f32[128,512]{1,0:T(8,128)}) custom-call(f32[128,512]{1,0:T(8,128)S(1)} %get-tuple-element.93.block_ref, bf16[128,512]{1,0:T(8,128)(2,1)S(1)} %collective-permute-done.19.sibling_ref, bf16[128,512]{1,0:T(8,128)(2,1)S(1)} %collective-permute-done.20.refs_0_, bf16[128,512]{1,0:T(8,128)(2,1)S(1)} %collective-permute-done.21.refs_1_), custom_call_target="tpu_custom_call" | custom-call | flops 1024 | bytes 1024 | tf_op jit(solution)/shard_map/weight_total/pallas_call | solution.py:402
  (21 shorter events, 0.2 us)
Async XLA Ops:
  0.6 9.5 %copy-start.1 = (bf16[128,4096]{1,0:T(8,128)(2,1)S(1)}, bf16[128,4096]{1,0:T(8,128)(2,1)}, u32[]{:S(2)}) copy-start(bf16[128,4096]{1,0:T(8,128)(2,1)} %refs_2_.4) | copy-start | bytes 3145732
  0.6 9.5 %copy-start = (bf16[128,4096]{1,0:T(8,128)(2,1)S(1)}, bf16[128,4096]{1,0:T(8,128)(2,1)}, u32[]{:S(2)}) copy-start(bf16[128,4096]{1,0:T(8,128)(2,1)} %refs_1_.3) | copy-start | bytes 3145732
  0.7 9.4 %collective-permute-start.1 = (bf16[128,512]{1,0:T(8,128)(2,1)}, bf16[128,512]{1,0:T(8,128)(2,1)S(1)}, u32[]{:S(2)}, u32[]{:S(2)}) collective-permute-start(bf16[128,512]{1,0:T(8,128)(2,1)} %refs_4_.1), channel_id=1, source_target_pairs={{0,1},{1,0},{2,3},{3,2},{4,5},{5,4},{6,7},{7,6},{8,9},{9,8},{10,11... | collective-permute-start | bytes 393224 | tf_op jit(solution)/shard_map/ppermute | solution.py:435
  3.7 6.5 %collective-permute-start = (bf16[128,512]{1,0:T(8,128)(2,1)}, bf16[128,512]{1,0:T(8,128)(2,1)S(1)}, u32[]{:S(2)}, u32[]{:S(2)}) collective-permute-start(bf16[128,512]{1,0:T(8,128)(2,1)} %refs_2_.5), channel_id=1, source_target_pairs={{0,1},{1,0},{2,3},{3,2},{4,5},{5,4},{6,7},{7,6},{8,9},{9,8},{10,11... | collective-permute-start | bytes 393224 | tf_op jit(solution)/shard_map/ppermute | solution.py:435
  5.1 12.9 %collective-permute-start.3 = (bf16[128,1024]{1,0:T(8,128)(2,1)S(1)}, bf16[128,1024]{1,0:T(8,128)(2,1)S(1)}, u32[]{:S(2)}, u32[]{:S(2)}) collective-permute-start(bf16[128,1024]{1,0:T(8,128)(2,1)S(1)} %get-tuple-element.57), channel_id=1, source_target_pairs={{0,4},{1,5},{2,6},{3,7},{4,0},{5,1},{6,2},{7,3},{8,12},{9,13},{10,... | collective-permute-start | bytes 786440 | tf_op jit(solution)/shard_map/ppermute | solution.py:435
  7.2 10.4 %collective-permute-start.4 = (bf16[128,1024]{1,0:T(8,128)(2,1)S(1)}, bf16[128,1024]{1,0:T(8,128)(2,1)S(1)}, u32[]{:S(2)}, u32[]{:S(2)}) collective-permute-start(bf16[128,1024]{1,0:T(8,128)(2,1)S(1)} %get-tuple-element.62), channel_id=1, source_target_pairs={{0,8},{1,9},{2,10},{3,11},{4,12},{5,13},{6,14},{7,15},{8,0},{9,1},... | collective-permute-start | bytes 786440 | tf_op jit(solution)/shard_map/ppermute | solution.py:435
  8.7 13.6 %collective-permute-start.5 = (bf16[128,1024]{1,0:T(8,128)(2,1)S(1)}, bf16[128,1024]{1,0:T(8,128)(2,1)S(1)}, u32[]{:S(2)}, u32[]{:S(2)}) collective-permute-start(bf16[128,1024]{1,0:T(8,128)(2,1)S(1)} %get-tuple-element.64), channel_id=1, source_target_pairs={{0,12},{1,13},{2,14},{3,15},{4,8},{5,9},{6,10},{7,11},{8,4},{9,5},... | collective-permute-start | bytes 786440 | tf_op jit(solution)/shard_map/ppermute | solution.py:435
  10.2 5.0 %copy-start.2 = (bf16[128,512]{1,0:T(8,128)(2,1)S(1)}, bf16[128,512]{1,0:T(8,128)(2,1)}, u32[]{:S(2)}) copy-start(bf16[128,512]{1,0:T(8,128)(2,1)} %refs_2_.5) | copy-start | bytes 393220
  10.2 5.0 %copy-start.3 = (bf16[128,512]{1,0:T(8,128)(2,1)S(1)}, bf16[128,512]{1,0:T(8,128)(2,1)}, u32[]{:S(2)}) copy-start(bf16[128,512]{1,0:T(8,128)(2,1)} %refs_4_.1) | copy-start | bytes 393220
  13.3 5.4 %collective-permute-start.2 = (bf16[128,512]{1,0:T(8,128)(2,1)S(1)}, bf16[128,512]{1,0:T(8,128)(2,1)S(1)}, u32[]{:S(2)}, u32[]{:S(2)}) collective-permute-start(bf16[128,512]{1,0:T(8,128)(2,1)S(1)} %get-tuple-element.56), channel_id=1, source_target_pairs={{0,1},{1,0},{2,3},{3,2},{4,5},{5,4},{6,7},{7,6},{8,9},{9,8},{10,11... | collective-permute-start | bytes 393224 | tf_op jit(solution)/shard_map/ppermute | solution.py:435
  15.2 7.5 %collective-permute-start.11 = (bf16[128,512]{1,0:T(8,128)(2,1)S(1)}, bf16[128,512]{1,0:T(8,128)(2,1)S(1)}, u32[]{:S(2)}, u32[]{:S(2)}) collective-permute-start(bf16[128,512]{1,0:T(8,128)(2,1)S(1)} %get-tuple-element.73), channel_id=1, source_target_pairs={{0,3},{1,2},{2,1},{3,0},{4,7},{5,6},{6,5},{7,4},{8,11},{9,10},{10,... | collective-permute-start | bytes 393224 | tf_op jit(solution)/shard_map/ppermute | solution.py:435
  17.6 5.1 %collective-permute-start.10 = (bf16[128,512]{1,0:T(8,128)(2,1)S(1)}, bf16[128,512]{1,0:T(8,128)(2,1)S(1)}, u32[]{:S(2)}, u32[]{:S(2)}) collective-permute-start(bf16[128,512]{1,0:T(8,128)(2,1)S(1)} %get-tuple-element.72), channel_id=1, source_target_pairs={{0,2},{1,3},{2,0},{3,1},{4,6},{5,7},{6,4},{7,5},{8,10},{9,11},{10,... | collective-permute-start | bytes 393224 | tf_op jit(solution)/shard_map/ppermute | solution.py:435
  18.8 5.4 %collective-permute-start.8 = (bf16[128,512]{1,0:T(8,128)(2,1)S(1)}, bf16[128,512]{1,0:T(8,128)(2,1)S(1)}, u32[]{:S(2)}, u32[]{:S(2)}) collective-permute-start(bf16[128,512]{1,0:T(8,128)(2,1)S(1)} %grads_total.2.refs_0_), channel_id=1, source_target_pairs={{0,8},{1,9},{2,10},{3,11},{4,12},{5,13},{6,14},{7,15},{8,0},{9,1},... | collective-permute-start | bytes 393224 | tf_op jit(solution)/shard_map/ppermute | solution.py:435
  20.8 5.5 %collective-permute-start.7 = (bf16[128,512]{1,0:T(8,128)(2,1)S(1)}, bf16[128,512]{1,0:T(8,128)(2,1)S(1)}, u32[]{:S(2)}, u32[]{:S(2)}) collective-permute-start(bf16[128,512]{1,0:T(8,128)(2,1)S(1)} %grads_total.2.refs_0_), channel_id=1, source_target_pairs={{0,4},{1,5},{2,6},{3,7},{4,0},{5,1},{6,2},{7,3},{8,12},{9,13},{10,... | collective-permute-start | bytes 393224 | tf_op jit(solution)/shard_map/ppermute | solution.py:435
  22.7 5.5 %collective-permute-start.12 = (bf16[128,512]{1,0:T(8,128)(2,1)S(1)}, bf16[128,512]{1,0:T(8,128)(2,1)S(1)}, u32[]{:S(2)}, u32[]{:S(2)}) collective-permute-start(bf16[128,512]{1,0:T(8,128)(2,1)S(1)} %grads_total.3.refs_1_), channel_id=1, source_target_pairs={{0,8},{1,9},{2,10},{3,11},{4,12},{5,13},{6,14},{7,15},{8,0},{9,1},... | collective-permute-start | bytes 393224 | tf_op jit(solution)/shard_map/ppermute | solution.py:435
  23.2 5.6 %collective-permute-start.14 = (bf16[128,512]{1,0:T(8,128)(2,1)S(1)}, bf16[128,512]{1,0:T(8,128)(2,1)S(1)}, u32[]{:S(2)}, u32[]{:S(2)}) collective-permute-start(bf16[128,512]{1,0:T(8,128)(2,1)S(1)} %grads_total.3.refs_1_), channel_id=1, source_target_pairs={{0,4},{1,5},{2,6},{3,7},{4,0},{5,1},{6,2},{7,3},{8,12},{9,13},{10,... | collective-permute-start | bytes 393224 | tf_op jit(solution)/shard_map/ppermute | solution.py:435
  24.2 9.1 %collective-permute-start.6 = (bf16[1024,512]{1,0:T(8,128)(2,1)S(1)}, bf16[1024,512]{1,0:T(8,128)(2,1)S(1)}, u32[]{:S(2)}, u32[]{:S(2)}) collective-permute-start(bf16[1024,512]{1,0:T(8,128)(2,1)S(1)} %turn_pieces.1.refs_0_), channel_id=1, source_target_pairs={{0,2},{1,3},{2,0},{3,1},{4,6},{5,7},{6,4},{7,5},{8,10},{9,11},{10,... | collective-permute-start | bytes 3145736 | tf_op jit(solution)/shard_map/ppermute | solution.py:435
  26.3 5.0 %collective-permute-start.9 = (bf16[128,512]{1,0:T(8,128)(2,1)S(1)}, bf16[128,512]{1,0:T(8,128)(2,1)S(1)}, u32[]{:S(2)}, u32[]{:S(2)}) collective-permute-start(bf16[128,512]{1,0:T(8,128)(2,1)S(1)} %collective-permute-done.7.refs_2_), channel_id=1, source_target_pairs={{0,8},{1,9},{2,10},{3,11},{4,12},{5,13},{6,14},{7,15},{8,0},{9,1},... | collective-permute-start | bytes 393224 | tf_op jit(solution)/shard_map/ppermute | solution.py:435
  28.3 5.0 %collective-permute-start.13 = (bf16[128,512]{1,0:T(8,128)(2,1)S(1)}, bf16[128,512]{1,0:T(8,128)(2,1)S(1)}, u32[]{:S(2)}, u32[]{:S(2)}) collective-permute-start(bf16[128,512]{1,0:T(8,128)(2,1)S(1)} %collective-permute-done.12.refs_5_), channel_id=1, source_target_pairs={{0,4},{1,5},{2,6},{3,7},{4,0},{5,1},{6,2},{7,3},{8,12},{9,13},{10,... | collective-permute-start | bytes 393224 | tf_op jit(solution)/shard_map/ppermute | solution.py:435
  33.7 6.5 %collective-permute-start.17 = (bf16[128,512]{1,0:T(8,128)(2,1)S(1)}, bf16[128,512]{1,0:T(8,128)(2,1)S(1)}, u32[]{:S(2)}, u32[]{:S(2)}) collective-permute-start(bf16[128,512]{1,0:T(8,128)(2,1)S(1)} %get-tuple-element.96), channel_id=1, source_target_pairs={{0,1},{1,0},{2,3},{3,2},{4,5},{5,4},{6,7},{7,6},{8,9},{9,8},{10,11... | collective-permute-start | bytes 393224 | tf_op jit(solution)/shard_map/ppermute | solution.py:435
  37.2 5.6 %collective-permute-start.15 = (bf16[128,512]{1,0:T(8,128)(2,1)S(1)}, bf16[128,512]{1,0:T(8,128)(2,1)S(1)}, u32[]{:S(2)}, u32[]{:S(2)}) collective-permute-start(bf16[128,512]{1,0:T(8,128)(2,1)S(1)} %get-tuple-element.90), channel_id=1, source_target_pairs={{0,1},{1,0},{2,3},{3,2},{4,5},{5,4},{6,7},{7,6},{8,9},{9,8},{10,11... | collective-permute-start | bytes 393224 | tf_op jit(solution)/shard_map/ppermute | solution.py:435
  38.1 8.8 %collective-permute-start.16 = (bf16[128,512]{1,0:T(8,128)(2,1)S(1)}, bf16[128,512]{1,0:T(8,128)(2,1)S(1)}, u32[]{:S(2)}, u32[]{:S(2)}) collective-permute-start(bf16[128,512]{1,0:T(8,128)(2,1)S(1)} %get-tuple-element.95), channel_id=1, source_target_pairs={{0,1},{1,0},{2,3},{3,2},{4,5},{5,4},{6,7},{7,6},{8,9},{9,8},{10,11... | collective-permute-start | bytes 393224 | tf_op jit(solution)/shard_map/ppermute | solution.py:435
  40.2 7.3 %collective-permute-start.18 = (bf16[128,512]{1,0:T(8,128)(2,1)S(1)}, bf16[128,512]{1,0:T(8,128)(2,1)S(1)}, u32[]{:S(2)}, u32[]{:S(2)}) collective-permute-start(bf16[128,512]{1,0:T(8,128)(2,1)S(1)} %relay_total.3), channel_id=1, source_target_pairs={{0,16},{1,17},{2,18},{3,19},{4,20},{5,21},{6,22},{7,23},{8,24},{9,... | collective-permute-start | bytes 393224 | tf_op jit(solution)/shard_map/ppermute | solution.py:435
  42.8 8.2 %collective-permute-start.21 = (bf16[128,512]{1,0:T(8,128)(2,1)S(1)}, bf16[128,512]{1,0:T(8,128)(2,1)S(1)}, u32[]{:S(2)}, u32[]{:S(2)}) collective-permute-start(bf16[128,512]{1,0:T(8,128)(2,1)S(1)} %relay_total.2), channel_id=1, source_target_pairs={{0,16},{1,17},{2,18},{3,19},{4,20},{5,21},{6,22},{7,23},{8,24},{9,... | collective-permute-start | bytes 393224 | tf_op jit(solution)/shard_map/ppermute | solution.py:435
  46.0 5.0 %collective-permute-start.20 = (bf16[128,512]{1,0:T(8,128)(2,1)S(1)}, bf16[128,512]{1,0:T(8,128)(2,1)S(1)}, u32[]{:S(2)}, u32[]{:S(2)}) collective-permute-start(bf16[128,512]{1,0:T(8,128)(2,1)S(1)} %get-tuple-element.98), channel_id=1, source_target_pairs={{0,1},{1,0},{2,3},{3,2},{4,5},{5,4},{6,7},{7,6},{8,9},{9,8},{10,11... | collective-permute-start | bytes 393224 | tf_op jit(solution)/shard_map/ppermute | solution.py:435
  47.6 3.4 %collective-permute-start.19 = (bf16[128,512]{1,0:T(8,128)(2,1)S(1)}, bf16[128,512]{1,0:T(8,128)(2,1)S(1)}, u32[]{:S(2)}, u32[]{:S(2)}) collective-permute-start(bf16[128,512]{1,0:T(8,128)(2,1)S(1)} %sibling_total.1), channel_id=1, source_target_pairs={{0,2},{1,3},{2,0},{3,1},{4,6},{5,7},{6,4},{7,5},{8,10},{9,11},{10,... | collective-permute-start | bytes 393224 | tf_op jit(solution)/shard_map/ppermute | solution.py:435

commit v21 on v20

--- a/solution.py
+++ b/solution.py
@@ -490,10 +490,11 @@
         from_far.append([send(value, far_steps=s) for s, value in enumerate(relayed, 1)])
     near, own_scores = after((near, own_scores), relayed)
     near = [send(value, s) for s, value in enumerate(near, 1)]
-    sibling = send(cross_call(cross_block, cross_near, from_far[0]), core_steps=1)
     query_gradient = query_call(
         [own_scores] + scores, [saved_keys] + [pair[0] for pair in visiting], rows
     )
+    from_far[0] = after(from_far[0], query_gradient)
+    sibling = send(cross_call(cross_block, cross_near, from_far[0]), core_steps=1)
     key_weight_grad, value_weight_grad = final_call(own_block, sibling, near, from_far[1])
     return query_gradient, key_weight_grad, value_weight_grad
 

time: 52.1 us -> 53.6 us (1.029)
  waiting for transfers between devices: 11.8 us -> 14.2 us
  starting transfers between devices: 26.2 us -> 25.3 us
    ppermute x22, waiting for transfers between devices: 11.8 us -> 14.2 us  [send(): return lax.ppermute(value, ('dp', 'ctx'), pairs)]
    ppermute x22, starting transfers between devices: 26.2 us -> 25.3 us  [send(): return lax.ppermute(value, ('dp', 'ctx'), pairs)]
  transfers between devices with their start and end apart: 22 -> 22, of which waited for: 9 -> 10; matrix products, arithmetic and copies ran while one was open for 0% -> 0% of each run, Pallas kernels for 23% -> 22%
where the time goes in v21:
time: 53.6 us; the launch traced here: 53.4 us
  starting transfers between devices  25.3 us (47%)
  waiting for transfers between devices  14.2 us (26%)
  Pallas kernels  13.1 us (24%)
  between operations  0.81 us (2%)
    ppermute x22, starting transfers between devices, send(): return lax.ppermute(value, ('dp', 'ctx'), pairs)  25.3 us
    ppermute x22, waiting for transfers between devices, send(): return lax.ppermute(value, ('dp', 'ctx'), pairs)  14.2 us
    pallas_call x2, Pallas kernels, block_call(): pl.pallas_call(functools.partial(block_kernel, ctx_count, step), in_specs...  5.52 us
    pallas_call x3, Pallas kernels, weight_call(): pl.pallas_call(functools.partial(weight_kernel, core_steps, z_steps, far,...  1.77 us
    pallas_call x1, Pallas kernels, query_call(): pl.pallas_call(functools.partial(query_kernel, len(keys)), in_specs=[WHOL...  1.73 us
    pallas_call x1, Pallas kernels, pieces_call(): pl.pallas_call(functools.partial(pieces_kernel, far), in_specs=[FAR], out...  1.39 us
    pallas_call x1, Pallas kernels, near_call(): pl.pallas_call(near_kernel, in_specs=[FAR] * len(values), out_specs=[WHOL...  1.24 us
  transfers between devices with their start and end apart: 22, of which 10 were waited for; matrix products, arithmetic and copies ran while one was open for 0% of the time, Pallas kernels for 22%

profile of v21, /device:TPU:0, one launch (start us, length us, event | category | flops | bytes accessed | tf_op | source)
XLA Modules:
  0.0 53.4 jit_solution(3690205015679278530)
XLA Ops:
  0.7 3.0 %collective-permute-start.1 = (bf16[128,512]{1,0:T(8,128)(2,1)}, bf16[128,512]{1,0:T(8,128)(2,1)S(1)}, u32[]{:S(2)}, u32[]{:S(2)}) collective-permute-start(bf16[128,512]{1,0:T(8,128)(2,1)} %refs_4_.1), channel_id=1, source_target_pairs={{0,1},{1,0},{2,3},{3,2},{4,5},{5,4},{6,7},{7,6},{8,9},{9,8},{10,11... | collective-permute-start | bytes 393224 | tf_op jit(solution)/shard_map/ppermute | solution.py:435
  3.7 0.1 collective-permute-start
  3.7 1.4 %pieces.1 = (bf16[128,1024]{1,0:T(8,128)(2,1)S(1)}, bf16[128,1024]{1,0:T(8,128)(2,1)S(1)}, bf16[128,1024]{1,0:T(8,128)(2,1)S(1)}, bf16[128,1024]{1,0:T(8,128)(2,1)S(1)}) custom-call(bf16[128,4096]{1,0:T(8,128)(2,1)} %in_hbm.1), custom_call_target="tpu_custom_call" | custom-call | flops 1024 | bytes 1024 | tf_op jit(solution)/shard_map/pieces/pallas_call | solution.py:227
  5.1 2.0 %collective-permute-start.3 = (bf16[128,1024]{1,0:T(8,128)(2,1)S(1)}, bf16[128,1024]{1,0:T(8,128)(2,1)S(1)}, u32[]{:S(2)}, u32[]{:S(2)}) collective-permute-start(bf16[128,1024]{1,0:T(8,128)(2,1)S(1)} %get-tuple-element.58), channel_id=1, source_target_pairs={{0,4},{1,5},{2,6},{3,7},{4,0},{5,1},{6,2},{7,3},{8,12},{9,13},{10,... | collective-permute-start | bytes 786440 | tf_op jit(solution)/shard_map/ppermute | solution.py:435
  7.2 1.6 %collective-permute-start.4 = (bf16[128,1024]{1,0:T(8,128)(2,1)S(1)}, bf16[128,1024]{1,0:T(8,128)(2,1)S(1)}, u32[]{:S(2)}, u32[]{:S(2)}) collective-permute-start(bf16[128,1024]{1,0:T(8,128)(2,1)S(1)} %get-tuple-element.63), channel_id=1, source_target_pairs={{0,8},{1,9},{2,10},{3,11},{4,12},{5,13},{6,14},{7,15},{8,0},{9,1},... | collective-permute-start | bytes 786440 | tf_op jit(solution)/shard_map/ppermute | solution.py:435
  8.7 0.0 collective-permute-start.5
  8.7 1.2 %bring_near.1 = (bf16[128,4096]{1,0:T(8,128)(2,1)S(1)}, f32[32,128]{1,0:T(8,128)S(1)}) custom-call(bf16[128,4096]{1,0:T(8,128)(2,1)} %refs_0_.3, f32[32,128]{1,0:T(8,128)} %bitcast.1), custom_call_target="tpu_custom_call" | custom-call | flops 1024 | bytes 1024 | tf_op jit(solution)/shard_map/bring_near/pallas_call | solution.py:185
  10.0 0.0 collective-permute-done.1.refs_4_
  10.0 0.2 collective-permute-done.refs_3_
  10.2 3.1 %visiting_keys.1 = (bf16[128,4096]{1,0:T(8,128)(2,1)S(1)}, bf16[128,512]{1,0:T(8,128)(2,1)S(1)}, bf16[128,512]{1,0:T(8,128)(2,1)S(1)}, f32[32,128]{1,0:T(8,128)S(1)}) custom-call(s32[1,4]{1,0:T(1,128)} %refs_0_.5, bf16[128,4096]{1,0:T(8,128)(2,1)S(1)} %copy-done, bf16[128,4096]{1,0:T(8,128)(2,1)S(1)} %copy-done.1, ...), custom_call_target="tpu_custom_call" | custom-call | flops 5000000000 | bytes 1024 | tf_op jit(solution)/shard_map/visiting_keys/pallas_call | solution.py:130
  13.3 1.8 %collective-permute-start.2 = (bf16[128,512]{1,0:T(8,128)(2,1)S(1)}, bf16[128,512]{1,0:T(8,128)(2,1)S(1)}, u32[]{:S(2)}, u32[]{:S(2)}) collective-permute-start(bf16[128,512]{1,0:T(8,128)(2,1)S(1)} %get-tuple-element.57), channel_id=1, source_target_pairs={{0,1},{1,0},{2,3},{3,2},{4,5},{5,4},{6,7},{7,6},{8,9},{9,8},{10,11... | collective-permute-start | bytes 393224 | tf_op jit(solution)/shard_map/ppermute | solution.py:435
  15.2 2.4 %own_keys.1 = (bf16[128,4096]{1,0:T(8,128)(2,1)S(1)}, f32[128,512]{1,0:T(8,128)S(1)}, bf16[128,512]{1,0:T(8,128)(2,1)S(1)}) custom-call(s32[1,4]{1,0:T(1,128)} %refs_0_.5, bf16[128,4096]{1,0:T(8,128)(2,1)S(1)} %copy-done, bf16[128,4096]{1,0:T(8,128)(2,1)S(1)} %copy-done.1, bf16[128,512]{1,0:T(8,128)(2,1)S(1)} %copy-done.2, bf16[128,512]{1,0:T(8,128)(2,1)S(1)} %copy-done.3, ...), custom_call_target="tpu_custom_call" | custom-call | flops 1024 | bytes 1024 | tf_op jit(solution)/shard_map/own_keys/pallas_call | solution.py:130
  17.6 0.4 collective-permute-start.10
  18.0 0.7 %collective-permute-done.2.refs_1_ = bf16[128,512]{1,0:T(8,128)(2,1)S(1)} collective-permute-done((bf16[128,512]{1,0:T(8,128)(2,1)S(1)}, bf16[128,512]{1,0:T(8,128)(2,1)S(1)}, u32[]{:S(2)}, u32[]{:S(2)}) %collective-permute-start.2) | collective-permute-done | bytes 131104 | tf_op jit(solution)/shard_map/ppermute | solution.py:435
  18.8 2.0 %collective-permute-start.8 = (bf16[128,512]{1,0:T(8,128)(2,1)S(1)}, bf16[128,512]{1,0:T(8,128)(2,1)S(1)}, u32[]{:S(2)}, u32[]{:S(2)}) collective-permute-start(bf16[128,512]{1,0:T(8,128)(2,1)S(1)} %grads_total.2.refs_0_), channel_id=1, source_target_pairs={{0,8},{1,9},{2,10},{3,11},{4,12},{5,13},{6,14},{7,15},{8,0},{9,1},... | collective-permute-start | bytes 393224 | tf_op jit(solution)/shard_map/ppermute | solution.py:435
  20.8 1.5 %collective-permute-start.7 = (bf16[128,512]{1,0:T(8,128)(2,1)S(1)}, bf16[128,512]{1,0:T(8,128)(2,1)S(1)}, u32[]{:S(2)}, u32[]{:S(2)}) collective-permute-start(bf16[128,512]{1,0:T(8,128)(2,1)S(1)} %grads_total.2.refs_0_), channel_id=1, source_target_pairs={{0,4},{1,5},{2,6},{3,7},{4,0},{5,1},{6,2},{7,3},{8,12},{9,13},{10,... | collective-permute-start | bytes 393224 | tf_op jit(solution)/shard_map/ppermute | solution.py:435
  22.3 0.3 turn_pieces.1.refs_0_
  22.7 0.0 collective-permute-done.11.refs_1_
  22.7 0.0 collective-permute-done.10.refs_0_
  22.7 0.5 collective-permute-start.12
  23.2 0.9 %collective-permute-start.14 = (bf16[128,512]{1,0:T(8,128)(2,1)S(1)}, bf16[128,512]{1,0:T(8,128)(2,1)S(1)}, u32[]{:S(2)}, u32[]{:S(2)}) collective-permute-start(bf16[128,512]{1,0:T(8,128)(2,1)S(1)} %grads_total.3.refs_1_), channel_id=1, source_target_pairs={{0,4},{1,5},{2,6},{3,7},{4,0},{5,1},{6,2},{7,3},{8,12},{9,13},{10,... | collective-permute-start | bytes 393224 | tf_op jit(solution)/shard_map/ppermute | solution.py:435
  24.2 2.2 %collective-permute-done.7.refs_2_ = bf16[128,512]{1,0:T(8,128)(2,1)S(1)} collective-permute-done((bf16[128,512]{1,0:T(8,128)(2,1)S(1)}, bf16[128,512]{1,0:T(8,128)(2,1)S(1)}, u32[]{:S(2)}, u32[]{:S(2)}) %collective-permute-start.7) | collective-permute-done | bytes 131104 | tf_op jit(solution)/shard_map/ppermute | solution.py:435
  26.3 0.0 collective-permute-start.9
  26.3 1.9 %collective-permute-done.12.refs_5_ = bf16[128,512]{1,0:T(8,128)(2,1)S(1)} collective-permute-done((bf16[128,512]{1,0:T(8,128)(2,1)S(1)}, bf16[128,512]{1,0:T(8,128)(2,1)S(1)}, u32[]{:S(2)}, u32[]{:S(2)}) %collective-permute-start.12) | collective-permute-done | bytes 131104 | tf_op jit(solution)/shard_map/ppermute | solution.py:435
  28.3 0.4 collective-permute-start.13
  28.6 0.2 collective-permute-done.14.refs_3_
  28.8 0.1 stack_grads.2
  28.9 2.4 %collective-permute-done.9.refs_0_ = bf16[128,512]{1,0:T(8,128)(2,1)S(1)} collective-permute-done((bf16[128,512]{1,0:T(8,128)(2,1)S(1)}, bf16[128,512]{1,0:T(8,128)(2,1)S(1)}, u32[]{:S(2)}, u32[]{:S(2)}) %collective-permute-start.9) | collective-permute-done | bytes 131104 | tf_op jit(solution)/shard_map/ppermute | solution.py:435
  31.3 1.9 %collective-permute-done.13.refs_1_ = bf16[128,512]{1,0:T(8,128)(2,1)S(1)} collective-permute-done((bf16[128,512]{1,0:T(8,128)(2,1)S(1)}, bf16[128,512]{1,0:T(8,128)(2,1)S(1)}, u32[]{:S(2)}, u32[]{:S(2)}) %collective-permute-start.13) | collective-permute-done | bytes 131104 | tf_op jit(solution)/shard_map/ppermute | solution.py:435
  33.2 0.0 collective-permute-done.6.refs_1_
  33.3 0.5 weight_far.2
  33.7 3.0 %collective-permute-start.17 = (bf16[128,512]{1,0:T(8,128)(2,1)S(1)}, bf16[128,512]{1,0:T(8,128)(2,1)S(1)}, u32[]{:S(2)}, u32[]{:S(2)}) collective-permute-start(bf16[128,512]{1,0:T(8,128)(2,1)S(1)} %get-tuple-element.97), channel_id=1, source_target_pairs={{0,1},{1,0},{2,3},{3,2},{4,5},{5,4},{6,7},{7,6},{8,9},{9,8},{10,11... | collective-permute-start | bytes 393224 | tf_op jit(solution)/shard_map/ppermute | solution.py:435
  36.7 0.5 weight_far.3
  37.2 0.1 collective-permute-start.15
  37.3 0.8 %weight_near.1 = (f32[128,512]{1,0:T(8,128)S(1)}, f32[128,512]{1,0:T(8,128)S(1)}, bf16[128,512]{1,0:T(8,128)(2,1)S(1)}, bf16[128,512]{1,0:T(8,128)(2,1)S(1)}) custom-call(bf16[1024,512]{1,0:T(8,128)(2,1)S(1)} %turn_pieces.1.refs_0_, bf16[1024,512]{1,0:T(8,128)(2,1)S(1)} %collective-permute-done.6.refs_1_, bf16[512,512]{1,0:T(8,128)(2,1)S(1)} %get-tuple-element.87.refs_2_, ...), custom_call_target="tpu_custom_call" | custom-call | flops 1024 | bytes 1024 | tf_op jit(solution)/shard_map/weight_near/pallas_call | solution.py:335
  38.1 1.6 %collective-permute-done.17.refs_0_ = bf16[128,512]{1,0:T(8,128)(2,1)S(1)} collective-permute-done((bf16[128,512]{1,0:T(8,128)(2,1)S(1)}, bf16[128,512]{1,0:T(8,128)(2,1)S(1)}, u32[]{:S(2)}, u32[]{:S(2)}) %collective-permute-start.17) | collective-permute-done | bytes 131104 | tf_op jit(solution)/shard_map/ppermute | solution.py:435
  39.7 3.4 %collective-permute-start.18 = (bf16[128,512]{1,0:T(8,128)(2,1)S(1)}, bf16[128,512]{1,0:T(8,128)(2,1)S(1)}, u32[]{:S(2)}, u32[]{:S(2)}) collective-permute-start(bf16[128,512]{1,0:T(8,128)(2,1)S(1)} %relay_total.3), channel_id=1, source_target_pairs={{0,16},{1,17},{2,18},{3,19},{4,20},{5,21},{6,22},{7,23},{8,24},{9,... | collective-permute-start | bytes 393224 | tf_op jit(solution)/shard_map/ppermute | solution.py:435
  43.1 2.1 %collective-permute-start.16 = (bf16[128,512]{1,0:T(8,128)(2,1)S(1)}, bf16[128,512]{1,0:T(8,128)(2,1)S(1)}, u32[]{:S(2)}, u32[]{:S(2)}) collective-permute-start(bf16[128,512]{1,0:T(8,128)(2,1)S(1)} %get-tuple-element.96), channel_id=1, source_target_pairs={{0,1},{1,0},{2,3},{3,2},{4,5},{5,4},{6,7},{7,6},{8,9},{9,8},{10,11... | collective-permute-start | bytes 393224 | tf_op jit(solution)/shard_map/ppermute | solution.py:435
  45.2 0.4 collective-permute-start.21
  45.6 2.0 %collective-permute-start.20 = (bf16[128,512]{1,0:T(8,128)(2,1)S(1)}, bf16[128,512]{1,0:T(8,128)(2,1)S(1)}, u32[]{:S(2)}, u32[]{:S(2)}) collective-permute-start(bf16[128,512]{1,0:T(8,128)(2,1)S(1)} %get-tuple-element.100), channel_id=1, source_target_pairs={{0,1},{1,0},{2,3},{3,2},{4,5},{5,4},{6,7},{7,6},{8,9},{9,8},{10,11... | collective-permute-start | bytes 393224 | tf_op jit(solution)/shard_map/ppermute | solution.py:435
  47.6 1.7 %query_gradient.1 = bf16[128,4096]{1,0:T(8,128)(2,1)} custom-call(bf16[128,4096]{1,0:T(8,128)(2,1)S(1)} %get-tuple-element.92.refs_0_, bf16[128,4096]{1,0:T(8,128)(2,1)S(1)} %get-tuple-element.93.refs_1_, bf16[128,512]{1,0:T(8,128)(2,1)S(1)} %copy-done.2, bf16[128,512]{1,0:T(8,128)(2,1)S(1)} %collective-permute-done.refs_3_), custom_call_target="tpu_custom_call" | custom-call | flops 1024 | bytes 1024 | tf_op jit(solution)/shard_map/query_gradient/pallas_call | solution.py:157
  49.4 0.0 collective-permute-done.18.refs_2_
  49.4 0.0 collective-permute-done.16.refs_1_
  49.4 0.1 collective-permute-start.19
  49.5 1.1 %collective-permute-done.20.refs_0_ = bf16[128,512]{1,0:T(8,128)(2,1)S(1)} collective-permute-done((bf16[128,512]{1,0:T(8,128)(2,1)S(1)}, bf16[128,512]{1,0:T(8,128)(2,1)S(1)}, u32[]{:S(2)}, u32[]{:S(2)}) %collective-permute-start.20) | collective-permute-done | bytes 131104 | tf_op jit(solution)/shard_map/ppermute | solution.py:435
  50.6 1.9 %collective-permute-done.21.refs_1_ = bf16[128,512]{1,0:T(8,128)(2,1)S(1)} collective-permute-done((bf16[128,512]{1,0:T(8,128)(2,1)S(1)}, bf16[128,512]{1,0:T(8,128)(2,1)S(1)}, u32[]{:S(2)}, u32[]{:S(2)}) %collective-permute-start.21) | collective-permute-done | bytes 131104 | tf_op jit(solution)/shard_map/ppermute | solution.py:435
  52.5 0.0 collective-permute-done.19.sibling_ref
  52.5 0.8 %weight_total.1 = (f32[128,512]{1,0:T(8,128)}, f32[128,512]{1,0:T(8,128)}) custom-call(f32[128,512]{1,0:T(8,128)S(1)} %get-tuple-element.94.block_ref, bf16[128,512]{1,0:T(8,128)(2,1)S(1)} %collective-permute-done.19.sibling_ref, bf16[128,512]{1,0:T(8,128)(2,1)S(1)} %collective-permute-done.20.refs_0_, bf16[128,512]{1,0:T(8,128)(2,1)S(1)} %collective-permute-done.21.refs_1_), custom_call_target="tpu_custom_call" | custom-call | flops 1024 | bytes 1024 | tf_op jit(solution)/shard_map/weight_total/pallas_call | solution.py:402
  (21 shorter events, 0.2 us)
Async XLA Ops:
  0.6 9.5 %copy-start.1 = (bf16[128,4096]{1,0:T(8,128)(2,1)S(1)}, bf16[128,4096]{1,0:T(8,128)(2,1)}, u32[]{:S(2)}) copy-start(bf16[128,4096]{1,0:T(8,128)(2,1)} %refs_2_.4) | copy-start | bytes 3145732
  0.6 9.5 %copy-start = (bf16[128,4096]{1,0:T(8,128)(2,1)S(1)}, bf16[128,4096]{1,0:T(8,128)(2,1)}, u32[]{:S(2)}) copy-start(bf16[128,4096]{1,0:T(8,128)(2,1)} %refs_1_.3) | copy-start | bytes 3145732
  0.7 9.4 %collective-permute-start.1 = (bf16[128,512]{1,0:T(8,128)(2,1)}, bf16[128,512]{1,0:T(8,128)(2,1)S(1)}, u32[]{:S(2)}, u32[]{:S(2)}) collective-permute-start(bf16[128,512]{1,0:T(8,128)(2,1)} %refs_4_.1), channel_id=1, source_target_pairs={{0,1},{1,0},{2,3},{3,2},{4,5},{5,4},{6,7},{7,6},{8,9},{9,8},{10,11... | collective-permute-start | bytes 393224 | tf_op jit(solution)/shard_map/ppermute | solution.py:435
  3.7 6.5 %collective-permute-start = (bf16[128,512]{1,0:T(8,128)(2,1)}, bf16[128,512]{1,0:T(8,128)(2,1)S(1)}, u32[]{:S(2)}, u32[]{:S(2)}) collective-permute-start(bf16[128,512]{1,0:T(8,128)(2,1)} %refs_2_.5), channel_id=1, source_target_pairs={{0,1},{1,0},{2,3},{3,2},{4,5},{5,4},{6,7},{7,6},{8,9},{9,8},{10,11... | collective-permute-start | bytes 393224 | tf_op jit(solution)/shard_map/ppermute | solution.py:435
  5.1 12.9 %collective-permute-start.3 = (bf16[128,1024]{1,0:T(8,128)(2,1)S(1)}, bf16[128,1024]{1,0:T(8,128)(2,1)S(1)}, u32[]{:S(2)}, u32[]{:S(2)}) collective-permute-start(bf16[128,1024]{1,0:T(8,128)(2,1)S(1)} %get-tuple-element.58), channel_id=1, source_target_pairs={{0,4},{1,5},{2,6},{3,7},{4,0},{5,1},{6,2},{7,3},{8,12},{9,13},{10,... | collective-permute-start | bytes 786440 | tf_op jit(solution)/shard_map/ppermute | solution.py:435
  7.2 10.4 %collective-permute-start.4 = (bf16[128,1024]{1,0:T(8,128)(2,1)S(1)}, bf16[128,1024]{1,0:T(8,128)(2,1)S(1)}, u32[]{:S(2)}, u32[]{:S(2)}) collective-permute-start(bf16[128,1024]{1,0:T(8,128)(2,1)S(1)} %get-tuple-element.63), channel_id=1, source_target_pairs={{0,8},{1,9},{2,10},{3,11},{4,12},{5,13},{6,14},{7,15},{8,0},{9,1},... | collective-permute-start | bytes 786440 | tf_op jit(solution)/shard_map/ppermute | solution.py:435
  8.7 13.6 %collective-permute-start.5 = (bf16[128,1024]{1,0:T(8,128)(2,1)S(1)}, bf16[128,1024]{1,0:T(8,128)(2,1)S(1)}, u32[]{:S(2)}, u32[]{:S(2)}) collective-permute-start(bf16[128,1024]{1,0:T(8,128)(2,1)S(1)} %get-tuple-element.65), channel_id=1, source_target_pairs={{0,12},{1,13},{2,14},{3,15},{4,8},{5,9},{6,10},{7,11},{8,4},{9,5},... | collective-permute-start | bytes 786440 | tf_op jit(solution)/shard_map/ppermute | solution.py:435
  10.2 5.0 %copy-start.2 = (bf16[128,512]{1,0:T(8,128)(2,1)S(1)}, bf16[128,512]{1,0:T(8,128)(2,1)}, u32[]{:S(2)}) copy-start(bf16[128,512]{1,0:T(8,128)(2,1)} %refs_2_.5) | copy-start | bytes 393220
  10.2 5.0 %copy-start.3 = (bf16[128,512]{1,0:T(8,128)(2,1)S(1)}, bf16[128,512]{1,0:T(8,128)(2,1)}, u32[]{:S(2)}) copy-start(bf16[128,512]{1,0:T(8,128)(2,1)} %refs_4_.1) | copy-start | bytes 393220
  13.3 5.4 %collective-permute-start.2 = (bf16[128,512]{1,0:T(8,128)(2,1)S(1)}, bf16[128,512]{1,0:T(8,128)(2,1)S(1)}, u32[]{:S(2)}, u32[]{:S(2)}) collective-permute-start(bf16[128,512]{1,0:T(8,128)(2,1)S(1)} %get-tuple-element.57), channel_id=1, source_target_pairs={{0,1},{1,0},{2,3},{3,2},{4,5},{5,4},{6,7},{7,6},{8,9},{9,8},{10,11... | collective-permute-start | bytes 393224 | tf_op jit(solution)/shard_map/ppermute | solution.py:435
  15.2 7.5 %collective-permute-start.11 = (bf16[128,512]{1,0:T(8,128)(2,1)S(1)}, bf16[128,512]{1,0:T(8,128)(2,1)S(1)}, u32[]{:S(2)}, u32[]{:S(2)}) collective-permute-start(bf16[128,512]{1,0:T(8,128)(2,1)S(1)} %get-tuple-element.74), channel_id=1, source_target_pairs={{0,3},{1,2},{2,1},{3,0},{4,7},{5,6},{6,5},{7,4},{8,11},{9,10},{10,... | collective-permute-start | bytes 393224 | tf_op jit(solution)/shard_map/ppermute | solution.py:435
  17.6 5.1 %collective-permute-start.10 = (bf16[128,512]{1,0:T(8,128)(2,1)S(1)}, bf16[128,512]{1,0:T(8,128)(2,1)S(1)}, u32[]{:S(2)}, u32[]{:S(2)}) collective-permute-start(bf16[128,512]{1,0:T(8,128)(2,1)S(1)} %get-tuple-element.73), channel_id=1, source_target_pairs={{0,2},{1,3},{2,0},{3,1},{4,6},{5,7},{6,4},{7,5},{8,10},{9,11},{10,... | collective-permute-start | bytes 393224 | tf_op jit(solution)/shard_map/ppermute | solution.py:435
  18.8 5.4 %collective-permute-start.8 = (bf16[128,512]{1,0:T(8,128)(2,1)S(1)}, bf16[128,512]{1,0:T(8,128)(2,1)S(1)}, u32[]{:S(2)}, u32[]{:S(2)}) collective-permute-start(bf16[128,512]{1,0:T(8,128)(2,1)S(1)} %grads_total.2.refs_0_), channel_id=1, source_target_pairs={{0,8},{1,9},{2,10},{3,11},{4,12},{5,13},{6,14},{7,15},{8,0},{9,1},... | collective-permute-start | bytes 393224 | tf_op jit(solution)/shard_map/ppermute | solution.py:435
  20.8 5.5 %collective-permute-start.7 = (bf16[128,512]{1,0:T(8,128)(2,1)S(1)}, bf16[128,512]{1,0:T(8,128)(2,1)S(1)}, u32[]{:S(2)}, u32[]{:S(2)}) collective-permute-start(bf16[128,512]{1,0:T(8,128)(2,1)S(1)} %grads_total.2.refs_0_), channel_id=1, source_target_pairs={{0,4},{1,5},{2,6},{3,7},{4,0},{5,1},{6,2},{7,3},{8,12},{9,13},{10,... | collective-permute-start | bytes 393224 | tf_op jit(solution)/shard_map/ppermute | solution.py:435
  22.7 5.5 %collective-permute-start.12 = (bf16[128,512]{1,0:T(8,128)(2,1)S(1)}, bf16[128,512]{1,0:T(8,128)(2,1)S(1)}, u32[]{:S(2)}, u32[]{:S(2)}) collective-permute-start(bf16[128,512]{1,0:T(8,128)(2,1)S(1)} %grads_total.3.refs_1_), channel_id=1, source_target_pairs={{0,8},{1,9},{2,10},{3,11},{4,12},{5,13},{6,14},{7,15},{8,0},{9,1},... | collective-permute-start | bytes 393224 | tf_op jit(solution)/shard_map/ppermute | solution.py:435
  23.2 5.6 %collective-permute-start.14 = (bf16[128,512]{1,0:T(8,128)(2,1)S(1)}, bf16[128,512]{1,0:T(8,128)(2,1)S(1)}, u32[]{:S(2)}, u32[]{:S(2)}) collective-permute-start(bf16[128,512]{1,0:T(8,128)(2,1)S(1)} %grads_total.3.refs_1_), channel_id=1, source_target_pairs={{0,4},{1,5},{2,6},{3,7},{4,0},{5,1},{6,2},{7,3},{8,12},{9,13},{10,... | collective-permute-start | bytes 393224 | tf_op jit(solution)/shard_map/ppermute | solution.py:435
  24.2 9.1 %collective-permute-start.6 = (bf16[1024,512]{1,0:T(8,128)(2,1)S(1)}, bf16[1024,512]{1,0:T(8,128)(2,1)S(1)}, u32[]{:S(2)}, u32[]{:S(2)}) collective-permute-start(bf16[1024,512]{1,0:T(8,128)(2,1)S(1)} %turn_pieces.1.refs_0_), channel_id=1, source_target_pairs={{0,2},{1,3},{2,0},{3,1},{4,6},{5,7},{6,4},{7,5},{8,10},{9,11},{10,... | collective-permute-start | bytes 3145736 | tf_op jit(solution)/shard_map/ppermute | solution.py:435
  26.3 5.0 %collective-permute-start.9 = (bf16[128,512]{1,0:T(8,128)(2,1)S(1)}, bf16[128,512]{1,0:T(8,128)(2,1)S(1)}, u32[]{:S(2)}, u32[]{:S(2)}) collective-permute-start(bf16[128,512]{1,0:T(8,128)(2,1)S(1)} %collective-permute-done.7.refs_2_), channel_id=1, source_target_pairs={{0,8},{1,9},{2,10},{3,11},{4,12},{5,13},{6,14},{7,15},{8,0},{9,1},... | collective-permute-start | bytes 393224 | tf_op jit(solution)/shard_map/ppermute | solution.py:435
  28.3 5.0 %collective-permute-start.13 = (bf16[128,512]{1,0:T(8,128)(2,1)S(1)}, bf16[128,512]{1,0:T(8,128)(2,1)S(1)}, u32[]{:S(2)}, u32[]{:S(2)}) collective-permute-start(bf16[128,512]{1,0:T(8,128)(2,1)S(1)} %collective-permute-done.12.refs_5_), channel_id=1, source_target_pairs={{0,4},{1,5},{2,6},{3,7},{4,0},{5,1},{6,2},{7,3},{8,12},{9,13},{10,... | collective-permute-start | bytes 393224 | tf_op jit(solution)/shard_map/ppermute | solution.py:435
  33.7 5.9 %collective-permute-start.17 = (bf16[128,512]{1,0:T(8,128)(2,1)S(1)}, bf16[128,512]{1,0:T(8,128)(2,1)S(1)}, u32[]{:S(2)}, u32[]{:S(2)}) collective-permute-start(bf16[128,512]{1,0:T(8,128)(2,1)S(1)} %get-tuple-element.97), channel_id=1, source_target_pairs={{0,1},{1,0},{2,3},{3,2},{4,5},{5,4},{6,7},{7,6},{8,9},{9,8},{10,11... | collective-permute-start | bytes 393224 | tf_op jit(solution)/shard_map/ppermute | solution.py:435
  37.2 7.9 %collective-permute-start.15 = (bf16[128,512]{1,0:T(8,128)(2,1)S(1)}, bf16[128,512]{1,0:T(8,128)(2,1)S(1)}, u32[]{:S(2)}, u32[]{:S(2)}) collective-permute-start(bf16[128,512]{1,0:T(8,128)(2,1)S(1)} %get-tuple-element.91), channel_id=1, source_target_pairs={{0,1},{1,0},{2,3},{3,2},{4,5},{5,4},{6,7},{7,6},{8,9},{9,8},{10,11... | collective-permute-start | bytes 393224 | tf_op jit(solution)/shard_map/ppermute | solution.py:435
  39.7 9.7 %collective-permute-start.18 = (bf16[128,512]{1,0:T(8,128)(2,1)S(1)}, bf16[128,512]{1,0:T(8,128)(2,1)S(1)}, u32[]{:S(2)}, u32[]{:S(2)}) collective-permute-start(bf16[128,512]{1,0:T(8,128)(2,1)S(1)} %relay_total.3), channel_id=1, source_target_pairs={{0,16},{1,17},{2,18},{3,19},{4,20},{5,21},{6,22},{7,23},{8,24},{9,... | collective-permute-start | bytes 393224 | tf_op jit(solution)/shard_map/ppermute | solution.py:435
  43.1 6.3 %collective-permute-start.16 = (bf16[128,512]{1,0:T(8,128)(2,1)S(1)}, bf16[128,512]{1,0:T(8,128)(2,1)S(1)}, u32[]{:S(2)}, u32[]{:S(2)}) collective-permute-start(bf16[128,512]{1,0:T(8,128)(2,1)S(1)} %get-tuple-element.96), channel_id=1, source_target_pairs={{0,1},{1,0},{2,3},{3,2},{4,5},{5,4},{6,7},{7,6},{8,9},{9,8},{10,11... | collective-permute-start | bytes 393224 | tf_op jit(solution)/shard_map/ppermute | solution.py:435
  45.2 7.3 %collective-permute-start.21 = (bf16[128,512]{1,0:T(8,128)(2,1)S(1)}, bf16[128,512]{1,0:T(8,128)(2,1)S(1)}, u32[]{:S(2)}, u32[]{:S(2)}) collective-permute-start(bf16[128,512]{1,0:T(8,128)(2,1)S(1)} %relay_total.2), channel_id=1, source_target_pairs={{0,16},{1,17},{2,18},{3,19},{4,20},{5,21},{6,22},{7,23},{8,24},{9,... | collective-permute-start | bytes 393224 | tf_op jit(solution)/shard_map/ppermute | solution.py:435
  45.6 5.0 %collective-permute-start.20 = (bf16[128,512]{1,0:T(8,128)(2,1)S(1)}, bf16[128,512]{1,0:T(8,128)(2,1)S(1)}, u32[]{:S(2)}, u32[]{:S(2)}) collective-permute-start(bf16[128,512]{1,0:T(8,128)(2,1)S(1)} %get-tuple-element.100), channel_id=1, source_target_pairs={{0,1},{1,0},{2,3},{3,2},{4,5},{5,4},{6,7},{7,6},{8,9},{9,8},{10,11... | collective-permute-start | bytes 393224 | tf_op jit(solution)/shard_map/ppermute | solution.py:435
  49.4 3.1 %collective-permute-start.19 = (bf16[128,512]{1,0:T(8,128)(2,1)S(1)}, bf16[128,512]{1,0:T(8,128)(2,1)S(1)}, u32[]{:S(2)}, u32[]{:S(2)}) collective-permute-start(bf16[128,512]{1,0:T(8,128)(2,1)S(1)} %sibling_total.1), channel_id=1, source_target_pairs={{0,2},{1,3},{2,0},{3,1},{4,6},{5,7},{6,4},{7,5},{8,10},{9,11},{10,... | collective-permute-start | bytes 393224 | tf_op jit(solution)/shard_map/ppermute | solution.py:435

commit v22 on v20

--- a/solution.py
+++ b/solution.py
@@ -13,6 +13,8 @@
 HEAD_SIZE = 128
 GROUP = QUERY_HEADS // KEY_VALUE_HEADS
 SCALE = 1.0 / math.sqrt(HEAD_SIZE)
+LOG2_E = math.log2(math.e)
+EXPONENT_SCALE = SCALE * LOG2_E
 CORES = 2
 MIDDLE = 2
 NEAR = 2
@@ -95,7 +97,7 @@
             refs[10][group, :] = delta
         else:
             delta = other_ref[group, :]
-        lse = lse_ref[group, :]
+        lse = lse_ref[group, :] * LOG2_E
         columns = slice(g * HEAD_SIZE, (g + 1) * HEAD_SIZE)
         scores = dot(k_ref[:, columns], q, NT)
         grad_probs = dot(v_ref[:, columns], do, NT)
@@ -103,7 +105,7 @@
         grad_scores = []
         for h in range(GROUP):
             cut = slice(h * rows, (h + 1) * rows)
-            probs = jnp.where(allowed, jnp.exp(scores[:, cut] * SCALE - lse[h : h + 1, :]), 0.0)
+            probs = jnp.where(allowed, jnp.exp2(scores[:, cut] * EXPONENT_SCALE - lse[h : h + 1, :]), 0.0)
             grad_scores.append(
                 (probs * (grad_probs[:, cut] - delta[h : h + 1, :])).astype(jnp.bfloat16)
             )

time: 52.1 us -> 52.1 us (level)
  no operation moved by 1% of the time
where the time goes in v22:
time: 52.1 us; the launch traced here: 51.9 us
  starting transfers between devices  26.1 us (50%)
  Pallas kernels  13.1 us (25%)
  waiting for transfers between devices  11.9 us (23%)
  between operations  0.81 us (2%)
    ppermute x22, starting transfers between devices, send(): return lax.ppermute(value, ('dp', 'ctx'), pairs)  26.1 us
    ppermute x22, waiting for transfers between devices, send(): return lax.ppermute(value, ('dp', 'ctx'), pairs)  11.9 us
    pallas_call x2, Pallas kernels, block_call(): pl.pallas_call(functools.partial(block_kernel, ctx_count, step), in_specs...  5.52 us
    pallas_call x3, Pallas kernels, weight_call(): pl.pallas_call(functools.partial(weight_kernel, core_steps, z_steps, far,...  1.77 us
    pallas_call x1, Pallas kernels, query_call(): pl.pallas_call(functools.partial(query_kernel, len(keys)), in_specs=[WHOL...  1.74 us
    pallas_call x1, Pallas kernels, pieces_call(): pl.pallas_call(functools.partial(pieces_kernel, far), in_specs=[FAR], out...  1.39 us
    pallas_call x1, Pallas kernels, near_call(): pl.pallas_call(near_kernel, in_specs=[FAR] * len(values), out_specs=[WHOL...  1.24 us
  transfers between devices with their start and end apart: 22, of which 9 were waited for; matrix products, arithmetic and copies ran while one was open for 0% of the time, Pallas kernels for 23%

profile of v22, /device:TPU:0, one launch (start us, length us, event | category | flops | bytes accessed | tf_op | source)
XLA Modules:
  0.0 51.9 jit_solution(7019320968677091936)
XLA Ops:
  0.7 3.0 %collective-permute-start.1 = (bf16[128,512]{1,0:T(8,128)(2,1)}, bf16[128,512]{1,0:T(8,128)(2,1)S(1)}, u32[]{:S(2)}, u32[]{:S(2)}) collective-permute-start(bf16[128,512]{1,0:T(8,128)(2,1)} %refs_4_.1), channel_id=1, source_target_pairs={{0,1},{1,0},{2,3},{3,2},{4,5},{5,4},{6,7},{7,6},{8,9},{9,8},{10,11... | collective-permute-start | bytes 393224 | tf_op jit(solution)/shard_map/ppermute | solution.py:437
  3.7 0.1 collective-permute-start
  3.7 1.4 %pieces.1 = (bf16[128,1024]{1,0:T(8,128)(2,1)S(1)}, bf16[128,1024]{1,0:T(8,128)(2,1)S(1)}, bf16[128,1024]{1,0:T(8,128)(2,1)S(1)}, bf16[128,1024]{1,0:T(8,128)(2,1)S(1)}) custom-call(bf16[128,4096]{1,0:T(8,128)(2,1)} %in_hbm.1), custom_call_target="tpu_custom_call" | custom-call | flops 1024 | bytes 1024 | tf_op jit(solution)/shard_map/pieces/pallas_call | solution.py:229
  5.1 2.0 %collective-permute-start.3 = (bf16[128,1024]{1,0:T(8,128)(2,1)S(1)}, bf16[128,1024]{1,0:T(8,128)(2,1)S(1)}, u32[]{:S(2)}, u32[]{:S(2)}) collective-permute-start(bf16[128,1024]{1,0:T(8,128)(2,1)S(1)} %get-tuple-element.57), channel_id=1, source_target_pairs={{0,4},{1,5},{2,6},{3,7},{4,0},{5,1},{6,2},{7,3},{8,12},{9,13},{10,... | collective-permute-start | bytes 786440 | tf_op jit(solution)/shard_map/ppermute | solution.py:437
  7.2 1.6 %collective-permute-start.4 = (bf16[128,1024]{1,0:T(8,128)(2,1)S(1)}, bf16[128,1024]{1,0:T(8,128)(2,1)S(1)}, u32[]{:S(2)}, u32[]{:S(2)}) collective-permute-start(bf16[128,1024]{1,0:T(8,128)(2,1)S(1)} %get-tuple-element.62), channel_id=1, source_target_pairs={{0,8},{1,9},{2,10},{3,11},{4,12},{5,13},{6,14},{7,15},{8,0},{9,1},... | collective-permute-start | bytes 786440 | tf_op jit(solution)/shard_map/ppermute | solution.py:437
  8.7 0.0 collective-permute-start.5
  8.7 1.2 %bring_near.1 = (bf16[128,4096]{1,0:T(8,128)(2,1)S(1)}, f32[32,128]{1,0:T(8,128)S(1)}) custom-call(bf16[128,4096]{1,0:T(8,128)(2,1)} %refs_0_.3, f32[32,128]{1,0:T(8,128)} %bitcast.1), custom_call_target="tpu_custom_call" | custom-call | flops 1024 | bytes 1024 | tf_op jit(solution)/shard_map/bring_near/pallas_call | solution.py:187
  10.0 0.0 collective-permute-done.1.refs_4_
  10.0 0.2 collective-permute-done.refs_3_
  10.2 3.2 %visiting_keys.1 = (bf16[128,4096]{1,0:T(8,128)(2,1)S(1)}, bf16[128,512]{1,0:T(8,128)(2,1)S(1)}, bf16[128,512]{1,0:T(8,128)(2,1)S(1)}, f32[32,128]{1,0:T(8,128)S(1)}) custom-call(s32[1,4]{1,0:T(1,128)} %refs_0_.5, bf16[128,4096]{1,0:T(8,128)(2,1)S(1)} %copy-done, bf16[128,4096]{1,0:T(8,128)(2,1)S(1)} %copy-done.1, ...), custom_call_target="tpu_custom_call" | custom-call | flops 5000000000 | bytes 1024 | tf_op jit(solution)/shard_map/visiting_keys/pallas_call | solution.py:132
  13.4 1.8 %collective-permute-start.2 = (bf16[128,512]{1,0:T(8,128)(2,1)S(1)}, bf16[128,512]{1,0:T(8,128)(2,1)S(1)}, u32[]{:S(2)}, u32[]{:S(2)}) collective-permute-start(bf16[128,512]{1,0:T(8,128)(2,1)S(1)} %get-tuple-element.56), channel_id=1, source_target_pairs={{0,1},{1,0},{2,3},{3,2},{4,5},{5,4},{6,7},{7,6},{8,9},{9,8},{10,11... | collective-permute-start | bytes 393224 | tf_op jit(solution)/shard_map/ppermute | solution.py:437
  15.2 0.0 collective-permute-start.11
  15.2 2.3 %own_keys.1 = (bf16[128,4096]{1,0:T(8,128)(2,1)S(1)}, f32[128,512]{1,0:T(8,128)S(1)}, bf16[128,512]{1,0:T(8,128)(2,1)S(1)}) custom-call(s32[1,4]{1,0:T(1,128)} %refs_0_.5, bf16[128,4096]{1,0:T(8,128)(2,1)S(1)} %copy-done, bf16[128,4096]{1,0:T(8,128)(2,1)S(1)} %copy-done.1, bf16[128,512]{1,0:T(8,128)(2,1)S(1)} %copy-done.2, bf16[128,512]{1,0:T(8,128)(2,1)S(1)} %copy-done.3, ...), custom_call_target="tpu_custom_call" | custom-call | flops 1024 | bytes 1024 | tf_op jit(solution)/shard_map/own_keys/pallas_call | solution.py:132
  17.5 0.0 collective-permute-done.4.refs_2_
  17.6 0.4 collective-permute-start.10
  18.0 0.0 collective-permute-done.3.refs_1_
  18.0 0.8 %collective-permute-done.2.refs_1_ = bf16[128,512]{1,0:T(8,128)(2,1)S(1)} collective-permute-done((bf16[128,512]{1,0:T(8,128)(2,1)S(1)}, bf16[128,512]{1,0:T(8,128)(2,1)S(1)}, u32[]{:S(2)}, u32[]{:S(2)}) %collective-permute-start.2) | collective-permute-done | bytes 131104 | tf_op jit(solution)/shard_map/ppermute | solution.py:437
  18.8 2.0 %collective-permute-start.8 = (bf16[128,512]{1,0:T(8,128)(2,1)S(1)}, bf16[128,512]{1,0:T(8,128)(2,1)S(1)}, u32[]{:S(2)}, u32[]{:S(2)}) collective-permute-start(bf16[128,512]{1,0:T(8,128)(2,1)S(1)} %grads_total.2.refs_0_), channel_id=1, source_target_pairs={{0,8},{1,9},{2,10},{3,11},{4,12},{5,13},{6,14},{7,15},{8,0},{9,1},... | collective-permute-start | bytes 393224 | tf_op jit(solution)/shard_map/ppermute | solution.py:437
  20.8 1.5 %collective-permute-start.7 = (bf16[128,512]{1,0:T(8,128)(2,1)S(1)}, bf16[128,512]{1,0:T(8,128)(2,1)S(1)}, u32[]{:S(2)}, u32[]{:S(2)}) collective-permute-start(bf16[128,512]{1,0:T(8,128)(2,1)S(1)} %grads_total.2.refs_0_), channel_id=1, source_target_pairs={{0,4},{1,5},{2,6},{3,7},{4,0},{5,1},{6,2},{7,3},{8,12},{9,13},{10,... | collective-permute-start | bytes 393224 | tf_op jit(solution)/shard_map/ppermute | solution.py:437
  22.4 0.0 collective-permute-done.5.refs_3_
  22.4 0.3 turn_pieces.1.refs_0_
  22.7 0.0 collective-permute-done.11.refs_1_
  22.7 0.0 collective-permute-done.10.refs_0_
  22.8 0.5 collective-permute-start.12
  23.3 0.9 %collective-permute-start.14 = (bf16[128,512]{1,0:T(8,128)(2,1)S(1)}, bf16[128,512]{1,0:T(8,128)(2,1)S(1)}, u32[]{:S(2)}, u32[]{:S(2)}) collective-permute-start(bf16[128,512]{1,0:T(8,128)(2,1)S(1)} %grads_total.3.refs_1_), channel_id=1, source_target_pairs={{0,4},{1,5},{2,6},{3,7},{4,0},{5,1},{6,2},{7,3},{8,12},{9,13},{10,... | collective-permute-start | bytes 393224 | tf_op jit(solution)/shard_map/ppermute | solution.py:437
  24.2 2.1 %collective-permute-done.7.refs_2_ = bf16[128,512]{1,0:T(8,128)(2,1)S(1)} collective-permute-done((bf16[128,512]{1,0:T(8,128)(2,1)S(1)}, bf16[128,512]{1,0:T(8,128)(2,1)S(1)}, u32[]{:S(2)}, u32[]{:S(2)}) %collective-permute-start.7) | collective-permute-done | bytes 131104 | tf_op jit(solution)/shard_map/ppermute | solution.py:437
  26.3 2.0 %collective-permute-done.12.refs_5_ = bf16[128,512]{1,0:T(8,128)(2,1)S(1)} collective-permute-done((bf16[128,512]{1,0:T(8,128)(2,1)S(1)}, bf16[128,512]{1,0:T(8,128)(2,1)S(1)}, u32[]{:S(2)}, u32[]{:S(2)}) %collective-permute-start.12) | collective-permute-done | bytes 131104 | tf_op jit(solution)/shard_map/ppermute | solution.py:437
  28.3 0.3 collective-permute-start.13
  28.7 0.2 collective-permute-done.14.refs_3_
  28.8 0.1 stack_grads.2
  28.9 2.4 %collective-permute-done.9.refs_0_ = bf16[128,512]{1,0:T(8,128)(2,1)S(1)} collective-permute-done((bf16[128,512]{1,0:T(8,128)(2,1)S(1)}, bf16[128,512]{1,0:T(8,128)(2,1)S(1)}, u32[]{:S(2)}, u32[]{:S(2)}) %collective-permute-start.9) | collective-permute-done | bytes 131104 | tf_op jit(solution)/shard_map/ppermute | solution.py:437
  31.3 2.0 %collective-permute-done.13.refs_1_ = bf16[128,512]{1,0:T(8,128)(2,1)S(1)} collective-permute-done((bf16[128,512]{1,0:T(8,128)(2,1)S(1)}, bf16[128,512]{1,0:T(8,128)(2,1)S(1)}, u32[]{:S(2)}, u32[]{:S(2)}) %collective-permute-start.13) | collective-permute-done | bytes 131104 | tf_op jit(solution)/shard_map/ppermute | solution.py:437
  33.3 0.5 weight_far.2
  33.8 3.0 %collective-permute-start.17 = (bf16[128,512]{1,0:T(8,128)(2,1)S(1)}, bf16[128,512]{1,0:T(8,128)(2,1)S(1)}, u32[]{:S(2)}, u32[]{:S(2)}) collective-permute-start(bf16[128,512]{1,0:T(8,128)(2,1)S(1)} %get-tuple-element.96), channel_id=1, source_target_pairs={{0,1},{1,0},{2,3},{3,2},{4,5},{5,4},{6,7},{7,6},{8,9},{9,8},{10,11... | collective-permute-start | bytes 393224 | tf_op jit(solution)/shard_map/ppermute | solution.py:437
  36.8 0.5 weight_far.3
  37.3 0.1 collective-permute-start.15
  37.4 0.8 %weight_near.1 = (f32[128,512]{1,0:T(8,128)S(1)}, f32[128,512]{1,0:T(8,128)S(1)}, bf16[128,512]{1,0:T(8,128)(2,1)S(1)}, bf16[128,512]{1,0:T(8,128)(2,1)S(1)}) custom-call(bf16[1024,512]{1,0:T(8,128)(2,1)S(1)} %turn_pieces.1.refs_0_, bf16[1024,512]{1,0:T(8,128)(2,1)S(1)} %collective-permute-done.6.refs_1_, bf16[512,512]{1,0:T(8,128)(2,1)S(1)} %get-tuple-element.86.refs_2_, ...), custom_call_target="tpu_custom_call" | custom-call | flops 1024 | bytes 1024 | tf_op jit(solution)/shard_map/weight_near/pallas_call | solution.py:337
  38.2 2.1 %collective-permute-start.16 = (bf16[128,512]{1,0:T(8,128)(2,1)S(1)}, bf16[128,512]{1,0:T(8,128)(2,1)S(1)}, u32[]{:S(2)}, u32[]{:S(2)}) collective-permute-start(bf16[128,512]{1,0:T(8,128)(2,1)S(1)} %get-tuple-element.95), channel_id=1, source_target_pairs={{0,1},{1,0},{2,3},{3,2},{4,5},{5,4},{6,7},{7,6},{8,9},{9,8},{10,11... | collective-permute-start | bytes 393224 | tf_op jit(solution)/shard_map/ppermute | solution.py:437
  40.2 0.0 collective-permute-done.17.refs_0_
  40.3 2.6 %collective-permute-start.18 = (bf16[128,512]{1,0:T(8,128)(2,1)S(1)}, bf16[128,512]{1,0:T(8,128)(2,1)S(1)}, u32[]{:S(2)}, u32[]{:S(2)}) collective-permute-start(bf16[128,512]{1,0:T(8,128)(2,1)S(1)} %relay_total.3), channel_id=1, source_target_pairs={{0,16},{1,17},{2,18},{3,19},{4,20},{5,21},{6,22},{7,23},{8,24},{9,... | collective-permute-start | bytes 393224 | tf_op jit(solution)/shard_map/ppermute | solution.py:437
  42.8 0.0 collective-permute-done.15.refs_0_
  42.9 3.2 %collective-permute-start.21 = (bf16[128,512]{1,0:T(8,128)(2,1)S(1)}, bf16[128,512]{1,0:T(8,128)(2,1)S(1)}, u32[]{:S(2)}, u32[]{:S(2)}) collective-permute-start(bf16[128,512]{1,0:T(8,128)(2,1)S(1)} %relay_total.2), channel_id=1, source_target_pairs={{0,16},{1,17},{2,18},{3,19},{4,20},{5,21},{6,22},{7,23},{8,24},{9,... | collective-permute-start | bytes 393224 | tf_op jit(solution)/shard_map/ppermute | solution.py:437
  46.0 0.9 %collective-permute-start.20 = (bf16[128,512]{1,0:T(8,128)(2,1)S(1)}, bf16[128,512]{1,0:T(8,128)(2,1)S(1)}, u32[]{:S(2)}, u32[]{:S(2)}) collective-permute-start(bf16[128,512]{1,0:T(8,128)(2,1)S(1)} %get-tuple-element.98), channel_id=1, source_target_pairs={{0,1},{1,0},{2,3},{3,2},{4,5},{5,4},{6,7},{7,6},{8,9},{9,8},{10,11... | collective-permute-start | bytes 393224 | tf_op jit(solution)/shard_map/ppermute | solution.py:437
  47.0 0.6 %collective-permute-done.18.refs_2_ = bf16[128,512]{1,0:T(8,128)(2,1)S(1)} collective-permute-done((bf16[128,512]{1,0:T(8,128)(2,1)S(1)}, bf16[128,512]{1,0:T(8,128)(2,1)S(1)}, u32[]{:S(2)}, u32[]{:S(2)}) %collective-permute-start.18) | collective-permute-done | bytes 131104 | tf_op jit(solution)/shard_map/ppermute | solution.py:437
  47.7 0.1 collective-permute-start.19
  47.7 1.7 %query_gradient.1 = bf16[128,4096]{1,0:T(8,128)(2,1)} custom-call(bf16[128,4096]{1,0:T(8,128)(2,1)S(1)} %get-tuple-element.91.refs_0_, bf16[128,4096]{1,0:T(8,128)(2,1)S(1)} %get-tuple-element.92.refs_1_, bf16[128,512]{1,0:T(8,128)(2,1)S(1)} %copy-done.2, bf16[128,512]{1,0:T(8,128)(2,1)S(1)} %collective-permute-done.refs_3_), custom_call_target="tpu_custom_call" | custom-call | flops 1024 | bytes 1024 | tf_op jit(solution)/shard_map/query_gradient/pallas_call | solution.py:159
  49.5 1.5 %collective-permute-done.20.refs_0_ = bf16[128,512]{1,0:T(8,128)(2,1)S(1)} collective-permute-done((bf16[128,512]{1,0:T(8,128)(2,1)S(1)}, bf16[128,512]{1,0:T(8,128)(2,1)S(1)}, u32[]{:S(2)}, u32[]{:S(2)}) %collective-permute-start.20) | collective-permute-done | bytes 131104 | tf_op jit(solution)/shard_map/ppermute | solution.py:437
  51.0 0.8 %weight_total.1 = (f32[128,512]{1,0:T(8,128)}, f32[128,512]{1,0:T(8,128)}) custom-call(f32[128,512]{1,0:T(8,128)S(1)} %get-tuple-element.93.block_ref, bf16[128,512]{1,0:T(8,128)(2,1)S(1)} %collective-permute-done.19.sibling_ref, bf16[128,512]{1,0:T(8,128)(2,1)S(1)} %collective-permute-done.20.refs_0_, bf16[128,512]{1,0:T(8,128)(2,1)S(1)} %collective-permute-done.21.refs_1_), custom_call_target="tpu_custom_call" | custom-call | flops 1024 | bytes 1024 | tf_op jit(solution)/shard_map/weight_total/pallas_call | solution.py:404
  (21 shorter events, 0.2 us)
Async XLA Ops:
  0.6 9.5 %copy-start.1 = (bf16[128,4096]{1,0:T(8,128)(2,1)S(1)}, bf16[128,4096]{1,0:T(8,128)(2,1)}, u32[]{:S(2)}) copy-start(bf16[128,4096]{1,0:T(8,128)(2,1)} %refs_2_.4) | copy-start | bytes 3145732
  0.6 9.5 %copy-start = (bf16[128,4096]{1,0:T(8,128)(2,1)S(1)}, bf16[128,4096]{1,0:T(8,128)(2,1)}, u32[]{:S(2)}) copy-start(bf16[128,4096]{1,0:T(8,128)(2,1)} %refs_1_.3) | copy-start | bytes 3145732
  0.7 9.4 %collective-permute-start.1 = (bf16[128,512]{1,0:T(8,128)(2,1)}, bf16[128,512]{1,0:T(8,128)(2,1)S(1)}, u32[]{:S(2)}, u32[]{:S(2)}) collective-permute-start(bf16[128,512]{1,0:T(8,128)(2,1)} %refs_4_.1), channel_id=1, source_target_pairs={{0,1},{1,0},{2,3},{3,2},{4,5},{5,4},{6,7},{7,6},{8,9},{9,8},{10,11... | collective-permute-start | bytes 393224 | tf_op jit(solution)/shard_map/ppermute | solution.py:437
  3.7 6.5 %collective-permute-start = (bf16[128,512]{1,0:T(8,128)(2,1)}, bf16[128,512]{1,0:T(8,128)(2,1)S(1)}, u32[]{:S(2)}, u32[]{:S(2)}) collective-permute-start(bf16[128,512]{1,0:T(8,128)(2,1)} %refs_2_.5), channel_id=1, source_target_pairs={{0,1},{1,0},{2,3},{3,2},{4,5},{5,4},{6,7},{7,6},{8,9},{9,8},{10,11... | collective-permute-start | bytes 393224 | tf_op jit(solution)/shard_map/ppermute | solution.py:437
  5.1 12.9 %collective-permute-start.3 = (bf16[128,1024]{1,0:T(8,128)(2,1)S(1)}, bf16[128,1024]{1,0:T(8,128)(2,1)S(1)}, u32[]{:S(2)}, u32[]{:S(2)}) collective-permute-start(bf16[128,1024]{1,0:T(8,128)(2,1)S(1)} %get-tuple-element.57), channel_id=1, source_target_pairs={{0,4},{1,5},{2,6},{3,7},{4,0},{5,1},{6,2},{7,3},{8,12},{9,13},{10,... | collective-permute-start | bytes 786440 | tf_op jit(solution)/shard_map/ppermute | solution.py:437
  7.2 10.4 %collective-permute-start.4 = (bf16[128,1024]{1,0:T(8,128)(2,1)S(1)}, bf16[128,1024]{1,0:T(8,128)(2,1)S(1)}, u32[]{:S(2)}, u32[]{:S(2)}) collective-permute-start(bf16[128,1024]{1,0:T(8,128)(2,1)S(1)} %get-tuple-element.62), channel_id=1, source_target_pairs={{0,8},{1,9},{2,10},{3,11},{4,12},{5,13},{6,14},{7,15},{8,0},{9,1},... | collective-permute-start | bytes 786440 | tf_op jit(solution)/shard_map/ppermute | solution.py:437
  8.7 13.6 %collective-permute-start.5 = (bf16[128,1024]{1,0:T(8,128)(2,1)S(1)}, bf16[128,1024]{1,0:T(8,128)(2,1)S(1)}, u32[]{:S(2)}, u32[]{:S(2)}) collective-permute-start(bf16[128,1024]{1,0:T(8,128)(2,1)S(1)} %get-tuple-element.64), channel_id=1, source_target_pairs={{0,12},{1,13},{2,14},{3,15},{4,8},{5,9},{6,10},{7,11},{8,4},{9,5},... | collective-permute-start | bytes 786440 | tf_op jit(solution)/shard_map/ppermute | solution.py:437
  10.2 5.0 %copy-start.2 = (bf16[128,512]{1,0:T(8,128)(2,1)S(1)}, bf16[128,512]{1,0:T(8,128)(2,1)}, u32[]{:S(2)}) copy-start(bf16[128,512]{1,0:T(8,128)(2,1)} %refs_2_.5) | copy-start | bytes 393220
  10.2 5.0 %copy-start.3 = (bf16[128,512]{1,0:T(8,128)(2,1)S(1)}, bf16[128,512]{1,0:T(8,128)(2,1)}, u32[]{:S(2)}) copy-start(bf16[128,512]{1,0:T(8,128)(2,1)} %refs_4_.1) | copy-start | bytes 393220
  13.4 5.4 %collective-permute-start.2 = (bf16[128,512]{1,0:T(8,128)(2,1)S(1)}, bf16[128,512]{1,0:T(8,128)(2,1)S(1)}, u32[]{:S(2)}, u32[]{:S(2)}) collective-permute-start(bf16[128,512]{1,0:T(8,128)(2,1)S(1)} %get-tuple-element.56), channel_id=1, source_target_pairs={{0,1},{1,0},{2,3},{3,2},{4,5},{5,4},{6,7},{7,6},{8,9},{9,8},{10,11... | collective-permute-start | bytes 393224 | tf_op jit(solution)/shard_map/ppermute | solution.py:437
  15.2 7.5 %collective-permute-start.11 = (bf16[128,512]{1,0:T(8,128)(2,1)S(1)}, bf16[128,512]{1,0:T(8,128)(2,1)S(1)}, u32[]{:S(2)}, u32[]{:S(2)}) collective-permute-start(bf16[128,512]{1,0:T(8,128)(2,1)S(1)} %get-tuple-element.73), channel_id=1, source_target_pairs={{0,3},{1,2},{2,1},{3,0},{4,7},{5,6},{6,5},{7,4},{8,11},{9,10},{10,... | collective-permute-start | bytes 393224 | tf_op jit(solution)/shard_map/ppermute | solution.py:437
  17.6 5.2 %collective-permute-start.10 = (bf16[128,512]{1,0:T(8,128)(2,1)S(1)}, bf16[128,512]{1,0:T(8,128)(2,1)S(1)}, u32[]{:S(2)}, u32[]{:S(2)}) collective-permute-start(bf16[128,512]{1,0:T(8,128)(2,1)S(1)} %get-tuple-element.72), channel_id=1, source_target_pairs={{0,2},{1,3},{2,0},{3,1},{4,6},{5,7},{6,4},{7,5},{8,10},{9,11},{10,... | collective-permute-start | bytes 393224 | tf_op jit(solution)/shard_map/ppermute | solution.py:437
  18.8 5.4 %collective-permute-start.8 = (bf16[128,512]{1,0:T(8,128)(2,1)S(1)}, bf16[128,512]{1,0:T(8,128)(2,1)S(1)}, u32[]{:S(2)}, u32[]{:S(2)}) collective-permute-start(bf16[128,512]{1,0:T(8,128)(2,1)S(1)} %grads_total.2.refs_0_), channel_id=1, source_target_pairs={{0,8},{1,9},{2,10},{3,11},{4,12},{5,13},{6,14},{7,15},{8,0},{9,1},... | collective-permute-start | bytes 393224 | tf_op jit(solution)/shard_map/ppermute | solution.py:437
  20.8 5.5 %collective-permute-start.7 = (bf16[128,512]{1,0:T(8,128)(2,1)S(1)}, bf16[128,512]{1,0:T(8,128)(2,1)S(1)}, u32[]{:S(2)}, u32[]{:S(2)}) collective-permute-start(bf16[128,512]{1,0:T(8,128)(2,1)S(1)} %grads_total.2.refs_0_), channel_id=1, source_target_pairs={{0,4},{1,5},{2,6},{3,7},{4,0},{5,1},{6,2},{7,3},{8,12},{9,13},{10,... | collective-permute-start | bytes 393224 | tf_op jit(solution)/shard_map/ppermute | solution.py:437
  22.8 5.6 %collective-permute-start.12 = (bf16[128,512]{1,0:T(8,128)(2,1)S(1)}, bf16[128,512]{1,0:T(8,128)(2,1)S(1)}, u32[]{:S(2)}, u32[]{:S(2)}) collective-permute-start(bf16[128,512]{1,0:T(8,128)(2,1)S(1)} %grads_total.3.refs_1_), channel_id=1, source_target_pairs={{0,8},{1,9},{2,10},{3,11},{4,12},{5,13},{6,14},{7,15},{8,0},{9,1},... | collective-permute-start | bytes 393224 | tf_op jit(solution)/shard_map/ppermute | solution.py:437
  23.3 5.5 %collective-permute-start.14 = (bf16[128,512]{1,0:T(8,128)(2,1)S(1)}, bf16[128,512]{1,0:T(8,128)(2,1)S(1)}, u32[]{:S(2)}, u32[]{:S(2)}) collective-permute-start(bf16[128,512]{1,0:T(8,128)(2,1)S(1)} %grads_total.3.refs_1_), channel_id=1, source_target_pairs={{0,4},{1,5},{2,6},{3,7},{4,0},{5,1},{6,2},{7,3},{8,12},{9,13},{10,... | collective-permute-start | bytes 393224 | tf_op jit(solution)/shard_map/ppermute | solution.py:437
  24.2 9.1 %collective-permute-start.6 = (bf16[1024,512]{1,0:T(8,128)(2,1)S(1)}, bf16[1024,512]{1,0:T(8,128)(2,1)S(1)}, u32[]{:S(2)}, u32[]{:S(2)}) collective-permute-start(bf16[1024,512]{1,0:T(8,128)(2,1)S(1)} %turn_pieces.1.refs_0_), channel_id=1, source_target_pairs={{0,2},{1,3},{2,0},{3,1},{4,6},{5,7},{6,4},{7,5},{8,10},{9,11},{10,... | collective-permute-start | bytes 3145736 | tf_op jit(solution)/shard_map/ppermute | solution.py:437
  26.3 5.0 %collective-permute-start.9 = (bf16[128,512]{1,0:T(8,128)(2,1)S(1)}, bf16[128,512]{1,0:T(8,128)(2,1)S(1)}, u32[]{:S(2)}, u32[]{:S(2)}) collective-permute-start(bf16[128,512]{1,0:T(8,128)(2,1)S(1)} %collective-permute-done.7.refs_2_), channel_id=1, source_target_pairs={{0,8},{1,9},{2,10},{3,11},{4,12},{5,13},{6,14},{7,15},{8,0},{9,1},... | collective-permute-start | bytes 393224 | tf_op jit(solution)/shard_map/ppermute | solution.py:437
  28.3 5.0 %collective-permute-start.13 = (bf16[128,512]{1,0:T(8,128)(2,1)S(1)}, bf16[128,512]{1,0:T(8,128)(2,1)S(1)}, u32[]{:S(2)}, u32[]{:S(2)}) collective-permute-start(bf16[128,512]{1,0:T(8,128)(2,1)S(1)} %collective-permute-done.12.refs_5_), channel_id=1, source_target_pairs={{0,4},{1,5},{2,6},{3,7},{4,0},{5,1},{6,2},{7,3},{8,12},{9,13},{10,... | collective-permute-start | bytes 393224 | tf_op jit(solution)/shard_map/ppermute | solution.py:437
  33.8 6.4 %collective-permute-start.17 = (bf16[128,512]{1,0:T(8,128)(2,1)S(1)}, bf16[128,512]{1,0:T(8,128)(2,1)S(1)}, u32[]{:S(2)}, u32[]{:S(2)}) collective-permute-start(bf16[128,512]{1,0:T(8,128)(2,1)S(1)} %get-tuple-element.96), channel_id=1, source_target_pairs={{0,1},{1,0},{2,3},{3,2},{4,5},{5,4},{6,7},{7,6},{8,9},{9,8},{10,11... | collective-permute-start | bytes 393224 | tf_op jit(solution)/shard_map/ppermute | solution.py:437
  37.3 5.6 %collective-permute-start.15 = (bf16[128,512]{1,0:T(8,128)(2,1)S(1)}, bf16[128,512]{1,0:T(8,128)(2,1)S(1)}, u32[]{:S(2)}, u32[]{:S(2)}) collective-permute-start(bf16[128,512]{1,0:T(8,128)(2,1)S(1)} %get-tuple-element.90), channel_id=1, source_target_pairs={{0,1},{1,0},{2,3},{3,2},{4,5},{5,4},{6,7},{7,6},{8,9},{9,8},{10,11... | collective-permute-start | bytes 393224 | tf_op jit(solution)/shard_map/ppermute | solution.py:437
  38.2 8.8 %collective-permute-start.16 = (bf16[128,512]{1,0:T(8,128)(2,1)S(1)}, bf16[128,512]{1,0:T(8,128)(2,1)S(1)}, u32[]{:S(2)}, u32[]{:S(2)}) collective-permute-start(bf16[128,512]{1,0:T(8,128)(2,1)S(1)} %get-tuple-element.95), channel_id=1, source_target_pairs={{0,1},{1,0},{2,3},{3,2},{4,5},{5,4},{6,7},{7,6},{8,9},{9,8},{10,11... | collective-permute-start | bytes 393224 | tf_op jit(solution)/shard_map/ppermute | solution.py:437
  40.3 7.3 %collective-permute-start.18 = (bf16[128,512]{1,0:T(8,128)(2,1)S(1)}, bf16[128,512]{1,0:T(8,128)(2,1)S(1)}, u32[]{:S(2)}, u32[]{:S(2)}) collective-permute-start(bf16[128,512]{1,0:T(8,128)(2,1)S(1)} %relay_total.3), channel_id=1, source_target_pairs={{0,16},{1,17},{2,18},{3,19},{4,20},{5,21},{6,22},{7,23},{8,24},{9,... | collective-permute-start | bytes 393224 | tf_op jit(solution)/shard_map/ppermute | solution.py:437
  42.9 8.2 %collective-permute-start.21 = (bf16[128,512]{1,0:T(8,128)(2,1)S(1)}, bf16[128,512]{1,0:T(8,128)(2,1)S(1)}, u32[]{:S(2)}, u32[]{:S(2)}) collective-permute-start(bf16[128,512]{1,0:T(8,128)(2,1)S(1)} %relay_total.2), channel_id=1, source_target_pairs={{0,16},{1,17},{2,18},{3,19},{4,20},{5,21},{6,22},{7,23},{8,24},{9,... | collective-permute-start | bytes 393224 | tf_op jit(solution)/shard_map/ppermute | solution.py:437
  46.0 5.0 %collective-permute-start.20 = (bf16[128,512]{1,0:T(8,128)(2,1)S(1)}, bf16[128,512]{1,0:T(8,128)(2,1)S(1)}, u32[]{:S(2)}, u32[]{:S(2)}) collective-permute-start(bf16[128,512]{1,0:T(8,128)(2,1)S(1)} %get-tuple-element.98), channel_id=1, source_target_pairs={{0,1},{1,0},{2,3},{3,2},{4,5},{5,4},{6,7},{7,6},{8,9},{9,8},{10,11... | collective-permute-start | bytes 393224 | tf_op jit(solution)/shard_map/ppermute | solution.py:437
  47.7 3.4 %collective-permute-start.19 = (bf16[128,512]{1,0:T(8,128)(2,1)S(1)}, bf16[128,512]{1,0:T(8,128)(2,1)S(1)}, u32[]{:S(2)}, u32[]{:S(2)}) collective-permute-start(bf16[128,512]{1,0:T(8,128)(2,1)S(1)} %sibling_total.1), channel_id=1, source_target_pairs={{0,2},{1,3},{2,0},{3,1},{4,6},{5,7},{6,4},{7,5},{8,10},{9,11},{10,... | collective-permute-start | bytes 393224 | tf_op jit(solution)/shard_map/ppermute | solution.py:437

commit v23 on v20

--- a/solution.py
+++ b/solution.py
@@ -483,7 +483,6 @@
         arrived.append([send(value, s) for s, value in enumerate(blocks, 1)])
     own_block, cross_block, *near = weights((0, 1), (0,), grads=grads)
     near, cross_near = near[0::2], near[1::2]
-    arrived[0] = after(arrived[0], own_block)
     cross_near = [send(value, s) for s, value in enumerate(cross_near, 1)]
     for part in range(2):
         relayed = relay_call(far - 1, away[part], arrived[part])

time: 52.1 us -> 52.1 us (level)
  no operation moved by 1% of the time
where the time goes in v23:
time: 52.1 us; the launch traced here: 51.8 us
  starting transfers between devices  26.2 us (50%)
  Pallas kernels  13.1 us (25%)
  waiting for transfers between devices  11.8 us (23%)
  between operations  0.81 us (2%)
    ppermute x22, starting transfers between devices, send(): return lax.ppermute(value, ('dp', 'ctx'), pairs)  26.2 us
    ppermute x22, waiting for transfers between devices, send(): return lax.ppermute(value, ('dp', 'ctx'), pairs)  11.8 us
    pallas_call x2, Pallas kernels, block_call(): pl.pallas_call(functools.partial(block_kernel, ctx_count, step), in_specs...  5.52 us
    pallas_call x3, Pallas kernels, weight_call(): pl.pallas_call(functools.partial(weight_kernel, core_steps, z_steps, far,...  1.77 us
    pallas_call x1, Pallas kernels, query_call(): pl.pallas_call(functools.partial(query_kernel, len(keys)), in_specs=[WHOL...  1.74 us
    pallas_call x1, Pallas kernels, pieces_call(): pl.pallas_call(functools.partial(pieces_kernel, far), in_specs=[FAR], out...  1.39 us
    pallas_call x1, Pallas kernels, near_call(): pl.pallas_call(near_kernel, in_specs=[FAR] * len(values), out_specs=[WHOL...  1.24 us
  transfers between devices with their start and end apart: 22, of which 9 were waited for; matrix products, arithmetic and copies ran while one was open for 0% of the time, Pallas kernels for 23%

profile of v23, /device:TPU:0, one launch (start us, length us, event | category | flops | bytes accessed | tf_op | source)
XLA Modules:
  0.0 51.8 jit_solution(3683272847803677295)
XLA Ops:
  0.7 3.0 %collective-permute-start.1 = (bf16[128,512]{1,0:T(8,128)(2,1)}, bf16[128,512]{1,0:T(8,128)(2,1)S(1)}, u32[]{:S(2)}, u32[]{:S(2)}) collective-permute-start(bf16[128,512]{1,0:T(8,128)(2,1)} %refs_4_.1), channel_id=1, source_target_pairs={{0,1},{1,0},{2,3},{3,2},{4,5},{5,4},{6,7},{7,6},{8,9},{9,8},{10,11... | collective-permute-start | bytes 393224 | tf_op jit(solution)/shard_map/ppermute | solution.py:435
  3.7 0.1 collective-permute-start
  3.7 1.4 %pieces.1 = (bf16[128,1024]{1,0:T(8,128)(2,1)S(1)}, bf16[128,1024]{1,0:T(8,128)(2,1)S(1)}, bf16[128,1024]{1,0:T(8,128)(2,1)S(1)}, bf16[128,1024]{1,0:T(8,128)(2,1)S(1)}) custom-call(bf16[128,4096]{1,0:T(8,128)(2,1)} %in_hbm.1), custom_call_target="tpu_custom_call" | custom-call | flops 1024 | bytes 1024 | tf_op jit(solution)/shard_map/pieces/pallas_call | solution.py:227
  5.1 2.0 %collective-permute-start.3 = (bf16[128,1024]{1,0:T(8,128)(2,1)S(1)}, bf16[128,1024]{1,0:T(8,128)(2,1)S(1)}, u32[]{:S(2)}, u32[]{:S(2)}) collective-permute-start(bf16[128,1024]{1,0:T(8,128)(2,1)S(1)} %get-tuple-element.56), channel_id=1, source_target_pairs={{0,4},{1,5},{2,6},{3,7},{4,0},{5,1},{6,2},{7,3},{8,12},{9,13},{10,... | collective-permute-start | bytes 786440 | tf_op jit(solution)/shard_map/ppermute | solution.py:435
  7.2 1.6 %collective-permute-start.4 = (bf16[128,1024]{1,0:T(8,128)(2,1)S(1)}, bf16[128,1024]{1,0:T(8,128)(2,1)S(1)}, u32[]{:S(2)}, u32[]{:S(2)}) collective-permute-start(bf16[128,1024]{1,0:T(8,128)(2,1)S(1)} %get-tuple-element.61), channel_id=1, source_target_pairs={{0,8},{1,9},{2,10},{3,11},{4,12},{5,13},{6,14},{7,15},{8,0},{9,1},... | collective-permute-start | bytes 786440 | tf_op jit(solution)/shard_map/ppermute | solution.py:435
  8.7 0.0 collective-permute-start.5
  8.7 1.2 %bring_near.1 = (bf16[128,4096]{1,0:T(8,128)(2,1)S(1)}, f32[32,128]{1,0:T(8,128)S(1)}) custom-call(bf16[128,4096]{1,0:T(8,128)(2,1)} %refs_0_.3, f32[32,128]{1,0:T(8,128)} %bitcast.1), custom_call_target="tpu_custom_call" | custom-call | flops 1024 | bytes 1024 | tf_op jit(solution)/shard_map/bring_near/pallas_call | solution.py:185
  10.0 0.0 collective-permute-done.1.refs_4_
  10.0 0.2 collective-permute-done.refs_3_
  10.2 3.1 %visiting_keys.1 = (bf16[128,4096]{1,0:T(8,128)(2,1)S(1)}, bf16[128,512]{1,0:T(8,128)(2,1)S(1)}, bf16[128,512]{1,0:T(8,128)(2,1)S(1)}, f32[32,128]{1,0:T(8,128)S(1)}) custom-call(s32[1,4]{1,0:T(1,128)} %refs_0_.5, bf16[128,4096]{1,0:T(8,128)(2,1)S(1)} %copy-done, bf16[128,4096]{1,0:T(8,128)(2,1)S(1)} %copy-done.1, ...), custom_call_target="tpu_custom_call" | custom-call | flops 5000000000 | bytes 1024 | tf_op jit(solution)/shard_map/visiting_keys/pallas_call | solution.py:130
  13.3 1.8 %collective-permute-start.2 = (bf16[128,512]{1,0:T(8,128)(2,1)S(1)}, bf16[128,512]{1,0:T(8,128)(2,1)S(1)}, u32[]{:S(2)}, u32[]{:S(2)}) collective-permute-start(bf16[128,512]{1,0:T(8,128)(2,1)S(1)} %get-tuple-element.55), channel_id=1, source_target_pairs={{0,1},{1,0},{2,3},{3,2},{4,5},{5,4},{6,7},{7,6},{8,9},{9,8},{10,11... | collective-permute-start | bytes 393224 | tf_op jit(solution)/shard_map/ppermute | solution.py:435
  15.2 0.0 collective-permute-start.11
  15.2 2.4 %own_keys.1 = (bf16[128,4096]{1,0:T(8,128)(2,1)S(1)}, f32[128,512]{1,0:T(8,128)S(1)}, bf16[128,512]{1,0:T(8,128)(2,1)S(1)}) custom-call(s32[1,4]{1,0:T(1,128)} %refs_0_.5, bf16[128,4096]{1,0:T(8,128)(2,1)S(1)} %copy-done, bf16[128,4096]{1,0:T(8,128)(2,1)S(1)} %copy-done.1, bf16[128,512]{1,0:T(8,128)(2,1)S(1)} %copy-done.2, bf16[128,512]{1,0:T(8,128)(2,1)S(1)} %copy-done.3, ...), custom_call_target="tpu_custom_call" | custom-call | flops 1024 | bytes 1024 | tf_op jit(solution)/shard_map/own_keys/pallas_call | solution.py:130
  17.6 0.0 collective-permute-done.4.refs_2_
  17.6 0.4 collective-permute-start.10
  18.0 0.0 collective-permute-done.3.refs_1_
  18.0 0.7 %collective-permute-done.2.refs_1_ = bf16[128,512]{1,0:T(8,128)(2,1)S(1)} collective-permute-done((bf16[128,512]{1,0:T(8,128)(2,1)S(1)}, bf16[128,512]{1,0:T(8,128)(2,1)S(1)}, u32[]{:S(2)}, u32[]{:S(2)}) %collective-permute-start.2) | collective-permute-done | bytes 131104 | tf_op jit(solution)/shard_map/ppermute | solution.py:435
  18.8 2.0 %collective-permute-start.8 = (bf16[128,512]{1,0:T(8,128)(2,1)S(1)}, bf16[128,512]{1,0:T(8,128)(2,1)S(1)}, u32[]{:S(2)}, u32[]{:S(2)}) collective-permute-start(bf16[128,512]{1,0:T(8,128)(2,1)S(1)} %grads_total.2.refs_0_), channel_id=1, source_target_pairs={{0,8},{1,9},{2,10},{3,11},{4,12},{5,13},{6,14},{7,15},{8,0},{9,1},... | collective-permute-start | bytes 393224 | tf_op jit(solution)/shard_map/ppermute | solution.py:435
  20.8 1.5 %collective-permute-start.7 = (bf16[128,512]{1,0:T(8,128)(2,1)S(1)}, bf16[128,512]{1,0:T(8,128)(2,1)S(1)}, u32[]{:S(2)}, u32[]{:S(2)}) collective-permute-start(bf16[128,512]{1,0:T(8,128)(2,1)S(1)} %grads_total.2.refs_0_), channel_id=1, source_target_pairs={{0,4},{1,5},{2,6},{3,7},{4,0},{5,1},{6,2},{7,3},{8,12},{9,13},{10,... | collective-permute-start | bytes 393224 | tf_op jit(solution)/shard_map/ppermute | solution.py:435
  22.3 0.0 collective-permute-done.5.refs_3_
  22.3 0.3 turn_pieces.1.refs_0_
  22.7 0.0 collective-permute-done.11.refs_1_
  22.7 0.5 collective-permute-start.12
  23.2 0.9 %collective-permute-start.14 = (bf16[128,512]{1,0:T(8,128)(2,1)S(1)}, bf16[128,512]{1,0:T(8,128)(2,1)S(1)}, u32[]{:S(2)}, u32[]{:S(2)}) collective-permute-start(bf16[128,512]{1,0:T(8,128)(2,1)S(1)} %grads_total.3.refs_1_), channel_id=1, source_target_pairs={{0,4},{1,5},{2,6},{3,7},{4,0},{5,1},{6,2},{7,3},{8,12},{9,13},{10,... | collective-permute-start | bytes 393224 | tf_op jit(solution)/shard_map/ppermute | solution.py:435
  24.2 0.0 collective-permute-start.6
  24.2 0.0 collective-permute-done.8.refs_4_
  24.2 2.2 %collective-permute-done.7.refs_2_ = bf16[128,512]{1,0:T(8,128)(2,1)S(1)} collective-permute-done((bf16[128,512]{1,0:T(8,128)(2,1)S(1)}, bf16[128,512]{1,0:T(8,128)(2,1)S(1)}, u32[]{:S(2)}, u32[]{:S(2)}) %collective-permute-start.7) | collective-permute-done | bytes 131104 | tf_op jit(solution)/shard_map/ppermute | solution.py:435
  26.3 1.9 %collective-permute-done.12.refs_5_ = bf16[128,512]{1,0:T(8,128)(2,1)S(1)} collective-permute-done((bf16[128,512]{1,0:T(8,128)(2,1)S(1)}, bf16[128,512]{1,0:T(8,128)(2,1)S(1)}, u32[]{:S(2)}, u32[]{:S(2)}) %collective-permute-start.12) | collective-permute-done | bytes 131104 | tf_op jit(solution)/shard_map/ppermute | solution.py:435
  28.3 0.4 collective-permute-start.13
  28.6 0.2 collective-permute-done.14.refs_3_
  28.8 0.1 stack_grads.2
  28.9 2.4 %collective-permute-done.9.refs_0_ = bf16[128,512]{1,0:T(8,128)(2,1)S(1)} collective-permute-done((bf16[128,512]{1,0:T(8,128)(2,1)S(1)}, bf16[128,512]{1,0:T(8,128)(2,1)S(1)}, u32[]{:S(2)}, u32[]{:S(2)}) %collective-permute-start.9) | collective-permute-done | bytes 131104 | tf_op jit(solution)/shard_map/ppermute | solution.py:435
  31.3 1.9 %collective-permute-done.13.refs_1_ = bf16[128,512]{1,0:T(8,128)(2,1)S(1)} collective-permute-done((bf16[128,512]{1,0:T(8,128)(2,1)S(1)}, bf16[128,512]{1,0:T(8,128)(2,1)S(1)}, u32[]{:S(2)}, u32[]{:S(2)}) %collective-permute-start.13) | collective-permute-done | bytes 131104 | tf_op jit(solution)/shard_map/ppermute | solution.py:435
  33.3 0.5 weight_far.2
  33.7 3.0 %collective-permute-start.17 = (bf16[128,512]{1,0:T(8,128)(2,1)S(1)}, bf16[128,512]{1,0:T(8,128)(2,1)S(1)}, u32[]{:S(2)}, u32[]{:S(2)}) collective-permute-start(bf16[128,512]{1,0:T(8,128)(2,1)S(1)} %get-tuple-element.95), channel_id=1, source_target_pairs={{0,1},{1,0},{2,3},{3,2},{4,5},{5,4},{6,7},{7,6},{8,9},{9,8},{10,11... | collective-permute-start | bytes 393224 | tf_op jit(solution)/shard_map/ppermute | solution.py:435
  36.7 0.5 weight_far.3
  37.2 0.1 collective-permute-start.15
  37.3 0.8 %weight_near.1 = (f32[128,512]{1,0:T(8,128)S(1)}, f32[128,512]{1,0:T(8,128)S(1)}, bf16[128,512]{1,0:T(8,128)(2,1)S(1)}, bf16[128,512]{1,0:T(8,128)(2,1)S(1)}) custom-call(bf16[1024,512]{1,0:T(8,128)(2,1)S(1)} %turn_pieces.1.refs_0_, bf16[1024,512]{1,0:T(8,128)(2,1)S(1)} %collective-permute-done.6.refs_1_, bf16[512,512]{1,0:T(8,128)(2,1)S(1)} %get-tuple-element.85.refs_2_, ...), custom_call_target="tpu_custom_call" | custom-call | flops 1024 | bytes 1024 | tf_op jit(solution)/shard_map/weight_near/pallas_call | solution.py:335
  38.1 2.1 %collective-permute-start.16 = (bf16[128,512]{1,0:T(8,128)(2,1)S(1)}, bf16[128,512]{1,0:T(8,128)(2,1)S(1)}, u32[]{:S(2)}, u32[]{:S(2)}) collective-permute-start(bf16[128,512]{1,0:T(8,128)(2,1)S(1)} %get-tuple-element.94), channel_id=1, source_target_pairs={{0,1},{1,0},{2,3},{3,2},{4,5},{5,4},{6,7},{7,6},{8,9},{9,8},{10,11... | collective-permute-start | bytes 393224 | tf_op jit(solution)/shard_map/ppermute | solution.py:435
  40.2 0.0 collective-permute-done.17.refs_0_
  40.2 2.6 %collective-permute-start.18 = (bf16[128,512]{1,0:T(8,128)(2,1)S(1)}, bf16[128,512]{1,0:T(8,128)(2,1)S(1)}, u32[]{:S(2)}, u32[]{:S(2)}) collective-permute-start(bf16[128,512]{1,0:T(8,128)(2,1)S(1)} %relay_total.3), channel_id=1, source_target_pairs={{0,16},{1,17},{2,18},{3,19},{4,20},{5,21},{6,22},{7,23},{8,24},{9,... | collective-permute-start | bytes 393224 | tf_op jit(solution)/shard_map/ppermute | solution.py:435
  42.8 3.2 %collective-permute-start.21 = (bf16[128,512]{1,0:T(8,128)(2,1)S(1)}, bf16[128,512]{1,0:T(8,128)(2,1)S(1)}, u32[]{:S(2)}, u32[]{:S(2)}) collective-permute-start(bf16[128,512]{1,0:T(8,128)(2,1)S(1)} %relay_total.2), channel_id=1, source_target_pairs={{0,16},{1,17},{2,18},{3,19},{4,20},{5,21},{6,22},{7,23},{8,24},{9,... | collective-permute-start | bytes 393224 | tf_op jit(solution)/shard_map/ppermute | solution.py:435
  46.0 0.9 %collective-permute-start.20 = (bf16[128,512]{1,0:T(8,128)(2,1)S(1)}, bf16[128,512]{1,0:T(8,128)(2,1)S(1)}, u32[]{:S(2)}, u32[]{:S(2)}) collective-permute-start(bf16[128,512]{1,0:T(8,128)(2,1)S(1)} %get-tuple-element.96), channel_id=1, source_target_pairs={{0,1},{1,0},{2,3},{3,2},{4,5},{5,4},{6,7},{7,6},{8,9},{9,8},{10,11... | collective-permute-start | bytes 393224 | tf_op jit(solution)/shard_map/ppermute | solution.py:435
  46.9 0.6 %collective-permute-done.18.refs_2_ = bf16[128,512]{1,0:T(8,128)(2,1)S(1)} collective-permute-done((bf16[128,512]{1,0:T(8,128)(2,1)S(1)}, bf16[128,512]{1,0:T(8,128)(2,1)S(1)}, u32[]{:S(2)}, u32[]{:S(2)}) %collective-permute-start.18) | collective-permute-done | bytes 131104 | tf_op jit(solution)/shard_map/ppermute | solution.py:435
  47.6 0.1 collective-permute-start.19
  47.7 1.7 %query_gradient.1 = bf16[128,4096]{1,0:T(8,128)(2,1)} custom-call(bf16[128,4096]{1,0:T(8,128)(2,1)S(1)} %get-tuple-element.90.refs_0_, bf16[128,4096]{1,0:T(8,128)(2,1)S(1)} %get-tuple-element.91.refs_1_, bf16[128,512]{1,0:T(8,128)(2,1)S(1)} %copy-done.2, bf16[128,512]{1,0:T(8,128)(2,1)S(1)} %collective-permute-done.refs_3_), custom_call_target="tpu_custom_call" | custom-call | flops 1024 | bytes 1024 | tf_op jit(solution)/shard_map/query_gradient/pallas_call | solution.py:157
  49.4 1.6 %collective-permute-done.20.refs_0_ = bf16[128,512]{1,0:T(8,128)(2,1)S(1)} collective-permute-done((bf16[128,512]{1,0:T(8,128)(2,1)S(1)}, bf16[128,512]{1,0:T(8,128)(2,1)S(1)}, u32[]{:S(2)}, u32[]{:S(2)}) %collective-permute-start.20) | collective-permute-done | bytes 131104 | tf_op jit(solution)/shard_map/ppermute | solution.py:435
  51.0 0.8 %weight_total.1 = (f32[128,512]{1,0:T(8,128)}, f32[128,512]{1,0:T(8,128)}) custom-call(f32[128,512]{1,0:T(8,128)S(1)} %get-tuple-element.92.block_ref, bf16[128,512]{1,0:T(8,128)(2,1)S(1)} %collective-permute-done.19.sibling_ref, bf16[128,512]{1,0:T(8,128)(2,1)S(1)} %collective-permute-done.20.refs_0_, bf16[128,512]{1,0:T(8,128)(2,1)S(1)} %collective-permute-done.21.refs_1_), custom_call_target="tpu_custom_call" | custom-call | flops 1024 | bytes 1024 | tf_op jit(solution)/shard_map/weight_total/pallas_call | solution.py:402
  (21 shorter events, 0.2 us)
Async XLA Ops:
  0.6 9.5 %copy-start.1 = (bf16[128,4096]{1,0:T(8,128)(2,1)S(1)}, bf16[128,4096]{1,0:T(8,128)(2,1)}, u32[]{:S(2)}) copy-start(bf16[128,4096]{1,0:T(8,128)(2,1)} %refs_2_.4) | copy-start | bytes 3145732
  0.6 9.5 %copy-start = (bf16[128,4096]{1,0:T(8,128)(2,1)S(1)}, bf16[128,4096]{1,0:T(8,128)(2,1)}, u32[]{:S(2)}) copy-start(bf16[128,4096]{1,0:T(8,128)(2,1)} %refs_1_.3) | copy-start | bytes 3145732
  0.7 9.4 %collective-permute-start.1 = (bf16[128,512]{1,0:T(8,128)(2,1)}, bf16[128,512]{1,0:T(8,128)(2,1)S(1)}, u32[]{:S(2)}, u32[]{:S(2)}) collective-permute-start(bf16[128,512]{1,0:T(8,128)(2,1)} %refs_4_.1), channel_id=1, source_target_pairs={{0,1},{1,0},{2,3},{3,2},{4,5},{5,4},{6,7},{7,6},{8,9},{9,8},{10,11... | collective-permute-start | bytes 393224 | tf_op jit(solution)/shard_map/ppermute | solution.py:435
  3.7 6.5 %collective-permute-start = (bf16[128,512]{1,0:T(8,128)(2,1)}, bf16[128,512]{1,0:T(8,128)(2,1)S(1)}, u32[]{:S(2)}, u32[]{:S(2)}) collective-permute-start(bf16[128,512]{1,0:T(8,128)(2,1)} %refs_2_.5), channel_id=1, source_target_pairs={{0,1},{1,0},{2,3},{3,2},{4,5},{5,4},{6,7},{7,6},{8,9},{9,8},{10,11... | collective-permute-start | bytes 393224 | tf_op jit(solution)/shard_map/ppermute | solution.py:435
  5.1 12.9 %collective-permute-start.3 = (bf16[128,1024]{1,0:T(8,128)(2,1)S(1)}, bf16[128,1024]{1,0:T(8,128)(2,1)S(1)}, u32[]{:S(2)}, u32[]{:S(2)}) collective-permute-start(bf16[128,1024]{1,0:T(8,128)(2,1)S(1)} %get-tuple-element.56), channel_id=1, source_target_pairs={{0,4},{1,5},{2,6},{3,7},{4,0},{5,1},{6,2},{7,3},{8,12},{9,13},{10,... | collective-permute-start | bytes 786440 | tf_op jit(solution)/shard_map/ppermute | solution.py:435
  7.2 10.4 %collective-permute-start.4 = (bf16[128,1024]{1,0:T(8,128)(2,1)S(1)}, bf16[128,1024]{1,0:T(8,128)(2,1)S(1)}, u32[]{:S(2)}, u32[]{:S(2)}) collective-permute-start(bf16[128,1024]{1,0:T(8,128)(2,1)S(1)} %get-tuple-element.61), channel_id=1, source_target_pairs={{0,8},{1,9},{2,10},{3,11},{4,12},{5,13},{6,14},{7,15},{8,0},{9,1},... | collective-permute-start | bytes 786440 | tf_op jit(solution)/shard_map/ppermute | solution.py:435
  8.7 13.6 %collective-permute-start.5 = (bf16[128,1024]{1,0:T(8,128)(2,1)S(1)}, bf16[128,1024]{1,0:T(8,128)(2,1)S(1)}, u32[]{:S(2)}, u32[]{:S(2)}) collective-permute-start(bf16[128,1024]{1,0:T(8,128)(2,1)S(1)} %get-tuple-element.63), channel_id=1, source_target_pairs={{0,12},{1,13},{2,14},{3,15},{4,8},{5,9},{6,10},{7,11},{8,4},{9,5},... | collective-permute-start | bytes 786440 | tf_op jit(solution)/shard_map/ppermute | solution.py:435
  10.2 5.0 %copy-start.2 = (bf16[128,512]{1,0:T(8,128)(2,1)S(1)}, bf16[128,512]{1,0:T(8,128)(2,1)}, u32[]{:S(2)}) copy-start(bf16[128,512]{1,0:T(8,128)(2,1)} %refs_2_.5) | copy-start | bytes 393220
  10.2 5.0 %copy-start.3 = (bf16[128,512]{1,0:T(8,128)(2,1)S(1)}, bf16[128,512]{1,0:T(8,128)(2,1)}, u32[]{:S(2)}) copy-start(bf16[128,512]{1,0:T(8,128)(2,1)} %refs_4_.1) | copy-start | bytes 393220
  13.3 5.4 %collective-permute-start.2 = (bf16[128,512]{1,0:T(8,128)(2,1)S(1)}, bf16[128,512]{1,0:T(8,128)(2,1)S(1)}, u32[]{:S(2)}, u32[]{:S(2)}) collective-permute-start(bf16[128,512]{1,0:T(8,128)(2,1)S(1)} %get-tuple-element.55), channel_id=1, source_target_pairs={{0,1},{1,0},{2,3},{3,2},{4,5},{5,4},{6,7},{7,6},{8,9},{9,8},{10,11... | collective-permute-start | bytes 393224 | tf_op jit(solution)/shard_map/ppermute | solution.py:435
  15.2 7.5 %collective-permute-start.11 = (bf16[128,512]{1,0:T(8,128)(2,1)S(1)}, bf16[128,512]{1,0:T(8,128)(2,1)S(1)}, u32[]{:S(2)}, u32[]{:S(2)}) collective-permute-start(bf16[128,512]{1,0:T(8,128)(2,1)S(1)} %get-tuple-element.72), channel_id=1, source_target_pairs={{0,3},{1,2},{2,1},{3,0},{4,7},{5,6},{6,5},{7,4},{8,11},{9,10},{10,... | collective-permute-start | bytes 393224 | tf_op jit(solution)/shard_map/ppermute | solution.py:435
  17.6 5.1 %collective-permute-start.10 = (bf16[128,512]{1,0:T(8,128)(2,1)S(1)}, bf16[128,512]{1,0:T(8,128)(2,1)S(1)}, u32[]{:S(2)}, u32[]{:S(2)}) collective-permute-start(bf16[128,512]{1,0:T(8,128)(2,1)S(1)} %get-tuple-element.71), channel_id=1, source_target_pairs={{0,2},{1,3},{2,0},{3,1},{4,6},{5,7},{6,4},{7,5},{8,10},{9,11},{10,... | collective-permute-start | bytes 393224 | tf_op jit(solution)/shard_map/ppermute | solution.py:435
  18.8 5.4 %collective-permute-start.8 = (bf16[128,512]{1,0:T(8,128)(2,1)S(1)}, bf16[128,512]{1,0:T(8,128)(2,1)S(1)}, u32[]{:S(2)}, u32[]{:S(2)}) collective-permute-start(bf16[128,512]{1,0:T(8,128)(2,1)S(1)} %grads_total.2.refs_0_), channel_id=1, source_target_pairs={{0,8},{1,9},{2,10},{3,11},{4,12},{5,13},{6,14},{7,15},{8,0},{9,1},... | collective-permute-start | bytes 393224 | tf_op jit(solution)/shard_map/ppermute | solution.py:435
  20.8 5.5 %collective-permute-start.7 = (bf16[128,512]{1,0:T(8,128)(2,1)S(1)}, bf16[128,512]{1,0:T(8,128)(2,1)S(1)}, u32[]{:S(2)}, u32[]{:S(2)}) collective-permute-start(bf16[128,512]{1,0:T(8,128)(2,1)S(1)} %grads_total.2.refs_0_), channel_id=1, source_target_pairs={{0,4},{1,5},{2,6},{3,7},{4,0},{5,1},{6,2},{7,3},{8,12},{9,13},{10,... | collective-permute-start | bytes 393224 | tf_op jit(solution)/shard_map/ppermute | solution.py:435
  22.7 5.5 %collective-permute-start.12 = (bf16[128,512]{1,0:T(8,128)(2,1)S(1)}, bf16[128,512]{1,0:T(8,128)(2,1)S(1)}, u32[]{:S(2)}, u32[]{:S(2)}) collective-permute-start(bf16[128,512]{1,0:T(8,128)(2,1)S(1)} %grads_total.3.refs_1_), channel_id=1, source_target_pairs={{0,8},{1,9},{2,10},{3,11},{4,12},{5,13},{6,14},{7,15},{8,0},{9,1},... | collective-permute-start | bytes 393224 | tf_op jit(solution)/shard_map/ppermute | solution.py:435
  23.2 5.6 %collective-permute-start.14 = (bf16[128,512]{1,0:T(8,128)(2,1)S(1)}, bf16[128,512]{1,0:T(8,128)(2,1)S(1)}, u32[]{:S(2)}, u32[]{:S(2)}) collective-permute-start(bf16[128,512]{1,0:T(8,128)(2,1)S(1)} %grads_total.3.refs_1_), channel_id=1, source_target_pairs={{0,4},{1,5},{2,6},{3,7},{4,0},{5,1},{6,2},{7,3},{8,12},{9,13},{10,... | collective-permute-start | bytes 393224 | tf_op jit(solution)/shard_map/ppermute | solution.py:435
  24.2 9.1 %collective-permute-start.6 = (bf16[1024,512]{1,0:T(8,128)(2,1)S(1)}, bf16[1024,512]{1,0:T(8,128)(2,1)S(1)}, u32[]{:S(2)}, u32[]{:S(2)}) collective-permute-start(bf16[1024,512]{1,0:T(8,128)(2,1)S(1)} %turn_pieces.1.refs_0_), channel_id=1, source_target_pairs={{0,2},{1,3},{2,0},{3,1},{4,6},{5,7},{6,4},{7,5},{8,10},{9,11},{10,... | collective-permute-start | bytes 3145736 | tf_op jit(solution)/shard_map/ppermute | solution.py:435
  26.3 5.0 %collective-permute-start.9 = (bf16[128,512]{1,0:T(8,128)(2,1)S(1)}, bf16[128,512]{1,0:T(8,128)(2,1)S(1)}, u32[]{:S(2)}, u32[]{:S(2)}) collective-permute-start(bf16[128,512]{1,0:T(8,128)(2,1)S(1)} %collective-permute-done.7.refs_2_), channel_id=1, source_target_pairs={{0,8},{1,9},{2,10},{3,11},{4,12},{5,13},{6,14},{7,15},{8,0},{9,1},... | collective-permute-start | bytes 393224 | tf_op jit(solution)/shard_map/ppermute | solution.py:435
  28.3 5.0 %collective-permute-start.13 = (bf16[128,512]{1,0:T(8,128)(2,1)S(1)}, bf16[128,512]{1,0:T(8,128)(2,1)S(1)}, u32[]{:S(2)}, u32[]{:S(2)}) collective-permute-start(bf16[128,512]{1,0:T(8,128)(2,1)S(1)} %collective-permute-done.12.refs_5_), channel_id=1, source_target_pairs={{0,4},{1,5},{2,6},{3,7},{4,0},{5,1},{6,2},{7,3},{8,12},{9,13},{10,... | collective-permute-start | bytes 393224 | tf_op jit(solution)/shard_map/ppermute | solution.py:435
  33.7 6.5 %collective-permute-start.17 = (bf16[128,512]{1,0:T(8,128)(2,1)S(1)}, bf16[128,512]{1,0:T(8,128)(2,1)S(1)}, u32[]{:S(2)}, u32[]{:S(2)}) collective-permute-start(bf16[128,512]{1,0:T(8,128)(2,1)S(1)} %get-tuple-element.95), channel_id=1, source_target_pairs={{0,1},{1,0},{2,3},{3,2},{4,5},{5,4},{6,7},{7,6},{8,9},{9,8},{10,11... | collective-permute-start | bytes 393224 | tf_op jit(solution)/shard_map/ppermute | solution.py:435
  37.2 5.6 %collective-permute-start.15 = (bf16[128,512]{1,0:T(8,128)(2,1)S(1)}, bf16[128,512]{1,0:T(8,128)(2,1)S(1)}, u32[]{:S(2)}, u32[]{:S(2)}) collective-permute-start(bf16[128,512]{1,0:T(8,128)(2,1)S(1)} %get-tuple-element.89), channel_id=1, source_target_pairs={{0,1},{1,0},{2,3},{3,2},{4,5},{5,4},{6,7},{7,6},{8,9},{9,8},{10,11... | collective-permute-start | bytes 393224 | tf_op jit(solution)/shard_map/ppermute | solution.py:435
  38.1 8.8 %collective-permute-start.16 = (bf16[128,512]{1,0:T(8,128)(2,1)S(1)}, bf16[128,512]{1,0:T(8,128)(2,1)S(1)}, u32[]{:S(2)}, u32[]{:S(2)}) collective-permute-start(bf16[128,512]{1,0:T(8,128)(2,1)S(1)} %get-tuple-element.94), channel_id=1, source_target_pairs={{0,1},{1,0},{2,3},{3,2},{4,5},{5,4},{6,7},{7,6},{8,9},{9,8},{10,11... | collective-permute-start | bytes 393224 | tf_op jit(solution)/shard_map/ppermute | solution.py:435
  40.2 7.3 %collective-permute-start.18 = (bf16[128,512]{1,0:T(8,128)(2,1)S(1)}, bf16[128,512]{1,0:T(8,128)(2,1)S(1)}, u32[]{:S(2)}, u32[]{:S(2)}) collective-permute-start(bf16[128,512]{1,0:T(8,128)(2,1)S(1)} %relay_total.3), channel_id=1, source_target_pairs={{0,16},{1,17},{2,18},{3,19},{4,20},{5,21},{6,22},{7,23},{8,24},{9,... | collective-permute-start | bytes 393224 | tf_op jit(solution)/shard_map/ppermute | solution.py:435
  42.8 8.2 %collective-permute-start.21 = (bf16[128,512]{1,0:T(8,128)(2,1)S(1)}, bf16[128,512]{1,0:T(8,128)(2,1)S(1)}, u32[]{:S(2)}, u32[]{:S(2)}) collective-permute-start(bf16[128,512]{1,0:T(8,128)(2,1)S(1)} %relay_total.2), channel_id=1, source_target_pairs={{0,16},{1,17},{2,18},{3,19},{4,20},{5,21},{6,22},{7,23},{8,24},{9,... | collective-permute-start | bytes 393224 | tf_op jit(solution)/shard_map/ppermute | solution.py:435
  46.0 5.0 %collective-permute-start.20 = (bf16[128,512]{1,0:T(8,128)(2,1)S(1)}, bf16[128,512]{1,0:T(8,128)(2,1)S(1)}, u32[]{:S(2)}, u32[]{:S(2)}) collective-permute-start(bf16[128,512]{1,0:T(8,128)(2,1)S(1)} %get-tuple-element.96), channel_id=1, source_target_pairs={{0,1},{1,0},{2,3},{3,2},{4,5},{5,4},{6,7},{7,6},{8,9},{9,8},{10,11... | collective-permute-start | bytes 393224 | tf_op jit(solution)/shard_map/ppermute | solution.py:435
  47.6 3.4 %collective-permute-start.19 = (bf16[128,512]{1,0:T(8,128)(2,1)S(1)}, bf16[128,512]{1,0:T(8,128)(2,1)S(1)}, u32[]{:S(2)}, u32[]{:S(2)}) collective-permute-start(bf16[128,512]{1,0:T(8,128)(2,1)S(1)} %sibling_total.1), channel_id=1, source_target_pairs={{0,2},{1,3},{2,0},{3,1},{4,6},{5,7},{6,4},{7,5},{8,10},{9,11},{10,... | collective-permute-start | bytes 393224 | tf_op jit(solution)/shard_map/ppermute | solution.py:435
